TPU v7x, 32 devices: a whole 2x2x4 slice. The times are simulated.
32 devices in a mesh: fsdp: 32 (over z, y, x, core), tp: 1.
Axes of the slice: x: 2, y: 2, z: 4, core: 2. Of those that a mesh axis runs over, the one named last changes fastest.
Arguments:
- gate_pre: bfloat16 [4096, 14336], P('fsdp', 'tp'), may hold values from -6 to 6
- up_pre: bfloat16 [4096, 14336], P('fsdp', 'tp'), may hold values from -6 to 6
- down_weight: bfloat16 [14336, 4096], P('tp', 'fsdp'), may hold values from -0.046875 to 0.046875
Outputs:
- mixed: bfloat16 [4096, 4096], P('fsdp', 'tp')
All inputs are finite; a program needn't handle non-finite values.
Results may differ from a plain program's by a relative error of at most 0.0049.
Values may be sent and summed in bfloat16 or wider, within the bound.
No kernel may reach another device: no remote copies, remote signals or barrier semaphores. Data moves between devices by JAX's collectives and lax.ppermute only.
A program may use at most 192 MiB of HBM per device.

v0:
```python
import jax
import jax.numpy as jnp
from jax import lax
from jax.sharding import PartitionSpec as P


def shards(gate_pre, up_pre, down_weight):
    hidden = (jax.nn.silu(gate_pre.astype(jnp.float32)) * up_pre.astype(jnp.float32)).astype(
        jnp.bfloat16
    )
    terms = jnp.dot(
        hidden,
        lax.all_gather(down_weight, "fsdp", axis=1, tiled=True),
        preferred_element_type=jnp.float32,
    )
    totals = lax.psum(terms, "tp")
    share = totals.shape[1] // lax.axis_size("tp")
    result = lax.dynamic_slice_in_dim(totals, lax.axis_index("tp") * share, share, 1)
    return result.astype(jnp.bfloat16)


def solution(mesh):
    return jax.shard_map(
        shards,
        mesh=mesh,
        in_specs=(P("fsdp", "tp"), P("fsdp", "tp"), P("tp", "fsdp")),
        out_specs=P("fsdp", "tp"),
        check_vma=False,
    )
```

profile of v0, /device:TPU:0, one launch (start us, length us, event | category | flops | bytes accessed | tf_op | source)
XLA Modules:
  0.0 673.1 jit_solution(3452844209910215353)
XLA Ops:
  6.5 0.0 all-gather.2.cloned.1.call-start
  6.5 0.7 all-gather.2.cloned.1.call-update
  7.3 617.1 %all-gather.2.cloned.1.call-done = bf16[14336,4096]{1,0:T(8,128)(2,1)} async-done(((bf16[14336,128]{1,0:T(8,128)(2,1)}), bf16[14336,4096]{1,0:T(8,128)(2,1)}) %all-gather.2.cloned.1.call-update) | async-done | bytes 117440528 | tf_op jit(solution)/shard_map/all_gather | solution.py:13
  624.4 41.9 %convolution_convert_fusion = bf16[128,4096]{1,0:T(8,128)(2,1)} fusion(bf16[14336,4096]{1,0:T(8,128)(2,1)} %all-gather.2.cloned.1.call-done, bf16[128,14336]{1,0:T(8,128)(2,1)} %param.4, bf16[128,14336]{1,0:T(8,128)(2,1)} %param.3), kind=kOutput, calls=%fused_computation.7 | convolution fusion | flops 15047589888 | bytes 125829120 | tf_op jit(solution)/shard_map/dot_general | solution.py:11
Async XLA Ops:
  6.5 617.9 %all-gather.2.cloned.1.call-start = ((), (), s32[]{:S(2)}) async-start(), calls=%async_computation | async-start | bytes 121110528 | tf_op jit(solution)/shard_map/all_gather | solution.py:13
Sparse Core Ops, SparseCore 0:
  8.9 615.4 all-gather.1
where the time goes:
time: 673 us
  waiting for transfers between devices  618 us (92%)
  matrix products  41.9 us (6%)
  between operations  13.4 us (2%)
    all_gather x1, waiting for transfers between devices, shards(): lax.all_gather(down_weight, 'fsdp', axis=1, tiled=True)  617 us
    dot_general x1, matrix products, shards(): jnp.dot(hidden, lax.all_gather(down_weight, 'fsdp', axis=1, tiled=True),...  41.9 us
  transfers between devices with their start and end apart: 1, of which 1 were waited for; matrix products, arithmetic and copies ran while one was open for 0% of the time, Pallas kernels for 0%

commit v1 on v0

v1 whole, which is shorter than its diff:
```python
import functools

import jax
import jax.numpy as jnp
from jax import lax
from jax.experimental import pallas as pl
from jax.experimental.pallas import tpu as pltpu
from jax.sharding import PartitionSpec as P

CORE, PLANE, PAIR = 1, 2, 8
LIMIT = 48 * 1024 * 1024


def flip(n, mask):
    return [(source, source ^ mask) for source in range(n)]


def along_z(n, pairs):
    low = PAIR
    return [(a * low + rest, b * low + rest) for a, b in pairs for rest in range(low)]


def silu_product(gate, up):
    return (jax.nn.silu(gate.astype(jnp.float32)) * up.astype(jnp.float32)).astype(jnp.bfloat16)


def product_kernel(choices, mid_ref, *refs):
    a_refs, refs = refs[:16], refs[16:]
    w_refs, refs = refs[: 4 * choices], refs[4 * choices :]
    outs, (a, w, a_sem, w_sem) = refs[:4], refs[4:]
    rows = a_refs[0].shape[0]
    columns = w_refs[0].shape[1]

    def w_copy(at, choice):
        return pltpu.make_async_copy(
            w_refs[4 * choice + at], w.at[:, pl.ds(at * columns, columns)], w_sem.at[at]
        )

    def a_copy(at):
        return pltpu.make_async_copy(a_refs[at], a.at[pl.ds(at * rows, rows)], a_sem.at[at])

    for at in range(4):
        if choices == 1:
            w_copy(at, 0).start()
        else:
            for choice in range(choices):

                @pl.when(mid_ref[0] == choice)
                def _():
                    w_copy(at, choice).start()

    for at in range(16):
        a_copy(at).start()
    for at in range(4):
        w_copy(at, 0).wait()
    order = (3, 1, 2, 0)
    for to in order:
        for half in range(2):
            at = 4 * to + 2 * half
            a_copy(at).wait()
            a_copy(at + 1).wait()
            total = jnp.dot(
                a[pl.ds(at * rows, 2 * rows)], w[...], preferred_element_type=jnp.float32
            )
            outs[to][2 * half] = total[:rows].astype(outs[to].dtype)
            outs[to][2 * half + 1] = total[rows:].astype(outs[to].dtype)


def product(mid, a_blocks, w_choices):
    rows, depth = a_blocks[0].shape
    columns = w_choices[0][0].shape[1]
    w_blocks = [block for choice in w_choices for block in choice]
    shape = (4, rows, 4 * columns)
    return pl.pallas_call(
        functools.partial(product_kernel, len(w_choices)),
        out_shape=[jax.ShapeDtypeStruct(shape, jnp.float32)]
        + [jax.ShapeDtypeStruct(shape, jnp.bfloat16)] * 3,
        in_specs=[pl.BlockSpec(memory_space=pltpu.SMEM)]
        + [pl.BlockSpec(memory_space=pl.ANY)] * (16 + len(w_blocks)),
        out_specs=[pl.BlockSpec(memory_space=pltpu.VMEM)] * 4,
        scratch_shapes=[
            pltpu.VMEM((16 * rows, depth), jnp.bfloat16),
            pltpu.VMEM((depth, 4 * columns), jnp.bfloat16),
            pltpu.SemaphoreType.DMA((16,)),
            pltpu.SemaphoreType.DMA((4,)),
        ],
        compiler_params=pltpu.CompilerParams(vmem_limit_bytes=LIMIT),
        cost_estimate=pl.CostEstimate(
            flops=2 * 16 * rows * depth * 4 * columns,
            bytes_accessed=2 * depth * (16 * rows + 4 * columns),
            transcendentals=0,
        ),
        name="product",
    )(mid, *a_blocks, *w_blocks)


def add_kernel(own, one, two, three, *outs):
    columns = own.shape[2] // 4
    for piece in range(4):
        for at in range(4):
            here = pl.ds(at * columns, columns)
            total = own[piece, :, here]
            for step, ref in ((1, one), (2, two), (3, three)):
                total += ref[piece, :, pl.ds((at ^ step) * columns, columns)].astype(jnp.float32)
            outs[piece][:, here] = total.astype(jnp.bfloat16)


def add(own, others):
    _, rows, columns = own.shape
    return pl.pallas_call(
        add_kernel,
        out_shape=[jax.ShapeDtypeStruct((rows, columns), jnp.bfloat16)] * 4,
        in_specs=[pl.BlockSpec(memory_space=pltpu.VMEM)] * 4,
        out_specs=[pl.BlockSpec(memory_space=pltpu.VMEM)] * 4,
        compiler_params=pltpu.CompilerParams(vmem_limit_bytes=LIMIT),
        cost_estimate=pl.CostEstimate(
            flops=12 * rows * columns, bytes_accessed=48 * rows * columns, transcendentals=0
        ),
        name="add",
    )(own, *others)


def assemble_kernel(place_ref, *refs):
    pieces, out = refs[:8], refs[8]
    columns = out.shape[1] // 32
    place = place_ref[0]
    for half in range(2):
        for piece in range(4):
            for at in range(4):
                index = ((piece >> 1) << 4) | (half << 3) | (at << 1) | (piece & 1)
                to = pl.multiple_of((place ^ index) * columns, columns)
                out[:, pl.ds(to, columns)] = pieces[4 * half + piece][:, pl.ds(at * columns, columns)]


def assemble(place, pieces):
    rows, columns = pieces[0].shape
    return pl.pallas_call(
        assemble_kernel,
        out_shape=jax.ShapeDtypeStruct((rows, 8 * columns), jnp.bfloat16),
        in_specs=[pl.BlockSpec(memory_space=pltpu.SMEM)]
        + [pl.BlockSpec(memory_space=pltpu.VMEM)] * 8,
        out_specs=pl.BlockSpec(memory_space=pltpu.VMEM),
        compiler_params=pltpu.CompilerParams(vmem_limit_bytes=LIMIT),
        name="assemble",
    )(place, *pieces)


def blocks(gate_pre, up_pre, down_weight):
    n = lax.axis_size("fsdp")
    me = lax.axis_index("fsdp")
    send = functools.partial(lax.ppermute, axis_name="fsdp")
    depth = gate_pre.shape[1] // 4
    plane = (me // PLANE) % 4
    z_low, z_high = (me // PAIR) % 2, me // (2 * PAIR)

    a, w = [None] * 4, [None] * 4
    for step in range(4):
        start = (plane ^ step) * depth
        hidden = silu_product(
            lax.dynamic_slice_in_dim(gate_pre, start, depth, 1),
            lax.dynamic_slice_in_dim(up_pre, start, depth, 1),
        )
        weight = lax.dynamic_slice_in_dim(down_weight, start, depth, 0)
        if step:
            hidden = send(hidden, perm=flip(n, step * PLANE))
            weight = send(weight, perm=flip(n, step * PLANE))
        a[step], w[step] = hidden, weight

    a_pair = [send(block, perm=flip(n, PAIR)) for block in a]
    w_mid = [send(block, perm=along_z(n, [(1, 2), (2, 1)])) for block in w]
    w_next = [send(block, perm=along_z(n, [(1, 0), (3, 1), (0, 2), (2, 3)])) for block in w]
    a_blocks = []
    for step in range(4):
        for block in (a[step], a_pair[step]):
            a_blocks += [block, send(block, perm=flip(n, CORE))]

    mid = (z_low ^ z_high).astype(jnp.int32).reshape(1)
    pieces = []
    for choices in ([w, w_mid], [w_next]):
        own, *others = product(mid, a_blocks, choices)
        others = [send(other, perm=flip(n, step * PLANE)) for step, other in zip((1, 2, 3), others)]
        summed = add(own, others)
        pieces += [summed[0]] + [
            send(summed[piece], perm=flip(n, (piece >> 1) * PAIR + (piece & 1) * CORE))
            for piece in (1, 2, 3)
        ]
    place = (z_low * 16 + z_high * 8 + plane * 2 + me % 2).astype(jnp.int32).reshape(1)
    return assemble(place, pieces)


def shards(gate_pre, up_pre, down_weight):
    hidden = silu_product(gate_pre, up_pre)
    terms = jnp.dot(
        hidden,
        lax.all_gather(down_weight, "fsdp", axis=1, tiled=True),
        preferred_element_type=jnp.float32,
    )
    totals = lax.psum(terms, "tp")
    share = totals.shape[1] // lax.axis_size("tp")
    result = lax.dynamic_slice_in_dim(totals, lax.axis_index("tp") * share, share, 1)
    return result.astype(jnp.bfloat16)


def solution(mesh):
    in_blocks = mesh.shape["tp"] == 1 and mesh.shape["fsdp"] == 4 * PAIR
    return jax.shard_map(
        blocks if in_blocks else shards,
        mesh=mesh,
        in_specs=(P("fsdp", "tp"), P("fsdp", "tp"), P("tp", "fsdp")),
        out_specs=P("fsdp", "tp"),
        check_vma=False,
    )
```

time: 673 us -> 302 us (0.45)
  waiting for transfers between devices: 618 us -> 154 us
  starting transfers between devices: 0.01 us -> 104 us
  matrix products: 41.9 us -> 0 us
  Pallas kernels: 0 us -> 31.4 us
  between operations: 13.4 us -> 0.3 us
  local copies, waits for them, and re-layouts: 0 us -> 7.19 us
    all_gather x1 -> x0, waiting for transfers between devices: 617 us -> none  [shards(): lax.all_gather(down_weight, 'fsdp', axis=1, tiled=True)]
    ppermute x0 -> x38, waiting for transfers between devices: none -> 154 us  [the longest x4 68.2 us: blocks(): a_pair = [send(block, perm=flip(n, PAIR)) for block in a]]
    ppermute x0 -> x38, starting transfers between devices: none -> 104 us  [the longest x4 74.2 us: blocks(): send(block, perm=along_z(n, [(1, 0), (3, 1), (0, 2), (2, 3)]))]
    dot_general x1 -> x0, matrix products: 41.9 us -> none  [shards(): jnp.dot(hidden, lax.all_gather(down_weight, 'fsdp', axis=1, tiled=True),...]
    pallas_call x0 -> x5, Pallas kernels: none -> 31.4 us  [the longest x2 29.6 us: product(): pl.pallas_call(functools.partial(product_kernel, len(w_choices)), out_sha...]
  transfers between devices with their start and end apart: 1 -> 38, of which waited for: 1 -> 13; matrix products, arithmetic and copies ran while one was open for 0% -> 0% of each run, Pallas kernels for 0% -> 10%
where the time goes in v1:
time: 302 us; the launch traced here: 301 us
  waiting for transfers between devices  154 us (51%)
  starting transfers between devices  104 us (34%)
  Pallas kernels  31.4 us (10%)
  local copies, waits for them, and re-layouts  7.19 us (2%)
  other arithmetic  4.39 us (1%)
    ppermute x4, starting transfers between devices, blocks(): send(block, perm=along_z(n, [(1, 0), (3, 1), (0, 2), (2, 3)]))  74.2 us
    ppermute x4, waiting for transfers between devices, blocks(): a_pair = [send(block, perm=flip(n, PAIR)) for block in a]  68.2 us
    ppermute x3, waiting for transfers between devices, blocks(): weight = send(weight, perm=flip(n, step * PLANE))  38 us
    pallas_call x2, Pallas kernels, product(): pl.pallas_call(functools.partial(product_kernel, len(w_choices)), out_sha...  29.6 us
    ppermute x3, waiting for transfers between devices, blocks(): hidden = send(hidden, perm=flip(n, step * PLANE))  18.8 us
    ppermute x6, waiting for transfers between devices, blocks(): send(other, perm=flip(n, step * PLANE))  14.4 us
    ppermute x4, waiting for transfers between devices, blocks(): send(block, perm=along_z(n, [(1, 0), (3, 1), (0, 2), (2, 3)]))  7.82 us
    ppermute x6, starting transfers between devices, blocks(): send(other, perm=flip(n, step * PLANE))  7.22 us
  transfers between devices with their start and end apart: 38, of which 13 were waited for; matrix products, arithmetic and copies ran while one was open for 0% of the time, Pallas kernels for 10%

profile of v1, /device:TPU:0, one launch (start us, length us, event | category | flops | bytes accessed | tf_op | source)
XLA Modules:
  0.0 301.5 jit_solution(3449782320399094689)
XLA Ops:
  0.0 4.4 %fusion.16 = (bf16[128,3584]{1,0:T(8,128)(2,1)S(1)}, bf16[128,3584]{1,0:T(8,128)(2,1)S(1)}, bf16[128,3584]{1,0:T(8,128)(2,1)S(1)}, bf16[128,3584]{1,0:T(8,128)(2,1)S(1)}) fusion(bf16[128,14336]{1,0:T(8,128)(2,1)} %param.4, s32[]{:T(128)S(6)} %select_n.54, bf16[128,14336]{1,0:T(8,128)(2,1)} %param.3, s32[]{:T(128)S(6)} %select_n.52, s32[]{:T(128)S(6)} %select_n.51, ...), kind=kLoop, calls=%fused_computation.24 | loop fusion | flops 14680064 | bytes 11010064 | tf_op jit(solution)/shard_map/convert_element_type | solution.py:24
  4.4 0.5 collective-permute-start
  4.9 2.6 collective-permute-start.1
  7.6 1.5 collective-permute-start.3
  9.1 1.5 collective-permute-start.7
  10.6 0.5 collective-permute-start.11
  11.1 1.2 constant_dynamic-slice_fusion
  12.2 1.5 collective-permute-start.15
  13.7 14.8 %collective-permute-done.1.refs_2_ = bf16[128,3584]{1,0:T(8,128)(2,1)S(1)} collective-permute-done((bf16[128,3584]{1,0:T(8,128)(2,1)S(1)}, bf16[128,3584]{1,0:T(8,128)(2,1)S(1)}, u32[]{:S(2)}, u32[]{:S(2)}) %collective-permute-start.1) | collective-permute-done | bytes 917536 | tf_op jit(solution)/shard_map/ppermute | solution.py:169
  28.5 1.7 collective-permute-start.16
  30.2 0.6 collective-permute-done.3.refs_4_
  30.8 2.4 collective-permute-start.17
  33.2 18.2 %collective-permute-done.7.refs_8_ = bf16[128,3584]{1,0:T(8,128)(2,1)S(1)} collective-permute-done((bf16[128,3584]{1,0:T(8,128)(2,1)S(1)}, bf16[128,3584]{1,0:T(8,128)(2,1)S(1)}, u32[]{:S(2)}, u32[]{:S(2)}) %collective-permute-start.7) | collective-permute-done | bytes 917536 | tf_op jit(solution)/shard_map/ppermute | solution.py:165
  51.4 0.7 collective-permute-start.18
  52.3 18.0 %collective-permute-done.15.refs_17_ = bf16[3584,128]{1,0:T(8,128)(2,1)} collective-permute-done((bf16[3584,128]{1,0:T(8,128)(2,1)S(1)}, bf16[3584,128]{1,0:T(8,128)(2,1)}, u32[]{:S(2)}, u32[]{:S(2)}) %collective-permute-start.15) | collective-permute-done | bytes 917536 | tf_op jit(solution)/shard_map/ppermute | solution.py:166
  70.2 20.1 %collective-permute-done.16.refs_18_ = bf16[3584,128]{1,0:T(8,128)(2,1)} collective-permute-done((bf16[3584,128]{1,0:T(8,128)(2,1)S(1)}, bf16[3584,128]{1,0:T(8,128)(2,1)}, u32[]{:S(2)}, u32[]{:S(2)}) %collective-permute-start.16) | collective-permute-done | bytes 917536 | tf_op jit(solution)/shard_map/ppermute | solution.py:166
  90.3 0.4 collective-permute-start.5
  90.8 0.9 copy-done.2
  91.7 1.6 collective-permute-start.9
  93.3 0.9 copy-done.4
  94.4 0.6 collective-permute-start.13
  95.0 18.6 %collective-permute-done.5.refs_6_ = bf16[128,3584]{1,0:T(8,128)(2,1)S(1)} collective-permute-done((bf16[128,3584]{1,0:T(8,128)(2,1)S(1)}, bf16[128,3584]{1,0:T(8,128)(2,1)S(1)}, u32[]{:S(2)}, u32[]{:S(2)}) %collective-permute-start.5) | collective-permute-done | bytes 917536 | tf_op jit(solution)/shard_map/ppermute | solution.py:169
  113.6 0.7 collective-permute-start.19
  114.3 0.7 collective-permute-start.20
  115.1 18.2 %collective-permute-done.9.refs_10_ = bf16[128,3584]{1,0:T(8,128)(2,1)S(1)} collective-permute-done((bf16[128,3584]{1,0:T(8,128)(2,1)S(1)}, bf16[128,3584]{1,0:T(8,128)(2,1)S(1)}, u32[]{:S(2)}, u32[]{:S(2)}) %collective-permute-start.9) | collective-permute-done | bytes 917536 | tf_op jit(solution)/shard_map/ppermute | solution.py:169
  133.3 0.7 collective-permute-start.21
  134.1 16.6 %collective-permute-done.13.refs_14_ = bf16[128,3584]{1,0:T(8,128)(2,1)} collective-permute-done((bf16[128,3584]{1,0:T(8,128)(2,1)S(1)}, bf16[128,3584]{1,0:T(8,128)(2,1)}, u32[]{:S(2)}, u32[]{:S(2)}) %collective-permute-start.13) | collective-permute-done | bytes 917536 | tf_op jit(solution)/shard_map/ppermute | solution.py:169
  150.7 0.6 collective-permute-start.14
  151.3 19.8 %collective-permute-start.28 = (bf16[3584,128]{1,0:T(8,128)(2,1)}, bf16[3584,128]{1,0:T(8,128)(2,1)}, u32[]{:S(2)}, u32[]{:S(2)}) collective-permute-start(bf16[3584,128]{1,0:T(8,128)(2,1)} %get-tuple-element.43.refs_16_), channel_id=1, source_target_pairs={{8,0},{9,1},{10,2},{11,3},{12,4},{13,5},{14,6},{15,7},{24,8},{25,9... | collective-permute-start | bytes 2752520 | tf_op jit(solution)/shard_map/ppermute | solution.py:171
  171.1 54.1 %collective-permute-start.29 = (bf16[3584,128]{1,0:T(8,128)(2,1)}, bf16[3584,128]{1,0:T(8,128)(2,1)}, u32[]{:S(2)}, u32[]{:S(2)}) collective-permute-start(bf16[3584,128]{1,0:T(8,128)(2,1)} %collective-permute-done.15.refs_17_), channel_id=1, source_target_pairs={{8,0},{9,1},{10,2},{11,3},{12,4},{13,5},{14,6},{15,7},{24,8},{25,9... | collective-permute-start | bytes 2752520 | tf_op jit(solution)/shard_map/ppermute | solution.py:171
  225.3 0.8 copy-done.15
  226.1 0.9 copy-done.16
  227.3 1.2 copy-done.3
  228.5 1.2 copy-done.5
  229.7 14.8 %product.2 = (f32[4,128,512]{2,1,0:T(8,128)}, bf16[4,128,512]{2,1,0:T(8,128)(2,1)S(1)}, bf16[4,128,512]{2,1,0:T(8,128)(2,1)S(1)}, bf16[4,128,512]{2,1,0:T(8,128)(2,1)S(1)}) custom-call(s32[1]{0:T(128)} %bitcast.1.mid_ref, bf16[128,3584]{1,0:T(8,128)(2,1)S(1)} %get-tuple-element.39.refs_0_, bf16[128,3584]{1,0:T(8,128)(2,1)S(1)} %collective-permute-done.refs_1_, ...), custom_call_target="tpu_custom_call" | custom-call | flops 7516192768 | bytes 18350080 | tf_op jit(solution)/shard_map/product/pallas_call | solution.py:74
  244.6 2.1 collective-permute-start.23
  246.8 1.5 collective-permute-start.24
  248.2 7.8 %collective-permute-done.31.refs_19_ = bf16[3584,128]{1,0:T(8,128)(2,1)} collective-permute-done((bf16[3584,128]{1,0:T(8,128)(2,1)}, bf16[3584,128]{1,0:T(8,128)(2,1)}, u32[]{:S(2)}, u32[]{:S(2)}) %collective-permute-start.31) | collective-permute-done | bytes 917536 | tf_op jit(solution)/shard_map/ppermute | solution.py:171
  256.0 14.8 %product.3 = (f32[4,128,512]{2,1,0:T(8,128)}, bf16[4,128,512]{2,1,0:T(8,128)(2,1)S(1)}, bf16[4,128,512]{2,1,0:T(8,128)(2,1)S(1)}, bf16[4,128,512]{2,1,0:T(8,128)(2,1)S(1)}) custom-call(s32[1]{0:T(128)} %bitcast.1.mid_ref, bf16[128,3584]{1,0:T(8,128)(2,1)S(1)} %get-tuple-element.39.refs_0_, bf16[128,3584]{1,0:T(8,128)(2,1)S(1)} %collective-permute-done.refs_1_, ...), custom_call_target="tpu_custom_call" | custom-call | flops 7516192768 | bytes 18350080 | tf_op jit(solution)/shard_map/product/pallas_call | solution.py:74
  270.9 1.5 collective-permute-start.33
  272.5 1.9 collective-permute-start.34
  274.8 1.7 collective-permute-start.26
  276.5 4.4 %collective-permute-done.32.one = bf16[4,128,512]{2,1,0:T(8,128)(2,1)S(1)} collective-permute-done((bf16[4,128,512]{2,1,0:T(8,128)(2,1)S(1)}, bf16[4,128,512]{2,1,0:T(8,128)(2,1)S(1)}, u32[]{:S(2)}, u32[]{:S(2)}) %collective-permute-start.32) | collective-permute-done | bytes 524320 | tf_op jit(solution)/shard_map/ppermute | solution.py:181
  280.8 10.0 %collective-permute-done.33.two = bf16[4,128,512]{2,1,0:T(8,128)(2,1)S(1)} collective-permute-done((bf16[4,128,512]{2,1,0:T(8,128)(2,1)S(1)}, bf16[4,128,512]{2,1,0:T(8,128)(2,1)S(1)}, u32[]{:S(2)}, u32[]{:S(2)}) %collective-permute-start.33) | collective-permute-done | bytes 524320 | tf_op jit(solution)/shard_map/ppermute | solution.py:181
  291.2 2.4 collective-permute-start.36
  293.7 4.3 %collective-permute-done.36.refs_6_ = bf16[128,512]{1,0:T(8,128)(2,1)S(1)} collective-permute-done((bf16[128,512]{1,0:T(8,128)(2,1)S(1)}, bf16[128,512]{1,0:T(8,128)(2,1)S(1)}, u32[]{:S(2)}, u32[]{:S(2)}) %collective-permute-start.36) | collective-permute-done | bytes 131104 | tf_op jit(solution)/shard_map/ppermute | solution.py:184
  297.9 2.3 collective-permute-done.37.refs_7_
  300.2 1.2 assemble.1
  (75 shorter events, 1.6 us)
Async XLA Ops:
  4.4 7.8 %collective-permute-start = (bf16[128,3584]{1,0:T(8,128)(2,1)S(1)}, bf16[128,3584]{1,0:T(8,128)(2,1)S(1)}, u32[]{:S(2)}, u32[]{:S(2)}) collective-permute-start(bf16[128,3584]{1,0:T(8,128)(2,1)S(1)} %get-tuple-element.39.refs_0_), channel_id=1, source_target_pairs={{0,1},{1,0},{2,3},{3,2},{4,5},{5,4},{6,7},{7,6},{8,9},{9,8},{10,11... | collective-permute-start | bytes 2752520 | tf_op jit(solution)/shard_map/ppermute | solution.py:175
  4.9 23.6 %collective-permute-start.1 = (bf16[128,3584]{1,0:T(8,128)(2,1)S(1)}, bf16[128,3584]{1,0:T(8,128)(2,1)S(1)}, u32[]{:S(2)}, u32[]{:S(2)}) collective-permute-start(bf16[128,3584]{1,0:T(8,128)(2,1)S(1)} %get-tuple-element.39.refs_0_), channel_id=1, source_target_pairs={{0,8},{1,9},{2,10},{3,11},{4,12},{5,13},{6,14},{7,15},{8,0},{9,1},... | collective-permute-start | bytes 2752520 | tf_op jit(solution)/shard_map/ppermute | solution.py:169
  7.6 23.2 %collective-permute-start.3 = (bf16[128,3584]{1,0:T(8,128)(2,1)S(1)}, bf16[128,3584]{1,0:T(8,128)(2,1)S(1)}, u32[]{:S(2)}, u32[]{:S(2)}) collective-permute-start(bf16[128,3584]{1,0:T(8,128)(2,1)S(1)} %get-tuple-element.38), channel_id=1, source_target_pairs={{0,2},{1,3},{2,0},{3,1},{4,6},{5,7},{6,4},{7,5},{8,10},{9,11},{10,... | collective-permute-start | bytes 2752520 | tf_op jit(solution)/shard_map/ppermute | solution.py:165
  9.1 42.4 %collective-permute-start.7 = (bf16[128,3584]{1,0:T(8,128)(2,1)S(1)}, bf16[128,3584]{1,0:T(8,128)(2,1)S(1)}, u32[]{:S(2)}, u32[]{:S(2)}) collective-permute-start(bf16[128,3584]{1,0:T(8,128)(2,1)S(1)} %get-tuple-element.40), channel_id=1, source_target_pairs={{0,4},{1,5},{2,6},{3,7},{4,0},{5,1},{6,2},{7,3},{8,12},{9,13},{10,... | collective-permute-start | bytes 2752520 | tf_op jit(solution)/shard_map/ppermute | solution.py:165
  10.6 41.6 %collective-permute-start.11 = (bf16[128,3584]{1,0:T(8,128)(2,1)S(1)}, bf16[128,3584]{1,0:T(8,128)(2,1)S(1)}, u32[]{:S(2)}, u32[]{:S(2)}) collective-permute-start(bf16[128,3584]{1,0:T(8,128)(2,1)S(1)} %get-tuple-element.37), channel_id=1, source_target_pairs={{0,6},{1,7},{2,4},{3,5},{4,2},{5,3},{6,0},{7,1},{8,14},{9,15},{10,... | collective-permute-start | bytes 2752520 | tf_op jit(solution)/shard_map/ppermute | solution.py:165
  12.2 58.0 %collective-permute-start.15 = (bf16[3584,128]{1,0:T(8,128)(2,1)S(1)}, bf16[3584,128]{1,0:T(8,128)(2,1)}, u32[]{:S(2)}, u32[]{:S(2)}) collective-permute-start(bf16[3584,128]{1,0:T(8,128)(2,1)S(1)} %get-tuple-element.42), channel_id=1, source_target_pairs={{0,2},{1,3},{2,0},{3,1},{4,6},{5,7},{6,4},{7,5},{8,10},{9,11},{10,... | collective-permute-start | bytes 2752520 | tf_op jit(solution)/shard_map/ppermute | solution.py:166
  28.5 61.8 %collective-permute-start.16 = (bf16[3584,128]{1,0:T(8,128)(2,1)S(1)}, bf16[3584,128]{1,0:T(8,128)(2,1)}, u32[]{:S(2)}, u32[]{:S(2)}) collective-permute-start(bf16[3584,128]{1,0:T(8,128)(2,1)S(1)} %get-tuple-element.44), channel_id=1, source_target_pairs={{0,4},{1,5},{2,6},{3,7},{4,0},{5,1},{6,2},{7,3},{8,12},{9,13},{10,... | collective-permute-start | bytes 2752520 | tf_op jit(solution)/shard_map/ppermute | solution.py:166
  30.8 60.9 %collective-permute-start.17 = (bf16[3584,128]{1,0:T(8,128)(2,1)S(1)}, bf16[3584,128]{1,0:T(8,128)(2,1)}, u32[]{:S(2)}, u32[]{:S(2)}) collective-permute-start(bf16[3584,128]{1,0:T(8,128)(2,1)S(1)} %get-tuple-element.41), channel_id=1, source_target_pairs={{0,6},{1,7},{2,4},{3,5},{4,2},{5,3},{6,0},{7,1},{8,14},{9,15},{10,... | collective-permute-start | bytes 2752520 | tf_op jit(solution)/shard_map/ppermute | solution.py:166
  51.4 62.1 %copy-start.7 = (bf16[128,3584]{1,0:T(8,128)(2,1)}, bf16[128,3584]{1,0:T(8,128)(2,1)S(1)}, u32[]{:S(2)}) copy-start(bf16[128,3584]{1,0:T(8,128)(2,1)S(1)} %collective-permute-done.7.refs_8_) | copy-start | bytes 2752516
  51.4 40.2 %collective-permute-start.18 = (bf16[3584,128]{1,0:T(8,128)(2,1)}, bf16[3584,128]{1,0:T(8,128)(2,1)S(1)}, u32[]{:S(2)}, u32[]{:S(2)}) collective-permute-start(bf16[3584,128]{1,0:T(8,128)(2,1)} %get-tuple-element.43.refs_16_), channel_id=1, source_target_pairs={{8,16},{9,17},{10,18},{11,19},{12,20},{13,21},{14,22},{15,23},{16,... | collective-permute-start | bytes 2752520 | tf_op jit(solution)/shard_map/ppermute | solution.py:170
  52.2 81.1 %copy-start.8 = (bf16[128,3584]{1,0:T(8,128)(2,1)}, bf16[128,3584]{1,0:T(8,128)(2,1)S(1)}, u32[]{:S(2)}) copy-start(bf16[128,3584]{1,0:T(8,128)(2,1)S(1)} %collective-permute-done.11.refs_12_) | copy-start | bytes 2752516
  52.2 41.2 %collective-permute-start.2 = (bf16[128,3584]{1,0:T(8,128)(2,1)S(1)}, bf16[128,3584]{1,0:T(8,128)(2,1)S(1)}, u32[]{:S(2)}, u32[]{:S(2)}) collective-permute-start(bf16[128,3584]{1,0:T(8,128)(2,1)S(1)} %collective-permute-done.1.refs_2_), channel_id=1, source_target_pairs={{0,1},{1,0},{2,3},{3,2},{4,5},{5,4},{6,7},{7,6},{8,9},{9,8},{10,11... | collective-permute-start | bytes 2752520 | tf_op jit(solution)/shard_map/ppermute | solution.py:175
  70.2 24.2 %collective-permute-start.4 = (bf16[128,3584]{1,0:T(8,128)(2,1)S(1)}, bf16[128,3584]{1,0:T(8,128)(2,1)S(1)}, u32[]{:S(2)}, u32[]{:S(2)}) collective-permute-start(bf16[128,3584]{1,0:T(8,128)(2,1)S(1)} %collective-permute-done.3.refs_4_), channel_id=1, source_target_pairs={{0,1},{1,0},{2,3},{3,2},{4,5},{5,4},{6,7},{7,6},{8,9},{9,8},{10,11... | collective-permute-start | bytes 2752520 | tf_op jit(solution)/shard_map/ppermute | solution.py:175
  90.3 23.3 %collective-permute-start.5 = (bf16[128,3584]{1,0:T(8,128)(2,1)S(1)}, bf16[128,3584]{1,0:T(8,128)(2,1)S(1)}, u32[]{:S(2)}, u32[]{:S(2)}) collective-permute-start(bf16[128,3584]{1,0:T(8,128)(2,1)S(1)} %collective-permute-done.3.refs_4_), channel_id=1, source_target_pairs={{0,8},{1,9},{2,10},{3,11},{4,12},{5,13},{6,14},{7,15},{8,0},{9,1},... | collective-permute-start | bytes 2752520 | tf_op jit(solution)/shard_map/ppermute | solution.py:169
  91.7 22.6 %collective-permute-start.8 = (bf16[128,3584]{1,0:T(8,128)(2,1)S(1)}, bf16[128,3584]{1,0:T(8,128)(2,1)S(1)}, u32[]{:S(2)}, u32[]{:S(2)}) collective-permute-start(bf16[128,3584]{1,0:T(8,128)(2,1)S(1)} %collective-permute-done.7.refs_8_), channel_id=1, source_target_pairs={{0,1},{1,0},{2,3},{3,2},{4,5},{5,4},{6,7},{7,6},{8,9},{9,8},{10,11... | collective-permute-start | bytes 2752520 | tf_op jit(solution)/shard_map/ppermute | solution.py:175
  91.7 133.5 %copy-start.14 = (bf16[3584,128]{1,0:T(8,128)(2,1)}, bf16[3584,128]{1,0:T(8,128)(2,1)S(1)}, u32[]{:S(2)}) copy-start(bf16[3584,128]{1,0:T(8,128)(2,1)S(1)} %collective-permute-done.18.refs_20_) | copy-start | bytes 2752516
  91.7 41.5 %collective-permute-start.9 = (bf16[128,3584]{1,0:T(8,128)(2,1)S(1)}, bf16[128,3584]{1,0:T(8,128)(2,1)S(1)}, u32[]{:S(2)}, u32[]{:S(2)}) collective-permute-start(bf16[128,3584]{1,0:T(8,128)(2,1)S(1)} %collective-permute-done.7.refs_8_), channel_id=1, source_target_pairs={{0,8},{1,9},{2,10},{3,11},{4,12},{5,13},{6,14},{7,15},{8,0},{9,1},... | collective-permute-start | bytes 2752520 | tf_op jit(solution)/shard_map/ppermute | solution.py:169
  94.3 39.7 %collective-permute-start.12 = (bf16[128,3584]{1,0:T(8,128)(2,1)S(1)}, bf16[128,3584]{1,0:T(8,128)(2,1)S(1)}, u32[]{:S(2)}, u32[]{:S(2)}) collective-permute-start(bf16[128,3584]{1,0:T(8,128)(2,1)S(1)} %collective-permute-done.11.refs_12_), channel_id=1, source_target_pairs={{0,1},{1,0},{2,3},{3,2},{4,5},{5,4},{6,7},{7,6},{8,9},{9,8},{10,11... | collective-permute-start | bytes 2752520 | tf_op jit(solution)/shard_map/ppermute | solution.py:175
  94.4 56.3 %copy-start.9 = (bf16[128,3584]{1,0:T(8,128)(2,1)}, bf16[128,3584]{1,0:T(8,128)(2,1)S(1)}, u32[]{:S(2)}) copy-start(bf16[128,3584]{1,0:T(8,128)(2,1)S(1)} %collective-permute-done.4.refs_5_) | copy-start | bytes 2752516
  94.4 56.3 %collective-permute-start.13 = (bf16[128,3584]{1,0:T(8,128)(2,1)S(1)}, bf16[128,3584]{1,0:T(8,128)(2,1)}, u32[]{:S(2)}, u32[]{:S(2)}) collective-permute-start(bf16[128,3584]{1,0:T(8,128)(2,1)S(1)} %collective-permute-done.11.refs_12_), channel_id=1, source_target_pairs={{0,8},{1,9},{2,10},{3,11},{4,12},{5,13},{6,14},{7,15},{8,0},{9,1},... | collective-permute-start | bytes 2752520 | tf_op jit(solution)/shard_map/ppermute | solution.py:169
  113.6 37.1 %collective-permute-start.19 = (bf16[3584,128]{1,0:T(8,128)(2,1)}, bf16[3584,128]{1,0:T(8,128)(2,1)S(1)}, u32[]{:S(2)}, u32[]{:S(2)}) collective-permute-start(bf16[3584,128]{1,0:T(8,128)(2,1)} %collective-permute-done.15.refs_17_), channel_id=1, source_target_pairs={{8,16},{9,17},{10,18},{11,19},{12,20},{13,21},{14,22},{15,23},{16,... | collective-permute-start | bytes 2752520 | tf_op jit(solution)/shard_map/ppermute | solution.py:170
  114.3 110.8 %copy-start.11 = (bf16[128,3584]{1,0:T(8,128)(2,1)}, bf16[128,3584]{1,0:T(8,128)(2,1)S(1)}, u32[]{:S(2)}) copy-start(bf16[128,3584]{1,0:T(8,128)(2,1)S(1)} %collective-permute-done.8.refs_9_) | copy-start | bytes 2752516
  114.3 37.0 %collective-permute-start.20 = (bf16[3584,128]{1,0:T(8,128)(2,1)}, bf16[3584,128]{1,0:T(8,128)(2,1)S(1)}, u32[]{:S(2)}, u32[]{:S(2)}) collective-permute-start(bf16[3584,128]{1,0:T(8,128)(2,1)} %collective-permute-done.16.refs_18_), channel_id=1, source_target_pairs={{8,16},{9,17},{10,18},{11,19},{12,20},{13,21},{14,22},{15,23},{16,... | collective-permute-start | bytes 2752520 | tf_op jit(solution)/shard_map/ppermute | solution.py:170
  133.3 92.0 %copy-start.12 = (bf16[128,3584]{1,0:T(8,128)(2,1)}, bf16[128,3584]{1,0:T(8,128)(2,1)S(1)}, u32[]{:S(2)}) copy-start(bf16[128,3584]{1,0:T(8,128)(2,1)S(1)} %collective-permute-done.9.refs_10_) | copy-start | bytes 2752516
  133.3 37.8 %collective-permute-start.21 = (bf16[3584,128]{1,0:T(8,128)(2,1)}, bf16[3584,128]{1,0:T(8,128)(2,1)S(1)}, u32[]{:S(2)}, u32[]{:S(2)}) collective-permute-start(bf16[3584,128]{1,0:T(8,128)(2,1)} %collective-permute-done.17.refs_19_), channel_id=1, source_target_pairs={{8,16},{9,17},{10,18},{11,19},{12,20},{13,21},{14,22},{15,23},{16,... | collective-permute-start | bytes 2752520 | tf_op jit(solution)/shard_map/ppermute | solution.py:170
  134.0 91.3 %copy-start.13 = (bf16[128,3584]{1,0:T(8,128)(2,1)}, bf16[128,3584]{1,0:T(8,128)(2,1)S(1)}, u32[]{:S(2)}) copy-start(bf16[128,3584]{1,0:T(8,128)(2,1)S(1)} %collective-permute-done.12.refs_13_) | copy-start | bytes 2752516
  134.0 91.2 %collective-permute-start.6 = (bf16[128,3584]{1,0:T(8,128)(2,1)S(1)}, bf16[128,3584]{1,0:T(8,128)(2,1)S(1)}, u32[]{:S(2)}, u32[]{:S(2)}) collective-permute-start(bf16[128,3584]{1,0:T(8,128)(2,1)S(1)} %collective-permute-done.5.refs_6_), channel_id=1, source_target_pairs={{0,1},{1,0},{2,3},{3,2},{4,5},{5,4},{6,7},{7,6},{8,9},{9,8},{10,11... | collective-permute-start | bytes 2752520 | tf_op jit(solution)/shard_map/ppermute | solution.py:175
  150.7 74.5 %collective-permute-start.10 = (bf16[128,3584]{1,0:T(8,128)(2,1)S(1)}, bf16[128,3584]{1,0:T(8,128)(2,1)S(1)}, u32[]{:S(2)}, u32[]{:S(2)}) collective-permute-start(bf16[128,3584]{1,0:T(8,128)(2,1)S(1)} %collective-permute-done.9.refs_10_), channel_id=1, source_target_pairs={{0,1},{1,0},{2,3},{3,2},{4,5},{5,4},{6,7},{7,6},{8,9},{9,8},{10,11... | collective-permute-start | bytes 2752520 | tf_op jit(solution)/shard_map/ppermute | solution.py:175
  150.7 74.5 %copy-start.17 = (bf16[3584,128]{1,0:T(8,128)(2,1)}, bf16[3584,128]{1,0:T(8,128)(2,1)S(1)}, u32[]{:S(2)}) copy-start(bf16[3584,128]{1,0:T(8,128)(2,1)S(1)} %collective-permute-done.19.refs_21_) | copy-start | bytes 2752516
  150.7 76.6 %collective-permute-start.14 = (bf16[128,3584]{1,0:T(8,128)(2,1)}, bf16[128,3584]{1,0:T(8,128)(2,1)}, u32[]{:S(2)}, u32[]{:S(2)}) collective-permute-start(bf16[128,3584]{1,0:T(8,128)(2,1)} %collective-permute-done.13.refs_14_), channel_id=1, source_target_pairs={{0,1},{1,0},{2,3},{3,2},{4,5},{5,4},{6,7},{7,6},{8,9},{9,8},{10,11... | collective-permute-start | bytes 2752520 | tf_op jit(solution)/shard_map/ppermute | solution.py:175
  151.3 74.0 %copy-start.18 = (bf16[3584,128]{1,0:T(8,128)(2,1)}, bf16[3584,128]{1,0:T(8,128)(2,1)S(1)}, u32[]{:S(2)}) copy-start(bf16[3584,128]{1,0:T(8,128)(2,1)S(1)} %collective-permute-done.20.refs_22_) | copy-start | bytes 2752516
  151.3 93.3 %collective-permute-start.28 = (bf16[3584,128]{1,0:T(8,128)(2,1)}, bf16[3584,128]{1,0:T(8,128)(2,1)}, u32[]{:S(2)}, u32[]{:S(2)}) collective-permute-start(bf16[3584,128]{1,0:T(8,128)(2,1)} %get-tuple-element.43.refs_16_), channel_id=1, source_target_pairs={{8,0},{9,1},{10,2},{11,3},{12,4},{13,5},{14,6},{15,7},{24,8},{25,9... | collective-permute-start | bytes 2752520 | tf_op jit(solution)/shard_map/ppermute | solution.py:171
  171.1 54.2 %copy-start.19 = (bf16[3584,128]{1,0:T(8,128)(2,1)}, bf16[3584,128]{1,0:T(8,128)(2,1)S(1)}, u32[]{:S(2)}) copy-start(bf16[3584,128]{1,0:T(8,128)(2,1)S(1)} %collective-permute-done.21.refs_23_) | copy-start | bytes 2752516
  171.1 75.7 %collective-permute-start.29 = (bf16[3584,128]{1,0:T(8,128)(2,1)}, bf16[3584,128]{1,0:T(8,128)(2,1)}, u32[]{:S(2)}, u32[]{:S(2)}) collective-permute-start(bf16[3584,128]{1,0:T(8,128)(2,1)} %collective-permute-done.15.refs_17_), channel_id=1, source_target_pairs={{8,0},{9,1},{10,2},{11,3},{12,4},{13,5},{14,6},{15,7},{24,8},{25,9... | collective-permute-start | bytes 2752520 | tf_op jit(solution)/shard_map/ppermute | solution.py:171
  225.2 23.1 %collective-permute-start.30 = (bf16[3584,128]{1,0:T(8,128)(2,1)}, bf16[3584,128]{1,0:T(8,128)(2,1)}, u32[]{:S(2)}, u32[]{:S(2)}) collective-permute-start(bf16[3584,128]{1,0:T(8,128)(2,1)} %collective-permute-done.16.refs_18_), channel_id=1, source_target_pairs={{8,0},{9,1},{10,2},{11,3},{12,4},{13,5},{14,6},{15,7},{24,8},{25,9... | collective-permute-start | bytes 2752520 | tf_op jit(solution)/shard_map/ppermute | solution.py:171
  227.1 29.0 %collective-permute-start.31 = (bf16[3584,128]{1,0:T(8,128)(2,1)}, bf16[3584,128]{1,0:T(8,128)(2,1)}, u32[]{:S(2)}, u32[]{:S(2)}) collective-permute-start(bf16[3584,128]{1,0:T(8,128)(2,1)} %collective-permute-done.17.refs_19_), channel_id=1, source_target_pairs={{8,0},{9,1},{10,2},{11,3},{12,4},{13,5},{14,6},{15,7},{24,8},{25,9... | collective-permute-start | bytes 2752520 | tf_op jit(solution)/shard_map/ppermute | solution.py:171
  244.5 28.0 %collective-permute-start.22 = (bf16[4,128,512]{2,1,0:T(8,128)(2,1)S(1)}, bf16[4,128,512]{2,1,0:T(8,128)(2,1)S(1)}, u32[]{:S(2)}, u32[]{:S(2)}) collective-permute-start(bf16[4,128,512]{2,1,0:T(8,128)(2,1)S(1)} %get-tuple-element.22), channel_id=1, source_target_pairs={{0,2},{1,3},{2,0},{3,1},{4,6},{5,7},{6,4},{7,5},{8,10},{9,11},{10,... | collective-permute-start | bytes 1572872 | tf_op jit(solution)/shard_map/ppermute | solution.py:181
  244.6 29.8 %collective-permute-start.23 = (bf16[4,128,512]{2,1,0:T(8,128)(2,1)S(1)}, bf16[4,128,512]{2,1,0:T(8,128)(2,1)S(1)}, u32[]{:S(2)}, u32[]{:S(2)}) collective-permute-start(bf16[4,128,512]{2,1,0:T(8,128)(2,1)S(1)} %get-tuple-element.23), channel_id=1, source_target_pairs={{0,4},{1,5},{2,6},{3,7},{4,0},{5,1},{6,2},{7,3},{8,12},{9,13},{10,... | collective-permute-start | bytes 1572872 | tf_op jit(solution)/shard_map/ppermute | solution.py:181
  246.8 27.7 %collective-permute-start.24 = (bf16[4,128,512]{2,1,0:T(8,128)(2,1)S(1)}, bf16[4,128,512]{2,1,0:T(8,128)(2,1)S(1)}, u32[]{:S(2)}, u32[]{:S(2)}) collective-permute-start(bf16[4,128,512]{2,1,0:T(8,128)(2,1)S(1)} %get-tuple-element.24), channel_id=1, source_target_pairs={{0,6},{1,7},{2,4},{3,5},{4,2},{5,3},{6,0},{7,1},{8,14},{9,15},{10,... | collective-permute-start | bytes 1572872 | tf_op jit(solution)/shard_map/ppermute | solution.py:181
  270.9 10.0 %collective-permute-start.32 = (bf16[4,128,512]{2,1,0:T(8,128)(2,1)S(1)}, bf16[4,128,512]{2,1,0:T(8,128)(2,1)S(1)}, u32[]{:S(2)}, u32[]{:S(2)}) collective-permute-start(bf16[4,128,512]{2,1,0:T(8,128)(2,1)S(1)} %get-tuple-element.30), channel_id=1, source_target_pairs={{0,2},{1,3},{2,0},{3,1},{4,6},{5,7},{6,4},{7,5},{8,10},{9,11},{10,... | collective-permute-start | bytes 1572872 | tf_op jit(solution)/shard_map/ppermute | solution.py:181
  270.9 19.9 %collective-permute-start.33 = (bf16[4,128,512]{2,1,0:T(8,128)(2,1)S(1)}, bf16[4,128,512]{2,1,0:T(8,128)(2,1)S(1)}, u32[]{:S(2)}, u32[]{:S(2)}) collective-permute-start(bf16[4,128,512]{2,1,0:T(8,128)(2,1)S(1)} %get-tuple-element.31), channel_id=1, source_target_pairs={{0,4},{1,5},{2,6},{3,7},{4,0},{5,1},{6,2},{7,3},{8,12},{9,13},{10,... | collective-permute-start | bytes 1572872 | tf_op jit(solution)/shard_map/ppermute | solution.py:181
  272.5 18.4 %collective-permute-start.34 = (bf16[4,128,512]{2,1,0:T(8,128)(2,1)S(1)}, bf16[4,128,512]{2,1,0:T(8,128)(2,1)S(1)}, u32[]{:S(2)}, u32[]{:S(2)}) collective-permute-start(bf16[4,128,512]{2,1,0:T(8,128)(2,1)S(1)} %get-tuple-element.32), channel_id=1, source_target_pairs={{0,6},{1,7},{2,4},{3,5},{4,2},{5,3},{6,0},{7,1},{8,14},{9,15},{10,... | collective-permute-start | bytes 1572872 | tf_op jit(solution)/shard_map/ppermute | solution.py:181
  274.7 18.9 %collective-permute-start.25 = (bf16[128,512]{1,0:T(8,128)(2,1)S(1)}, bf16[128,512]{1,0:T(8,128)(2,1)S(1)}, u32[]{:S(2)}, u32[]{:S(2)}) collective-permute-start(bf16[128,512]{1,0:T(8,128)(2,1)S(1)} %get-tuple-element.26), channel_id=1, source_target_pairs={{0,1},{1,0},{2,3},{3,2},{4,5},{5,4},{6,7},{7,6},{8,9},{9,8},{10,11... | collective-permute-start | bytes 393224 | tf_op jit(solution)/shard_map/ppermute | solution.py:184
  274.8 18.9 %collective-permute-start.26 = (bf16[128,512]{1,0:T(8,128)(2,1)S(1)}, bf16[128,512]{1,0:T(8,128)(2,1)S(1)}, u32[]{:S(2)}, u32[]{:S(2)}) collective-permute-start(bf16[128,512]{1,0:T(8,128)(2,1)S(1)} %get-tuple-element.27), channel_id=1, source_target_pairs={{0,8},{1,9},{2,10},{3,11},{4,12},{5,13},{6,14},{7,15},{8,0},{9,1},... | collective-permute-start | bytes 393224 | tf_op jit(solution)/shard_map/ppermute | solution.py:184
  280.8 12.8 %collective-permute-start.27 = (bf16[128,512]{1,0:T(8,128)(2,1)S(1)}, bf16[128,512]{1,0:T(8,128)(2,1)S(1)}, u32[]{:S(2)}, u32[]{:S(2)}) collective-permute-start(bf16[128,512]{1,0:T(8,128)(2,1)S(1)} %get-tuple-element.28), channel_id=1, source_target_pairs={{0,9},{1,8},{2,11},{3,10},{4,13},{5,12},{6,15},{7,14},{8,1},{9,0},... | collective-permute-start | bytes 393224 | tf_op jit(solution)/shard_map/ppermute | solution.py:184
  291.1 2.6 collective-permute-start.35
  291.2 6.8 %collective-permute-start.36 = (bf16[128,512]{1,0:T(8,128)(2,1)S(1)}, bf16[128,512]{1,0:T(8,128)(2,1)S(1)}, u32[]{:S(2)}, u32[]{:S(2)}) collective-permute-start(bf16[128,512]{1,0:T(8,128)(2,1)S(1)} %get-tuple-element.35), channel_id=1, source_target_pairs={{0,8},{1,9},{2,10},{3,11},{4,12},{5,13},{6,14},{7,15},{8,0},{9,1},... | collective-permute-start | bytes 393224 | tf_op jit(solution)/shard_map/ppermute | solution.py:184
  293.6 6.6 %collective-permute-start.37 = (bf16[128,512]{1,0:T(8,128)(2,1)S(1)}, bf16[128,512]{1,0:T(8,128)(2,1)S(1)}, u32[]{:S(2)}, u32[]{:S(2)}) collective-permute-start(bf16[128,512]{1,0:T(8,128)(2,1)S(1)} %get-tuple-element.36), channel_id=1, source_target_pairs={{0,9},{1,8},{2,11},{3,10},{4,13},{5,12},{6,15},{7,14},{8,1},{9,0},... | collective-permute-start | bytes 393224 | tf_op jit(solution)/shard_map/ppermute | solution.py:184
  (10 other events, 102.0 us)

commit v2 on v1

v2 whole, which is shorter than its diff:
```python
import functools

import jax
import jax.numpy as jnp
from jax import lax
from jax.experimental import pallas as pl
from jax.experimental.pallas import tpu as pltpu
from jax.sharding import PartitionSpec as P

CORE, PLANE, PAIR = 1, 2, 8
LIMIT = 48 * 1024 * 1024
LANES = 128


def flip(n, mask):
    return [(source, source ^ mask) for source in range(n)]


def along_z(n, pairs):
    low = PAIR
    return [(a * low + rest, b * low + rest) for a, b in pairs for rest in range(low)]


def silu_product(gate, up):
    return (jax.nn.silu(gate.astype(jnp.float32)) * up.astype(jnp.float32)).astype(jnp.bfloat16)


def pack_kernel(apart, plane_ref, gate, up, weight, *refs):
    a, w = refs[-2:] if apart else (refs[-1].at[0], refs[-1].at[1])
    hidden = silu_product(gate[...], up[...])
    for tile in range(a.shape[0]):
        a[tile] = hidden[:, tile * LANES : (tile + 1) * LANES]
        w[tile] = weight[pl.ds(tile * LANES, LANES)]


def pack(plane, step, gate, up, weight, apart, after=()):
    rows, columns = gate.shape[0], weight.shape[1]
    tiles = gate.shape[1] // (4 * LANES)
    steps = 4
    share = tiles // steps
    if apart:
        shape = (tiles, rows, LANES)
        out_shape = [jax.ShapeDtypeStruct(shape, jnp.bfloat16)] * 2
        out_specs = [pl.BlockSpec((share, rows, LANES), lambda at, plane: (at, 0, 0))] * 2
    else:
        shape = (2, tiles, rows, LANES)
        out_shape = jax.ShapeDtypeStruct(shape, jnp.bfloat16)
        out_specs = pl.BlockSpec((2, share, rows, LANES), lambda at, plane: (0, at, 0, 0))

    def here(at, plane):
        return (plane[0] ^ step) * steps + at

    across = pl.BlockSpec((rows, share * LANES), lambda at, plane: (0, here(at, plane)))
    down = pl.BlockSpec((share * LANES, columns), lambda at, plane: (here(at, plane), 0))
    return pl.pallas_call(
        functools.partial(pack_kernel, apart),
        out_shape=out_shape,
        grid_spec=pltpu.PrefetchScalarGridSpec(
            num_scalar_prefetch=1,
            grid=(steps,),
            in_specs=[across, across, down] + [pl.BlockSpec(memory_space=pl.ANY)] * len(after),
            out_specs=out_specs,
        ),
        compiler_params=pltpu.CompilerParams(vmem_limit_bytes=LIMIT),
        cost_estimate=pl.CostEstimate(
            flops=0, bytes_accessed=10 * rows * tiles * LANES, transcendentals=rows * tiles * LANES
        ),
        name="pack",
    )(plane, gate, up, weight, *after)


def unpack_kernel(count, *refs):
    sources, (a, w, sem) = refs[:count], refs[-3:]
    copies = []
    for at in range(count):
        for kind, out in enumerate((a, w)):
            to = out if count == 1 else out.at[at]
            copies.append(
                pltpu.make_async_copy(sources[at].at[kind], to, sem.at[2 * at + kind])
            )
    for copy in copies:
        copy.start()
    for copy in copies:
        copy.wait()


def unpack(packed, after):
    count, shape = len(packed), packed[0].shape[1:]
    if count > 1:
        shape = (count,) + shape
    return pl.pallas_call(
        functools.partial(unpack_kernel, count),
        out_shape=[jax.ShapeDtypeStruct(shape, jnp.bfloat16)] * 2,
        in_specs=[pl.BlockSpec(memory_space=pl.ANY)] * (count + len(after)),
        out_specs=[pl.BlockSpec(memory_space=pl.ANY)] * 2,
        scratch_shapes=[pltpu.SemaphoreType.DMA((2 * count,))],
        cost_estimate=pl.CostEstimate(
            flops=0, bytes_accessed=4 * packed[0].size * count, transcendentals=0
        ),
        name="unpack",
    )(*packed, *after)


def hold_kernel(*refs):
    source, out, sem = refs[0], refs[-2], refs[-1]
    copy = pltpu.make_async_copy(source, out, sem)
    copy.start()
    copy.wait()


def hold(array, after):
    return pl.pallas_call(
        hold_kernel,
        out_shape=jax.ShapeDtypeStruct(array.shape, array.dtype),
        in_specs=[pl.BlockSpec(memory_space=pl.ANY)] * (1 + len(after)),
        out_specs=pl.BlockSpec(memory_space=pl.ANY),
        scratch_shapes=[pltpu.SemaphoreType.DMA],
        cost_estimate=pl.CostEstimate(flops=0, bytes_accessed=4 * array.size, transcendentals=0),
        name="hold",
    )(array, *after)


def product_kernel(a_at, w_at, own, mid_ref, *refs):
    groups = len(a_at) // 4
    outs, (a, w, a_sem, w_sem) = refs[-4 - groups : -4], refs[-4:]
    rows = a.shape[1] // len(a_at)
    tiles, _, columns = w.shape
    columns //= 4

    def pick(at):
        ref, index = at
        return refs[ref] if index is None else refs[ref].at[index]

    def w_copy(at, choice):
        return pltpu.make_async_copy(
            pick(w_at[choice][at]), w.at[:, :, pl.ds(at * columns, columns)], w_sem.at[at]
        )

    def a_copy(at):
        return pltpu.make_async_copy(
            pick(a_at[at]), a.at[:, pl.ds(at * rows, rows)], a_sem.at[at]
        )

    for at in range(4):
        if len(w_at) == 1:
            w_copy(at, 0).start()
        else:
            for choice in range(len(w_at)):

                @pl.when(mid_ref[0] == choice)
                def _():
                    w_copy(at, choice).start()

    for at in range(len(a_at)):
        a_copy(at).start()
    for at in range(4):
        w_copy(at, 0).wait()
    for group in range(groups):
        for at in range(4 * group, 4 * group + 4):
            a_copy(at).wait()
        left = jnp.concatenate(
            [a[tile, pl.ds(4 * group * rows, 4 * rows)] for tile in range(tiles)], axis=1
        )
        total = jnp.dot(
            left,
            w[...].reshape(tiles * LANES, 4 * columns),
            preferred_element_type=jnp.float32,
        )
        outs[group][...] = total.reshape(4, rows, 4 * columns).astype(outs[group].dtype)


def product(mid, groups, a_blocks, w_choices, own, after=()):
    arrays = []

    def at(block):
        array, index = block
        for known, other in enumerate(arrays):
            if other is array:
                return known, index
        arrays.append(array)
        return len(arrays) - 1, index

    a_at = [at(block) for group in groups for block in a_blocks[group]]
    w_at = [[at(block) for block in choice] for choice in w_choices]
    tiles, rows, _ = a_blocks[0][0][0].shape
    columns = w_choices[-1][0][0].shape[-1]
    shape = (4, rows, 4 * columns)
    count = len(arrays) + len(after)
    return pl.pallas_call(
        functools.partial(product_kernel, a_at, w_at, own),
        out_shape=[
            jax.ShapeDtypeStruct(shape, jnp.float32 if group == own else jnp.bfloat16)
            for group in groups
        ],
        in_specs=[pl.BlockSpec(memory_space=pltpu.SMEM)]
        + [pl.BlockSpec(memory_space=pl.ANY)] * count,
        out_specs=[pl.BlockSpec(memory_space=pltpu.VMEM)] * len(groups),
        scratch_shapes=[
            pltpu.VMEM((tiles, len(a_at) * rows, LANES), jnp.bfloat16),
            pltpu.VMEM((tiles, LANES, 4 * columns), jnp.bfloat16),
            pltpu.SemaphoreType.DMA((len(a_at),)),
            pltpu.SemaphoreType.DMA((4,)),
        ],
        compiler_params=pltpu.CompilerParams(vmem_limit_bytes=LIMIT),
        cost_estimate=pl.CostEstimate(
            flops=2 * len(a_at) * rows * tiles * LANES * 4 * columns,
            bytes_accessed=2 * tiles * LANES * (len(a_at) * rows + 4 * columns),
            transcendentals=0,
        ),
        name="product",
    )(mid, *arrays, *after)


def add_kernel(own, one, two, three, *outs):
    columns = own.shape[2] // 4
    for piece in range(4):
        for at in range(4):
            here = pl.ds(at * columns, columns)
            total = own[piece, :, here]
            for step, ref in ((1, one), (2, two), (3, three)):
                total += ref[piece, :, pl.ds((at ^ step) * columns, columns)].astype(jnp.float32)
            outs[piece][:, here] = total.astype(jnp.bfloat16)


def add(own, others):
    _, rows, columns = own.shape
    return pl.pallas_call(
        add_kernel,
        out_shape=[jax.ShapeDtypeStruct((rows, columns), jnp.bfloat16)] * 4,
        in_specs=[pl.BlockSpec(memory_space=pltpu.VMEM)] * 4,
        out_specs=[pl.BlockSpec(memory_space=pltpu.VMEM)] * 4,
        compiler_params=pltpu.CompilerParams(vmem_limit_bytes=LIMIT),
        cost_estimate=pl.CostEstimate(
            flops=12 * rows * columns, bytes_accessed=48 * rows * columns, transcendentals=0
        ),
        name="add",
    )(own, *others)


def assemble_kernel(place_ref, *refs):
    pieces, out = refs[:8], refs[8]
    columns = out.shape[1] // 32
    place = place_ref[0]
    for half in range(2):
        for piece in range(4):
            for at in range(4):
                index = ((piece >> 1) << 4) | (half << 3) | (at << 1) | (piece & 1)
                to = pl.multiple_of((place ^ index) * columns, columns)
                out[:, pl.ds(to, columns)] = pieces[4 * half + piece][:, pl.ds(at * columns, columns)]


def assemble(place, pieces):
    rows, columns = pieces[0].shape
    return pl.pallas_call(
        assemble_kernel,
        out_shape=jax.ShapeDtypeStruct((rows, 8 * columns), jnp.bfloat16),
        in_specs=[pl.BlockSpec(memory_space=pltpu.SMEM)]
        + [pl.BlockSpec(memory_space=pltpu.VMEM)] * 8,
        out_specs=pl.BlockSpec(memory_space=pltpu.VMEM),
        compiler_params=pltpu.CompilerParams(vmem_limit_bytes=LIMIT),
        name="assemble",
    )(place, *pieces)


def blocks(gate_pre, up_pre, down_weight):
    n = lax.axis_size("fsdp")
    me = lax.axis_index("fsdp")
    plane = (me // PLANE) % 4
    z_low, z_high = (me // PAIR) % 2, me // (2 * PAIR)
    at_plane = plane.astype(jnp.int32).reshape(1)
    inputs = (gate_pre, up_pre, down_weight)

    def send(array, perm):
        return lax.ppermute(array, "fsdp", perm=perm)

    def to_mid(array):
        return send(array, along_z(n, [(1, 2), (2, 1)]))

    def to_next(array):
        return send(array, along_z(n, [(1, 0), (3, 1), (0, 2), (2, 3)]))

    def to_core(array):
        return send(array, flip(n, CORE))

    def to_pair(array):
        return send(array, flip(n, PAIR))

    a_0, w_0 = pack(at_plane, 0, *inputs, apart=True)
    packed_1 = pack(at_plane, 1, *inputs, apart=False, after=(a_0,))
    packed_2 = pack(at_plane, 2, *inputs, apart=False, after=(packed_1,))
    pair_0, mid_0, next_0 = to_pair(a_0), to_mid(w_0), to_next(w_0)
    got_1 = send(packed_1, flip(n, PLANE))
    got_2 = send(packed_2, flip(n, 2 * PLANE))

    a_12, w_12 = unpack([got_1, got_2], after=(pair_0, mid_0, next_0))
    packed_3 = pack(at_plane, 3, *inputs, apart=False, after=(a_12,))
    pair_12, mid_12 = to_pair(a_12), to_mid(w_12)
    got_3 = send(packed_3, flip(n, 3 * PLANE))
    core_0, core_pair_0 = to_core(a_0), to_core(pair_0)

    a_3, w_3 = unpack([got_3], after=(pair_12, mid_12, core_0, core_pair_0))
    pair_3, mid_3 = to_pair(a_3), to_mid(w_3)
    next_12 = to_next(hold(w_12, after=(a_3,)))
    core_12, core_pair_12 = to_core(a_12), to_core(pair_12)
    core_3, core_pair_3 = to_core(a_3), to_core(pair_3)
    next_3 = to_next(hold(w_3, after=(pair_3,)))

    a_blocks = [
        [(a_0, None), (core_0, None), (pair_0, None), (core_pair_0, None)],
        [(a_12, 0), (core_12, 0), (pair_12, 0), (core_pair_12, 0)],
        [(a_12, 1), (core_12, 1), (pair_12, 1), (core_pair_12, 1)],
        [(a_3, None), (core_3, None), (pair_3, None), (core_pair_3, None)],
    ]
    w_first = [(w_0, None), (w_12, 0), (w_12, 1), (w_3, None)]
    w_mid = [(mid_0, None), (mid_12, 0), (mid_12, 1), (mid_3, None)]
    w_next = [(next_0, None), (next_12, 0), (next_12, 1), (next_3, None)]
    mid = (z_low ^ z_high).astype(jnp.int32).reshape(1)
    pieces = []
    for choices, calls in (([w_first, w_mid], ([3, 1, 2, 0],)), ([w_next], ([3], [1, 2], [0]))):
        totals, last = {}, ()
        for groups in calls:
            outs = product(mid, groups, a_blocks, choices, 0, last)
            totals.update(zip(groups, outs))
            last = (outs[0],)
        others = [send(totals[step], flip(n, step * PLANE)) for step in (1, 2, 3)]
        summed = add(totals[0], others)
        pieces += [summed[0]] + [
            send(summed[piece], flip(n, (piece >> 1) * PAIR + (piece & 1) * CORE))
            for piece in (1, 2, 3)
        ]
    place = (z_low * 16 + z_high * 8 + plane * 2 + me % 2).astype(jnp.int32).reshape(1)
    return assemble(place, pieces)


def shards(gate_pre, up_pre, down_weight):
    hidden = silu_product(gate_pre, up_pre)
    terms = jnp.dot(
        hidden,
        lax.all_gather(down_weight, "fsdp", axis=1, tiled=True),
        preferred_element_type=jnp.float32,
    )
    totals = lax.psum(terms, "tp")
    share = totals.shape[1] // lax.axis_size("tp")
    result = lax.dynamic_slice_in_dim(totals, lax.axis_index("tp") * share, share, 1)
    return result.astype(jnp.bfloat16)


def solution(mesh):
    in_blocks = mesh.shape["tp"] == 1 and mesh.shape["fsdp"] == 4 * PAIR
    return jax.shard_map(
        blocks if in_blocks else shards,
        mesh=mesh,
        in_specs=(P("fsdp", "tp"), P("fsdp", "tp"), P("tp", "fsdp")),
        out_specs=P("fsdp", "tp"),
        check_vma=False,
    )
```

time: 302 us -> 492 us (1.63)
  Pallas kernels: 31.4 us -> 297 us
  waiting for transfers between devices: 154 us -> 87 us
  starting transfers between devices: 104 us -> 96.9 us
    pallas_call x2 -> x12, Pallas kernels: 29.6 us -> 296 us  [the longest x2 169 us: unpack(): pl.pallas_call(functools.partial(unpack_kernel, count), out_shape=[jax.Sh...]
    ppermute x38 -> x30, waiting for transfers between devices: 154 us -> 87 us  [send(): return lax.ppermute(array, 'fsdp', perm=perm)]
    ppermute x38 -> x30, starting transfers between devices: 104 us -> 96.9 us  [send(): return lax.ppermute(array, 'fsdp', perm=perm)]
    unnamed x40 -> x44, local copies, waits for them, and re-layouts: 6.03 us -> 10.4 us
  transfers between devices with their start and end apart: 38 -> 30, of which waited for: 13 -> 7; matrix products, arithmetic and copies ran while one was open for 0% -> 0% of each run, Pallas kernels for 10% -> 59%
where the time goes in v2:
time: 492 us
  Pallas kernels  297 us (60%)
  starting transfers between devices  96.9 us (20%)
  waiting for transfers between devices  87 us (18%)
  local copies, waits for them, and re-layouts  10.4 us (2%)
    pallas_call x2, Pallas kernels, unpack(): pl.pallas_call(functools.partial(unpack_kernel, count), out_shape=[jax.Sh...  169 us
    ppermute x30, starting transfers between devices, send(): return lax.ppermute(array, 'fsdp', perm=perm)  96.9 us
    ppermute x30, waiting for transfers between devices, send(): return lax.ppermute(array, 'fsdp', perm=perm)  87 us
    pallas_call x2, Pallas kernels, hold(): pl.pallas_call(hold_kernel, out_shape=jax.ShapeDtypeStruct(array.shape, a...  85.6 us
    pallas_call x4, Pallas kernels, product(): pl.pallas_call(functools.partial(product_kernel, a_at, w_at, own), out_sh...  28 us
    pallas_call x4, Pallas kernels, pack(): pl.pallas_call(functools.partial(pack_kernel, apart), out_shape=out_shape...  12.9 us
    unnamed x44, local copies, waits for them, and re-layouts  10.4 us
  transfers between devices with their start and end apart: 30, of which 7 were waited for; matrix products, arithmetic and copies ran while one was open for 0% of the time, Pallas kernels for 59%

profile of v2, /device:TPU:0, one launch (start us, length us, event | category | flops | bytes accessed | tf_op | source)
XLA Modules:
  0.0 491.8 jit_solution(11114295602306520484)
XLA Ops:
  0.0 2.0 copy-done
  2.0 3.8 pack.4
  5.8 3.2 pack.5.refs_0_
  9.0 3.0 collective-permute-start
  12.0 2.9 pack.6
  14.9 1.6 collective-permute-start.1
  16.5 1.6 collective-permute-start.2
  18.1 0.7 collective-permute-start.3
  18.8 3.8 collective-permute-start.4
  22.6 17.4 %collective-permute-done.2.refs_2_.refs_10_ = bf16[28,128,128]{2,1,0:T(8,128)(2,1)S(1)} collective-permute-done((bf16[28,128,128]{2,1,0:T(8,128)(2,1)}, bf16[28,128,128]{2,1,0:T(8,128)(2,1)S(1)}, u32[]{:S(2)}, u32[]{:S(2)}) %collective-permute-start.2) | collective-permute-done | bytes 917536 | tf_op jit(solution)/shard_map/ppermute | solution.py:274
  40.0 17.9 %collective-permute-done.4.refs_4_ = bf16[28,128,128]{2,1,0:T(8,128)(2,1)S(1)} collective-permute-done((bf16[28,128,128]{2,1,0:T(8,128)(2,1)S(1)}, bf16[28,128,128]{2,1,0:T(8,128)(2,1)S(1)}, u32[]{:S(2)}, u32[]{:S(2)}) %collective-permute-start.4) | collective-permute-done | bytes 917536 | tf_op jit(solution)/shard_map/ppermute | solution.py:274
  57.9 1.3 copy-done.20
  59.4 112.3 %unpack.2 = (bf16[2,28,128,128]{3,2,1,0:T(8,128)(2,1)}, bf16[2,28,128,128]{3,2,1,0:T(8,128)(2,1)}) custom-call(bf16[2,28,128,128]{3,2,1,0:T(8,128)(2,1)} %copy-done.20, bf16[2,28,128,128]{3,2,1,0:T(8,128)(2,1)} %collective-permute-done.1.refs_1_, bf16[28,128,128]{2,1,0:T(8,128)(2,1)} %copy-done.4, bf16[28,128,128]{2,1,0:T(8,128)(2,1)} %copy-done.21, ...), custom_call_target="tpu_custom_call" | custom-call | bytes 7340032 | tf_op jit(solution)/shard_map/unpack/pallas_call | solution.py:91
  171.8 3.0 pack.7
  174.8 5.1 %collective-permute-start.6 = (bf16[2,28,128,128]{3,2,1,0:T(8,128)(2,1)}, bf16[2,28,128,128]{3,2,1,0:T(8,128)(2,1)}, u32[]{:S(2)}, u32[]{:S(2)}) collective-permute-start(bf16[2,28,128,128]{3,2,1,0:T(8,128)(2,1)} %get-tuple-element.27.refs_0_.refs_4_), channel_id=1, source_target_pairs={{0,8},{1,9},{2,10},{3,11},{4,12},{5,13},{6,14},{7,15},{8,0},{9,1},... | collective-permute-start | bytes 5505032 | tf_op jit(solution)/shard_map/ppermute | solution.py:274
  180.4 2.0 collective-permute-start.7
  182.9 2.4 collective-permute-done.9.refs_4_.refs_11_.refs_3_
  185.3 34.4 %collective-permute-done.5.refs_0_ = bf16[2,28,128,128]{3,2,1,0:T(8,128)(2,1)S(1)} collective-permute-done((bf16[2,28,128,128]{3,2,1,0:T(8,128)(2,1)S(1)}, bf16[2,28,128,128]{3,2,1,0:T(8,128)(2,1)S(1)}, u32[]{:S(2)}, u32[]{:S(2)}) %collective-permute-start.5) | collective-permute-done | bytes 1835040 | tf_op jit(solution)/shard_map/ppermute | solution.py:274
  219.8 1.3 copy-done.18
  221.1 56.7 %unpack.3 = (bf16[28,128,128]{2,1,0:T(8,128)(2,1)}, bf16[28,128,128]{2,1,0:T(8,128)(2,1)}) custom-call(bf16[2,28,128,128]{3,2,1,0:T(8,128)(2,1)} %copy-done.18, bf16[2,28,128,128]{3,2,1,0:T(8,128)(2,1)} %collective-permute-done.6.refs_1_.refs_6_.refs_2_, bf16[2,28,128,128]{3,2,1,0:T(8,128)(2,1)} %collective-permute-done.7.refs_2_.refs_16_, ...), custom_call_target="tpu_custom_call" | custom-call | bytes 3670016 | tf_op jit(solution)/shard_map/unpack/pallas_call | solution.py:91
  277.8 1.2 collective-permute-start.11
  279.5 56.7 %hold.2 = bf16[2,28,128,128]{3,2,1,0:T(8,128)(2,1)} custom-call(bf16[2,28,128,128]{3,2,1,0:T(8,128)(2,1)} %get-tuple-element.28.refs_13_.refs_0_, bf16[28,128,128]{2,1,0:T(8,128)(2,1)} %get-tuple-element.29.refs_0_.refs_1_), custom_call_target="tpu_custom_call" | custom-call | bytes 3670016 | tf_op jit(solution)/shard_map/hold/pallas_call | solution.py:112
  336.2 2.9 collective-permute-start.22
  339.1 1.6 collective-permute-start.15
  340.7 1.0 copy-done.12
  341.7 28.9 %hold.3 = bf16[28,128,128]{2,1,0:T(8,128)(2,1)} custom-call(bf16[28,128,128]{2,1,0:T(8,128)(2,1)} %get-tuple-element.30.refs_14_.refs_0_, bf16[28,128,128]{2,1,0:T(8,128)(2,1)} %copy-done.12), custom_call_target="tpu_custom_call" | custom-call | bytes 1835008 | tf_op jit(solution)/shard_map/hold/pallas_call | solution.py:112
  370.6 0.9 copy-done.15
  371.6 1.0 collective-permute-start.23
  372.6 1.2 copy-done.13
  373.7 1.2 copy-done.16
  374.9 11.8 %product.4 = (bf16[4,128,512]{2,1,0:T(8,128)(2,1)S(1)}, bf16[4,128,512]{2,1,0:T(8,128)(2,1)S(1)}, bf16[4,128,512]{2,1,0:T(8,128)(2,1)S(1)}, f32[4,128,512]{2,1,0:T(8,128)}) custom-call(s32[1]{0:T(128)} %bitcast.1.mid_ref, bf16[28,128,128]{2,1,0:T(8,128)(2,1)S(1)} %copy-done.11, bf16[28,128,128]{2,1,0:T(8,128)(2,1)S(1)} %copy-done.16, ...), custom_call_target="tpu_custom_call" | custom-call | flops 7516192768 | bytes 18350080 | tf_op jit(solution)/shard_map/product/pallas_call | solution.py:189
  386.7 1.6 collective-permute-start.16
  388.3 1.5 collective-permute-start.17
  390.3 8.3 %collective-permute-done.23.refs_6_ = bf16[28,128,128]{2,1,0:T(8,128)(2,1)S(1)} collective-permute-done((bf16[28,128,128]{2,1,0:T(8,128)(2,1)}, bf16[28,128,128]{2,1,0:T(8,128)(2,1)S(1)}, u32[]{:S(2)}, u32[]{:S(2)}) %collective-permute-start.23) | collective-permute-done | bytes 917536 | tf_op jit(solution)/shard_map/ppermute | solution.py:274
  398.5 4.1 product.5.refs_7_
  402.7 7.1 %product.6 = (bf16[4,128,512]{2,1,0:T(8,128)(2,1)S(1)}, bf16[4,128,512]{2,1,0:T(8,128)(2,1)S(1)}) custom-call(s32[1]{0:T(128)} %bitcast.1.mid_ref, bf16[2,28,128,128]{3,2,1,0:T(8,128)(2,1)} %get-tuple-element.27.refs_0_.refs_4_, bf16[2,28,128,128]{3,2,1,0:T(8,128)(2,1)} %collective-permute-done.13.refs_5_.refs_1_, ...), custom_call_target="tpu_custom_call" | custom-call | flops 3758096384 | bytes 11010048 | tf_op jit(solution)/shard_map/product/pallas_call | solution.py:189
  409.8 1.1 collective-permute-start.24
  410.9 1.5 collective-permute-start.25
  412.4 1.0 collective-permute-start.26
  413.7 5.0 %product.7.own = f32[4,128,512]{2,1,0:T(8,128)} custom-call(s32[1]{0:T(128)} %bitcast.1.mid_ref, bf16[28,128,128]{2,1,0:T(8,128)(2,1)} %get-tuple-element.25.refs_0_.refs_8_, bf16[28,128,128]{2,1,0:T(8,128)(2,1)S(1)} %copy-done.8, bf16[28,128,128]{2,1,0:T(8,128)(2,1)S(1)} %copy-done.6, bf16[28,128,128]{2,1,0:T(8,128)(2,1)S(1)} %copy-done.10, ...), custom_call_target="tpu_custom_call" | custom-call | flops 1879048192 | bytes 7340032 | tf_op jit(solution)/shard_map/product/pallas_call | solution.py:189
  418.7 47.2 %collective-permute-start.20 = (bf16[128,512]{1,0:T(8,128)(2,1)S(1)}, bf16[128,512]{1,0:T(8,128)(2,1)S(1)}, u32[]{:S(2)}, u32[]{:S(2)}) collective-permute-start(bf16[128,512]{1,0:T(8,128)(2,1)S(1)} %get-tuple-element.37), channel_id=1, source_target_pairs={{0,8},{1,9},{2,10},{3,11},{4,12},{5,13},{6,14},{7,15},{8,0},{9,1},... | collective-permute-start | bytes 393224 | tf_op jit(solution)/shard_map/ppermute | solution.py:274
  466.0 3.0 collective-permute-start.21
  469.0 1.2 copy-done.3
  470.5 2.3 collective-permute-start.27
  472.8 11.1 %collective-permute-start.28 = (bf16[128,512]{1,0:T(8,128)(2,1)S(1)}, bf16[128,512]{1,0:T(8,128)(2,1)S(1)}, u32[]{:S(2)}, u32[]{:S(2)}) collective-permute-start(bf16[128,512]{1,0:T(8,128)(2,1)S(1)} %get-tuple-element.43), channel_id=1, source_target_pairs={{0,8},{1,9},{2,10},{3,11},{4,12},{5,13},{6,14},{7,15},{8,0},{9,1},... | collective-permute-start | bytes 393224 | tf_op jit(solution)/shard_map/ppermute | solution.py:274
  484.0 4.3 collective-permute-done.28.refs_6_
  488.2 2.3 collective-permute-done.29.refs_7_
  490.5 1.2 assemble.1
  (71 shorter events, 3.0 us)
Async XLA Ops:
  0.0 2.0 copy-start
  5.8 13.0 %copy-start.17 = (bf16[28,128,128]{2,1,0:T(8,128)(2,1)}, bf16[28,128,128]{2,1,0:T(8,128)(2,1)S(1)}, u32[]{:S(2)}) copy-start(bf16[28,128,128]{2,1,0:T(8,128)(2,1)S(1)} %get-tuple-element.26.refs_12_) | copy-start | bytes 2752516
  9.0 48.9 %collective-permute-start = (bf16[2,28,128,128]{3,2,1,0:T(8,128)(2,1)S(1)}, bf16[2,28,128,128]{3,2,1,0:T(8,128)(2,1)S(1)}, u32[]{:S(2)}, u32[]{:S(2)}) collective-permute-start(bf16[2,28,128,128]{3,2,1,0:T(8,128)(2,1)S(1)} %pack.5.refs_0_), channel_id=1, source_target_pairs={{0,2},{1,3},{2,0},{3,1},{4,6},{5,7},{6,4},{7,5},{8,10},{9,11},{10,... | collective-permute-start | bytes 5505032 | tf_op jit(solution)/shard_map/ppermute | solution.py:274
  14.9 44.3 %collective-permute-start.1 = (bf16[2,28,128,128]{3,2,1,0:T(8,128)(2,1)S(1)}, bf16[2,28,128,128]{3,2,1,0:T(8,128)(2,1)}, u32[]{:S(2)}, u32[]{:S(2)}) collective-permute-start(bf16[2,28,128,128]{3,2,1,0:T(8,128)(2,1)S(1)} %pack.6), channel_id=1, source_target_pairs={{0,4},{1,5},{2,6},{3,7},{4,0},{5,1},{6,2},{7,3},{8,12},{9,13},{10,... | collective-permute-start | bytes 5505032 | tf_op jit(solution)/shard_map/ppermute | solution.py:274
  16.5 23.5 %collective-permute-start.2 = (bf16[28,128,128]{2,1,0:T(8,128)(2,1)}, bf16[28,128,128]{2,1,0:T(8,128)(2,1)S(1)}, u32[]{:S(2)}, u32[]{:S(2)}) collective-permute-start(bf16[28,128,128]{2,1,0:T(8,128)(2,1)} %get-tuple-element.25.refs_0_.refs_8_), channel_id=1, source_target_pairs={{0,8},{1,9},{2,10},{3,11},{4,12},{5,13},{6,14},{7,15},{8,0},{9,1},... | collective-permute-start | bytes 2752520 | tf_op jit(solution)/shard_map/ppermute | solution.py:274
  18.1 21.9 %collective-permute-start.3 = (bf16[28,128,128]{2,1,0:T(8,128)(2,1)S(1)}, bf16[28,128,128]{2,1,0:T(8,128)(2,1)S(1)}, u32[]{:S(2)}, u32[]{:S(2)}) collective-permute-start(bf16[28,128,128]{2,1,0:T(8,128)(2,1)S(1)} %get-tuple-element.26.refs_12_), channel_id=1, source_target_pairs={{8,16},{9,17},{10,18},{11,19},{12,20},{13,21},{14,22},{15,23},{16,... | collective-permute-start | bytes 2752520 | tf_op jit(solution)/shard_map/ppermute | solution.py:274
  18.8 39.1 %collective-permute-start.4 = (bf16[28,128,128]{2,1,0:T(8,128)(2,1)S(1)}, bf16[28,128,128]{2,1,0:T(8,128)(2,1)S(1)}, u32[]{:S(2)}, u32[]{:S(2)}) collective-permute-start(bf16[28,128,128]{2,1,0:T(8,128)(2,1)S(1)} %get-tuple-element.26.refs_12_), channel_id=1, source_target_pairs={{8,0},{9,1},{10,2},{11,3},{12,4},{13,5},{14,6},{15,7},{24,8},{25,9... | collective-permute-start | bytes 2752520 | tf_op jit(solution)/shard_map/ppermute | solution.py:274
  40.0 19.2 %copy-start.4 = (bf16[28,128,128]{2,1,0:T(8,128)(2,1)}, bf16[28,128,128]{2,1,0:T(8,128)(2,1)S(1)}, u32[]{:S(2)}) copy-start(bf16[28,128,128]{2,1,0:T(8,128)(2,1)S(1)} %collective-permute-done.2.refs_2_.refs_10_) | copy-start | bytes 2752516
  40.0 142.4 %collective-permute-start.8 = (bf16[28,128,128]{2,1,0:T(8,128)(2,1)}, bf16[28,128,128]{2,1,0:T(8,128)(2,1)S(1)}, u32[]{:S(2)}, u32[]{:S(2)}) collective-permute-start(bf16[28,128,128]{2,1,0:T(8,128)(2,1)} %get-tuple-element.25.refs_0_.refs_8_), channel_id=1, source_target_pairs={{0,1},{1,0},{2,3},{3,2},{4,5},{5,4},{6,7},{7,6},{8,9},{9,8},{10,11... | collective-permute-start | bytes 2752520 | tf_op jit(solution)/shard_map/ppermute | solution.py:274
  40.0 17.9 %copy-start.21 = (bf16[28,128,128]{2,1,0:T(8,128)(2,1)}, bf16[28,128,128]{2,1,0:T(8,128)(2,1)S(1)}, u32[]{:S(2)}) copy-start(bf16[28,128,128]{2,1,0:T(8,128)(2,1)S(1)} %collective-permute-done.3.refs_3_.refs_15_) | copy-start | bytes 2752516
  57.9 1.5 copy-start.1
  57.9 1.3 copy-start.20
  171.7 8.7 %copy-start.19 = (bf16[2,28,128,128]{3,2,1,0:T(8,128)(2,1)S(1)}, bf16[2,28,128,128]{3,2,1,0:T(8,128)(2,1)}, u32[]{:S(2)}) copy-start(bf16[2,28,128,128]{3,2,1,0:T(8,128)(2,1)} %get-tuple-element.28.refs_13_.refs_0_) | copy-start | bytes 5505028
  171.8 10.6 %copy-start.5 = (bf16[28,128,128]{2,1,0:T(8,128)(2,1)S(1)}, bf16[28,128,128]{2,1,0:T(8,128)(2,1)}, u32[]{:S(2)}) copy-start(bf16[28,128,128]{2,1,0:T(8,128)(2,1)} %copy-done.4) | copy-start | bytes 2752516
  174.8 46.2 %collective-permute-start.6 = (bf16[2,28,128,128]{3,2,1,0:T(8,128)(2,1)}, bf16[2,28,128,128]{3,2,1,0:T(8,128)(2,1)}, u32[]{:S(2)}, u32[]{:S(2)}) collective-permute-start(bf16[2,28,128,128]{3,2,1,0:T(8,128)(2,1)} %get-tuple-element.27.refs_0_.refs_4_), channel_id=1, source_target_pairs={{0,8},{1,9},{2,10},{3,11},{4,12},{5,13},{6,14},{7,15},{8,0},{9,1},... | collective-permute-start | bytes 5505032 | tf_op jit(solution)/shard_map/ppermute | solution.py:274
  179.9 39.9 %collective-permute-start.5 = (bf16[2,28,128,128]{3,2,1,0:T(8,128)(2,1)S(1)}, bf16[2,28,128,128]{3,2,1,0:T(8,128)(2,1)S(1)}, u32[]{:S(2)}, u32[]{:S(2)}) collective-permute-start(bf16[2,28,128,128]{3,2,1,0:T(8,128)(2,1)S(1)} %pack.7), channel_id=1, source_target_pairs={{0,6},{1,7},{2,4},{3,5},{4,2},{5,3},{6,0},{7,1},{8,14},{9,15},{10,... | collective-permute-start | bytes 5505032 | tf_op jit(solution)/shard_map/ppermute | solution.py:274
  180.4 40.6 %collective-permute-start.7 = (bf16[2,28,128,128]{3,2,1,0:T(8,128)(2,1)S(1)}, bf16[2,28,128,128]{3,2,1,0:T(8,128)(2,1)}, u32[]{:S(2)}, u32[]{:S(2)}) collective-permute-start(bf16[2,28,128,128]{3,2,1,0:T(8,128)(2,1)S(1)} %copy-done.19), channel_id=1, source_target_pairs={{8,16},{9,17},{10,18},{11,19},{12,20},{13,21},{14,22},{15,23},{16,... | collective-permute-start | bytes 5505032 | tf_op jit(solution)/shard_map/ppermute | solution.py:274
  182.4 2.9 collective-permute-start.9
  182.4 38.6 %copy-start.7 = (bf16[28,128,128]{2,1,0:T(8,128)(2,1)}, bf16[28,128,128]{2,1,0:T(8,128)(2,1)S(1)}, u32[]{:S(2)}) copy-start(bf16[28,128,128]{2,1,0:T(8,128)(2,1)S(1)} %collective-permute-done.8.refs_3_.refs_9_.refs_1_) | copy-start | bytes 2752516
  182.4 156.7 %collective-permute-start.13 = (bf16[2,28,128,128]{3,2,1,0:T(8,128)(2,1)}, bf16[2,28,128,128]{3,2,1,0:T(8,128)(2,1)}, u32[]{:S(2)}, u32[]{:S(2)}) collective-permute-start(bf16[2,28,128,128]{3,2,1,0:T(8,128)(2,1)} %get-tuple-element.27.refs_0_.refs_4_), channel_id=1, source_target_pairs={{0,1},{1,0},{2,3},{3,2},{4,5},{5,4},{6,7},{7,6},{8,9},{9,8},{10,11... | collective-permute-start | bytes 5505032 | tf_op jit(solution)/shard_map/ppermute | solution.py:274
  185.3 35.7 %copy-start.9 = (bf16[28,128,128]{2,1,0:T(8,128)(2,1)}, bf16[28,128,128]{2,1,0:T(8,128)(2,1)S(1)}, u32[]{:S(2)}) copy-start(bf16[28,128,128]{2,1,0:T(8,128)(2,1)S(1)} %collective-permute-done.9.refs_4_.refs_11_.refs_3_) | copy-start | bytes 2752516
  219.8 1.3 copy-start.18
  277.8 62.9 %collective-permute-start.11 = (bf16[28,128,128]{2,1,0:T(8,128)(2,1)}, bf16[28,128,128]{2,1,0:T(8,128)(2,1)S(1)}, u32[]{:S(2)}, u32[]{:S(2)}) collective-permute-start(bf16[28,128,128]{2,1,0:T(8,128)(2,1)} %get-tuple-element.29.refs_0_.refs_1_), channel_id=1, source_target_pairs={{0,8},{1,9},{2,10},{3,11},{4,12},{5,13},{6,14},{7,15},{8,0},{9,1},... | collective-permute-start | bytes 2752520 | tf_op jit(solution)/shard_map/ppermute | solution.py:274
  279.0 93.6 %collective-permute-start.14 = (bf16[2,28,128,128]{3,2,1,0:T(8,128)(2,1)}, bf16[2,28,128,128]{3,2,1,0:T(8,128)(2,1)}, u32[]{:S(2)}, u32[]{:S(2)}) collective-permute-start(bf16[2,28,128,128]{3,2,1,0:T(8,128)(2,1)} %collective-permute-done.6.refs_1_.refs_6_.refs_2_), channel_id=1, source_target_pairs={{0,1},{1,0},{2,3},{3,2},{4,5},{5,4},{6,7},{7,6},{8,9},{9,8},{10,11... | collective-permute-start | bytes 5505032 | tf_op jit(solution)/shard_map/ppermute | solution.py:274
  279.0 91.6 %collective-permute-start.10 = (bf16[28,128,128]{2,1,0:T(8,128)(2,1)}, bf16[28,128,128]{2,1,0:T(8,128)(2,1)S(1)}, u32[]{:S(2)}, u32[]{:S(2)}) collective-permute-start(bf16[28,128,128]{2,1,0:T(8,128)(2,1)} %get-tuple-element.29.refs_0_.refs_1_), channel_id=1, source_target_pairs={{0,1},{1,0},{2,3},{3,2},{4,5},{5,4},{6,7},{7,6},{8,9},{9,8},{10,11... | collective-permute-start | bytes 2752520 | tf_op jit(solution)/shard_map/ppermute | solution.py:274
  336.2 36.4 %copy-start.11 = (bf16[28,128,128]{2,1,0:T(8,128)(2,1)S(1)}, bf16[28,128,128]{2,1,0:T(8,128)(2,1)}, u32[]{:S(2)}) copy-start(bf16[28,128,128]{2,1,0:T(8,128)(2,1)} %get-tuple-element.29.refs_0_.refs_1_) | copy-start | bytes 2752516
  336.2 54.1 %collective-permute-start.22 = (bf16[2,28,128,128]{3,2,1,0:T(8,128)(2,1)}, bf16[2,28,128,128]{3,2,1,0:T(8,128)(2,1)}, u32[]{:S(2)}, u32[]{:S(2)}) collective-permute-start(bf16[2,28,128,128]{3,2,1,0:T(8,128)(2,1)} %hold.2), channel_id=1, source_target_pairs={{8,0},{9,1},{10,2},{11,3},{12,4},{13,5},{14,6},{15,7},{24,8},{25,9... | collective-permute-start | bytes 5505032 | tf_op jit(solution)/shard_map/ppermute | solution.py:274
  339.1 33.5 %collective-permute-start.15 = (bf16[28,128,128]{2,1,0:T(8,128)(2,1)}, bf16[28,128,128]{2,1,0:T(8,128)(2,1)}, u32[]{:S(2)}, u32[]{:S(2)}) collective-permute-start(bf16[28,128,128]{2,1,0:T(8,128)(2,1)} %get-tuple-element.30.refs_14_.refs_0_), channel_id=1, source_target_pairs={{8,16},{9,17},{10,18},{11,19},{12,20},{13,21},{14,22},{15,23},{16,... | collective-permute-start | bytes 2752520 | tf_op jit(solution)/shard_map/ppermute | solution.py:274
  340.7 31.8 %collective-permute-start.12 = (bf16[28,128,128]{2,1,0:T(8,128)(2,1)S(1)}, bf16[28,128,128]{2,1,0:T(8,128)(2,1)}, u32[]{:S(2)}, u32[]{:S(2)}) collective-permute-start(bf16[28,128,128]{2,1,0:T(8,128)(2,1)S(1)} %collective-permute-done.11.refs_2_.refs_1_), channel_id=1, source_target_pairs={{0,1},{1,0},{2,3},{3,2},{4,5},{5,4},{6,7},{7,6},{8,9},{9,8},{10,11... | collective-permute-start | bytes 2752520 | tf_op jit(solution)/shard_map/ppermute | solution.py:274
  371.6 27.0 %collective-permute-start.23 = (bf16[28,128,128]{2,1,0:T(8,128)(2,1)}, bf16[28,128,128]{2,1,0:T(8,128)(2,1)S(1)}, u32[]{:S(2)}, u32[]{:S(2)}) collective-permute-start(bf16[28,128,128]{2,1,0:T(8,128)(2,1)} %hold.3), channel_id=1, source_target_pairs={{8,0},{9,1},{10,2},{11,3},{12,4},{13,5},{14,6},{15,7},{24,8},{25,9... | collective-permute-start | bytes 2752520 | tf_op jit(solution)/shard_map/ppermute | solution.py:274
  374.9 23.6 %copy-start.2 = (bf16[28,128,128]{2,1,0:T(8,128)(2,1)S(1)}, bf16[28,128,128]{2,1,0:T(8,128)(2,1)}, u32[]{:S(2)}) copy-start(bf16[28,128,128]{2,1,0:T(8,128)(2,1)} %copy-done.1) | copy-start | bytes 2752516
  386.7 25.7 %collective-permute-start.16 = (bf16[4,128,512]{2,1,0:T(8,128)(2,1)S(1)}, bf16[4,128,512]{2,1,0:T(8,128)(2,1)S(1)}, u32[]{:S(2)}, u32[]{:S(2)}) collective-permute-start(bf16[4,128,512]{2,1,0:T(8,128)(2,1)S(1)} %get-tuple-element.32), channel_id=1, source_target_pairs={{0,2},{1,3},{2,0},{3,1},{4,6},{5,7},{6,4},{7,5},{8,10},{9,11},{10,... | collective-permute-start | bytes 1572872 | tf_op jit(solution)/shard_map/ppermute | solution.py:274
  388.3 25.1 %collective-permute-start.17 = (bf16[4,128,512]{2,1,0:T(8,128)(2,1)S(1)}, bf16[4,128,512]{2,1,0:T(8,128)(2,1)S(1)}, u32[]{:S(2)}, u32[]{:S(2)}) collective-permute-start(bf16[4,128,512]{2,1,0:T(8,128)(2,1)S(1)} %get-tuple-element.33), channel_id=1, source_target_pairs={{0,4},{1,5},{2,6},{3,7},{4,0},{5,1},{6,2},{7,3},{8,12},{9,13},{10,... | collective-permute-start | bytes 1572872 | tf_op jit(solution)/shard_map/ppermute | solution.py:274
  389.8 23.6 %collective-permute-start.18 = (bf16[4,128,512]{2,1,0:T(8,128)(2,1)S(1)}, bf16[4,128,512]{2,1,0:T(8,128)(2,1)S(1)}, u32[]{:S(2)}, u32[]{:S(2)}) collective-permute-start(bf16[4,128,512]{2,1,0:T(8,128)(2,1)S(1)} %get-tuple-element.34), channel_id=1, source_target_pairs={{0,6},{1,7},{2,4},{3,5},{4,2},{5,3},{6,0},{7,1},{8,14},{9,15},{10,... | collective-permute-start | bytes 1572872 | tf_op jit(solution)/shard_map/ppermute | solution.py:274
  402.7 10.7 %copy-start.14 = (f32[4,128,512]{2,1,0:T(8,128)S(1)}, f32[4,128,512]{2,1,0:T(8,128)}, u32[]{:S(2)}) copy-start(f32[4,128,512]{2,1,0:T(8,128)} %get-tuple-element.31.own) | copy-start | bytes 3145732
  402.7 11.0 %copy-start.10 = (bf16[28,128,128]{2,1,0:T(8,128)(2,1)S(1)}, bf16[28,128,128]{2,1,0:T(8,128)(2,1)}, u32[]{:S(2)}) copy-start(bf16[28,128,128]{2,1,0:T(8,128)(2,1)} %copy-done.9) | copy-start | bytes 2752516
  409.8 3.9 copy-start.6
  409.8 3.9 copy-start.8
  409.8 56.2 %collective-permute-start.24 = (bf16[4,128,512]{2,1,0:T(8,128)(2,1)S(1)}, bf16[4,128,512]{2,1,0:T(8,128)(2,1)S(1)}, u32[]{:S(2)}, u32[]{:S(2)}) collective-permute-start(bf16[4,128,512]{2,1,0:T(8,128)(2,1)S(1)} %get-tuple-element.39.refs_7_), channel_id=1, source_target_pairs={{0,2},{1,3},{2,0},{3,1},{4,6},{5,7},{6,4},{7,5},{8,10},{9,11},{10,... | collective-permute-start | bytes 1572872 | tf_op jit(solution)/shard_map/ppermute | solution.py:274
  410.9 58.1 %collective-permute-start.25 = (bf16[4,128,512]{2,1,0:T(8,128)(2,1)S(1)}, bf16[4,128,512]{2,1,0:T(8,128)(2,1)S(1)}, u32[]{:S(2)}, u32[]{:S(2)}) collective-permute-start(bf16[4,128,512]{2,1,0:T(8,128)(2,1)S(1)} %get-tuple-element.40), channel_id=1, source_target_pairs={{0,4},{1,5},{2,6},{3,7},{4,0},{5,1},{6,2},{7,3},{8,12},{9,13},{10,... | collective-permute-start | bytes 1572872 | tf_op jit(solution)/shard_map/ppermute | solution.py:274
  412.4 56.6 %collective-permute-start.26 = (bf16[4,128,512]{2,1,0:T(8,128)(2,1)S(1)}, bf16[4,128,512]{2,1,0:T(8,128)(2,1)S(1)}, u32[]{:S(2)}, u32[]{:S(2)}) collective-permute-start(bf16[4,128,512]{2,1,0:T(8,128)(2,1)S(1)} %product.5.refs_7_), channel_id=1, source_target_pairs={{0,6},{1,7},{2,4},{3,5},{4,2},{5,3},{6,0},{7,1},{8,14},{9,15},{10,... | collective-permute-start | bytes 1572872 | tf_op jit(solution)/shard_map/ppermute | solution.py:274
  413.6 70.3 %collective-permute-start.19 = (bf16[128,512]{1,0:T(8,128)(2,1)S(1)}, bf16[128,512]{1,0:T(8,128)(2,1)S(1)}, u32[]{:S(2)}, u32[]{:S(2)}) collective-permute-start(bf16[128,512]{1,0:T(8,128)(2,1)S(1)} %get-tuple-element.36), channel_id=1, source_target_pairs={{0,1},{1,0},{2,3},{3,2},{4,5},{5,4},{6,7},{7,6},{8,9},{9,8},{10,11... | collective-permute-start | bytes 393224 | tf_op jit(solution)/shard_map/ppermute | solution.py:274
  418.7 65.2 %collective-permute-start.20 = (bf16[128,512]{1,0:T(8,128)(2,1)S(1)}, bf16[128,512]{1,0:T(8,128)(2,1)S(1)}, u32[]{:S(2)}, u32[]{:S(2)}) collective-permute-start(bf16[128,512]{1,0:T(8,128)(2,1)S(1)} %get-tuple-element.37), channel_id=1, source_target_pairs={{0,8},{1,9},{2,10},{3,11},{4,12},{5,13},{6,14},{7,15},{8,0},{9,1},... | collective-permute-start | bytes 393224 | tf_op jit(solution)/shard_map/ppermute | solution.py:274
  466.0 18.0 %collective-permute-start.21 = (bf16[128,512]{1,0:T(8,128)(2,1)S(1)}, bf16[128,512]{1,0:T(8,128)(2,1)S(1)}, u32[]{:S(2)}, u32[]{:S(2)}) collective-permute-start(bf16[128,512]{1,0:T(8,128)(2,1)S(1)} %get-tuple-element.38), channel_id=1, source_target_pairs={{0,9},{1,8},{2,11},{3,10},{4,13},{5,12},{6,15},{7,14},{8,1},{9,0},... | collective-permute-start | bytes 393224 | tf_op jit(solution)/shard_map/ppermute | solution.py:274
  469.0 1.2 copy-start.3
  470.5 13.5 %collective-permute-start.27 = (bf16[128,512]{1,0:T(8,128)(2,1)S(1)}, bf16[128,512]{1,0:T(8,128)(2,1)S(1)}, u32[]{:S(2)}, u32[]{:S(2)}) collective-permute-start(bf16[128,512]{1,0:T(8,128)(2,1)S(1)} %get-tuple-element.42), channel_id=1, source_target_pairs={{0,1},{1,0},{2,3},{3,2},{4,5},{5,4},{6,7},{7,6},{8,9},{9,8},{10,11... | collective-permute-start | bytes 393224 | tf_op jit(solution)/shard_map/ppermute | solution.py:274
  472.8 15.4 %collective-permute-start.28 = (bf16[128,512]{1,0:T(8,128)(2,1)S(1)}, bf16[128,512]{1,0:T(8,128)(2,1)S(1)}, u32[]{:S(2)}, u32[]{:S(2)}) collective-permute-start(bf16[128,512]{1,0:T(8,128)(2,1)S(1)} %get-tuple-element.43), channel_id=1, source_target_pairs={{0,8},{1,9},{2,10},{3,11},{4,12},{5,13},{6,14},{7,15},{8,0},{9,1},... | collective-permute-start | bytes 393224 | tf_op jit(solution)/shard_map/ppermute | solution.py:274
  483.9 6.6 %collective-permute-start.29 = (bf16[128,512]{1,0:T(8,128)(2,1)S(1)}, bf16[128,512]{1,0:T(8,128)(2,1)S(1)}, u32[]{:S(2)}, u32[]{:S(2)}) collective-permute-start(bf16[128,512]{1,0:T(8,128)(2,1)S(1)} %get-tuple-element.44), channel_id=1, source_target_pairs={{0,9},{1,8},{2,11},{3,10},{4,13},{5,12},{6,15},{7,14},{8,1},{9,0},... | collective-permute-start | bytes 393224 | tf_op jit(solution)/shard_map/ppermute | solution.py:274
  (4 other events, 4.3 us)

commit v3 on v2

v3 whole, which is shorter than its diff:
```python
import functools

import jax
import jax.numpy as jnp
from jax import lax
from jax.experimental import pallas as pl
from jax.experimental.pallas import tpu as pltpu
from jax.sharding import PartitionSpec as P

CORE, PLANE, PAIR = 1, 2, 8
LIMIT = 60 * 1024 * 1024
LANES = 128


def flip(n, mask):
    return [(source, source ^ mask) for source in range(n)]


def along_z(n, pairs):
    low = PAIR
    return [(a * low + rest, b * low + rest) for a, b in pairs for rest in range(low)]


def silu_product(gate, up):
    return (jax.nn.silu(gate.astype(jnp.float32)) * up.astype(jnp.float32)).astype(jnp.bfloat16)


def pack_kernel(apart, count, plane_ref, *refs):
    outs = refs[len(refs) - count - apart :]
    pairs = [(outs[0], outs[1])] if apart else []
    pairs += [(out.at[0], out.at[1]) for out in outs[2 * apart :]]
    for at, (a, w) in enumerate(pairs):
        gate, up, weight = refs[3 * at : 3 * at + 3]
        hidden = silu_product(gate[...], up[...])
        for tile in range(a.shape[0]):
            a[tile] = hidden[:, tile * LANES : (tile + 1) * LANES]
            w[tile] = weight[pl.ds(tile * LANES, LANES)]


def pack(plane, steps, gate, up, weight, after=()):
    rows, columns = gate.shape[0], weight.shape[1]
    tiles = gate.shape[1] // (4 * LANES)
    grid = 4
    share = tiles // grid
    apart = int(steps[0] == 0)
    single = jax.ShapeDtypeStruct((tiles, rows, LANES), jnp.bfloat16)
    double = jax.ShapeDtypeStruct((2, tiles, rows, LANES), jnp.bfloat16)
    single_spec = pl.BlockSpec((share, rows, LANES), lambda at, plane: (at, 0, 0))
    double_spec = pl.BlockSpec((2, share, rows, LANES), lambda at, plane: (0, at, 0, 0))
    others = len(steps) - apart
    in_specs = []
    for step in steps:

        def across(at, plane, step=step):
            return 0, (plane[0] ^ step) * grid + at

        def down(at, plane, step=step):
            return (plane[0] ^ step) * grid + at, 0

        wide = pl.BlockSpec((rows, share * LANES), across)
        in_specs += [wide, wide, pl.BlockSpec((share * LANES, columns), down)]
    in_specs += [pl.BlockSpec(memory_space=pl.ANY)] * len(after)
    return pl.pallas_call(
        functools.partial(pack_kernel, apart, len(steps)),
        out_shape=[single] * (2 * apart) + [double] * others,
        grid_spec=pltpu.PrefetchScalarGridSpec(
            num_scalar_prefetch=1,
            grid=(grid,),
            in_specs=in_specs,
            out_specs=[single_spec] * (2 * apart) + [double_spec] * others,
        ),
        compiler_params=pltpu.CompilerParams(vmem_limit_bytes=LIMIT),
        cost_estimate=pl.CostEstimate(
            flops=0,
            bytes_accessed=10 * rows * tiles * LANES * len(steps),
            transcendentals=rows * tiles * LANES * len(steps),
        ),
        name="pack",
    )(plane, *[gate, up, weight] * len(steps), *after)


def unpack_pair_kernel(one, two, *refs):
    a, w, held, in_sem, out_sem = refs[-5:]
    ways = [
        (source.at[kind], out.at[at])
        for at, source in enumerate((one, two))
        for kind, out in enumerate((a, w))
    ]
    into = [
        pltpu.make_async_copy(source, held.at[at], in_sem.at[at])
        for at, (source, _) in enumerate(ways)
    ]
    out_of = [
        pltpu.make_async_copy(held.at[at], to, out_sem.at[at]) for at, (_, to) in enumerate(ways)
    ]
    for copy in into:
        copy.start()
    for copy_in, copy_out in zip(into, out_of):
        copy_in.wait()
        copy_out.start()
    for copy in out_of:
        copy.wait()


def unpack_pair(one, two, after):
    return pl.pallas_call(
        unpack_pair_kernel,
        out_shape=[jax.ShapeDtypeStruct(one.shape, one.dtype)] * 2,
        in_specs=[pl.BlockSpec(memory_space=pl.ANY)] * (2 + len(after)),
        out_specs=[pl.BlockSpec(memory_space=pl.ANY)] * 2,
        scratch_shapes=[
            pltpu.VMEM((4,) + one.shape[1:], one.dtype),
            pltpu.SemaphoreType.DMA((4,)),
            pltpu.SemaphoreType.DMA((4,)),
        ],
        compiler_params=pltpu.CompilerParams(vmem_limit_bytes=LIMIT),
        cost_estimate=pl.CostEstimate(flops=0, bytes_accessed=8 * one.size, transcendentals=0),
        name="unpack_pair",
    )(one, two, *after)


def reorder_kernel(count, order_ref, packed, w_12, *refs):
    outs, (held, in_sem, out_sem) = refs[-3 - count : -3], refs[-3:]
    into = [
        pltpu.make_async_copy(source, held.at[at], in_sem.at[at])
        for at, source in enumerate((packed.at[0], w_12.at[0], w_12.at[1], packed.at[1]))
    ]
    out_of = [
        pltpu.make_async_copy(held.at[order_ref[at]], out, out_sem.at[at])
        for at, out in enumerate(outs)
    ]
    for copy in into:
        copy.start()
    for copy in into:
        copy.wait()
    for copy in out_of:
        copy.start()
    for copy in out_of:
        copy.wait()


def reorder(order, packed, w_12, after):
    shape, count = packed.shape[1:], order.shape[0]
    return pl.pallas_call(
        functools.partial(reorder_kernel, count),
        out_shape=[jax.ShapeDtypeStruct(shape, packed.dtype)] * count,
        in_specs=[pl.BlockSpec(memory_space=pltpu.SMEM)]
        + [pl.BlockSpec(memory_space=pl.ANY)] * (2 + len(after)),
        out_specs=[pl.BlockSpec(memory_space=pl.ANY)] * count,
        scratch_shapes=[
            pltpu.VMEM((4,) + shape, packed.dtype),
            pltpu.SemaphoreType.DMA((4,)),
            pltpu.SemaphoreType.DMA((count,)),
        ],
        compiler_params=pltpu.CompilerParams(vmem_limit_bytes=LIMIT),
        cost_estimate=pl.CostEstimate(flops=0, bytes_accessed=8 * packed.size, transcendentals=0),
        name="reorder",
    )(order, packed, w_12, *after)


def product_kernel(a_at, w_at, choice_ref, *refs):
    groups = len(a_at) // 4
    outs, (a, w, a_sem, w_sem) = refs[-4 - groups : -4], refs[-4:]
    rows = a.shape[1] // len(a_at)
    wide = len(w_at[0])
    tiles, _, columns = w.shape
    columns //= wide

    def pick(at):
        ref, index = at
        return refs[ref] if index is None else refs[ref].at[index]

    def w_copy(at, choice):
        return pltpu.make_async_copy(
            pick(w_at[choice][at]), w.at[:, :, pl.ds(at * columns, columns)], w_sem.at[at]
        )

    def a_copy(at):
        return pltpu.make_async_copy(
            pick(a_at[at]), a.at[:, pl.ds(at * rows, rows)], a_sem.at[at]
        )

    for at in range(wide):
        for choice in range(len(w_at)):

            @pl.when(choice_ref[0] == choice)
            def _():
                w_copy(at, choice).start()

    for at in range(len(a_at)):
        a_copy(at).start()
    for at in range(wide):
        w_copy(at, 0).wait()
    for group in range(groups):
        for at in range(4 * group, 4 * group + 4):
            a_copy(at).wait()
        left = jnp.concatenate(
            [a[tile, pl.ds(4 * group * rows, 4 * rows)] for tile in range(tiles)], axis=1
        )
        total = jnp.dot(
            left,
            w[...].reshape(tiles * LANES, wide * columns),
            preferred_element_type=jnp.float32,
        )
        outs[group][...] = total.reshape(4, rows, wide * columns).astype(outs[group].dtype)


def product(choice, groups, a_blocks, w_choices, after=()):
    arrays = []

    def at(block):
        array, index = block
        for known, other in enumerate(arrays):
            if other is array:
                return known, index
        arrays.append(array)
        return len(arrays) - 1, index

    a_at = [at(block) for group in groups for block in a_blocks[group]]
    w_at = [[at(block) for block in choice] for choice in w_choices]
    tiles, rows, _ = a_blocks[0][0][0].shape
    columns = w_choices[-1][0][0].shape[-1]
    wide = len(w_choices[0])
    shape = (4, rows, wide * columns)
    count = len(arrays) + len(after)
    return pl.pallas_call(
        functools.partial(product_kernel, a_at, w_at),
        out_shape=[
            jax.ShapeDtypeStruct(shape, jnp.float32 if group == 0 else jnp.bfloat16)
            for group in groups
        ],
        in_specs=[pl.BlockSpec(memory_space=pltpu.SMEM)]
        + [pl.BlockSpec(memory_space=pl.ANY)] * count,
        out_specs=[pl.BlockSpec(memory_space=pltpu.VMEM)] * len(groups),
        scratch_shapes=[
            pltpu.VMEM((tiles, len(a_at) * rows, LANES), jnp.bfloat16),
            pltpu.VMEM((tiles, LANES, wide * columns), jnp.bfloat16),
            pltpu.SemaphoreType.DMA((len(a_at),)),
            pltpu.SemaphoreType.DMA((wide,)),
        ],
        compiler_params=pltpu.CompilerParams(vmem_limit_bytes=LIMIT),
        cost_estimate=pl.CostEstimate(
            flops=2 * len(a_at) * rows * tiles * LANES * wide * columns,
            bytes_accessed=2 * tiles * LANES * (len(a_at) * rows + wide * columns),
            transcendentals=0,
        ),
        name="product",
    )(choice, *arrays, *after)


def add_kernel(relative, own, one, two, three, *refs):
    blocks_wide, outs = own.shape[2] // LANES, refs[-4:]
    for piece in range(4):
        for at in range(blocks_wide):
            here = pl.ds(at * LANES, LANES)
            total = own[piece, :, here]
            for step, ref in ((1, one), (2, two), (3, three)):
                source = at ^ step if relative else at
                total += ref[piece, :, pl.ds(source * LANES, LANES)].astype(jnp.float32)
            outs[piece][:, here] = total.astype(jnp.bfloat16)


def add(own, others, relative, after=()):
    _, rows, columns = own.shape
    return pl.pallas_call(
        functools.partial(add_kernel, relative),
        out_shape=[jax.ShapeDtypeStruct((rows, columns), jnp.bfloat16)] * 4,
        in_specs=[pl.BlockSpec(memory_space=pltpu.VMEM)] * 4
        + [pl.BlockSpec(memory_space=pl.ANY)] * len(after),
        out_specs=[pl.BlockSpec(memory_space=pltpu.VMEM)] * 4,
        compiler_params=pltpu.CompilerParams(vmem_limit_bytes=LIMIT),
        cost_estimate=pl.CostEstimate(
            flops=12 * rows * columns, bytes_accessed=48 * rows * columns, transcendentals=0
        ),
        name="add",
    )(own, *others, *after)


def assemble_kernel(groups, place_ref, *refs):
    out = refs[-1]
    for ref, (fixed, first, relative) in zip(refs, groups):
        place = place_ref[0] if relative else place_ref[1]
        for at in range(ref.shape[1] // LANES):
            index = fixed | ((first + at) << 1)
            to = pl.multiple_of((place ^ index) * LANES, LANES)
            out[:, pl.ds(to, LANES)] = ref[:, pl.ds(at * LANES, LANES)]


def assemble(place, pieces):
    arrays = [piece[0] for piece in pieces]
    rows = arrays[0].shape[0]
    columns = sum(array.shape[1] for array in arrays)
    return pl.pallas_call(
        functools.partial(assemble_kernel, [piece[1:] for piece in pieces]),
        out_shape=jax.ShapeDtypeStruct((rows, columns), jnp.bfloat16),
        in_specs=[pl.BlockSpec(memory_space=pltpu.SMEM)]
        + [pl.BlockSpec(memory_space=pltpu.VMEM)] * len(arrays),
        out_specs=pl.BlockSpec(memory_space=pltpu.VMEM),
        compiler_params=pltpu.CompilerParams(vmem_limit_bytes=LIMIT),
        name="assemble",
    )(place, *arrays)


def blocks(gate_pre, up_pre, down_weight):
    n = lax.axis_size("fsdp")
    me = lax.axis_index("fsdp")
    plane = (me // PLANE) % 4
    z_low, z_high = (me // PAIR) % 2, me // (2 * PAIR)
    at_plane = plane.astype(jnp.int32).reshape(1)
    inputs = (gate_pre, up_pre, down_weight)

    def send(array, perm):
        return lax.ppermute(array, "fsdp", perm=perm)

    def to_mid(array):
        return send(array, along_z(n, [(1, 2), (2, 1)]))

    def to_next(array):
        return send(array, along_z(n, [(1, 0), (3, 1), (0, 2), (2, 3)]))

    def to_core(array):
        return send(array, flip(n, CORE))

    def to_pair(array):
        return send(array, flip(n, PAIR))

    a_0, w_0, packed_1, packed_2 = pack(at_plane, (0, 1, 2), *inputs)
    pair_0, mid_0, next_0 = to_pair(a_0), to_mid(w_0), to_next(w_0)
    got_1 = send(packed_1, flip(n, PLANE))
    got_2 = send(packed_2, flip(n, 2 * PLANE))

    (packed_3,) = pack(at_plane, (3,), *inputs, after=(pair_0,))
    got_3 = send(packed_3, flip(n, 3 * PLANE))
    a_12, w_12 = unpack_pair(got_1, got_2, after=(pair_0, mid_0, next_0))
    pair_12, mid_12 = to_pair(a_12), to_mid(w_12)
    core_0, core_pair_0 = to_core(a_0), to_core(pair_0)

    order = jnp.array([[1, 2, 3], [1, 3, 2], [2, 3, 1], [3, 2, 1]], jnp.int32)[plane]
    known = jnp.array([0, 3], jnp.int32)
    a_3, w_3, ordered_1 = reorder(
        jnp.concatenate([known, order[:1]]), got_3, w_12, after=(core_0, core_pair_0)
    )
    pair_3, mid_3 = to_pair(a_3), to_mid(w_3)
    core_12, core_pair_12 = to_core(a_12), to_core(pair_12)
    ordered_2, ordered_3 = reorder(
        order[1:], got_3, w_12, after=(pair_3, mid_3, core_12, core_pair_12)
    )
    next_1, next_2, next_3 = to_next(ordered_1), to_next(ordered_2), to_next(ordered_3)
    core_3, core_pair_3 = to_core(a_3), to_core(pair_3)

    a_blocks = [
        [(a_0, None), (core_0, None), (pair_0, None), (core_pair_0, None)],
        [(a_12, 0), (core_12, 0), (pair_12, 0), (core_pair_12, 0)],
        [(a_12, 1), (core_12, 1), (pair_12, 1), (core_pair_12, 1)],
        [(a_3, None), (core_3, None), (pair_3, None), (core_pair_3, None)],
    ]
    w_own = [(w_0, None), (w_12, 0), (w_12, 1), (w_3, None)]
    w_mid = [(mid_0, None), (mid_12, 0), (mid_12, 1), (mid_3, None)]
    first, one, two, three = [(block, None) for block in (next_0, next_1, next_2, next_3)]
    w_low = [[first, one], [one, first], [one, two], [one, two]]
    w_high = [[two, three], [two, three], [first, three], [three, first]]
    mid = (z_low ^ z_high).astype(jnp.int32).reshape(1)
    pieces, summing, last = [], [], ()
    for choice, w_choices, calls in (
        (mid, [w_own, w_mid], ([3, 1, 2, 0],)),
        (at_plane, w_low, ([3, 1, 2, 0],)),
        (at_plane, w_high, ([3, 1, 2], [0])),
    ):
        totals = {}
        for groups in calls:
            outs = product(choice, groups, a_blocks, w_choices, last)
            totals.update(zip(groups, outs))
            last = (outs[0],)
        others = [send(totals[step], flip(n, step * PLANE)) for step in (1, 2, 3)]
        summing.append((totals[0], others))
        last = tuple(others)
    for at, (half, start) in enumerate(((0, 0), (1, 0), (1, 2))):
        later = tuple(summing[at + 1][0:1]) if at < 2 else ()
        summed = add(*summing[at], half == 0, later)
        for piece in range(4):
            mask = (piece >> 1) * PAIR + (piece & 1) * CORE
            block = send(summed[piece], flip(n, mask)) if mask else summed[piece]
            fixed = ((piece >> 1) << 4) | (half << 3) | (piece & 1)
            pieces.append((block, fixed, start, half == 0))
    across = z_low * 16 + z_high * 8 + me % 2
    place = jnp.stack([across + plane * 2, across]).astype(jnp.int32)
    return assemble(place, pieces)


def shards(gate_pre, up_pre, down_weight):
    hidden = silu_product(gate_pre, up_pre)
    terms = jnp.dot(
        hidden,
        lax.all_gather(down_weight, "fsdp", axis=1, tiled=True),
        preferred_element_type=jnp.float32,
    )
    totals = lax.psum(terms, "tp")
    share = totals.shape[1] // lax.axis_size("tp")
    result = lax.dynamic_slice_in_dim(totals, lax.axis_index("tp") * share, share, 1)
    return result.astype(jnp.bfloat16)


def solution(mesh):
    in_blocks = mesh.shape["tp"] == 1 and mesh.shape["fsdp"] == 4 * PAIR
    return jax.shard_map(
        blocks if in_blocks else shards,
        mesh=mesh,
        in_specs=(P("fsdp", "tp"), P("fsdp", "tp"), P("tp", "fsdp")),
        out_specs=P("fsdp", "tp"),
        check_vma=False,
    )
```

time: 492 us -> 282 us (0.57)
  Pallas kernels: 297 us -> 74.3 us
  waiting for transfers between devices: 87 us -> 126 us
  starting transfers between devices: 96.9 us -> 73 us
    pallas_call x15 -> x13, Pallas kernels: 297 us -> 74.3 us  [the longest x4 43.3 us: product(): pl.pallas_call(functools.partial(product_kernel, a_at, w_at), out_shape=[...]
    ppermute x30 -> x37, waiting for transfers between devices: 87 us -> 126 us  [send(): return lax.ppermute(array, 'fsdp', perm=perm)]
    ppermute x30 -> x37, starting transfers between devices: 96.9 us -> 73 us  [send(): return lax.ppermute(array, 'fsdp', perm=perm)]
    unnamed x44 -> x54, local copies, waits for them, and re-layouts: 10.4 us -> 5.61 us
  transfers between devices with their start and end apart: 30 -> 37, of which waited for: 7 -> 13; matrix products, arithmetic and copies ran while one was open for 0% -> 1% of each run, Pallas kernels for 59% -> 19%
where the time goes in v3:
time: 282 us
  waiting for transfers between devices  126 us (45%)
  Pallas kernels  74.3 us (26%)
  starting transfers between devices  73 us (26%)
  local copies, waits for them, and re-layouts  6.95 us (2%)
    ppermute x37, waiting for transfers between devices, send(): return lax.ppermute(array, 'fsdp', perm=perm)  126 us
    ppermute x37, starting transfers between devices, send(): return lax.ppermute(array, 'fsdp', perm=perm)  73 us
    pallas_call x4, Pallas kernels, product(): pl.pallas_call(functools.partial(product_kernel, a_at, w_at), out_shape=[...  43.3 us
    pallas_call x2, Pallas kernels, pack(): pl.pallas_call(functools.partial(pack_kernel, apart, len(steps)), out_sha...  10.6 us
    pallas_call x2, Pallas kernels, reorder(): pl.pallas_call(functools.partial(reorder_kernel, count), out_shape=[jax.S...  8.28 us
    pallas_call x3, Pallas kernels, add(): pl.pallas_call(functools.partial(add_kernel, relative), out_shape=[jax.Sh...  6.6 us
  transfers between devices with their start and end apart: 37, of which 13 were waited for; matrix products, arithmetic and copies ran while one was open for 1% of the time, Pallas kernels for 19%

profile of v3, /device:TPU:0, one launch (start us, length us, event | category | flops | bytes accessed | tf_op | source)
XLA Modules:
  0.0 281.8 jit_solution(1039306282655920108)
XLA Ops:
  0.0 6.4 %pack.2 = (bf16[28,128,128]{2,1,0:T(8,128)(2,1)}, bf16[28,128,128]{2,1,0:T(8,128)(2,1)}, bf16[2,28,128,128]{3,2,1,0:T(8,128)(2,1)}, bf16[2,28,128,128]{3,2,1,0:T(8,128)(2,1)}) custom-call(s32[1]{0:T(128)} %bitcast.4.plane_ref.choice_ref, bf16[128,14336]{1,0:T(8,128)(2,1)} %refs_0_.3, bf16[128,14336]{1,0:T(8,128)(2,1)} %refs_1_.3, ...), custom_call_target="tpu_custom_call" | custom-call | bytes 13762560 | tf_op jit(solution)/shard_map/pack/pallas_call | solution.py:63
  6.4 3.0 %collective-permute-start.2 = (bf16[2,28,128,128]{3,2,1,0:T(8,128)(2,1)}, bf16[2,28,128,128]{3,2,1,0:T(8,128)(2,1)S(1)}, u32[]{:S(2)}, u32[]{:S(2)}) collective-permute-start(bf16[2,28,128,128]{3,2,1,0:T(8,128)(2,1)} %get-tuple-element.40), channel_id=1, source_target_pairs={{0,2},{1,3},{2,0},{3,1},{4,6},{5,7},{6,4},{7,5},{8,10},{9,11},{10,... | collective-permute-start | bytes 5505032 | tf_op jit(solution)/shard_map/ppermute | solution.py:313
  9.4 1.5 collective-permute-start.3
  11.0 2.6 collective-permute-start.5
  13.6 0.7 collective-permute-start.4
  14.3 3.4 %collective-permute-start = (bf16[28,128,128]{2,1,0:T(8,128)(2,1)}, bf16[28,128,128]{2,1,0:T(8,128)(2,1)S(1)}, u32[]{:S(2)}, u32[]{:S(2)}) collective-permute-start(bf16[28,128,128]{2,1,0:T(8,128)(2,1)} %get-tuple-element.39.refs_8_.refs_0_), channel_id=1, source_target_pairs={{0,8},{1,9},{2,10},{3,11},{4,12},{5,13},{6,14},{7,15},{8,0},{9,1},... | collective-permute-start | bytes 2752520 | tf_op jit(solution)/shard_map/ppermute | solution.py:313
  17.7 17.1 %collective-permute-done.5.refs_2_.refs_12_.refs_10_.refs_6_ = bf16[28,128,128]{2,1,0:T(8,128)(2,1)S(1)} collective-permute-done((bf16[28,128,128]{2,1,0:T(8,128)(2,1)}, bf16[28,128,128]{2,1,0:T(8,128)(2,1)S(1)}, u32[]{:S(2)}, u32[]{:S(2)}) %collective-permute-start.5) | collective-permute-done | bytes 917536 | tf_op jit(solution)/shard_map/ppermute | solution.py:313
  34.7 17.9 %collective-permute-done.refs_3_.refs_0_.refs_10_.refs_2_ = bf16[28,128,128]{2,1,0:T(8,128)(2,1)S(1)} collective-permute-done((bf16[28,128,128]{2,1,0:T(8,128)(2,1)}, bf16[28,128,128]{2,1,0:T(8,128)(2,1)S(1)}, u32[]{:S(2)}, u32[]{:S(2)}) %collective-permute-start) | collective-permute-done | bytes 917536 | tf_op jit(solution)/shard_map/ppermute | solution.py:313
  52.7 0.9 copy-done.2
  54.2 3.1 %unpack_pair.1 = (bf16[2,28,128,128]{3,2,1,0:T(8,128)(2,1)}, bf16[2,28,128,128]{3,2,1,0:T(8,128)(2,1)}) custom-call(bf16[2,28,128,128]{3,2,1,0:T(8,128)(2,1)} %copy-done.10, bf16[2,28,128,128]{3,2,1,0:T(8,128)(2,1)} %collective-permute-done.3.two, bf16[28,128,128]{2,1,0:T(8,128)(2,1)} %copy-done.2, bf16[28,128,128]{2,1,0:T(8,128)(2,1)} %copy-done.14, ...), custom_call_target="tpu_custom_call" | custom-call | bytes 7340032 | tf_op jit(solution)/shard_map/unpack_pair/pallas_call | solution.py:106
  57.3 3.0 %collective-permute-start.12 = (bf16[2,28,128,128]{3,2,1,0:T(8,128)(2,1)}, bf16[2,28,128,128]{3,2,1,0:T(8,128)(2,1)}, u32[]{:S(2)}, u32[]{:S(2)}) collective-permute-start(bf16[2,28,128,128]{3,2,1,0:T(8,128)(2,1)} %get-tuple-element.45.refs_4_), channel_id=1, source_target_pairs={{0,8},{1,9},{2,10},{3,11},{4,12},{5,13},{6,14},{7,15},{8,0},{9,1},... | collective-permute-start | bytes 5505032 | tf_op jit(solution)/shard_map/ppermute | solution.py:313
  60.2 4.1 %pack.3 = bf16[2,28,128,128]{3,2,1,0:T(8,128)(2,1)} custom-call(s32[1]{0:T(128)} %bitcast.4.plane_ref.choice_ref, bf16[128,14336]{1,0:T(8,128)(2,1)} %refs_0_.3, bf16[128,14336]{1,0:T(8,128)(2,1)} %refs_1_.3, bf16[14336,128]{1,0:T(8,128)(2,1)} %refs_2_.3, bf16[28,128,128]{2,1,0:T(8,128)(2,1)} %copy-done.2), custom_call_target="tpu_custom_call" | custom-call | bytes 4587520 | tf_op jit(solution)/shard_map/pack/pallas_call | solution.py:63
  66.6 34.1 %collective-permute-done.12.refs_6_ = bf16[2,28,128,128]{3,2,1,0:T(8,128)(2,1)} collective-permute-done((bf16[2,28,128,128]{3,2,1,0:T(8,128)(2,1)}, bf16[2,28,128,128]{3,2,1,0:T(8,128)(2,1)}, u32[]{:S(2)}, u32[]{:S(2)}) %collective-permute-start.12) | collective-permute-done | bytes 1835040 | tf_op jit(solution)/shard_map/ppermute | solution.py:313
  100.7 1.9 collective-permute-start.14
  102.6 4.6 %collective-permute-done.1.packed = bf16[2,28,128,128]{3,2,1,0:T(8,128)(2,1)} collective-permute-done((bf16[2,28,128,128]{3,2,1,0:T(8,128)(2,1)}, bf16[2,28,128,128]{3,2,1,0:T(8,128)(2,1)}, u32[]{:S(2)}, u32[]{:S(2)}) %collective-permute-start.1) | collective-permute-done | bytes 1835040 | tf_op jit(solution)/shard_map/ppermute | solution.py:313
  107.2 4.3 %reorder.2 = (bf16[28,128,128]{2,1,0:T(8,128)(2,1)}, bf16[28,128,128]{2,1,0:T(8,128)(2,1)}, bf16[28,128,128]{2,1,0:T(8,128)(2,1)}) custom-call(s32[3]{0:T(128)} %pad_add_fusion.1.order_ref, bf16[2,28,128,128]{3,2,1,0:T(8,128)(2,1)} %collective-permute-done.1.packed, bf16[2,28,128,128]{3,2,1,0:T(8,128)(2,1)} %get-tuple-element.43.w_12.refs_13_, ...), custom_call_target="tpu_custom_call" | custom-call | bytes 7340032 | tf_op jit(solution)/shard_map/reorder/pallas_call | solution.py:144
  111.9 1.6 collective-permute-start.15
  113.5 19.3 %collective-permute-done.9.refs_2_.refs_0_ = bf16[28,128,128]{2,1,0:T(8,128)(2,1)S(1)} collective-permute-done((bf16[28,128,128]{2,1,0:T(8,128)(2,1)}, bf16[28,128,128]{2,1,0:T(8,128)(2,1)S(1)}, u32[]{:S(2)}, u32[]{:S(2)}) %collective-permute-start.9) | collective-permute-done | bytes 917536 | tf_op jit(solution)/shard_map/ppermute | solution.py:313
  133.5 34.2 %collective-permute-start.19 = (bf16[28,128,128]{2,1,0:T(8,128)(2,1)}, bf16[28,128,128]{2,1,0:T(8,128)(2,1)}, u32[]{:S(2)}, u32[]{:S(2)}) collective-permute-start(bf16[28,128,128]{2,1,0:T(8,128)(2,1)} %get-tuple-element.51), channel_id=1, source_target_pairs={{8,0},{9,1},{10,2},{11,3},{12,4},{13,5},{14,6},{15,7},{24,8},{25,9... | collective-permute-start | bytes 2752520 | tf_op jit(solution)/shard_map/ppermute | solution.py:313
  167.8 4.0 %reorder.3 = (bf16[28,128,128]{2,1,0:T(8,128)(2,1)}, bf16[28,128,128]{2,1,0:T(8,128)(2,1)}) custom-call(s32[2]{0:T(128)} %slice_bitcast_fusion.order_ref, bf16[2,28,128,128]{3,2,1,0:T(8,128)(2,1)} %collective-permute-done.1.packed, bf16[2,28,128,128]{3,2,1,0:T(8,128)(2,1)} %get-tuple-element.43.w_12.refs_13_, bf16[28,128,128]{2,1,0:T(8,128)(2,1)} %copy-done.4, ...), custom_call_target="tpu_custom_call" | custom-call | bytes 7340032 | tf_op jit(solution)/shard_map/reorder/pallas_call | solution.py:144
  171.9 15.1 %product.4 = (bf16[4,128,512]{2,1,0:T(8,128)(2,1)}, bf16[4,128,512]{2,1,0:T(8,128)(2,1)}, bf16[4,128,512]{2,1,0:T(8,128)(2,1)}, f32[4,128,512]{2,1,0:T(8,128)}) custom-call(s32[1]{0:T(128)} %bitcast.2.choice_ref, bf16[28,128,128]{2,1,0:T(8,128)(2,1)} %get-tuple-element.44.refs_0_, bf16[28,128,128]{2,1,0:T(8,128)(2,1)} %collective-permute-done.8.refs_1_, ...), custom_call_target="tpu_custom_call" | custom-call | flops 7516192768 | bytes 18350080 | tf_op jit(solution)/shard_map/product/pallas_call | solution.py:226
  188.2 2.4 collective-permute-start.18
  190.6 2.1 collective-permute-start.27
  192.7 9.5 %collective-permute-done.16.refs_15_.one = bf16[4,128,512]{2,1,0:T(8,128)(2,1)S(1)} collective-permute-done((bf16[4,128,512]{2,1,0:T(8,128)(2,1)}, bf16[4,128,512]{2,1,0:T(8,128)(2,1)S(1)}, u32[]{:S(2)}, u32[]{:S(2)}) %collective-permute-start.16) | collective-permute-done | bytes 524320 | tf_op jit(solution)/shard_map/ppermute | solution.py:313
  202.2 9.9 %collective-permute-done.17.refs_16_.two = bf16[4,128,512]{2,1,0:T(8,128)(2,1)S(1)} collective-permute-done((bf16[4,128,512]{2,1,0:T(8,128)(2,1)}, bf16[4,128,512]{2,1,0:T(8,128)(2,1)S(1)}, u32[]{:S(2)}, u32[]{:S(2)}) %collective-permute-start.17) | collective-permute-done | bytes 524320 | tf_op jit(solution)/shard_map/ppermute | solution.py:313
  212.1 0.8 copy-done.8
  213.1 1.0 copy-done.5
  214.1 13.8 %product.5 = (bf16[4,128,256]{2,1,0:T(8,128)(2,1)}, bf16[4,128,256]{2,1,0:T(8,128)(2,1)}, bf16[4,128,256]{2,1,0:T(8,128)(2,1)}, f32[4,128,256]{2,1,0:T(8,128)}) custom-call(s32[1]{0:T(128)} %bitcast.4.plane_ref.choice_ref, bf16[28,128,128]{2,1,0:T(8,128)(2,1)} %get-tuple-element.44.refs_0_, bf16[28,128,128]{2,1,0:T(8,128)(2,1)} %collective-permute-done.8.refs_1_, ...), custom_call_target="tpu_custom_call" | custom-call | flops 3758096384 | bytes 16515072 | tf_op jit(solution)/shard_map/product/pallas_call | solution.py:226
  228.0 1.8 collective-permute-start.24
  229.8 1.1 collective-permute-start.25
  231.5 5.8 %collective-permute-done.24.refs_11_.one = bf16[4,128,256]{2,1,0:T(8,128)(2,1)S(1)} collective-permute-done((bf16[4,128,256]{2,1,0:T(8,128)(2,1)}, bf16[4,128,256]{2,1,0:T(8,128)(2,1)S(1)}, u32[]{:S(2)}, u32[]{:S(2)}) %collective-permute-start.24) | collective-permute-done | bytes 262176 | tf_op jit(solution)/shard_map/ppermute | solution.py:313
  237.3 4.6 %collective-permute-done.25.refs_12_.two = bf16[4,128,256]{2,1,0:T(8,128)(2,1)S(1)} collective-permute-done((bf16[4,128,256]{2,1,0:T(8,128)(2,1)}, bf16[4,128,256]{2,1,0:T(8,128)(2,1)S(1)}, u32[]{:S(2)}, u32[]{:S(2)}) %collective-permute-start.25) | collective-permute-done | bytes 262176 | tf_op jit(solution)/shard_map/ppermute | solution.py:313
  242.6 0.7 copy-done.13
  243.3 9.8 %product.6 = (bf16[4,128,256]{2,1,0:T(8,128)(2,1)}, bf16[4,128,256]{2,1,0:T(8,128)(2,1)}, bf16[4,128,256]{2,1,0:T(8,128)(2,1)}) custom-call(s32[1]{0:T(128)} %bitcast.4.plane_ref.choice_ref, bf16[28,128,128]{2,1,0:T(8,128)(2,1)} %get-tuple-element.44.refs_0_, bf16[28,128,128]{2,1,0:T(8,128)(2,1)} %collective-permute-done.8.refs_1_, ...), custom_call_target="tpu_custom_call" | custom-call | flops 2818572288 | bytes 12845056 | tf_op jit(solution)/shard_map/product/pallas_call | solution.py:226
  253.3 2.5 collective-permute-start.32
  255.8 0.9 collective-permute-start.33
  256.7 2.6 add.39
  259.3 1.7 collective-permute-start.22
  261.1 4.5 %product.7.refs_0_.own = f32[4,128,256]{2,1,0:T(8,128)} custom-call(s32[1]{0:T(128)} %bitcast.4.plane_ref.choice_ref, bf16[28,128,128]{2,1,0:T(8,128)(2,1)} %get-tuple-element.39.refs_8_.refs_0_, bf16[28,128,128]{2,1,0:T(8,128)(2,1)} %collective-permute-done.6.refs_0_.refs_9_.refs_1_, bf16[28,128,128]{2,1,0:T(8,128)(2,1)} %copy-done.2, ...), custom_call_target="tpu_custom_call" | custom-call | flops 939524096 | bytes 5505024 | tf_op jit(solution)/shard_map/product/pallas_call | solution.py:226
  265.7 2.0 add.40
  267.7 1.5 collective-permute-start.28
  269.9 2.0 add.41
  271.9 0.8 collective-permute-start.30
  273.4 0.7 collective-permute-start.35
  274.1 0.7 collective-permute-start.36
  275.4 0.9 collective-permute-done.30.refs_7_
  276.3 2.3 collective-permute-done.35.refs_10_
  279.3 2.5 assemble.1
  (98 shorter events, 9.9 us)
Async XLA Ops:
  6.4 46.2 %collective-permute-start.2 = (bf16[2,28,128,128]{3,2,1,0:T(8,128)(2,1)}, bf16[2,28,128,128]{3,2,1,0:T(8,128)(2,1)S(1)}, u32[]{:S(2)}, u32[]{:S(2)}) collective-permute-start(bf16[2,28,128,128]{3,2,1,0:T(8,128)(2,1)} %get-tuple-element.40), channel_id=1, source_target_pairs={{0,2},{1,3},{2,0},{3,1},{4,6},{5,7},{6,4},{7,5},{8,10},{9,11},{10,... | collective-permute-start | bytes 5505032 | tf_op jit(solution)/shard_map/ppermute | solution.py:313
  9.4 43.2 %collective-permute-start.3 = (bf16[2,28,128,128]{3,2,1,0:T(8,128)(2,1)}, bf16[2,28,128,128]{3,2,1,0:T(8,128)(2,1)}, u32[]{:S(2)}, u32[]{:S(2)}) collective-permute-start(bf16[2,28,128,128]{3,2,1,0:T(8,128)(2,1)} %get-tuple-element.41), channel_id=1, source_target_pairs={{0,4},{1,5},{2,6},{3,7},{4,0},{5,1},{6,2},{7,3},{8,12},{9,13},{10,... | collective-permute-start | bytes 5505032 | tf_op jit(solution)/shard_map/ppermute | solution.py:313
  11.0 23.8 %collective-permute-start.5 = (bf16[28,128,128]{2,1,0:T(8,128)(2,1)}, bf16[28,128,128]{2,1,0:T(8,128)(2,1)S(1)}, u32[]{:S(2)}, u32[]{:S(2)}) collective-permute-start(bf16[28,128,128]{2,1,0:T(8,128)(2,1)} %get-tuple-element.42.refs_12_), channel_id=1, source_target_pairs={{8,0},{9,1},{10,2},{11,3},{12,4},{13,5},{14,6},{15,7},{24,8},{25,9... | collective-permute-start | bytes 2752520 | tf_op jit(solution)/shard_map/ppermute | solution.py:313
  13.6 21.2 %collective-permute-start.4 = (bf16[28,128,128]{2,1,0:T(8,128)(2,1)}, bf16[28,128,128]{2,1,0:T(8,128)(2,1)S(1)}, u32[]{:S(2)}, u32[]{:S(2)}) collective-permute-start(bf16[28,128,128]{2,1,0:T(8,128)(2,1)} %get-tuple-element.42.refs_12_), channel_id=1, source_target_pairs={{8,16},{9,17},{10,18},{11,19},{12,20},{13,21},{14,22},{15,23},{16,... | collective-permute-start | bytes 2752520 | tf_op jit(solution)/shard_map/ppermute | solution.py:313
  14.3 38.4 %collective-permute-start = (bf16[28,128,128]{2,1,0:T(8,128)(2,1)}, bf16[28,128,128]{2,1,0:T(8,128)(2,1)S(1)}, u32[]{:S(2)}, u32[]{:S(2)}) collective-permute-start(bf16[28,128,128]{2,1,0:T(8,128)(2,1)} %get-tuple-element.39.refs_8_.refs_0_), channel_id=1, source_target_pairs={{0,8},{1,9},{2,10},{3,11},{4,12},{5,13},{6,14},{7,15},{8,0},{9,1},... | collective-permute-start | bytes 2752520 | tf_op jit(solution)/shard_map/ppermute | solution.py:313
  34.7 17.9 %copy-start.1 = (bf16[28,128,128]{2,1,0:T(8,128)(2,1)}, bf16[28,128,128]{2,1,0:T(8,128)(2,1)S(1)}, u32[]{:S(2)}) copy-start(bf16[28,128,128]{2,1,0:T(8,128)(2,1)S(1)} %collective-permute-done.5.refs_2_.refs_12_.refs_10_.refs_6_) | copy-start | bytes 2752516
  34.7 17.9 %copy-start.14 = (bf16[28,128,128]{2,1,0:T(8,128)(2,1)}, bf16[28,128,128]{2,1,0:T(8,128)(2,1)S(1)}, u32[]{:S(2)}) copy-start(bf16[28,128,128]{2,1,0:T(8,128)(2,1)S(1)} %collective-permute-done.4.refs_1_.refs_15_) | copy-start | bytes 2752516
  57.3 7.6 %copy-start.3 = (bf16[28,128,128]{2,1,0:T(8,128)(2,1)S(1)}, bf16[28,128,128]{2,1,0:T(8,128)(2,1)}, u32[]{:S(2)}) copy-start(bf16[28,128,128]{2,1,0:T(8,128)(2,1)} %copy-done.2) | copy-start | bytes 2752516
  57.3 43.5 %collective-permute-start.12 = (bf16[2,28,128,128]{3,2,1,0:T(8,128)(2,1)}, bf16[2,28,128,128]{3,2,1,0:T(8,128)(2,1)}, u32[]{:S(2)}, u32[]{:S(2)}) collective-permute-start(bf16[2,28,128,128]{3,2,1,0:T(8,128)(2,1)} %get-tuple-element.45.refs_4_), channel_id=1, source_target_pairs={{0,8},{1,9},{2,10},{3,11},{4,12},{5,13},{6,14},{7,15},{8,0},{9,1},... | collective-permute-start | bytes 5505032 | tf_op jit(solution)/shard_map/ppermute | solution.py:313
  64.3 42.9 %collective-permute-start.1 = (bf16[2,28,128,128]{3,2,1,0:T(8,128)(2,1)}, bf16[2,28,128,128]{3,2,1,0:T(8,128)(2,1)}, u32[]{:S(2)}, u32[]{:S(2)}) collective-permute-start(bf16[2,28,128,128]{3,2,1,0:T(8,128)(2,1)} %pack.3), channel_id=1, source_target_pairs={{0,6},{1,7},{2,4},{3,5},{4,2},{5,3},{6,0},{7,1},{8,14},{9,15},{10,... | collective-permute-start | bytes 5505032 | tf_op jit(solution)/shard_map/ppermute | solution.py:313
  64.8 35.9 %collective-permute-start.6 = (bf16[28,128,128]{2,1,0:T(8,128)(2,1)}, bf16[28,128,128]{2,1,0:T(8,128)(2,1)}, u32[]{:S(2)}, u32[]{:S(2)}) collective-permute-start(bf16[28,128,128]{2,1,0:T(8,128)(2,1)} %get-tuple-element.39.refs_8_.refs_0_), channel_id=1, source_target_pairs={{0,1},{1,0},{2,3},{3,2},{4,5},{5,4},{6,7},{7,6},{8,9},{9,8},{10,11... | collective-permute-start | bytes 2752520 | tf_op jit(solution)/shard_map/ppermute | solution.py:313
  64.8 37.8 %collective-permute-start.7 = (bf16[28,128,128]{2,1,0:T(8,128)(2,1)S(1)}, bf16[28,128,128]{2,1,0:T(8,128)(2,1)}, u32[]{:S(2)}, u32[]{:S(2)}) collective-permute-start(bf16[28,128,128]{2,1,0:T(8,128)(2,1)S(1)} %copy-done.3), channel_id=1, source_target_pairs={{0,1},{1,0},{2,3},{3,2},{4,5},{5,4},{6,7},{7,6},{8,9},{9,8},{10,11... | collective-permute-start | bytes 2752520 | tf_op jit(solution)/shard_map/ppermute | solution.py:313
  65.3 48.2 %collective-permute-start.11 = (bf16[2,28,128,128]{3,2,1,0:T(8,128)(2,1)}, bf16[2,28,128,128]{3,2,1,0:T(8,128)(2,1)S(1)}, u32[]{:S(2)}, u32[]{:S(2)}) collective-permute-start(bf16[2,28,128,128]{3,2,1,0:T(8,128)(2,1)} %get-tuple-element.45.refs_4_), channel_id=1, source_target_pairs={{0,1},{1,0},{2,3},{3,2},{4,5},{5,4},{6,7},{7,6},{8,9},{9,8},{10,11... | collective-permute-start | bytes 5505032 | tf_op jit(solution)/shard_map/ppermute | solution.py:313
  100.7 67.0 %collective-permute-start.13 = (bf16[2,28,128,128]{3,2,1,0:T(8,128)(2,1)}, bf16[2,28,128,128]{3,2,1,0:T(8,128)(2,1)}, u32[]{:S(2)}, u32[]{:S(2)}) collective-permute-start(bf16[2,28,128,128]{3,2,1,0:T(8,128)(2,1)} %collective-permute-done.12.refs_6_), channel_id=1, source_target_pairs={{0,1},{1,0},{2,3},{3,2},{4,5},{5,4},{6,7},{7,6},{8,9},{9,8},{10,11... | collective-permute-start | bytes 5505032 | tf_op jit(solution)/shard_map/ppermute | solution.py:313
  100.7 71.1 %collective-permute-start.14 = (bf16[2,28,128,128]{3,2,1,0:T(8,128)(2,1)}, bf16[2,28,128,128]{3,2,1,0:T(8,128)(2,1)}, u32[]{:S(2)}, u32[]{:S(2)}) collective-permute-start(bf16[2,28,128,128]{3,2,1,0:T(8,128)(2,1)} %get-tuple-element.43.w_12.refs_13_), channel_id=1, source_target_pairs={{8,16},{9,17},{10,18},{11,19},{12,20},{13,21},{14,22},{15,23},{16,... | collective-permute-start | bytes 5505032 | tf_op jit(solution)/shard_map/ppermute | solution.py:313
  111.5 21.4 %collective-permute-start.9 = (bf16[28,128,128]{2,1,0:T(8,128)(2,1)}, bf16[28,128,128]{2,1,0:T(8,128)(2,1)S(1)}, u32[]{:S(2)}, u32[]{:S(2)}) collective-permute-start(bf16[28,128,128]{2,1,0:T(8,128)(2,1)} %get-tuple-element.44.refs_0_), channel_id=1, source_target_pairs={{0,8},{1,9},{2,10},{3,11},{4,12},{5,13},{6,14},{7,15},{8,0},{9,1},... | collective-permute-start | bytes 2752520 | tf_op jit(solution)/shard_map/ppermute | solution.py:313
  111.9 21.6 %collective-permute-start.15 = (bf16[28,128,128]{2,1,0:T(8,128)(2,1)}, bf16[28,128,128]{2,1,0:T(8,128)(2,1)}, u32[]{:S(2)}, u32[]{:S(2)}) collective-permute-start(bf16[28,128,128]{2,1,0:T(8,128)(2,1)} %get-tuple-element.46.refs_14_), channel_id=1, source_target_pairs={{8,16},{9,17},{10,18},{11,19},{12,20},{13,21},{14,22},{15,23},{16,... | collective-permute-start | bytes 2752520 | tf_op jit(solution)/shard_map/ppermute | solution.py:313
  113.5 54.3 %copy-start = (bf16[2,28,128,128]{3,2,1,0:T(8,128)(2,1)}, bf16[2,28,128,128]{3,2,1,0:T(8,128)(2,1)S(1)}, u32[]{:S(2)}) copy-start(bf16[2,28,128,128]{3,2,1,0:T(8,128)(2,1)S(1)} %collective-permute-done.11.refs_5_.refs_2_) | copy-start | bytes 5505028
  113.5 58.4 %collective-permute-start.8 = (bf16[28,128,128]{2,1,0:T(8,128)(2,1)}, bf16[28,128,128]{2,1,0:T(8,128)(2,1)}, u32[]{:S(2)}, u32[]{:S(2)}) collective-permute-start(bf16[28,128,128]{2,1,0:T(8,128)(2,1)} %get-tuple-element.44.refs_0_), channel_id=1, source_target_pairs={{0,1},{1,0},{2,3},{3,2},{4,5},{5,4},{6,7},{7,6},{8,9},{9,8},{10,11... | collective-permute-start | bytes 2752520 | tf_op jit(solution)/shard_map/ppermute | solution.py:313
  132.9 34.9 %copy-start.4 = (bf16[28,128,128]{2,1,0:T(8,128)(2,1)}, bf16[28,128,128]{2,1,0:T(8,128)(2,1)S(1)}, u32[]{:S(2)}) copy-start(bf16[28,128,128]{2,1,0:T(8,128)(2,1)S(1)} %collective-permute-done.9.refs_2_.refs_0_) | copy-start | bytes 2752516
  132.9 39.0 %collective-permute-start.10 = (bf16[28,128,128]{2,1,0:T(8,128)(2,1)S(1)}, bf16[28,128,128]{2,1,0:T(8,128)(2,1)}, u32[]{:S(2)}, u32[]{:S(2)}) collective-permute-start(bf16[28,128,128]{2,1,0:T(8,128)(2,1)S(1)} %collective-permute-done.9.refs_2_.refs_0_), channel_id=1, source_target_pairs={{0,1},{1,0},{2,3},{3,2},{4,5},{5,4},{6,7},{7,6},{8,9},{9,8},{10,11... | collective-permute-start | bytes 2752520 | tf_op jit(solution)/shard_map/ppermute | solution.py:313
  133.5 57.1 %collective-permute-start.19 = (bf16[28,128,128]{2,1,0:T(8,128)(2,1)}, bf16[28,128,128]{2,1,0:T(8,128)(2,1)}, u32[]{:S(2)}, u32[]{:S(2)}) collective-permute-start(bf16[28,128,128]{2,1,0:T(8,128)(2,1)} %get-tuple-element.51), channel_id=1, source_target_pairs={{8,0},{9,1},{10,2},{11,3},{12,4},{13,5},{14,6},{15,7},{24,8},{25,9... | collective-permute-start | bytes 2752520 | tf_op jit(solution)/shard_map/ppermute | solution.py:313
  171.8 40.3 %collective-permute-start.20 = (bf16[28,128,128]{2,1,0:T(8,128)(2,1)}, bf16[28,128,128]{2,1,0:T(8,128)(2,1)S(1)}, u32[]{:S(2)}, u32[]{:S(2)}) collective-permute-start(bf16[28,128,128]{2,1,0:T(8,128)(2,1)} %get-tuple-element.52), channel_id=1, source_target_pairs={{8,0},{9,1},{10,2},{11,3},{12,4},{13,5},{14,6},{15,7},{24,8},{25,9... | collective-permute-start | bytes 2752520 | tf_op jit(solution)/shard_map/ppermute | solution.py:313
  187.1 15.1 %collective-permute-start.16 = (bf16[4,128,512]{2,1,0:T(8,128)(2,1)}, bf16[4,128,512]{2,1,0:T(8,128)(2,1)S(1)}, u32[]{:S(2)}, u32[]{:S(2)}) collective-permute-start(bf16[4,128,512]{2,1,0:T(8,128)(2,1)} %get-tuple-element.48), channel_id=1, source_target_pairs={{0,2},{1,3},{2,0},{3,1},{4,6},{5,7},{6,4},{7,5},{8,10},{9,11},{10,... | collective-permute-start | bytes 1572872 | tf_op jit(solution)/shard_map/ppermute | solution.py:313
  187.7 24.4 %collective-permute-start.17 = (bf16[4,128,512]{2,1,0:T(8,128)(2,1)}, bf16[4,128,512]{2,1,0:T(8,128)(2,1)S(1)}, u32[]{:S(2)}, u32[]{:S(2)}) collective-permute-start(bf16[4,128,512]{2,1,0:T(8,128)(2,1)} %get-tuple-element.49), channel_id=1, source_target_pairs={{0,4},{1,5},{2,6},{3,7},{4,0},{5,1},{6,2},{7,3},{8,12},{9,13},{10,... | collective-permute-start | bytes 1572872 | tf_op jit(solution)/shard_map/ppermute | solution.py:313
  188.2 23.9 %collective-permute-start.18 = (bf16[4,128,512]{2,1,0:T(8,128)(2,1)}, bf16[4,128,512]{2,1,0:T(8,128)(2,1)S(1)}, u32[]{:S(2)}, u32[]{:S(2)}) collective-permute-start(bf16[4,128,512]{2,1,0:T(8,128)(2,1)} %get-tuple-element.50), channel_id=1, source_target_pairs={{0,6},{1,7},{2,4},{3,5},{4,2},{5,3},{6,0},{7,1},{8,14},{9,15},{10,... | collective-permute-start | bytes 1572872 | tf_op jit(solution)/shard_map/ppermute | solution.py:313
  190.6 40.9 %collective-permute-start.27 = (bf16[28,128,128]{2,1,0:T(8,128)(2,1)}, bf16[28,128,128]{2,1,0:T(8,128)(2,1)S(1)}, u32[]{:S(2)}, u32[]{:S(2)}) collective-permute-start(bf16[28,128,128]{2,1,0:T(8,128)(2,1)} %get-tuple-element.61), channel_id=1, source_target_pairs={{8,0},{9,1},{10,2},{11,3},{12,4},{13,5},{14,6},{15,7},{24,8},{25,9... | collective-permute-start | bytes 2752520 | tf_op jit(solution)/shard_map/ppermute | solution.py:313
  202.2 9.9 %copy-start.7 = (bf16[4,128,512]{2,1,0:T(8,128)(2,1)}, bf16[4,128,512]{2,1,0:T(8,128)(2,1)S(1)}, u32[]{:S(2)}) copy-start(bf16[4,128,512]{2,1,0:T(8,128)(2,1)S(1)} %collective-permute-done.16.refs_15_.one) | copy-start | bytes 1572868
  228.0 9.3 %collective-permute-start.24 = (bf16[4,128,256]{2,1,0:T(8,128)(2,1)}, bf16[4,128,256]{2,1,0:T(8,128)(2,1)S(1)}, u32[]{:S(2)}, u32[]{:S(2)}) collective-permute-start(bf16[4,128,256]{2,1,0:T(8,128)(2,1)} %get-tuple-element.58), channel_id=1, source_target_pairs={{0,2},{1,3},{2,0},{3,1},{4,6},{5,7},{6,4},{7,5},{8,10},{9,11},{10,... | collective-permute-start | bytes 786440 | tf_op jit(solution)/shard_map/ppermute | solution.py:313
  229.8 12.1 %collective-permute-start.25 = (bf16[4,128,256]{2,1,0:T(8,128)(2,1)}, bf16[4,128,256]{2,1,0:T(8,128)(2,1)S(1)}, u32[]{:S(2)}, u32[]{:S(2)}) collective-permute-start(bf16[4,128,256]{2,1,0:T(8,128)(2,1)} %get-tuple-element.59), channel_id=1, source_target_pairs={{0,4},{1,5},{2,6},{3,7},{4,0},{5,1},{6,2},{7,3},{8,12},{9,13},{10,... | collective-permute-start | bytes 786440 | tf_op jit(solution)/shard_map/ppermute | solution.py:313
  230.9 11.0 %collective-permute-start.26 = (bf16[4,128,256]{2,1,0:T(8,128)(2,1)}, bf16[4,128,256]{2,1,0:T(8,128)(2,1)S(1)}, u32[]{:S(2)}, u32[]{:S(2)}) collective-permute-start(bf16[4,128,256]{2,1,0:T(8,128)(2,1)} %get-tuple-element.60), channel_id=1, source_target_pairs={{0,6},{1,7},{2,4},{3,5},{4,2},{5,3},{6,0},{7,1},{8,14},{9,15},{10,... | collective-permute-start | bytes 786440 | tf_op jit(solution)/shard_map/ppermute | solution.py:313
  231.5 10.4 %copy-start.6 = (bf16[28,128,128]{2,1,0:T(8,128)(2,1)}, bf16[28,128,128]{2,1,0:T(8,128)(2,1)S(1)}, u32[]{:S(2)}) copy-start(bf16[28,128,128]{2,1,0:T(8,128)(2,1)S(1)} %collective-permute-done.27.refs_9_.refs_5_) | copy-start | bytes 2752516
  253.1 7.9 %collective-permute-start.31 = (bf16[4,128,256]{2,1,0:T(8,128)(2,1)}, bf16[4,128,256]{2,1,0:T(8,128)(2,1)S(1)}, u32[]{:S(2)}, u32[]{:S(2)}) collective-permute-start(bf16[4,128,256]{2,1,0:T(8,128)(2,1)} %get-tuple-element.67), channel_id=1, source_target_pairs={{0,2},{1,3},{2,0},{3,1},{4,6},{5,7},{6,4},{7,5},{8,10},{9,11},{10,... | collective-permute-start | bytes 786440 | tf_op jit(solution)/shard_map/ppermute | solution.py:313
  253.3 14.4 %collective-permute-start.32 = (bf16[4,128,256]{2,1,0:T(8,128)(2,1)}, bf16[4,128,256]{2,1,0:T(8,128)(2,1)S(1)}, u32[]{:S(2)}, u32[]{:S(2)}) collective-permute-start(bf16[4,128,256]{2,1,0:T(8,128)(2,1)} %get-tuple-element.68), channel_id=1, source_target_pairs={{0,4},{1,5},{2,6},{3,7},{4,0},{5,1},{6,2},{7,3},{8,12},{9,13},{10,... | collective-permute-start | bytes 786440 | tf_op jit(solution)/shard_map/ppermute | solution.py:313
  255.8 13.3 %collective-permute-start.33 = (bf16[4,128,256]{2,1,0:T(8,128)(2,1)}, bf16[4,128,256]{2,1,0:T(8,128)(2,1)S(1)}, u32[]{:S(2)}, u32[]{:S(2)}) collective-permute-start(bf16[4,128,256]{2,1,0:T(8,128)(2,1)} %get-tuple-element.62.refs_7_), channel_id=1, source_target_pairs={{0,6},{1,7},{2,4},{3,5},{4,2},{5,3},{6,0},{7,1},{8,14},{9,15},{10,... | collective-permute-start | bytes 786440 | tf_op jit(solution)/shard_map/ppermute | solution.py:313
  259.3 12.6 %collective-permute-start.21 = (bf16[128,512]{1,0:T(8,128)(2,1)}, bf16[128,512]{1,0:T(8,128)(2,1)S(1)}, u32[]{:S(2)}, u32[]{:S(2)}) collective-permute-start(bf16[128,512]{1,0:T(8,128)(2,1)} %get-tuple-element.55), channel_id=1, source_target_pairs={{0,1},{1,0},{2,3},{3,2},{4,5},{5,4},{6,7},{7,6},{8,9},{9,8},{10,11... | collective-permute-start | bytes 393224 | tf_op jit(solution)/shard_map/ppermute | solution.py:313
  259.3 13.4 %collective-permute-start.22 = (bf16[128,512]{1,0:T(8,128)(2,1)}, bf16[128,512]{1,0:T(8,128)(2,1)S(1)}, u32[]{:S(2)}, u32[]{:S(2)}) collective-permute-start(bf16[128,512]{1,0:T(8,128)(2,1)} %get-tuple-element.56), channel_id=1, source_target_pairs={{0,8},{1,9},{2,10},{3,11},{4,12},{5,13},{6,14},{7,15},{8,0},{9,1},... | collective-permute-start | bytes 393224 | tf_op jit(solution)/shard_map/ppermute | solution.py:313
  261.0 4.6 %copy-start.15 = (bf16[4,128,256]{2,1,0:T(8,128)(2,1)}, bf16[4,128,256]{2,1,0:T(8,128)(2,1)S(1)}, u32[]{:S(2)}) copy-start(bf16[4,128,256]{2,1,0:T(8,128)(2,1)S(1)} %collective-permute-done.31.one) | copy-start | bytes 786436
  261.0 12.4 %collective-permute-start.23 = (bf16[128,512]{1,0:T(8,128)(2,1)}, bf16[128,512]{1,0:T(8,128)(2,1)S(1)}, u32[]{:S(2)}, u32[]{:S(2)}) collective-permute-start(bf16[128,512]{1,0:T(8,128)(2,1)} %get-tuple-element.57), channel_id=1, source_target_pairs={{0,9},{1,8},{2,11},{3,10},{4,13},{5,12},{6,15},{7,14},{8,1},{9,0},... | collective-permute-start | bytes 393224 | tf_op jit(solution)/shard_map/ppermute | solution.py:313
  267.7 6.4 %collective-permute-start.28 = (bf16[128,256]{1,0:T(8,128)(2,1)}, bf16[128,256]{1,0:T(8,128)(2,1)S(1)}, u32[]{:S(2)}, u32[]{:S(2)}) collective-permute-start(bf16[128,256]{1,0:T(8,128)(2,1)} %get-tuple-element.64), channel_id=1, source_target_pairs={{0,1},{1,0},{2,3},{3,2},{4,5},{5,4},{6,7},{7,6},{8,9},{9,8},{10,11... | collective-permute-start | bytes 196616 | tf_op jit(solution)/shard_map/ppermute | solution.py:313
  269.2 6.3 %collective-permute-start.29 = (bf16[128,256]{1,0:T(8,128)(2,1)}, bf16[128,256]{1,0:T(8,128)(2,1)S(1)}, u32[]{:S(2)}, u32[]{:S(2)}) collective-permute-start(bf16[128,256]{1,0:T(8,128)(2,1)} %get-tuple-element.65), channel_id=1, source_target_pairs={{0,8},{1,9},{2,10},{3,11},{4,12},{5,13},{6,14},{7,15},{8,0},{9,1},... | collective-permute-start | bytes 196616 | tf_op jit(solution)/shard_map/ppermute | solution.py:313
  271.9 6.8 %copy-start.18 = (bf16[128,512]{1,0:T(8,128)(2,1)}, bf16[128,512]{1,0:T(8,128)(2,1)S(1)}, u32[]{:S(2)}) copy-start(bf16[128,512]{1,0:T(8,128)(2,1)S(1)} %collective-permute-done.21.refs_1_) | copy-start | bytes 393220
  271.9 4.4 %collective-permute-start.30 = (bf16[128,256]{1,0:T(8,128)(2,1)}, bf16[128,256]{1,0:T(8,128)(2,1)S(1)}, u32[]{:S(2)}, u32[]{:S(2)}) collective-permute-start(bf16[128,256]{1,0:T(8,128)(2,1)} %get-tuple-element.66), channel_id=1, source_target_pairs={{0,9},{1,8},{2,11},{3,10},{4,13},{5,12},{6,15},{7,14},{8,1},{9,0},... | collective-permute-start | bytes 196616 | tf_op jit(solution)/shard_map/ppermute | solution.py:313
  272.7 6.0 %copy-start.19 = (bf16[128,512]{1,0:T(8,128)(2,1)}, bf16[128,512]{1,0:T(8,128)(2,1)S(1)}, u32[]{:S(2)}) copy-start(bf16[128,512]{1,0:T(8,128)(2,1)S(1)} %collective-permute-done.22.refs_2_) | copy-start | bytes 393220
  272.7 3.6 %collective-permute-start.34 = (bf16[128,256]{1,0:T(8,128)(2,1)}, bf16[128,256]{1,0:T(8,128)(2,1)S(1)}, u32[]{:S(2)}, u32[]{:S(2)}) collective-permute-start(bf16[128,256]{1,0:T(8,128)(2,1)} %get-tuple-element.70), channel_id=1, source_target_pairs={{0,1},{1,0},{2,3},{3,2},{4,5},{5,4},{6,7},{7,6},{8,9},{9,8},{10,11... | collective-permute-start | bytes 196616 | tf_op jit(solution)/shard_map/ppermute | solution.py:313
  273.4 5.3 %copy-start.20 = (bf16[128,512]{1,0:T(8,128)(2,1)}, bf16[128,512]{1,0:T(8,128)(2,1)S(1)}, u32[]{:S(2)}) copy-start(bf16[128,512]{1,0:T(8,128)(2,1)S(1)} %collective-permute-done.23.refs_3_) | copy-start | bytes 393220
  273.4 5.2 %collective-permute-start.35 = (bf16[128,256]{1,0:T(8,128)(2,1)}, bf16[128,256]{1,0:T(8,128)(2,1)S(1)}, u32[]{:S(2)}, u32[]{:S(2)}) collective-permute-start(bf16[128,256]{1,0:T(8,128)(2,1)} %get-tuple-element.71), channel_id=1, source_target_pairs={{0,8},{1,9},{2,10},{3,11},{4,12},{5,13},{6,14},{7,15},{8,0},{9,1},... | collective-permute-start | bytes 196616 | tf_op jit(solution)/shard_map/ppermute | solution.py:313
  274.1 4.6 %collective-permute-start.36 = (bf16[128,256]{1,0:T(8,128)(2,1)}, bf16[128,256]{1,0:T(8,128)(2,1)S(1)}, u32[]{:S(2)}, u32[]{:S(2)}) collective-permute-start(bf16[128,256]{1,0:T(8,128)(2,1)} %get-tuple-element.72), channel_id=1, source_target_pairs={{0,9},{1,8},{2,11},{3,10},{4,13},{5,12},{6,15},{7,14},{8,1},{9,0},... | collective-permute-start | bytes 196616 | tf_op jit(solution)/shard_map/ppermute | solution.py:313
  (16 other events, 28.1 us)

commit v4 on v3

--- a/solution.py
+++ b/solution.py
@@ -8,7 +8,7 @@
 from jax.sharding import PartitionSpec as P
 
 CORE, PLANE, PAIR = 1, 2, 8
-LIMIT = 60 * 1024 * 1024
+LIMIT = 24 * 1024 * 1024
 LANES = 128
 
 
@@ -158,13 +158,49 @@
     )(order, packed, w_12, *after)
 
 
-def product_kernel(a_at, w_at, choice_ref, *refs):
-    groups = len(a_at) // 4
-    outs, (a, w, a_sem, w_sem) = refs[-4 - groups : -4], refs[-4:]
-    rows = a.shape[1] // len(a_at)
-    wide = len(w_at[0])
+def stack_kernel(first, count, *refs):
+    sources, stack_ref, sem = refs[-2 - count : -2], refs[-2], refs[-1]
+    rows = sources[0].shape[-2]
+    copies, at = [], 0
+    for source in sources:
+        parts = [source] if len(source.shape) == 3 else [source.at[0], source.at[1]]
+        for part in parts:
+            to = stack_ref.at[:, pl.ds((first + at) * rows, rows)]
+            copies.append(pltpu.make_async_copy(part, to, sem.at[at]))
+            at += 1
+    for copy in copies:
+        copy.start()
+    for copy in copies:
+        copy.wait()
+
+
+def stack(first, blocks, before=None):
+    tiles, rows, lanes = blocks[0].shape[-3:]
+    shape = (tiles, 16 * rows, lanes)
+    held = [] if before is None else [pltpu.with_memory_space_constraint(before, pltpu.VMEM)]
+    count = sum(block.size for block in blocks) // (tiles * rows * lanes)
+    return pl.pallas_call(
+        functools.partial(stack_kernel, first, len(blocks)),
+        out_shape=pltpu.VMEM(shape, blocks[0].dtype),
+        in_specs=[pl.BlockSpec(memory_space=pltpu.VMEM)] * len(held)
+        + [pl.BlockSpec(memory_space=pl.ANY)] * len(blocks),
+        out_specs=pl.BlockSpec(memory_space=pltpu.VMEM),
+        scratch_shapes=[pltpu.SemaphoreType.DMA((count,))],
+        input_output_aliases={0: 0} if held else {},
+        compiler_params=pltpu.CompilerParams(vmem_limit_bytes=LIMIT),
+        cost_estimate=pl.CostEstimate(
+            flops=0, bytes_accessed=4 * count * tiles * rows * lanes, transcendentals=0
+        ),
+        name="stack",
+    )(*held, *blocks)
+
+
+def product_kernel(places, w_at, choice_ref, a, *refs):
+    groups, wide = len(places), len(w_at[0])
+    outs, (w, w_sem) = refs[-2 - groups : -2], refs[-2:]
     tiles, _, columns = w.shape
     columns //= wide
+    rows = a.shape[1] // 16
 
     def pick(at):
         ref, index = at
@@ -175,11 +211,6 @@
             pick(w_at[choice][at]), w.at[:, :, pl.ds(at * columns, columns)], w_sem.at[at]
         )
 
-    def a_copy(at):
-        return pltpu.make_async_copy(
-            pick(a_at[at]), a.at[:, pl.ds(at * rows, rows)], a_sem.at[at]
-        )
-
     for at in range(wide):
         for choice in range(len(w_at)):
 
@@ -187,25 +218,27 @@
             def _():
                 w_copy(at, choice).start()
 
-    for at in range(len(a_at)):
-        a_copy(at).start()
     for at in range(wide):
         w_copy(at, 0).wait()
-    for group in range(groups):
-        for at in range(4 * group, 4 * group + 4):
-            a_copy(at).wait()
-        left = jnp.concatenate(
-            [a[tile, pl.ds(4 * group * rows, 4 * rows)] for tile in range(tiles)], axis=1
-        )
-        total = jnp.dot(
-            left,
-            w[...].reshape(tiles * LANES, wide * columns),
-            preferred_element_type=jnp.float32,
-        )
-        outs[group][...] = total.reshape(4, rows, wide * columns).astype(outs[group].dtype)
-
-
-def product(choice, groups, a_blocks, w_choices, after=()):
+    right = w[...].reshape(tiles * LANES, wide * columns)
+    for place, out in zip(places, outs):
+        for half in range(2):
+            here = [(place[2 * half + at], at) for at in range(2)]
+            left = jnp.concatenate(
+                [
+                    jnp.concatenate(
+                        [a[tile, pl.ds(block * rows, rows)] for tile in range(tiles)], axis=1
+                    )
+                    for block, _ in here
+                ],
+                axis=0,
+            )
+            total = jnp.dot(left, right, preferred_element_type=jnp.float32)
+            for _, at in here:
+                out[2 * half + at] = total[at * rows : (at + 1) * rows].astype(out.dtype)
+
+
+def product(choice, groups, places, rows_stack, w_choices, after=()):
     arrays = []
 
     def at(block):
@@ -216,36 +249,37 @@
         arrays.append(array)
         return len(arrays) - 1, index
 
-    a_at = [at(block) for group in groups for block in a_blocks[group]]
-    w_at = [[at(block) for block in choice] for choice in w_choices]
-    tiles, rows, _ = a_blocks[0][0][0].shape
+    w_at = [[at(block) for block in blocks] for blocks in w_choices]
+    tiles, rows, _ = rows_stack.shape
+    rows //= 16
     columns = w_choices[-1][0][0].shape[-1]
     wide = len(w_choices[0])
     shape = (4, rows, wide * columns)
     count = len(arrays) + len(after)
     return pl.pallas_call(
-        functools.partial(product_kernel, a_at, w_at),
+        functools.partial(product_kernel, [places[group] for group in groups], w_at),
         out_shape=[
             jax.ShapeDtypeStruct(shape, jnp.float32 if group == 0 else jnp.bfloat16)
             for group in groups
         ],
-        in_specs=[pl.BlockSpec(memory_space=pltpu.SMEM)]
+        in_specs=[
+            pl.BlockSpec(memory_space=pltpu.SMEM),
+            pl.BlockSpec(memory_space=pltpu.VMEM),
+        ]
         + [pl.BlockSpec(memory_space=pl.ANY)] * count,
         out_specs=[pl.BlockSpec(memory_space=pltpu.VMEM)] * len(groups),
         scratch_shapes=[
-            pltpu.VMEM((tiles, len(a_at) * rows, LANES), jnp.bfloat16),
             pltpu.VMEM((tiles, LANES, wide * columns), jnp.bfloat16),
-            pltpu.SemaphoreType.DMA((len(a_at),)),
             pltpu.SemaphoreType.DMA((wide,)),
         ],
         compiler_params=pltpu.CompilerParams(vmem_limit_bytes=LIMIT),
         cost_estimate=pl.CostEstimate(
-            flops=2 * len(a_at) * rows * tiles * LANES * wide * columns,
-            bytes_accessed=2 * tiles * LANES * (len(a_at) * rows + wide * columns),
+            flops=8 * len(groups) * rows * tiles * LANES * wide * columns,
+            bytes_accessed=2 * tiles * LANES * (4 * len(groups) * rows + wide * columns),
             transcendentals=0,
         ),
         name="product",
-    )(choice, *arrays, *after)
+    )(choice, pltpu.with_memory_space_constraint(rows_stack, pltpu.VMEM), *arrays, *after)
 
 
 def add_kernel(relative, own, one, two, three, *refs):
@@ -307,7 +341,10 @@
     plane = (me // PLANE) % 4
     z_low, z_high = (me // PAIR) % 2, me // (2 * PAIR)
     at_plane = plane.astype(jnp.int32).reshape(1)
-    inputs = (gate_pre, up_pre, down_weight)
+    inputs = [
+        pltpu.with_memory_space_constraint(array, pltpu.HBM)
+        for array in (gate_pre, up_pre, down_weight)
+    ]
 
     def send(array, perm):
         return lax.ppermute(array, "fsdp", perm=perm)
@@ -336,9 +373,10 @@
     core_0, core_pair_0 = to_core(a_0), to_core(pair_0)
 
     order = jnp.array([[1, 2, 3], [1, 3, 2], [2, 3, 1], [3, 2, 1]], jnp.int32)[plane]
+    a_12, got_3 = lax.optimization_barrier((a_12, got_3))
     known = jnp.array([0, 3], jnp.int32)
     a_3, w_3, ordered_1 = reorder(
-        jnp.concatenate([known, order[:1]]), got_3, w_12, after=(core_0, core_pair_0)
+        jnp.concatenate([known, order[:1]]), got_3, w_12, after=(core_0, core_pair_0, mid_12)
     )
     pair_3, mid_3 = to_pair(a_3), to_mid(w_3)
     core_12, core_pair_12 = to_core(a_12), to_core(pair_12)
@@ -348,40 +386,50 @@
     next_1, next_2, next_3 = to_next(ordered_1), to_next(ordered_2), to_next(ordered_3)
     core_3, core_pair_3 = to_core(a_3), to_core(pair_3)
 
-    a_blocks = [
-        [(a_0, None), (core_0, None), (pair_0, None), (core_pair_0, None)],
-        [(a_12, 0), (core_12, 0), (pair_12, 0), (core_pair_12, 0)],
-        [(a_12, 1), (core_12, 1), (pair_12, 1), (core_pair_12, 1)],
-        [(a_3, None), (core_3, None), (pair_3, None), (core_pair_3, None)],
-    ]
+    rows_stack = stack(0, [a_0, pair_0, core_0, core_pair_0])
+    rows_stack = stack(4, [a_12, pair_12, core_12, core_pair_12], rows_stack)
+    rows_stack = stack(12, [a_3, pair_3, core_3, core_pair_3], rows_stack)
+    places = [(0, 2, 1, 3), (4, 8, 6, 10), (5, 9, 7, 11), (12, 14, 13, 15)]
     w_own = [(w_0, None), (w_12, 0), (w_12, 1), (w_3, None)]
     w_mid = [(mid_0, None), (mid_12, 0), (mid_12, 1), (mid_3, None)]
-    first, one, two, three = [(block, None) for block in (next_0, next_1, next_2, next_3)]
-    w_low = [[first, one], [one, first], [one, two], [one, two]]
-    w_high = [[two, three], [two, three], [first, three], [three, first]]
     mid = (z_low ^ z_high).astype(jnp.int32).reshape(1)
-    pieces, summing, last = [], [], ()
-    for choice, w_choices, calls in (
-        (mid, [w_own, w_mid], ([3, 1, 2, 0],)),
-        (at_plane, w_low, ([3, 1, 2, 0],)),
-        (at_plane, w_high, ([3, 1, 2], [0])),
-    ):
+
+    def totals_of(choice, w_choices, calls, after=()):
         totals = {}
         for groups in calls:
-            outs = product(choice, groups, a_blocks, w_choices, last)
+            outs = product(choice, groups, places, rows_stack, w_choices, after)
             totals.update(zip(groups, outs))
-            last = (outs[0],)
-        others = [send(totals[step], flip(n, step * PLANE)) for step in (1, 2, 3)]
-        summing.append((totals[0], others))
-        last = tuple(others)
-    for at, (half, start) in enumerate(((0, 0), (1, 0), (1, 2))):
-        later = tuple(summing[at + 1][0:1]) if at < 2 else ()
-        summed = add(*summing[at], half == 0, later)
+            after = (outs[0],)
+        return [totals[group] for group in range(4)]
+
+    def across_plane(totals):
+        return [send(totals[step], flip(n, step * PLANE)) for step in (1, 2, 3)]
+
+    pieces = []
+
+    def spread(totals, others, half, start, after=()):
+        summed, received = add(totals[0], others, half == 0, after), []
         for piece in range(4):
             mask = (piece >> 1) * PAIR + (piece & 1) * CORE
             block = send(summed[piece], flip(n, mask)) if mask else summed[piece]
             fixed = ((piece >> 1) << 4) | (half << 3) | (piece & 1)
             pieces.append((block, fixed, start, half == 0))
+            received.append(block)
+        return received[1:]
+
+    own = totals_of(mid, [w_own, w_mid], ([3, 1, 2, 0],))
+    *own, next_1 = lax.optimization_barrier((*own, next_1))
+    own_sums = across_plane(own)
+    first, one, two, three = [(block, None) for block in (next_0, next_1, next_2, next_3)]
+    w_low = [[first, one], [one, first], [one, two], [one, two]]
+    w_high = [[two, three], [two, three], [first, three], [three, first]]
+    low = totals_of(at_plane, w_low, ([3, 1, 2, 0],), tuple(own_sums))
+    low_sums = across_plane(low)
+    own_spread = spread(own, own_sums, 0, 0, (low[0],))
+    high = totals_of(at_plane, w_high, ([3], [1, 2], [0]), (*low_sums, *own_spread))
+    high_sums = across_plane(high)
+    spread(low, low_sums, 1, 0, (high[0],))
+    spread(high, high_sums, 1, 2)
     across = z_low * 16 + z_high * 8 + me % 2
     place = jnp.stack([across + plane * 2, across]).astype(jnp.int32)
     return assemble(place, pieces)

time: 282 us -> 243 us (0.86)
  starting transfers between devices: 73 us -> 42.1 us
  Pallas kernels: 74.3 us -> 49 us
  waiting for transfers between devices: 126 us -> 147 us
  local copies, waits for them, and re-layouts: 6.95 us -> 3.25 us
    ppermute x37, starting transfers between devices: 73 us -> 42.1 us  [send(): return lax.ppermute(array, 'fsdp', perm=perm)]
    ppermute x37, waiting for transfers between devices: 126 us -> 147 us  [send(): return lax.ppermute(array, 'fsdp', perm=perm)]
    pallas_call x4 -> x8, Pallas kernels: 43.3 us -> 26.5 us  [the longest x5 19.6 us: product(): pl.pallas_call(functools.partial(product_kernel, [places[group] for group...]
    pallas_call x3, Pallas kernels: 6.6 us -> 1.6 us  [add(): pl.pallas_call(functools.partial(add_kernel, relative), out_shape=[jax.Sh...]
    unnamed x54 -> x14, local copies, waits for them, and re-layouts: 5.61 us -> 2.5 us
  transfers between devices with their start and end apart: 37 -> 37, of which waited for: 13 -> 17; matrix products, arithmetic and copies ran while one was open for 1% -> 0% of each run, Pallas kernels for 19% -> 16%
where the time goes in v4:
time: 243 us; the launch traced here: 242 us
  waiting for transfers between devices  147 us (60%)
  Pallas kernels  49 us (20%)
  starting transfers between devices  42.1 us (17%)
  local copies, waits for them, and re-layouts  3.25 us (1%)
    ppermute x37, waiting for transfers between devices, send(): return lax.ppermute(array, 'fsdp', perm=perm)  147 us
    ppermute x37, starting transfers between devices, send(): return lax.ppermute(array, 'fsdp', perm=perm)  42.1 us
    pallas_call x5, Pallas kernels, product(): pl.pallas_call(functools.partial(product_kernel, [places[group] for group...  19.6 us
    pallas_call x2, Pallas kernels, pack(): pl.pallas_call(functools.partial(pack_kernel, apart, len(steps)), out_sha...  9.38 us
    pallas_call x2, Pallas kernels, reorder(): pl.pallas_call(functools.partial(reorder_kernel, count), out_shape=[jax.S...  6.93 us
    pallas_call x3, Pallas kernels, stack(): pl.pallas_call(functools.partial(stack_kernel, first, len(blocks)), out_s...  6.87 us
  transfers between devices with their start and end apart: 37, of which 17 were waited for; matrix products, arithmetic and copies ran while one was open for 0% of the time, Pallas kernels for 16%

profile of v4, /device:TPU:0, one launch (start us, length us, event | category | flops | bytes accessed | tf_op | source)
XLA Modules:
  0.0 242.3 jit_solution(4018677968273272139)
XLA Ops:
  0.0 5.3 %pack.2 = (bf16[28,128,128]{2,1,0:T(8,128)(2,1)}, bf16[28,128,128]{2,1,0:T(8,128)(2,1)S(1)}, bf16[2,28,128,128]{3,2,1,0:T(8,128)(2,1)S(1)}, bf16[2,28,128,128]{3,2,1,0:T(8,128)(2,1)S(1)}) custom-call(s32[1]{0:T(128)} %bitcast.3.plane_ref.choice_ref, bf16[128,14336]{1,0:T(8,128)(2,1)} %refs_0_.3, bf16[128,14336]{1,0:T(8,128)(2,1)} %refs_1_.3, ...), custom_call_target="tpu_custom_call" | custom-call | bytes 13762560 | tf_op jit(solution)/shard_map/pack/pallas_call | solution.py:63
  5.3 3.0 %collective-permute-start.3 = (bf16[2,28,128,128]{3,2,1,0:T(8,128)(2,1)S(1)}, bf16[2,28,128,128]{3,2,1,0:T(8,128)(2,1)S(1)}, u32[]{:S(2)}, u32[]{:S(2)}) collective-permute-start(bf16[2,28,128,128]{3,2,1,0:T(8,128)(2,1)S(1)} %get-tuple-element.46), channel_id=1, source_target_pairs={{0,2},{1,3},{2,0},{3,1},{4,6},{5,7},{6,4},{7,5},{8,10},{9,11},{10,... | collective-permute-start | bytes 5505032 | tf_op jit(solution)/shard_map/ppermute | solution.py:350
  8.3 1.5 collective-permute-start.4
  9.8 1.6 collective-permute-start
  12.1 3.8 %collective-permute-start.6 = (bf16[28,128,128]{2,1,0:T(8,128)(2,1)S(1)}, bf16[28,128,128]{2,1,0:T(8,128)(2,1)S(1)}, u32[]{:S(2)}, u32[]{:S(2)}) collective-permute-start(bf16[28,128,128]{2,1,0:T(8,128)(2,1)S(1)} %get-tuple-element.48.refs_0_), channel_id=1, source_target_pairs={{8,0},{9,1},{10,2},{11,3},{12,4},{13,5},{14,6},{15,7},{24,8},{25,9... | collective-permute-start | bytes 2752520 | tf_op jit(solution)/shard_map/ppermute | solution.py:350
  16.0 17.4 %collective-permute-done.refs_1_.refs_0_.refs_3_ = bf16[28,128,128]{2,1,0:T(8,128)(2,1)S(1)} collective-permute-done((bf16[28,128,128]{2,1,0:T(8,128)(2,1)}, bf16[28,128,128]{2,1,0:T(8,128)(2,1)S(1)}, u32[]{:S(2)}, u32[]{:S(2)}) %collective-permute-start) | collective-permute-done | bytes 917536 | tf_op jit(solution)/shard_map/ppermute | solution.py:350
  33.4 4.1 %pack.3 = bf16[2,28,128,128]{3,2,1,0:T(8,128)(2,1)} custom-call(s32[1]{0:T(128)} %bitcast.3.plane_ref.choice_ref, bf16[128,14336]{1,0:T(8,128)(2,1)} %refs_0_.3, bf16[128,14336]{1,0:T(8,128)(2,1)} %refs_1_.3, bf16[14336,128]{1,0:T(8,128)(2,1)} %refs_2_.3, bf16[28,128,128]{2,1,0:T(8,128)(2,1)S(1)} %collective-permute-done.refs_1_.refs_0_.refs_3_), custom_call_target="tpu_custom_call" | custom-call | bytes 4587520 | tf_op jit(solution)/shard_map/pack/pallas_call | solution.py:63
  37.5 13.8 %collective-permute-done.6.refs_2_.refs_0_ = bf16[28,128,128]{2,1,0:T(8,128)(2,1)S(1)} collective-permute-done((bf16[28,128,128]{2,1,0:T(8,128)(2,1)S(1)}, bf16[28,128,128]{2,1,0:T(8,128)(2,1)S(1)}, u32[]{:S(2)}, u32[]{:S(2)}) %collective-permute-start.6) | collective-permute-done | bytes 917536 | tf_op jit(solution)/shard_map/ppermute | solution.py:350
  51.3 37.9 %collective-permute-done.4.two = bf16[2,28,128,128]{3,2,1,0:T(8,128)(2,1)S(1)} collective-permute-done((bf16[2,28,128,128]{3,2,1,0:T(8,128)(2,1)S(1)}, bf16[2,28,128,128]{3,2,1,0:T(8,128)(2,1)S(1)}, u32[]{:S(2)}, u32[]{:S(2)}) %collective-permute-start.4) | collective-permute-done | bytes 1835040 | tf_op jit(solution)/shard_map/ppermute | solution.py:350
  89.1 2.8 %unpack_pair.1 = (bf16[2,28,128,128]{3,2,1,0:T(8,128)(2,1)}, bf16[2,28,128,128]{3,2,1,0:T(8,128)(2,1)}) custom-call(bf16[2,28,128,128]{3,2,1,0:T(8,128)(2,1)S(1)} %collective-permute-done.3.one, bf16[2,28,128,128]{3,2,1,0:T(8,128)(2,1)S(1)} %collective-permute-done.4.two, bf16[28,128,128]{2,1,0:T(8,128)(2,1)S(1)} %collective-permute-done.refs_1_.refs_0_.refs_3_, ...), custom_call_target="tpu_custom_call" | custom-call | bytes 7340032 | tf_op jit(solution)/shard_map/unpack_pair/pallas_call | solution.py:106
  92.0 1.6 collective-permute-start.8
  93.6 1.9 collective-permute-start.11
  96.9 18.7 %collective-permute-done.8.refs_2_ = bf16[2,28,128,128]{3,2,1,0:T(8,128)(2,1)} collective-permute-done((bf16[2,28,128,128]{3,2,1,0:T(8,128)(2,1)}, bf16[2,28,128,128]{3,2,1,0:T(8,128)(2,1)}, u32[]{:S(2)}, u32[]{:S(2)}) %collective-permute-start.8) | collective-permute-done | bytes 1835040 | tf_op jit(solution)/shard_map/ppermute | solution.py:350
  115.6 3.9 %reorder.2 = (bf16[28,128,128]{2,1,0:T(8,128)(2,1)}, bf16[28,128,128]{2,1,0:T(8,128)(2,1)}, bf16[28,128,128]{2,1,0:T(8,128)(2,1)S(1)}) custom-call(s32[3]{0:T(128)S(1)} %pad_add_fusion.1.order_ref, bf16[2,28,128,128]{3,2,1,0:T(8,128)(2,1)} %collective-permute-done.7.packed, bf16[2,28,128,128]{3,2,1,0:T(8,128)(2,1)} %get-tuple-element.52.w_12.refs_1_, ...), custom_call_target="tpu_custom_call" | custom-call | bytes 7340032 | tf_op jit(solution)/shard_map/reorder/pallas_call | solution.py:144
  120.5 4.6 %collective-permute-start.12 = (bf16[28,128,128]{2,1,0:T(8,128)(2,1)}, bf16[28,128,128]{2,1,0:T(8,128)(2,1)}, u32[]{:S(2)}, u32[]{:S(2)}) collective-permute-start(bf16[28,128,128]{2,1,0:T(8,128)(2,1)} %get-tuple-element.53.refs_1_), channel_id=1, source_target_pairs={{0,8},{1,9},{2,10},{3,11},{4,12},{5,13},{6,14},{7,15},{8,0},{9,1},... | collective-permute-start | bytes 2752520 | tf_op jit(solution)/shard_map/ppermute | solution.py:350
  125.1 1.6 collective-permute-start.15
  126.7 16.9 %collective-permute-done.12.refs_2_.refs_0_ = bf16[28,128,128]{2,1,0:T(8,128)(2,1)} collective-permute-done((bf16[28,128,128]{2,1,0:T(8,128)(2,1)}, bf16[28,128,128]{2,1,0:T(8,128)(2,1)}, u32[]{:S(2)}, u32[]{:S(2)}) %collective-permute-start.12) | collective-permute-done | bytes 917536 | tf_op jit(solution)/shard_map/ppermute | solution.py:350
  143.6 2.6 %collective-permute-start.16 = (bf16[28,128,128]{2,1,0:T(8,128)(2,1)}, bf16[28,128,128]{2,1,0:T(8,128)(2,1)S(1)}, u32[]{:S(2)}, u32[]{:S(2)}) collective-permute-start(bf16[28,128,128]{2,1,0:T(8,128)(2,1)} %copy-done.6), channel_id=1, source_target_pairs={{8,0},{9,1},{10,2},{11,3},{12,4},{13,5},{14,6},{15,7},{24,8},{25,9... | collective-permute-start | bytes 2752520 | tf_op jit(solution)/shard_map/ppermute | solution.py:350
  147.4 1.5 stack.15.refs_0_
  149.0 3.0 %reorder.3 = (bf16[28,128,128]{2,1,0:T(8,128)(2,1)S(1)}, bf16[28,128,128]{2,1,0:T(8,128)(2,1)S(1)}) custom-call(s32[2]{0:T(128)S(1)} %slice_bitcast_fusion.order_ref, bf16[2,28,128,128]{3,2,1,0:T(8,128)(2,1)} %collective-permute-done.7.packed, bf16[2,28,128,128]{3,2,1,0:T(8,128)(2,1)} %get-tuple-element.52.w_12.refs_1_, ...), custom_call_target="tpu_custom_call" | custom-call | bytes 7340032 | tf_op jit(solution)/shard_map/reorder/pallas_call | solution.py:144
  152.0 1.6 collective-permute-start.20
  153.7 3.2 %stack.16.refs_0_ = bf16[28,2048,128]{2,1,0:T(8,128)(2,1)S(1)} custom-call(bf16[28,2048,128]{2,1,0:T(8,128)(2,1)S(1)} %stack.15.refs_0_, bf16[2,28,128,128]{3,2,1,0:T(8,128)(2,1)} %get-tuple-element.50.refs_1_, bf16[2,28,128,128]{3,2,1,0:T(8,128)(2,1)} %collective-permute-done.8.refs_2_, ...), custom_call_target="tpu_custom_call", output_to_operand_aliasing={{}: (0, {})} | custom-call | bytes 14680064 | tf_op jit(solution)/shard_map/stack/pallas_call | solution.py:182
  156.9 2.2 stack.17.a
  159.4 9.7 %product.5 = (bf16[4,128,512]{2,1,0:T(8,128)(2,1)S(1)}, bf16[4,128,512]{2,1,0:T(8,128)(2,1)S(1)}, bf16[4,128,512]{2,1,0:T(8,128)(2,1)S(1)}, f32[4,128,512]{2,1,0:T(8,128)S(1)}) custom-call(s32[1]{0:T(128)} %bitcast.2.choice_ref, bf16[28,2048,128]{2,1,0:T(8,128)(2,1)S(1)} %stack.17.a, bf16[28,128,128]{2,1,0:T(8,128)(2,1)S(1)} %copy-done.5, ...), custom_call_target="tpu_custom_call" | custom-call | flops 7516192768 | bytes 18350080 | tf_op jit(solution)/shard_map/product/pallas_call | solution.py:259
  169.2 2.0 collective-permute-start.18
  171.2 1.4 collective-permute-start.19
  172.6 1.3 collective-permute-start.27
  173.9 10.0 %collective-permute-done.17.refs_3_.one = bf16[4,128,512]{2,1,0:T(8,128)(2,1)S(1)} collective-permute-done((bf16[4,128,512]{2,1,0:T(8,128)(2,1)S(1)}, bf16[4,128,512]{2,1,0:T(8,128)(2,1)S(1)}, u32[]{:S(2)}, u32[]{:S(2)}) %collective-permute-start.17) | collective-permute-done | bytes 524320 | tf_op jit(solution)/shard_map/ppermute | solution.py:350
  183.9 9.5 %collective-permute-done.18.refs_4_.two = bf16[4,128,512]{2,1,0:T(8,128)(2,1)S(1)} collective-permute-done((bf16[4,128,512]{2,1,0:T(8,128)(2,1)S(1)}, bf16[4,128,512]{2,1,0:T(8,128)(2,1)S(1)}, u32[]{:S(2)}, u32[]{:S(2)}) %collective-permute-start.18) | collective-permute-done | bytes 524320 | tf_op jit(solution)/shard_map/ppermute | solution.py:350
  193.5 1.6 collective-permute-done.19.refs_5_.three
  195.1 4.5 %product.6 = (bf16[4,128,256]{2,1,0:T(8,128)(2,1)S(1)}, bf16[4,128,256]{2,1,0:T(8,128)(2,1)S(1)}, bf16[4,128,256]{2,1,0:T(8,128)(2,1)S(1)}, f32[4,128,256]{2,1,0:T(8,128)S(1)}) custom-call(s32[1]{0:T(128)} %bitcast.3.plane_ref.choice_ref, bf16[28,2048,128]{2,1,0:T(8,128)(2,1)S(1)} %stack.17.a, ...), custom_call_target="tpu_custom_call" | custom-call | flops 3758096384 | bytes 16515072 | tf_op jit(solution)/shard_map/product/pallas_call | solution.py:259
  200.8 1.5 collective-permute-start.25
  203.5 2.5 %collective-permute-done.27.refs_1_ = bf16[28,128,128]{2,1,0:T(8,128)(2,1)S(1)} collective-permute-done((bf16[28,128,128]{2,1,0:T(8,128)(2,1)S(1)}, bf16[28,128,128]{2,1,0:T(8,128)(2,1)S(1)}, u32[]{:S(2)}, u32[]{:S(2)}) %collective-permute-start.27) | collective-permute-done | bytes 917536 | tf_op jit(solution)/shard_map/ppermute | solution.py:350
  206.0 2.4 collective-permute-start.22
  208.4 3.9 %collective-permute-done.22.refs_7_.refs_2_ = bf16[128,512]{1,0:T(8,128)(2,1)S(1)} collective-permute-done((bf16[128,512]{1,0:T(8,128)(2,1)S(1)}, bf16[128,512]{1,0:T(8,128)(2,1)S(1)}, u32[]{:S(2)}, u32[]{:S(2)}) %collective-permute-start.22) | collective-permute-done | bytes 131104 | tf_op jit(solution)/shard_map/ppermute | solution.py:350
  212.3 1.9 collective-permute-done.23.refs_8_.refs_3_
  214.8 1.5 product.7.refs_3_
  216.3 2.5 %product.8 = (bf16[4,128,256]{2,1,0:T(8,128)(2,1)S(1)}, bf16[4,128,256]{2,1,0:T(8,128)(2,1)S(1)}) custom-call(s32[1]{0:T(128)} %bitcast.3.plane_ref.choice_ref, bf16[28,2048,128]{2,1,0:T(8,128)(2,1)S(1)} %stack.17.a, bf16[28,128,128]{2,1,0:T(8,128)(2,1)S(1)} %collective-permute-done.20.refs_2_.refs_0_, ...), custom_call_target="tpu_custom_call" | custom-call | flops 1879048192 | bytes 9175040 | tf_op jit(solution)/shard_map/product/pallas_call | solution.py:259
  218.8 1.3 collective-permute-start.31
  220.9 1.5 collective-permute-start.33
  222.3 1.5 product.9.refs_0_.own
  224.6 3.6 %collective-permute-done.31.one = bf16[4,128,256]{2,1,0:T(8,128)(2,1)} collective-permute-done((bf16[4,128,256]{2,1,0:T(8,128)(2,1)S(1)}, bf16[4,128,256]{2,1,0:T(8,128)(2,1)}, u32[]{:S(2)}, u32[]{:S(2)}) %collective-permute-start.31) | collective-permute-done | bytes 262176 | tf_op jit(solution)/shard_map/ppermute | solution.py:350
  228.1 3.7 %collective-permute-done.32.two = bf16[4,128,256]{2,1,0:T(8,128)(2,1)} collective-permute-done((bf16[4,128,256]{2,1,0:T(8,128)(2,1)S(1)}, bf16[4,128,256]{2,1,0:T(8,128)(2,1)}, u32[]{:S(2)}, u32[]{:S(2)}) %collective-permute-start.32) | collective-permute-done | bytes 262176 | tf_op jit(solution)/shard_map/ppermute | solution.py:350
  231.9 1.7 collective-permute-done.33.three
  233.6 1.2 add.41
  234.9 1.5 collective-permute-start.35
  236.9 2.6 %collective-permute-done.35.refs_10_ = bf16[128,256]{1,0:T(8,128)(2,1)S(1)} collective-permute-done((bf16[128,256]{1,0:T(8,128)(2,1)S(1)}, bf16[128,256]{1,0:T(8,128)(2,1)S(1)}, u32[]{:S(2)}, u32[]{:S(2)}) %collective-permute-start.35) | collective-permute-done | bytes 65568 | tf_op jit(solution)/shard_map/ppermute | solution.py:350
  240.5 1.8 assemble.1
  (62 shorter events, 10.8 us)
Async XLA Ops:
  5.3 32.1 %copy-start.4 = (bf16[28,128,128]{2,1,0:T(8,128)(2,1)}, bf16[28,128,128]{2,1,0:T(8,128)(2,1)S(1)}, u32[]{:S(2)}) copy-start(bf16[28,128,128]{2,1,0:T(8,128)(2,1)S(1)} %get-tuple-element.48.refs_0_) | copy-start | bytes 2752516
  5.3 46.0 %collective-permute-start.3 = (bf16[2,28,128,128]{3,2,1,0:T(8,128)(2,1)S(1)}, bf16[2,28,128,128]{3,2,1,0:T(8,128)(2,1)S(1)}, u32[]{:S(2)}, u32[]{:S(2)}) collective-permute-start(bf16[2,28,128,128]{3,2,1,0:T(8,128)(2,1)S(1)} %get-tuple-element.46), channel_id=1, source_target_pairs={{0,2},{1,3},{2,0},{3,1},{4,6},{5,7},{6,4},{7,5},{8,10},{9,11},{10,... | collective-permute-start | bytes 5505032 | tf_op jit(solution)/shard_map/ppermute | solution.py:350
  8.3 80.8 %collective-permute-start.4 = (bf16[2,28,128,128]{3,2,1,0:T(8,128)(2,1)S(1)}, bf16[2,28,128,128]{3,2,1,0:T(8,128)(2,1)S(1)}, u32[]{:S(2)}, u32[]{:S(2)}) collective-permute-start(bf16[2,28,128,128]{3,2,1,0:T(8,128)(2,1)S(1)} %get-tuple-element.47), channel_id=1, source_target_pairs={{0,4},{1,5},{2,6},{3,7},{4,0},{5,1},{6,2},{7,3},{8,12},{9,13},{10,... | collective-permute-start | bytes 5505032 | tf_op jit(solution)/shard_map/ppermute | solution.py:350
  9.8 23.5 %collective-permute-start = (bf16[28,128,128]{2,1,0:T(8,128)(2,1)}, bf16[28,128,128]{2,1,0:T(8,128)(2,1)S(1)}, u32[]{:S(2)}, u32[]{:S(2)}) collective-permute-start(bf16[28,128,128]{2,1,0:T(8,128)(2,1)} %get-tuple-element.45.refs_0_), channel_id=1, source_target_pairs={{0,8},{1,9},{2,10},{3,11},{4,12},{5,13},{6,14},{7,15},{8,0},{9,1},... | collective-permute-start | bytes 2752520 | tf_op jit(solution)/shard_map/ppermute | solution.py:350
  11.4 26.0 %collective-permute-start.5 = (bf16[28,128,128]{2,1,0:T(8,128)(2,1)S(1)}, bf16[28,128,128]{2,1,0:T(8,128)(2,1)S(1)}, u32[]{:S(2)}, u32[]{:S(2)}) collective-permute-start(bf16[28,128,128]{2,1,0:T(8,128)(2,1)S(1)} %get-tuple-element.48.refs_0_), channel_id=1, source_target_pairs={{8,16},{9,17},{10,18},{11,19},{12,20},{13,21},{14,22},{15,23},{16,... | collective-permute-start | bytes 2752520 | tf_op jit(solution)/shard_map/ppermute | solution.py:350
  12.1 39.1 %collective-permute-start.6 = (bf16[28,128,128]{2,1,0:T(8,128)(2,1)S(1)}, bf16[28,128,128]{2,1,0:T(8,128)(2,1)S(1)}, u32[]{:S(2)}, u32[]{:S(2)}) collective-permute-start(bf16[28,128,128]{2,1,0:T(8,128)(2,1)S(1)} %get-tuple-element.48.refs_0_), channel_id=1, source_target_pairs={{8,0},{9,1},{10,2},{11,3},{12,4},{13,5},{14,6},{15,7},{24,8},{25,9... | collective-permute-start | bytes 2752520 | tf_op jit(solution)/shard_map/ppermute | solution.py:350
  37.4 58.6 %collective-permute-start.7 = (bf16[2,28,128,128]{3,2,1,0:T(8,128)(2,1)}, bf16[2,28,128,128]{3,2,1,0:T(8,128)(2,1)}, u32[]{:S(2)}, u32[]{:S(2)}) collective-permute-start(bf16[2,28,128,128]{3,2,1,0:T(8,128)(2,1)} %pack.3), channel_id=1, source_target_pairs={{0,6},{1,7},{2,4},{3,5},{4,2},{5,3},{6,0},{7,1},{8,14},{9,15},{10,... | collective-permute-start | bytes 5505032 | tf_op jit(solution)/shard_map/ppermute | solution.py:350
  37.5 54.5 %copy-start.2 = (bf16[28,128,128]{2,1,0:T(8,128)(2,1)}, bf16[28,128,128]{2,1,0:T(8,128)(2,1)S(1)}, u32[]{:S(2)}) copy-start(bf16[28,128,128]{2,1,0:T(8,128)(2,1)S(1)} %collective-permute-done.5.refs_1_.refs_3_) | copy-start | bytes 2752516
  92.0 23.6 %collective-permute-start.8 = (bf16[2,28,128,128]{3,2,1,0:T(8,128)(2,1)}, bf16[2,28,128,128]{3,2,1,0:T(8,128)(2,1)}, u32[]{:S(2)}, u32[]{:S(2)}) collective-permute-start(bf16[2,28,128,128]{3,2,1,0:T(8,128)(2,1)} %get-tuple-element.50.refs_1_), channel_id=1, source_target_pairs={{0,8},{1,9},{2,10},{3,11},{4,12},{5,13},{6,14},{7,15},{8,0},{9,1},... | collective-permute-start | bytes 5505032 | tf_op jit(solution)/shard_map/ppermute | solution.py:350
  93.6 22.0 %collective-permute-start.11 = (bf16[2,28,128,128]{3,2,1,0:T(8,128)(2,1)}, bf16[2,28,128,128]{3,2,1,0:T(8,128)(2,1)}, u32[]{:S(2)}, u32[]{:S(2)}) collective-permute-start(bf16[2,28,128,128]{3,2,1,0:T(8,128)(2,1)} %get-tuple-element.52.w_12.refs_1_), channel_id=1, source_target_pairs={{8,16},{9,17},{10,18},{11,19},{12,20},{13,21},{14,22},{15,23},{16,... | collective-permute-start | bytes 5505032 | tf_op jit(solution)/shard_map/ppermute | solution.py:350
  95.5 20.1 %collective-permute-start.1 = (bf16[28,128,128]{2,1,0:T(8,128)(2,1)}, bf16[28,128,128]{2,1,0:T(8,128)(2,1)S(1)}, u32[]{:S(2)}, u32[]{:S(2)}) collective-permute-start(bf16[28,128,128]{2,1,0:T(8,128)(2,1)} %get-tuple-element.45.refs_0_), channel_id=1, source_target_pairs={{0,1},{1,0},{2,3},{3,2},{4,5},{5,4},{6,7},{7,6},{8,9},{9,8},{10,11... | collective-permute-start | bytes 2752520 | tf_op jit(solution)/shard_map/ppermute | solution.py:350
  95.5 20.1 %collective-permute-start.2 = (bf16[28,128,128]{2,1,0:T(8,128)(2,1)S(1)}, bf16[28,128,128]{2,1,0:T(8,128)(2,1)}, u32[]{:S(2)}, u32[]{:S(2)}) collective-permute-start(bf16[28,128,128]{2,1,0:T(8,128)(2,1)S(1)} %collective-permute-done.refs_1_.refs_0_.refs_3_), channel_id=1, source_target_pairs={{0,1},{1,0},{2,3},{3,2},{4,5},{5,4},{6,7},{7,6},{8,9},{9,8},{10,11... | collective-permute-start | bytes 2752520 | tf_op jit(solution)/shard_map/ppermute | solution.py:350
  96.0 47.5 %collective-permute-start.9 = (bf16[2,28,128,128]{3,2,1,0:T(8,128)(2,1)}, bf16[2,28,128,128]{3,2,1,0:T(8,128)(2,1)}, u32[]{:S(2)}, u32[]{:S(2)}) collective-permute-start(bf16[2,28,128,128]{3,2,1,0:T(8,128)(2,1)} %get-tuple-element.50.refs_1_), channel_id=1, source_target_pairs={{0,1},{1,0},{2,3},{3,2},{4,5},{5,4},{6,7},{7,6},{8,9},{9,8},{10,11... | collective-permute-start | bytes 5505032 | tf_op jit(solution)/shard_map/ppermute | solution.py:350
  115.6 33.4 %collective-permute-start.10 = (bf16[2,28,128,128]{3,2,1,0:T(8,128)(2,1)}, bf16[2,28,128,128]{3,2,1,0:T(8,128)(2,1)}, u32[]{:S(2)}, u32[]{:S(2)}) collective-permute-start(bf16[2,28,128,128]{3,2,1,0:T(8,128)(2,1)} %collective-permute-done.8.refs_2_), channel_id=1, source_target_pairs={{0,1},{1,0},{2,3},{3,2},{4,5},{5,4},{6,7},{7,6},{8,9},{9,8},{10,11... | collective-permute-start | bytes 5505032 | tf_op jit(solution)/shard_map/ppermute | solution.py:350
  115.6 3.9 %copy-start = (bf16[28,128,128]{2,1,0:T(8,128)(2,1)}, bf16[28,128,128]{2,1,0:T(8,128)(2,1)S(1)}, u32[]{:S(2)}) copy-start(bf16[28,128,128]{2,1,0:T(8,128)(2,1)S(1)} %collective-permute-done.1.refs_2_.refs_0_) | copy-start | bytes 2752516
  119.5 1.0 copy-start.6
  120.5 23.1 %collective-permute-start.12 = (bf16[28,128,128]{2,1,0:T(8,128)(2,1)}, bf16[28,128,128]{2,1,0:T(8,128)(2,1)}, u32[]{:S(2)}, u32[]{:S(2)}) collective-permute-start(bf16[28,128,128]{2,1,0:T(8,128)(2,1)} %get-tuple-element.53.refs_1_), channel_id=1, source_target_pairs={{0,8},{1,9},{2,10},{3,11},{4,12},{5,13},{6,14},{7,15},{8,0},{9,1},... | collective-permute-start | bytes 2752520 | tf_op jit(solution)/shard_map/ppermute | solution.py:350
  125.1 23.9 %collective-permute-start.15 = (bf16[28,128,128]{2,1,0:T(8,128)(2,1)}, bf16[28,128,128]{2,1,0:T(8,128)(2,1)}, u32[]{:S(2)}, u32[]{:S(2)}) collective-permute-start(bf16[28,128,128]{2,1,0:T(8,128)(2,1)} %get-tuple-element.54.refs_2_), channel_id=1, source_target_pairs={{8,16},{9,17},{10,18},{11,19},{12,20},{13,21},{14,22},{15,23},{16,... | collective-permute-start | bytes 2752520 | tf_op jit(solution)/shard_map/ppermute | solution.py:350
  126.7 30.2 %collective-permute-start.13 = (bf16[28,128,128]{2,1,0:T(8,128)(2,1)}, bf16[28,128,128]{2,1,0:T(8,128)(2,1)}, u32[]{:S(2)}, u32[]{:S(2)}) collective-permute-start(bf16[28,128,128]{2,1,0:T(8,128)(2,1)} %get-tuple-element.53.refs_1_), channel_id=1, source_target_pairs={{0,1},{1,0},{2,3},{3,2},{4,5},{5,4},{6,7},{7,6},{8,9},{9,8},{10,11... | collective-permute-start | bytes 2752520 | tf_op jit(solution)/shard_map/ppermute | solution.py:350
  143.6 13.3 %collective-permute-start.14 = (bf16[28,128,128]{2,1,0:T(8,128)(2,1)}, bf16[28,128,128]{2,1,0:T(8,128)(2,1)}, u32[]{:S(2)}, u32[]{:S(2)}) collective-permute-start(bf16[28,128,128]{2,1,0:T(8,128)(2,1)} %collective-permute-done.12.refs_2_.refs_0_), channel_id=1, source_target_pairs={{0,1},{1,0},{2,3},{3,2},{4,5},{5,4},{6,7},{7,6},{8,9},{9,8},{10,11... | collective-permute-start | bytes 2752520 | tf_op jit(solution)/shard_map/ppermute | solution.py:350
  143.6 25.5 %collective-permute-start.16 = (bf16[28,128,128]{2,1,0:T(8,128)(2,1)}, bf16[28,128,128]{2,1,0:T(8,128)(2,1)S(1)}, u32[]{:S(2)}, u32[]{:S(2)}) collective-permute-start(bf16[28,128,128]{2,1,0:T(8,128)(2,1)} %copy-done.6), channel_id=1, source_target_pairs={{8,0},{9,1},{10,2},{11,3},{12,4},{13,5},{14,6},{15,7},{24,8},{25,9... | collective-permute-start | bytes 2752520 | tf_op jit(solution)/shard_map/ppermute | solution.py:350
  146.2 1.2 copy-start.1
  152.0 43.1 %collective-permute-start.20 = (bf16[28,128,128]{2,1,0:T(8,128)(2,1)S(1)}, bf16[28,128,128]{2,1,0:T(8,128)(2,1)S(1)}, u32[]{:S(2)}, u32[]{:S(2)}) collective-permute-start(bf16[28,128,128]{2,1,0:T(8,128)(2,1)S(1)} %get-tuple-element.65), channel_id=1, source_target_pairs={{8,0},{9,1},{10,2},{11,3},{12,4},{13,5},{14,6},{15,7},{24,8},{25,9... | collective-permute-start | bytes 2752520 | tf_op jit(solution)/shard_map/ppermute | solution.py:350
  156.8 2.3 copy-start.3
  156.8 2.6 %copy-start.5 = (bf16[28,128,128]{2,1,0:T(8,128)(2,1)S(1)}, bf16[28,128,128]{2,1,0:T(8,128)(2,1)}, u32[]{:S(2)}) copy-start(bf16[28,128,128]{2,1,0:T(8,128)(2,1)} %copy-done.4) | copy-start | bytes 2752516
  169.1 14.9 %collective-permute-start.17 = (bf16[4,128,512]{2,1,0:T(8,128)(2,1)S(1)}, bf16[4,128,512]{2,1,0:T(8,128)(2,1)S(1)}, u32[]{:S(2)}, u32[]{:S(2)}) collective-permute-start(bf16[4,128,512]{2,1,0:T(8,128)(2,1)S(1)} %get-tuple-element.61), channel_id=1, source_target_pairs={{0,2},{1,3},{2,0},{3,1},{4,6},{5,7},{6,4},{7,5},{8,10},{9,11},{10,... | collective-permute-start | bytes 1572872 | tf_op jit(solution)/shard_map/ppermute | solution.py:350
  169.2 24.3 %collective-permute-start.18 = (bf16[4,128,512]{2,1,0:T(8,128)(2,1)S(1)}, bf16[4,128,512]{2,1,0:T(8,128)(2,1)S(1)}, u32[]{:S(2)}, u32[]{:S(2)}) collective-permute-start(bf16[4,128,512]{2,1,0:T(8,128)(2,1)S(1)} %get-tuple-element.62), channel_id=1, source_target_pairs={{0,4},{1,5},{2,6},{3,7},{4,0},{5,1},{6,2},{7,3},{8,12},{9,13},{10,... | collective-permute-start | bytes 1572872 | tf_op jit(solution)/shard_map/ppermute | solution.py:350
  171.2 23.9 %collective-permute-start.19 = (bf16[4,128,512]{2,1,0:T(8,128)(2,1)S(1)}, bf16[4,128,512]{2,1,0:T(8,128)(2,1)S(1)}, u32[]{:S(2)}, u32[]{:S(2)}) collective-permute-start(bf16[4,128,512]{2,1,0:T(8,128)(2,1)S(1)} %get-tuple-element.63), channel_id=1, source_target_pairs={{0,6},{1,7},{2,4},{3,5},{4,2},{5,3},{6,0},{7,1},{8,14},{9,15},{10,... | collective-permute-start | bytes 1572872 | tf_op jit(solution)/shard_map/ppermute | solution.py:350
  172.6 33.4 %collective-permute-start.27 = (bf16[28,128,128]{2,1,0:T(8,128)(2,1)S(1)}, bf16[28,128,128]{2,1,0:T(8,128)(2,1)S(1)}, u32[]{:S(2)}, u32[]{:S(2)}) collective-permute-start(bf16[28,128,128]{2,1,0:T(8,128)(2,1)S(1)} %get-tuple-element.74), channel_id=1, source_target_pairs={{8,0},{9,1},{10,2},{11,3},{12,4},{13,5},{14,6},{15,7},{24,8},{25,9... | collective-permute-start | bytes 2752520 | tf_op jit(solution)/shard_map/ppermute | solution.py:350
  199.9 8.5 %collective-permute-start.21 = (bf16[128,512]{1,0:T(8,128)(2,1)S(1)}, bf16[128,512]{1,0:T(8,128)(2,1)S(1)}, u32[]{:S(2)}, u32[]{:S(2)}) collective-permute-start(bf16[128,512]{1,0:T(8,128)(2,1)S(1)} %get-tuple-element.68), channel_id=1, source_target_pairs={{0,1},{1,0},{2,3},{3,2},{4,5},{5,4},{6,7},{7,6},{8,9},{9,8},{10,11... | collective-permute-start | bytes 393224 | tf_op jit(solution)/shard_map/ppermute | solution.py:350
  200.0 14.3 %collective-permute-start.24 = (bf16[4,128,256]{2,1,0:T(8,128)(2,1)S(1)}, bf16[4,128,256]{2,1,0:T(8,128)(2,1)S(1)}, u32[]{:S(2)}, u32[]{:S(2)}) collective-permute-start(bf16[4,128,256]{2,1,0:T(8,128)(2,1)S(1)} %get-tuple-element.71), channel_id=1, source_target_pairs={{0,2},{1,3},{2,0},{3,1},{4,6},{5,7},{6,4},{7,5},{8,10},{9,11},{10,... | collective-permute-start | bytes 786440 | tf_op jit(solution)/shard_map/ppermute | solution.py:350
  200.8 14.0 %collective-permute-start.25 = (bf16[4,128,256]{2,1,0:T(8,128)(2,1)S(1)}, bf16[4,128,256]{2,1,0:T(8,128)(2,1)S(1)}, u32[]{:S(2)}, u32[]{:S(2)}) collective-permute-start(bf16[4,128,256]{2,1,0:T(8,128)(2,1)S(1)} %get-tuple-element.72), channel_id=1, source_target_pairs={{0,4},{1,5},{2,6},{3,7},{4,0},{5,1},{6,2},{7,3},{8,12},{9,13},{10,... | collective-permute-start | bytes 786440 | tf_op jit(solution)/shard_map/ppermute | solution.py:350
  202.3 12.5 %collective-permute-start.26 = (bf16[4,128,256]{2,1,0:T(8,128)(2,1)S(1)}, bf16[4,128,256]{2,1,0:T(8,128)(2,1)S(1)}, u32[]{:S(2)}, u32[]{:S(2)}) collective-permute-start(bf16[4,128,256]{2,1,0:T(8,128)(2,1)S(1)} %get-tuple-element.73), channel_id=1, source_target_pairs={{0,6},{1,7},{2,4},{3,5},{4,2},{5,3},{6,0},{7,1},{8,14},{9,15},{10,... | collective-permute-start | bytes 786440 | tf_op jit(solution)/shard_map/ppermute | solution.py:350
  206.0 6.3 %collective-permute-start.22 = (bf16[128,512]{1,0:T(8,128)(2,1)S(1)}, bf16[128,512]{1,0:T(8,128)(2,1)S(1)}, u32[]{:S(2)}, u32[]{:S(2)}) collective-permute-start(bf16[128,512]{1,0:T(8,128)(2,1)S(1)} %get-tuple-element.69), channel_id=1, source_target_pairs={{0,8},{1,9},{2,10},{3,11},{4,12},{5,13},{6,14},{7,15},{8,0},{9,1},... | collective-permute-start | bytes 393224 | tf_op jit(solution)/shard_map/ppermute | solution.py:350
  208.4 5.9 %collective-permute-start.23 = (bf16[128,512]{1,0:T(8,128)(2,1)S(1)}, bf16[128,512]{1,0:T(8,128)(2,1)S(1)}, u32[]{:S(2)}, u32[]{:S(2)}) collective-permute-start(bf16[128,512]{1,0:T(8,128)(2,1)S(1)} %get-tuple-element.70), channel_id=1, source_target_pairs={{0,9},{1,8},{2,11},{3,10},{4,13},{5,12},{6,15},{7,14},{8,1},{9,0},... | collective-permute-start | bytes 393224 | tf_op jit(solution)/shard_map/ppermute | solution.py:350
  218.8 9.4 %collective-permute-start.31 = (bf16[4,128,256]{2,1,0:T(8,128)(2,1)S(1)}, bf16[4,128,256]{2,1,0:T(8,128)(2,1)}, u32[]{:S(2)}, u32[]{:S(2)}) collective-permute-start(bf16[4,128,256]{2,1,0:T(8,128)(2,1)S(1)} %get-tuple-element.75.refs_3_), channel_id=1, source_target_pairs={{0,2},{1,3},{2,0},{3,1},{4,6},{5,7},{6,4},{7,5},{8,10},{9,11},{10,... | collective-permute-start | bytes 786440 | tf_op jit(solution)/shard_map/ppermute | solution.py:350
  220.1 11.8 %collective-permute-start.32 = (bf16[4,128,256]{2,1,0:T(8,128)(2,1)S(1)}, bf16[4,128,256]{2,1,0:T(8,128)(2,1)}, u32[]{:S(2)}, u32[]{:S(2)}) collective-permute-start(bf16[4,128,256]{2,1,0:T(8,128)(2,1)S(1)} %get-tuple-element.80), channel_id=1, source_target_pairs={{0,4},{1,5},{2,6},{3,7},{4,0},{5,1},{6,2},{7,3},{8,12},{9,13},{10,... | collective-permute-start | bytes 786440 | tf_op jit(solution)/shard_map/ppermute | solution.py:350
  220.9 12.7 %collective-permute-start.33 = (bf16[4,128,256]{2,1,0:T(8,128)(2,1)S(1)}, bf16[4,128,256]{2,1,0:T(8,128)(2,1)}, u32[]{:S(2)}, u32[]{:S(2)}) collective-permute-start(bf16[4,128,256]{2,1,0:T(8,128)(2,1)S(1)} %product.7.refs_3_), channel_id=1, source_target_pairs={{0,6},{1,7},{2,4},{3,5},{4,2},{5,3},{6,0},{7,1},{8,14},{9,15},{10,... | collective-permute-start | bytes 786440 | tf_op jit(solution)/shard_map/ppermute | solution.py:350
  224.0 12.5 %collective-permute-start.28 = (bf16[128,256]{1,0:T(8,128)(2,1)S(1)}, bf16[128,256]{1,0:T(8,128)(2,1)S(1)}, u32[]{:S(2)}, u32[]{:S(2)}) collective-permute-start(bf16[128,256]{1,0:T(8,128)(2,1)S(1)} %get-tuple-element.77), channel_id=1, source_target_pairs={{0,1},{1,0},{2,3},{3,2},{4,5},{5,4},{6,7},{7,6},{8,9},{9,8},{10,11... | collective-permute-start | bytes 196616 | tf_op jit(solution)/shard_map/ppermute | solution.py:350
  224.1 12.8 %collective-permute-start.29 = (bf16[128,256]{1,0:T(8,128)(2,1)S(1)}, bf16[128,256]{1,0:T(8,128)(2,1)S(1)}, u32[]{:S(2)}, u32[]{:S(2)}) collective-permute-start(bf16[128,256]{1,0:T(8,128)(2,1)S(1)} %get-tuple-element.78), channel_id=1, source_target_pairs={{0,8},{1,9},{2,10},{3,11},{4,12},{5,13},{6,14},{7,15},{8,0},{9,1},... | collective-permute-start | bytes 196616 | tf_op jit(solution)/shard_map/ppermute | solution.py:350
  228.1 8.7 %collective-permute-start.30 = (bf16[128,256]{1,0:T(8,128)(2,1)S(1)}, bf16[128,256]{1,0:T(8,128)(2,1)S(1)}, u32[]{:S(2)}, u32[]{:S(2)}) collective-permute-start(bf16[128,256]{1,0:T(8,128)(2,1)S(1)} %get-tuple-element.79), channel_id=1, source_target_pairs={{0,9},{1,8},{2,11},{3,10},{4,13},{5,12},{6,15},{7,14},{8,1},{9,0},... | collective-permute-start | bytes 196616 | tf_op jit(solution)/shard_map/ppermute | solution.py:350
  234.8 2.0 collective-permute-start.34
  234.9 4.5 %collective-permute-start.35 = (bf16[128,256]{1,0:T(8,128)(2,1)S(1)}, bf16[128,256]{1,0:T(8,128)(2,1)S(1)}, u32[]{:S(2)}, u32[]{:S(2)}) collective-permute-start(bf16[128,256]{1,0:T(8,128)(2,1)S(1)} %get-tuple-element.83), channel_id=1, source_target_pairs={{0,8},{1,9},{2,10},{3,11},{4,12},{5,13},{6,14},{7,15},{8,0},{9,1},... | collective-permute-start | bytes 196616 | tf_op jit(solution)/shard_map/ppermute | solution.py:350
  236.4 4.1 %collective-permute-start.36 = (bf16[128,256]{1,0:T(8,128)(2,1)S(1)}, bf16[128,256]{1,0:T(8,128)(2,1)S(1)}, u32[]{:S(2)}, u32[]{:S(2)}) collective-permute-start(bf16[128,256]{1,0:T(8,128)(2,1)S(1)} %get-tuple-element.84), channel_id=1, source_target_pairs={{0,9},{1,8},{2,11},{3,10},{4,13},{5,12},{6,15},{7,14},{8,1},{9,0},... | collective-permute-start | bytes 196616 | tf_op jit(solution)/shard_map/ppermute | solution.py:350

commit v5 on v4

--- a/solution.py
+++ b/solution.py
@@ -367,6 +367,7 @@
     got_2 = send(packed_2, flip(n, 2 * PLANE))
 
     (packed_3,) = pack(at_plane, (3,), *inputs, after=(pair_0,))
+    packed_3, got_1, got_2 = lax.optimization_barrier((packed_3, got_1, got_2))
     got_3 = send(packed_3, flip(n, 3 * PLANE))
     a_12, w_12 = unpack_pair(got_1, got_2, after=(pair_0, mid_0, next_0))
     pair_12, mid_12 = to_pair(a_12), to_mid(w_12)
@@ -380,14 +381,15 @@
     )
     pair_3, mid_3 = to_pair(a_3), to_mid(w_3)
     core_12, core_pair_12 = to_core(a_12), to_core(pair_12)
+    rows_stack = stack(0, [a_0, pair_0, core_0, core_pair_0])
+    rows_stack = stack(4, [a_12, pair_12, core_12, core_pair_12], rows_stack)
+    pair_3, mid_3, rows_stack = lax.optimization_barrier((pair_3, mid_3, rows_stack))
     ordered_2, ordered_3 = reorder(
         order[1:], got_3, w_12, after=(pair_3, mid_3, core_12, core_pair_12)
     )
     next_1, next_2, next_3 = to_next(ordered_1), to_next(ordered_2), to_next(ordered_3)
     core_3, core_pair_3 = to_core(a_3), to_core(pair_3)
 
-    rows_stack = stack(0, [a_0, pair_0, core_0, core_pair_0])
-    rows_stack = stack(4, [a_12, pair_12, core_12, core_pair_12], rows_stack)
     rows_stack = stack(12, [a_3, pair_3, core_3, core_pair_3], rows_stack)
     places = [(0, 2, 1, 3), (4, 8, 6, 10), (5, 9, 7, 11), (12, 14, 13, 15)]
     w_own = [(w_0, None), (w_12, 0), (w_12, 1), (w_3, None)]
@@ -408,25 +410,23 @@
     pieces = []
 
     def spread(totals, others, half, start, after=()):
-        summed, received = add(totals[0], others, half == 0, after), []
+        summed = add(totals[0], others, half == 0, after)
         for piece in range(4):
             mask = (piece >> 1) * PAIR + (piece & 1) * CORE
             block = send(summed[piece], flip(n, mask)) if mask else summed[piece]
             fixed = ((piece >> 1) << 4) | (half << 3) | (piece & 1)
             pieces.append((block, fixed, start, half == 0))
-            received.append(block)
-        return received[1:]
-
-    own = totals_of(mid, [w_own, w_mid], ([3, 1, 2, 0],))
-    *own, next_1 = lax.optimization_barrier((*own, next_1))
+
+    own = totals_of(mid, [w_own, w_mid], ([3, 1, 2], [0]))
+    own[1], own[2], own[3], next_1 = lax.optimization_barrier((*own[1:], next_1))
     own_sums = across_plane(own)
     first, one, two, three = [(block, None) for block in (next_0, next_1, next_2, next_3)]
     w_low = [[first, one], [one, first], [one, two], [one, two]]
     w_high = [[two, three], [two, three], [first, three], [three, first]]
     low = totals_of(at_plane, w_low, ([3, 1, 2, 0],), tuple(own_sums))
     low_sums = across_plane(low)
-    own_spread = spread(own, own_sums, 0, 0, (low[0],))
-    high = totals_of(at_plane, w_high, ([3], [1, 2], [0]), (*low_sums, *own_spread))
+    spread(own, own_sums, 0, 0, (low[0],))
+    high = totals_of(at_plane, w_high, ([3, 1, 2], [0]), tuple(low_sums))
     high_sums = across_plane(high)
     spread(low, low_sums, 1, 0, (high[0],))
     spread(high, high_sums, 1, 2)

time: 243 us -> 239 us (0.984)
  waiting for transfers between devices: 147 us -> 106 us
  local copies, waits for them, and re-layouts: 3.25 us -> 32.8 us
  starting transfers between devices: 42.1 us -> 51.5 us
    ppermute x37, waiting for transfers between devices: 147 us -> 106 us  [send(): return lax.ppermute(array, 'fsdp', perm=perm)]
    unnamed x14 -> x48, local copies, waits for them, and re-layouts: 2.5 us -> 32 us
    ppermute x37, starting transfers between devices: 42.1 us -> 51.5 us  [send(): return lax.ppermute(array, 'fsdp', perm=perm)]
  transfers between devices with their start and end apart: 37 -> 37, of which waited for: 17 -> 14; matrix products, arithmetic and copies ran while one was open for 0% -> 0% of each run, Pallas kernels for 16% -> 15%
where the time goes in v5:
time: 239 us; the launch traced here: 238 us
  waiting for transfers between devices  106 us (44%)
  starting transfers between devices  51.5 us (22%)
  Pallas kernels  47.6 us (20%)
  local copies, waits for them, and re-layouts  32.8 us (14%)
    ppermute x37, waiting for transfers between devices, send(): return lax.ppermute(array, 'fsdp', perm=perm)  106 us
    ppermute x37, starting transfers between devices, send(): return lax.ppermute(array, 'fsdp', perm=perm)  51.5 us
    unnamed x48, local copies, waits for them, and re-layouts  32 us
    pallas_call x5, Pallas kernels, product(): pl.pallas_call(functools.partial(product_kernel, [places[group] for group...  21.2 us
    pallas_call x2, Pallas kernels, pack(): pl.pallas_call(functools.partial(pack_kernel, apart, len(steps)), out_sha...  8.16 us
    pallas_call x3, Pallas kernels, stack(): pl.pallas_call(functools.partial(stack_kernel, first, len(blocks)), out_s...  7.25 us
    pallas_call x2, Pallas kernels, reorder(): pl.pallas_call(functools.partial(reorder_kernel, count), out_shape=[jax.S...  5.48 us
  transfers between devices with their start and end apart: 37, of which 14 were waited for; matrix products, arithmetic and copies ran while one was open for 0% of the time, Pallas kernels for 15%

profile of v5, /device:TPU:0, one launch (start us, length us, event | category | flops | bytes accessed | tf_op | source)
XLA Modules:
  0.0 238.4 jit_solution(9844459030152832663)
XLA Ops:
  0.0 5.3 %pack.2 = (bf16[28,128,128]{2,1,0:T(8,128)(2,1)}, bf16[28,128,128]{2,1,0:T(8,128)(2,1)S(1)}, bf16[2,28,128,128]{3,2,1,0:T(8,128)(2,1)S(1)}, bf16[2,28,128,128]{3,2,1,0:T(8,128)(2,1)S(1)}) custom-call(s32[1]{0:T(128)} %bitcast.4.plane_ref.choice_ref, bf16[128,14336]{1,0:T(8,128)(2,1)} %refs_0_.3, bf16[128,14336]{1,0:T(8,128)(2,1)} %refs_1_.3, ...), custom_call_target="tpu_custom_call" | custom-call | bytes 13762560 | tf_op jit(solution)/shard_map/pack/pallas_call | solution.py:63
  5.3 3.0 %collective-permute-start.1 = (bf16[2,28,128,128]{3,2,1,0:T(8,128)(2,1)S(1)}, bf16[2,28,128,128]{3,2,1,0:T(8,128)(2,1)S(1)}, u32[]{:S(2)}, u32[]{:S(2)}) collective-permute-start(bf16[2,28,128,128]{3,2,1,0:T(8,128)(2,1)S(1)} %get-tuple-element.51), channel_id=1, source_target_pairs={{0,2},{1,3},{2,0},{3,1},{4,6},{5,7},{6,4},{7,5},{8,10},{9,11},{10,... | collective-permute-start | bytes 5505032 | tf_op jit(solution)/shard_map/ppermute | solution.py:350
  8.3 1.5 collective-permute-start.2
  9.8 1.6 collective-permute-start
  12.1 3.8 %collective-permute-start.4 = (bf16[28,128,128]{2,1,0:T(8,128)(2,1)S(1)}, bf16[28,128,128]{2,1,0:T(8,128)(2,1)S(1)}, u32[]{:S(2)}, u32[]{:S(2)}) collective-permute-start(bf16[28,128,128]{2,1,0:T(8,128)(2,1)S(1)} %get-tuple-element.55.refs_0_), channel_id=1, source_target_pairs={{8,0},{9,1},{10,2},{11,3},{12,4},{13,5},{14,6},{15,7},{24,8},{25,9... | collective-permute-start | bytes 2752520 | tf_op jit(solution)/shard_map/ppermute | solution.py:350
  16.0 17.5 %collective-permute-done.refs_3_.refs_0_.refs_1_ = bf16[28,128,128]{2,1,0:T(8,128)(2,1)} collective-permute-done((bf16[28,128,128]{2,1,0:T(8,128)(2,1)}, bf16[28,128,128]{2,1,0:T(8,128)(2,1)}, u32[]{:S(2)}, u32[]{:S(2)}) %collective-permute-start) | collective-permute-done | bytes 917536 | tf_op jit(solution)/shard_map/ppermute | solution.py:350
  33.5 2.9 %pack.3 = bf16[2,28,128,128]{3,2,1,0:T(8,128)(2,1)S(1)} custom-call(s32[1]{0:T(128)} %bitcast.4.plane_ref.choice_ref, bf16[128,14336]{1,0:T(8,128)(2,1)} %refs_0_.3, bf16[128,14336]{1,0:T(8,128)(2,1)} %refs_1_.3, bf16[14336,128]{1,0:T(8,128)(2,1)} %refs_2_.3, bf16[28,128,128]{2,1,0:T(8,128)(2,1)} %collective-permute-done.refs_3_.refs_0_.refs_1_), custom_call_target="tpu_custom_call" | custom-call | bytes 4587520 | tf_op jit(solution)/shard_map/pack/pallas_call | solution.py:63
  36.3 12.0 %collective-permute-done.1.one = bf16[2,28,128,128]{3,2,1,0:T(8,128)(2,1)S(1)} collective-permute-done((bf16[2,28,128,128]{3,2,1,0:T(8,128)(2,1)S(1)}, bf16[2,28,128,128]{3,2,1,0:T(8,128)(2,1)S(1)}, u32[]{:S(2)}, u32[]{:S(2)}) %collective-permute-start.1) | collective-permute-done | bytes 1835040 | tf_op jit(solution)/shard_map/ppermute | solution.py:350
  48.3 1.5 collective-permute-done.2.two
  49.8 1.5 collective-permute-start.5
  51.3 2.2 unpack_pair.1
  53.6 4.4 %collective-permute-start.11 = (bf16[2,28,128,128]{3,2,1,0:T(8,128)(2,1)}, bf16[2,28,128,128]{3,2,1,0:T(8,128)(2,1)}, u32[]{:S(2)}, u32[]{:S(2)}) collective-permute-start(bf16[2,28,128,128]{3,2,1,0:T(8,128)(2,1)} %get-tuple-element.62.refs_1_), channel_id=1, source_target_pairs={{0,8},{1,9},{2,10},{3,11},{4,12},{5,13},{6,14},{7,15},{8,0},{9,1},... | collective-permute-start | bytes 5505032 | tf_op jit(solution)/shard_map/ppermute | solution.py:350
  58.0 1.9 collective-permute-start.8
  60.4 30.9 %collective-permute-done.5.packed = bf16[2,28,128,128]{3,2,1,0:T(8,128)(2,1)S(1)} collective-permute-done((bf16[2,28,128,128]{3,2,1,0:T(8,128)(2,1)S(1)}, bf16[2,28,128,128]{3,2,1,0:T(8,128)(2,1)S(1)}, u32[]{:S(2)}, u32[]{:S(2)}) %collective-permute-start.5) | collective-permute-done | bytes 1835040 | tf_op jit(solution)/shard_map/ppermute | solution.py:350
  92.5 3.3 %collective-permute-done.11.refs_2_ = bf16[2,28,128,128]{3,2,1,0:T(8,128)(2,1)} collective-permute-done((bf16[2,28,128,128]{3,2,1,0:T(8,128)(2,1)}, bf16[2,28,128,128]{3,2,1,0:T(8,128)(2,1)}, u32[]{:S(2)}, u32[]{:S(2)}) %collective-permute-start.11) | collective-permute-done | bytes 1835040 | tf_op jit(solution)/shard_map/ppermute | solution.py:350
  96.6 1.5 copy-done.12
  98.1 2.8 %reorder.2 = (bf16[28,128,128]{2,1,0:T(8,128)(2,1)}, bf16[28,128,128]{2,1,0:T(8,128)(2,1)S(1)}, bf16[28,128,128]{2,1,0:T(8,128)(2,1)}) custom-call(s32[3]{0:T(128)S(1)} %pad_add_fusion.1.order_ref, bf16[2,28,128,128]{3,2,1,0:T(8,128)(2,1)S(1)} %copy-done.12, bf16[2,28,128,128]{3,2,1,0:T(8,128)(2,1)S(1)} %get-tuple-element.59.w_12.refs_1_, ...), custom_call_target="tpu_custom_call" | custom-call | bytes 7340032 | tf_op jit(solution)/shard_map/reorder/pallas_call | solution.py:144
  101.6 6.4 %collective-permute-start.9 = (bf16[28,128,128]{2,1,0:T(8,128)(2,1)}, bf16[28,128,128]{2,1,0:T(8,128)(2,1)}, u32[]{:S(2)}, u32[]{:S(2)}) collective-permute-start(bf16[28,128,128]{2,1,0:T(8,128)(2,1)} %get-tuple-element.60.refs_1_), channel_id=1, source_target_pairs={{0,8},{1,9},{2,10},{3,11},{4,12},{5,13},{6,14},{7,15},{8,0},{9,1},... | collective-permute-start | bytes 2752520 | tf_op jit(solution)/shard_map/ppermute | solution.py:350
  108.0 2.0 stack.15.refs_0_
  110.1 3.2 %stack.16.refs_0_ = bf16[28,2048,128]{2,1,0:T(8,128)(2,1)S(1)} custom-call(bf16[28,2048,128]{2,1,0:T(8,128)(2,1)S(1)} %stack.15.refs_0_, bf16[2,28,128,128]{3,2,1,0:T(8,128)(2,1)} %get-tuple-element.62.refs_1_, bf16[2,28,128,128]{3,2,1,0:T(8,128)(2,1)} %collective-permute-done.11.refs_2_, ...), custom_call_target="tpu_custom_call", output_to_operand_aliasing={{}: (0, {})} | custom-call | bytes 14680064 | tf_op jit(solution)/shard_map/stack/pallas_call | solution.py:182
  113.3 5.2 %copy-done = bf16[28,2048,128]{2,1,0:T(8,128)(2,1)} copy-done((bf16[28,2048,128]{2,1,0:T(8,128)(2,1)}, bf16[28,2048,128]{2,1,0:T(8,128)(2,1)S(1)}, u32[]{:S(2)}) %copy-start) | copy-done | bytes 14680088
  119.4 8.7 %collective-permute-done.9.refs_2_.refs_0_ = bf16[28,128,128]{2,1,0:T(8,128)(2,1)} collective-permute-done((bf16[28,128,128]{2,1,0:T(8,128)(2,1)}, bf16[28,128,128]{2,1,0:T(8,128)(2,1)}, u32[]{:S(2)}, u32[]{:S(2)}) %collective-permute-start.9) | collective-permute-done | bytes 917536 | tf_op jit(solution)/shard_map/ppermute | solution.py:350
  128.1 2.0 collective-permute-start.16
  131.4 1.5 copy-done.13
  132.9 2.7 %reorder.3 = (bf16[28,128,128]{2,1,0:T(8,128)(2,1)}, bf16[28,128,128]{2,1,0:T(8,128)(2,1)}) custom-call(s32[2]{0:T(128)S(1)} %slice_bitcast_fusion.order_ref, bf16[2,28,128,128]{3,2,1,0:T(8,128)(2,1)S(1)} %copy-done.13, bf16[2,28,128,128]{3,2,1,0:T(8,128)(2,1)S(1)} %get-tuple-element.59.w_12.refs_1_, ...), custom_call_target="tpu_custom_call" | custom-call | bytes 7340032 | tf_op jit(solution)/shard_map/reorder/pallas_call | solution.py:144
  135.7 5.2 %copy-done.1 = bf16[28,2048,128]{2,1,0:T(8,128)(2,1)S(1)} copy-done((bf16[28,2048,128]{2,1,0:T(8,128)(2,1)S(1)}, bf16[28,2048,128]{2,1,0:T(8,128)(2,1)}, u32[]{:S(2)}) %copy-start.1) | copy-done | bytes 14680088
  140.9 2.0 stack.17.a
  142.9 5.2 %copy-done.2 = bf16[28,2048,128]{2,1,0:T(8,128)(2,1)} copy-done((bf16[28,2048,128]{2,1,0:T(8,128)(2,1)}, bf16[28,2048,128]{2,1,0:T(8,128)(2,1)S(1)}, u32[]{:S(2)}) %copy-start.2) | copy-done | bytes 14680088
  148.1 5.2 %copy-done.3 = bf16[28,2048,128]{2,1,0:T(8,128)(2,1)S(1)} copy-done((bf16[28,2048,128]{2,1,0:T(8,128)(2,1)S(1)}, bf16[28,2048,128]{2,1,0:T(8,128)(2,1)}, u32[]{:S(2)}) %copy-start.3) | copy-done | bytes 14680088
  155.6 6.5 %product.5 = (bf16[4,128,512]{2,1,0:T(8,128)(2,1)S(1)}, bf16[4,128,512]{2,1,0:T(8,128)(2,1)S(1)}, bf16[4,128,512]{2,1,0:T(8,128)(2,1)S(1)}) custom-call(s32[1]{0:T(128)} %bitcast.2.choice_ref, bf16[28,2048,128]{2,1,0:T(8,128)(2,1)S(1)} %copy-done.3, bf16[28,128,128]{2,1,0:T(8,128)(2,1)S(1)} %copy-done.15, ...), custom_call_target="tpu_custom_call" | custom-call | flops 5637144576 | bytes 14680064 | tf_op jit(solution)/shard_map/product/pallas_call | solution.py:259
  163.3 2.4 %collective-permute-start.19 = (bf16[4,128,512]{2,1,0:T(8,128)(2,1)S(1)}, bf16[4,128,512]{2,1,0:T(8,128)(2,1)S(1)}, u32[]{:S(2)}, u32[]{:S(2)}) collective-permute-start(bf16[4,128,512]{2,1,0:T(8,128)(2,1)S(1)} %get-tuple-element.72.refs_6_), channel_id=1, source_target_pairs={{0,6},{1,7},{2,4},{3,5},{4,2},{5,3},{6,0},{7,1},{8,14},{9,15},{10,... | collective-permute-start | bytes 1572872 | tf_op jit(solution)/shard_map/ppermute | solution.py:350
  165.7 3.7 %collective-permute-start.27 = (bf16[28,128,128]{2,1,0:T(8,128)(2,1)}, bf16[28,128,128]{2,1,0:T(8,128)(2,1)S(1)}, u32[]{:S(2)}, u32[]{:S(2)}) collective-permute-start(bf16[28,128,128]{2,1,0:T(8,128)(2,1)} %get-tuple-element.83), channel_id=1, source_target_pairs={{8,0},{9,1},{10,2},{11,3},{12,4},{13,5},{14,6},{15,7},{24,8},{25,9... | collective-permute-start | bytes 2752520 | tf_op jit(solution)/shard_map/ppermute | solution.py:350
  169.5 1.8 collective-permute-done.20.refs_2_.refs_0_
  171.3 5.8 %collective-permute-done.17.refs_3_.one = bf16[4,128,512]{2,1,0:T(8,128)(2,1)S(1)} collective-permute-done((bf16[4,128,512]{2,1,0:T(8,128)(2,1)S(1)}, bf16[4,128,512]{2,1,0:T(8,128)(2,1)S(1)}, u32[]{:S(2)}, u32[]{:S(2)}) %collective-permute-start.17) | collective-permute-done | bytes 524320 | tf_op jit(solution)/shard_map/ppermute | solution.py:350
  177.0 10.8 %collective-permute-done.18.refs_4_.two = bf16[4,128,512]{2,1,0:T(8,128)(2,1)S(1)} collective-permute-done((bf16[4,128,512]{2,1,0:T(8,128)(2,1)S(1)}, bf16[4,128,512]{2,1,0:T(8,128)(2,1)S(1)}, u32[]{:S(2)}, u32[]{:S(2)}) %collective-permute-start.18) | collective-permute-done | bytes 524320 | tf_op jit(solution)/shard_map/ppermute | solution.py:350
  187.8 5.3 %product.7 = (bf16[4,128,256]{2,1,0:T(8,128)(2,1)S(1)}, bf16[4,128,256]{2,1,0:T(8,128)(2,1)S(1)}, bf16[4,128,256]{2,1,0:T(8,128)(2,1)S(1)}, f32[4,128,256]{2,1,0:T(8,128)S(1)}) custom-call(s32[1]{0:T(128)} %bitcast.4.plane_ref.choice_ref, bf16[28,2048,128]{2,1,0:T(8,128)(2,1)S(1)} %copy-done.4, ...), custom_call_target="tpu_custom_call" | custom-call | flops 3758096384 | bytes 16515072 | tf_op jit(solution)/shard_map/product/pallas_call | solution.py:259
  193.1 1.4 collective-permute-start.24
  196.7 5.7 %collective-permute-done.24.refs_3_.one = bf16[4,128,256]{2,1,0:T(8,128)(2,1)S(1)} collective-permute-done((bf16[4,128,256]{2,1,0:T(8,128)(2,1)S(1)}, bf16[4,128,256]{2,1,0:T(8,128)(2,1)S(1)}, u32[]{:S(2)}, u32[]{:S(2)}) %collective-permute-start.24) | collective-permute-done | bytes 262176 | tf_op jit(solution)/shard_map/ppermute | solution.py:350
  202.4 3.1 %collective-permute-done.25.refs_4_.two = bf16[4,128,256]{2,1,0:T(8,128)(2,1)S(1)} collective-permute-done((bf16[4,128,256]{2,1,0:T(8,128)(2,1)S(1)}, bf16[4,128,256]{2,1,0:T(8,128)(2,1)S(1)}, u32[]{:S(2)}, u32[]{:S(2)}) %collective-permute-start.25) | collective-permute-done | bytes 262176 | tf_op jit(solution)/shard_map/ppermute | solution.py:350
  205.6 1.6 collective-permute-done.26.refs_5_.three
  207.2 4.2 %product.8 = (bf16[4,128,256]{2,1,0:T(8,128)(2,1)S(1)}, bf16[4,128,256]{2,1,0:T(8,128)(2,1)S(1)}, bf16[4,128,256]{2,1,0:T(8,128)(2,1)S(1)}) custom-call(s32[1]{0:T(128)} %bitcast.4.plane_ref.choice_ref, bf16[28,2048,128]{2,1,0:T(8,128)(2,1)S(1)} %copy-done.4, bf16[28,128,128]{2,1,0:T(8,128)(2,1)} %collective-permute-done.20.refs_2_.refs_0_, ...), custom_call_target="tpu_custom_call" | custom-call | flops 2818572288 | bytes 12845056 | tf_op jit(solution)/shard_map/product/pallas_call | solution.py:259
  213.1 1.8 collective-permute-start.33
  214.9 2.8 %product.6.own = f32[4,128,512]{2,1,0:T(8,128)S(1)} custom-call(s32[1]{0:T(128)} %bitcast.2.choice_ref, bf16[28,2048,128]{2,1,0:T(8,128)(2,1)S(1)} %copy-done.4, bf16[28,128,128]{2,1,0:T(8,128)(2,1)S(1)} %copy-done.16, bf16[2,28,128,128]{3,2,1,0:T(8,128)(2,1)S(1)} %get-tuple-element.59.w_12.refs_1_, bf16[28,128,128]{2,1,0:T(8,128)(2,1)S(1)} %copy-done.19, ...), custom_call_target="tpu_custom_call" | custom-call | flops 1879048192 | bytes 7340032 | tf_op jit(solution)/shard_map/product/pallas_call | solution.py:259
  218.1 3.6 %collective-permute-start.22 = (bf16[128,512]{1,0:T(8,128)(2,1)S(1)}, bf16[128,512]{1,0:T(8,128)(2,1)S(1)}, u32[]{:S(2)}, u32[]{:S(2)}) collective-permute-start(bf16[128,512]{1,0:T(8,128)(2,1)S(1)} %get-tuple-element.78), channel_id=1, source_target_pairs={{0,8},{1,9},{2,10},{3,11},{4,12},{5,13},{6,14},{7,15},{8,0},{9,1},... | collective-permute-start | bytes 393224 | tf_op jit(solution)/shard_map/ppermute | solution.py:350
  221.8 2.3 product.9.refs_0_.own
  225.0 1.5 collective-permute-start.28
  234.3 2.4 collective-permute-done.35.refs_10_
  236.6 1.8 assemble.1
  (96 shorter events, 22.8 us)
Async XLA Ops:
  5.3 31.0 %copy-start.14 = (bf16[28,128,128]{2,1,0:T(8,128)(2,1)}, bf16[28,128,128]{2,1,0:T(8,128)(2,1)S(1)}, u32[]{:S(2)}) copy-start(bf16[28,128,128]{2,1,0:T(8,128)(2,1)S(1)} %get-tuple-element.55.refs_0_) | copy-start | bytes 2752516
  5.3 43.0 %collective-permute-start.1 = (bf16[2,28,128,128]{3,2,1,0:T(8,128)(2,1)S(1)}, bf16[2,28,128,128]{3,2,1,0:T(8,128)(2,1)S(1)}, u32[]{:S(2)}, u32[]{:S(2)}) collective-permute-start(bf16[2,28,128,128]{3,2,1,0:T(8,128)(2,1)S(1)} %get-tuple-element.51), channel_id=1, source_target_pairs={{0,2},{1,3},{2,0},{3,1},{4,6},{5,7},{6,4},{7,5},{8,10},{9,11},{10,... | collective-permute-start | bytes 5505032 | tf_op jit(solution)/shard_map/ppermute | solution.py:350
  8.3 41.5 %collective-permute-start.2 = (bf16[2,28,128,128]{3,2,1,0:T(8,128)(2,1)S(1)}, bf16[2,28,128,128]{3,2,1,0:T(8,128)(2,1)S(1)}, u32[]{:S(2)}, u32[]{:S(2)}) collective-permute-start(bf16[2,28,128,128]{3,2,1,0:T(8,128)(2,1)S(1)} %get-tuple-element.52), channel_id=1, source_target_pairs={{0,4},{1,5},{2,6},{3,7},{4,0},{5,1},{6,2},{7,3},{8,12},{9,13},{10,... | collective-permute-start | bytes 5505032 | tf_op jit(solution)/shard_map/ppermute | solution.py:350
  9.8 23.6 %collective-permute-start = (bf16[28,128,128]{2,1,0:T(8,128)(2,1)}, bf16[28,128,128]{2,1,0:T(8,128)(2,1)}, u32[]{:S(2)}, u32[]{:S(2)}) collective-permute-start(bf16[28,128,128]{2,1,0:T(8,128)(2,1)} %get-tuple-element.50.refs_0_), channel_id=1, source_target_pairs={{0,8},{1,9},{2,10},{3,11},{4,12},{5,13},{6,14},{7,15},{8,0},{9,1},... | collective-permute-start | bytes 2752520 | tf_op jit(solution)/shard_map/ppermute | solution.py:350
  11.4 39.9 %collective-permute-start.3 = (bf16[28,128,128]{2,1,0:T(8,128)(2,1)S(1)}, bf16[28,128,128]{2,1,0:T(8,128)(2,1)S(1)}, u32[]{:S(2)}, u32[]{:S(2)}) collective-permute-start(bf16[28,128,128]{2,1,0:T(8,128)(2,1)S(1)} %get-tuple-element.55.refs_0_), channel_id=1, source_target_pairs={{8,16},{9,17},{10,18},{11,19},{12,20},{13,21},{14,22},{15,23},{16,... | collective-permute-start | bytes 2752520 | tf_op jit(solution)/shard_map/ppermute | solution.py:350
  12.1 39.2 %collective-permute-start.4 = (bf16[28,128,128]{2,1,0:T(8,128)(2,1)S(1)}, bf16[28,128,128]{2,1,0:T(8,128)(2,1)S(1)}, u32[]{:S(2)}, u32[]{:S(2)}) collective-permute-start(bf16[28,128,128]{2,1,0:T(8,128)(2,1)S(1)} %get-tuple-element.55.refs_0_), channel_id=1, source_target_pairs={{8,0},{9,1},{10,2},{11,3},{12,4},{13,5},{14,6},{15,7},{24,8},{25,9... | collective-permute-start | bytes 2752520 | tf_op jit(solution)/shard_map/ppermute | solution.py:350
  49.8 41.5 %collective-permute-start.5 = (bf16[2,28,128,128]{3,2,1,0:T(8,128)(2,1)S(1)}, bf16[2,28,128,128]{3,2,1,0:T(8,128)(2,1)S(1)}, u32[]{:S(2)}, u32[]{:S(2)}) collective-permute-start(bf16[2,28,128,128]{3,2,1,0:T(8,128)(2,1)S(1)} %pack.3), channel_id=1, source_target_pairs={{0,6},{1,7},{2,4},{3,5},{4,2},{5,3},{6,0},{7,1},{8,14},{9,15},{10,... | collective-permute-start | bytes 5505032 | tf_op jit(solution)/shard_map/ppermute | solution.py:350
  53.6 42.2 %collective-permute-start.11 = (bf16[2,28,128,128]{3,2,1,0:T(8,128)(2,1)}, bf16[2,28,128,128]{3,2,1,0:T(8,128)(2,1)}, u32[]{:S(2)}, u32[]{:S(2)}) collective-permute-start(bf16[2,28,128,128]{3,2,1,0:T(8,128)(2,1)} %get-tuple-element.62.refs_1_), channel_id=1, source_target_pairs={{0,8},{1,9},{2,10},{3,11},{4,12},{5,13},{6,14},{7,15},{8,0},{9,1},... | collective-permute-start | bytes 5505032 | tf_op jit(solution)/shard_map/ppermute | solution.py:350
  58.0 38.6 %collective-permute-start.8 = (bf16[2,28,128,128]{3,2,1,0:T(8,128)(2,1)S(1)}, bf16[2,28,128,128]{3,2,1,0:T(8,128)(2,1)}, u32[]{:S(2)}, u32[]{:S(2)}) collective-permute-start(bf16[2,28,128,128]{3,2,1,0:T(8,128)(2,1)S(1)} %get-tuple-element.59.w_12.refs_1_), channel_id=1, source_target_pairs={{8,16},{9,17},{10,18},{11,19},{12,20},{13,21},{14,22},{15,23},{16,... | collective-permute-start | bytes 5505032 | tf_op jit(solution)/shard_map/ppermute | solution.py:350
  59.8 36.7 %collective-permute-start.6 = (bf16[28,128,128]{2,1,0:T(8,128)(2,1)}, bf16[28,128,128]{2,1,0:T(8,128)(2,1)}, u32[]{:S(2)}, u32[]{:S(2)}) collective-permute-start(bf16[28,128,128]{2,1,0:T(8,128)(2,1)} %get-tuple-element.50.refs_0_), channel_id=1, source_target_pairs={{0,1},{1,0},{2,3},{3,2},{4,5},{5,4},{6,7},{7,6},{8,9},{9,8},{10,11... | collective-permute-start | bytes 2752520 | tf_op jit(solution)/shard_map/ppermute | solution.py:350
  59.9 36.7 %collective-permute-start.7 = (bf16[28,128,128]{2,1,0:T(8,128)(2,1)}, bf16[28,128,128]{2,1,0:T(8,128)(2,1)}, u32[]{:S(2)}, u32[]{:S(2)}) collective-permute-start(bf16[28,128,128]{2,1,0:T(8,128)(2,1)} %collective-permute-done.refs_3_.refs_0_.refs_1_), channel_id=1, source_target_pairs={{0,1},{1,0},{2,3},{3,2},{4,5},{5,4},{6,7},{7,6},{8,9},{9,8},{10,11... | collective-permute-start | bytes 2752520 | tf_op jit(solution)/shard_map/ppermute | solution.py:350
  92.5 17.6 %collective-permute-start.12 = (bf16[2,28,128,128]{3,2,1,0:T(8,128)(2,1)}, bf16[2,28,128,128]{3,2,1,0:T(8,128)(2,1)}, u32[]{:S(2)}, u32[]{:S(2)}) collective-permute-start(bf16[2,28,128,128]{3,2,1,0:T(8,128)(2,1)} %get-tuple-element.62.refs_1_), channel_id=1, source_target_pairs={{0,1},{1,0},{2,3},{3,2},{4,5},{5,4},{6,7},{7,6},{8,9},{9,8},{10,11... | collective-permute-start | bytes 5505032 | tf_op jit(solution)/shard_map/ppermute | solution.py:350
  95.8 14.3 %collective-permute-start.13 = (bf16[2,28,128,128]{3,2,1,0:T(8,128)(2,1)}, bf16[2,28,128,128]{3,2,1,0:T(8,128)(2,1)}, u32[]{:S(2)}, u32[]{:S(2)}) collective-permute-start(bf16[2,28,128,128]{3,2,1,0:T(8,128)(2,1)} %collective-permute-done.11.refs_2_), channel_id=1, source_target_pairs={{0,1},{1,0},{2,3},{3,2},{4,5},{5,4},{6,7},{7,6},{8,9},{9,8},{10,11... | collective-permute-start | bytes 5505032 | tf_op jit(solution)/shard_map/ppermute | solution.py:350
  100.9 9.1 %copy-start.17 = (bf16[28,128,128]{2,1,0:T(8,128)(2,1)}, bf16[28,128,128]{2,1,0:T(8,128)(2,1)S(1)}, u32[]{:S(2)}) copy-start(bf16[28,128,128]{2,1,0:T(8,128)(2,1)S(1)} %get-tuple-element.61.refs_2_) | copy-start | bytes 2752516
  100.9 17.6 %collective-permute-start.10 = (bf16[28,128,128]{2,1,0:T(8,128)(2,1)S(1)}, bf16[28,128,128]{2,1,0:T(8,128)(2,1)S(1)}, u32[]{:S(2)}, u32[]{:S(2)}) collective-permute-start(bf16[28,128,128]{2,1,0:T(8,128)(2,1)S(1)} %get-tuple-element.61.refs_2_), channel_id=1, source_target_pairs={{8,16},{9,17},{10,18},{11,19},{12,20},{13,21},{14,22},{15,23},{16,... | collective-permute-start | bytes 2752520 | tf_op jit(solution)/shard_map/ppermute | solution.py:350
  101.6 26.5 %collective-permute-start.9 = (bf16[28,128,128]{2,1,0:T(8,128)(2,1)}, bf16[28,128,128]{2,1,0:T(8,128)(2,1)}, u32[]{:S(2)}, u32[]{:S(2)}) collective-permute-start(bf16[28,128,128]{2,1,0:T(8,128)(2,1)} %get-tuple-element.60.refs_1_), channel_id=1, source_target_pairs={{0,8},{1,9},{2,10},{3,11},{4,12},{5,13},{6,14},{7,15},{8,0},{9,1},... | collective-permute-start | bytes 2752520 | tf_op jit(solution)/shard_map/ppermute | solution.py:350
  110.0 25.7 %collective-permute-start.14 = (bf16[28,128,128]{2,1,0:T(8,128)(2,1)}, bf16[28,128,128]{2,1,0:T(8,128)(2,1)}, u32[]{:S(2)}, u32[]{:S(2)}) collective-permute-start(bf16[28,128,128]{2,1,0:T(8,128)(2,1)} %get-tuple-element.60.refs_1_), channel_id=1, source_target_pairs={{0,1},{1,0},{2,3},{3,2},{4,5},{5,4},{6,7},{7,6},{8,9},{9,8},{10,11... | collective-permute-start | bytes 2752520 | tf_op jit(solution)/shard_map/ppermute | solution.py:350
  113.3 5.2 %copy-start = (bf16[28,2048,128]{2,1,0:T(8,128)(2,1)}, bf16[28,2048,128]{2,1,0:T(8,128)(2,1)S(1)}, u32[]{:S(2)}) copy-start(bf16[28,2048,128]{2,1,0:T(8,128)(2,1)S(1)} %stack.16.refs_0_) | copy-start | bytes 44040196
  128.1 7.6 %collective-permute-start.15 = (bf16[28,128,128]{2,1,0:T(8,128)(2,1)}, bf16[28,128,128]{2,1,0:T(8,128)(2,1)}, u32[]{:S(2)}, u32[]{:S(2)}) collective-permute-start(bf16[28,128,128]{2,1,0:T(8,128)(2,1)} %collective-permute-done.9.refs_2_.refs_0_), channel_id=1, source_target_pairs={{0,1},{1,0},{2,3},{3,2},{4,5},{5,4},{6,7},{7,6},{8,9},{9,8},{10,11... | collective-permute-start | bytes 2752520 | tf_op jit(solution)/shard_map/ppermute | solution.py:350
  128.1 34.0 %collective-permute-start.16 = (bf16[28,128,128]{2,1,0:T(8,128)(2,1)}, bf16[28,128,128]{2,1,0:T(8,128)(2,1)}, u32[]{:S(2)}, u32[]{:S(2)}) collective-permute-start(bf16[28,128,128]{2,1,0:T(8,128)(2,1)} %get-tuple-element.69), channel_id=1, source_target_pairs={{8,0},{9,1},{10,2},{11,3},{12,4},{13,5},{14,6},{15,7},{24,8},{25,9... | collective-permute-start | bytes 2752520 | tf_op jit(solution)/shard_map/ppermute | solution.py:350
  132.9 15.2 %copy-start.7 = (bf16[28,128,128]{2,1,0:T(8,128)(2,1)S(1)}, bf16[28,128,128]{2,1,0:T(8,128)(2,1)}, u32[]{:S(2)}) copy-start(bf16[28,128,128]{2,1,0:T(8,128)(2,1)} %copy-done.5) | copy-start | bytes 2752516
  132.9 15.2 %copy-start.18 = (bf16[28,128,128]{2,1,0:T(8,128)(2,1)S(1)}, bf16[28,128,128]{2,1,0:T(8,128)(2,1)}, u32[]{:S(2)}) copy-start(bf16[28,128,128]{2,1,0:T(8,128)(2,1)} %copy-done.17) | copy-start | bytes 2752516
  135.6 35.7 %collective-permute-start.20 = (bf16[28,128,128]{2,1,0:T(8,128)(2,1)}, bf16[28,128,128]{2,1,0:T(8,128)(2,1)}, u32[]{:S(2)}, u32[]{:S(2)}) collective-permute-start(bf16[28,128,128]{2,1,0:T(8,128)(2,1)} %get-tuple-element.74), channel_id=1, source_target_pairs={{8,0},{9,1},{10,2},{11,3},{12,4},{13,5},{14,6},{15,7},{24,8},{25,9... | collective-permute-start | bytes 2752520 | tf_op jit(solution)/shard_map/ppermute | solution.py:350
  135.7 5.2 %copy-start.1 = (bf16[28,2048,128]{2,1,0:T(8,128)(2,1)S(1)}, bf16[28,2048,128]{2,1,0:T(8,128)(2,1)}, u32[]{:S(2)}) copy-start(bf16[28,2048,128]{2,1,0:T(8,128)(2,1)} %copy-done) | copy-start | bytes 44040196
  142.9 5.2 %copy-start.2 = (bf16[28,2048,128]{2,1,0:T(8,128)(2,1)}, bf16[28,2048,128]{2,1,0:T(8,128)(2,1)S(1)}, u32[]{:S(2)}) copy-start(bf16[28,2048,128]{2,1,0:T(8,128)(2,1)S(1)} %stack.17.a) | copy-start | bytes 44040196
  155.6 32.2 %copy-start.4 = (bf16[28,2048,128]{2,1,0:T(8,128)(2,1)S(1)}, bf16[28,2048,128]{2,1,0:T(8,128)(2,1)}, u32[]{:S(2)}) copy-start(bf16[28,2048,128]{2,1,0:T(8,128)(2,1)} %copy-done.2) | copy-start | bytes 44040196
  162.2 14.8 %collective-permute-start.17 = (bf16[4,128,512]{2,1,0:T(8,128)(2,1)S(1)}, bf16[4,128,512]{2,1,0:T(8,128)(2,1)S(1)}, u32[]{:S(2)}, u32[]{:S(2)}) collective-permute-start(bf16[4,128,512]{2,1,0:T(8,128)(2,1)S(1)} %get-tuple-element.70), channel_id=1, source_target_pairs={{0,2},{1,3},{2,0},{3,1},{4,6},{5,7},{6,4},{7,5},{8,10},{9,11},{10,... | collective-permute-start | bytes 1572872 | tf_op jit(solution)/shard_map/ppermute | solution.py:350
  162.8 25.0 %collective-permute-start.18 = (bf16[4,128,512]{2,1,0:T(8,128)(2,1)S(1)}, bf16[4,128,512]{2,1,0:T(8,128)(2,1)S(1)}, u32[]{:S(2)}, u32[]{:S(2)}) collective-permute-start(bf16[4,128,512]{2,1,0:T(8,128)(2,1)S(1)} %get-tuple-element.71), channel_id=1, source_target_pairs={{0,4},{1,5},{2,6},{3,7},{4,0},{5,1},{6,2},{7,3},{8,12},{9,13},{10,... | collective-permute-start | bytes 1572872 | tf_op jit(solution)/shard_map/ppermute | solution.py:350
  163.3 24.5 %collective-permute-start.19 = (bf16[4,128,512]{2,1,0:T(8,128)(2,1)S(1)}, bf16[4,128,512]{2,1,0:T(8,128)(2,1)S(1)}, u32[]{:S(2)}, u32[]{:S(2)}) collective-permute-start(bf16[4,128,512]{2,1,0:T(8,128)(2,1)S(1)} %get-tuple-element.72.refs_6_), channel_id=1, source_target_pairs={{0,6},{1,7},{2,4},{3,5},{4,2},{5,3},{6,0},{7,1},{8,14},{9,15},{10,... | collective-permute-start | bytes 1572872 | tf_op jit(solution)/shard_map/ppermute | solution.py:350
  165.7 30.9 %collective-permute-start.27 = (bf16[28,128,128]{2,1,0:T(8,128)(2,1)}, bf16[28,128,128]{2,1,0:T(8,128)(2,1)S(1)}, u32[]{:S(2)}, u32[]{:S(2)}) collective-permute-start(bf16[28,128,128]{2,1,0:T(8,128)(2,1)} %get-tuple-element.83), channel_id=1, source_target_pairs={{8,0},{9,1},{10,2},{11,3},{12,4},{13,5},{14,6},{15,7},{24,8},{25,9... | collective-permute-start | bytes 2752520 | tf_op jit(solution)/shard_map/ppermute | solution.py:350
  193.1 9.3 %collective-permute-start.24 = (bf16[4,128,256]{2,1,0:T(8,128)(2,1)S(1)}, bf16[4,128,256]{2,1,0:T(8,128)(2,1)S(1)}, u32[]{:S(2)}, u32[]{:S(2)}) collective-permute-start(bf16[4,128,256]{2,1,0:T(8,128)(2,1)S(1)} %get-tuple-element.80), channel_id=1, source_target_pairs={{0,2},{1,3},{2,0},{3,1},{4,6},{5,7},{6,4},{7,5},{8,10},{9,11},{10,... | collective-permute-start | bytes 786440 | tf_op jit(solution)/shard_map/ppermute | solution.py:350
  194.5 11.0 %collective-permute-start.25 = (bf16[4,128,256]{2,1,0:T(8,128)(2,1)S(1)}, bf16[4,128,256]{2,1,0:T(8,128)(2,1)S(1)}, u32[]{:S(2)}, u32[]{:S(2)}) collective-permute-start(bf16[4,128,256]{2,1,0:T(8,128)(2,1)S(1)} %get-tuple-element.81), channel_id=1, source_target_pairs={{0,4},{1,5},{2,6},{3,7},{4,0},{5,1},{6,2},{7,3},{8,12},{9,13},{10,... | collective-permute-start | bytes 786440 | tf_op jit(solution)/shard_map/ppermute | solution.py:350
  195.3 19.6 %copy-start.10 = (bf16[28,128,128]{2,1,0:T(8,128)(2,1)S(1)}, bf16[28,128,128]{2,1,0:T(8,128)(2,1)}, u32[]{:S(2)}) copy-start(bf16[28,128,128]{2,1,0:T(8,128)(2,1)} %copy-done.8) | copy-start | bytes 2752516
  195.3 19.6 %copy-start.16 = (bf16[28,128,128]{2,1,0:T(8,128)(2,1)S(1)}, bf16[28,128,128]{2,1,0:T(8,128)(2,1)}, u32[]{:S(2)}) copy-start(bf16[28,128,128]{2,1,0:T(8,128)(2,1)} %copy-done.14) | copy-start | bytes 2752516
  195.3 19.6 %copy-start.19 = (bf16[28,128,128]{2,1,0:T(8,128)(2,1)S(1)}, bf16[28,128,128]{2,1,0:T(8,128)(2,1)}, u32[]{:S(2)}) copy-start(bf16[28,128,128]{2,1,0:T(8,128)(2,1)} %copy-done.17) | copy-start | bytes 2752516
  195.3 11.8 %collective-permute-start.26 = (bf16[4,128,256]{2,1,0:T(8,128)(2,1)S(1)}, bf16[4,128,256]{2,1,0:T(8,128)(2,1)S(1)}, u32[]{:S(2)}, u32[]{:S(2)}) collective-permute-start(bf16[4,128,256]{2,1,0:T(8,128)(2,1)S(1)} %get-tuple-element.82), channel_id=1, source_target_pairs={{0,6},{1,7},{2,4},{3,5},{4,2},{5,3},{6,0},{7,1},{8,14},{9,15},{10,... | collective-permute-start | bytes 786440 | tf_op jit(solution)/shard_map/ppermute | solution.py:350
  211.4 10.3 %collective-permute-start.31 = (bf16[4,128,256]{2,1,0:T(8,128)(2,1)S(1)}, bf16[4,128,256]{2,1,0:T(8,128)(2,1)S(1)}, u32[]{:S(2)}, u32[]{:S(2)}) collective-permute-start(bf16[4,128,256]{2,1,0:T(8,128)(2,1)S(1)} %get-tuple-element.89), channel_id=1, source_target_pairs={{0,2},{1,3},{2,0},{3,1},{4,6},{5,7},{6,4},{7,5},{8,10},{9,11},{10,... | collective-permute-start | bytes 786440 | tf_op jit(solution)/shard_map/ppermute | solution.py:350
  212.2 12.1 %collective-permute-start.32 = (bf16[4,128,256]{2,1,0:T(8,128)(2,1)S(1)}, bf16[4,128,256]{2,1,0:T(8,128)(2,1)S(1)}, u32[]{:S(2)}, u32[]{:S(2)}) collective-permute-start(bf16[4,128,256]{2,1,0:T(8,128)(2,1)S(1)} %get-tuple-element.90), channel_id=1, source_target_pairs={{0,4},{1,5},{2,6},{3,7},{4,0},{5,1},{6,2},{7,3},{8,12},{9,13},{10,... | collective-permute-start | bytes 786440 | tf_op jit(solution)/shard_map/ppermute | solution.py:350
  213.1 13.4 %collective-permute-start.33 = (bf16[4,128,256]{2,1,0:T(8,128)(2,1)S(1)}, bf16[4,128,256]{2,1,0:T(8,128)(2,1)}, u32[]{:S(2)}, u32[]{:S(2)}) collective-permute-start(bf16[4,128,256]{2,1,0:T(8,128)(2,1)S(1)} %get-tuple-element.84.refs_3_), channel_id=1, source_target_pairs={{0,6},{1,7},{2,4},{3,5},{4,2},{5,3},{6,0},{7,1},{8,14},{9,15},{10,... | collective-permute-start | bytes 786440 | tf_op jit(solution)/shard_map/ppermute | solution.py:350
  218.0 12.0 %collective-permute-start.21 = (bf16[128,512]{1,0:T(8,128)(2,1)S(1)}, bf16[128,512]{1,0:T(8,128)(2,1)S(1)}, u32[]{:S(2)}, u32[]{:S(2)}) collective-permute-start(bf16[128,512]{1,0:T(8,128)(2,1)S(1)} %get-tuple-element.77), channel_id=1, source_target_pairs={{0,1},{1,0},{2,3},{3,2},{4,5},{5,4},{6,7},{7,6},{8,9},{9,8},{10,11... | collective-permute-start | bytes 393224 | tf_op jit(solution)/shard_map/ppermute | solution.py:350
  218.1 12.8 %collective-permute-start.22 = (bf16[128,512]{1,0:T(8,128)(2,1)S(1)}, bf16[128,512]{1,0:T(8,128)(2,1)S(1)}, u32[]{:S(2)}, u32[]{:S(2)}) collective-permute-start(bf16[128,512]{1,0:T(8,128)(2,1)S(1)} %get-tuple-element.78), channel_id=1, source_target_pairs={{0,8},{1,9},{2,10},{3,11},{4,12},{5,13},{6,14},{7,15},{8,0},{9,1},... | collective-permute-start | bytes 393224 | tf_op jit(solution)/shard_map/ppermute | solution.py:350
  221.7 10.0 %collective-permute-start.23 = (bf16[128,512]{1,0:T(8,128)(2,1)S(1)}, bf16[128,512]{1,0:T(8,128)(2,1)S(1)}, u32[]{:S(2)}, u32[]{:S(2)}) collective-permute-start(bf16[128,512]{1,0:T(8,128)(2,1)S(1)} %get-tuple-element.79), channel_id=1, source_target_pairs={{0,9},{1,8},{2,11},{3,10},{4,13},{5,12},{6,15},{7,14},{8,1},{9,0},... | collective-permute-start | bytes 393224 | tf_op jit(solution)/shard_map/ppermute | solution.py:350
  225.0 7.2 %collective-permute-start.28 = (bf16[128,256]{1,0:T(8,128)(2,1)S(1)}, bf16[128,256]{1,0:T(8,128)(2,1)S(1)}, u32[]{:S(2)}, u32[]{:S(2)}) collective-permute-start(bf16[128,256]{1,0:T(8,128)(2,1)S(1)} %get-tuple-element.86), channel_id=1, source_target_pairs={{0,1},{1,0},{2,3},{3,2},{4,5},{5,4},{6,7},{7,6},{8,9},{9,8},{10,11... | collective-permute-start | bytes 196616 | tf_op jit(solution)/shard_map/ppermute | solution.py:350
  226.5 6.7 %collective-permute-start.29 = (bf16[128,256]{1,0:T(8,128)(2,1)S(1)}, bf16[128,256]{1,0:T(8,128)(2,1)S(1)}, u32[]{:S(2)}, u32[]{:S(2)}) collective-permute-start(bf16[128,256]{1,0:T(8,128)(2,1)S(1)} %get-tuple-element.87), channel_id=1, source_target_pairs={{0,8},{1,9},{2,10},{3,11},{4,12},{5,13},{6,14},{7,15},{8,0},{9,1},... | collective-permute-start | bytes 196616 | tf_op jit(solution)/shard_map/ppermute | solution.py:350
  230.0 4.2 %collective-permute-start.30 = (bf16[128,256]{1,0:T(8,128)(2,1)S(1)}, bf16[128,256]{1,0:T(8,128)(2,1)S(1)}, u32[]{:S(2)}, u32[]{:S(2)}) collective-permute-start(bf16[128,256]{1,0:T(8,128)(2,1)S(1)} %get-tuple-element.88), channel_id=1, source_target_pairs={{0,9},{1,8},{2,11},{3,10},{4,13},{5,12},{6,15},{7,14},{8,1},{9,0},... | collective-permute-start | bytes 196616 | tf_op jit(solution)/shard_map/ppermute | solution.py:350
  230.9 3.4 %collective-permute-start.34 = (bf16[128,256]{1,0:T(8,128)(2,1)S(1)}, bf16[128,256]{1,0:T(8,128)(2,1)S(1)}, u32[]{:S(2)}, u32[]{:S(2)}) collective-permute-start(bf16[128,256]{1,0:T(8,128)(2,1)S(1)} %get-tuple-element.92), channel_id=1, source_target_pairs={{0,1},{1,0},{2,3},{3,2},{4,5},{5,4},{6,7},{7,6},{8,9},{9,8},{10,11... | collective-permute-start | bytes 196616 | tf_op jit(solution)/shard_map/ppermute | solution.py:350
  231.7 4.9 %collective-permute-start.35 = (bf16[128,256]{1,0:T(8,128)(2,1)S(1)}, bf16[128,256]{1,0:T(8,128)(2,1)S(1)}, u32[]{:S(2)}, u32[]{:S(2)}) collective-permute-start(bf16[128,256]{1,0:T(8,128)(2,1)S(1)} %get-tuple-element.93), channel_id=1, source_target_pairs={{0,8},{1,9},{2,10},{3,11},{4,12},{5,13},{6,14},{7,15},{8,0},{9,1},... | collective-permute-start | bytes 196616 | tf_op jit(solution)/shard_map/ppermute | solution.py:350
  232.2 4.4 %collective-permute-start.36 = (bf16[128,256]{1,0:T(8,128)(2,1)S(1)}, bf16[128,256]{1,0:T(8,128)(2,1)S(1)}, u32[]{:S(2)}, u32[]{:S(2)}) collective-permute-start(bf16[128,256]{1,0:T(8,128)(2,1)S(1)} %get-tuple-element.94), channel_id=1, source_target_pairs={{0,9},{1,8},{2,11},{3,10},{4,13},{5,12},{6,15},{7,14},{8,1},{9,0},... | collective-permute-start | bytes 196616 | tf_op jit(solution)/shard_map/ppermute | solution.py:350
  (13 other events, 21.2 us)

commit v6 on v5

--- a/solution.py
+++ b/solution.py
@@ -37,12 +37,11 @@
             w[tile] = weight[pl.ds(tile * LANES, LANES)]
 
 
-def pack(plane, steps, gate, up, weight, after=()):
+def pack(plane, steps, gate, up, weight, apart, after=()):
     rows, columns = gate.shape[0], weight.shape[1]
     tiles = gate.shape[1] // (4 * LANES)
     grid = 4
     share = tiles // grid
-    apart = int(steps[0] == 0)
     single = jax.ShapeDtypeStruct((tiles, rows, LANES), jnp.bfloat16)
     double = jax.ShapeDtypeStruct((2, tiles, rows, LANES), jnp.bfloat16)
     single_spec = pl.BlockSpec((share, rows, LANES), lambda at, plane: (at, 0, 0))
@@ -119,11 +118,11 @@
     )(one, two, *after)
 
 
-def reorder_kernel(count, order_ref, packed, w_12, *refs):
+def reorder_kernel(count, order_ref, w_12, w_3, *refs):
     outs, (held, in_sem, out_sem) = refs[-3 - count : -3], refs[-3:]
     into = [
         pltpu.make_async_copy(source, held.at[at], in_sem.at[at])
-        for at, source in enumerate((packed.at[0], w_12.at[0], w_12.at[1], packed.at[1]))
+        for at, source in enumerate((w_12.at[0], w_12.at[1], w_3))
     ]
     out_of = [
         pltpu.make_async_copy(held.at[order_ref[at]], out, out_sem.at[at])
@@ -139,27 +138,29 @@
         copy.wait()
 
 
-def reorder(order, packed, w_12, after):
-    shape, count = packed.shape[1:], order.shape[0]
+def reorder(order, w_12, w_3, after=()):
+    shape, count = w_3.shape, order.shape[0]
     return pl.pallas_call(
         functools.partial(reorder_kernel, count),
-        out_shape=[jax.ShapeDtypeStruct(shape, packed.dtype)] * count,
+        out_shape=[jax.ShapeDtypeStruct(shape, w_3.dtype)] * count,
         in_specs=[pl.BlockSpec(memory_space=pltpu.SMEM)]
         + [pl.BlockSpec(memory_space=pl.ANY)] * (2 + len(after)),
         out_specs=[pl.BlockSpec(memory_space=pl.ANY)] * count,
         scratch_shapes=[
-            pltpu.VMEM((4,) + shape, packed.dtype),
-            pltpu.SemaphoreType.DMA((4,)),
+            pltpu.VMEM((3,) + shape, w_3.dtype),
+            pltpu.SemaphoreType.DMA((3,)),
             pltpu.SemaphoreType.DMA((count,)),
         ],
         compiler_params=pltpu.CompilerParams(vmem_limit_bytes=LIMIT),
-        cost_estimate=pl.CostEstimate(flops=0, bytes_accessed=8 * packed.size, transcendentals=0),
+        cost_estimate=pl.CostEstimate(
+            flops=0, bytes_accessed=2 * (3 + count) * w_3.size, transcendentals=0
+        ),
         name="reorder",
-    )(order, packed, w_12, *after)
+    )(order, w_12, w_3, *after)
 
 
 def stack_kernel(first, count, *refs):
-    sources, stack_ref, sem = refs[-2 - count : -2], refs[-2], refs[-1]
+    sources, (stack_ref, token, sem) = refs[-3 - count : -3], refs[-3:]
     rows = sources[0].shape[-2]
     copies, at = [], 0
     for source in sources:
@@ -170,6 +171,7 @@
             at += 1
     for copy in copies:
         copy.start()
+    token[...] = jnp.zeros_like(token)
     for copy in copies:
         copy.wait()
 
@@ -181,10 +183,13 @@
     count = sum(block.size for block in blocks) // (tiles * rows * lanes)
     return pl.pallas_call(
         functools.partial(stack_kernel, first, len(blocks)),
-        out_shape=pltpu.VMEM(shape, blocks[0].dtype),
+        out_shape=[
+            pltpu.VMEM(shape, blocks[0].dtype),
+            jax.ShapeDtypeStruct((8, LANES), jnp.float32),
+        ],
         in_specs=[pl.BlockSpec(memory_space=pltpu.VMEM)] * len(held)
         + [pl.BlockSpec(memory_space=pl.ANY)] * len(blocks),
-        out_specs=pl.BlockSpec(memory_space=pltpu.VMEM),
+        out_specs=[pl.BlockSpec(memory_space=pltpu.VMEM)] * 2,
         scratch_shapes=[pltpu.SemaphoreType.DMA((count,))],
         input_output_aliases={0: 0} if held else {},
         compiler_params=pltpu.CompilerParams(vmem_limit_bytes=LIMIT),
@@ -361,36 +366,31 @@
     def to_pair(array):
         return send(array, flip(n, PAIR))
 
-    a_0, w_0, packed_1, packed_2 = pack(at_plane, (0, 1, 2), *inputs)
+    a_0, w_0, packed_1, packed_2 = pack(at_plane, (0, 1, 2), *inputs, 1)
     pair_0, mid_0, next_0 = to_pair(a_0), to_mid(w_0), to_next(w_0)
     got_1 = send(packed_1, flip(n, PLANE))
     got_2 = send(packed_2, flip(n, 2 * PLANE))
 
-    (packed_3,) = pack(at_plane, (3,), *inputs, after=(pair_0,))
-    packed_3, got_1, got_2 = lax.optimization_barrier((packed_3, got_1, got_2))
-    got_3 = send(packed_3, flip(n, 3 * PLANE))
-    a_12, w_12 = unpack_pair(got_1, got_2, after=(pair_0, mid_0, next_0))
+    sent_a, sent_w = pack(at_plane, (3,), *inputs, 1, after=(pair_0,))
+    sent_a, sent_w, got_1, got_2 = lax.optimization_barrier((sent_a, sent_w, got_1, got_2))
+    a_3, w_3 = send(sent_a, flip(n, 3 * PLANE)), send(sent_w, flip(n, 3 * PLANE))
+    core_0, core_pair_0 = to_core(a_0), to_core(pair_0)
+    a_12, w_12 = unpack_pair(got_1, got_2, (mid_0, next_0, core_0, core_pair_0))
     pair_12, mid_12 = to_pair(a_12), to_mid(w_12)
-    core_0, core_pair_0 = to_core(a_0), to_core(pair_0)
-
-    order = jnp.array([[1, 2, 3], [1, 3, 2], [2, 3, 1], [3, 2, 1]], jnp.int32)[plane]
-    a_12, got_3 = lax.optimization_barrier((a_12, got_3))
-    known = jnp.array([0, 3], jnp.int32)
-    a_3, w_3, ordered_1 = reorder(
-        jnp.concatenate([known, order[:1]]), got_3, w_12, after=(core_0, core_pair_0, mid_12)
-    )
+
+    order = jnp.array([[0, 1, 2], [0, 2, 1], [1, 2, 0], [2, 1, 0]], jnp.int32)[plane]
+    rows_stack, token = stack(0, [a_0, pair_0, core_0, core_pair_0])
+    a_3, w_3, a_12, mid_12, _ = lax.optimization_barrier((a_3, w_3, a_12, mid_12, token))
     pair_3, mid_3 = to_pair(a_3), to_mid(w_3)
     core_12, core_pair_12 = to_core(a_12), to_core(pair_12)
-    rows_stack = stack(0, [a_0, pair_0, core_0, core_pair_0])
-    rows_stack = stack(4, [a_12, pair_12, core_12, core_pair_12], rows_stack)
-    pair_3, mid_3, rows_stack = lax.optimization_barrier((pair_3, mid_3, rows_stack))
-    ordered_2, ordered_3 = reorder(
-        order[1:], got_3, w_12, after=(pair_3, mid_3, core_12, core_pair_12)
-    )
+    (ordered_1,) = reorder(order[:1], w_12, w_3)
+    rows_stack, token = stack(4, [a_12, pair_12, core_12, core_pair_12], rows_stack)
+    ordered_2, ordered_3 = reorder(order[1:], w_12, w_3, after=(pair_3, mid_3, token))
     next_1, next_2, next_3 = to_next(ordered_1), to_next(ordered_2), to_next(ordered_3)
+    pair_3, token, _ = lax.optimization_barrier((pair_3, token, ordered_1))
     core_3, core_pair_3 = to_core(a_3), to_core(pair_3)
 
-    rows_stack = stack(12, [a_3, pair_3, core_3, core_pair_3], rows_stack)
+    rows_stack, _ = stack(12, [a_3, pair_3, core_3, core_pair_3], rows_stack)
     places = [(0, 2, 1, 3), (4, 8, 6, 10), (5, 9, 7, 11), (12, 14, 13, 15)]
     w_own = [(w_0, None), (w_12, 0), (w_12, 1), (w_3, None)]
     w_mid = [(mid_0, None), (mid_12, 0), (mid_12, 1), (mid_3, None)]
@@ -416,6 +416,7 @@
             block = send(summed[piece], flip(n, mask)) if mask else summed[piece]
             fixed = ((piece >> 1) << 4) | (half << 3) | (piece & 1)
             pieces.append((block, fixed, start, half == 0))
+        return summed[0]
 
     own = totals_of(mid, [w_own, w_mid], ([3, 1, 2], [0]))
     own[1], own[2], own[3], next_1 = lax.optimization_barrier((*own[1:], next_1))
@@ -423,10 +424,10 @@
     first, one, two, three = [(block, None) for block in (next_0, next_1, next_2, next_3)]
     w_low = [[first, one], [one, first], [one, two], [one, two]]
     w_high = [[two, three], [two, three], [first, three], [three, first]]
-    low = totals_of(at_plane, w_low, ([3, 1, 2, 0],), tuple(own_sums))
+    low = totals_of(at_plane, w_low, ([3, 1, 2, 0],), (*own_sums, own[0]))
     low_sums = across_plane(low)
-    spread(own, own_sums, 0, 0, (low[0],))
-    high = totals_of(at_plane, w_high, ([3, 1, 2], [0]), tuple(low_sums))
+    summed = spread(own, own_sums, 0, 0, (low[0],))
+    high = totals_of(at_plane, w_high, ([3, 1, 2], [0]), (*low_sums, summed))
     high_sums = across_plane(high)
     spread(low, low_sums, 1, 0, (high[0],))
     spread(high, high_sums, 1, 2)

time: 239 us -> 264 us (1.10)
  starting transfers between devices: 51.5 us -> 73.4 us
  waiting for transfers between devices: 106 us -> 110 us
  Pallas kernels: 47.6 us -> 44.1 us
    ppermute x37 -> x38, starting transfers between devices: 51.5 us -> 73.4 us  [send(): return lax.ppermute(array, 'fsdp', perm=perm)]
    ppermute x37 -> x38, waiting for transfers between devices: 106 us -> 110 us  [send(): return lax.ppermute(array, 'fsdp', perm=perm)]
    unnamed x48 -> x66, local copies, waits for them, and re-layouts: 32 us -> 34.5 us
  transfers between devices with their start and end apart: 37 -> 38, of which waited for: 14 -> 16; matrix products, arithmetic and copies ran while one was open for 0% -> 0% of each run, Pallas kernels for 15% -> 12%
where the time goes in v6:
time: 264 us
  waiting for transfers between devices  110 us (42%)
  starting transfers between devices  73.4 us (28%)
  Pallas kernels  44.1 us (17%)
  local copies, waits for them, and re-layouts  35.3 us (13%)
    ppermute x38, waiting for transfers between devices, send(): return lax.ppermute(array, 'fsdp', perm=perm)  110 us
    ppermute x38, starting transfers between devices, send(): return lax.ppermute(array, 'fsdp', perm=perm)  73.4 us
    unnamed x66, local copies, waits for them, and re-layouts  34.5 us
    pallas_call x5, Pallas kernels, product(): pl.pallas_call(functools.partial(product_kernel, [places[group] for group...  21.2 us
    pallas_call x2, Pallas kernels, pack(): pl.pallas_call(functools.partial(pack_kernel, apart, len(steps)), out_sha...  7.62 us
    pallas_call x3, Pallas kernels, stack(): pl.pallas_call(functools.partial(stack_kernel, first, len(blocks)), out_s...  6.99 us
  transfers between devices with their start and end apart: 38, of which 16 were waited for; matrix products, arithmetic and copies ran while one was open for 0% of the time, Pallas kernels for 12%

profile of v6, /device:TPU:0, one launch (start us, length us, event | category | flops | bytes accessed | tf_op | source)
XLA Modules:
  0.0 263.6 jit_solution(13943358563654592953)
XLA Ops:
  0.0 4.8 %pack.2 = (bf16[28,128,128]{2,1,0:T(8,128)(2,1)S(1)}, bf16[28,128,128]{2,1,0:T(8,128)(2,1)S(1)}, bf16[2,28,128,128]{3,2,1,0:T(8,128)(2,1)S(1)}, bf16[2,28,128,128]{3,2,1,0:T(8,128)(2,1)S(1)}) custom-call(s32[1]{0:T(128)} %bitcast.3.plane_ref.choice_ref, bf16[128,14336]{1,0:T(8,128)(2,1)} %refs_0_.3, bf16[128,14336]{1,0:T(8,128)(2,1)} %refs_1_.3, ...), custom_call_target="tpu_custom_call" | custom-call | bytes 13762560 | tf_op jit(solution)/shard_map/pack/pallas_call | solution.py:62
  4.8 3.0 %collective-permute-start.3 = (bf16[2,28,128,128]{3,2,1,0:T(8,128)(2,1)S(1)}, bf16[2,28,128,128]{3,2,1,0:T(8,128)(2,1)S(1)}, u32[]{:S(2)}, u32[]{:S(2)}) collective-permute-start(bf16[2,28,128,128]{3,2,1,0:T(8,128)(2,1)S(1)} %get-tuple-element.58), channel_id=1, source_target_pairs={{0,2},{1,3},{2,0},{3,1},{4,6},{5,7},{6,4},{7,5},{8,10},{9,11},{10,... | collective-permute-start | bytes 5505032 | tf_op jit(solution)/shard_map/ppermute | solution.py:355
  7.9 1.5 collective-permute-start.4
  9.4 1.6 collective-permute-start
  11.7 19.2 %collective-permute-done.refs_1_.refs_3_ = bf16[28,128,128]{2,1,0:T(8,128)(2,1)S(1)} collective-permute-done((bf16[28,128,128]{2,1,0:T(8,128)(2,1)S(1)}, bf16[28,128,128]{2,1,0:T(8,128)(2,1)S(1)}, u32[]{:S(2)}, u32[]{:S(2)}) %collective-permute-start) | collective-permute-done | bytes 917536 | tf_op jit(solution)/shard_map/ppermute | solution.py:355
  30.9 2.6 collective-permute-start.8
  33.5 14.4 %collective-permute-done.3.one = bf16[2,28,128,128]{3,2,1,0:T(8,128)(2,1)S(1)} collective-permute-done((bf16[2,28,128,128]{3,2,1,0:T(8,128)(2,1)S(1)}, bf16[2,28,128,128]{3,2,1,0:T(8,128)(2,1)S(1)}, u32[]{:S(2)}, u32[]{:S(2)}) %collective-permute-start.3) | collective-permute-done | bytes 1835040 | tf_op jit(solution)/shard_map/ppermute | solution.py:355
  47.9 2.8 %pack.3 = (bf16[28,128,128]{2,1,0:T(8,128)(2,1)S(1)}, bf16[28,128,128]{2,1,0:T(8,128)(2,1)S(1)}) custom-call(s32[1]{0:T(128)} %bitcast.3.plane_ref.choice_ref, bf16[128,14336]{1,0:T(8,128)(2,1)} %refs_0_.3, bf16[128,14336]{1,0:T(8,128)(2,1)} %refs_1_.3, bf16[14336,128]{1,0:T(8,128)(2,1)} %refs_2_.3, ...), custom_call_target="tpu_custom_call" | custom-call | bytes 4587520 | tf_op jit(solution)/shard_map/pack/pallas_call | solution.py:62
  51.7 2.2 unpack_pair.1
  54.7 8.0 %collective-permute-start.10 = (bf16[2,28,128,128]{3,2,1,0:T(8,128)(2,1)}, bf16[2,28,128,128]{3,2,1,0:T(8,128)(2,1)}, u32[]{:S(2)}, u32[]{:S(2)}) collective-permute-start(bf16[2,28,128,128]{3,2,1,0:T(8,128)(2,1)} %get-tuple-element.67.refs_1_), channel_id=1, source_target_pairs={{0,8},{1,9},{2,10},{3,11},{4,12},{5,13},{6,14},{7,15},{8,0},{9,1},... | collective-permute-start | bytes 5505032 | tf_op jit(solution)/shard_map/ppermute | solution.py:355
  63.2 2.4 collective-permute-start.6
  65.6 21.4 %collective-permute-done.5.refs_1_ = bf16[28,128,128]{2,1,0:T(8,128)(2,1)} collective-permute-done((bf16[28,128,128]{2,1,0:T(8,128)(2,1)S(1)}, bf16[28,128,128]{2,1,0:T(8,128)(2,1)}, u32[]{:S(2)}, u32[]{:S(2)}) %collective-permute-start.5) | collective-permute-done | bytes 917536 | tf_op jit(solution)/shard_map/ppermute | solution.py:355
  87.0 17.7 %collective-permute-done.6.w_3.refs_2_ = bf16[28,128,128]{2,1,0:T(8,128)(2,1)S(1)} collective-permute-done((bf16[28,128,128]{2,1,0:T(8,128)(2,1)S(1)}, bf16[28,128,128]{2,1,0:T(8,128)(2,1)S(1)}, u32[]{:S(2)}, u32[]{:S(2)}) %collective-permute-start.6) | collective-permute-done | bytes 917536 | tf_op jit(solution)/shard_map/ppermute | solution.py:355
  104.7 1.2 copy-done.8
  107.4 1.2 copy-done.11
  108.6 1.2 copy-done.13
  109.8 1.2 copy-done.15
  113.3 1.7 collective-permute-start.16
  114.9 1.7 reorder.2
  116.6 3.2 %stack.16 = (bf16[28,2048,128]{2,1,0:T(8,128)(2,1)S(1)}, f32[8,128]{1,0:T(8,128)S(1)}) custom-call(bf16[28,2048,128]{2,1,0:T(8,128)(2,1)S(1)} %get-tuple-element.55.refs_0_, bf16[2,28,128,128]{3,2,1,0:T(8,128)(2,1)} %get-tuple-element.67.refs_1_, bf16[2,28,128,128]{3,2,1,0:T(8,128)(2,1)} %collective-permute-done.10.refs_2_, ...), custom_call_target="tpu_custom_call", output_to_operand_aliasing={{0}: (0, {})} | custom-call | bytes 14680064 | tf_op jit(solution)/shard_map/stack/pallas_call | solution.py:184
  119.8 5.2 %copy-done = bf16[28,2048,128]{2,1,0:T(8,128)(2,1)} copy-done((bf16[28,2048,128]{2,1,0:T(8,128)(2,1)}, bf16[28,2048,128]{2,1,0:T(8,128)(2,1)S(1)}, u32[]{:S(2)}) %copy-start) | copy-done | bytes 14680088
  125.0 4.0 %collective-permute-done.13.refs_2_.refs_0_ = bf16[28,128,128]{2,1,0:T(8,128)(2,1)} collective-permute-done((bf16[28,128,128]{2,1,0:T(8,128)(2,1)}, bf16[28,128,128]{2,1,0:T(8,128)(2,1)}, u32[]{:S(2)}, u32[]{:S(2)}) %collective-permute-start.13) | collective-permute-done | bytes 917536 | tf_op jit(solution)/shard_map/ppermute | solution.py:355
  129.3 2.2 reorder.3
  132.5 29.9 %collective-permute-start.21 = (bf16[28,128,128]{2,1,0:T(8,128)(2,1)}, bf16[28,128,128]{2,1,0:T(8,128)(2,1)}, u32[]{:S(2)}, u32[]{:S(2)}) collective-permute-start(bf16[28,128,128]{2,1,0:T(8,128)(2,1)} %get-tuple-element.82), channel_id=1, source_target_pairs={{8,0},{9,1},{10,2},{11,3},{12,4},{13,5},{14,6},{15,7},{24,8},{25,9... | collective-permute-start | bytes 2752520 | tf_op jit(solution)/shard_map/ppermute | solution.py:355
  162.4 5.2 %copy-done.1 = bf16[28,2048,128]{2,1,0:T(8,128)(2,1)S(1)} copy-done((bf16[28,2048,128]{2,1,0:T(8,128)(2,1)S(1)}, bf16[28,2048,128]{2,1,0:T(8,128)(2,1)}, u32[]{:S(2)}) %copy-start.1) | copy-done | bytes 14680088
  167.6 2.8 %stack.17 = (bf16[28,2048,128]{2,1,0:T(8,128)(2,1)S(1)}, f32[8,128]{1,0:T(8,128)}) custom-call(bf16[28,2048,128]{2,1,0:T(8,128)(2,1)S(1)} %copy-done.1, bf16[28,128,128]{2,1,0:T(8,128)(2,1)} %collective-permute-done.5.refs_1_, bf16[28,128,128]{2,1,0:T(8,128)(2,1)} %collective-permute-done.13.refs_2_.refs_0_, ...), custom_call_target="tpu_custom_call", output_to_operand_aliasing={{0}: (0, {})} | custom-call | bytes 7340032 | tf_op jit(solution)/shard_map/stack/pallas_call | solution.py:184
  170.4 5.2 %copy-done.2 = bf16[28,2048,128]{2,1,0:T(8,128)(2,1)} copy-done((bf16[28,2048,128]{2,1,0:T(8,128)(2,1)}, bf16[28,2048,128]{2,1,0:T(8,128)(2,1)S(1)}, u32[]{:S(2)}) %copy-start.2) | copy-done | bytes 14680088
  175.6 5.2 %copy-done.3 = bf16[28,2048,128]{2,1,0:T(8,128)(2,1)S(1)} copy-done((bf16[28,2048,128]{2,1,0:T(8,128)(2,1)S(1)}, bf16[28,2048,128]{2,1,0:T(8,128)(2,1)}, u32[]{:S(2)}) %copy-start.3) | copy-done | bytes 14680088
  180.8 6.5 %product.5 = (bf16[4,128,512]{2,1,0:T(8,128)(2,1)S(1)}, bf16[4,128,512]{2,1,0:T(8,128)(2,1)}, bf16[4,128,512]{2,1,0:T(8,128)(2,1)S(1)}) custom-call(s32[1]{0:T(128)} %bitcast.2.choice_ref, bf16[28,2048,128]{2,1,0:T(8,128)(2,1)S(1)} %copy-done.3, bf16[28,128,128]{2,1,0:T(8,128)(2,1)S(1)} %copy-done.17, ...), custom_call_target="tpu_custom_call" | custom-call | flops 5637144576 | bytes 14680064 | tf_op jit(solution)/shard_map/product/pallas_call | solution.py:264
  188.4 2.4 collective-permute-start.20
  190.9 1.3 collective-permute-start.28
  192.2 2.8 %product.6.refs_6_.own = f32[4,128,512]{2,1,0:T(8,128)S(1)} custom-call(s32[1]{0:T(128)} %bitcast.2.choice_ref, bf16[28,2048,128]{2,1,0:T(8,128)(2,1)S(1)} %copy-done.3, bf16[28,128,128]{2,1,0:T(8,128)(2,1)S(1)} %copy-done.18, bf16[2,28,128,128]{3,2,1,0:T(8,128)(2,1)S(1)} %get-tuple-element.66.w_12.refs_1_, ...), custom_call_target="tpu_custom_call" | custom-call | flops 1879048192 | bytes 7340032 | tf_op jit(solution)/shard_map/product/pallas_call | solution.py:264
  194.9 7.5 %collective-permute-done.18.refs_3_.one = bf16[4,128,512]{2,1,0:T(8,128)(2,1)S(1)} collective-permute-done((bf16[4,128,512]{2,1,0:T(8,128)(2,1)}, bf16[4,128,512]{2,1,0:T(8,128)(2,1)S(1)}, u32[]{:S(2)}, u32[]{:S(2)}) %collective-permute-start.18) | collective-permute-done | bytes 524320 | tf_op jit(solution)/shard_map/ppermute | solution.py:355
  203.3 8.8 %collective-permute-done.20.refs_5_.three = bf16[4,128,512]{2,1,0:T(8,128)(2,1)S(1)} collective-permute-done((bf16[4,128,512]{2,1,0:T(8,128)(2,1)S(1)}, bf16[4,128,512]{2,1,0:T(8,128)(2,1)S(1)}, u32[]{:S(2)}, u32[]{:S(2)}) %collective-permute-start.20) | collective-permute-done | bytes 524320 | tf_op jit(solution)/shard_map/ppermute | solution.py:355
  216.2 5.3 %product.7 = (bf16[4,128,256]{2,1,0:T(8,128)(2,1)S(1)}, bf16[4,128,256]{2,1,0:T(8,128)(2,1)S(1)}, bf16[4,128,256]{2,1,0:T(8,128)(2,1)S(1)}, f32[4,128,256]{2,1,0:T(8,128)S(1)}) custom-call(s32[1]{0:T(128)} %bitcast.3.plane_ref.choice_ref, bf16[28,2048,128]{2,1,0:T(8,128)(2,1)S(1)} %bitcast.9, bf16[28,128,128]{2,1,0:T(8,128)(2,1)S(1)} %copy-done.5, ...), custom_call_target="tpu_custom_call" | custom-call | flops 3758096384 | bytes 16515072 | tf_op jit(solution)/shard_map/product/pallas_call | solution.py:264
  221.5 2.2 collective-permute-start.25
  223.7 1.5 collective-permute-start.27
  226.4 4.5 %collective-permute-done.25.refs_3_.one = bf16[4,128,256]{2,1,0:T(8,128)(2,1)S(1)} collective-permute-done((bf16[4,128,256]{2,1,0:T(8,128)(2,1)S(1)}, bf16[4,128,256]{2,1,0:T(8,128)(2,1)S(1)}, u32[]{:S(2)}, u32[]{:S(2)}) %collective-permute-start.25) | collective-permute-done | bytes 262176 | tf_op jit(solution)/shard_map/ppermute | solution.py:355
  230.9 4.5 %collective-permute-done.26.refs_4_.two = bf16[4,128,256]{2,1,0:T(8,128)(2,1)S(1)} collective-permute-done((bf16[4,128,256]{2,1,0:T(8,128)(2,1)S(1)}, bf16[4,128,256]{2,1,0:T(8,128)(2,1)S(1)}, u32[]{:S(2)}, u32[]{:S(2)}) %collective-permute-start.26) | collective-permute-done | bytes 262176 | tf_op jit(solution)/shard_map/ppermute | solution.py:355
  235.5 1.2 copy-done.20
  236.6 4.3 %product.8 = (bf16[4,128,256]{2,1,0:T(8,128)(2,1)S(1)}, bf16[4,128,256]{2,1,0:T(8,128)(2,1)S(1)}, bf16[4,128,256]{2,1,0:T(8,128)(2,1)S(1)}) custom-call(s32[1]{0:T(128)} %bitcast.3.plane_ref.choice_ref, bf16[28,2048,128]{2,1,0:T(8,128)(2,1)S(1)} %bitcast.9, bf16[28,128,128]{2,1,0:T(8,128)(2,1)} %collective-permute-done.21.refs_2_.refs_0_, ...), custom_call_target="tpu_custom_call" | custom-call | flops 2818572288 | bytes 12845056 | tf_op jit(solution)/shard_map/product/pallas_call | solution.py:264
  241.8 2.6 %collective-permute-start.34 = (bf16[4,128,256]{2,1,0:T(8,128)(2,1)S(1)}, bf16[4,128,256]{2,1,0:T(8,128)(2,1)S(1)}, u32[]{:S(2)}, u32[]{:S(2)}) collective-permute-start(bf16[4,128,256]{2,1,0:T(8,128)(2,1)S(1)} %get-tuple-element.92.refs_3_), channel_id=1, source_target_pairs={{0,6},{1,7},{2,4},{3,5},{4,2},{5,3},{6,0},{7,1},{8,14},{9,15},{10,... | collective-permute-start | bytes 786440 | tf_op jit(solution)/shard_map/ppermute | solution.py:355
  244.5 1.9 collective-permute-start.23
  246.4 2.7 %collective-permute-done.32.one = bf16[4,128,256]{2,1,0:T(8,128)(2,1)S(1)} collective-permute-done((bf16[4,128,256]{2,1,0:T(8,128)(2,1)S(1)}, bf16[4,128,256]{2,1,0:T(8,128)(2,1)S(1)}, u32[]{:S(2)}, u32[]{:S(2)}) %collective-permute-start.32) | collective-permute-done | bytes 262176 | tf_op jit(solution)/shard_map/ppermute | solution.py:355
  249.0 2.3 product.9.refs_0_.own
  252.0 1.9 collective-permute-start.29
  258.9 2.7 %collective-permute-done.36.refs_10_ = bf16[128,256]{1,0:T(8,128)(2,1)S(1)} collective-permute-done((bf16[128,256]{1,0:T(8,128)(2,1)S(1)}, bf16[128,256]{1,0:T(8,128)(2,1)S(1)}, u32[]{:S(2)}, u32[]{:S(2)}) %collective-permute-start.36) | collective-permute-done | bytes 65568 | tf_op jit(solution)/shard_map/ppermute | solution.py:355
  261.8 1.8 assemble.1
  (115 shorter events, 22.1 us)
Async XLA Ops:
  4.8 45.9 %copy-start.16 = (bf16[28,128,128]{2,1,0:T(8,128)(2,1)}, bf16[28,128,128]{2,1,0:T(8,128)(2,1)S(1)}, u32[]{:S(2)}) copy-start(bf16[28,128,128]{2,1,0:T(8,128)(2,1)S(1)} %get-tuple-element.64.refs_0_) | copy-start | bytes 2752516
  4.8 45.9 %copy-start.26 = (bf16[28,128,128]{2,1,0:T(8,128)(2,1)}, bf16[28,128,128]{2,1,0:T(8,128)(2,1)S(1)}, u32[]{:S(2)}) copy-start(bf16[28,128,128]{2,1,0:T(8,128)(2,1)S(1)} %get-tuple-element.54.refs_0_) | copy-start | bytes 2752516
  4.8 43.0 %collective-permute-start.3 = (bf16[2,28,128,128]{3,2,1,0:T(8,128)(2,1)S(1)}, bf16[2,28,128,128]{3,2,1,0:T(8,128)(2,1)S(1)}, u32[]{:S(2)}, u32[]{:S(2)}) collective-permute-start(bf16[2,28,128,128]{3,2,1,0:T(8,128)(2,1)S(1)} %get-tuple-element.58), channel_id=1, source_target_pairs={{0,2},{1,3},{2,0},{3,1},{4,6},{5,7},{6,4},{7,5},{8,10},{9,11},{10,... | collective-permute-start | bytes 5505032 | tf_op jit(solution)/shard_map/ppermute | solution.py:355
  7.9 42.9 %collective-permute-start.4 = (bf16[2,28,128,128]{3,2,1,0:T(8,128)(2,1)S(1)}, bf16[2,28,128,128]{3,2,1,0:T(8,128)(2,1)S(1)}, u32[]{:S(2)}, u32[]{:S(2)}) collective-permute-start(bf16[2,28,128,128]{3,2,1,0:T(8,128)(2,1)S(1)} %get-tuple-element.59), channel_id=1, source_target_pairs={{0,4},{1,5},{2,6},{3,7},{4,0},{5,1},{6,2},{7,3},{8,12},{9,13},{10,... | collective-permute-start | bytes 5505032 | tf_op jit(solution)/shard_map/ppermute | solution.py:355
  9.4 21.5 %collective-permute-start = (bf16[28,128,128]{2,1,0:T(8,128)(2,1)S(1)}, bf16[28,128,128]{2,1,0:T(8,128)(2,1)S(1)}, u32[]{:S(2)}, u32[]{:S(2)}) collective-permute-start(bf16[28,128,128]{2,1,0:T(8,128)(2,1)S(1)} %get-tuple-element.54.refs_0_), channel_id=1, source_target_pairs={{0,8},{1,9},{2,10},{3,11},{4,12},{5,13},{6,14},{7,15},{8,0},{9,1},... | collective-permute-start | bytes 2752520 | tf_op jit(solution)/shard_map/ppermute | solution.py:355
  11.0 39.8 %collective-permute-start.1 = (bf16[28,128,128]{2,1,0:T(8,128)(2,1)S(1)}, bf16[28,128,128]{2,1,0:T(8,128)(2,1)S(1)}, u32[]{:S(2)}, u32[]{:S(2)}) collective-permute-start(bf16[28,128,128]{2,1,0:T(8,128)(2,1)S(1)} %get-tuple-element.54.refs_0_), channel_id=1, source_target_pairs={{0,1},{1,0},{2,3},{3,2},{4,5},{5,4},{6,7},{7,6},{8,9},{9,8},{10,11... | collective-permute-start | bytes 2752520 | tf_op jit(solution)/shard_map/ppermute | solution.py:355
  11.0 39.8 %collective-permute-start.7 = (bf16[28,128,128]{2,1,0:T(8,128)(2,1)S(1)}, bf16[28,128,128]{2,1,0:T(8,128)(2,1)S(1)}, u32[]{:S(2)}, u32[]{:S(2)}) collective-permute-start(bf16[28,128,128]{2,1,0:T(8,128)(2,1)S(1)} %get-tuple-element.64.refs_0_), channel_id=1, source_target_pairs={{8,16},{9,17},{10,18},{11,19},{12,20},{13,21},{14,22},{15,23},{16,... | collective-permute-start | bytes 2752520 | tf_op jit(solution)/shard_map/ppermute | solution.py:355
  30.9 19.8 %copy-start.10 = (bf16[28,128,128]{2,1,0:T(8,128)(2,1)}, bf16[28,128,128]{2,1,0:T(8,128)(2,1)S(1)}, u32[]{:S(2)}) copy-start(bf16[28,128,128]{2,1,0:T(8,128)(2,1)S(1)} %collective-permute-done.refs_1_.refs_3_) | copy-start | bytes 2752516
  30.9 20.8 %collective-permute-start.8 = (bf16[28,128,128]{2,1,0:T(8,128)(2,1)S(1)}, bf16[28,128,128]{2,1,0:T(8,128)(2,1)S(1)}, u32[]{:S(2)}, u32[]{:S(2)}) collective-permute-start(bf16[28,128,128]{2,1,0:T(8,128)(2,1)S(1)} %get-tuple-element.64.refs_0_), channel_id=1, source_target_pairs={{8,0},{9,1},{10,2},{11,3},{12,4},{13,5},{14,6},{15,7},{24,8},{25,9... | collective-permute-start | bytes 2752520 | tf_op jit(solution)/shard_map/ppermute | solution.py:355
  47.9 3.8 %collective-permute-start.2 = (bf16[28,128,128]{2,1,0:T(8,128)(2,1)S(1)}, bf16[28,128,128]{2,1,0:T(8,128)(2,1)S(1)}, u32[]{:S(2)}, u32[]{:S(2)}) collective-permute-start(bf16[28,128,128]{2,1,0:T(8,128)(2,1)S(1)} %collective-permute-done.refs_1_.refs_3_), channel_id=1, source_target_pairs={{0,1},{1,0},{2,3},{3,2},{4,5},{5,4},{6,7},{7,6},{8,9},{9,8},{10,11... | collective-permute-start | bytes 2752520 | tf_op jit(solution)/shard_map/ppermute | solution.py:355
  53.9 50.7 %collective-permute-start.9 = (bf16[2,28,128,128]{3,2,1,0:T(8,128)(2,1)S(1)}, bf16[2,28,128,128]{3,2,1,0:T(8,128)(2,1)S(1)}, u32[]{:S(2)}, u32[]{:S(2)}) collective-permute-start(bf16[2,28,128,128]{3,2,1,0:T(8,128)(2,1)S(1)} %get-tuple-element.66.w_12.refs_1_), channel_id=1, source_target_pairs={{8,16},{9,17},{10,18},{11,19},{12,20},{13,21},{14,22},{15,23},{16,... | collective-permute-start | bytes 5505032 | tf_op jit(solution)/shard_map/ppermute | solution.py:355
  54.7 51.2 %collective-permute-start.10 = (bf16[2,28,128,128]{3,2,1,0:T(8,128)(2,1)}, bf16[2,28,128,128]{3,2,1,0:T(8,128)(2,1)}, u32[]{:S(2)}, u32[]{:S(2)}) collective-permute-start(bf16[2,28,128,128]{3,2,1,0:T(8,128)(2,1)} %get-tuple-element.67.refs_1_), channel_id=1, source_target_pairs={{0,8},{1,9},{2,10},{3,11},{4,12},{5,13},{6,14},{7,15},{8,0},{9,1},... | collective-permute-start | bytes 5505032 | tf_op jit(solution)/shard_map/ppermute | solution.py:355
  62.7 24.3 %collective-permute-start.5 = (bf16[28,128,128]{2,1,0:T(8,128)(2,1)S(1)}, bf16[28,128,128]{2,1,0:T(8,128)(2,1)}, u32[]{:S(2)}, u32[]{:S(2)}) collective-permute-start(bf16[28,128,128]{2,1,0:T(8,128)(2,1)S(1)} %get-tuple-element.60), channel_id=1, source_target_pairs={{0,6},{1,7},{2,4},{3,5},{4,2},{5,3},{6,0},{7,1},{8,14},{9,15},{10,... | collective-permute-start | bytes 2752520 | tf_op jit(solution)/shard_map/ppermute | solution.py:355
  63.2 41.5 %collective-permute-start.6 = (bf16[28,128,128]{2,1,0:T(8,128)(2,1)S(1)}, bf16[28,128,128]{2,1,0:T(8,128)(2,1)S(1)}, u32[]{:S(2)}, u32[]{:S(2)}) collective-permute-start(bf16[28,128,128]{2,1,0:T(8,128)(2,1)S(1)} %get-tuple-element.61), channel_id=1, source_target_pairs={{0,6},{1,7},{2,4},{3,5},{4,2},{5,3},{6,0},{7,1},{8,14},{9,15},{10,... | collective-permute-start | bytes 2752520 | tf_op jit(solution)/shard_map/ppermute | solution.py:355
  105.9 10.7 %collective-permute-start.11 = (bf16[2,28,128,128]{3,2,1,0:T(8,128)(2,1)}, bf16[2,28,128,128]{3,2,1,0:T(8,128)(2,1)}, u32[]{:S(2)}, u32[]{:S(2)}) collective-permute-start(bf16[2,28,128,128]{3,2,1,0:T(8,128)(2,1)} %get-tuple-element.67.refs_1_), channel_id=1, source_target_pairs={{0,1},{1,0},{2,3},{3,2},{4,5},{5,4},{6,7},{7,6},{8,9},{9,8},{10,11... | collective-permute-start | bytes 5505032 | tf_op jit(solution)/shard_map/ppermute | solution.py:355
  105.9 10.7 %collective-permute-start.12 = (bf16[2,28,128,128]{3,2,1,0:T(8,128)(2,1)}, bf16[2,28,128,128]{3,2,1,0:T(8,128)(2,1)}, u32[]{:S(2)}, u32[]{:S(2)}) collective-permute-start(bf16[2,28,128,128]{3,2,1,0:T(8,128)(2,1)} %collective-permute-done.10.refs_2_), channel_id=1, source_target_pairs={{0,1},{1,0},{2,3},{3,2},{4,5},{5,4},{6,7},{7,6},{8,9},{9,8},{10,11... | collective-permute-start | bytes 5505032 | tf_op jit(solution)/shard_map/ppermute | solution.py:355
  106.4 22.6 %collective-permute-start.13 = (bf16[28,128,128]{2,1,0:T(8,128)(2,1)}, bf16[28,128,128]{2,1,0:T(8,128)(2,1)}, u32[]{:S(2)}, u32[]{:S(2)}) collective-permute-start(bf16[28,128,128]{2,1,0:T(8,128)(2,1)} %collective-permute-done.5.refs_1_), channel_id=1, source_target_pairs={{0,8},{1,9},{2,10},{3,11},{4,12},{5,13},{6,14},{7,15},{8,0},{9,1},... | collective-permute-start | bytes 2752520 | tf_op jit(solution)/shard_map/ppermute | solution.py:355
  113.2 49.2 %collective-permute-start.14 = (bf16[28,128,128]{2,1,0:T(8,128)(2,1)}, bf16[28,128,128]{2,1,0:T(8,128)(2,1)}, u32[]{:S(2)}, u32[]{:S(2)}) collective-permute-start(bf16[28,128,128]{2,1,0:T(8,128)(2,1)} %collective-permute-done.5.refs_1_), channel_id=1, source_target_pairs={{0,1},{1,0},{2,3},{3,2},{4,5},{5,4},{6,7},{7,6},{8,9},{9,8},{10,11... | collective-permute-start | bytes 2752520 | tf_op jit(solution)/shard_map/ppermute | solution.py:355
  113.3 16.1 %collective-permute-start.16 = (bf16[28,128,128]{2,1,0:T(8,128)(2,1)S(1)}, bf16[28,128,128]{2,1,0:T(8,128)(2,1)}, u32[]{:S(2)}, u32[]{:S(2)}) collective-permute-start(bf16[28,128,128]{2,1,0:T(8,128)(2,1)S(1)} %collective-permute-done.6.w_3.refs_2_), channel_id=1, source_target_pairs={{8,16},{9,17},{10,18},{11,19},{12,20},{13,21},{14,22},{15,23},{16,... | collective-permute-start | bytes 2752520 | tf_op jit(solution)/shard_map/ppermute | solution.py:355
  129.0 33.5 %collective-permute-start.15 = (bf16[28,128,128]{2,1,0:T(8,128)(2,1)}, bf16[28,128,128]{2,1,0:T(8,128)(2,1)}, u32[]{:S(2)}, u32[]{:S(2)}) collective-permute-start(bf16[28,128,128]{2,1,0:T(8,128)(2,1)} %collective-permute-done.13.refs_2_.refs_0_), channel_id=1, source_target_pairs={{0,1},{1,0},{2,3},{3,2},{4,5},{5,4},{6,7},{7,6},{8,9},{9,8},{10,11... | collective-permute-start | bytes 2752520 | tf_op jit(solution)/shard_map/ppermute | solution.py:355
  129.0 58.4 %collective-permute-start.17 = (bf16[28,128,128]{2,1,0:T(8,128)(2,1)}, bf16[28,128,128]{2,1,0:T(8,128)(2,1)}, u32[]{:S(2)}, u32[]{:S(2)}) collective-permute-start(bf16[28,128,128]{2,1,0:T(8,128)(2,1)} %reorder.2), channel_id=1, source_target_pairs={{8,0},{9,1},{10,2},{11,3},{12,4},{13,5},{14,6},{15,7},{24,8},{25,9... | collective-permute-start | bytes 2752520 | tf_op jit(solution)/shard_map/ppermute | solution.py:355
  132.5 62.4 %collective-permute-start.21 = (bf16[28,128,128]{2,1,0:T(8,128)(2,1)}, bf16[28,128,128]{2,1,0:T(8,128)(2,1)}, u32[]{:S(2)}, u32[]{:S(2)}) collective-permute-start(bf16[28,128,128]{2,1,0:T(8,128)(2,1)} %get-tuple-element.82), channel_id=1, source_target_pairs={{8,0},{9,1},{10,2},{11,3},{12,4},{13,5},{14,6},{15,7},{24,8},{25,9... | collective-permute-start | bytes 2752520 | tf_op jit(solution)/shard_map/ppermute | solution.py:355
  167.6 8.0 %copy-start.17 = (bf16[28,128,128]{2,1,0:T(8,128)(2,1)S(1)}, bf16[28,128,128]{2,1,0:T(8,128)(2,1)}, u32[]{:S(2)}) copy-start(bf16[28,128,128]{2,1,0:T(8,128)(2,1)} %copy-done.16) | copy-start | bytes 2752516
  180.8 11.4 %copy-start.18 = (bf16[28,128,128]{2,1,0:T(8,128)(2,1)S(1)}, bf16[28,128,128]{2,1,0:T(8,128)(2,1)}, u32[]{:S(2)}) copy-start(bf16[28,128,128]{2,1,0:T(8,128)(2,1)} %copy-done.16) | copy-start | bytes 2752516
  180.8 32.2 %slice-start = ((s8[14680064]{0:T(1024)(128)(4,1)}), s8[4194304]{0:T(1024)(128)(4,1)S(1)}, s32[]{:S(2)}) async-start(s8[14680064]{0:T(1024)(128)(4,1)} %bitcast.8), calls=%async_computation | async-start | bytes 8388608
  180.8 32.2 %slice-start.1 = ((s8[14680064]{0:T(1024)(128)(4,1)}), s8[4194304]{0:T(1024)(128)(4,1)S(1)}, s32[]{:S(2)}) async-start(s8[14680064]{0:T(1024)(128)(4,1)} %bitcast.8), calls=%async_computation.1 | async-start | bytes 8388608
  187.3 15.1 %collective-permute-start.18 = (bf16[4,128,512]{2,1,0:T(8,128)(2,1)}, bf16[4,128,512]{2,1,0:T(8,128)(2,1)S(1)}, u32[]{:S(2)}, u32[]{:S(2)}) collective-permute-start(bf16[4,128,512]{2,1,0:T(8,128)(2,1)} %get-tuple-element.78), channel_id=1, source_target_pairs={{0,2},{1,3},{2,0},{3,1},{4,6},{5,7},{6,4},{7,5},{8,10},{9,11},{10,... | collective-permute-start | bytes 1572872 | tf_op jit(solution)/shard_map/ppermute | solution.py:355
  187.9 14.6 %collective-permute-start.19 = (bf16[4,128,512]{2,1,0:T(8,128)(2,1)S(1)}, bf16[4,128,512]{2,1,0:T(8,128)(2,1)S(1)}, u32[]{:S(2)}, u32[]{:S(2)}) collective-permute-start(bf16[4,128,512]{2,1,0:T(8,128)(2,1)S(1)} %get-tuple-element.79), channel_id=1, source_target_pairs={{0,4},{1,5},{2,6},{3,7},{4,0},{5,1},{6,2},{7,3},{8,12},{9,13},{10,... | collective-permute-start | bytes 1572872 | tf_op jit(solution)/shard_map/ppermute | solution.py:355
  188.4 23.7 %collective-permute-start.20 = (bf16[4,128,512]{2,1,0:T(8,128)(2,1)S(1)}, bf16[4,128,512]{2,1,0:T(8,128)(2,1)S(1)}, u32[]{:S(2)}, u32[]{:S(2)}) collective-permute-start(bf16[4,128,512]{2,1,0:T(8,128)(2,1)S(1)} %get-tuple-element.80.refs_6_), channel_id=1, source_target_pairs={{0,6},{1,7},{2,4},{3,5},{4,2},{5,3},{6,0},{7,1},{8,14},{9,15},{10,... | collective-permute-start | bytes 1572872 | tf_op jit(solution)/shard_map/ppermute | solution.py:355
  190.9 22.1 %slice-start.2 = ((s8[14680064]{0:T(1024)(128)(4,1)}), s8[4194304]{0:T(1024)(128)(4,1)S(1)}, s32[]{:S(2)}) async-start(s8[14680064]{0:T(1024)(128)(4,1)} %bitcast.8), calls=%async_computation.2 | async-start | bytes 8388608
  190.9 22.1 %slice-start.3 = ((s8[14680064]{0:T(1024)(128)(4,1)}), s8[2097152]{0:T(1024)(128)(4,1)S(1)}, s32[]{:S(2)}) async-start(s8[14680064]{0:T(1024)(128)(4,1)} %bitcast.8), calls=%async_computation.3 | async-start | bytes 4194304
  190.9 34.6 %collective-permute-start.28 = (bf16[28,128,128]{2,1,0:T(8,128)(2,1)}, bf16[28,128,128]{2,1,0:T(8,128)(2,1)S(1)}, u32[]{:S(2)}, u32[]{:S(2)}) collective-permute-start(bf16[28,128,128]{2,1,0:T(8,128)(2,1)} %copy-done.28), channel_id=1, source_target_pairs={{8,0},{9,1},{10,2},{11,3},{12,4},{13,5},{14,6},{15,7},{24,8},{25,9... | collective-permute-start | bytes 2752520 | tf_op jit(solution)/shard_map/ppermute | solution.py:355
  221.5 9.4 %collective-permute-start.25 = (bf16[4,128,256]{2,1,0:T(8,128)(2,1)S(1)}, bf16[4,128,256]{2,1,0:T(8,128)(2,1)S(1)}, u32[]{:S(2)}, u32[]{:S(2)}) collective-permute-start(bf16[4,128,256]{2,1,0:T(8,128)(2,1)S(1)} %get-tuple-element.88), channel_id=1, source_target_pairs={{0,2},{1,3},{2,0},{3,1},{4,6},{5,7},{6,4},{7,5},{8,10},{9,11},{10,... | collective-permute-start | bytes 786440 | tf_op jit(solution)/shard_map/ppermute | solution.py:355
  223.7 11.7 %collective-permute-start.26 = (bf16[4,128,256]{2,1,0:T(8,128)(2,1)S(1)}, bf16[4,128,256]{2,1,0:T(8,128)(2,1)S(1)}, u32[]{:S(2)}, u32[]{:S(2)}) collective-permute-start(bf16[4,128,256]{2,1,0:T(8,128)(2,1)S(1)} %get-tuple-element.89), channel_id=1, source_target_pairs={{0,4},{1,5},{2,6},{3,7},{4,0},{5,1},{6,2},{7,3},{8,12},{9,13},{10,... | collective-permute-start | bytes 786440 | tf_op jit(solution)/shard_map/ppermute | solution.py:355
  223.7 11.7 %collective-permute-start.27 = (bf16[4,128,256]{2,1,0:T(8,128)(2,1)S(1)}, bf16[4,128,256]{2,1,0:T(8,128)(2,1)S(1)}, u32[]{:S(2)}, u32[]{:S(2)}) collective-permute-start(bf16[4,128,256]{2,1,0:T(8,128)(2,1)S(1)} %get-tuple-element.90), channel_id=1, source_target_pairs={{0,6},{1,7},{2,4},{3,5},{4,2},{5,3},{6,0},{7,1},{8,14},{9,15},{10,... | collective-permute-start | bytes 786440 | tf_op jit(solution)/shard_map/ppermute | solution.py:355
  236.6 12.4 %copy-start.21 = (bf16[28,128,128]{2,1,0:T(8,128)(2,1)S(1)}, bf16[28,128,128]{2,1,0:T(8,128)(2,1)}, u32[]{:S(2)}) copy-start(bf16[28,128,128]{2,1,0:T(8,128)(2,1)} %copy-done.19) | copy-start | bytes 2752516
  240.9 8.1 %collective-permute-start.32 = (bf16[4,128,256]{2,1,0:T(8,128)(2,1)S(1)}, bf16[4,128,256]{2,1,0:T(8,128)(2,1)S(1)}, u32[]{:S(2)}, u32[]{:S(2)}) collective-permute-start(bf16[4,128,256]{2,1,0:T(8,128)(2,1)S(1)} %get-tuple-element.97), channel_id=1, source_target_pairs={{0,2},{1,3},{2,0},{3,1},{4,6},{5,7},{6,4},{7,5},{8,10},{9,11},{10,... | collective-permute-start | bytes 786440 | tf_op jit(solution)/shard_map/ppermute | solution.py:355
  241.3 10.8 %collective-permute-start.33 = (bf16[4,128,256]{2,1,0:T(8,128)(2,1)S(1)}, bf16[4,128,256]{2,1,0:T(8,128)(2,1)S(1)}, u32[]{:S(2)}, u32[]{:S(2)}) collective-permute-start(bf16[4,128,256]{2,1,0:T(8,128)(2,1)S(1)} %get-tuple-element.98), channel_id=1, source_target_pairs={{0,4},{1,5},{2,6},{3,7},{4,0},{5,1},{6,2},{7,3},{8,12},{9,13},{10,... | collective-permute-start | bytes 786440 | tf_op jit(solution)/shard_map/ppermute | solution.py:355
  241.8 12.1 %collective-permute-start.34 = (bf16[4,128,256]{2,1,0:T(8,128)(2,1)S(1)}, bf16[4,128,256]{2,1,0:T(8,128)(2,1)S(1)}, u32[]{:S(2)}, u32[]{:S(2)}) collective-permute-start(bf16[4,128,256]{2,1,0:T(8,128)(2,1)S(1)} %get-tuple-element.92.refs_3_), channel_id=1, source_target_pairs={{0,6},{1,7},{2,4},{3,5},{4,2},{5,3},{6,0},{7,1},{8,14},{9,15},{10,... | collective-permute-start | bytes 786440 | tf_op jit(solution)/shard_map/ppermute | solution.py:355
  244.5 10.0 %collective-permute-start.22 = (bf16[128,512]{1,0:T(8,128)(2,1)S(1)}, bf16[128,512]{1,0:T(8,128)(2,1)S(1)}, u32[]{:S(2)}, u32[]{:S(2)}) collective-permute-start(bf16[128,512]{1,0:T(8,128)(2,1)S(1)} %get-tuple-element.85), channel_id=1, source_target_pairs={{0,1},{1,0},{2,3},{3,2},{4,5},{5,4},{6,7},{7,6},{8,9},{9,8},{10,11... | collective-permute-start | bytes 393224 | tf_op jit(solution)/shard_map/ppermute | solution.py:355
  244.5 11.1 %collective-permute-start.23 = (bf16[128,512]{1,0:T(8,128)(2,1)S(1)}, bf16[128,512]{1,0:T(8,128)(2,1)S(1)}, u32[]{:S(2)}, u32[]{:S(2)}) collective-permute-start(bf16[128,512]{1,0:T(8,128)(2,1)S(1)} %get-tuple-element.86), channel_id=1, source_target_pairs={{0,8},{1,9},{2,10},{3,11},{4,12},{5,13},{6,14},{7,15},{8,0},{9,1},... | collective-permute-start | bytes 393224 | tf_op jit(solution)/shard_map/ppermute | solution.py:355
  249.0 7.3 %collective-permute-start.24 = (bf16[128,512]{1,0:T(8,128)(2,1)S(1)}, bf16[128,512]{1,0:T(8,128)(2,1)S(1)}, u32[]{:S(2)}, u32[]{:S(2)}) collective-permute-start(bf16[128,512]{1,0:T(8,128)(2,1)S(1)} %get-tuple-element.87), channel_id=1, source_target_pairs={{0,9},{1,8},{2,11},{3,10},{4,13},{5,12},{6,15},{7,14},{8,1},{9,0},... | collective-permute-start | bytes 393224 | tf_op jit(solution)/shard_map/ppermute | solution.py:355
  252.0 4.6 %collective-permute-start.29 = (bf16[128,256]{1,0:T(8,128)(2,1)S(1)}, bf16[128,256]{1,0:T(8,128)(2,1)S(1)}, u32[]{:S(2)}, u32[]{:S(2)}) collective-permute-start(bf16[128,256]{1,0:T(8,128)(2,1)S(1)} %get-tuple-element.94), channel_id=1, source_target_pairs={{0,1},{1,0},{2,3},{3,2},{4,5},{5,4},{6,7},{7,6},{8,9},{9,8},{10,11... | collective-permute-start | bytes 196616 | tf_op jit(solution)/shard_map/ppermute | solution.py:355
  254.0 5.0 %collective-permute-start.30 = (bf16[128,256]{1,0:T(8,128)(2,1)S(1)}, bf16[128,256]{1,0:T(8,128)(2,1)S(1)}, u32[]{:S(2)}, u32[]{:S(2)}) collective-permute-start(bf16[128,256]{1,0:T(8,128)(2,1)S(1)} %get-tuple-element.95), channel_id=1, source_target_pairs={{0,8},{1,9},{2,10},{3,11},{4,12},{5,13},{6,14},{7,15},{8,0},{9,1},... | collective-permute-start | bytes 196616 | tf_op jit(solution)/shard_map/ppermute | solution.py:355
  254.5 4.5 %collective-permute-start.31 = (bf16[128,256]{1,0:T(8,128)(2,1)S(1)}, bf16[128,256]{1,0:T(8,128)(2,1)S(1)}, u32[]{:S(2)}, u32[]{:S(2)}) collective-permute-start(bf16[128,256]{1,0:T(8,128)(2,1)S(1)} %get-tuple-element.96), channel_id=1, source_target_pairs={{0,9},{1,8},{2,11},{3,10},{4,13},{5,12},{6,15},{7,14},{8,1},{9,0},... | collective-permute-start | bytes 196616 | tf_op jit(solution)/shard_map/ppermute | solution.py:355
  255.6 3.3 %collective-permute-start.35 = (bf16[128,256]{1,0:T(8,128)(2,1)S(1)}, bf16[128,256]{1,0:T(8,128)(2,1)S(1)}, u32[]{:S(2)}, u32[]{:S(2)}) collective-permute-start(bf16[128,256]{1,0:T(8,128)(2,1)S(1)} %get-tuple-element.100), channel_id=1, source_target_pairs={{0,1},{1,0},{2,3},{3,2},{4,5},{5,4},{6,7},{7,6},{8,9},{9,8},{10,11... | collective-permute-start | bytes 196616 | tf_op jit(solution)/shard_map/ppermute | solution.py:355
  256.3 5.3 %collective-permute-start.36 = (bf16[128,256]{1,0:T(8,128)(2,1)S(1)}, bf16[128,256]{1,0:T(8,128)(2,1)S(1)}, u32[]{:S(2)}, u32[]{:S(2)}) collective-permute-start(bf16[128,256]{1,0:T(8,128)(2,1)S(1)} %get-tuple-element.101), channel_id=1, source_target_pairs={{0,8},{1,9},{2,10},{3,11},{4,12},{5,13},{6,14},{7,15},{8,0},{9,1},... | collective-permute-start | bytes 196616 | tf_op jit(solution)/shard_map/ppermute | solution.py:355
  256.7 5.1 %collective-permute-start.37 = (bf16[128,256]{1,0:T(8,128)(2,1)S(1)}, bf16[128,256]{1,0:T(8,128)(2,1)S(1)}, u32[]{:S(2)}, u32[]{:S(2)}) collective-permute-start(bf16[128,256]{1,0:T(8,128)(2,1)S(1)} %get-tuple-element.102), channel_id=1, source_target_pairs={{0,9},{1,8},{2,11},{3,10},{4,13},{5,12},{6,15},{7,14},{8,1},{9,0},... | collective-permute-start | bytes 196616 | tf_op jit(solution)/shard_map/ppermute | solution.py:355
  (23 other events, 61.2 us)

commit v7 on v5

--- a/solution.py
+++ b/solution.py
@@ -8,7 +8,7 @@
 from jax.sharding import PartitionSpec as P
 
 CORE, PLANE, PAIR = 1, 2, 8
-LIMIT = 24 * 1024 * 1024
+LIMIT = 10 * 1024 * 1024
 LANES = 128
 
 
@@ -416,6 +416,7 @@
             block = send(summed[piece], flip(n, mask)) if mask else summed[piece]
             fixed = ((piece >> 1) << 4) | (half << 3) | (piece & 1)
             pieces.append((block, fixed, start, half == 0))
+        return summed[0]
 
     own = totals_of(mid, [w_own, w_mid], ([3, 1, 2], [0]))
     own[1], own[2], own[3], next_1 = lax.optimization_barrier((*own[1:], next_1))
@@ -423,10 +424,10 @@
     first, one, two, three = [(block, None) for block in (next_0, next_1, next_2, next_3)]
     w_low = [[first, one], [one, first], [one, two], [one, two]]
     w_high = [[two, three], [two, three], [first, three], [three, first]]
-    low = totals_of(at_plane, w_low, ([3, 1, 2, 0],), tuple(own_sums))
+    low = totals_of(at_plane, w_low, ([3, 1, 2, 0],), (*own_sums, own[0]))
     low_sums = across_plane(low)
-    spread(own, own_sums, 0, 0, (low[0],))
-    high = totals_of(at_plane, w_high, ([3, 1, 2], [0]), tuple(low_sums))
+    summed = spread(own, own_sums, 0, 0, (low[0],))
+    high = totals_of(at_plane, w_high, ([3, 1, 2], [0]), (*low_sums, summed))
     high_sums = across_plane(high)
     spread(low, low_sums, 1, 0, (high[0],))
     spread(high, high_sums, 1, 2)

time: 239 us -> 231 us (0.967)
  local copies, waits for them, and re-layouts: 32.8 us -> 27.8 us
  Pallas kernels: 47.6 us -> 44.2 us
  waiting for transfers between devices: 106 us -> 109 us
    unnamed x48 -> x40, local copies, waits for them, and re-layouts: 32 us -> 27 us
    ppermute x37, waiting for transfers between devices: 106 us -> 109 us  [send(): return lax.ppermute(array, 'fsdp', perm=perm)]
  transfers between devices with their start and end apart: 37 -> 37, of which waited for: 14 -> 17; matrix products, arithmetic and copies ran while one was open for 0% -> 0% of each run, Pallas kernels for 15% -> 15%
where the time goes in v7:
time: 231 us
  waiting for transfers between devices  109 us (47%)
  starting transfers between devices  49.6 us (21%)
  Pallas kernels  44.2 us (19%)
  local copies, waits for them, and re-layouts  27.8 us (12%)
    ppermute x37, waiting for transfers between devices, send(): return lax.ppermute(array, 'fsdp', perm=perm)  109 us
    ppermute x37, starting transfers between devices, send(): return lax.ppermute(array, 'fsdp', perm=perm)  49.6 us
    unnamed x40, local copies, waits for them, and re-layouts  27 us
    pallas_call x5, Pallas kernels, product(): pl.pallas_call(functools.partial(product_kernel, [places[group] for group...  19.5 us
    pallas_call x2, Pallas kernels, pack(): pl.pallas_call(functools.partial(pack_kernel, apart, len(steps)), out_sha...  8.16 us
    pallas_call x3, Pallas kernels, stack(): pl.pallas_call(functools.partial(stack_kernel, first, len(blocks)), out_s...  7.25 us
    pallas_call x2, Pallas kernels, reorder(): pl.pallas_call(functools.partial(reorder_kernel, count), out_shape=[jax.S...  4.76 us
  transfers between devices with their start and end apart: 37, of which 17 were waited for; matrix products, arithmetic and copies ran while one was open for 0% of the time, Pallas kernels for 15%

profile of v7, /device:TPU:0, one launch (start us, length us, event | category | flops | bytes accessed | tf_op | source)
XLA Modules:
  0.0 230.9 jit_solution(7744993771402148568)
XLA Ops:
  0.0 5.3 %pack.2 = (bf16[28,128,128]{2,1,0:T(8,128)(2,1)}, bf16[28,128,128]{2,1,0:T(8,128)(2,1)S(1)}, bf16[2,28,128,128]{3,2,1,0:T(8,128)(2,1)S(1)}, bf16[2,28,128,128]{3,2,1,0:T(8,128)(2,1)S(1)}) custom-call(s32[1]{0:T(128)} %bitcast.4.plane_ref.choice_ref, bf16[128,14336]{1,0:T(8,128)(2,1)} %refs_0_.3, bf16[128,14336]{1,0:T(8,128)(2,1)} %refs_1_.3, ...), custom_call_target="tpu_custom_call" | custom-call | bytes 13762560 | tf_op jit(solution)/shard_map/pack/pallas_call | solution.py:63
  5.3 3.0 %collective-permute-start.1 = (bf16[2,28,128,128]{3,2,1,0:T(8,128)(2,1)S(1)}, bf16[2,28,128,128]{3,2,1,0:T(8,128)(2,1)S(1)}, u32[]{:S(2)}, u32[]{:S(2)}) collective-permute-start(bf16[2,28,128,128]{3,2,1,0:T(8,128)(2,1)S(1)} %get-tuple-element.51), channel_id=1, source_target_pairs={{0,2},{1,3},{2,0},{3,1},{4,6},{5,7},{6,4},{7,5},{8,10},{9,11},{10,... | collective-permute-start | bytes 5505032 | tf_op jit(solution)/shard_map/ppermute | solution.py:350
  8.3 1.5 collective-permute-start.2
  9.8 1.6 collective-permute-start
  12.1 3.8 %collective-permute-start.4 = (bf16[28,128,128]{2,1,0:T(8,128)(2,1)S(1)}, bf16[28,128,128]{2,1,0:T(8,128)(2,1)S(1)}, u32[]{:S(2)}, u32[]{:S(2)}) collective-permute-start(bf16[28,128,128]{2,1,0:T(8,128)(2,1)S(1)} %get-tuple-element.55.refs_0_), channel_id=1, source_target_pairs={{8,0},{9,1},{10,2},{11,3},{12,4},{13,5},{14,6},{15,7},{24,8},{25,9... | collective-permute-start | bytes 2752520 | tf_op jit(solution)/shard_map/ppermute | solution.py:350
  16.0 17.5 %collective-permute-done.refs_3_.refs_0_.refs_1_ = bf16[28,128,128]{2,1,0:T(8,128)(2,1)} collective-permute-done((bf16[28,128,128]{2,1,0:T(8,128)(2,1)}, bf16[28,128,128]{2,1,0:T(8,128)(2,1)}, u32[]{:S(2)}, u32[]{:S(2)}) %collective-permute-start) | collective-permute-done | bytes 917536 | tf_op jit(solution)/shard_map/ppermute | solution.py:350
  33.5 2.9 %pack.3 = bf16[2,28,128,128]{3,2,1,0:T(8,128)(2,1)S(1)} custom-call(s32[1]{0:T(128)} %bitcast.4.plane_ref.choice_ref, bf16[128,14336]{1,0:T(8,128)(2,1)} %refs_0_.3, bf16[128,14336]{1,0:T(8,128)(2,1)} %refs_1_.3, bf16[14336,128]{1,0:T(8,128)(2,1)} %refs_2_.3, bf16[28,128,128]{2,1,0:T(8,128)(2,1)} %collective-permute-done.refs_3_.refs_0_.refs_1_), custom_call_target="tpu_custom_call" | custom-call | bytes 4587520 | tf_op jit(solution)/shard_map/pack/pallas_call | solution.py:63
  36.3 12.0 %collective-permute-done.1.one = bf16[2,28,128,128]{3,2,1,0:T(8,128)(2,1)S(1)} collective-permute-done((bf16[2,28,128,128]{3,2,1,0:T(8,128)(2,1)S(1)}, bf16[2,28,128,128]{3,2,1,0:T(8,128)(2,1)S(1)}, u32[]{:S(2)}, u32[]{:S(2)}) %collective-permute-start.1) | collective-permute-done | bytes 1835040 | tf_op jit(solution)/shard_map/ppermute | solution.py:350
  48.3 1.5 collective-permute-done.2.two
  49.8 1.5 collective-permute-start.5
  51.3 2.2 unpack_pair.1
  53.6 4.4 %collective-permute-start.11 = (bf16[2,28,128,128]{3,2,1,0:T(8,128)(2,1)}, bf16[2,28,128,128]{3,2,1,0:T(8,128)(2,1)}, u32[]{:S(2)}, u32[]{:S(2)}) collective-permute-start(bf16[2,28,128,128]{3,2,1,0:T(8,128)(2,1)} %get-tuple-element.62.refs_1_), channel_id=1, source_target_pairs={{0,8},{1,9},{2,10},{3,11},{4,12},{5,13},{6,14},{7,15},{8,0},{9,1},... | collective-permute-start | bytes 5505032 | tf_op jit(solution)/shard_map/ppermute | solution.py:350
  58.0 1.9 collective-permute-start.8
  60.4 30.9 %collective-permute-done.5.packed = bf16[2,28,128,128]{3,2,1,0:T(8,128)(2,1)S(1)} collective-permute-done((bf16[2,28,128,128]{3,2,1,0:T(8,128)(2,1)S(1)}, bf16[2,28,128,128]{3,2,1,0:T(8,128)(2,1)S(1)}, u32[]{:S(2)}, u32[]{:S(2)}) %collective-permute-start.5) | collective-permute-done | bytes 1835040 | tf_op jit(solution)/shard_map/ppermute | solution.py:350
  92.5 3.3 %collective-permute-done.11.refs_2_ = bf16[2,28,128,128]{3,2,1,0:T(8,128)(2,1)} collective-permute-done((bf16[2,28,128,128]{3,2,1,0:T(8,128)(2,1)}, bf16[2,28,128,128]{3,2,1,0:T(8,128)(2,1)}, u32[]{:S(2)}, u32[]{:S(2)}) %collective-permute-start.11) | collective-permute-done | bytes 1835040 | tf_op jit(solution)/shard_map/ppermute | solution.py:350
  96.6 1.5 copy-done.10
  98.1 2.8 %reorder.2 = (bf16[28,128,128]{2,1,0:T(8,128)(2,1)}, bf16[28,128,128]{2,1,0:T(8,128)(2,1)S(1)}, bf16[28,128,128]{2,1,0:T(8,128)(2,1)}) custom-call(s32[3]{0:T(128)S(1)} %pad_add_fusion.1.order_ref, bf16[2,28,128,128]{3,2,1,0:T(8,128)(2,1)S(1)} %copy-done.10, bf16[2,28,128,128]{3,2,1,0:T(8,128)(2,1)S(1)} %get-tuple-element.59.w_12.refs_1_, ...), custom_call_target="tpu_custom_call" | custom-call | bytes 7340032 | tf_op jit(solution)/shard_map/reorder/pallas_call | solution.py:144
  101.6 6.4 %collective-permute-start.9 = (bf16[28,128,128]{2,1,0:T(8,128)(2,1)}, bf16[28,128,128]{2,1,0:T(8,128)(2,1)}, u32[]{:S(2)}, u32[]{:S(2)}) collective-permute-start(bf16[28,128,128]{2,1,0:T(8,128)(2,1)} %get-tuple-element.60.refs_1_), channel_id=1, source_target_pairs={{0,8},{1,9},{2,10},{3,11},{4,12},{5,13},{6,14},{7,15},{8,0},{9,1},... | collective-permute-start | bytes 2752520 | tf_op jit(solution)/shard_map/ppermute | solution.py:350
  108.0 2.0 stack.15.refs_0_
  110.2 3.2 %stack.16.refs_0_ = bf16[28,2048,128]{2,1,0:T(8,128)(2,1)S(1)} custom-call(bf16[28,2048,128]{2,1,0:T(8,128)(2,1)S(1)} %stack.15.refs_0_, bf16[2,28,128,128]{3,2,1,0:T(8,128)(2,1)} %get-tuple-element.62.refs_1_, bf16[2,28,128,128]{3,2,1,0:T(8,128)(2,1)} %collective-permute-done.11.refs_2_, ...), custom_call_target="tpu_custom_call", output_to_operand_aliasing={{}: (0, {})} | custom-call | bytes 14680064 | tf_op jit(solution)/shard_map/stack/pallas_call | solution.py:182
  113.4 5.2 %copy-done = bf16[28,2048,128]{2,1,0:T(8,128)(2,1)} copy-done((bf16[28,2048,128]{2,1,0:T(8,128)(2,1)}, bf16[28,2048,128]{2,1,0:T(8,128)(2,1)S(1)}, u32[]{:S(2)}) %copy-start) | copy-done | bytes 14680088
  119.4 8.7 %collective-permute-done.9.refs_2_.refs_0_ = bf16[28,128,128]{2,1,0:T(8,128)(2,1)} collective-permute-done((bf16[28,128,128]{2,1,0:T(8,128)(2,1)}, bf16[28,128,128]{2,1,0:T(8,128)(2,1)}, u32[]{:S(2)}, u32[]{:S(2)}) %collective-permute-start.9) | collective-permute-done | bytes 917536 | tf_op jit(solution)/shard_map/ppermute | solution.py:350
  128.2 2.0 collective-permute-start.16
  131.4 1.5 copy-done.11
  132.9 1.9 reorder.3
  135.0 5.2 %copy-done.1 = bf16[28,2048,128]{2,1,0:T(8,128)(2,1)S(1)} copy-done((bf16[28,2048,128]{2,1,0:T(8,128)(2,1)S(1)}, bf16[28,2048,128]{2,1,0:T(8,128)(2,1)}, u32[]{:S(2)}) %copy-start.1) | copy-done | bytes 14680088
  140.2 2.0 stack.17.a
  142.2 5.2 %copy-done.2 = bf16[28,2048,128]{2,1,0:T(8,128)(2,1)} copy-done((bf16[28,2048,128]{2,1,0:T(8,128)(2,1)}, bf16[28,2048,128]{2,1,0:T(8,128)(2,1)S(1)}, u32[]{:S(2)}) %copy-start.2) | copy-done | bytes 14680088
  147.4 5.2 %copy-done.3 = bf16[28,2048,128]{2,1,0:T(8,128)(2,1)S(1)} copy-done((bf16[28,2048,128]{2,1,0:T(8,128)(2,1)S(1)}, bf16[28,2048,128]{2,1,0:T(8,128)(2,1)}, u32[]{:S(2)}) %copy-start.3) | copy-done | bytes 14680088
  152.6 6.5 %product.5 = (bf16[4,128,512]{2,1,0:T(8,128)(2,1)S(1)}, bf16[4,128,512]{2,1,0:T(8,128)(2,1)S(1)}, bf16[4,128,512]{2,1,0:T(8,128)(2,1)S(1)}) custom-call(s32[1]{0:T(128)} %bitcast.2.choice_ref, bf16[28,2048,128]{2,1,0:T(8,128)(2,1)S(1)} %copy-done.3, bf16[28,128,128]{2,1,0:T(8,128)(2,1)S(1)} %copy-done.13, ...), custom_call_target="tpu_custom_call" | custom-call | flops 5637144576 | bytes 14680064 | tf_op jit(solution)/shard_map/product/pallas_call | solution.py:259
  160.2 2.4 %collective-permute-start.19 = (bf16[4,128,512]{2,1,0:T(8,128)(2,1)S(1)}, bf16[4,128,512]{2,1,0:T(8,128)(2,1)S(1)}, u32[]{:S(2)}, u32[]{:S(2)}) collective-permute-start(bf16[4,128,512]{2,1,0:T(8,128)(2,1)S(1)} %get-tuple-element.72.refs_6_), channel_id=1, source_target_pairs={{0,6},{1,7},{2,4},{3,5},{4,2},{5,3},{6,0},{7,1},{8,14},{9,15},{10,... | collective-permute-start | bytes 1572872 | tf_op jit(solution)/shard_map/ppermute | solution.py:350
  162.7 3.7 %collective-permute-start.27 = (bf16[28,128,128]{2,1,0:T(8,128)(2,1)S(1)}, bf16[28,128,128]{2,1,0:T(8,128)(2,1)S(1)}, u32[]{:S(2)}, u32[]{:S(2)}) collective-permute-start(bf16[28,128,128]{2,1,0:T(8,128)(2,1)S(1)} %get-tuple-element.83), channel_id=1, source_target_pairs={{8,0},{9,1},{10,2},{11,3},{12,4},{13,5},{14,6},{15,7},{24,8},{25,9... | collective-permute-start | bytes 2752520 | tf_op jit(solution)/shard_map/ppermute | solution.py:350
  166.4 2.8 %product.6.refs_6_.own = f32[4,128,512]{2,1,0:T(8,128)S(1)} custom-call(s32[1]{0:T(128)} %bitcast.2.choice_ref, bf16[28,2048,128]{2,1,0:T(8,128)(2,1)S(1)} %copy-done.3, bf16[28,128,128]{2,1,0:T(8,128)(2,1)S(1)} %copy-done.13, bf16[2,28,128,128]{3,2,1,0:T(8,128)(2,1)S(1)} %get-tuple-element.59.w_12.refs_1_, bf16[28,128,128]{2,1,0:T(8,128)(2,1)S(1)} %copy-done.15, ...), custom_call_target="tpu_custom_call" | custom-call | flops 1879048192 | bytes 7340032 | tf_op jit(solution)/shard_map/product/pallas_call | solution.py:259
  169.2 2.0 collective-permute-done.20.refs_2_.refs_0_
  171.2 2.8 %collective-permute-done.17.refs_3_.one = bf16[4,128,512]{2,1,0:T(8,128)(2,1)S(1)} collective-permute-done((bf16[4,128,512]{2,1,0:T(8,128)(2,1)S(1)}, bf16[4,128,512]{2,1,0:T(8,128)(2,1)S(1)}, u32[]{:S(2)}, u32[]{:S(2)}) %collective-permute-start.17) | collective-permute-done | bytes 524320 | tf_op jit(solution)/shard_map/ppermute | solution.py:350
  174.0 10.8 %collective-permute-done.18.refs_4_.two = bf16[4,128,512]{2,1,0:T(8,128)(2,1)S(1)} collective-permute-done((bf16[4,128,512]{2,1,0:T(8,128)(2,1)S(1)}, bf16[4,128,512]{2,1,0:T(8,128)(2,1)S(1)}, u32[]{:S(2)}, u32[]{:S(2)}) %collective-permute-start.18) | collective-permute-done | bytes 524320 | tf_op jit(solution)/shard_map/ppermute | solution.py:350
  184.8 5.3 %product.7 = (bf16[4,128,256]{2,1,0:T(8,128)(2,1)S(1)}, bf16[4,128,256]{2,1,0:T(8,128)(2,1)S(1)}, bf16[4,128,256]{2,1,0:T(8,128)(2,1)S(1)}, f32[4,128,256]{2,1,0:T(8,128)S(1)}) custom-call(s32[1]{0:T(128)} %bitcast.4.plane_ref.choice_ref, bf16[28,2048,128]{2,1,0:T(8,128)(2,1)S(1)} %bitcast.9, ...), custom_call_target="tpu_custom_call" | custom-call | flops 3758096384 | bytes 16515072 | tf_op jit(solution)/shard_map/product/pallas_call | solution.py:259
  190.1 1.4 collective-permute-start.24
  192.0 1.6 collective-permute-start.26
  193.9 5.5 %collective-permute-done.24.refs_3_.one = bf16[4,128,256]{2,1,0:T(8,128)(2,1)S(1)} collective-permute-done((bf16[4,128,256]{2,1,0:T(8,128)(2,1)S(1)}, bf16[4,128,256]{2,1,0:T(8,128)(2,1)S(1)}, u32[]{:S(2)}, u32[]{:S(2)}) %collective-permute-start.24) | collective-permute-done | bytes 262176 | tf_op jit(solution)/shard_map/ppermute | solution.py:350
  199.4 4.7 %collective-permute-done.25.refs_4_.two = bf16[4,128,256]{2,1,0:T(8,128)(2,1)S(1)} collective-permute-done((bf16[4,128,256]{2,1,0:T(8,128)(2,1)S(1)}, bf16[4,128,256]{2,1,0:T(8,128)(2,1)S(1)}, u32[]{:S(2)}, u32[]{:S(2)}) %collective-permute-start.25) | collective-permute-done | bytes 262176 | tf_op jit(solution)/shard_map/ppermute | solution.py:350
  204.1 3.4 %product.8 = (bf16[4,128,256]{2,1,0:T(8,128)(2,1)S(1)}, bf16[4,128,256]{2,1,0:T(8,128)(2,1)S(1)}, bf16[4,128,256]{2,1,0:T(8,128)(2,1)S(1)}) custom-call(s32[1]{0:T(128)} %bitcast.4.plane_ref.choice_ref, bf16[28,2048,128]{2,1,0:T(8,128)(2,1)S(1)} %bitcast.9, bf16[28,128,128]{2,1,0:T(8,128)(2,1)S(1)} %collective-permute-done.20.refs_2_.refs_0_, ...), custom_call_target="tpu_custom_call" | custom-call | flops 2818572288 | bytes 12845056 | tf_op jit(solution)/shard_map/product/pallas_call | solution.py:259
  209.6 1.5 collective-permute-start.33
  211.1 2.3 collective-permute-start.22
  213.4 3.5 %collective-permute-done.31.one = bf16[4,128,256]{2,1,0:T(8,128)(2,1)S(1)} collective-permute-done((bf16[4,128,256]{2,1,0:T(8,128)(2,1)S(1)}, bf16[4,128,256]{2,1,0:T(8,128)(2,1)S(1)}, u32[]{:S(2)}, u32[]{:S(2)}) %collective-permute-start.31) | collective-permute-done | bytes 262176 | tf_op jit(solution)/shard_map/ppermute | solution.py:350
  216.8 1.5 product.9.refs_0_.own
  226.4 2.0 collective-permute-done.35.refs_10_
  229.2 1.8 assemble.1
  (89 shorter events, 19.1 us)
Async XLA Ops:
  5.3 31.0 %copy-start.12 = (bf16[28,128,128]{2,1,0:T(8,128)(2,1)}, bf16[28,128,128]{2,1,0:T(8,128)(2,1)S(1)}, u32[]{:S(2)}) copy-start(bf16[28,128,128]{2,1,0:T(8,128)(2,1)S(1)} %get-tuple-element.55.refs_0_) | copy-start | bytes 2752516
  5.3 43.0 %collective-permute-start.1 = (bf16[2,28,128,128]{3,2,1,0:T(8,128)(2,1)S(1)}, bf16[2,28,128,128]{3,2,1,0:T(8,128)(2,1)S(1)}, u32[]{:S(2)}, u32[]{:S(2)}) collective-permute-start(bf16[2,28,128,128]{3,2,1,0:T(8,128)(2,1)S(1)} %get-tuple-element.51), channel_id=1, source_target_pairs={{0,2},{1,3},{2,0},{3,1},{4,6},{5,7},{6,4},{7,5},{8,10},{9,11},{10,... | collective-permute-start | bytes 5505032 | tf_op jit(solution)/shard_map/ppermute | solution.py:350
  8.3 41.5 %collective-permute-start.2 = (bf16[2,28,128,128]{3,2,1,0:T(8,128)(2,1)S(1)}, bf16[2,28,128,128]{3,2,1,0:T(8,128)(2,1)S(1)}, u32[]{:S(2)}, u32[]{:S(2)}) collective-permute-start(bf16[2,28,128,128]{3,2,1,0:T(8,128)(2,1)S(1)} %get-tuple-element.52), channel_id=1, source_target_pairs={{0,4},{1,5},{2,6},{3,7},{4,0},{5,1},{6,2},{7,3},{8,12},{9,13},{10,... | collective-permute-start | bytes 5505032 | tf_op jit(solution)/shard_map/ppermute | solution.py:350
  9.8 23.6 %collective-permute-start = (bf16[28,128,128]{2,1,0:T(8,128)(2,1)}, bf16[28,128,128]{2,1,0:T(8,128)(2,1)}, u32[]{:S(2)}, u32[]{:S(2)}) collective-permute-start(bf16[28,128,128]{2,1,0:T(8,128)(2,1)} %get-tuple-element.50.refs_0_), channel_id=1, source_target_pairs={{0,8},{1,9},{2,10},{3,11},{4,12},{5,13},{6,14},{7,15},{8,0},{9,1},... | collective-permute-start | bytes 2752520 | tf_op jit(solution)/shard_map/ppermute | solution.py:350
  11.4 39.9 %collective-permute-start.3 = (bf16[28,128,128]{2,1,0:T(8,128)(2,1)S(1)}, bf16[28,128,128]{2,1,0:T(8,128)(2,1)S(1)}, u32[]{:S(2)}, u32[]{:S(2)}) collective-permute-start(bf16[28,128,128]{2,1,0:T(8,128)(2,1)S(1)} %get-tuple-element.55.refs_0_), channel_id=1, source_target_pairs={{8,16},{9,17},{10,18},{11,19},{12,20},{13,21},{14,22},{15,23},{16,... | collective-permute-start | bytes 2752520 | tf_op jit(solution)/shard_map/ppermute | solution.py:350
  12.1 39.2 %collective-permute-start.4 = (bf16[28,128,128]{2,1,0:T(8,128)(2,1)S(1)}, bf16[28,128,128]{2,1,0:T(8,128)(2,1)S(1)}, u32[]{:S(2)}, u32[]{:S(2)}) collective-permute-start(bf16[28,128,128]{2,1,0:T(8,128)(2,1)S(1)} %get-tuple-element.55.refs_0_), channel_id=1, source_target_pairs={{8,0},{9,1},{10,2},{11,3},{12,4},{13,5},{14,6},{15,7},{24,8},{25,9... | collective-permute-start | bytes 2752520 | tf_op jit(solution)/shard_map/ppermute | solution.py:350
  49.8 41.5 %collective-permute-start.5 = (bf16[2,28,128,128]{3,2,1,0:T(8,128)(2,1)S(1)}, bf16[2,28,128,128]{3,2,1,0:T(8,128)(2,1)S(1)}, u32[]{:S(2)}, u32[]{:S(2)}) collective-permute-start(bf16[2,28,128,128]{3,2,1,0:T(8,128)(2,1)S(1)} %pack.3), channel_id=1, source_target_pairs={{0,6},{1,7},{2,4},{3,5},{4,2},{5,3},{6,0},{7,1},{8,14},{9,15},{10,... | collective-permute-start | bytes 5505032 | tf_op jit(solution)/shard_map/ppermute | solution.py:350
  53.6 42.2 %collective-permute-start.11 = (bf16[2,28,128,128]{3,2,1,0:T(8,128)(2,1)}, bf16[2,28,128,128]{3,2,1,0:T(8,128)(2,1)}, u32[]{:S(2)}, u32[]{:S(2)}) collective-permute-start(bf16[2,28,128,128]{3,2,1,0:T(8,128)(2,1)} %get-tuple-element.62.refs_1_), channel_id=1, source_target_pairs={{0,8},{1,9},{2,10},{3,11},{4,12},{5,13},{6,14},{7,15},{8,0},{9,1},... | collective-permute-start | bytes 5505032 | tf_op jit(solution)/shard_map/ppermute | solution.py:350
  58.0 38.6 %collective-permute-start.8 = (bf16[2,28,128,128]{3,2,1,0:T(8,128)(2,1)S(1)}, bf16[2,28,128,128]{3,2,1,0:T(8,128)(2,1)}, u32[]{:S(2)}, u32[]{:S(2)}) collective-permute-start(bf16[2,28,128,128]{3,2,1,0:T(8,128)(2,1)S(1)} %get-tuple-element.59.w_12.refs_1_), channel_id=1, source_target_pairs={{8,16},{9,17},{10,18},{11,19},{12,20},{13,21},{14,22},{15,23},{16,... | collective-permute-start | bytes 5505032 | tf_op jit(solution)/shard_map/ppermute | solution.py:350
  59.8 36.7 %collective-permute-start.6 = (bf16[28,128,128]{2,1,0:T(8,128)(2,1)}, bf16[28,128,128]{2,1,0:T(8,128)(2,1)}, u32[]{:S(2)}, u32[]{:S(2)}) collective-permute-start(bf16[28,128,128]{2,1,0:T(8,128)(2,1)} %get-tuple-element.50.refs_0_), channel_id=1, source_target_pairs={{0,1},{1,0},{2,3},{3,2},{4,5},{5,4},{6,7},{7,6},{8,9},{9,8},{10,11... | collective-permute-start | bytes 2752520 | tf_op jit(solution)/shard_map/ppermute | solution.py:350
  59.9 36.7 %collective-permute-start.7 = (bf16[28,128,128]{2,1,0:T(8,128)(2,1)}, bf16[28,128,128]{2,1,0:T(8,128)(2,1)}, u32[]{:S(2)}, u32[]{:S(2)}) collective-permute-start(bf16[28,128,128]{2,1,0:T(8,128)(2,1)} %collective-permute-done.refs_3_.refs_0_.refs_1_), channel_id=1, source_target_pairs={{0,1},{1,0},{2,3},{3,2},{4,5},{5,4},{6,7},{7,6},{8,9},{9,8},{10,11... | collective-permute-start | bytes 2752520 | tf_op jit(solution)/shard_map/ppermute | solution.py:350
  92.5 17.6 %collective-permute-start.12 = (bf16[2,28,128,128]{3,2,1,0:T(8,128)(2,1)}, bf16[2,28,128,128]{3,2,1,0:T(8,128)(2,1)}, u32[]{:S(2)}, u32[]{:S(2)}) collective-permute-start(bf16[2,28,128,128]{3,2,1,0:T(8,128)(2,1)} %get-tuple-element.62.refs_1_), channel_id=1, source_target_pairs={{0,1},{1,0},{2,3},{3,2},{4,5},{5,4},{6,7},{7,6},{8,9},{9,8},{10,11... | collective-permute-start | bytes 5505032 | tf_op jit(solution)/shard_map/ppermute | solution.py:350
  95.8 14.4 %collective-permute-start.13 = (bf16[2,28,128,128]{3,2,1,0:T(8,128)(2,1)}, bf16[2,28,128,128]{3,2,1,0:T(8,128)(2,1)}, u32[]{:S(2)}, u32[]{:S(2)}) collective-permute-start(bf16[2,28,128,128]{3,2,1,0:T(8,128)(2,1)} %collective-permute-done.11.refs_2_), channel_id=1, source_target_pairs={{0,1},{1,0},{2,3},{3,2},{4,5},{5,4},{6,7},{7,6},{8,9},{9,8},{10,11... | collective-permute-start | bytes 5505032 | tf_op jit(solution)/shard_map/ppermute | solution.py:350
  100.9 9.1 %copy-start.14 = (bf16[28,128,128]{2,1,0:T(8,128)(2,1)}, bf16[28,128,128]{2,1,0:T(8,128)(2,1)S(1)}, u32[]{:S(2)}) copy-start(bf16[28,128,128]{2,1,0:T(8,128)(2,1)S(1)} %get-tuple-element.61.refs_2_) | copy-start | bytes 2752516
  100.9 17.6 %collective-permute-start.10 = (bf16[28,128,128]{2,1,0:T(8,128)(2,1)S(1)}, bf16[28,128,128]{2,1,0:T(8,128)(2,1)S(1)}, u32[]{:S(2)}, u32[]{:S(2)}) collective-permute-start(bf16[28,128,128]{2,1,0:T(8,128)(2,1)S(1)} %get-tuple-element.61.refs_2_), channel_id=1, source_target_pairs={{8,16},{9,17},{10,18},{11,19},{12,20},{13,21},{14,22},{15,23},{16,... | collective-permute-start | bytes 2752520 | tf_op jit(solution)/shard_map/ppermute | solution.py:350
  101.6 26.5 %collective-permute-start.9 = (bf16[28,128,128]{2,1,0:T(8,128)(2,1)}, bf16[28,128,128]{2,1,0:T(8,128)(2,1)}, u32[]{:S(2)}, u32[]{:S(2)}) collective-permute-start(bf16[28,128,128]{2,1,0:T(8,128)(2,1)} %get-tuple-element.60.refs_1_), channel_id=1, source_target_pairs={{0,8},{1,9},{2,10},{3,11},{4,12},{5,13},{6,14},{7,15},{8,0},{9,1},... | collective-permute-start | bytes 2752520 | tf_op jit(solution)/shard_map/ppermute | solution.py:350
  110.1 24.9 %collective-permute-start.14 = (bf16[28,128,128]{2,1,0:T(8,128)(2,1)}, bf16[28,128,128]{2,1,0:T(8,128)(2,1)}, u32[]{:S(2)}, u32[]{:S(2)}) collective-permute-start(bf16[28,128,128]{2,1,0:T(8,128)(2,1)} %get-tuple-element.60.refs_1_), channel_id=1, source_target_pairs={{0,1},{1,0},{2,3},{3,2},{4,5},{5,4},{6,7},{7,6},{8,9},{9,8},{10,11... | collective-permute-start | bytes 2752520 | tf_op jit(solution)/shard_map/ppermute | solution.py:350
  113.3 5.2 %copy-start = (bf16[28,2048,128]{2,1,0:T(8,128)(2,1)}, bf16[28,2048,128]{2,1,0:T(8,128)(2,1)S(1)}, u32[]{:S(2)}) copy-start(bf16[28,2048,128]{2,1,0:T(8,128)(2,1)S(1)} %stack.16.refs_0_) | copy-start | bytes 44040196
  128.2 6.8 %collective-permute-start.15 = (bf16[28,128,128]{2,1,0:T(8,128)(2,1)}, bf16[28,128,128]{2,1,0:T(8,128)(2,1)}, u32[]{:S(2)}, u32[]{:S(2)}) collective-permute-start(bf16[28,128,128]{2,1,0:T(8,128)(2,1)} %collective-permute-done.9.refs_2_.refs_0_), channel_id=1, source_target_pairs={{0,1},{1,0},{2,3},{3,2},{4,5},{5,4},{6,7},{7,6},{8,9},{9,8},{10,11... | collective-permute-start | bytes 2752520 | tf_op jit(solution)/shard_map/ppermute | solution.py:350
  128.2 30.9 %collective-permute-start.16 = (bf16[28,128,128]{2,1,0:T(8,128)(2,1)}, bf16[28,128,128]{2,1,0:T(8,128)(2,1)}, u32[]{:S(2)}, u32[]{:S(2)}) collective-permute-start(bf16[28,128,128]{2,1,0:T(8,128)(2,1)} %get-tuple-element.69), channel_id=1, source_target_pairs={{8,0},{9,1},{10,2},{11,3},{12,4},{13,5},{14,6},{15,7},{24,8},{25,9... | collective-permute-start | bytes 2752520 | tf_op jit(solution)/shard_map/ppermute | solution.py:350
  132.9 14.5 %copy-start.6 = (bf16[28,128,128]{2,1,0:T(8,128)(2,1)S(1)}, bf16[28,128,128]{2,1,0:T(8,128)(2,1)}, u32[]{:S(2)}) copy-start(bf16[28,128,128]{2,1,0:T(8,128)(2,1)} %copy-done.4) | copy-start | bytes 2752516
  132.9 14.5 %copy-start.8 = (bf16[28,128,128]{2,1,0:T(8,128)(2,1)S(1)}, bf16[28,128,128]{2,1,0:T(8,128)(2,1)}, u32[]{:S(2)}) copy-start(bf16[28,128,128]{2,1,0:T(8,128)(2,1)} %copy-done.7) | copy-start | bytes 2752516
  132.9 14.5 %copy-start.13 = (bf16[28,128,128]{2,1,0:T(8,128)(2,1)S(1)}, bf16[28,128,128]{2,1,0:T(8,128)(2,1)}, u32[]{:S(2)}) copy-start(bf16[28,128,128]{2,1,0:T(8,128)(2,1)} %copy-done.12) | copy-start | bytes 2752516
  132.9 14.5 %copy-start.15 = (bf16[28,128,128]{2,1,0:T(8,128)(2,1)S(1)}, bf16[28,128,128]{2,1,0:T(8,128)(2,1)}, u32[]{:S(2)}) copy-start(bf16[28,128,128]{2,1,0:T(8,128)(2,1)} %copy-done.14) | copy-start | bytes 2752516
  134.9 36.3 %collective-permute-start.20 = (bf16[28,128,128]{2,1,0:T(8,128)(2,1)S(1)}, bf16[28,128,128]{2,1,0:T(8,128)(2,1)S(1)}, u32[]{:S(2)}, u32[]{:S(2)}) collective-permute-start(bf16[28,128,128]{2,1,0:T(8,128)(2,1)S(1)} %get-tuple-element.74), channel_id=1, source_target_pairs={{8,0},{9,1},{10,2},{11,3},{12,4},{13,5},{14,6},{15,7},{24,8},{25,9... | collective-permute-start | bytes 2752520 | tf_op jit(solution)/shard_map/ppermute | solution.py:350
  152.6 32.2 %slice-start = ((s8[14680064]{0:T(1024)(128)(4,1)}), s8[4194304]{0:T(1024)(128)(4,1)S(1)}, s32[]{:S(2)}) async-start(s8[14680064]{0:T(1024)(128)(4,1)} %bitcast.8), calls=%async_computation | async-start | bytes 8388608
  152.6 32.2 %slice-start.1 = ((s8[14680064]{0:T(1024)(128)(4,1)}), s8[4194304]{0:T(1024)(128)(4,1)S(1)}, s32[]{:S(2)}) async-start(s8[14680064]{0:T(1024)(128)(4,1)} %bitcast.8), calls=%async_computation.1 | async-start | bytes 8388608
  159.1 14.8 %collective-permute-start.17 = (bf16[4,128,512]{2,1,0:T(8,128)(2,1)S(1)}, bf16[4,128,512]{2,1,0:T(8,128)(2,1)S(1)}, u32[]{:S(2)}, u32[]{:S(2)}) collective-permute-start(bf16[4,128,512]{2,1,0:T(8,128)(2,1)S(1)} %get-tuple-element.70), channel_id=1, source_target_pairs={{0,2},{1,3},{2,0},{3,1},{4,6},{5,7},{6,4},{7,5},{8,10},{9,11},{10,... | collective-permute-start | bytes 1572872 | tf_op jit(solution)/shard_map/ppermute | solution.py:350
  159.7 25.0 %collective-permute-start.18 = (bf16[4,128,512]{2,1,0:T(8,128)(2,1)S(1)}, bf16[4,128,512]{2,1,0:T(8,128)(2,1)S(1)}, u32[]{:S(2)}, u32[]{:S(2)}) collective-permute-start(bf16[4,128,512]{2,1,0:T(8,128)(2,1)S(1)} %get-tuple-element.71), channel_id=1, source_target_pairs={{0,4},{1,5},{2,6},{3,7},{4,0},{5,1},{6,2},{7,3},{8,12},{9,13},{10,... | collective-permute-start | bytes 1572872 | tf_op jit(solution)/shard_map/ppermute | solution.py:350
  160.2 24.5 %collective-permute-start.19 = (bf16[4,128,512]{2,1,0:T(8,128)(2,1)S(1)}, bf16[4,128,512]{2,1,0:T(8,128)(2,1)S(1)}, u32[]{:S(2)}, u32[]{:S(2)}) collective-permute-start(bf16[4,128,512]{2,1,0:T(8,128)(2,1)S(1)} %get-tuple-element.72.refs_6_), channel_id=1, source_target_pairs={{0,6},{1,7},{2,4},{3,5},{4,2},{5,3},{6,0},{7,1},{8,14},{9,15},{10,... | collective-permute-start | bytes 1572872 | tf_op jit(solution)/shard_map/ppermute | solution.py:350
  162.7 22.1 %slice-start.2 = ((s8[14680064]{0:T(1024)(128)(4,1)}), s8[4194304]{0:T(1024)(128)(4,1)S(1)}, s32[]{:S(2)}) async-start(s8[14680064]{0:T(1024)(128)(4,1)} %bitcast.8), calls=%async_computation.2 | async-start | bytes 8388608
  162.7 22.1 %slice-start.3 = ((s8[14680064]{0:T(1024)(128)(4,1)}), s8[2097152]{0:T(1024)(128)(4,1)S(1)}, s32[]{:S(2)}) async-start(s8[14680064]{0:T(1024)(128)(4,1)} %bitcast.8), calls=%async_computation.3 | async-start | bytes 4194304
  162.7 31.2 %collective-permute-start.27 = (bf16[28,128,128]{2,1,0:T(8,128)(2,1)S(1)}, bf16[28,128,128]{2,1,0:T(8,128)(2,1)S(1)}, u32[]{:S(2)}, u32[]{:S(2)}) collective-permute-start(bf16[28,128,128]{2,1,0:T(8,128)(2,1)S(1)} %get-tuple-element.83), channel_id=1, source_target_pairs={{8,0},{9,1},{10,2},{11,3},{12,4},{13,5},{14,6},{15,7},{24,8},{25,9... | collective-permute-start | bytes 2752520 | tf_op jit(solution)/shard_map/ppermute | solution.py:350
  190.1 9.3 %collective-permute-start.24 = (bf16[4,128,256]{2,1,0:T(8,128)(2,1)S(1)}, bf16[4,128,256]{2,1,0:T(8,128)(2,1)S(1)}, u32[]{:S(2)}, u32[]{:S(2)}) collective-permute-start(bf16[4,128,256]{2,1,0:T(8,128)(2,1)S(1)} %get-tuple-element.80), channel_id=1, source_target_pairs={{0,2},{1,3},{2,0},{3,1},{4,6},{5,7},{6,4},{7,5},{8,10},{9,11},{10,... | collective-permute-start | bytes 786440 | tf_op jit(solution)/shard_map/ppermute | solution.py:350
  191.5 12.6 %collective-permute-start.25 = (bf16[4,128,256]{2,1,0:T(8,128)(2,1)S(1)}, bf16[4,128,256]{2,1,0:T(8,128)(2,1)S(1)}, u32[]{:S(2)}, u32[]{:S(2)}) collective-permute-start(bf16[4,128,256]{2,1,0:T(8,128)(2,1)S(1)} %get-tuple-element.81), channel_id=1, source_target_pairs={{0,4},{1,5},{2,6},{3,7},{4,0},{5,1},{6,2},{7,3},{8,12},{9,13},{10,... | collective-permute-start | bytes 786440 | tf_op jit(solution)/shard_map/ppermute | solution.py:350
  192.0 12.1 %collective-permute-start.26 = (bf16[4,128,256]{2,1,0:T(8,128)(2,1)S(1)}, bf16[4,128,256]{2,1,0:T(8,128)(2,1)S(1)}, u32[]{:S(2)}, u32[]{:S(2)}) collective-permute-start(bf16[4,128,256]{2,1,0:T(8,128)(2,1)S(1)} %get-tuple-element.82), channel_id=1, source_target_pairs={{0,6},{1,7},{2,4},{3,5},{4,2},{5,3},{6,0},{7,1},{8,14},{9,15},{10,... | collective-permute-start | bytes 786440 | tf_op jit(solution)/shard_map/ppermute | solution.py:350
  207.5 9.3 %collective-permute-start.31 = (bf16[4,128,256]{2,1,0:T(8,128)(2,1)S(1)}, bf16[4,128,256]{2,1,0:T(8,128)(2,1)S(1)}, u32[]{:S(2)}, u32[]{:S(2)}) collective-permute-start(bf16[4,128,256]{2,1,0:T(8,128)(2,1)S(1)} %get-tuple-element.89), channel_id=1, source_target_pairs={{0,2},{1,3},{2,0},{3,1},{4,6},{5,7},{6,4},{7,5},{8,10},{9,11},{10,... | collective-permute-start | bytes 786440 | tf_op jit(solution)/shard_map/ppermute | solution.py:350
  208.3 11.5 %collective-permute-start.32 = (bf16[4,128,256]{2,1,0:T(8,128)(2,1)S(1)}, bf16[4,128,256]{2,1,0:T(8,128)(2,1)S(1)}, u32[]{:S(2)}, u32[]{:S(2)}) collective-permute-start(bf16[4,128,256]{2,1,0:T(8,128)(2,1)S(1)} %get-tuple-element.90), channel_id=1, source_target_pairs={{0,4},{1,5},{2,6},{3,7},{4,0},{5,1},{6,2},{7,3},{8,12},{9,13},{10,... | collective-permute-start | bytes 786440 | tf_op jit(solution)/shard_map/ppermute | solution.py:350
  209.6 11.3 %collective-permute-start.33 = (bf16[4,128,256]{2,1,0:T(8,128)(2,1)S(1)}, bf16[4,128,256]{2,1,0:T(8,128)(2,1)S(1)}, u32[]{:S(2)}, u32[]{:S(2)}) collective-permute-start(bf16[4,128,256]{2,1,0:T(8,128)(2,1)S(1)} %get-tuple-element.84.refs_3_), channel_id=1, source_target_pairs={{0,6},{1,7},{2,4},{3,5},{4,2},{5,3},{6,0},{7,1},{8,14},{9,15},{10,... | collective-permute-start | bytes 786440 | tf_op jit(solution)/shard_map/ppermute | solution.py:350
  211.1 11.1 %collective-permute-start.21 = (bf16[128,512]{1,0:T(8,128)(2,1)S(1)}, bf16[128,512]{1,0:T(8,128)(2,1)S(1)}, u32[]{:S(2)}, u32[]{:S(2)}) collective-permute-start(bf16[128,512]{1,0:T(8,128)(2,1)S(1)} %get-tuple-element.77), channel_id=1, source_target_pairs={{0,1},{1,0},{2,3},{3,2},{4,5},{5,4},{6,7},{7,6},{8,9},{9,8},{10,11... | collective-permute-start | bytes 393224 | tf_op jit(solution)/shard_map/ppermute | solution.py:350
  211.1 11.5 %collective-permute-start.22 = (bf16[128,512]{1,0:T(8,128)(2,1)S(1)}, bf16[128,512]{1,0:T(8,128)(2,1)S(1)}, u32[]{:S(2)}, u32[]{:S(2)}) collective-permute-start(bf16[128,512]{1,0:T(8,128)(2,1)S(1)} %get-tuple-element.78), channel_id=1, source_target_pairs={{0,8},{1,9},{2,10},{3,11},{4,12},{5,13},{6,14},{7,15},{8,0},{9,1},... | collective-permute-start | bytes 393224 | tf_op jit(solution)/shard_map/ppermute | solution.py:350
  216.8 6.4 %collective-permute-start.23 = (bf16[128,512]{1,0:T(8,128)(2,1)S(1)}, bf16[128,512]{1,0:T(8,128)(2,1)S(1)}, u32[]{:S(2)}, u32[]{:S(2)}) collective-permute-start(bf16[128,512]{1,0:T(8,128)(2,1)S(1)} %get-tuple-element.79), channel_id=1, source_target_pairs={{0,9},{1,8},{2,11},{3,10},{4,13},{5,12},{6,15},{7,14},{8,1},{9,0},... | collective-permute-start | bytes 393224 | tf_op jit(solution)/shard_map/ppermute | solution.py:350
  219.8 4.6 %collective-permute-start.28 = (bf16[128,256]{1,0:T(8,128)(2,1)S(1)}, bf16[128,256]{1,0:T(8,128)(2,1)S(1)}, u32[]{:S(2)}, u32[]{:S(2)}) collective-permute-start(bf16[128,256]{1,0:T(8,128)(2,1)S(1)} %get-tuple-element.86), channel_id=1, source_target_pairs={{0,1},{1,0},{2,3},{3,2},{4,5},{5,4},{6,7},{7,6},{8,9},{9,8},{10,11... | collective-permute-start | bytes 196616 | tf_op jit(solution)/shard_map/ppermute | solution.py:350
  220.9 4.3 %collective-permute-start.29 = (bf16[128,256]{1,0:T(8,128)(2,1)S(1)}, bf16[128,256]{1,0:T(8,128)(2,1)S(1)}, u32[]{:S(2)}, u32[]{:S(2)}) collective-permute-start(bf16[128,256]{1,0:T(8,128)(2,1)S(1)} %get-tuple-element.87), channel_id=1, source_target_pairs={{0,8},{1,9},{2,10},{3,11},{4,12},{5,13},{6,14},{7,15},{8,0},{9,1},... | collective-permute-start | bytes 196616 | tf_op jit(solution)/shard_map/ppermute | solution.py:350
  222.2 4.1 %collective-permute-start.30 = (bf16[128,256]{1,0:T(8,128)(2,1)S(1)}, bf16[128,256]{1,0:T(8,128)(2,1)S(1)}, u32[]{:S(2)}, u32[]{:S(2)}) collective-permute-start(bf16[128,256]{1,0:T(8,128)(2,1)S(1)} %get-tuple-element.88), channel_id=1, source_target_pairs={{0,9},{1,8},{2,11},{3,10},{4,13},{5,12},{6,15},{7,14},{8,1},{9,0},... | collective-permute-start | bytes 196616 | tf_op jit(solution)/shard_map/ppermute | solution.py:350
  222.6 3.8 %collective-permute-start.34 = (bf16[128,256]{1,0:T(8,128)(2,1)S(1)}, bf16[128,256]{1,0:T(8,128)(2,1)S(1)}, u32[]{:S(2)}, u32[]{:S(2)}) collective-permute-start(bf16[128,256]{1,0:T(8,128)(2,1)S(1)} %get-tuple-element.92), channel_id=1, source_target_pairs={{0,1},{1,0},{2,3},{3,2},{4,5},{5,4},{6,7},{7,6},{8,9},{9,8},{10,11... | collective-permute-start | bytes 196616 | tf_op jit(solution)/shard_map/ppermute | solution.py:350
  223.3 5.1 %collective-permute-start.35 = (bf16[128,256]{1,0:T(8,128)(2,1)S(1)}, bf16[128,256]{1,0:T(8,128)(2,1)S(1)}, u32[]{:S(2)}, u32[]{:S(2)}) collective-permute-start(bf16[128,256]{1,0:T(8,128)(2,1)S(1)} %get-tuple-element.93), channel_id=1, source_target_pairs={{0,8},{1,9},{2,10},{3,11},{4,12},{5,13},{6,14},{7,15},{8,0},{9,1},... | collective-permute-start | bytes 196616 | tf_op jit(solution)/shard_map/ppermute | solution.py:350
  224.4 4.7 %collective-permute-start.36 = (bf16[128,256]{1,0:T(8,128)(2,1)S(1)}, bf16[128,256]{1,0:T(8,128)(2,1)S(1)}, u32[]{:S(2)}, u32[]{:S(2)}) collective-permute-start(bf16[128,256]{1,0:T(8,128)(2,1)S(1)} %get-tuple-element.94), channel_id=1, source_target_pairs={{0,9},{1,8},{2,11},{3,10},{4,13},{5,12},{6,15},{7,14},{8,1},{9,0},... | collective-permute-start | bytes 196616 | tf_op jit(solution)/shard_map/ppermute | solution.py:350
  (9 other events, 24.1 us)

commit v8 on v7

--- a/solution.py
+++ b/solution.py
@@ -43,8 +43,8 @@
     grid = 4
     share = tiles // grid
     apart = int(steps[0] == 0)
-    single = jax.ShapeDtypeStruct((tiles, rows, LANES), jnp.bfloat16)
-    double = jax.ShapeDtypeStruct((2, tiles, rows, LANES), jnp.bfloat16)
+    single = pltpu.HBM((tiles, rows, LANES), jnp.bfloat16)
+    double = pltpu.HBM((2, tiles, rows, LANES), jnp.bfloat16)
     single_spec = pl.BlockSpec((share, rows, LANES), lambda at, plane: (at, 0, 0))
     double_spec = pl.BlockSpec((2, share, rows, LANES), lambda at, plane: (0, at, 0, 0))
     others = len(steps) - apart
@@ -105,7 +105,7 @@
 def unpack_pair(one, two, after):
     return pl.pallas_call(
         unpack_pair_kernel,
-        out_shape=[jax.ShapeDtypeStruct(one.shape, one.dtype)] * 2,
+        out_shape=[pltpu.HBM(one.shape, one.dtype)] * 2,
         in_specs=[pl.BlockSpec(memory_space=pl.ANY)] * (2 + len(after)),
         out_specs=[pl.BlockSpec(memory_space=pl.ANY)] * 2,
         scratch_shapes=[
@@ -143,7 +143,7 @@
     shape, count = packed.shape[1:], order.shape[0]
     return pl.pallas_call(
         functools.partial(reorder_kernel, count),
-        out_shape=[jax.ShapeDtypeStruct(shape, packed.dtype)] * count,
+        out_shape=[pltpu.HBM(shape, packed.dtype)] * count,
         in_specs=[pl.BlockSpec(memory_space=pltpu.SMEM)]
         + [pl.BlockSpec(memory_space=pl.ANY)] * (2 + len(after)),
         out_specs=[pl.BlockSpec(memory_space=pl.ANY)] * count,
@@ -158,41 +158,101 @@
     )(order, packed, w_12, *after)
 
 
-def stack_kernel(first, count, *refs):
-    sources, stack_ref, sem = refs[-2 - count : -2], refs[-2], refs[-1]
-    rows = sources[0].shape[-2]
-    copies, at = [], 0
-    for source in sources:
-        parts = [source] if len(source.shape) == 3 else [source.at[0], source.at[1]]
-        for part in parts:
-            to = stack_ref.at[:, pl.ds((first + at) * rows, rows)]
-            copies.append(pltpu.make_async_copy(part, to, sem.at[at]))
-            at += 1
-    for copy in copies:
-        copy.start()
-    for copy in copies:
-        copy.wait()
-
-
-def stack(first, blocks, before=None):
-    tiles, rows, lanes = blocks[0].shape[-3:]
-    shape = (tiles, 16 * rows, lanes)
-    held = [] if before is None else [pltpu.with_memory_space_constraint(before, pltpu.VMEM)]
-    count = sum(block.size for block in blocks) // (tiles * rows * lanes)
-    return pl.pallas_call(
-        functools.partial(stack_kernel, first, len(blocks)),
-        out_shape=pltpu.VMEM(shape, blocks[0].dtype),
-        in_specs=[pl.BlockSpec(memory_space=pltpu.VMEM)] * len(held)
-        + [pl.BlockSpec(memory_space=pl.ANY)] * len(blocks),
-        out_specs=pl.BlockSpec(memory_space=pltpu.VMEM),
-        scratch_shapes=[pltpu.SemaphoreType.DMA((count,))],
-        input_output_aliases={0: 0} if held else {},
+def far(arrays):
+    return [pltpu.with_memory_space_constraint(array, pltpu.HBM) for array in arrays]
+
+
+def multiply(a, right, place, out):
+    tiles, rows = a.shape[0], a.shape[1] // 16
+    for half in range(2):
+        left = jnp.concatenate(
+            [
+                jnp.concatenate([a[tile, pl.ds(block * rows, rows)] for tile in range(tiles)], axis=1)
+                for block in place[2 * half : 2 * half + 2]
+            ],
+            axis=0,
+        )
+        total = jnp.dot(left, right, preferred_element_type=jnp.float32)
+        for at in range(2):
+            out[2 * half + at] = total[at * rows : (at + 1) * rows].astype(out.dtype)
+
+
+def stack_product_kernel(places, a_at, w_at, choice_ref, *refs):
+    stack_ref, *outs, w, a_sem, w_sem = refs[-7:]
+    tiles, _, columns = w.shape
+    columns //= len(w_at[0])
+    rows = stack_ref.shape[1] // 16
+
+    def pick(at):
+        ref, index = at
+        return refs[ref] if index is None else refs[ref].at[index]
+
+    def w_copy(at, choice):
+        return pltpu.make_async_copy(
+            pick(w_at[choice][at]), w.at[:, :, pl.ds(at * columns, columns)], w_sem.at[at]
+        )
+
+    def a_copy(at):
+        return pltpu.make_async_copy(
+            pick(a_at[at]), stack_ref.at[:, pl.ds(at * rows, rows)], a_sem.at[at]
+        )
+
+    for at in range(len(w_at[0])):
+        for choice in range(len(w_at)):
+
+            @pl.when(choice_ref[0] == choice)
+            def _():
+                w_copy(at, choice).start()
+
+    for group in (1, 2, 3, 0):
+        for at in places[group]:
+            a_copy(at).start()
+    for at in range(len(w_at[0])):
+        w_copy(at, 0).wait()
+    right = w[...].reshape(tiles * LANES, len(w_at[0]) * columns)
+    for group in (1, 2, 3):
+        for at in places[group]:
+            a_copy(at).wait()
+        multiply(stack_ref, right, places[group], outs[group - 1])
+    for at in places[0]:
+        a_copy(at).wait()
+
+
+def stack_product(choice, places, a_blocks, w_choices):
+    arrays = []
+
+    def at(block):
+        array, index = block
+        for known, other in enumerate(arrays):
+            if other is array:
+                return known, index
+        arrays.append(array)
+        return len(arrays) - 1, index
+
+    a_at = [at(block) for block in a_blocks]
+    w_at = [[at(block) for block in blocks] for blocks in w_choices]
+    tiles, rows, _ = a_blocks[0][0].shape
+    wide = len(w_choices[0]) * w_choices[0][0][0].shape[-1]
+    return pl.pallas_call(
+        functools.partial(stack_product_kernel, places, a_at, w_at),
+        out_shape=[pltpu.VMEM((tiles, 16 * rows, LANES), jnp.bfloat16)]
+        + [jax.ShapeDtypeStruct((4, rows, wide), jnp.bfloat16)] * 3,
+        in_specs=[pl.BlockSpec(memory_space=pltpu.SMEM)]
+        + [pl.BlockSpec(memory_space=pl.ANY)] * len(arrays),
+        out_specs=[pl.BlockSpec(memory_space=pltpu.VMEM)] * 4,
+        scratch_shapes=[
+            pltpu.VMEM((tiles, LANES, wide), jnp.bfloat16),
+            pltpu.SemaphoreType.DMA((16,)),
+            pltpu.SemaphoreType.DMA((len(w_at[0]),)),
+        ],
         compiler_params=pltpu.CompilerParams(vmem_limit_bytes=LIMIT),
         cost_estimate=pl.CostEstimate(
-            flops=0, bytes_accessed=4 * count * tiles * rows * lanes, transcendentals=0
+            flops=24 * rows * tiles * LANES * wide,
+            bytes_accessed=2 * tiles * LANES * (16 * rows + wide),
+            transcendentals=0,
         ),
-        name="stack",
-    )(*held, *blocks)
+        name="stack_product",
+    )(choice, *arrays)
 
 
 def product_kernel(places, w_at, choice_ref, a, *refs):
@@ -200,7 +260,6 @@
     outs, (w, w_sem) = refs[-2 - groups : -2], refs[-2:]
     tiles, _, columns = w.shape
     columns //= wide
-    rows = a.shape[1] // 16
 
     def pick(at):
         ref, index = at
@@ -222,20 +281,7 @@
         w_copy(at, 0).wait()
     right = w[...].reshape(tiles * LANES, wide * columns)
     for place, out in zip(places, outs):
-        for half in range(2):
-            here = [(place[2 * half + at], at) for at in range(2)]
-            left = jnp.concatenate(
-                [
-                    jnp.concatenate(
-                        [a[tile, pl.ds(block * rows, rows)] for tile in range(tiles)], axis=1
-                    )
-                    for block, _ in here
-                ],
-                axis=0,
-            )
-            total = jnp.dot(left, right, preferred_element_type=jnp.float32)
-            for _, at in here:
-                out[2 * half + at] = total[at * rows : (at + 1) * rows].astype(out.dtype)
+        multiply(a, right, place, out)
 
 
 def product(choice, groups, places, rows_stack, w_choices, after=()):
@@ -381,16 +427,17 @@
     )
     pair_3, mid_3 = to_pair(a_3), to_mid(w_3)
     core_12, core_pair_12 = to_core(a_12), to_core(pair_12)
-    rows_stack = stack(0, [a_0, pair_0, core_0, core_pair_0])
-    rows_stack = stack(4, [a_12, pair_12, core_12, core_pair_12], rows_stack)
-    pair_3, mid_3, rows_stack = lax.optimization_barrier((pair_3, mid_3, rows_stack))
     ordered_2, ordered_3 = reorder(
         order[1:], got_3, w_12, after=(pair_3, mid_3, core_12, core_pair_12)
     )
     next_1, next_2, next_3 = to_next(ordered_1), to_next(ordered_2), to_next(ordered_3)
     core_3, core_pair_3 = to_core(a_3), to_core(pair_3)
 
-    rows_stack = stack(12, [a_3, pair_3, core_3, core_pair_3], rows_stack)
+    a_0, w_0, a_12, w_12, a_3, w_3 = far([a_0, w_0, a_12, w_12, a_3, w_3])
+    a_blocks = [(block, None) for block in (a_0, pair_0, core_0, core_pair_0)]
+    for block in (a_12, pair_12, core_12, core_pair_12):
+        a_blocks += [(block, 0), (block, 1)]
+    a_blocks += [(block, None) for block in (a_3, pair_3, core_3, core_pair_3)]
     places = [(0, 2, 1, 3), (4, 8, 6, 10), (5, 9, 7, 11), (12, 14, 13, 15)]
     w_own = [(w_0, None), (w_12, 0), (w_12, 1), (w_3, None)]
     w_mid = [(mid_0, None), (mid_12, 0), (mid_12, 1), (mid_3, None)]
@@ -402,7 +449,7 @@
             outs = product(choice, groups, places, rows_stack, w_choices, after)
             totals.update(zip(groups, outs))
             after = (outs[0],)
-        return [totals[group] for group in range(4)]
+        return [totals[group] for group in sorted(totals)]
 
     def across_plane(totals):
         return [send(totals[step], flip(n, step * PLANE)) for step in (1, 2, 3)]
@@ -418,16 +465,19 @@
             pieces.append((block, fixed, start, half == 0))
         return summed[0]
 
-    own = totals_of(mid, [w_own, w_mid], ([3, 1, 2], [0]))
+    rows_stack, *own = stack_product(mid, places, a_blocks, [w_own, w_mid])
+    own = totals_of(mid, [w_own, w_mid], ([0],), (own[0],)) + own
     own[1], own[2], own[3], next_1 = lax.optimization_barrier((*own[1:], next_1))
     own_sums = across_plane(own)
     first, one, two, three = [(block, None) for block in (next_0, next_1, next_2, next_3)]
     w_low = [[first, one], [one, first], [one, two], [one, two]]
     w_high = [[two, three], [two, three], [first, three], [three, first]]
-    low = totals_of(at_plane, w_low, ([3, 1, 2, 0],), (*own_sums, own[0]))
+    low = totals_of(at_plane, w_low, ([3, 1, 2, 0],), (own[0],))
+    low[1], low[2], low[3], *own_sums = lax.optimization_barrier((*low[1:], *own_sums))
     low_sums = across_plane(low)
     summed = spread(own, own_sums, 0, 0, (low[0],))
-    high = totals_of(at_plane, w_high, ([3, 1, 2], [0]), (*low_sums, summed))
+    high = totals_of(at_plane, w_high, ([3, 1, 2], [0]), (low[0], summed))
+    high[1], high[2], high[3], *low_sums = lax.optimization_barrier((*high[1:], *low_sums))
     high_sums = across_plane(high)
     spread(low, low_sums, 1, 0, (high[0],))
     spread(high, high_sums, 1, 2)

time: 231 us -> 220 us (0.952)
  local copies, waits for them, and re-layouts: 27.8 us -> 11.9 us
  waiting for transfers between devices: 109 us -> 114 us
  starting transfers between devices: 49.6 us -> 45.3 us
  Pallas kernels: 44.2 us -> 47.7 us
    unnamed x40 -> x28, local copies, waits for them, and re-layouts: 27 us -> 11.1 us
    ppermute x37, waiting for transfers between devices: 109 us -> 114 us  [send(): return lax.ppermute(array, 'fsdp', perm=perm)]
    pallas_call x6 -> x4, Pallas kernels: 14.2 us -> 19.6 us  [the longest x1 9.06 us: stack_product(): pl.pallas_call(functools.partial(stack_product_kernel, places, a_at, w_at...]
    pallas_call x5 -> x4, Pallas kernels: 19.5 us -> 14.3 us  [product(): pl.pallas_call(functools.partial(product_kernel, [places[group] for group...]
    ppermute x37, starting transfers between devices: 49.6 us -> 45.3 us  [send(): return lax.ppermute(array, 'fsdp', perm=perm)]
  transfers between devices with their start and end apart: 37 -> 37, of which waited for: 17 -> 14; matrix products, arithmetic and copies ran while one was open for 0% -> 0% of each run, Pallas kernels for 15% -> 18%
where the time goes in v8:
time: 220 us
  waiting for transfers between devices  114 us (52%)
  Pallas kernels  47.7 us (22%)
  starting transfers between devices  45.3 us (21%)
  local copies, waits for them, and re-layouts  11.9 us (5%)
    ppermute x37, waiting for transfers between devices, send(): return lax.ppermute(array, 'fsdp', perm=perm)  114 us
    ppermute x37, starting transfers between devices, send(): return lax.ppermute(array, 'fsdp', perm=perm)  45.3 us
    pallas_call x4, Pallas kernels, product(): pl.pallas_call(functools.partial(product_kernel, [places[group] for group...  14.3 us
    unnamed x28, local copies, waits for them, and re-layouts  11.1 us
    pallas_call x2, Pallas kernels, pack(): pl.pallas_call(functools.partial(pack_kernel, apart, len(steps)), out_sha...  10.4 us
    pallas_call x1, Pallas kernels, stack_product(): pl.pallas_call(functools.partial(stack_product_kernel, places, a_at, w_at...  9.06 us
    pallas_call x2, Pallas kernels, reorder(): pl.pallas_call(functools.partial(reorder_kernel, count), out_shape=[pltpu...  7.81 us
  transfers between devices with their start and end apart: 37, of which 14 were waited for; matrix products, arithmetic and copies ran while one was open for 0% of the time, Pallas kernels for 18%

profile of v8, /device:TPU:0, one launch (start us, length us, event | category | flops | bytes accessed | tf_op | source)
XLA Modules:
  0.0 219.6 jit_solution(17629913119730698225)
XLA Ops:
  0.0 6.3 %pack.2 = (bf16[28,128,128]{2,1,0:T(8,128)(2,1)}, bf16[28,128,128]{2,1,0:T(8,128)(2,1)}, bf16[2,28,128,128]{3,2,1,0:T(8,128)(2,1)}, bf16[2,28,128,128]{3,2,1,0:T(8,128)(2,1)}) custom-call(s32[1]{0:T(128)} %bitcast.3.plane_ref.choice_ref, bf16[128,14336]{1,0:T(8,128)(2,1)} %refs_0_.3, bf16[128,14336]{1,0:T(8,128)(2,1)} %refs_1_.3, ...), custom_call_target="tpu_custom_call" | custom-call | bytes 13762560 | tf_op jit(solution)/shard_map/pack/pallas_call | solution.py:63
  6.3 3.0 %collective-permute-start.3 = (bf16[2,28,128,128]{3,2,1,0:T(8,128)(2,1)}, bf16[2,28,128,128]{3,2,1,0:T(8,128)(2,1)S(1)}, u32[]{:S(2)}, u32[]{:S(2)}) collective-permute-start(bf16[2,28,128,128]{3,2,1,0:T(8,128)(2,1)} %get-tuple-element.61), channel_id=1, source_target_pairs={{0,2},{1,3},{2,0},{3,1},{4,6},{5,7},{6,4},{7,5},{8,10},{9,11},{10,... | collective-permute-start | bytes 5505032 | tf_op jit(solution)/shard_map/ppermute | solution.py:396
  9.3 1.5 collective-permute-start.4
  10.8 1.6 collective-permute-start
  12.4 2.6 %collective-permute-start.6 = (bf16[28,128,128]{2,1,0:T(8,128)(2,1)}, bf16[28,128,128]{2,1,0:T(8,128)(2,1)S(1)}, u32[]{:S(2)}, u32[]{:S(2)}) collective-permute-start(bf16[28,128,128]{2,1,0:T(8,128)(2,1)} %get-tuple-element.65.refs_12_.refs_0_), channel_id=1, source_target_pairs={{8,0},{9,1},{10,2},{11,3},{12,4},{13,5},{14,6},{15,7},{24,8},{25,9... | collective-permute-start | bytes 2752520 | tf_op jit(solution)/shard_map/ppermute | solution.py:396
  15.7 18.7 %collective-permute-done.refs_3_.refs_0_.refs_1_ = bf16[28,128,128]{2,1,0:T(8,128)(2,1)} collective-permute-done((bf16[28,128,128]{2,1,0:T(8,128)(2,1)}, bf16[28,128,128]{2,1,0:T(8,128)(2,1)}, u32[]{:S(2)}, u32[]{:S(2)}) %collective-permute-start) | collective-permute-done | bytes 917536 | tf_op jit(solution)/shard_map/ppermute | solution.py:396
  34.4 4.1 %pack.3 = bf16[2,28,128,128]{3,2,1,0:T(8,128)(2,1)} custom-call(s32[1]{0:T(128)} %bitcast.3.plane_ref.choice_ref, bf16[128,14336]{1,0:T(8,128)(2,1)} %refs_0_.3, bf16[128,14336]{1,0:T(8,128)(2,1)} %refs_1_.3, bf16[14336,128]{1,0:T(8,128)(2,1)} %refs_2_.3, bf16[28,128,128]{2,1,0:T(8,128)(2,1)} %collective-permute-done.refs_3_.refs_0_.refs_1_), custom_call_target="tpu_custom_call" | custom-call | bytes 4587520 | tf_op jit(solution)/shard_map/pack/pallas_call | solution.py:63
  38.5 11.0 %collective-permute-done.3.one = bf16[2,28,128,128]{3,2,1,0:T(8,128)(2,1)S(1)} collective-permute-done((bf16[2,28,128,128]{3,2,1,0:T(8,128)(2,1)}, bf16[2,28,128,128]{3,2,1,0:T(8,128)(2,1)S(1)}, u32[]{:S(2)}, u32[]{:S(2)}) %collective-permute-start.3) | collective-permute-done | bytes 1835040 | tf_op jit(solution)/shard_map/ppermute | solution.py:396
  49.5 1.5 collective-permute-done.4.two
  51.0 1.5 collective-permute-start.7
  52.5 2.8 %unpack_pair.1 = (bf16[2,28,128,128]{3,2,1,0:T(8,128)(2,1)}, bf16[2,28,128,128]{3,2,1,0:T(8,128)(2,1)}) custom-call(bf16[2,28,128,128]{3,2,1,0:T(8,128)(2,1)S(1)} %collective-permute-done.3.one, bf16[2,28,128,128]{3,2,1,0:T(8,128)(2,1)S(1)} %collective-permute-done.4.two, bf16[28,128,128]{2,1,0:T(8,128)(2,1)} %collective-permute-done.refs_3_.refs_0_.refs_1_, ...), custom_call_target="tpu_custom_call" | custom-call | bytes 7340032 | tf_op jit(solution)/shard_map/unpack_pair/pallas_call | solution.py:106
  55.3 4.7 %collective-permute-start.8 = (bf16[2,28,128,128]{3,2,1,0:T(8,128)(2,1)}, bf16[2,28,128,128]{3,2,1,0:T(8,128)(2,1)}, u32[]{:S(2)}, u32[]{:S(2)}) collective-permute-start(bf16[2,28,128,128]{3,2,1,0:T(8,128)(2,1)} %get-tuple-element.68.refs_4_), channel_id=1, source_target_pairs={{0,8},{1,9},{2,10},{3,11},{4,12},{5,13},{6,14},{7,15},{8,0},{9,1},... | collective-permute-start | bytes 5505032 | tf_op jit(solution)/shard_map/ppermute | solution.py:396
  61.4 31.4 %collective-permute-done.7.packed = bf16[2,28,128,128]{3,2,1,0:T(8,128)(2,1)} collective-permute-done((bf16[2,28,128,128]{3,2,1,0:T(8,128)(2,1)}, bf16[2,28,128,128]{3,2,1,0:T(8,128)(2,1)}, u32[]{:S(2)}, u32[]{:S(2)}) %collective-permute-start.7) | collective-permute-done | bytes 1835040 | tf_op jit(solution)/shard_map/ppermute | solution.py:396
  92.8 4.7 %collective-permute-done.8.refs_5_ = bf16[2,28,128,128]{3,2,1,0:T(8,128)(2,1)} collective-permute-done((bf16[2,28,128,128]{3,2,1,0:T(8,128)(2,1)}, bf16[2,28,128,128]{3,2,1,0:T(8,128)(2,1)}, u32[]{:S(2)}, u32[]{:S(2)}) %collective-permute-start.8) | collective-permute-done | bytes 1835040 | tf_op jit(solution)/shard_map/ppermute | solution.py:396
  98.3 1.2 copy-done.2
  99.5 1.5 copy-done
  101.0 1.5 copy-done.3
  102.5 3.8 %reorder.2 = (bf16[28,128,128]{2,1,0:T(8,128)(2,1)}, bf16[28,128,128]{2,1,0:T(8,128)(2,1)}, bf16[28,128,128]{2,1,0:T(8,128)(2,1)}) custom-call(s32[3]{0:T(128)S(1)} %pad_add_fusion.1.order_ref, bf16[2,28,128,128]{3,2,1,0:T(8,128)(2,1)} %collective-permute-done.7.packed, bf16[2,28,128,128]{3,2,1,0:T(8,128)(2,1)S(1)} %copy-done, ...), custom_call_target="tpu_custom_call" | custom-call | bytes 7340032 | tf_op jit(solution)/shard_map/reorder/pallas_call | solution.py:144
  106.4 3.4 %collective-permute-start.12 = (bf16[28,128,128]{2,1,0:T(8,128)(2,1)}, bf16[28,128,128]{2,1,0:T(8,128)(2,1)}, u32[]{:S(2)}, u32[]{:S(2)}) collective-permute-start(bf16[28,128,128]{2,1,0:T(8,128)(2,1)} %get-tuple-element.71.refs_8_), channel_id=1, source_target_pairs={{0,8},{1,9},{2,10},{3,11},{4,12},{5,13},{6,14},{7,15},{8,0},{9,1},... | collective-permute-start | bytes 2752520 | tf_op jit(solution)/shard_map/ppermute | solution.py:396
  110.6 18.9 %collective-permute-done.12.refs_9_.refs_0_ = bf16[28,128,128]{2,1,0:T(8,128)(2,1)} collective-permute-done((bf16[28,128,128]{2,1,0:T(8,128)(2,1)}, bf16[28,128,128]{2,1,0:T(8,128)(2,1)}, u32[]{:S(2)}, u32[]{:S(2)}) %collective-permute-start.12) | collective-permute-done | bytes 917536 | tf_op jit(solution)/shard_map/ppermute | solution.py:396
  129.5 5.3 %collective-permute-start.16 = (bf16[28,128,128]{2,1,0:T(8,128)(2,1)}, bf16[28,128,128]{2,1,0:T(8,128)(2,1)}, u32[]{:S(2)}, u32[]{:S(2)}) collective-permute-start(bf16[28,128,128]{2,1,0:T(8,128)(2,1)} %get-tuple-element.77), channel_id=1, source_target_pairs={{8,0},{9,1},{10,2},{11,3},{12,4},{13,5},{14,6},{15,7},{24,8},{25,9... | collective-permute-start | bytes 2752520 | tf_op jit(solution)/shard_map/ppermute | solution.py:396
  135.0 4.0 %reorder.3 = (bf16[28,128,128]{2,1,0:T(8,128)(2,1)}, bf16[28,128,128]{2,1,0:T(8,128)(2,1)}) custom-call(s32[2]{0:T(128)S(1)} %slice_bitcast_fusion.order_ref, bf16[2,28,128,128]{3,2,1,0:T(8,128)(2,1)} %collective-permute-done.7.packed, bf16[2,28,128,128]{3,2,1,0:T(8,128)(2,1)S(1)} %copy-done.1, ...), custom_call_target="tpu_custom_call" | custom-call | bytes 7340032 | tf_op jit(solution)/shard_map/reorder/pallas_call | solution.py:144
  139.3 1.5 collective-permute-start.24
  140.8 1.5 copy-done.4
  142.3 1.2 copy-done.7
  143.5 1.2 copy-done.9
  144.7 1.5 copy-done.11
  146.2 1.5 copy-done.13
  147.7 9.1 %stack_product.1 = (bf16[28,2048,128]{2,1,0:T(8,128)(2,1)S(1)}, bf16[4,128,512]{2,1,0:T(8,128)(2,1)S(1)}, bf16[4,128,512]{2,1,0:T(8,128)(2,1)S(1)}, bf16[4,128,512]{2,1,0:T(8,128)(2,1)S(1)}) custom-call(s32[1]{0:T(128)} %bitcast.2.choice_ref, bf16[28,128,128]{2,1,0:T(8,128)(2,1)} %get-tuple-element.60.refs_0_, ...), custom_call_target="tpu_custom_call" | custom-call | flops 5637144576 | bytes 18350080 | tf_op jit(solution)/shard_map/stack_product/pallas_call | solution.py:236
  157.8 2.4 %collective-permute-start.20 = (bf16[4,128,512]{2,1,0:T(8,128)(2,1)S(1)}, bf16[4,128,512]{2,1,0:T(8,128)(2,1)S(1)}, u32[]{:S(2)}, u32[]{:S(2)}) collective-permute-start(bf16[4,128,512]{2,1,0:T(8,128)(2,1)S(1)} %get-tuple-element.85), channel_id=1, source_target_pairs={{0,6},{1,7},{2,4},{3,5},{4,2},{5,3},{6,0},{7,1},{8,14},{9,15},{10,... | collective-permute-start | bytes 1572872 | tf_op jit(solution)/shard_map/ppermute | solution.py:396
  160.3 4.1 %product.4.refs_3_.own = f32[4,128,512]{2,1,0:T(8,128)S(1)} custom-call(s32[1]{0:T(128)} %bitcast.2.choice_ref, bf16[28,2048,128]{2,1,0:T(8,128)(2,1)S(1)} %get-tuple-element.73.a, bf16[28,128,128]{2,1,0:T(8,128)(2,1)} %get-tuple-element.65.refs_12_.refs_0_, bf16[2,28,128,128]{3,2,1,0:T(8,128)(2,1)} %get-tuple-element.70.w_12.refs_13_.refs_1_, ...), custom_call_target="tpu_custom_call" | custom-call | flops 1879048192 | bytes 7340032 | tf_op jit(solution)/shard_map/product/pallas_call | solution.py:305
  164.4 11.2 %collective-permute-done.17.refs_2_.refs_0_ = bf16[28,128,128]{2,1,0:T(8,128)(2,1)S(1)} collective-permute-done((bf16[28,128,128]{2,1,0:T(8,128)(2,1)}, bf16[28,128,128]{2,1,0:T(8,128)(2,1)S(1)}, u32[]{:S(2)}, u32[]{:S(2)}) %collective-permute-start.17) | collective-permute-done | bytes 917536 | tf_op jit(solution)/shard_map/ppermute | solution.py:396
  175.6 5.3 %product.5 = (bf16[4,128,256]{2,1,0:T(8,128)(2,1)S(1)}, bf16[4,128,256]{2,1,0:T(8,128)(2,1)S(1)}, bf16[4,128,256]{2,1,0:T(8,128)(2,1)S(1)}, f32[4,128,256]{2,1,0:T(8,128)S(1)}) custom-call(s32[1]{0:T(128)} %bitcast.3.plane_ref.choice_ref, bf16[28,2048,128]{2,1,0:T(8,128)(2,1)S(1)} %get-tuple-element.73.a, ...), custom_call_target="tpu_custom_call" | custom-call | flops 3758096384 | bytes 16515072 | tf_op jit(solution)/shard_map/product/pallas_call | solution.py:305
  181.0 0.8 collective-permute-start.25
  182.2 2.3 %collective-permute-start.27 = (bf16[4,128,256]{2,1,0:T(8,128)(2,1)S(1)}, bf16[4,128,256]{2,1,0:T(8,128)(2,1)S(1)}, u32[]{:S(2)}, u32[]{:S(2)}) collective-permute-start(bf16[4,128,256]{2,1,0:T(8,128)(2,1)S(1)} %get-tuple-element.100), channel_id=1, source_target_pairs={{0,6},{1,7},{2,4},{3,5},{4,2},{5,3},{6,0},{7,1},{8,14},{9,15},{10,... | collective-permute-start | bytes 786440 | tf_op jit(solution)/shard_map/ppermute | solution.py:396
  184.5 0.8 add.39
  185.4 7.6 %collective-permute-done.24.refs_1_ = bf16[28,128,128]{2,1,0:T(8,128)(2,1)S(1)} collective-permute-done((bf16[28,128,128]{2,1,0:T(8,128)(2,1)}, bf16[28,128,128]{2,1,0:T(8,128)(2,1)S(1)}, u32[]{:S(2)}, u32[]{:S(2)}) %collective-permute-start.24) | collective-permute-done | bytes 917536 | tf_op jit(solution)/shard_map/ppermute | solution.py:396
  193.0 3.4 %product.6 = (bf16[4,128,256]{2,1,0:T(8,128)(2,1)S(1)}, bf16[4,128,256]{2,1,0:T(8,128)(2,1)S(1)}, bf16[4,128,256]{2,1,0:T(8,128)(2,1)S(1)}) custom-call(s32[1]{0:T(128)} %bitcast.3.plane_ref.choice_ref, bf16[28,2048,128]{2,1,0:T(8,128)(2,1)S(1)} %get-tuple-element.73.a, bf16[28,128,128]{2,1,0:T(8,128)(2,1)S(1)} %collective-permute-done.17.refs_2_.refs_0_, ...), custom_call_target="tpu_custom_call" | custom-call | flops 2818572288 | bytes 12845056 | tf_op jit(solution)/shard_map/product/pallas_call | solution.py:305
  197.5 2.5 %collective-permute-start.33 = (bf16[4,128,256]{2,1,0:T(8,128)(2,1)S(1)}, bf16[4,128,256]{2,1,0:T(8,128)(2,1)S(1)}, u32[]{:S(2)}, u32[]{:S(2)}) collective-permute-start(bf16[4,128,256]{2,1,0:T(8,128)(2,1)S(1)} %get-tuple-element.110.refs_3_), channel_id=1, source_target_pairs={{0,6},{1,7},{2,4},{3,5},{4,2},{5,3},{6,0},{7,1},{8,14},{9,15},{10,... | collective-permute-start | bytes 786440 | tf_op jit(solution)/shard_map/ppermute | solution.py:396
  200.0 2.0 collective-permute-start.22
  202.0 3.3 %collective-permute-done.31.one = bf16[4,128,256]{2,1,0:T(8,128)(2,1)S(1)} collective-permute-done((bf16[4,128,256]{2,1,0:T(8,128)(2,1)S(1)}, bf16[4,128,256]{2,1,0:T(8,128)(2,1)S(1)}, u32[]{:S(2)}, u32[]{:S(2)}) %collective-permute-start.31) | collective-permute-done | bytes 262176 | tf_op jit(solution)/shard_map/ppermute | solution.py:396
  205.3 1.5 product.7.refs_0_.own
  206.9 1.4 collective-permute-done.32.two
  209.0 1.2 collective-permute-start.29
  211.4 1.2 collective-permute-start.35
  213.3 1.2 collective-permute-done.30.refs_7_
  214.5 2.0 collective-permute-done.35.refs_10_
  217.3 2.3 %assemble.1 = bf16[128,4096]{1,0:T(8,128)(2,1)} custom-call(s32[2]{0:T(128)S(1)} %pad_add_fusion.place_ref, bf16[128,512]{1,0:T(8,128)(2,1)S(1)} %get-tuple-element.90.refs_4_.refs_0_, bf16[128,512]{1,0:T(8,128)(2,1)} %collective-permute-done.21.refs_1_, bf16[128,512]{1,0:T(8,128)(2,1)} %collective-permute-done.22.refs_2_, ...), custom_call_target="tpu_custom_call" | custom-call | tf_op jit(solution)/shard_map/assemble/pallas_call | solution.py:373
  (73 shorter events, 10.0 us)
Async XLA Ops:
  6.3 43.2 %collective-permute-start.3 = (bf16[2,28,128,128]{3,2,1,0:T(8,128)(2,1)}, bf16[2,28,128,128]{3,2,1,0:T(8,128)(2,1)S(1)}, u32[]{:S(2)}, u32[]{:S(2)}) collective-permute-start(bf16[2,28,128,128]{3,2,1,0:T(8,128)(2,1)} %get-tuple-element.61), channel_id=1, source_target_pairs={{0,2},{1,3},{2,0},{3,1},{4,6},{5,7},{6,4},{7,5},{8,10},{9,11},{10,... | collective-permute-start | bytes 5505032 | tf_op jit(solution)/shard_map/ppermute | solution.py:396
  9.3 41.7 %collective-permute-start.4 = (bf16[2,28,128,128]{3,2,1,0:T(8,128)(2,1)}, bf16[2,28,128,128]{3,2,1,0:T(8,128)(2,1)S(1)}, u32[]{:S(2)}, u32[]{:S(2)}) collective-permute-start(bf16[2,28,128,128]{3,2,1,0:T(8,128)(2,1)} %get-tuple-element.62), channel_id=1, source_target_pairs={{0,4},{1,5},{2,6},{3,7},{4,0},{5,1},{6,2},{7,3},{8,12},{9,13},{10,... | collective-permute-start | bytes 5505032 | tf_op jit(solution)/shard_map/ppermute | solution.py:396
  10.8 23.6 %collective-permute-start = (bf16[28,128,128]{2,1,0:T(8,128)(2,1)}, bf16[28,128,128]{2,1,0:T(8,128)(2,1)}, u32[]{:S(2)}, u32[]{:S(2)}) collective-permute-start(bf16[28,128,128]{2,1,0:T(8,128)(2,1)} %get-tuple-element.60.refs_0_), channel_id=1, source_target_pairs={{0,8},{1,9},{2,10},{3,11},{4,12},{5,13},{6,14},{7,15},{8,0},{9,1},... | collective-permute-start | bytes 2752520 | tf_op jit(solution)/shard_map/ppermute | solution.py:396
  12.4 40.1 %collective-permute-start.6 = (bf16[28,128,128]{2,1,0:T(8,128)(2,1)}, bf16[28,128,128]{2,1,0:T(8,128)(2,1)S(1)}, u32[]{:S(2)}, u32[]{:S(2)}) collective-permute-start(bf16[28,128,128]{2,1,0:T(8,128)(2,1)} %get-tuple-element.65.refs_12_.refs_0_), channel_id=1, source_target_pairs={{8,0},{9,1},{10,2},{11,3},{12,4},{13,5},{14,6},{15,7},{24,8},{25,9... | collective-permute-start | bytes 2752520 | tf_op jit(solution)/shard_map/ppermute | solution.py:396
  15.0 37.5 %collective-permute-start.5 = (bf16[28,128,128]{2,1,0:T(8,128)(2,1)}, bf16[28,128,128]{2,1,0:T(8,128)(2,1)S(1)}, u32[]{:S(2)}, u32[]{:S(2)}) collective-permute-start(bf16[28,128,128]{2,1,0:T(8,128)(2,1)} %get-tuple-element.65.refs_12_.refs_0_), channel_id=1, source_target_pairs={{8,16},{9,17},{10,18},{11,19},{12,20},{13,21},{14,22},{15,23},{16,... | collective-permute-start | bytes 2752520 | tf_op jit(solution)/shard_map/ppermute | solution.py:396
  51.0 41.8 %collective-permute-start.7 = (bf16[2,28,128,128]{3,2,1,0:T(8,128)(2,1)}, bf16[2,28,128,128]{3,2,1,0:T(8,128)(2,1)}, u32[]{:S(2)}, u32[]{:S(2)}) collective-permute-start(bf16[2,28,128,128]{3,2,1,0:T(8,128)(2,1)} %pack.3), channel_id=1, source_target_pairs={{0,6},{1,7},{2,4},{3,5},{4,2},{5,3},{6,0},{7,1},{8,14},{9,15},{10,... | collective-permute-start | bytes 5505032 | tf_op jit(solution)/shard_map/ppermute | solution.py:396
  52.5 2.8 %copy-start.8 = (bf16[28,128,128]{2,1,0:T(8,128)(2,1)}, bf16[28,128,128]{2,1,0:T(8,128)(2,1)S(1)}, u32[]{:S(2)}) copy-start(bf16[28,128,128]{2,1,0:T(8,128)(2,1)S(1)} %collective-permute-done.5.refs_1_.refs_15_.refs_3_) | copy-start | bytes 2752516
  55.3 42.2 %collective-permute-start.8 = (bf16[2,28,128,128]{3,2,1,0:T(8,128)(2,1)}, bf16[2,28,128,128]{3,2,1,0:T(8,128)(2,1)}, u32[]{:S(2)}, u32[]{:S(2)}) collective-permute-start(bf16[2,28,128,128]{3,2,1,0:T(8,128)(2,1)} %get-tuple-element.68.refs_4_), channel_id=1, source_target_pairs={{0,8},{1,9},{2,10},{3,11},{4,12},{5,13},{6,14},{7,15},{8,0},{9,1},... | collective-permute-start | bytes 5505032 | tf_op jit(solution)/shard_map/ppermute | solution.py:396
  60.0 38.3 %collective-permute-start.11 = (bf16[2,28,128,128]{3,2,1,0:T(8,128)(2,1)}, bf16[2,28,128,128]{3,2,1,0:T(8,128)(2,1)S(1)}, u32[]{:S(2)}, u32[]{:S(2)}) collective-permute-start(bf16[2,28,128,128]{3,2,1,0:T(8,128)(2,1)} %get-tuple-element.70.w_12.refs_13_.refs_1_), channel_id=1, source_target_pairs={{8,16},{9,17},{10,18},{11,19},{12,20},{13,21},{14,22},{15,23},{16,... | collective-permute-start | bytes 5505032 | tf_op jit(solution)/shard_map/ppermute | solution.py:396
  60.8 37.5 %collective-permute-start.1 = (bf16[28,128,128]{2,1,0:T(8,128)(2,1)}, bf16[28,128,128]{2,1,0:T(8,128)(2,1)}, u32[]{:S(2)}, u32[]{:S(2)}) collective-permute-start(bf16[28,128,128]{2,1,0:T(8,128)(2,1)} %get-tuple-element.60.refs_0_), channel_id=1, source_target_pairs={{0,1},{1,0},{2,3},{3,2},{4,5},{5,4},{6,7},{7,6},{8,9},{9,8},{10,11... | collective-permute-start | bytes 2752520 | tf_op jit(solution)/shard_map/ppermute | solution.py:396
  60.9 37.4 %collective-permute-start.2 = (bf16[28,128,128]{2,1,0:T(8,128)(2,1)}, bf16[28,128,128]{2,1,0:T(8,128)(2,1)}, u32[]{:S(2)}, u32[]{:S(2)}) collective-permute-start(bf16[28,128,128]{2,1,0:T(8,128)(2,1)} %collective-permute-done.refs_3_.refs_0_.refs_1_), channel_id=1, source_target_pairs={{0,1},{1,0},{2,3},{3,2},{4,5},{5,4},{6,7},{7,6},{8,9},{9,8},{10,11... | collective-permute-start | bytes 2752520 | tf_op jit(solution)/shard_map/ppermute | solution.py:396
  92.8 42.2 %collective-permute-start.9 = (bf16[2,28,128,128]{3,2,1,0:T(8,128)(2,1)}, bf16[2,28,128,128]{3,2,1,0:T(8,128)(2,1)S(1)}, u32[]{:S(2)}, u32[]{:S(2)}) collective-permute-start(bf16[2,28,128,128]{3,2,1,0:T(8,128)(2,1)} %get-tuple-element.68.refs_4_), channel_id=1, source_target_pairs={{0,1},{1,0},{2,3},{3,2},{4,5},{5,4},{6,7},{7,6},{8,9},{9,8},{10,11... | collective-permute-start | bytes 5505032 | tf_op jit(solution)/shard_map/ppermute | solution.py:396
  97.5 37.4 %collective-permute-start.10 = (bf16[2,28,128,128]{3,2,1,0:T(8,128)(2,1)}, bf16[2,28,128,128]{3,2,1,0:T(8,128)(2,1)S(1)}, u32[]{:S(2)}, u32[]{:S(2)}) collective-permute-start(bf16[2,28,128,128]{3,2,1,0:T(8,128)(2,1)} %collective-permute-done.8.refs_5_), channel_id=1, source_target_pairs={{0,1},{1,0},{2,3},{3,2},{4,5},{5,4},{6,7},{7,6},{8,9},{9,8},{10,11... | collective-permute-start | bytes 5505032 | tf_op jit(solution)/shard_map/ppermute | solution.py:396
  99.5 1.5 copy-start
  101.0 1.5 copy-start.3
  102.5 32.4 %copy-start.1 = (bf16[2,28,128,128]{3,2,1,0:T(8,128)(2,1)S(1)}, bf16[2,28,128,128]{3,2,1,0:T(8,128)(2,1)}, u32[]{:S(2)}) copy-start(bf16[2,28,128,128]{3,2,1,0:T(8,128)(2,1)} %get-tuple-element.70.w_12.refs_13_.refs_1_) | copy-start | bytes 5505028
  106.4 23.1 %collective-permute-start.12 = (bf16[28,128,128]{2,1,0:T(8,128)(2,1)}, bf16[28,128,128]{2,1,0:T(8,128)(2,1)}, u32[]{:S(2)}, u32[]{:S(2)}) collective-permute-start(bf16[28,128,128]{2,1,0:T(8,128)(2,1)} %get-tuple-element.71.refs_8_), channel_id=1, source_target_pairs={{0,8},{1,9},{2,10},{3,11},{4,12},{5,13},{6,14},{7,15},{8,0},{9,1},... | collective-permute-start | bytes 2752520 | tf_op jit(solution)/shard_map/ppermute | solution.py:396
  109.8 19.7 %collective-permute-start.15 = (bf16[28,128,128]{2,1,0:T(8,128)(2,1)}, bf16[28,128,128]{2,1,0:T(8,128)(2,1)S(1)}, u32[]{:S(2)}, u32[]{:S(2)}) collective-permute-start(bf16[28,128,128]{2,1,0:T(8,128)(2,1)} %get-tuple-element.72.refs_14_.refs_2_), channel_id=1, source_target_pairs={{8,16},{9,17},{10,18},{11,19},{12,20},{13,21},{14,22},{15,23},{16,... | collective-permute-start | bytes 2752520 | tf_op jit(solution)/shard_map/ppermute | solution.py:396
  110.5 30.3 %collective-permute-start.13 = (bf16[28,128,128]{2,1,0:T(8,128)(2,1)}, bf16[28,128,128]{2,1,0:T(8,128)(2,1)}, u32[]{:S(2)}, u32[]{:S(2)}) collective-permute-start(bf16[28,128,128]{2,1,0:T(8,128)(2,1)} %get-tuple-element.71.refs_8_), channel_id=1, source_target_pairs={{0,1},{1,0},{2,3},{3,2},{4,5},{5,4},{6,7},{7,6},{8,9},{9,8},{10,11... | collective-permute-start | bytes 2752520 | tf_op jit(solution)/shard_map/ppermute | solution.py:396
  129.5 11.3 %collective-permute-start.14 = (bf16[28,128,128]{2,1,0:T(8,128)(2,1)}, bf16[28,128,128]{2,1,0:T(8,128)(2,1)}, u32[]{:S(2)}, u32[]{:S(2)}) collective-permute-start(bf16[28,128,128]{2,1,0:T(8,128)(2,1)} %collective-permute-done.12.refs_9_.refs_0_), channel_id=1, source_target_pairs={{0,1},{1,0},{2,3},{3,2},{4,5},{5,4},{6,7},{7,6},{8,9},{9,8},{10,11... | collective-permute-start | bytes 2752520 | tf_op jit(solution)/shard_map/ppermute | solution.py:396
  129.5 9.4 %copy-start.6 = (bf16[28,128,128]{2,1,0:T(8,128)(2,1)}, bf16[28,128,128]{2,1,0:T(8,128)(2,1)S(1)}, u32[]{:S(2)}) copy-start(bf16[28,128,128]{2,1,0:T(8,128)(2,1)S(1)} %collective-permute-done.15.refs_17_.refs_5_.refs_1_) | copy-start | bytes 2752516
  129.5 27.2 %collective-permute-start.16 = (bf16[28,128,128]{2,1,0:T(8,128)(2,1)}, bf16[28,128,128]{2,1,0:T(8,128)(2,1)}, u32[]{:S(2)}, u32[]{:S(2)}) collective-permute-start(bf16[28,128,128]{2,1,0:T(8,128)(2,1)} %get-tuple-element.77), channel_id=1, source_target_pairs={{8,0},{9,1},{10,2},{11,3},{12,4},{13,5},{14,6},{15,7},{24,8},{25,9... | collective-permute-start | bytes 2752520 | tf_op jit(solution)/shard_map/ppermute | solution.py:396
  134.9 4.0 %copy-start.12 = (bf16[2,28,128,128]{3,2,1,0:T(8,128)(2,1)}, bf16[2,28,128,128]{3,2,1,0:T(8,128)(2,1)S(1)}, u32[]{:S(2)}) copy-start(bf16[2,28,128,128]{3,2,1,0:T(8,128)(2,1)S(1)} %collective-permute-done.10.refs_7_.refs_3_) | copy-start | bytes 5505028
  135.0 4.0 %copy-start.10 = (bf16[2,28,128,128]{3,2,1,0:T(8,128)(2,1)}, bf16[2,28,128,128]{3,2,1,0:T(8,128)(2,1)S(1)}, u32[]{:S(2)}) copy-start(bf16[2,28,128,128]{3,2,1,0:T(8,128)(2,1)S(1)} %collective-permute-done.9.refs_6_.refs_2_) | copy-start | bytes 5505028
  139.0 36.7 %collective-permute-start.17 = (bf16[28,128,128]{2,1,0:T(8,128)(2,1)}, bf16[28,128,128]{2,1,0:T(8,128)(2,1)S(1)}, u32[]{:S(2)}, u32[]{:S(2)}) collective-permute-start(bf16[28,128,128]{2,1,0:T(8,128)(2,1)} %get-tuple-element.79), channel_id=1, source_target_pairs={{8,0},{9,1},{10,2},{11,3},{12,4},{13,5},{14,6},{15,7},{24,8},{25,9... | collective-permute-start | bytes 2752520 | tf_op jit(solution)/shard_map/ppermute | solution.py:396
  139.3 53.7 %collective-permute-start.24 = (bf16[28,128,128]{2,1,0:T(8,128)(2,1)}, bf16[28,128,128]{2,1,0:T(8,128)(2,1)S(1)}, u32[]{:S(2)}, u32[]{:S(2)}) collective-permute-start(bf16[28,128,128]{2,1,0:T(8,128)(2,1)} %get-tuple-element.94), channel_id=1, source_target_pairs={{8,0},{9,1},{10,2},{11,3},{12,4},{13,5},{14,6},{15,7},{24,8},{25,9... | collective-permute-start | bytes 2752520 | tf_op jit(solution)/shard_map/ppermute | solution.py:396
  140.8 1.5 copy-start.4
  144.7 1.5 copy-start.11
  146.2 1.5 copy-start.13
  147.7 12.6 %copy-start.5 = (bf16[2,28,128,128]{3,2,1,0:T(8,128)(2,1)S(1)}, bf16[2,28,128,128]{3,2,1,0:T(8,128)(2,1)}, u32[]{:S(2)}) copy-start(bf16[2,28,128,128]{3,2,1,0:T(8,128)(2,1)} %copy-done.2) | copy-start | bytes 5505028
  156.7 24.2 %collective-permute-start.18 = (bf16[4,128,512]{2,1,0:T(8,128)(2,1)S(1)}, bf16[4,128,512]{2,1,0:T(8,128)(2,1)S(1)}, u32[]{:S(2)}, u32[]{:S(2)}) collective-permute-start(bf16[4,128,512]{2,1,0:T(8,128)(2,1)S(1)} %get-tuple-element.83.refs_6_), channel_id=1, source_target_pairs={{0,2},{1,3},{2,0},{3,1},{4,6},{5,7},{6,4},{7,5},{8,10},{9,11},{10,... | collective-permute-start | bytes 1572872 | tf_op jit(solution)/shard_map/ppermute | solution.py:396
  157.3 23.6 %collective-permute-start.19 = (bf16[4,128,512]{2,1,0:T(8,128)(2,1)S(1)}, bf16[4,128,512]{2,1,0:T(8,128)(2,1)S(1)}, u32[]{:S(2)}, u32[]{:S(2)}) collective-permute-start(bf16[4,128,512]{2,1,0:T(8,128)(2,1)S(1)} %get-tuple-element.84), channel_id=1, source_target_pairs={{0,4},{1,5},{2,6},{3,7},{4,0},{5,1},{6,2},{7,3},{8,12},{9,13},{10,... | collective-permute-start | bytes 1572872 | tf_op jit(solution)/shard_map/ppermute | solution.py:396
  157.8 23.1 %collective-permute-start.20 = (bf16[4,128,512]{2,1,0:T(8,128)(2,1)S(1)}, bf16[4,128,512]{2,1,0:T(8,128)(2,1)S(1)}, u32[]{:S(2)}, u32[]{:S(2)}) collective-permute-start(bf16[4,128,512]{2,1,0:T(8,128)(2,1)S(1)} %get-tuple-element.85), channel_id=1, source_target_pairs={{0,6},{1,7},{2,4},{3,5},{4,2},{5,3},{6,0},{7,1},{8,14},{9,15},{10,... | collective-permute-start | bytes 1572872 | tf_op jit(solution)/shard_map/ppermute | solution.py:396
  181.0 15.4 %collective-permute-start.25 = (bf16[4,128,256]{2,1,0:T(8,128)(2,1)S(1)}, bf16[4,128,256]{2,1,0:T(8,128)(2,1)S(1)}, u32[]{:S(2)}, u32[]{:S(2)}) collective-permute-start(bf16[4,128,256]{2,1,0:T(8,128)(2,1)S(1)} %get-tuple-element.98), channel_id=1, source_target_pairs={{0,2},{1,3},{2,0},{3,1},{4,6},{5,7},{6,4},{7,5},{8,10},{9,11},{10,... | collective-permute-start | bytes 786440 | tf_op jit(solution)/shard_map/ppermute | solution.py:396
  181.8 14.6 %collective-permute-start.26 = (bf16[4,128,256]{2,1,0:T(8,128)(2,1)S(1)}, bf16[4,128,256]{2,1,0:T(8,128)(2,1)S(1)}, u32[]{:S(2)}, u32[]{:S(2)}) collective-permute-start(bf16[4,128,256]{2,1,0:T(8,128)(2,1)S(1)} %get-tuple-element.99), channel_id=1, source_target_pairs={{0,4},{1,5},{2,6},{3,7},{4,0},{5,1},{6,2},{7,3},{8,12},{9,13},{10,... | collective-permute-start | bytes 786440 | tf_op jit(solution)/shard_map/ppermute | solution.py:396
  182.2 14.2 %collective-permute-start.27 = (bf16[4,128,256]{2,1,0:T(8,128)(2,1)S(1)}, bf16[4,128,256]{2,1,0:T(8,128)(2,1)S(1)}, u32[]{:S(2)}, u32[]{:S(2)}) collective-permute-start(bf16[4,128,256]{2,1,0:T(8,128)(2,1)S(1)} %get-tuple-element.100), channel_id=1, source_target_pairs={{0,6},{1,7},{2,4},{3,5},{4,2},{5,3},{6,0},{7,1},{8,14},{9,15},{10,... | collective-permute-start | bytes 786440 | tf_op jit(solution)/shard_map/ppermute | solution.py:396
  196.4 8.9 %collective-permute-start.31 = (bf16[4,128,256]{2,1,0:T(8,128)(2,1)S(1)}, bf16[4,128,256]{2,1,0:T(8,128)(2,1)S(1)}, u32[]{:S(2)}, u32[]{:S(2)}) collective-permute-start(bf16[4,128,256]{2,1,0:T(8,128)(2,1)S(1)} %get-tuple-element.108), channel_id=1, source_target_pairs={{0,2},{1,3},{2,0},{3,1},{4,6},{5,7},{6,4},{7,5},{8,10},{9,11},{10,... | collective-permute-start | bytes 786440 | tf_op jit(solution)/shard_map/ppermute | solution.py:396
  197.0 11.3 %collective-permute-start.32 = (bf16[4,128,256]{2,1,0:T(8,128)(2,1)S(1)}, bf16[4,128,256]{2,1,0:T(8,128)(2,1)S(1)}, u32[]{:S(2)}, u32[]{:S(2)}) collective-permute-start(bf16[4,128,256]{2,1,0:T(8,128)(2,1)S(1)} %get-tuple-element.109), channel_id=1, source_target_pairs={{0,4},{1,5},{2,6},{3,7},{4,0},{5,1},{6,2},{7,3},{8,12},{9,13},{10,... | collective-permute-start | bytes 786440 | tf_op jit(solution)/shard_map/ppermute | solution.py:396
  197.5 11.5 %collective-permute-start.33 = (bf16[4,128,256]{2,1,0:T(8,128)(2,1)S(1)}, bf16[4,128,256]{2,1,0:T(8,128)(2,1)S(1)}, u32[]{:S(2)}, u32[]{:S(2)}) collective-permute-start(bf16[4,128,256]{2,1,0:T(8,128)(2,1)S(1)} %get-tuple-element.110.refs_3_), channel_id=1, source_target_pairs={{0,6},{1,7},{2,4},{3,5},{4,2},{5,3},{6,0},{7,1},{8,14},{9,15},{10,... | collective-permute-start | bytes 786440 | tf_op jit(solution)/shard_map/ppermute | solution.py:396
  200.0 10.4 %collective-permute-start.21 = (bf16[128,512]{1,0:T(8,128)(2,1)}, bf16[128,512]{1,0:T(8,128)(2,1)}, u32[]{:S(2)}, u32[]{:S(2)}) collective-permute-start(bf16[128,512]{1,0:T(8,128)(2,1)} %get-tuple-element.91), channel_id=1, source_target_pairs={{0,1},{1,0},{2,3},{3,2},{4,5},{5,4},{6,7},{7,6},{8,9},{9,8},{10,11... | collective-permute-start | bytes 393224 | tf_op jit(solution)/shard_map/ppermute | solution.py:396
  200.0 10.7 %collective-permute-start.22 = (bf16[128,512]{1,0:T(8,128)(2,1)}, bf16[128,512]{1,0:T(8,128)(2,1)}, u32[]{:S(2)}, u32[]{:S(2)}) collective-permute-start(bf16[128,512]{1,0:T(8,128)(2,1)} %get-tuple-element.92), channel_id=1, source_target_pairs={{0,8},{1,9},{2,10},{3,11},{4,12},{5,13},{6,14},{7,15},{8,0},{9,1},... | collective-permute-start | bytes 393224 | tf_op jit(solution)/shard_map/ppermute | solution.py:396
  205.3 6.1 %collective-permute-start.23 = (bf16[128,512]{1,0:T(8,128)(2,1)}, bf16[128,512]{1,0:T(8,128)(2,1)}, u32[]{:S(2)}, u32[]{:S(2)}) collective-permute-start(bf16[128,512]{1,0:T(8,128)(2,1)} %get-tuple-element.93), channel_id=1, source_target_pairs={{0,9},{1,8},{2,11},{3,10},{4,13},{5,12},{6,15},{7,14},{8,1},{9,0},... | collective-permute-start | bytes 393224 | tf_op jit(solution)/shard_map/ppermute | solution.py:396
  208.3 4.2 %collective-permute-start.28 = (bf16[128,256]{1,0:T(8,128)(2,1)S(1)}, bf16[128,256]{1,0:T(8,128)(2,1)S(1)}, u32[]{:S(2)}, u32[]{:S(2)}) collective-permute-start(bf16[128,256]{1,0:T(8,128)(2,1)S(1)} %get-tuple-element.105), channel_id=1, source_target_pairs={{0,1},{1,0},{2,3},{3,2},{4,5},{5,4},{6,7},{7,6},{8,9},{9,8},{10,11... | collective-permute-start | bytes 196616 | tf_op jit(solution)/shard_map/ppermute | solution.py:396
  209.0 4.3 %collective-permute-start.29 = (bf16[128,256]{1,0:T(8,128)(2,1)S(1)}, bf16[128,256]{1,0:T(8,128)(2,1)S(1)}, u32[]{:S(2)}, u32[]{:S(2)}) collective-permute-start(bf16[128,256]{1,0:T(8,128)(2,1)S(1)} %get-tuple-element.106), channel_id=1, source_target_pairs={{0,8},{1,9},{2,10},{3,11},{4,12},{5,13},{6,14},{7,15},{8,0},{9,1},... | collective-permute-start | bytes 196616 | tf_op jit(solution)/shard_map/ppermute | solution.py:396
  210.4 4.1 %collective-permute-start.30 = (bf16[128,256]{1,0:T(8,128)(2,1)S(1)}, bf16[128,256]{1,0:T(8,128)(2,1)S(1)}, u32[]{:S(2)}, u32[]{:S(2)}) collective-permute-start(bf16[128,256]{1,0:T(8,128)(2,1)S(1)} %get-tuple-element.107), channel_id=1, source_target_pairs={{0,9},{1,8},{2,11},{3,10},{4,13},{5,12},{6,15},{7,14},{8,1},{9,0},... | collective-permute-start | bytes 196616 | tf_op jit(solution)/shard_map/ppermute | solution.py:396
  210.7 3.8 %collective-permute-start.34 = (bf16[128,256]{1,0:T(8,128)(2,1)S(1)}, bf16[128,256]{1,0:T(8,128)(2,1)S(1)}, u32[]{:S(2)}, u32[]{:S(2)}) collective-permute-start(bf16[128,256]{1,0:T(8,128)(2,1)S(1)} %get-tuple-element.112), channel_id=1, source_target_pairs={{0,1},{1,0},{2,3},{3,2},{4,5},{5,4},{6,7},{7,6},{8,9},{9,8},{10,11... | collective-permute-start | bytes 196616 | tf_op jit(solution)/shard_map/ppermute | solution.py:396
  211.4 5.2 %collective-permute-start.35 = (bf16[128,256]{1,0:T(8,128)(2,1)S(1)}, bf16[128,256]{1,0:T(8,128)(2,1)S(1)}, u32[]{:S(2)}, u32[]{:S(2)}) collective-permute-start(bf16[128,256]{1,0:T(8,128)(2,1)S(1)} %get-tuple-element.113), channel_id=1, source_target_pairs={{0,8},{1,9},{2,10},{3,11},{4,12},{5,13},{6,14},{7,15},{8,0},{9,1},... | collective-permute-start | bytes 196616 | tf_op jit(solution)/shard_map/ppermute | solution.py:396
  212.6 4.7 %collective-permute-start.36 = (bf16[128,256]{1,0:T(8,128)(2,1)S(1)}, bf16[128,256]{1,0:T(8,128)(2,1)S(1)}, u32[]{:S(2)}, u32[]{:S(2)}) collective-permute-start(bf16[128,256]{1,0:T(8,128)(2,1)S(1)} %get-tuple-element.114), channel_id=1, source_target_pairs={{0,9},{1,8},{2,11},{3,10},{4,13},{5,12},{6,15},{7,14},{8,1},{9,0},... | collective-permute-start | bytes 196616 | tf_op jit(solution)/shard_map/ppermute | solution.py:396
  (3 other events, 3.6 us)

commit v9 on v8

--- a/solution.py
+++ b/solution.py
@@ -139,13 +139,13 @@
         copy.wait()
 
 
-def reorder(order, packed, w_12, after):
+def reorder(order, packed, w_12):
     shape, count = packed.shape[1:], order.shape[0]
     return pl.pallas_call(
         functools.partial(reorder_kernel, count),
         out_shape=[pltpu.HBM(shape, packed.dtype)] * count,
         in_specs=[pl.BlockSpec(memory_space=pltpu.SMEM)]
-        + [pl.BlockSpec(memory_space=pl.ANY)] * (2 + len(after)),
+        + [pl.BlockSpec(memory_space=pl.ANY)] * 2,
         out_specs=[pl.BlockSpec(memory_space=pl.ANY)] * count,
         scratch_shapes=[
             pltpu.VMEM((4,) + shape, packed.dtype),
@@ -155,7 +155,7 @@
         compiler_params=pltpu.CompilerParams(vmem_limit_bytes=LIMIT),
         cost_estimate=pl.CostEstimate(flops=0, bytes_accessed=8 * packed.size, transcendentals=0),
         name="reorder",
-    )(order, packed, w_12, *after)
+    )(order, packed, *far([w_12]))
 
 
 def far(arrays):
@@ -420,20 +420,22 @@
     core_0, core_pair_0 = to_core(a_0), to_core(pair_0)
 
     order = jnp.array([[1, 2, 3], [1, 3, 2], [2, 3, 1], [3, 2, 1]], jnp.int32)[plane]
-    a_12, got_3 = lax.optimization_barrier((a_12, got_3))
+    got_3, core_0, core_pair_0 = lax.optimization_barrier((got_3, core_0, core_pair_0))
     known = jnp.array([0, 3], jnp.int32)
-    a_3, w_3, ordered_1 = reorder(
-        jnp.concatenate([known, order[:1]]), got_3, w_12, after=(core_0, core_pair_0, mid_12)
+    a_3, w_3, ordered_1 = reorder(jnp.concatenate([known, order[:1]]), got_3, w_12)
+    w_3, mid_12 = lax.optimization_barrier((w_3, mid_12))
+    pair_3, mid_3 = to_pair(a_3), to_mid(w_3)
+    a_12, pair_12, a_3 = lax.optimization_barrier((a_12, pair_12, a_3))
+    core_12, core_pair_12 = to_core(a_12), to_core(pair_12)
+    got_3, pair_3, mid_3, core_12, core_pair_12 = lax.optimization_barrier(
+        (got_3, pair_3, mid_3, core_12, core_pair_12)
     )
-    pair_3, mid_3 = to_pair(a_3), to_mid(w_3)
-    core_12, core_pair_12 = to_core(a_12), to_core(pair_12)
-    ordered_2, ordered_3 = reorder(
-        order[1:], got_3, w_12, after=(pair_3, mid_3, core_12, core_pair_12)
-    )
+    ordered_2, ordered_3 = reorder(order[1:], got_3, w_12)
     next_1, next_2, next_3 = to_next(ordered_1), to_next(ordered_2), to_next(ordered_3)
     core_3, core_pair_3 = to_core(a_3), to_core(pair_3)
 
     a_0, w_0, a_12, w_12, a_3, w_3 = far([a_0, w_0, a_12, w_12, a_3, w_3])
+    mid_0, mid_12, mid_3, core_12, core_pair_12 = far([mid_0, mid_12, mid_3, core_12, core_pair_12])
     a_blocks = [(block, None) for block in (a_0, pair_0, core_0, core_pair_0)]
     for block in (a_12, pair_12, core_12, core_pair_12):
         a_blocks += [(block, 0), (block, 1)]

time: 220 us -> 218 us (level)
  local copies, waits for them, and re-layouts: 11.9 us -> 3.74 us
  starting transfers between devices: 45.3 us -> 52.1 us
  Pallas kernels: 47.7 us -> 50.2 us
    unnamed x28 -> x14, local copies, waits for them, and re-layouts: 11.1 us -> 2.99 us
    ppermute x37, starting transfers between devices: 45.3 us -> 52.1 us  [send(): return lax.ppermute(array, 'fsdp', perm=perm)]
    ppermute x37, waiting for transfers between devices: 114 us -> 112 us  [send(): return lax.ppermute(array, 'fsdp', perm=perm)]
  transfers between devices with their start and end apart: 37 -> 37, of which waited for: 14 -> 16; matrix products, arithmetic and copies ran while one was open for 0% -> 0% of each run, Pallas kernels for 18% -> 19%
where the time goes in v9:
time: 218 us
  waiting for transfers between devices  112 us (51%)
  starting transfers between devices  52.1 us (24%)
  Pallas kernels  50.2 us (23%)
  local copies, waits for them, and re-layouts  3.74 us (2%)
    ppermute x37, waiting for transfers between devices, send(): return lax.ppermute(array, 'fsdp', perm=perm)  112 us
    ppermute x37, starting transfers between devices, send(): return lax.ppermute(array, 'fsdp', perm=perm)  52.1 us
    pallas_call x4, Pallas kernels, product(): pl.pallas_call(functools.partial(product_kernel, [places[group] for group...  14.5 us
    pallas_call x1, Pallas kernels, stack_product(): pl.pallas_call(functools.partial(stack_product_kernel, places, a_at, w_at...  11.1 us
    pallas_call x2, Pallas kernels, pack(): pl.pallas_call(functools.partial(pack_kernel, apart, len(steps)), out_sha...  10.4 us
    pallas_call x2, Pallas kernels, reorder(): pl.pallas_call(functools.partial(reorder_kernel, count), out_shape=[pltpu...  8.02 us
  transfers between devices with their start and end apart: 37, of which 16 were waited for; matrix products, arithmetic and copies ran while one was open for 0% of the time, Pallas kernels for 19%

profile of v9, /device:TPU:0, one launch (start us, length us, event | category | flops | bytes accessed | tf_op | source)
XLA Modules:
  0.0 218.0 jit_solution(8891326582541110117)
XLA Ops:
  0.0 6.3 %pack.2 = (bf16[28,128,128]{2,1,0:T(8,128)(2,1)}, bf16[28,128,128]{2,1,0:T(8,128)(2,1)}, bf16[2,28,128,128]{3,2,1,0:T(8,128)(2,1)}, bf16[2,28,128,128]{3,2,1,0:T(8,128)(2,1)}) custom-call(s32[1]{0:T(128)} %bitcast.3.plane_ref.choice_ref, bf16[128,14336]{1,0:T(8,128)(2,1)} %refs_0_.3, bf16[128,14336]{1,0:T(8,128)(2,1)} %refs_1_.3, ...), custom_call_target="tpu_custom_call" | custom-call | bytes 13762560 | tf_op jit(solution)/shard_map/pack/pallas_call | solution.py:63
  6.3 3.0 %collective-permute-start.1 = (bf16[2,28,128,128]{3,2,1,0:T(8,128)(2,1)}, bf16[2,28,128,128]{3,2,1,0:T(8,128)(2,1)S(1)}, u32[]{:S(2)}, u32[]{:S(2)}) collective-permute-start(bf16[2,28,128,128]{3,2,1,0:T(8,128)(2,1)} %get-tuple-element.72), channel_id=1, source_target_pairs={{0,2},{1,3},{2,0},{3,1},{4,6},{5,7},{6,4},{7,5},{8,10},{9,11},{10,... | collective-permute-start | bytes 5505032 | tf_op jit(solution)/shard_map/ppermute | solution.py:396
  9.3 1.5 collective-permute-start.2
  10.8 1.6 collective-permute-start
  12.4 2.6 %collective-permute-start.7 = (bf16[28,128,128]{2,1,0:T(8,128)(2,1)}, bf16[28,128,128]{2,1,0:T(8,128)(2,1)S(1)}, u32[]{:S(2)}, u32[]{:S(2)}) collective-permute-start(bf16[28,128,128]{2,1,0:T(8,128)(2,1)} %get-tuple-element.79.refs_12_.refs_0_), channel_id=1, source_target_pairs={{8,0},{9,1},{10,2},{11,3},{12,4},{13,5},{14,6},{15,7},{24,8},{25,9... | collective-permute-start | bytes 2752520 | tf_op jit(solution)/shard_map/ppermute | solution.py:396
  15.0 0.7 collective-permute-start.6
  15.7 18.6 %collective-permute-done.refs_3_.refs_0_.refs_1_ = bf16[28,128,128]{2,1,0:T(8,128)(2,1)S(1)} collective-permute-done((bf16[28,128,128]{2,1,0:T(8,128)(2,1)}, bf16[28,128,128]{2,1,0:T(8,128)(2,1)S(1)}, u32[]{:S(2)}, u32[]{:S(2)}) %collective-permute-start) | collective-permute-done | bytes 917536 | tf_op jit(solution)/shard_map/ppermute | solution.py:396
  34.3 4.1 %pack.3 = bf16[2,28,128,128]{3,2,1,0:T(8,128)(2,1)} custom-call(s32[1]{0:T(128)} %bitcast.3.plane_ref.choice_ref, bf16[128,14336]{1,0:T(8,128)(2,1)} %refs_0_.3, bf16[128,14336]{1,0:T(8,128)(2,1)} %refs_1_.3, bf16[14336,128]{1,0:T(8,128)(2,1)} %refs_2_.3, bf16[28,128,128]{2,1,0:T(8,128)(2,1)S(1)} %collective-permute-done.refs_3_.refs_0_.refs_1_), custom_call_target="tpu_custom_call" | custom-call | bytes 4587520 | tf_op jit(solution)/shard_map/pack/pallas_call | solution.py:63
  38.4 11.1 %collective-permute-done.1.one = bf16[2,28,128,128]{3,2,1,0:T(8,128)(2,1)S(1)} collective-permute-done((bf16[2,28,128,128]{3,2,1,0:T(8,128)(2,1)}, bf16[2,28,128,128]{3,2,1,0:T(8,128)(2,1)S(1)}, u32[]{:S(2)}, u32[]{:S(2)}) %collective-permute-start.1) | collective-permute-done | bytes 1835040 | tf_op jit(solution)/shard_map/ppermute | solution.py:396
  49.5 1.5 collective-permute-done.2.two
  51.0 1.5 collective-permute-start.3
  52.5 2.7 %unpack_pair.1 = (bf16[2,28,128,128]{3,2,1,0:T(8,128)(2,1)}, bf16[2,28,128,128]{3,2,1,0:T(8,128)(2,1)}) custom-call(bf16[2,28,128,128]{3,2,1,0:T(8,128)(2,1)S(1)} %collective-permute-done.1.one, bf16[2,28,128,128]{3,2,1,0:T(8,128)(2,1)S(1)} %collective-permute-done.2.two, bf16[28,128,128]{2,1,0:T(8,128)(2,1)S(1)} %collective-permute-done.refs_3_.refs_0_.refs_1_, ...), custom_call_target="tpu_custom_call" | custom-call | bytes 7340032 | tf_op jit(solution)/shard_map/unpack_pair/pallas_call | solution.py:106
  55.3 4.7 %collective-permute-start.8 = (bf16[2,28,128,128]{3,2,1,0:T(8,128)(2,1)}, bf16[2,28,128,128]{3,2,1,0:T(8,128)(2,1)}, u32[]{:S(2)}, u32[]{:S(2)}) collective-permute-start(bf16[2,28,128,128]{3,2,1,0:T(8,128)(2,1)} %get-tuple-element.84.refs_4_), channel_id=1, source_target_pairs={{0,8},{1,9},{2,10},{3,11},{4,12},{5,13},{6,14},{7,15},{8,0},{9,1},... | collective-permute-start | bytes 5505032 | tf_op jit(solution)/shard_map/ppermute | solution.py:396
  60.5 1.9 collective-permute-start.10
  62.4 0.7 constant_dynamic-slice_fusion
  63.2 0.8 collective-permute-done.4.refs_2_
  63.9 28.8 %collective-permute-done.3.packed = bf16[2,28,128,128]{3,2,1,0:T(8,128)(2,1)} collective-permute-done((bf16[2,28,128,128]{3,2,1,0:T(8,128)(2,1)}, bf16[2,28,128,128]{3,2,1,0:T(8,128)(2,1)}, u32[]{:S(2)}, u32[]{:S(2)}) %collective-permute-start.3) | collective-permute-done | bytes 1835040 | tf_op jit(solution)/shard_map/ppermute | solution.py:396
  92.8 4.2 %reorder.2 = (bf16[28,128,128]{2,1,0:T(8,128)(2,1)}, bf16[28,128,128]{2,1,0:T(8,128)(2,1)}, bf16[28,128,128]{2,1,0:T(8,128)(2,1)}) custom-call(s32[3]{0:T(128)S(1)} %pad_add_fusion.1.order_ref, bf16[2,28,128,128]{3,2,1,0:T(8,128)(2,1)} %collective-permute-done.3.packed, bf16[2,28,128,128]{3,2,1,0:T(8,128)(2,1)} %get-tuple-element.82.w_12.refs_13_.refs_1_), custom_call_target="tpu_custom_call" | custom-call | bytes 7340032 | tf_op jit(solution)/shard_map/reorder/pallas_call | solution.py:144
  98.0 0.7 collective-permute-start.11
  98.7 9.6 %collective-permute-start.9 = (bf16[28,128,128]{2,1,0:T(8,128)(2,1)}, bf16[28,128,128]{2,1,0:T(8,128)(2,1)}, u32[]{:S(2)}, u32[]{:S(2)}) collective-permute-start(bf16[28,128,128]{2,1,0:T(8,128)(2,1)} %get-tuple-element.90.refs_8_), channel_id=1, source_target_pairs={{0,8},{1,9},{2,10},{3,11},{4,12},{5,13},{6,14},{7,15},{8,0},{9,1},... | collective-permute-start | bytes 2752520 | tf_op jit(solution)/shard_map/ppermute | solution.py:396
  108.3 19.8 %collective-permute-done.9.refs_9_ = bf16[28,128,128]{2,1,0:T(8,128)(2,1)} collective-permute-done((bf16[28,128,128]{2,1,0:T(8,128)(2,1)}, bf16[28,128,128]{2,1,0:T(8,128)(2,1)}, u32[]{:S(2)}, u32[]{:S(2)}) %collective-permute-start.9) | collective-permute-done | bytes 917536 | tf_op jit(solution)/shard_map/ppermute | solution.py:396
  128.2 1.1 copy-done.5
  130.0 1.6 collective-permute-start.16
  131.7 3.8 %reorder.3 = (bf16[28,128,128]{2,1,0:T(8,128)(2,1)}, bf16[28,128,128]{2,1,0:T(8,128)(2,1)}) custom-call(s32[2]{0:T(128)S(1)} %slice_bitcast_fusion.order_ref, bf16[2,28,128,128]{3,2,1,0:T(8,128)(2,1)} %collective-permute-done.3.packed, bf16[2,28,128,128]{3,2,1,0:T(8,128)(2,1)} %get-tuple-element.82.w_12.refs_13_.refs_1_), custom_call_target="tpu_custom_call" | custom-call | bytes 7340032 | tf_op jit(solution)/shard_map/reorder/pallas_call | solution.py:144
  135.9 2.8 %collective-permute-start.24 = (bf16[28,128,128]{2,1,0:T(8,128)(2,1)}, bf16[28,128,128]{2,1,0:T(8,128)(2,1)S(1)}, u32[]{:S(2)}, u32[]{:S(2)}) collective-permute-start(bf16[28,128,128]{2,1,0:T(8,128)(2,1)} %get-tuple-element.116), channel_id=1, source_target_pairs={{8,0},{9,1},{10,2},{11,3},{12,4},{13,5},{14,6},{15,7},{24,8},{25,9... | collective-permute-start | bytes 2752520 | tf_op jit(solution)/shard_map/ppermute | solution.py:396
  138.7 1.2 copy-done.2
  139.8 11.1 %stack_product.1 = (bf16[28,2048,128]{2,1,0:T(8,128)(2,1)S(1)}, bf16[4,128,512]{2,1,0:T(8,128)(2,1)S(1)}, bf16[4,128,512]{2,1,0:T(8,128)(2,1)S(1)}, bf16[4,128,512]{2,1,0:T(8,128)(2,1)S(1)}) custom-call(s32[1]{0:T(128)} %bitcast.2.choice_ref, bf16[28,128,128]{2,1,0:T(8,128)(2,1)} %get-tuple-element.71.refs_0_, ...), custom_call_target="tpu_custom_call" | custom-call | flops 5637144576 | bytes 18350080 | tf_op jit(solution)/shard_map/stack_product/pallas_call | solution.py:236
  150.9 2.7 %collective-permute-done.16.refs_1_ = bf16[28,128,128]{2,1,0:T(8,128)(2,1)} collective-permute-done((bf16[28,128,128]{2,1,0:T(8,128)(2,1)}, bf16[28,128,128]{2,1,0:T(8,128)(2,1)}, u32[]{:S(2)}, u32[]{:S(2)}) %collective-permute-start.16) | collective-permute-done | bytes 917536 | tf_op jit(solution)/shard_map/ppermute | solution.py:396
  154.6 2.4 %collective-permute-start.20 = (bf16[4,128,512]{2,1,0:T(8,128)(2,1)S(1)}, bf16[4,128,512]{2,1,0:T(8,128)(2,1)S(1)}, u32[]{:S(2)}, u32[]{:S(2)}) collective-permute-start(bf16[4,128,512]{2,1,0:T(8,128)(2,1)S(1)} %get-tuple-element.107), channel_id=1, source_target_pairs={{0,6},{1,7},{2,4},{3,5},{4,2},{5,3},{6,0},{7,1},{8,14},{9,15},{10,... | collective-permute-start | bytes 1572872 | tf_op jit(solution)/shard_map/ppermute | solution.py:396
  157.1 4.1 %product.4.refs_3_.own = f32[4,128,512]{2,1,0:T(8,128)S(1)} custom-call(s32[1]{0:T(128)} %bitcast.2.choice_ref, bf16[28,2048,128]{2,1,0:T(8,128)(2,1)S(1)} %get-tuple-element.94.a, bf16[28,128,128]{2,1,0:T(8,128)(2,1)} %get-tuple-element.79.refs_12_.refs_0_, bf16[2,28,128,128]{3,2,1,0:T(8,128)(2,1)} %get-tuple-element.82.w_12.refs_13_.refs_1_, ...), custom_call_target="tpu_custom_call" | custom-call | flops 1879048192 | bytes 7340032 | tf_op jit(solution)/shard_map/product/pallas_call | solution.py:305
  161.2 11.9 %collective-permute-done.17.refs_2_.refs_0_ = bf16[28,128,128]{2,1,0:T(8,128)(2,1)S(1)} collective-permute-done((bf16[28,128,128]{2,1,0:T(8,128)(2,1)}, bf16[28,128,128]{2,1,0:T(8,128)(2,1)S(1)}, u32[]{:S(2)}, u32[]{:S(2)}) %collective-permute-start.17) | collective-permute-done | bytes 917536 | tf_op jit(solution)/shard_map/ppermute | solution.py:396
  173.2 5.3 %product.5 = (bf16[4,128,256]{2,1,0:T(8,128)(2,1)S(1)}, bf16[4,128,256]{2,1,0:T(8,128)(2,1)S(1)}, bf16[4,128,256]{2,1,0:T(8,128)(2,1)S(1)}, f32[4,128,256]{2,1,0:T(8,128)S(1)}) custom-call(s32[1]{0:T(128)} %bitcast.3.plane_ref.choice_ref, bf16[28,2048,128]{2,1,0:T(8,128)(2,1)S(1)} %get-tuple-element.94.a, ...), custom_call_target="tpu_custom_call" | custom-call | flops 3758096384 | bytes 16515072 | tf_op jit(solution)/shard_map/product/pallas_call | solution.py:305
  179.5 2.6 %collective-permute-start.27 = (bf16[4,128,256]{2,1,0:T(8,128)(2,1)S(1)}, bf16[4,128,256]{2,1,0:T(8,128)(2,1)S(1)}, u32[]{:S(2)}, u32[]{:S(2)}) collective-permute-start(bf16[4,128,256]{2,1,0:T(8,128)(2,1)S(1)} %get-tuple-element.122), channel_id=1, source_target_pairs={{0,6},{1,7},{2,4},{3,5},{4,2},{5,3},{6,0},{7,1},{8,14},{9,15},{10,... | collective-permute-start | bytes 786440 | tf_op jit(solution)/shard_map/ppermute | solution.py:396
  182.1 0.9 add.39
  182.9 7.6 %collective-permute-done.24.refs_1_ = bf16[28,128,128]{2,1,0:T(8,128)(2,1)S(1)} collective-permute-done((bf16[28,128,128]{2,1,0:T(8,128)(2,1)}, bf16[28,128,128]{2,1,0:T(8,128)(2,1)S(1)}, u32[]{:S(2)}, u32[]{:S(2)}) %collective-permute-start.24) | collective-permute-done | bytes 917536 | tf_op jit(solution)/shard_map/ppermute | solution.py:396
  190.5 3.6 %product.6 = (bf16[4,128,256]{2,1,0:T(8,128)(2,1)S(1)}, bf16[4,128,256]{2,1,0:T(8,128)(2,1)S(1)}, bf16[4,128,256]{2,1,0:T(8,128)(2,1)S(1)}) custom-call(s32[1]{0:T(128)} %bitcast.3.plane_ref.choice_ref, bf16[28,2048,128]{2,1,0:T(8,128)(2,1)S(1)} %get-tuple-element.94.a, bf16[28,128,128]{2,1,0:T(8,128)(2,1)S(1)} %collective-permute-done.17.refs_2_.refs_0_, ...), custom_call_target="tpu_custom_call" | custom-call | flops 2818572288 | bytes 12845056 | tf_op jit(solution)/shard_map/product/pallas_call | solution.py:305
  195.1 2.7 %collective-permute-start.33 = (bf16[4,128,256]{2,1,0:T(8,128)(2,1)S(1)}, bf16[4,128,256]{2,1,0:T(8,128)(2,1)S(1)}, u32[]{:S(2)}, u32[]{:S(2)}) collective-permute-start(bf16[4,128,256]{2,1,0:T(8,128)(2,1)S(1)} %get-tuple-element.132.refs_3_), channel_id=1, source_target_pairs={{0,6},{1,7},{2,4},{3,5},{4,2},{5,3},{6,0},{7,1},{8,14},{9,15},{10,... | collective-permute-start | bytes 786440 | tf_op jit(solution)/shard_map/ppermute | solution.py:396
  197.7 2.6 %collective-permute-start.22 = (bf16[128,512]{1,0:T(8,128)(2,1)}, bf16[128,512]{1,0:T(8,128)(2,1)}, u32[]{:S(2)}, u32[]{:S(2)}) collective-permute-start(bf16[128,512]{1,0:T(8,128)(2,1)} %get-tuple-element.114), channel_id=1, source_target_pairs={{0,8},{1,9},{2,10},{3,11},{4,12},{5,13},{6,14},{7,15},{8,0},{9,1},... | collective-permute-start | bytes 393224 | tf_op jit(solution)/shard_map/ppermute | solution.py:396
  200.4 2.7 %collective-permute-done.31.one = bf16[4,128,256]{2,1,0:T(8,128)(2,1)S(1)} collective-permute-done((bf16[4,128,256]{2,1,0:T(8,128)(2,1)S(1)}, bf16[4,128,256]{2,1,0:T(8,128)(2,1)S(1)}, u32[]{:S(2)}, u32[]{:S(2)}) %collective-permute-start.31) | collective-permute-done | bytes 262176 | tf_op jit(solution)/shard_map/ppermute | solution.py:396
  203.1 1.5 product.7.refs_0_.own
  204.7 1.2 collective-permute-done.32.two
  206.0 1.6 collective-permute-start.28
  207.5 1.1 collective-permute-start.29
  209.9 1.1 collective-permute-start.35
  211.9 1.0 collective-permute-done.30.refs_7_
  212.9 2.0 collective-permute-done.35.refs_10_
  214.9 0.8 collective-permute-done.36.refs_11_
  215.7 2.3 %assemble.1 = bf16[128,4096]{1,0:T(8,128)(2,1)} custom-call(s32[2]{0:T(128)S(1)} %pad_add_fusion.place_ref, bf16[128,512]{1,0:T(8,128)(2,1)S(1)} %get-tuple-element.112.refs_4_.refs_0_, bf16[128,512]{1,0:T(8,128)(2,1)} %collective-permute-done.21.refs_1_, bf16[128,512]{1,0:T(8,128)(2,1)} %collective-permute-done.22.refs_2_, ...), custom_call_target="tpu_custom_call" | custom-call | tf_op jit(solution)/shard_map/assemble/pallas_call | solution.py:373
  (59 shorter events, 8.0 us)
Async XLA Ops:
  6.3 43.2 %collective-permute-start.1 = (bf16[2,28,128,128]{3,2,1,0:T(8,128)(2,1)}, bf16[2,28,128,128]{3,2,1,0:T(8,128)(2,1)S(1)}, u32[]{:S(2)}, u32[]{:S(2)}) collective-permute-start(bf16[2,28,128,128]{3,2,1,0:T(8,128)(2,1)} %get-tuple-element.72), channel_id=1, source_target_pairs={{0,2},{1,3},{2,0},{3,1},{4,6},{5,7},{6,4},{7,5},{8,10},{9,11},{10,... | collective-permute-start | bytes 5505032 | tf_op jit(solution)/shard_map/ppermute | solution.py:396
  9.3 41.7 %collective-permute-start.2 = (bf16[2,28,128,128]{3,2,1,0:T(8,128)(2,1)}, bf16[2,28,128,128]{3,2,1,0:T(8,128)(2,1)S(1)}, u32[]{:S(2)}, u32[]{:S(2)}) collective-permute-start(bf16[2,28,128,128]{3,2,1,0:T(8,128)(2,1)} %get-tuple-element.73), channel_id=1, source_target_pairs={{0,4},{1,5},{2,6},{3,7},{4,0},{5,1},{6,2},{7,3},{8,12},{9,13},{10,... | collective-permute-start | bytes 5505032 | tf_op jit(solution)/shard_map/ppermute | solution.py:396
  10.8 23.5 %collective-permute-start = (bf16[28,128,128]{2,1,0:T(8,128)(2,1)}, bf16[28,128,128]{2,1,0:T(8,128)(2,1)S(1)}, u32[]{:S(2)}, u32[]{:S(2)}) collective-permute-start(bf16[28,128,128]{2,1,0:T(8,128)(2,1)} %get-tuple-element.71.refs_0_), channel_id=1, source_target_pairs={{0,8},{1,9},{2,10},{3,11},{4,12},{5,13},{6,14},{7,15},{8,0},{9,1},... | collective-permute-start | bytes 2752520 | tf_op jit(solution)/shard_map/ppermute | solution.py:396
  12.4 40.1 %collective-permute-start.7 = (bf16[28,128,128]{2,1,0:T(8,128)(2,1)}, bf16[28,128,128]{2,1,0:T(8,128)(2,1)S(1)}, u32[]{:S(2)}, u32[]{:S(2)}) collective-permute-start(bf16[28,128,128]{2,1,0:T(8,128)(2,1)} %get-tuple-element.79.refs_12_.refs_0_), channel_id=1, source_target_pairs={{8,0},{9,1},{10,2},{11,3},{12,4},{13,5},{14,6},{15,7},{24,8},{25,9... | collective-permute-start | bytes 2752520 | tf_op jit(solution)/shard_map/ppermute | solution.py:396
  15.0 37.5 %collective-permute-start.6 = (bf16[28,128,128]{2,1,0:T(8,128)(2,1)}, bf16[28,128,128]{2,1,0:T(8,128)(2,1)S(1)}, u32[]{:S(2)}, u32[]{:S(2)}) collective-permute-start(bf16[28,128,128]{2,1,0:T(8,128)(2,1)} %get-tuple-element.79.refs_12_.refs_0_), channel_id=1, source_target_pairs={{8,16},{9,17},{10,18},{11,19},{12,20},{13,21},{14,22},{15,23},{16,... | collective-permute-start | bytes 2752520 | tf_op jit(solution)/shard_map/ppermute | solution.py:396
  51.0 41.8 %collective-permute-start.3 = (bf16[2,28,128,128]{3,2,1,0:T(8,128)(2,1)}, bf16[2,28,128,128]{3,2,1,0:T(8,128)(2,1)}, u32[]{:S(2)}, u32[]{:S(2)}) collective-permute-start(bf16[2,28,128,128]{3,2,1,0:T(8,128)(2,1)} %pack.3), channel_id=1, source_target_pairs={{0,6},{1,7},{2,4},{3,5},{4,2},{5,3},{6,0},{7,1},{8,14},{9,15},{10,... | collective-permute-start | bytes 5505032 | tf_op jit(solution)/shard_map/ppermute | solution.py:396
  52.5 2.7 %copy-start = (bf16[28,128,128]{2,1,0:T(8,128)(2,1)}, bf16[28,128,128]{2,1,0:T(8,128)(2,1)S(1)}, u32[]{:S(2)}) copy-start(bf16[28,128,128]{2,1,0:T(8,128)(2,1)S(1)} %collective-permute-done.6.refs_1_.refs_15_.refs_3_) | copy-start | bytes 2752516
  55.3 42.2 %collective-permute-start.8 = (bf16[2,28,128,128]{3,2,1,0:T(8,128)(2,1)}, bf16[2,28,128,128]{3,2,1,0:T(8,128)(2,1)}, u32[]{:S(2)}, u32[]{:S(2)}) collective-permute-start(bf16[2,28,128,128]{3,2,1,0:T(8,128)(2,1)} %get-tuple-element.84.refs_4_), channel_id=1, source_target_pairs={{0,8},{1,9},{2,10},{3,11},{4,12},{5,13},{6,14},{7,15},{8,0},{9,1},... | collective-permute-start | bytes 5505032 | tf_op jit(solution)/shard_map/ppermute | solution.py:396
  60.0 4.0 %collective-permute-start.4 = (bf16[28,128,128]{2,1,0:T(8,128)(2,1)}, bf16[28,128,128]{2,1,0:T(8,128)(2,1)S(1)}, u32[]{:S(2)}, u32[]{:S(2)}) collective-permute-start(bf16[28,128,128]{2,1,0:T(8,128)(2,1)} %get-tuple-element.71.refs_0_), channel_id=1, source_target_pairs={{0,1},{1,0},{2,3},{3,2},{4,5},{5,4},{6,7},{7,6},{8,9},{9,8},{10,11... | collective-permute-start | bytes 2752520 | tf_op jit(solution)/shard_map/ppermute | solution.py:396
  60.0 4.0 %collective-permute-start.5 = (bf16[28,128,128]{2,1,0:T(8,128)(2,1)S(1)}, bf16[28,128,128]{2,1,0:T(8,128)(2,1)}, u32[]{:S(2)}, u32[]{:S(2)}) collective-permute-start(bf16[28,128,128]{2,1,0:T(8,128)(2,1)S(1)} %collective-permute-done.refs_3_.refs_0_.refs_1_), channel_id=1, source_target_pairs={{0,1},{1,0},{2,3},{3,2},{4,5},{5,4},{6,7},{7,6},{8,9},{9,8},{10,11... | collective-permute-start | bytes 2752520 | tf_op jit(solution)/shard_map/ppermute | solution.py:396
  60.5 37.5 %collective-permute-start.10 = (bf16[2,28,128,128]{3,2,1,0:T(8,128)(2,1)}, bf16[2,28,128,128]{3,2,1,0:T(8,128)(2,1)}, u32[]{:S(2)}, u32[]{:S(2)}) collective-permute-start(bf16[2,28,128,128]{3,2,1,0:T(8,128)(2,1)} %get-tuple-element.82.w_12.refs_13_.refs_1_), channel_id=1, source_target_pairs={{8,16},{9,17},{10,18},{11,19},{12,20},{13,21},{14,22},{15,23},{16,... | collective-permute-start | bytes 5505032 | tf_op jit(solution)/shard_map/ppermute | solution.py:396
  63.2 34.3 %copy-start.4 = (bf16[2,28,128,128]{3,2,1,0:T(8,128)(2,1)S(1)}, bf16[2,28,128,128]{3,2,1,0:T(8,128)(2,1)}, u32[]{:S(2)}) copy-start(bf16[2,28,128,128]{3,2,1,0:T(8,128)(2,1)} %get-tuple-element.84.refs_4_) | copy-start | bytes 5505028
  63.9 33.0 %copy-start.1 = (bf16[28,128,128]{2,1,0:T(8,128)(2,1)}, bf16[28,128,128]{2,1,0:T(8,128)(2,1)S(1)}, u32[]{:S(2)}) copy-start(bf16[28,128,128]{2,1,0:T(8,128)(2,1)S(1)} %collective-permute-done.4.refs_2_) | copy-start | bytes 2752516
  97.5 30.6 %collective-permute-start.12 = (bf16[2,28,128,128]{3,2,1,0:T(8,128)(2,1)S(1)}, bf16[2,28,128,128]{3,2,1,0:T(8,128)(2,1)S(1)}, u32[]{:S(2)}, u32[]{:S(2)}) collective-permute-start(bf16[2,28,128,128]{3,2,1,0:T(8,128)(2,1)S(1)} %copy-done.4), channel_id=1, source_target_pairs={{0,1},{1,0},{2,3},{3,2},{4,5},{5,4},{6,7},{7,6},{8,9},{9,8},{10,11... | collective-permute-start | bytes 5505032 | tf_op jit(solution)/shard_map/ppermute | solution.py:396
  97.5 30.6 %collective-permute-start.13 = (bf16[2,28,128,128]{3,2,1,0:T(8,128)(2,1)}, bf16[2,28,128,128]{3,2,1,0:T(8,128)(2,1)S(1)}, u32[]{:S(2)}, u32[]{:S(2)}) collective-permute-start(bf16[2,28,128,128]{3,2,1,0:T(8,128)(2,1)} %collective-permute-done.8.refs_5_), channel_id=1, source_target_pairs={{0,1},{1,0},{2,3},{3,2},{4,5},{5,4},{6,7},{7,6},{8,9},{9,8},{10,11... | collective-permute-start | bytes 5505032 | tf_op jit(solution)/shard_map/ppermute | solution.py:396
  98.0 10.3 %collective-permute-start.11 = (bf16[28,128,128]{2,1,0:T(8,128)(2,1)}, bf16[28,128,128]{2,1,0:T(8,128)(2,1)S(1)}, u32[]{:S(2)}, u32[]{:S(2)}) collective-permute-start(bf16[28,128,128]{2,1,0:T(8,128)(2,1)} %get-tuple-element.87.refs_14_.refs_2_), channel_id=1, source_target_pairs={{8,16},{9,17},{10,18},{11,19},{12,20},{13,21},{14,22},{15,23},{16,... | collective-permute-start | bytes 2752520 | tf_op jit(solution)/shard_map/ppermute | solution.py:396
  98.7 29.4 %collective-permute-start.9 = (bf16[28,128,128]{2,1,0:T(8,128)(2,1)}, bf16[28,128,128]{2,1,0:T(8,128)(2,1)}, u32[]{:S(2)}, u32[]{:S(2)}) collective-permute-start(bf16[28,128,128]{2,1,0:T(8,128)(2,1)} %get-tuple-element.90.refs_8_), channel_id=1, source_target_pairs={{0,8},{1,9},{2,10},{3,11},{4,12},{5,13},{6,14},{7,15},{8,0},{9,1},... | collective-permute-start | bytes 2752520 | tf_op jit(solution)/shard_map/ppermute | solution.py:396
  108.3 30.3 %collective-permute-start.14 = (bf16[28,128,128]{2,1,0:T(8,128)(2,1)}, bf16[28,128,128]{2,1,0:T(8,128)(2,1)}, u32[]{:S(2)}, u32[]{:S(2)}) collective-permute-start(bf16[28,128,128]{2,1,0:T(8,128)(2,1)} %get-tuple-element.90.refs_8_), channel_id=1, source_target_pairs={{0,1},{1,0},{2,3},{3,2},{4,5},{5,4},{6,7},{7,6},{8,9},{9,8},{10,11... | collective-permute-start | bytes 2752520 | tf_op jit(solution)/shard_map/ppermute | solution.py:396
  108.3 19.9 %copy-start.3 = (bf16[28,128,128]{2,1,0:T(8,128)(2,1)}, bf16[28,128,128]{2,1,0:T(8,128)(2,1)S(1)}, u32[]{:S(2)}) copy-start(bf16[28,128,128]{2,1,0:T(8,128)(2,1)S(1)} %collective-permute-done.11.refs_17_.refs_5_) | copy-start | bytes 2752516
  128.1 1.2 copy-start.5
  128.1 1.9 copy-start.6
  128.1 10.5 %collective-permute-start.15 = (bf16[28,128,128]{2,1,0:T(8,128)(2,1)}, bf16[28,128,128]{2,1,0:T(8,128)(2,1)}, u32[]{:S(2)}, u32[]{:S(2)}) collective-permute-start(bf16[28,128,128]{2,1,0:T(8,128)(2,1)} %collective-permute-done.9.refs_9_), channel_id=1, source_target_pairs={{0,1},{1,0},{2,3},{3,2},{4,5},{5,4},{6,7},{7,6},{8,9},{9,8},{10,11... | collective-permute-start | bytes 2752520 | tf_op jit(solution)/shard_map/ppermute | solution.py:396
  130.0 23.6 %collective-permute-start.16 = (bf16[28,128,128]{2,1,0:T(8,128)(2,1)}, bf16[28,128,128]{2,1,0:T(8,128)(2,1)}, u32[]{:S(2)}, u32[]{:S(2)}) collective-permute-start(bf16[28,128,128]{2,1,0:T(8,128)(2,1)} %get-tuple-element.98), channel_id=1, source_target_pairs={{8,0},{9,1},{10,2},{11,3},{12,4},{13,5},{14,6},{15,7},{24,8},{25,9... | collective-permute-start | bytes 2752520 | tf_op jit(solution)/shard_map/ppermute | solution.py:396
  135.6 37.6 %collective-permute-start.17 = (bf16[28,128,128]{2,1,0:T(8,128)(2,1)}, bf16[28,128,128]{2,1,0:T(8,128)(2,1)S(1)}, u32[]{:S(2)}, u32[]{:S(2)}) collective-permute-start(bf16[28,128,128]{2,1,0:T(8,128)(2,1)} %get-tuple-element.101), channel_id=1, source_target_pairs={{8,0},{9,1},{10,2},{11,3},{12,4},{13,5},{14,6},{15,7},{24,8},{25,9... | collective-permute-start | bytes 2752520 | tf_op jit(solution)/shard_map/ppermute | solution.py:396
  135.9 54.6 %collective-permute-start.24 = (bf16[28,128,128]{2,1,0:T(8,128)(2,1)}, bf16[28,128,128]{2,1,0:T(8,128)(2,1)S(1)}, u32[]{:S(2)}, u32[]{:S(2)}) collective-permute-start(bf16[28,128,128]{2,1,0:T(8,128)(2,1)} %get-tuple-element.116), channel_id=1, source_target_pairs={{8,0},{9,1},{10,2},{11,3},{12,4},{13,5},{14,6},{15,7},{24,8},{25,9... | collective-permute-start | bytes 2752520 | tf_op jit(solution)/shard_map/ppermute | solution.py:396
  138.6 1.2 copy-start.2
  153.6 24.9 %collective-permute-start.18 = (bf16[4,128,512]{2,1,0:T(8,128)(2,1)S(1)}, bf16[4,128,512]{2,1,0:T(8,128)(2,1)S(1)}, u32[]{:S(2)}, u32[]{:S(2)}) collective-permute-start(bf16[4,128,512]{2,1,0:T(8,128)(2,1)S(1)} %get-tuple-element.105.refs_6_), channel_id=1, source_target_pairs={{0,2},{1,3},{2,0},{3,1},{4,6},{5,7},{6,4},{7,5},{8,10},{9,11},{10,... | collective-permute-start | bytes 1572872 | tf_op jit(solution)/shard_map/ppermute | solution.py:396
  154.1 24.4 %collective-permute-start.19 = (bf16[4,128,512]{2,1,0:T(8,128)(2,1)S(1)}, bf16[4,128,512]{2,1,0:T(8,128)(2,1)S(1)}, u32[]{:S(2)}, u32[]{:S(2)}) collective-permute-start(bf16[4,128,512]{2,1,0:T(8,128)(2,1)S(1)} %get-tuple-element.106), channel_id=1, source_target_pairs={{0,4},{1,5},{2,6},{3,7},{4,0},{5,1},{6,2},{7,3},{8,12},{9,13},{10,... | collective-permute-start | bytes 1572872 | tf_op jit(solution)/shard_map/ppermute | solution.py:396
  154.6 23.9 %collective-permute-start.20 = (bf16[4,128,512]{2,1,0:T(8,128)(2,1)S(1)}, bf16[4,128,512]{2,1,0:T(8,128)(2,1)S(1)}, u32[]{:S(2)}, u32[]{:S(2)}) collective-permute-start(bf16[4,128,512]{2,1,0:T(8,128)(2,1)S(1)} %get-tuple-element.107), channel_id=1, source_target_pairs={{0,6},{1,7},{2,4},{3,5},{4,2},{5,3},{6,0},{7,1},{8,14},{9,15},{10,... | collective-permute-start | bytes 1572872 | tf_op jit(solution)/shard_map/ppermute | solution.py:396
  178.5 15.6 %collective-permute-start.25 = (bf16[4,128,256]{2,1,0:T(8,128)(2,1)S(1)}, bf16[4,128,256]{2,1,0:T(8,128)(2,1)S(1)}, u32[]{:S(2)}, u32[]{:S(2)}) collective-permute-start(bf16[4,128,256]{2,1,0:T(8,128)(2,1)S(1)} %get-tuple-element.120), channel_id=1, source_target_pairs={{0,2},{1,3},{2,0},{3,1},{4,6},{5,7},{6,4},{7,5},{8,10},{9,11},{10,... | collective-permute-start | bytes 786440 | tf_op jit(solution)/shard_map/ppermute | solution.py:396
  179.0 15.2 %collective-permute-start.26 = (bf16[4,128,256]{2,1,0:T(8,128)(2,1)S(1)}, bf16[4,128,256]{2,1,0:T(8,128)(2,1)S(1)}, u32[]{:S(2)}, u32[]{:S(2)}) collective-permute-start(bf16[4,128,256]{2,1,0:T(8,128)(2,1)S(1)} %get-tuple-element.121), channel_id=1, source_target_pairs={{0,4},{1,5},{2,6},{3,7},{4,0},{5,1},{6,2},{7,3},{8,12},{9,13},{10,... | collective-permute-start | bytes 786440 | tf_op jit(solution)/shard_map/ppermute | solution.py:396
  179.5 14.7 %collective-permute-start.27 = (bf16[4,128,256]{2,1,0:T(8,128)(2,1)S(1)}, bf16[4,128,256]{2,1,0:T(8,128)(2,1)S(1)}, u32[]{:S(2)}, u32[]{:S(2)}) collective-permute-start(bf16[4,128,256]{2,1,0:T(8,128)(2,1)S(1)} %get-tuple-element.122), channel_id=1, source_target_pairs={{0,6},{1,7},{2,4},{3,5},{4,2},{5,3},{6,0},{7,1},{8,14},{9,15},{10,... | collective-permute-start | bytes 786440 | tf_op jit(solution)/shard_map/ppermute | solution.py:396
  194.2 8.9 %collective-permute-start.31 = (bf16[4,128,256]{2,1,0:T(8,128)(2,1)S(1)}, bf16[4,128,256]{2,1,0:T(8,128)(2,1)S(1)}, u32[]{:S(2)}, u32[]{:S(2)}) collective-permute-start(bf16[4,128,256]{2,1,0:T(8,128)(2,1)S(1)} %get-tuple-element.130), channel_id=1, source_target_pairs={{0,2},{1,3},{2,0},{3,1},{4,6},{5,7},{6,4},{7,5},{8,10},{9,11},{10,... | collective-permute-start | bytes 786440 | tf_op jit(solution)/shard_map/ppermute | solution.py:396
  194.6 11.4 %collective-permute-start.32 = (bf16[4,128,256]{2,1,0:T(8,128)(2,1)S(1)}, bf16[4,128,256]{2,1,0:T(8,128)(2,1)S(1)}, u32[]{:S(2)}, u32[]{:S(2)}) collective-permute-start(bf16[4,128,256]{2,1,0:T(8,128)(2,1)S(1)} %get-tuple-element.131), channel_id=1, source_target_pairs={{0,4},{1,5},{2,6},{3,7},{4,0},{5,1},{6,2},{7,3},{8,12},{9,13},{10,... | collective-permute-start | bytes 786440 | tf_op jit(solution)/shard_map/ppermute | solution.py:396
  195.1 12.5 %collective-permute-start.33 = (bf16[4,128,256]{2,1,0:T(8,128)(2,1)S(1)}, bf16[4,128,256]{2,1,0:T(8,128)(2,1)S(1)}, u32[]{:S(2)}, u32[]{:S(2)}) collective-permute-start(bf16[4,128,256]{2,1,0:T(8,128)(2,1)S(1)} %get-tuple-element.132.refs_3_), channel_id=1, source_target_pairs={{0,6},{1,7},{2,4},{3,5},{4,2},{5,3},{6,0},{7,1},{8,14},{9,15},{10,... | collective-permute-start | bytes 786440 | tf_op jit(solution)/shard_map/ppermute | solution.py:396
  197.7 11.0 %collective-permute-start.21 = (bf16[128,512]{1,0:T(8,128)(2,1)}, bf16[128,512]{1,0:T(8,128)(2,1)}, u32[]{:S(2)}, u32[]{:S(2)}) collective-permute-start(bf16[128,512]{1,0:T(8,128)(2,1)} %get-tuple-element.113), channel_id=1, source_target_pairs={{0,1},{1,0},{2,3},{3,2},{4,5},{5,4},{6,7},{7,6},{8,9},{9,8},{10,11... | collective-permute-start | bytes 393224 | tf_op jit(solution)/shard_map/ppermute | solution.py:396
  197.7 11.5 %collective-permute-start.22 = (bf16[128,512]{1,0:T(8,128)(2,1)}, bf16[128,512]{1,0:T(8,128)(2,1)}, u32[]{:S(2)}, u32[]{:S(2)}) collective-permute-start(bf16[128,512]{1,0:T(8,128)(2,1)} %get-tuple-element.114), channel_id=1, source_target_pairs={{0,8},{1,9},{2,10},{3,11},{4,12},{5,13},{6,14},{7,15},{8,0},{9,1},... | collective-permute-start | bytes 393224 | tf_op jit(solution)/shard_map/ppermute | solution.py:396
  203.1 6.8 %collective-permute-start.23 = (bf16[128,512]{1,0:T(8,128)(2,1)}, bf16[128,512]{1,0:T(8,128)(2,1)}, u32[]{:S(2)}, u32[]{:S(2)}) collective-permute-start(bf16[128,512]{1,0:T(8,128)(2,1)} %get-tuple-element.115), channel_id=1, source_target_pairs={{0,9},{1,8},{2,11},{3,10},{4,13},{5,12},{6,15},{7,14},{8,1},{9,0},... | collective-permute-start | bytes 393224 | tf_op jit(solution)/shard_map/ppermute | solution.py:396
  206.0 5.0 %collective-permute-start.28 = (bf16[128,256]{1,0:T(8,128)(2,1)S(1)}, bf16[128,256]{1,0:T(8,128)(2,1)S(1)}, u32[]{:S(2)}, u32[]{:S(2)}) collective-permute-start(bf16[128,256]{1,0:T(8,128)(2,1)S(1)} %get-tuple-element.127), channel_id=1, source_target_pairs={{0,1},{1,0},{2,3},{3,2},{4,5},{5,4},{6,7},{7,6},{8,9},{9,8},{10,11... | collective-permute-start | bytes 196616 | tf_op jit(solution)/shard_map/ppermute | solution.py:396
  207.5 4.3 %collective-permute-start.29 = (bf16[128,256]{1,0:T(8,128)(2,1)S(1)}, bf16[128,256]{1,0:T(8,128)(2,1)S(1)}, u32[]{:S(2)}, u32[]{:S(2)}) collective-permute-start(bf16[128,256]{1,0:T(8,128)(2,1)S(1)} %get-tuple-element.128), channel_id=1, source_target_pairs={{0,8},{1,9},{2,10},{3,11},{4,12},{5,13},{6,14},{7,15},{8,0},{9,1},... | collective-permute-start | bytes 196616 | tf_op jit(solution)/shard_map/ppermute | solution.py:396
  208.7 4.2 %collective-permute-start.30 = (bf16[128,256]{1,0:T(8,128)(2,1)S(1)}, bf16[128,256]{1,0:T(8,128)(2,1)S(1)}, u32[]{:S(2)}, u32[]{:S(2)}) collective-permute-start(bf16[128,256]{1,0:T(8,128)(2,1)S(1)} %get-tuple-element.129), channel_id=1, source_target_pairs={{0,9},{1,8},{2,11},{3,10},{4,13},{5,12},{6,15},{7,14},{8,1},{9,0},... | collective-permute-start | bytes 196616 | tf_op jit(solution)/shard_map/ppermute | solution.py:396
  209.2 3.7 %collective-permute-start.34 = (bf16[128,256]{1,0:T(8,128)(2,1)S(1)}, bf16[128,256]{1,0:T(8,128)(2,1)S(1)}, u32[]{:S(2)}, u32[]{:S(2)}) collective-permute-start(bf16[128,256]{1,0:T(8,128)(2,1)S(1)} %get-tuple-element.134), channel_id=1, source_target_pairs={{0,1},{1,0},{2,3},{3,2},{4,5},{5,4},{6,7},{7,6},{8,9},{9,8},{10,11... | collective-permute-start | bytes 196616 | tf_op jit(solution)/shard_map/ppermute | solution.py:396
  209.9 5.0 %collective-permute-start.35 = (bf16[128,256]{1,0:T(8,128)(2,1)S(1)}, bf16[128,256]{1,0:T(8,128)(2,1)S(1)}, u32[]{:S(2)}, u32[]{:S(2)}) collective-permute-start(bf16[128,256]{1,0:T(8,128)(2,1)S(1)} %get-tuple-element.135), channel_id=1, source_target_pairs={{0,8},{1,9},{2,10},{3,11},{4,12},{5,13},{6,14},{7,15},{8,0},{9,1},... | collective-permute-start | bytes 196616 | tf_op jit(solution)/shard_map/ppermute | solution.py:396
  211.0 4.7 %collective-permute-start.36 = (bf16[128,256]{1,0:T(8,128)(2,1)S(1)}, bf16[128,256]{1,0:T(8,128)(2,1)S(1)}, u32[]{:S(2)}, u32[]{:S(2)}) collective-permute-start(bf16[128,256]{1,0:T(8,128)(2,1)S(1)} %get-tuple-element.136), channel_id=1, source_target_pairs={{0,9},{1,8},{2,11},{3,10},{4,13},{5,12},{6,15},{7,14},{8,1},{9,0},... | collective-permute-start | bytes 196616 | tf_op jit(solution)/shard_map/ppermute | solution.py:396

commit v10 on v9

--- a/solution.py
+++ b/solution.py
@@ -328,24 +328,29 @@
     )(choice, pltpu.with_memory_space_constraint(rows_stack, pltpu.VMEM), *arrays, *after)
 
 
-def add_kernel(relative, own, one, two, three, *refs):
-    blocks_wide, outs = own.shape[2] // LANES, refs[-4:]
-    for piece in range(4):
-        for at in range(blocks_wide):
-            here = pl.ds(at * LANES, LANES)
-            total = own[piece, :, here]
-            for step, ref in ((1, one), (2, two), (3, three)):
-                source = at ^ step if relative else at
-                total += ref[piece, :, pl.ds(source * LANES, LANES)].astype(jnp.float32)
-            outs[piece][:, here] = total.astype(jnp.bfloat16)
-
-
-def add(own, others, relative, after=()):
-    _, rows, columns = own.shape
-    return pl.pallas_call(
-        functools.partial(add_kernel, relative),
+def add_kernel(kinds, *refs):
+    outs, first = refs[-4:], 0
+    for kind, relative in enumerate(kinds):
+        own, *others = refs[4 * kind : 4 * kind + 4]
+        blocks_wide = own.shape[2] // LANES
+        for piece in range(4):
+            for at in range(blocks_wide):
+                total = own[piece, :, pl.ds(at * LANES, LANES)]
+                for step, ref in zip((1, 2, 3), others):
+                    source = at ^ step if relative else at
+                    total += ref[piece, :, pl.ds(source * LANES, LANES)].astype(jnp.float32)
+                outs[piece][:, pl.ds((first + at) * LANES, LANES)] = total.astype(jnp.bfloat16)
+        first += blocks_wide
+
+
+def add(terms, kinds, after=()):
+    rows = terms[0][0].shape[1]
+    columns = sum(own.shape[2] for own, *_ in terms)
+    arrays = [array for group in terms for array in group]
+    return pl.pallas_call(
+        functools.partial(add_kernel, kinds),
         out_shape=[jax.ShapeDtypeStruct((rows, columns), jnp.bfloat16)] * 4,
-        in_specs=[pl.BlockSpec(memory_space=pltpu.VMEM)] * 4
+        in_specs=[pl.BlockSpec(memory_space=pltpu.VMEM)] * len(arrays)
         + [pl.BlockSpec(memory_space=pl.ANY)] * len(after),
         out_specs=[pl.BlockSpec(memory_space=pltpu.VMEM)] * 4,
         compiler_params=pltpu.CompilerParams(vmem_limit_bytes=LIMIT),
@@ -353,16 +358,15 @@
             flops=12 * rows * columns, bytes_accessed=48 * rows * columns, transcendentals=0
         ),
         name="add",
-    )(own, *others, *after)
+    )(*arrays, *after)
 
 
 def assemble_kernel(groups, place_ref, *refs):
     out = refs[-1]
-    for ref, (fixed, first, relative) in zip(refs, groups):
-        place = place_ref[0] if relative else place_ref[1]
-        for at in range(ref.shape[1] // LANES):
-            index = fixed | ((first + at) << 1)
-            to = pl.multiple_of((place ^ index) * LANES, LANES)
+    for ref, (fixed, parts) in zip(refs, groups):
+        for at, (half, block) in enumerate(parts):
+            index = fixed | (half << 3) | (block << 1)
+            to = pl.multiple_of((place_ref[half] ^ index) * LANES, LANES)
             out[:, pl.ds(to, LANES)] = ref[:, pl.ds(at * LANES, LANES)]
 
 
@@ -422,16 +426,15 @@
     order = jnp.array([[1, 2, 3], [1, 3, 2], [2, 3, 1], [3, 2, 1]], jnp.int32)[plane]
     got_3, core_0, core_pair_0 = lax.optimization_barrier((got_3, core_0, core_pair_0))
     known = jnp.array([0, 3], jnp.int32)
-    a_3, w_3, ordered_1 = reorder(jnp.concatenate([known, order[:1]]), got_3, w_12)
-    w_3, mid_12 = lax.optimization_barrier((w_3, mid_12))
-    pair_3, mid_3 = to_pair(a_3), to_mid(w_3)
+    a_3, w_3, ordered_1, ordered_2 = reorder(jnp.concatenate([known, order[:2]]), got_3, w_12)
+    pair_3 = to_pair(a_3)
     a_12, pair_12, a_3 = lax.optimization_barrier((a_12, pair_12, a_3))
     core_12, core_pair_12 = to_core(a_12), to_core(pair_12)
-    got_3, pair_3, mid_3, core_12, core_pair_12 = lax.optimization_barrier(
-        (got_3, pair_3, mid_3, core_12, core_pair_12)
-    )
-    ordered_2, ordered_3 = reorder(order[1:], got_3, w_12)
-    next_1, next_2, next_3 = to_next(ordered_1), to_next(ordered_2), to_next(ordered_3)
+    w_3, mid_12, core_12 = lax.optimization_barrier((w_3, mid_12, core_12))
+    mid_3 = to_mid(w_3)
+    ordered_1, pair_3 = lax.optimization_barrier((ordered_1, pair_3))
+    ordered_2, mid_3 = lax.optimization_barrier((ordered_2, mid_3))
+    next_1, next_2 = to_next(ordered_1), to_next(ordered_2)
     core_3, core_pair_3 = to_core(a_3), to_core(pair_3)
 
     a_0, w_0, a_12, w_12, a_3, w_3 = far([a_0, w_0, a_12, w_12, a_3, w_3])
@@ -458,18 +461,18 @@
 
     pieces = []
 
-    def spread(totals, others, half, start, after=()):
-        summed = add(totals[0], others, half == 0, after)
+    def spread(terms, kinds, parts, after=()):
+        summed = add(terms, kinds, after)
         for piece in range(4):
             mask = (piece >> 1) * PAIR + (piece & 1) * CORE
             block = send(summed[piece], flip(n, mask)) if mask else summed[piece]
-            fixed = ((piece >> 1) << 4) | (half << 3) | (piece & 1)
-            pieces.append((block, fixed, start, half == 0))
-        return summed[0]
+            pieces.append((block, ((piece >> 1) << 4) | (piece & 1), parts))
 
     rows_stack, *own = stack_product(mid, places, a_blocks, [w_own, w_mid])
     own = totals_of(mid, [w_own, w_mid], ([0],), (own[0],)) + own
-    own[1], own[2], own[3], next_1 = lax.optimization_barrier((*own[1:], next_1))
+    own[1], got_3 = lax.optimization_barrier((own[1], got_3))
+    (ordered_3,) = reorder(order[2:], got_3, w_12)
+    next_3 = to_next(ordered_3)
     own_sums = across_plane(own)
     first, one, two, three = [(block, None) for block in (next_0, next_1, next_2, next_3)]
     w_low = [[first, one], [one, first], [one, two], [one, two]]
@@ -477,12 +480,16 @@
     low = totals_of(at_plane, w_low, ([3, 1, 2, 0],), (own[0],))
     low[1], low[2], low[3], *own_sums = lax.optimization_barrier((*low[1:], *own_sums))
     low_sums = across_plane(low)
-    summed = spread(own, own_sums, 0, 0, (low[0],))
-    high = totals_of(at_plane, w_high, ([3, 1, 2], [0]), (low[0], summed))
+    high = totals_of(at_plane, w_high, ([3, 1, 2], [0]), (low[0],))
     high[1], high[2], high[3], *low_sums = lax.optimization_barrier((*high[1:], *low_sums))
     high_sums = across_plane(high)
-    spread(low, low_sums, 1, 0, (high[0],))
-    spread(high, high_sums, 1, 2)
+    spread(
+        [(own[0], *own_sums), (low[0], *low_sums)],
+        (True, False),
+        [(0, 0), (0, 1), (0, 2), (0, 3), (1, 0), (1, 1)],
+        (high[0],),
+    )
+    spread([(high[0], *high_sums)], (False,), [(1, 2), (1, 3)])
     across = z_low * 16 + z_high * 8 + me % 2
     place = jnp.stack([across + plane * 2, across]).astype(jnp.int32)
     return assemble(place, pieces)

time: 218 us -> 227 us (1.041)
  starting transfers between devices: 52.1 us -> 65.9 us
  waiting for transfers between devices: 112 us -> 107 us
    ppermute x37 -> x34, starting transfers between devices: 52.1 us -> 65.9 us  [send(): return lax.ppermute(array, 'fsdp', perm=perm)]
    ppermute x37 -> x34, waiting for transfers between devices: 112 us -> 107 us  [send(): return lax.ppermute(array, 'fsdp', perm=perm)]
  transfers between devices with their start and end apart: 37 -> 34, of which waited for: 16 -> 19; matrix products, arithmetic and copies ran while one was open for 0% -> 1% of each run, Pallas kernels for 19% -> 18%
where the time goes in v10:
time: 227 us; the launch traced here: 226 us
  waiting for transfers between devices  107 us (47%)
  starting transfers between devices  65.9 us (29%)
  Pallas kernels  48.8 us (21%)
  local copies, waits for them, and re-layouts  3.77 us (2%)
    ppermute x34, waiting for transfers between devices, send(): return lax.ppermute(array, 'fsdp', perm=perm)  107 us
    ppermute x34, starting transfers between devices, send(): return lax.ppermute(array, 'fsdp', perm=perm)  65.9 us
    pallas_call x4, Pallas kernels, product(): pl.pallas_call(functools.partial(product_kernel, [places[group] for group...  14.2 us
    pallas_call x1, Pallas kernels, stack_product(): pl.pallas_call(functools.partial(stack_product_kernel, places, a_at, w_at...  11 us
    pallas_call x2, Pallas kernels, pack(): pl.pallas_call(functools.partial(pack_kernel, apart, len(steps)), out_sha...  10.4 us
    pallas_call x2, Pallas kernels, reorder(): pl.pallas_call(functools.partial(reorder_kernel, count), out_shape=[pltpu...  8.07 us
  transfers between devices with their start and end apart: 34, of which 19 were waited for; matrix products, arithmetic and copies ran while one was open for 1% of the time, Pallas kernels for 18%

profile of v10, /device:TPU:0, one launch (start us, length us, event | category | flops | bytes accessed | tf_op | source)
XLA Modules:
  0.0 226.2 jit_solution(16167278568161535438)
XLA Ops:
  0.0 6.3 %pack.2 = (bf16[28,128,128]{2,1,0:T(8,128)(2,1)}, bf16[28,128,128]{2,1,0:T(8,128)(2,1)}, bf16[2,28,128,128]{3,2,1,0:T(8,128)(2,1)}, bf16[2,28,128,128]{3,2,1,0:T(8,128)(2,1)}) custom-call(s32[1]{0:T(128)} %bitcast.3.plane_ref.choice_ref, bf16[128,14336]{1,0:T(8,128)(2,1)} %refs_0_.3, bf16[128,14336]{1,0:T(8,128)(2,1)} %refs_1_.3, ...), custom_call_target="tpu_custom_call" | custom-call | bytes 13762560 | tf_op jit(solution)/shard_map/pack/pallas_call | solution.py:63
  6.3 3.0 %collective-permute-start.1 = (bf16[2,28,128,128]{3,2,1,0:T(8,128)(2,1)}, bf16[2,28,128,128]{3,2,1,0:T(8,128)(2,1)S(1)}, u32[]{:S(2)}, u32[]{:S(2)}) collective-permute-start(bf16[2,28,128,128]{3,2,1,0:T(8,128)(2,1)} %get-tuple-element.65), channel_id=1, source_target_pairs={{0,2},{1,3},{2,0},{3,1},{4,6},{5,7},{6,4},{7,5},{8,10},{9,11},{10,... | collective-permute-start | bytes 5505032 | tf_op jit(solution)/shard_map/ppermute | solution.py:400
  9.3 1.5 collective-permute-start.2
  10.8 1.6 collective-permute-start
  12.4 2.6 %collective-permute-start.7 = (bf16[28,128,128]{2,1,0:T(8,128)(2,1)}, bf16[28,128,128]{2,1,0:T(8,128)(2,1)S(1)}, u32[]{:S(2)}, u32[]{:S(2)}) collective-permute-start(bf16[28,128,128]{2,1,0:T(8,128)(2,1)} %get-tuple-element.72.refs_12_.refs_0_), channel_id=1, source_target_pairs={{8,0},{9,1},{10,2},{11,3},{12,4},{13,5},{14,6},{15,7},{24,8},{25,9... | collective-permute-start | bytes 2752520 | tf_op jit(solution)/shard_map/ppermute | solution.py:400
  15.0 0.7 collective-permute-start.6
  15.7 18.6 %collective-permute-done.refs_3_.refs_0_.refs_1_ = bf16[28,128,128]{2,1,0:T(8,128)(2,1)S(1)} collective-permute-done((bf16[28,128,128]{2,1,0:T(8,128)(2,1)}, bf16[28,128,128]{2,1,0:T(8,128)(2,1)S(1)}, u32[]{:S(2)}, u32[]{:S(2)}) %collective-permute-start) | collective-permute-done | bytes 917536 | tf_op jit(solution)/shard_map/ppermute | solution.py:400
  34.3 4.0 %pack.3 = bf16[2,28,128,128]{3,2,1,0:T(8,128)(2,1)} custom-call(s32[1]{0:T(128)} %bitcast.3.plane_ref.choice_ref, bf16[128,14336]{1,0:T(8,128)(2,1)} %refs_0_.3, bf16[128,14336]{1,0:T(8,128)(2,1)} %refs_1_.3, bf16[14336,128]{1,0:T(8,128)(2,1)} %refs_2_.3, bf16[28,128,128]{2,1,0:T(8,128)(2,1)S(1)} %collective-permute-done.refs_3_.refs_0_.refs_1_), custom_call_target="tpu_custom_call" | custom-call | bytes 4587520 | tf_op jit(solution)/shard_map/pack/pallas_call | solution.py:63
  38.4 11.2 %collective-permute-done.1.one = bf16[2,28,128,128]{3,2,1,0:T(8,128)(2,1)S(1)} collective-permute-done((bf16[2,28,128,128]{3,2,1,0:T(8,128)(2,1)}, bf16[2,28,128,128]{3,2,1,0:T(8,128)(2,1)S(1)}, u32[]{:S(2)}, u32[]{:S(2)}) %collective-permute-start.1) | collective-permute-done | bytes 1835040 | tf_op jit(solution)/shard_map/ppermute | solution.py:400
  49.5 1.5 collective-permute-done.2.two
  51.0 1.5 collective-permute-start.3
  52.5 2.9 %unpack_pair.1 = (bf16[2,28,128,128]{3,2,1,0:T(8,128)(2,1)}, bf16[2,28,128,128]{3,2,1,0:T(8,128)(2,1)}) custom-call(bf16[2,28,128,128]{3,2,1,0:T(8,128)(2,1)S(1)} %collective-permute-done.1.one, bf16[2,28,128,128]{3,2,1,0:T(8,128)(2,1)S(1)} %collective-permute-done.2.two, bf16[28,128,128]{2,1,0:T(8,128)(2,1)S(1)} %collective-permute-done.refs_3_.refs_0_.refs_1_, ...), custom_call_target="tpu_custom_call" | custom-call | bytes 7340032 | tf_op jit(solution)/shard_map/unpack_pair/pallas_call | solution.py:106
  55.4 4.7 %collective-permute-start.8 = (bf16[2,28,128,128]{3,2,1,0:T(8,128)(2,1)}, bf16[2,28,128,128]{3,2,1,0:T(8,128)(2,1)}, u32[]{:S(2)}, u32[]{:S(2)}) collective-permute-start(bf16[2,28,128,128]{3,2,1,0:T(8,128)(2,1)} %get-tuple-element.77.refs_4_), channel_id=1, source_target_pairs={{0,8},{1,9},{2,10},{3,11},{4,12},{5,13},{6,14},{7,15},{8,0},{9,1},... | collective-permute-start | bytes 5505032 | tf_op jit(solution)/shard_map/ppermute | solution.py:400
  60.6 0.7 constant_dynamic-slice_fusion
  61.4 2.0 collective-permute-start.9
  64.1 28.7 %collective-permute-done.3.packed = bf16[2,28,128,128]{3,2,1,0:T(8,128)(2,1)} collective-permute-done((bf16[2,28,128,128]{3,2,1,0:T(8,128)(2,1)}, bf16[2,28,128,128]{3,2,1,0:T(8,128)(2,1)}, u32[]{:S(2)}, u32[]{:S(2)}) %collective-permute-start.3) | collective-permute-done | bytes 1835040 | tf_op jit(solution)/shard_map/ppermute | solution.py:400
  92.8 4.4 %reorder.2 = (bf16[28,128,128]{2,1,0:T(8,128)(2,1)}, bf16[28,128,128]{2,1,0:T(8,128)(2,1)}, bf16[28,128,128]{2,1,0:T(8,128)(2,1)}, bf16[28,128,128]{2,1,0:T(8,128)(2,1)}) custom-call(s32[4]{0:T(128)S(1)} %pad_add_fusion.1.order_ref, bf16[2,28,128,128]{3,2,1,0:T(8,128)(2,1)} %collective-permute-done.3.packed, ...), custom_call_target="tpu_custom_call" | custom-call | bytes 7340032 | tf_op jit(solution)/shard_map/reorder/pallas_call | solution.py:144
  97.6 1.7 collective-permute-start.12
  99.6 1.8 collective-permute-done.10.refs_6_
  101.4 1.2 copy-done.5
  102.6 0.7 collective-permute-start.15
  103.5 17.1 %collective-permute-done.12.refs_9_ = bf16[28,128,128]{2,1,0:T(8,128)(2,1)} collective-permute-done((bf16[28,128,128]{2,1,0:T(8,128)(2,1)}, bf16[28,128,128]{2,1,0:T(8,128)(2,1)}, u32[]{:S(2)}, u32[]{:S(2)}) %collective-permute-start.12) | collective-permute-done | bytes 917536 | tf_op jit(solution)/shard_map/ppermute | solution.py:400
  121.3 3.6 %collective-permute-start.16 = (bf16[28,128,128]{2,1,0:T(8,128)(2,1)}, bf16[28,128,128]{2,1,0:T(8,128)(2,1)S(1)}, u32[]{:S(2)}, u32[]{:S(2)}) collective-permute-start(bf16[28,128,128]{2,1,0:T(8,128)(2,1)} %get-tuple-element.90), channel_id=1, source_target_pairs={{8,0},{9,1},{10,2},{11,3},{12,4},{13,5},{14,6},{15,7},{24,8},{25,9... | collective-permute-start | bytes 2752520 | tf_op jit(solution)/shard_map/ppermute | solution.py:400
  124.9 26.4 %collective-permute-start.17 = (bf16[28,128,128]{2,1,0:T(8,128)(2,1)}, bf16[28,128,128]{2,1,0:T(8,128)(2,1)S(1)}, u32[]{:S(2)}, u32[]{:S(2)}) collective-permute-start(bf16[28,128,128]{2,1,0:T(8,128)(2,1)} %get-tuple-element.91), channel_id=1, source_target_pairs={{8,0},{9,1},{10,2},{11,3},{12,4},{13,5},{14,6},{15,7},{24,8},{25,9... | collective-permute-start | bytes 2752520 | tf_op jit(solution)/shard_map/ppermute | solution.py:400
  151.3 1.2 copy-done.2
  152.5 11.0 %stack_product.1 = (bf16[28,2048,128]{2,1,0:T(8,128)(2,1)S(1)}, bf16[4,128,512]{2,1,0:T(8,128)(2,1)S(1)}, bf16[4,128,512]{2,1,0:T(8,128)(2,1)S(1)}, bf16[4,128,512]{2,1,0:T(8,128)(2,1)S(1)}) custom-call(s32[1]{0:T(128)} %bitcast.2.choice_ref, bf16[28,128,128]{2,1,0:T(8,128)(2,1)} %get-tuple-element.64.refs_0_, ...), custom_call_target="tpu_custom_call" | custom-call | flops 5637144576 | bytes 18350080 | tf_op jit(solution)/shard_map/stack_product/pallas_call | solution.py:236
  163.5 3.7 %reorder.3 = bf16[28,128,128]{2,1,0:T(8,128)(2,1)} custom-call(s32[1]{0:T(128)} %bitcast.5.order_ref, bf16[2,28,128,128]{3,2,1,0:T(8,128)(2,1)} %collective-permute-done.3.packed, bf16[2,28,128,128]{3,2,1,0:T(8,128)(2,1)} %get-tuple-element.75.w_12.refs_13_.refs_1_), custom_call_target="tpu_custom_call" | custom-call | bytes 7340032 | tf_op jit(solution)/shard_map/reorder/pallas_call | solution.py:144
  167.2 1.7 collective-permute-start.21
  170.0 2.4 %collective-permute-start.20 = (bf16[4,128,512]{2,1,0:T(8,128)(2,1)S(1)}, bf16[4,128,512]{2,1,0:T(8,128)(2,1)S(1)}, u32[]{:S(2)}, u32[]{:S(2)}) collective-permute-start(bf16[4,128,512]{2,1,0:T(8,128)(2,1)S(1)} %get-tuple-element.97), channel_id=1, source_target_pairs={{0,6},{1,7},{2,4},{3,5},{4,2},{5,3},{6,0},{7,1},{8,14},{9,15},{10,... | collective-permute-start | bytes 1572872 | tf_op jit(solution)/shard_map/ppermute | solution.py:400
  172.4 4.1 %product.4.refs_3_.refs_0_ = f32[4,128,512]{2,1,0:T(8,128)S(1)} custom-call(s32[1]{0:T(128)} %bitcast.2.choice_ref, bf16[28,2048,128]{2,1,0:T(8,128)(2,1)S(1)} %get-tuple-element.88.a, bf16[28,128,128]{2,1,0:T(8,128)(2,1)} %get-tuple-element.72.refs_12_.refs_0_, bf16[2,28,128,128]{3,2,1,0:T(8,128)(2,1)} %get-tuple-element.75.w_12.refs_13_.refs_1_, ...), custom_call_target="tpu_custom_call" | custom-call | flops 1879048192 | bytes 7340032 | tf_op jit(solution)/shard_map/product/pallas_call | solution.py:305
  176.5 4.5 %product.5 = (bf16[4,128,256]{2,1,0:T(8,128)(2,1)S(1)}, bf16[4,128,256]{2,1,0:T(8,128)(2,1)S(1)}, bf16[4,128,256]{2,1,0:T(8,128)(2,1)S(1)}, f32[4,128,256]{2,1,0:T(8,128)S(1)}) custom-call(s32[1]{0:T(128)} %bitcast.3.plane_ref.choice_ref, bf16[28,2048,128]{2,1,0:T(8,128)(2,1)S(1)} %get-tuple-element.88.a, ...), custom_call_target="tpu_custom_call" | custom-call | flops 3758096384 | bytes 16515072 | tf_op jit(solution)/shard_map/product/pallas_call | solution.py:305
  181.0 2.7 %collective-permute-done.18.refs_1_ = bf16[4,128,512]{2,1,0:T(8,128)(2,1)S(1)} collective-permute-done((bf16[4,128,512]{2,1,0:T(8,128)(2,1)S(1)}, bf16[4,128,512]{2,1,0:T(8,128)(2,1)S(1)}, u32[]{:S(2)}, u32[]{:S(2)}) %collective-permute-start.18) | collective-permute-done | bytes 524320 | tf_op jit(solution)/shard_map/ppermute | solution.py:400
  183.8 8.6 %collective-permute-done.19.refs_2_ = bf16[4,128,512]{2,1,0:T(8,128)(2,1)S(1)} collective-permute-done((bf16[4,128,512]{2,1,0:T(8,128)(2,1)S(1)}, bf16[4,128,512]{2,1,0:T(8,128)(2,1)S(1)}, u32[]{:S(2)}, u32[]{:S(2)}) %collective-permute-start.19) | collective-permute-done | bytes 524320 | tf_op jit(solution)/shard_map/ppermute | solution.py:400
  192.4 1.6 collective-permute-start.22
  194.3 1.6 collective-permute-start.24
  195.9 4.1 %product.6 = (bf16[4,128,256]{2,1,0:T(8,128)(2,1)S(1)}, bf16[4,128,256]{2,1,0:T(8,128)(2,1)S(1)}, bf16[4,128,256]{2,1,0:T(8,128)(2,1)}) custom-call(s32[1]{0:T(128)} %bitcast.3.plane_ref.choice_ref, bf16[28,2048,128]{2,1,0:T(8,128)(2,1)S(1)} %get-tuple-element.88.a, bf16[28,128,128]{2,1,0:T(8,128)(2,1)S(1)} %collective-permute-done.17.refs_2_.refs_0_, ...), custom_call_target="tpu_custom_call" | custom-call | flops 2818572288 | bytes 12845056 | tf_op jit(solution)/shard_map/product/pallas_call | solution.py:305
  200.5 3.4 %collective-permute-done.23.refs_6_ = bf16[4,128,256]{2,1,0:T(8,128)(2,1)S(1)} collective-permute-done((bf16[4,128,256]{2,1,0:T(8,128)(2,1)S(1)}, bf16[4,128,256]{2,1,0:T(8,128)(2,1)S(1)}, u32[]{:S(2)}, u32[]{:S(2)}) %collective-permute-start.23) | collective-permute-done | bytes 262176 | tf_op jit(solution)/shard_map/ppermute | solution.py:400
  203.8 1.3 collective-permute-done.24.refs_7_
  205.6 0.9 collective-permute-start.29
  206.5 2.1 collective-permute-start.30
  208.6 1.5 product.7.refs_8_.refs_0_
  210.6 1.2 collective-permute-done.28.refs_1_
  212.4 3.1 %collective-permute-done.29.refs_2_ = bf16[4,128,256]{2,1,0:T(8,128)(2,1)S(1)} collective-permute-done((bf16[4,128,256]{2,1,0:T(8,128)(2,1)}, bf16[4,128,256]{2,1,0:T(8,128)(2,1)S(1)}, u32[]{:S(2)}, u32[]{:S(2)}) %collective-permute-start.29) | collective-permute-done | bytes 262176 | tf_op jit(solution)/shard_map/ppermute | solution.py:400
  215.8 1.8 collective-permute-start.33
  217.6 0.7 collective-permute-done.26.refs_2_
  218.3 3.3 %collective-permute-done.27.refs_3_ = bf16[128,768]{1,0:T(8,128)(2,1)S(1)} collective-permute-done((bf16[128,768]{1,0:T(8,128)(2,1)S(1)}, bf16[128,768]{1,0:T(8,128)(2,1)S(1)}, u32[]{:S(2)}, u32[]{:S(2)}) %collective-permute-start.27) | collective-permute-done | bytes 196640 | tf_op jit(solution)/shard_map/ppermute | solution.py:400
  221.6 2.3 %collective-permute-done.32.refs_6_ = bf16[128,256]{1,0:T(8,128)(2,1)S(1)} collective-permute-done((bf16[128,256]{1,0:T(8,128)(2,1)S(1)}, bf16[128,256]{1,0:T(8,128)(2,1)S(1)}, u32[]{:S(2)}, u32[]{:S(2)}) %collective-permute-start.32) | collective-permute-done | bytes 65568 | tf_op jit(solution)/shard_map/ppermute | solution.py:400
  224.4 1.8 assemble.1
  (51 shorter events, 7.1 us)
Async XLA Ops:
  6.3 43.2 %collective-permute-start.1 = (bf16[2,28,128,128]{3,2,1,0:T(8,128)(2,1)}, bf16[2,28,128,128]{3,2,1,0:T(8,128)(2,1)S(1)}, u32[]{:S(2)}, u32[]{:S(2)}) collective-permute-start(bf16[2,28,128,128]{3,2,1,0:T(8,128)(2,1)} %get-tuple-element.65), channel_id=1, source_target_pairs={{0,2},{1,3},{2,0},{3,1},{4,6},{5,7},{6,4},{7,5},{8,10},{9,11},{10,... | collective-permute-start | bytes 5505032 | tf_op jit(solution)/shard_map/ppermute | solution.py:400
  9.3 41.7 %collective-permute-start.2 = (bf16[2,28,128,128]{3,2,1,0:T(8,128)(2,1)}, bf16[2,28,128,128]{3,2,1,0:T(8,128)(2,1)S(1)}, u32[]{:S(2)}, u32[]{:S(2)}) collective-permute-start(bf16[2,28,128,128]{3,2,1,0:T(8,128)(2,1)} %get-tuple-element.66), channel_id=1, source_target_pairs={{0,4},{1,5},{2,6},{3,7},{4,0},{5,1},{6,2},{7,3},{8,12},{9,13},{10,... | collective-permute-start | bytes 5505032 | tf_op jit(solution)/shard_map/ppermute | solution.py:400
  10.8 23.5 %collective-permute-start = (bf16[28,128,128]{2,1,0:T(8,128)(2,1)}, bf16[28,128,128]{2,1,0:T(8,128)(2,1)S(1)}, u32[]{:S(2)}, u32[]{:S(2)}) collective-permute-start(bf16[28,128,128]{2,1,0:T(8,128)(2,1)} %get-tuple-element.64.refs_0_), channel_id=1, source_target_pairs={{0,8},{1,9},{2,10},{3,11},{4,12},{5,13},{6,14},{7,15},{8,0},{9,1},... | collective-permute-start | bytes 2752520 | tf_op jit(solution)/shard_map/ppermute | solution.py:400
  12.4 40.1 %collective-permute-start.7 = (bf16[28,128,128]{2,1,0:T(8,128)(2,1)}, bf16[28,128,128]{2,1,0:T(8,128)(2,1)S(1)}, u32[]{:S(2)}, u32[]{:S(2)}) collective-permute-start(bf16[28,128,128]{2,1,0:T(8,128)(2,1)} %get-tuple-element.72.refs_12_.refs_0_), channel_id=1, source_target_pairs={{8,0},{9,1},{10,2},{11,3},{12,4},{13,5},{14,6},{15,7},{24,8},{25,9... | collective-permute-start | bytes 2752520 | tf_op jit(solution)/shard_map/ppermute | solution.py:400
  15.0 37.5 %collective-permute-start.6 = (bf16[28,128,128]{2,1,0:T(8,128)(2,1)}, bf16[28,128,128]{2,1,0:T(8,128)(2,1)S(1)}, u32[]{:S(2)}, u32[]{:S(2)}) collective-permute-start(bf16[28,128,128]{2,1,0:T(8,128)(2,1)} %get-tuple-element.72.refs_12_.refs_0_), channel_id=1, source_target_pairs={{8,16},{9,17},{10,18},{11,19},{12,20},{13,21},{14,22},{15,23},{16,... | collective-permute-start | bytes 2752520 | tf_op jit(solution)/shard_map/ppermute | solution.py:400
  51.0 41.8 %collective-permute-start.3 = (bf16[2,28,128,128]{3,2,1,0:T(8,128)(2,1)}, bf16[2,28,128,128]{3,2,1,0:T(8,128)(2,1)}, u32[]{:S(2)}, u32[]{:S(2)}) collective-permute-start(bf16[2,28,128,128]{3,2,1,0:T(8,128)(2,1)} %pack.3), channel_id=1, source_target_pairs={{0,6},{1,7},{2,4},{3,5},{4,2},{5,3},{6,0},{7,1},{8,14},{9,15},{10,... | collective-permute-start | bytes 5505032 | tf_op jit(solution)/shard_map/ppermute | solution.py:400
  52.5 2.9 %copy-start = (bf16[28,128,128]{2,1,0:T(8,128)(2,1)}, bf16[28,128,128]{2,1,0:T(8,128)(2,1)S(1)}, u32[]{:S(2)}) copy-start(bf16[28,128,128]{2,1,0:T(8,128)(2,1)S(1)} %collective-permute-done.6.refs_1_.refs_15_.refs_3_) | copy-start | bytes 2752516
  55.4 42.2 %collective-permute-start.8 = (bf16[2,28,128,128]{3,2,1,0:T(8,128)(2,1)}, bf16[2,28,128,128]{3,2,1,0:T(8,128)(2,1)}, u32[]{:S(2)}, u32[]{:S(2)}) collective-permute-start(bf16[2,28,128,128]{3,2,1,0:T(8,128)(2,1)} %get-tuple-element.77.refs_4_), channel_id=1, source_target_pairs={{0,8},{1,9},{2,10},{3,11},{4,12},{5,13},{6,14},{7,15},{8,0},{9,1},... | collective-permute-start | bytes 5505032 | tf_op jit(solution)/shard_map/ppermute | solution.py:400
  60.1 4.0 %collective-permute-start.4 = (bf16[28,128,128]{2,1,0:T(8,128)(2,1)}, bf16[28,128,128]{2,1,0:T(8,128)(2,1)S(1)}, u32[]{:S(2)}, u32[]{:S(2)}) collective-permute-start(bf16[28,128,128]{2,1,0:T(8,128)(2,1)} %get-tuple-element.64.refs_0_), channel_id=1, source_target_pairs={{0,1},{1,0},{2,3},{3,2},{4,5},{5,4},{6,7},{7,6},{8,9},{9,8},{10,11... | collective-permute-start | bytes 2752520 | tf_op jit(solution)/shard_map/ppermute | solution.py:400
  60.1 4.0 %collective-permute-start.5 = (bf16[28,128,128]{2,1,0:T(8,128)(2,1)S(1)}, bf16[28,128,128]{2,1,0:T(8,128)(2,1)}, u32[]{:S(2)}, u32[]{:S(2)}) collective-permute-start(bf16[28,128,128]{2,1,0:T(8,128)(2,1)S(1)} %collective-permute-done.refs_3_.refs_0_.refs_1_), channel_id=1, source_target_pairs={{0,1},{1,0},{2,3},{3,2},{4,5},{5,4},{6,7},{7,6},{8,9},{9,8},{10,11... | collective-permute-start | bytes 2752520 | tf_op jit(solution)/shard_map/ppermute | solution.py:400
  61.4 36.2 %copy-start.4 = (bf16[2,28,128,128]{3,2,1,0:T(8,128)(2,1)S(1)}, bf16[2,28,128,128]{3,2,1,0:T(8,128)(2,1)}, u32[]{:S(2)}) copy-start(bf16[2,28,128,128]{3,2,1,0:T(8,128)(2,1)} %get-tuple-element.77.refs_4_) | copy-start | bytes 5505028
  61.4 38.2 %collective-permute-start.9 = (bf16[2,28,128,128]{3,2,1,0:T(8,128)(2,1)}, bf16[2,28,128,128]{3,2,1,0:T(8,128)(2,1)}, u32[]{:S(2)}, u32[]{:S(2)}) collective-permute-start(bf16[2,28,128,128]{3,2,1,0:T(8,128)(2,1)} %get-tuple-element.75.w_12.refs_13_.refs_1_), channel_id=1, source_target_pairs={{8,16},{9,17},{10,18},{11,19},{12,20},{13,21},{14,22},{15,23},{16,... | collective-permute-start | bytes 5505032 | tf_op jit(solution)/shard_map/ppermute | solution.py:400
  64.1 33.1 %copy-start.1 = (bf16[28,128,128]{2,1,0:T(8,128)(2,1)}, bf16[28,128,128]{2,1,0:T(8,128)(2,1)S(1)}, u32[]{:S(2)}) copy-start(bf16[28,128,128]{2,1,0:T(8,128)(2,1)S(1)} %collective-permute-done.4.refs_2_) | copy-start | bytes 2752516
  97.6 3.8 %collective-permute-start.10 = (bf16[2,28,128,128]{3,2,1,0:T(8,128)(2,1)S(1)}, bf16[2,28,128,128]{3,2,1,0:T(8,128)(2,1)S(1)}, u32[]{:S(2)}, u32[]{:S(2)}) collective-permute-start(bf16[2,28,128,128]{3,2,1,0:T(8,128)(2,1)S(1)} %copy-done.4), channel_id=1, source_target_pairs={{0,1},{1,0},{2,3},{3,2},{4,5},{5,4},{6,7},{7,6},{8,9},{9,8},{10,11... | collective-permute-start | bytes 5505032 | tf_op jit(solution)/shard_map/ppermute | solution.py:400
  97.6 23.1 %collective-permute-start.12 = (bf16[28,128,128]{2,1,0:T(8,128)(2,1)}, bf16[28,128,128]{2,1,0:T(8,128)(2,1)}, u32[]{:S(2)}, u32[]{:S(2)}) collective-permute-start(bf16[28,128,128]{2,1,0:T(8,128)(2,1)} %get-tuple-element.81.refs_8_), channel_id=1, source_target_pairs={{0,8},{1,9},{2,10},{3,11},{4,12},{5,13},{6,14},{7,15},{8,0},{9,1},... | collective-permute-start | bytes 2752520 | tf_op jit(solution)/shard_map/ppermute | solution.py:400
  99.3 52.0 %collective-permute-start.11 = (bf16[2,28,128,128]{3,2,1,0:T(8,128)(2,1)}, bf16[2,28,128,128]{3,2,1,0:T(8,128)(2,1)}, u32[]{:S(2)}, u32[]{:S(2)}) collective-permute-start(bf16[2,28,128,128]{3,2,1,0:T(8,128)(2,1)} %collective-permute-done.8.refs_5_), channel_id=1, source_target_pairs={{0,1},{1,0},{2,3},{3,2},{4,5},{5,4},{6,7},{7,6},{8,9},{9,8},{10,11... | collective-permute-start | bytes 5505032 | tf_op jit(solution)/shard_map/ppermute | solution.py:400
  101.4 1.2 copy-start.5
  102.6 22.3 %collective-permute-start.15 = (bf16[28,128,128]{2,1,0:T(8,128)(2,1)}, bf16[28,128,128]{2,1,0:T(8,128)(2,1)S(1)}, u32[]{:S(2)}, u32[]{:S(2)}) collective-permute-start(bf16[28,128,128]{2,1,0:T(8,128)(2,1)} %get-tuple-element.84.refs_14_.refs_2_), channel_id=1, source_target_pairs={{8,16},{9,17},{10,18},{11,19},{12,20},{13,21},{14,22},{15,23},{16,... | collective-permute-start | bytes 2752520 | tf_op jit(solution)/shard_map/ppermute | solution.py:400
  103.3 48.0 %collective-permute-start.13 = (bf16[28,128,128]{2,1,0:T(8,128)(2,1)}, bf16[28,128,128]{2,1,0:T(8,128)(2,1)}, u32[]{:S(2)}, u32[]{:S(2)}) collective-permute-start(bf16[28,128,128]{2,1,0:T(8,128)(2,1)} %get-tuple-element.81.refs_8_), channel_id=1, source_target_pairs={{0,1},{1,0},{2,3},{3,2},{4,5},{5,4},{6,7},{7,6},{8,9},{9,8},{10,11... | collective-permute-start | bytes 2752520 | tf_op jit(solution)/shard_map/ppermute | solution.py:400
  120.7 30.6 %collective-permute-start.14 = (bf16[28,128,128]{2,1,0:T(8,128)(2,1)}, bf16[28,128,128]{2,1,0:T(8,128)(2,1)}, u32[]{:S(2)}, u32[]{:S(2)}) collective-permute-start(bf16[28,128,128]{2,1,0:T(8,128)(2,1)} %collective-permute-done.12.refs_9_), channel_id=1, source_target_pairs={{0,1},{1,0},{2,3},{3,2},{4,5},{5,4},{6,7},{7,6},{8,9},{9,8},{10,11... | collective-permute-start | bytes 2752520 | tf_op jit(solution)/shard_map/ppermute | solution.py:400
  121.3 48.6 %collective-permute-start.16 = (bf16[28,128,128]{2,1,0:T(8,128)(2,1)}, bf16[28,128,128]{2,1,0:T(8,128)(2,1)S(1)}, u32[]{:S(2)}, u32[]{:S(2)}) collective-permute-start(bf16[28,128,128]{2,1,0:T(8,128)(2,1)} %get-tuple-element.90), channel_id=1, source_target_pairs={{8,0},{9,1},{10,2},{11,3},{12,4},{13,5},{14,6},{15,7},{24,8},{25,9... | collective-permute-start | bytes 2752520 | tf_op jit(solution)/shard_map/ppermute | solution.py:400
  124.9 26.4 %copy-start.3 = (bf16[28,128,128]{2,1,0:T(8,128)(2,1)}, bf16[28,128,128]{2,1,0:T(8,128)(2,1)S(1)}, u32[]{:S(2)}) copy-start(bf16[28,128,128]{2,1,0:T(8,128)(2,1)S(1)} %collective-permute-done.15.refs_17_.refs_5_) | copy-start | bytes 2752516
  124.9 51.6 %collective-permute-start.17 = (bf16[28,128,128]{2,1,0:T(8,128)(2,1)}, bf16[28,128,128]{2,1,0:T(8,128)(2,1)S(1)}, u32[]{:S(2)}, u32[]{:S(2)}) collective-permute-start(bf16[28,128,128]{2,1,0:T(8,128)(2,1)} %get-tuple-element.91), channel_id=1, source_target_pairs={{8,0},{9,1},{10,2},{11,3},{12,4},{13,5},{14,6},{15,7},{24,8},{25,9... | collective-permute-start | bytes 2752520 | tf_op jit(solution)/shard_map/ppermute | solution.py:400
  151.3 1.2 copy-start.2
  167.2 28.7 %collective-permute-start.21 = (bf16[28,128,128]{2,1,0:T(8,128)(2,1)}, bf16[28,128,128]{2,1,0:T(8,128)(2,1)S(1)}, u32[]{:S(2)}, u32[]{:S(2)}) collective-permute-start(bf16[28,128,128]{2,1,0:T(8,128)(2,1)} %reorder.3), channel_id=1, source_target_pairs={{8,0},{9,1},{10,2},{11,3},{12,4},{13,5},{14,6},{15,7},{24,8},{25,9... | collective-permute-start | bytes 2752520 | tf_op jit(solution)/shard_map/ppermute | solution.py:400
  168.9 14.9 %collective-permute-start.18 = (bf16[4,128,512]{2,1,0:T(8,128)(2,1)S(1)}, bf16[4,128,512]{2,1,0:T(8,128)(2,1)S(1)}, u32[]{:S(2)}, u32[]{:S(2)}) collective-permute-start(bf16[4,128,512]{2,1,0:T(8,128)(2,1)S(1)} %get-tuple-element.95.refs_6_), channel_id=1, source_target_pairs={{0,2},{1,3},{2,0},{3,1},{4,6},{5,7},{6,4},{7,5},{8,10},{9,11},{10,... | collective-permute-start | bytes 1572872 | tf_op jit(solution)/shard_map/ppermute | solution.py:400
  169.4 23.0 %collective-permute-start.19 = (bf16[4,128,512]{2,1,0:T(8,128)(2,1)S(1)}, bf16[4,128,512]{2,1,0:T(8,128)(2,1)S(1)}, u32[]{:S(2)}, u32[]{:S(2)}) collective-permute-start(bf16[4,128,512]{2,1,0:T(8,128)(2,1)S(1)} %get-tuple-element.96), channel_id=1, source_target_pairs={{0,4},{1,5},{2,6},{3,7},{4,0},{5,1},{6,2},{7,3},{8,12},{9,13},{10,... | collective-permute-start | bytes 1572872 | tf_op jit(solution)/shard_map/ppermute | solution.py:400
  170.0 22.5 %collective-permute-start.20 = (bf16[4,128,512]{2,1,0:T(8,128)(2,1)S(1)}, bf16[4,128,512]{2,1,0:T(8,128)(2,1)S(1)}, u32[]{:S(2)}, u32[]{:S(2)}) collective-permute-start(bf16[4,128,512]{2,1,0:T(8,128)(2,1)S(1)} %get-tuple-element.97), channel_id=1, source_target_pairs={{0,6},{1,7},{2,4},{3,5},{4,2},{5,3},{6,0},{7,1},{8,14},{9,15},{10,... | collective-permute-start | bytes 1572872 | tf_op jit(solution)/shard_map/ppermute | solution.py:400
  192.4 8.1 %collective-permute-start.22 = (bf16[4,128,256]{2,1,0:T(8,128)(2,1)S(1)}, bf16[4,128,256]{2,1,0:T(8,128)(2,1)S(1)}, u32[]{:S(2)}, u32[]{:S(2)}) collective-permute-start(bf16[4,128,256]{2,1,0:T(8,128)(2,1)S(1)} %get-tuple-element.106), channel_id=1, source_target_pairs={{0,2},{1,3},{2,0},{3,1},{4,6},{5,7},{6,4},{7,5},{8,10},{9,11},{10,... | collective-permute-start | bytes 786440 | tf_op jit(solution)/shard_map/ppermute | solution.py:400
  194.0 9.8 %collective-permute-start.23 = (bf16[4,128,256]{2,1,0:T(8,128)(2,1)S(1)}, bf16[4,128,256]{2,1,0:T(8,128)(2,1)S(1)}, u32[]{:S(2)}, u32[]{:S(2)}) collective-permute-start(bf16[4,128,256]{2,1,0:T(8,128)(2,1)S(1)} %get-tuple-element.107), channel_id=1, source_target_pairs={{0,4},{1,5},{2,6},{3,7},{4,0},{5,1},{6,2},{7,3},{8,12},{9,13},{10,... | collective-permute-start | bytes 786440 | tf_op jit(solution)/shard_map/ppermute | solution.py:400
  194.3 10.8 %collective-permute-start.24 = (bf16[4,128,256]{2,1,0:T(8,128)(2,1)S(1)}, bf16[4,128,256]{2,1,0:T(8,128)(2,1)S(1)}, u32[]{:S(2)}, u32[]{:S(2)}) collective-permute-start(bf16[4,128,256]{2,1,0:T(8,128)(2,1)S(1)} %get-tuple-element.108), channel_id=1, source_target_pairs={{0,6},{1,7},{2,4},{3,5},{4,2},{5,3},{6,0},{7,1},{8,14},{9,15},{10,... | collective-permute-start | bytes 786440 | tf_op jit(solution)/shard_map/ppermute | solution.py:400
  205.1 6.7 %collective-permute-start.28 = (bf16[4,128,256]{2,1,0:T(8,128)(2,1)S(1)}, bf16[4,128,256]{2,1,0:T(8,128)(2,1)S(1)}, u32[]{:S(2)}, u32[]{:S(2)}) collective-permute-start(bf16[4,128,256]{2,1,0:T(8,128)(2,1)S(1)} %get-tuple-element.116), channel_id=1, source_target_pairs={{0,2},{1,3},{2,0},{3,1},{4,6},{5,7},{6,4},{7,5},{8,10},{9,11},{10,... | collective-permute-start | bytes 786440 | tf_op jit(solution)/shard_map/ppermute | solution.py:400
  205.6 9.8 %collective-permute-start.29 = (bf16[4,128,256]{2,1,0:T(8,128)(2,1)}, bf16[4,128,256]{2,1,0:T(8,128)(2,1)S(1)}, u32[]{:S(2)}, u32[]{:S(2)}) collective-permute-start(bf16[4,128,256]{2,1,0:T(8,128)(2,1)} %get-tuple-element.117), channel_id=1, source_target_pairs={{0,4},{1,5},{2,6},{3,7},{4,0},{5,1},{6,2},{7,3},{8,12},{9,13},{10,... | collective-permute-start | bytes 786440 | tf_op jit(solution)/shard_map/ppermute | solution.py:400
  206.5 9.0 %collective-permute-start.30 = (bf16[4,128,256]{2,1,0:T(8,128)(2,1)S(1)}, bf16[4,128,256]{2,1,0:T(8,128)(2,1)S(1)}, u32[]{:S(2)}, u32[]{:S(2)}) collective-permute-start(bf16[4,128,256]{2,1,0:T(8,128)(2,1)S(1)} %get-tuple-element.118.refs_3_), channel_id=1, source_target_pairs={{0,6},{1,7},{2,4},{3,5},{4,2},{5,3},{6,0},{7,1},{8,14},{9,15},{10,... | collective-permute-start | bytes 786440 | tf_op jit(solution)/shard_map/ppermute | solution.py:400
  210.5 5.3 %collective-permute-start.25 = (bf16[128,768]{1,0:T(8,128)(2,1)S(1)}, bf16[128,768]{1,0:T(8,128)(2,1)S(1)}, u32[]{:S(2)}, u32[]{:S(2)}) collective-permute-start(bf16[128,768]{1,0:T(8,128)(2,1)S(1)} %get-tuple-element.113), channel_id=1, source_target_pairs={{0,1},{1,0},{2,3},{3,2},{4,5},{5,4},{6,7},{7,6},{8,9},{9,8},{10,11... | collective-permute-start | bytes 589832 | tf_op jit(solution)/shard_map/ppermute | solution.py:400
  210.5 7.8 %collective-permute-start.26 = (bf16[128,768]{1,0:T(8,128)(2,1)S(1)}, bf16[128,768]{1,0:T(8,128)(2,1)S(1)}, u32[]{:S(2)}, u32[]{:S(2)}) collective-permute-start(bf16[128,768]{1,0:T(8,128)(2,1)S(1)} %get-tuple-element.114), channel_id=1, source_target_pairs={{0,8},{1,9},{2,10},{3,11},{4,12},{5,13},{6,14},{7,15},{8,0},{9,1},... | collective-permute-start | bytes 589832 | tf_op jit(solution)/shard_map/ppermute | solution.py:400
  211.8 9.8 %collective-permute-start.27 = (bf16[128,768]{1,0:T(8,128)(2,1)S(1)}, bf16[128,768]{1,0:T(8,128)(2,1)S(1)}, u32[]{:S(2)}, u32[]{:S(2)}) collective-permute-start(bf16[128,768]{1,0:T(8,128)(2,1)S(1)} %get-tuple-element.115), channel_id=1, source_target_pairs={{0,9},{1,8},{2,11},{3,10},{4,13},{5,12},{6,15},{7,14},{8,1},{9,0},... | collective-permute-start | bytes 589832 | tf_op jit(solution)/shard_map/ppermute | solution.py:400
  215.6 6.0 %collective-permute-start.31 = (bf16[128,256]{1,0:T(8,128)(2,1)S(1)}, bf16[128,256]{1,0:T(8,128)(2,1)S(1)}, u32[]{:S(2)}, u32[]{:S(2)}) collective-permute-start(bf16[128,256]{1,0:T(8,128)(2,1)S(1)} %get-tuple-element.120), channel_id=1, source_target_pairs={{0,1},{1,0},{2,3},{3,2},{4,5},{5,4},{6,7},{7,6},{8,9},{9,8},{10,11... | collective-permute-start | bytes 196616 | tf_op jit(solution)/shard_map/ppermute | solution.py:400
  215.7 8.2 %collective-permute-start.32 = (bf16[128,256]{1,0:T(8,128)(2,1)S(1)}, bf16[128,256]{1,0:T(8,128)(2,1)S(1)}, u32[]{:S(2)}, u32[]{:S(2)}) collective-permute-start(bf16[128,256]{1,0:T(8,128)(2,1)S(1)} %get-tuple-element.121), channel_id=1, source_target_pairs={{0,8},{1,9},{2,10},{3,11},{4,12},{5,13},{6,14},{7,15},{8,0},{9,1},... | collective-permute-start | bytes 196616 | tf_op jit(solution)/shard_map/ppermute | solution.py:400
  215.8 8.7 %collective-permute-start.33 = (bf16[128,256]{1,0:T(8,128)(2,1)S(1)}, bf16[128,256]{1,0:T(8,128)(2,1)S(1)}, u32[]{:S(2)}, u32[]{:S(2)}) collective-permute-start(bf16[128,256]{1,0:T(8,128)(2,1)S(1)} %get-tuple-element.122), channel_id=1, source_target_pairs={{0,9},{1,8},{2,11},{3,10},{4,13},{5,12},{6,15},{7,14},{8,1},{9,0},... | collective-permute-start | bytes 196616 | tf_op jit(solution)/shard_map/ppermute | solution.py:400

commit v11 on v10

--- a/solution.py
+++ b/solution.py
@@ -430,10 +430,10 @@
     pair_3 = to_pair(a_3)
     a_12, pair_12, a_3 = lax.optimization_barrier((a_12, pair_12, a_3))
     core_12, core_pair_12 = to_core(a_12), to_core(pair_12)
-    w_3, mid_12, core_12 = lax.optimization_barrier((w_3, mid_12, core_12))
     mid_3 = to_mid(w_3)
-    ordered_1, pair_3 = lax.optimization_barrier((ordered_1, pair_3))
-    ordered_2, mid_3 = lax.optimization_barrier((ordered_2, mid_3))
+    ordered_1, ordered_2, pair_3, mid_3, mid_12 = lax.optimization_barrier(
+        (ordered_1, ordered_2, pair_3, mid_3, mid_12)
+    )
     next_1, next_2 = to_next(ordered_1), to_next(ordered_2)
     core_3, core_pair_3 = to_core(a_3), to_core(pair_3)
 
@@ -470,7 +470,7 @@
 
     rows_stack, *own = stack_product(mid, places, a_blocks, [w_own, w_mid])
     own = totals_of(mid, [w_own, w_mid], ([0],), (own[0],)) + own
-    own[1], got_3 = lax.optimization_barrier((own[1], got_3))
+    own[0], got_3 = lax.optimization_barrier((own[0], got_3))
     (ordered_3,) = reorder(order[2:], got_3, w_12)
     next_3 = to_next(ordered_3)
     own_sums = across_plane(own)

time: 227 us -> 213 us (0.938)
  starting transfers between devices: 65.9 us -> 47.2 us
  waiting for transfers between devices: 107 us -> 112 us
    ppermute x34, starting transfers between devices: 65.9 us -> 47.2 us  [send(): return lax.ppermute(array, 'fsdp', perm=perm)]
    ppermute x34, waiting for transfers between devices: 107 us -> 112 us  [send(): return lax.ppermute(array, 'fsdp', perm=perm)]
  transfers between devices with their start and end apart: 34 -> 34, of which waited for: 19 -> 15; matrix products, arithmetic and copies ran while one was open for 1% -> 1% of each run, Pallas kernels for 18% -> 19%
where the time goes in v11:
time: 213 us
  waiting for transfers between devices  112 us (53%)
  Pallas kernels  48.1 us (23%)
  starting transfers between devices  47.2 us (22%)
  local copies, waits for them, and re-layouts  4.57 us (2%)
    ppermute x34, waiting for transfers between devices, send(): return lax.ppermute(array, 'fsdp', perm=perm)  112 us
    ppermute x34, starting transfers between devices, send(): return lax.ppermute(array, 'fsdp', perm=perm)  47.2 us
    pallas_call x4, Pallas kernels, product(): pl.pallas_call(functools.partial(product_kernel, [places[group] for group...  14.2 us
    pallas_call x1, Pallas kernels, stack_product(): pl.pallas_call(functools.partial(stack_product_kernel, places, a_at, w_at...  10.5 us
    pallas_call x2, Pallas kernels, pack(): pl.pallas_call(functools.partial(pack_kernel, apart, len(steps)), out_sha...  10.4 us
    pallas_call x2, Pallas kernels, reorder(): pl.pallas_call(functools.partial(reorder_kernel, count), out_shape=[pltpu...  8.02 us
  transfers between devices with their start and end apart: 34, of which 15 were waited for; matrix products, arithmetic and copies ran while one was open for 1% of the time, Pallas kernels for 19%

profile of v11, /device:TPU:0, one launch (start us, length us, event | category | flops | bytes accessed | tf_op | source)
XLA Modules:
  0.0 212.6 jit_solution(991043184886389460)
XLA Ops:
  0.0 6.3 %pack.2 = (bf16[28,128,128]{2,1,0:T(8,128)(2,1)}, bf16[28,128,128]{2,1,0:T(8,128)(2,1)}, bf16[2,28,128,128]{3,2,1,0:T(8,128)(2,1)}, bf16[2,28,128,128]{3,2,1,0:T(8,128)(2,1)}) custom-call(s32[1]{0:T(128)} %bitcast.3.plane_ref.choice_ref, bf16[128,14336]{1,0:T(8,128)(2,1)} %refs_0_.3, bf16[128,14336]{1,0:T(8,128)(2,1)} %refs_1_.3, ...), custom_call_target="tpu_custom_call" | custom-call | bytes 13762560 | tf_op jit(solution)/shard_map/pack/pallas_call | solution.py:63
  6.3 3.0 %collective-permute-start.1 = (bf16[2,28,128,128]{3,2,1,0:T(8,128)(2,1)}, bf16[2,28,128,128]{3,2,1,0:T(8,128)(2,1)S(1)}, u32[]{:S(2)}, u32[]{:S(2)}) collective-permute-start(bf16[2,28,128,128]{3,2,1,0:T(8,128)(2,1)} %get-tuple-element.63), channel_id=1, source_target_pairs={{0,2},{1,3},{2,0},{3,1},{4,6},{5,7},{6,4},{7,5},{8,10},{9,11},{10,... | collective-permute-start | bytes 5505032 | tf_op jit(solution)/shard_map/ppermute | solution.py:400
  9.3 1.5 collective-permute-start.2
  10.9 1.6 collective-permute-start
  12.4 2.6 %collective-permute-start.7 = (bf16[28,128,128]{2,1,0:T(8,128)(2,1)}, bf16[28,128,128]{2,1,0:T(8,128)(2,1)S(1)}, u32[]{:S(2)}, u32[]{:S(2)}) collective-permute-start(bf16[28,128,128]{2,1,0:T(8,128)(2,1)} %get-tuple-element.70.refs_12_.refs_0_), channel_id=1, source_target_pairs={{8,0},{9,1},{10,2},{11,3},{12,4},{13,5},{14,6},{15,7},{24,8},{25,9... | collective-permute-start | bytes 2752520 | tf_op jit(solution)/shard_map/ppermute | solution.py:400
  15.0 0.7 collective-permute-start.6
  15.7 18.6 %collective-permute-done.refs_3_.refs_0_.refs_1_ = bf16[28,128,128]{2,1,0:T(8,128)(2,1)S(1)} collective-permute-done((bf16[28,128,128]{2,1,0:T(8,128)(2,1)}, bf16[28,128,128]{2,1,0:T(8,128)(2,1)S(1)}, u32[]{:S(2)}, u32[]{:S(2)}) %collective-permute-start) | collective-permute-done | bytes 917536 | tf_op jit(solution)/shard_map/ppermute | solution.py:400
  34.4 4.1 %pack.3 = bf16[2,28,128,128]{3,2,1,0:T(8,128)(2,1)} custom-call(s32[1]{0:T(128)} %bitcast.3.plane_ref.choice_ref, bf16[128,14336]{1,0:T(8,128)(2,1)} %refs_0_.3, bf16[128,14336]{1,0:T(8,128)(2,1)} %refs_1_.3, bf16[14336,128]{1,0:T(8,128)(2,1)} %refs_2_.3, bf16[28,128,128]{2,1,0:T(8,128)(2,1)S(1)} %collective-permute-done.refs_3_.refs_0_.refs_1_), custom_call_target="tpu_custom_call" | custom-call | bytes 4587520 | tf_op jit(solution)/shard_map/pack/pallas_call | solution.py:63
  38.4 11.1 %collective-permute-done.1.one = bf16[2,28,128,128]{3,2,1,0:T(8,128)(2,1)S(1)} collective-permute-done((bf16[2,28,128,128]{3,2,1,0:T(8,128)(2,1)}, bf16[2,28,128,128]{3,2,1,0:T(8,128)(2,1)S(1)}, u32[]{:S(2)}, u32[]{:S(2)}) %collective-permute-start.1) | collective-permute-done | bytes 1835040 | tf_op jit(solution)/shard_map/ppermute | solution.py:400
  49.6 1.5 collective-permute-done.2.two
  51.0 1.5 collective-permute-start.3
  52.5 2.7 %unpack_pair.1 = (bf16[2,28,128,128]{3,2,1,0:T(8,128)(2,1)}, bf16[2,28,128,128]{3,2,1,0:T(8,128)(2,1)}) custom-call(bf16[2,28,128,128]{3,2,1,0:T(8,128)(2,1)S(1)} %collective-permute-done.1.one, bf16[2,28,128,128]{3,2,1,0:T(8,128)(2,1)S(1)} %collective-permute-done.2.two, bf16[28,128,128]{2,1,0:T(8,128)(2,1)S(1)} %collective-permute-done.refs_3_.refs_0_.refs_1_, ...), custom_call_target="tpu_custom_call" | custom-call | bytes 7340032 | tf_op jit(solution)/shard_map/unpack_pair/pallas_call | solution.py:106
  55.3 4.7 %collective-permute-start.8 = (bf16[2,28,128,128]{3,2,1,0:T(8,128)(2,1)}, bf16[2,28,128,128]{3,2,1,0:T(8,128)(2,1)}, u32[]{:S(2)}, u32[]{:S(2)}) collective-permute-start(bf16[2,28,128,128]{3,2,1,0:T(8,128)(2,1)} %get-tuple-element.75.refs_4_), channel_id=1, source_target_pairs={{0,8},{1,9},{2,10},{3,11},{4,12},{5,13},{6,14},{7,15},{8,0},{9,1},... | collective-permute-start | bytes 5505032 | tf_op jit(solution)/shard_map/ppermute | solution.py:400
  60.5 1.9 collective-permute-start.13
  62.4 0.7 constant_dynamic-slice_fusion
  63.2 0.8 collective-permute-done.4.refs_2_
  64.0 28.8 %collective-permute-done.3.packed = bf16[2,28,128,128]{3,2,1,0:T(8,128)(2,1)} collective-permute-done((bf16[2,28,128,128]{3,2,1,0:T(8,128)(2,1)}, bf16[2,28,128,128]{3,2,1,0:T(8,128)(2,1)}, u32[]{:S(2)}, u32[]{:S(2)}) %collective-permute-start.3) | collective-permute-done | bytes 1835040 | tf_op jit(solution)/shard_map/ppermute | solution.py:400
  92.8 4.4 %reorder.2 = (bf16[28,128,128]{2,1,0:T(8,128)(2,1)}, bf16[28,128,128]{2,1,0:T(8,128)(2,1)}, bf16[28,128,128]{2,1,0:T(8,128)(2,1)}, bf16[28,128,128]{2,1,0:T(8,128)(2,1)}) custom-call(s32[4]{0:T(128)S(1)} %pad_add_fusion.1.order_ref, bf16[2,28,128,128]{3,2,1,0:T(8,128)(2,1)} %collective-permute-done.3.packed, ...), custom_call_target="tpu_custom_call" | custom-call | bytes 7340032 | tf_op jit(solution)/shard_map/reorder/pallas_call | solution.py:144
  97.2 1.6 collective-permute-start.11
  98.9 1.6 collective-permute-start.12
  101.0 16.6 %collective-permute-done.11.refs_9_ = bf16[28,128,128]{2,1,0:T(8,128)(2,1)} collective-permute-done((bf16[28,128,128]{2,1,0:T(8,128)(2,1)}, bf16[28,128,128]{2,1,0:T(8,128)(2,1)}, u32[]{:S(2)}, u32[]{:S(2)}) %collective-permute-start.11) | collective-permute-done | bytes 917536 | tf_op jit(solution)/shard_map/ppermute | solution.py:400
  117.6 0.6 slice.14
  118.2 7.9 %collective-permute-start.16 = (bf16[28,128,128]{2,1,0:T(8,128)(2,1)}, bf16[28,128,128]{2,1,0:T(8,128)(2,1)S(1)}, u32[]{:S(2)}, u32[]{:S(2)}) collective-permute-start(bf16[28,128,128]{2,1,0:T(8,128)(2,1)} %get-tuple-element.87), channel_id=1, source_target_pairs={{8,0},{9,1},{10,2},{11,3},{12,4},{13,5},{14,6},{15,7},{24,8},{25,9... | collective-permute-start | bytes 2752520 | tf_op jit(solution)/shard_map/ppermute | solution.py:400
  126.1 0.9 copy-done.3
  127.0 1.2 copy-done.2
  128.2 1.2 copy-done.4
  129.4 10.5 %stack_product.1 = (bf16[28,2048,128]{2,1,0:T(8,128)(2,1)S(1)}, bf16[4,128,512]{2,1,0:T(8,128)(2,1)S(1)}, bf16[4,128,512]{2,1,0:T(8,128)(2,1)S(1)}, bf16[4,128,512]{2,1,0:T(8,128)(2,1)S(1)}) custom-call(s32[1]{0:T(128)} %bitcast.2.choice_ref, bf16[28,128,128]{2,1,0:T(8,128)(2,1)} %get-tuple-element.62.refs_0_, ...), custom_call_target="tpu_custom_call" | custom-call | flops 5637144576 | bytes 18350080 | tf_op jit(solution)/shard_map/stack_product/pallas_call | solution.py:236
  139.8 4.1 %product.4.refs_3_.refs_0_ = f32[4,128,512]{2,1,0:T(8,128)S(1)} custom-call(s32[1]{0:T(128)} %bitcast.2.choice_ref, bf16[28,2048,128]{2,1,0:T(8,128)(2,1)S(1)} %get-tuple-element.84.a, bf16[28,128,128]{2,1,0:T(8,128)(2,1)} %get-tuple-element.70.refs_12_.refs_0_, bf16[2,28,128,128]{3,2,1,0:T(8,128)(2,1)} %get-tuple-element.73.w_12.refs_13_.refs_1_, ...), custom_call_target="tpu_custom_call" | custom-call | flops 1879048192 | bytes 7340032 | tf_op jit(solution)/shard_map/product/pallas_call | solution.py:305
  143.9 3.6 %reorder.3 = bf16[28,128,128]{2,1,0:T(8,128)(2,1)} custom-call(s32[1]{0:T(128)} %bitcast.5.order_ref, bf16[2,28,128,128]{3,2,1,0:T(8,128)(2,1)} %collective-permute-done.3.packed, bf16[2,28,128,128]{3,2,1,0:T(8,128)(2,1)} %get-tuple-element.73.w_12.refs_13_.refs_1_), custom_call_target="tpu_custom_call" | custom-call | bytes 7340032 | tf_op jit(solution)/shard_map/reorder/pallas_call | solution.py:144
  147.6 2.2 %collective-permute-start.21 = (bf16[28,128,128]{2,1,0:T(8,128)(2,1)}, bf16[28,128,128]{2,1,0:T(8,128)(2,1)S(1)}, u32[]{:S(2)}, u32[]{:S(2)}) collective-permute-start(bf16[28,128,128]{2,1,0:T(8,128)(2,1)} %reorder.3), channel_id=1, source_target_pairs={{8,0},{9,1},{10,2},{11,3},{12,4},{13,5},{14,6},{15,7},{24,8},{25,9... | collective-permute-start | bytes 2752520 | tf_op jit(solution)/shard_map/ppermute | solution.py:400
  150.3 1.5 collective-permute-start.20
  151.8 1.5 collective-permute-start.18
  153.3 13.4 %collective-permute-done.17.refs_2_.refs_0_ = bf16[28,128,128]{2,1,0:T(8,128)(2,1)S(1)} collective-permute-done((bf16[28,128,128]{2,1,0:T(8,128)(2,1)}, bf16[28,128,128]{2,1,0:T(8,128)(2,1)S(1)}, u32[]{:S(2)}, u32[]{:S(2)}) %collective-permute-start.17) | collective-permute-done | bytes 917536 | tf_op jit(solution)/shard_map/ppermute | solution.py:400
  166.7 4.5 %product.5 = (bf16[4,128,256]{2,1,0:T(8,128)(2,1)S(1)}, bf16[4,128,256]{2,1,0:T(8,128)(2,1)S(1)}, bf16[4,128,256]{2,1,0:T(8,128)(2,1)S(1)}, f32[4,128,256]{2,1,0:T(8,128)S(1)}) custom-call(s32[1]{0:T(128)} %bitcast.3.plane_ref.choice_ref, bf16[28,2048,128]{2,1,0:T(8,128)(2,1)S(1)} %get-tuple-element.84.a, ...), custom_call_target="tpu_custom_call" | custom-call | flops 3758096384 | bytes 16515072 | tf_op jit(solution)/shard_map/product/pallas_call | solution.py:305
  171.2 3.3 %collective-permute-done.19.refs_2_ = bf16[4,128,512]{2,1,0:T(8,128)(2,1)S(1)} collective-permute-done((bf16[4,128,512]{2,1,0:T(8,128)(2,1)S(1)}, bf16[4,128,512]{2,1,0:T(8,128)(2,1)S(1)}, u32[]{:S(2)}, u32[]{:S(2)}) %collective-permute-start.19) | collective-permute-done | bytes 524320 | tf_op jit(solution)/shard_map/ppermute | solution.py:400
  174.5 1.2 collective-permute-done.18.refs_1_
  176.8 2.4 %collective-permute-start.24 = (bf16[4,128,256]{2,1,0:T(8,128)(2,1)S(1)}, bf16[4,128,256]{2,1,0:T(8,128)(2,1)S(1)}, u32[]{:S(2)}, u32[]{:S(2)}) collective-permute-start(bf16[4,128,256]{2,1,0:T(8,128)(2,1)S(1)} %get-tuple-element.104), channel_id=1, source_target_pairs={{0,6},{1,7},{2,4},{3,5},{4,2},{5,3},{6,0},{7,1},{8,14},{9,15},{10,... | collective-permute-start | bytes 786440 | tf_op jit(solution)/shard_map/ppermute | solution.py:400
  179.2 6.7 %collective-permute-done.21.refs_1_ = bf16[28,128,128]{2,1,0:T(8,128)(2,1)S(1)} collective-permute-done((bf16[28,128,128]{2,1,0:T(8,128)(2,1)}, bf16[28,128,128]{2,1,0:T(8,128)(2,1)S(1)}, u32[]{:S(2)}, u32[]{:S(2)}) %collective-permute-start.21) | collective-permute-done | bytes 917536 | tf_op jit(solution)/shard_map/ppermute | solution.py:400
  186.0 4.1 %product.6 = (bf16[4,128,256]{2,1,0:T(8,128)(2,1)S(1)}, bf16[4,128,256]{2,1,0:T(8,128)(2,1)S(1)}, bf16[4,128,256]{2,1,0:T(8,128)(2,1)}) custom-call(s32[1]{0:T(128)} %bitcast.3.plane_ref.choice_ref, bf16[28,2048,128]{2,1,0:T(8,128)(2,1)S(1)} %get-tuple-element.84.a, bf16[28,128,128]{2,1,0:T(8,128)(2,1)S(1)} %collective-permute-done.17.refs_2_.refs_0_, ...), custom_call_target="tpu_custom_call" | custom-call | flops 2818572288 | bytes 12845056 | tf_op jit(solution)/shard_map/product/pallas_call | solution.py:305
  191.2 2.5 %collective-permute-start.30 = (bf16[4,128,256]{2,1,0:T(8,128)(2,1)S(1)}, bf16[4,128,256]{2,1,0:T(8,128)(2,1)S(1)}, u32[]{:S(2)}, u32[]{:S(2)}) collective-permute-start(bf16[4,128,256]{2,1,0:T(8,128)(2,1)S(1)} %get-tuple-element.114.refs_3_), channel_id=1, source_target_pairs={{0,6},{1,7},{2,4},{3,5},{4,2},{5,3},{6,0},{7,1},{8,14},{9,15},{10,... | collective-permute-start | bytes 786440 | tf_op jit(solution)/shard_map/ppermute | solution.py:400
  193.7 1.5 product.7.refs_8_.refs_0_
  195.6 2.3 %collective-permute-start.26 = (bf16[128,768]{1,0:T(8,128)(2,1)S(1)}, bf16[128,768]{1,0:T(8,128)(2,1)S(1)}, u32[]{:S(2)}, u32[]{:S(2)}) collective-permute-start(bf16[128,768]{1,0:T(8,128)(2,1)S(1)} %get-tuple-element.110), channel_id=1, source_target_pairs={{0,8},{1,9},{2,10},{3,11},{4,12},{5,13},{6,14},{7,15},{8,0},{9,1},... | collective-permute-start | bytes 589832 | tf_op jit(solution)/shard_map/ppermute | solution.py:400
  197.9 1.4 collective-permute-done.28.refs_1_
  199.4 4.8 %collective-permute-done.29.refs_2_ = bf16[4,128,256]{2,1,0:T(8,128)(2,1)S(1)} collective-permute-done((bf16[4,128,256]{2,1,0:T(8,128)(2,1)}, bf16[4,128,256]{2,1,0:T(8,128)(2,1)S(1)}, u32[]{:S(2)}, u32[]{:S(2)}) %collective-permute-start.29) | collective-permute-done | bytes 262176 | tf_op jit(solution)/shard_map/ppermute | solution.py:400
  204.4 2.3 %collective-permute-start.32 = (bf16[128,256]{1,0:T(8,128)(2,1)S(1)}, bf16[128,256]{1,0:T(8,128)(2,1)S(1)}, u32[]{:S(2)}, u32[]{:S(2)}) collective-permute-start(bf16[128,256]{1,0:T(8,128)(2,1)S(1)} %get-tuple-element.117), channel_id=1, source_target_pairs={{0,8},{1,9},{2,10},{3,11},{4,12},{5,13},{6,14},{7,15},{8,0},{9,1},... | collective-permute-start | bytes 196616 | tf_op jit(solution)/shard_map/ppermute | solution.py:400
  207.4 2.0 collective-permute-done.32.refs_6_
  209.4 1.4 collective-permute-done.33.refs_7_
  210.8 1.8 assemble.1
  (49 shorter events, 5.1 us)
Async XLA Ops:
  6.3 43.2 %collective-permute-start.1 = (bf16[2,28,128,128]{3,2,1,0:T(8,128)(2,1)}, bf16[2,28,128,128]{3,2,1,0:T(8,128)(2,1)S(1)}, u32[]{:S(2)}, u32[]{:S(2)}) collective-permute-start(bf16[2,28,128,128]{3,2,1,0:T(8,128)(2,1)} %get-tuple-element.63), channel_id=1, source_target_pairs={{0,2},{1,3},{2,0},{3,1},{4,6},{5,7},{6,4},{7,5},{8,10},{9,11},{10,... | collective-permute-start | bytes 5505032 | tf_op jit(solution)/shard_map/ppermute | solution.py:400
  9.3 41.7 %collective-permute-start.2 = (bf16[2,28,128,128]{3,2,1,0:T(8,128)(2,1)}, bf16[2,28,128,128]{3,2,1,0:T(8,128)(2,1)S(1)}, u32[]{:S(2)}, u32[]{:S(2)}) collective-permute-start(bf16[2,28,128,128]{3,2,1,0:T(8,128)(2,1)} %get-tuple-element.64), channel_id=1, source_target_pairs={{0,4},{1,5},{2,6},{3,7},{4,0},{5,1},{6,2},{7,3},{8,12},{9,13},{10,... | collective-permute-start | bytes 5505032 | tf_op jit(solution)/shard_map/ppermute | solution.py:400
  10.9 23.5 %collective-permute-start = (bf16[28,128,128]{2,1,0:T(8,128)(2,1)}, bf16[28,128,128]{2,1,0:T(8,128)(2,1)S(1)}, u32[]{:S(2)}, u32[]{:S(2)}) collective-permute-start(bf16[28,128,128]{2,1,0:T(8,128)(2,1)} %get-tuple-element.62.refs_0_), channel_id=1, source_target_pairs={{0,8},{1,9},{2,10},{3,11},{4,12},{5,13},{6,14},{7,15},{8,0},{9,1},... | collective-permute-start | bytes 2752520 | tf_op jit(solution)/shard_map/ppermute | solution.py:400
  12.4 40.1 %collective-permute-start.7 = (bf16[28,128,128]{2,1,0:T(8,128)(2,1)}, bf16[28,128,128]{2,1,0:T(8,128)(2,1)S(1)}, u32[]{:S(2)}, u32[]{:S(2)}) collective-permute-start(bf16[28,128,128]{2,1,0:T(8,128)(2,1)} %get-tuple-element.70.refs_12_.refs_0_), channel_id=1, source_target_pairs={{8,0},{9,1},{10,2},{11,3},{12,4},{13,5},{14,6},{15,7},{24,8},{25,9... | collective-permute-start | bytes 2752520 | tf_op jit(solution)/shard_map/ppermute | solution.py:400
  15.0 37.5 %collective-permute-start.6 = (bf16[28,128,128]{2,1,0:T(8,128)(2,1)}, bf16[28,128,128]{2,1,0:T(8,128)(2,1)S(1)}, u32[]{:S(2)}, u32[]{:S(2)}) collective-permute-start(bf16[28,128,128]{2,1,0:T(8,128)(2,1)} %get-tuple-element.70.refs_12_.refs_0_), channel_id=1, source_target_pairs={{8,16},{9,17},{10,18},{11,19},{12,20},{13,21},{14,22},{15,23},{16,... | collective-permute-start | bytes 2752520 | tf_op jit(solution)/shard_map/ppermute | solution.py:400
  51.0 41.8 %collective-permute-start.3 = (bf16[2,28,128,128]{3,2,1,0:T(8,128)(2,1)}, bf16[2,28,128,128]{3,2,1,0:T(8,128)(2,1)}, u32[]{:S(2)}, u32[]{:S(2)}) collective-permute-start(bf16[2,28,128,128]{3,2,1,0:T(8,128)(2,1)} %pack.3), channel_id=1, source_target_pairs={{0,6},{1,7},{2,4},{3,5},{4,2},{5,3},{6,0},{7,1},{8,14},{9,15},{10,... | collective-permute-start | bytes 5505032 | tf_op jit(solution)/shard_map/ppermute | solution.py:400
  52.5 2.7 %copy-start = (bf16[28,128,128]{2,1,0:T(8,128)(2,1)}, bf16[28,128,128]{2,1,0:T(8,128)(2,1)S(1)}, u32[]{:S(2)}) copy-start(bf16[28,128,128]{2,1,0:T(8,128)(2,1)S(1)} %collective-permute-done.6.refs_1_.refs_15_.refs_3_) | copy-start | bytes 2752516
  55.3 45.2 %collective-permute-start.8 = (bf16[2,28,128,128]{3,2,1,0:T(8,128)(2,1)}, bf16[2,28,128,128]{3,2,1,0:T(8,128)(2,1)}, u32[]{:S(2)}, u32[]{:S(2)}) collective-permute-start(bf16[2,28,128,128]{3,2,1,0:T(8,128)(2,1)} %get-tuple-element.75.refs_4_), channel_id=1, source_target_pairs={{0,8},{1,9},{2,10},{3,11},{4,12},{5,13},{6,14},{7,15},{8,0},{9,1},... | collective-permute-start | bytes 5505032 | tf_op jit(solution)/shard_map/ppermute | solution.py:400
  60.0 4.0 %collective-permute-start.4 = (bf16[28,128,128]{2,1,0:T(8,128)(2,1)}, bf16[28,128,128]{2,1,0:T(8,128)(2,1)S(1)}, u32[]{:S(2)}, u32[]{:S(2)}) collective-permute-start(bf16[28,128,128]{2,1,0:T(8,128)(2,1)} %get-tuple-element.62.refs_0_), channel_id=1, source_target_pairs={{0,1},{1,0},{2,3},{3,2},{4,5},{5,4},{6,7},{7,6},{8,9},{9,8},{10,11... | collective-permute-start | bytes 2752520 | tf_op jit(solution)/shard_map/ppermute | solution.py:400
  60.0 4.0 %collective-permute-start.5 = (bf16[28,128,128]{2,1,0:T(8,128)(2,1)S(1)}, bf16[28,128,128]{2,1,0:T(8,128)(2,1)}, u32[]{:S(2)}, u32[]{:S(2)}) collective-permute-start(bf16[28,128,128]{2,1,0:T(8,128)(2,1)S(1)} %collective-permute-done.refs_3_.refs_0_.refs_1_), channel_id=1, source_target_pairs={{0,1},{1,0},{2,3},{3,2},{4,5},{5,4},{6,7},{7,6},{8,9},{9,8},{10,11... | collective-permute-start | bytes 2752520 | tf_op jit(solution)/shard_map/ppermute | solution.py:400
  60.5 40.5 %collective-permute-start.13 = (bf16[2,28,128,128]{3,2,1,0:T(8,128)(2,1)}, bf16[2,28,128,128]{3,2,1,0:T(8,128)(2,1)}, u32[]{:S(2)}, u32[]{:S(2)}) collective-permute-start(bf16[2,28,128,128]{3,2,1,0:T(8,128)(2,1)} %get-tuple-element.73.w_12.refs_13_.refs_1_), channel_id=1, source_target_pairs={{8,16},{9,17},{10,18},{11,19},{12,20},{13,21},{14,22},{15,23},{16,... | collective-permute-start | bytes 5505032 | tf_op jit(solution)/shard_map/ppermute | solution.py:400
  64.0 33.3 %copy-start.1 = (bf16[28,128,128]{2,1,0:T(8,128)(2,1)}, bf16[28,128,128]{2,1,0:T(8,128)(2,1)S(1)}, u32[]{:S(2)}) copy-start(bf16[28,128,128]{2,1,0:T(8,128)(2,1)S(1)} %collective-permute-done.4.refs_2_) | copy-start | bytes 2752516
  97.2 20.4 %collective-permute-start.11 = (bf16[28,128,128]{2,1,0:T(8,128)(2,1)}, bf16[28,128,128]{2,1,0:T(8,128)(2,1)}, u32[]{:S(2)}, u32[]{:S(2)}) collective-permute-start(bf16[28,128,128]{2,1,0:T(8,128)(2,1)} %get-tuple-element.77.refs_8_), channel_id=1, source_target_pairs={{0,8},{1,9},{2,10},{3,11},{4,12},{5,13},{6,14},{7,15},{8,0},{9,1},... | collective-permute-start | bytes 2752520 | tf_op jit(solution)/shard_map/ppermute | solution.py:400
  98.9 18.7 %collective-permute-start.12 = (bf16[28,128,128]{2,1,0:T(8,128)(2,1)}, bf16[28,128,128]{2,1,0:T(8,128)(2,1)}, u32[]{:S(2)}, u32[]{:S(2)}) collective-permute-start(bf16[28,128,128]{2,1,0:T(8,128)(2,1)} %get-tuple-element.80.refs_14_.refs_2_), channel_id=1, source_target_pairs={{8,16},{9,17},{10,18},{11,19},{12,20},{13,21},{14,22},{15,23},{16,... | collective-permute-start | bytes 2752520 | tf_op jit(solution)/shard_map/ppermute | solution.py:400
  100.5 26.5 %collective-permute-start.9 = (bf16[2,28,128,128]{3,2,1,0:T(8,128)(2,1)}, bf16[2,28,128,128]{3,2,1,0:T(8,128)(2,1)}, u32[]{:S(2)}, u32[]{:S(2)}) collective-permute-start(bf16[2,28,128,128]{3,2,1,0:T(8,128)(2,1)} %get-tuple-element.75.refs_4_), channel_id=1, source_target_pairs={{0,1},{1,0},{2,3},{3,2},{4,5},{5,4},{6,7},{7,6},{8,9},{9,8},{10,11... | collective-permute-start | bytes 5505032 | tf_op jit(solution)/shard_map/ppermute | solution.py:400
  100.5 26.5 %collective-permute-start.10 = (bf16[2,28,128,128]{3,2,1,0:T(8,128)(2,1)}, bf16[2,28,128,128]{3,2,1,0:T(8,128)(2,1)}, u32[]{:S(2)}, u32[]{:S(2)}) collective-permute-start(bf16[2,28,128,128]{3,2,1,0:T(8,128)(2,1)} %collective-permute-done.8.refs_5_), channel_id=1, source_target_pairs={{0,1},{1,0},{2,3},{3,2},{4,5},{5,4},{6,7},{7,6},{8,9},{9,8},{10,11... | collective-permute-start | bytes 5505032 | tf_op jit(solution)/shard_map/ppermute | solution.py:400
  101.0 25.1 %collective-permute-start.14 = (bf16[28,128,128]{2,1,0:T(8,128)(2,1)}, bf16[28,128,128]{2,1,0:T(8,128)(2,1)S(1)}, u32[]{:S(2)}, u32[]{:S(2)}) collective-permute-start(bf16[28,128,128]{2,1,0:T(8,128)(2,1)} %get-tuple-element.77.refs_8_), channel_id=1, source_target_pairs={{0,1},{1,0},{2,3},{3,2},{4,5},{5,4},{6,7},{7,6},{8,9},{9,8},{10,11... | collective-permute-start | bytes 2752520 | tf_op jit(solution)/shard_map/ppermute | solution.py:400
  117.6 9.4 %collective-permute-start.15 = (bf16[28,128,128]{2,1,0:T(8,128)(2,1)}, bf16[28,128,128]{2,1,0:T(8,128)(2,1)}, u32[]{:S(2)}, u32[]{:S(2)}) collective-permute-start(bf16[28,128,128]{2,1,0:T(8,128)(2,1)} %collective-permute-done.11.refs_9_), channel_id=1, source_target_pairs={{0,1},{1,0},{2,3},{3,2},{4,5},{5,4},{6,7},{7,6},{8,9},{9,8},{10,11... | collective-permute-start | bytes 2752520 | tf_op jit(solution)/shard_map/ppermute | solution.py:400
  118.2 33.6 %collective-permute-start.16 = (bf16[28,128,128]{2,1,0:T(8,128)(2,1)}, bf16[28,128,128]{2,1,0:T(8,128)(2,1)S(1)}, u32[]{:S(2)}, u32[]{:S(2)}) collective-permute-start(bf16[28,128,128]{2,1,0:T(8,128)(2,1)} %get-tuple-element.87), channel_id=1, source_target_pairs={{8,0},{9,1},{10,2},{11,3},{12,4},{13,5},{14,6},{15,7},{24,8},{25,9... | collective-permute-start | bytes 2752520 | tf_op jit(solution)/shard_map/ppermute | solution.py:400
  126.1 0.9 copy-start.3
  127.0 39.7 %collective-permute-start.17 = (bf16[28,128,128]{2,1,0:T(8,128)(2,1)}, bf16[28,128,128]{2,1,0:T(8,128)(2,1)S(1)}, u32[]{:S(2)}, u32[]{:S(2)}) collective-permute-start(bf16[28,128,128]{2,1,0:T(8,128)(2,1)} %get-tuple-element.88), channel_id=1, source_target_pairs={{8,0},{9,1},{10,2},{11,3},{12,4},{13,5},{14,6},{15,7},{24,8},{25,9... | collective-permute-start | bytes 2752520 | tf_op jit(solution)/shard_map/ppermute | solution.py:400
  127.0 1.2 copy-start.2
  128.2 1.2 copy-start.4
  147.6 38.4 %collective-permute-start.21 = (bf16[28,128,128]{2,1,0:T(8,128)(2,1)}, bf16[28,128,128]{2,1,0:T(8,128)(2,1)S(1)}, u32[]{:S(2)}, u32[]{:S(2)}) collective-permute-start(bf16[28,128,128]{2,1,0:T(8,128)(2,1)} %reorder.3), channel_id=1, source_target_pairs={{8,0},{9,1},{10,2},{11,3},{12,4},{13,5},{14,6},{15,7},{24,8},{25,9... | collective-permute-start | bytes 2752520 | tf_op jit(solution)/shard_map/ppermute | solution.py:400
  149.8 24.7 %collective-permute-start.19 = (bf16[4,128,512]{2,1,0:T(8,128)(2,1)S(1)}, bf16[4,128,512]{2,1,0:T(8,128)(2,1)S(1)}, u32[]{:S(2)}, u32[]{:S(2)}) collective-permute-start(bf16[4,128,512]{2,1,0:T(8,128)(2,1)S(1)} %get-tuple-element.92), channel_id=1, source_target_pairs={{0,4},{1,5},{2,6},{3,7},{4,0},{5,1},{6,2},{7,3},{8,12},{9,13},{10,... | collective-permute-start | bytes 1572872 | tf_op jit(solution)/shard_map/ppermute | solution.py:400
  150.3 24.2 %collective-permute-start.20 = (bf16[4,128,512]{2,1,0:T(8,128)(2,1)S(1)}, bf16[4,128,512]{2,1,0:T(8,128)(2,1)S(1)}, u32[]{:S(2)}, u32[]{:S(2)}) collective-permute-start(bf16[4,128,512]{2,1,0:T(8,128)(2,1)S(1)} %get-tuple-element.93), channel_id=1, source_target_pairs={{0,6},{1,7},{2,4},{3,5},{4,2},{5,3},{6,0},{7,1},{8,14},{9,15},{10,... | collective-permute-start | bytes 1572872 | tf_op jit(solution)/shard_map/ppermute | solution.py:400
  151.8 24.0 %collective-permute-start.18 = (bf16[4,128,512]{2,1,0:T(8,128)(2,1)S(1)}, bf16[4,128,512]{2,1,0:T(8,128)(2,1)S(1)}, u32[]{:S(2)}, u32[]{:S(2)}) collective-permute-start(bf16[4,128,512]{2,1,0:T(8,128)(2,1)S(1)} %get-tuple-element.85.refs_6_), channel_id=1, source_target_pairs={{0,2},{1,3},{2,0},{3,1},{4,6},{5,7},{6,4},{7,5},{8,10},{9,11},{10,... | collective-permute-start | bytes 1572872 | tf_op jit(solution)/shard_map/ppermute | solution.py:400
  175.7 14.3 %collective-permute-start.22 = (bf16[4,128,256]{2,1,0:T(8,128)(2,1)S(1)}, bf16[4,128,256]{2,1,0:T(8,128)(2,1)S(1)}, u32[]{:S(2)}, u32[]{:S(2)}) collective-permute-start(bf16[4,128,256]{2,1,0:T(8,128)(2,1)S(1)} %get-tuple-element.102), channel_id=1, source_target_pairs={{0,2},{1,3},{2,0},{3,1},{4,6},{5,7},{6,4},{7,5},{8,10},{9,11},{10,... | collective-permute-start | bytes 786440 | tf_op jit(solution)/shard_map/ppermute | solution.py:400
  176.3 13.8 %collective-permute-start.23 = (bf16[4,128,256]{2,1,0:T(8,128)(2,1)S(1)}, bf16[4,128,256]{2,1,0:T(8,128)(2,1)S(1)}, u32[]{:S(2)}, u32[]{:S(2)}) collective-permute-start(bf16[4,128,256]{2,1,0:T(8,128)(2,1)S(1)} %get-tuple-element.103), channel_id=1, source_target_pairs={{0,4},{1,5},{2,6},{3,7},{4,0},{5,1},{6,2},{7,3},{8,12},{9,13},{10,... | collective-permute-start | bytes 786440 | tf_op jit(solution)/shard_map/ppermute | solution.py:400
  176.8 13.3 %collective-permute-start.24 = (bf16[4,128,256]{2,1,0:T(8,128)(2,1)S(1)}, bf16[4,128,256]{2,1,0:T(8,128)(2,1)S(1)}, u32[]{:S(2)}, u32[]{:S(2)}) collective-permute-start(bf16[4,128,256]{2,1,0:T(8,128)(2,1)S(1)} %get-tuple-element.104), channel_id=1, source_target_pairs={{0,6},{1,7},{2,4},{3,5},{4,2},{5,3},{6,0},{7,1},{8,14},{9,15},{10,... | collective-permute-start | bytes 786440 | tf_op jit(solution)/shard_map/ppermute | solution.py:400
  190.1 9.3 %collective-permute-start.28 = (bf16[4,128,256]{2,1,0:T(8,128)(2,1)S(1)}, bf16[4,128,256]{2,1,0:T(8,128)(2,1)S(1)}, u32[]{:S(2)}, u32[]{:S(2)}) collective-permute-start(bf16[4,128,256]{2,1,0:T(8,128)(2,1)S(1)} %get-tuple-element.112), channel_id=1, source_target_pairs={{0,2},{1,3},{2,0},{3,1},{4,6},{5,7},{6,4},{7,5},{8,10},{9,11},{10,... | collective-permute-start | bytes 786440 | tf_op jit(solution)/shard_map/ppermute | solution.py:400
  190.7 13.5 %collective-permute-start.29 = (bf16[4,128,256]{2,1,0:T(8,128)(2,1)}, bf16[4,128,256]{2,1,0:T(8,128)(2,1)S(1)}, u32[]{:S(2)}, u32[]{:S(2)}) collective-permute-start(bf16[4,128,256]{2,1,0:T(8,128)(2,1)} %get-tuple-element.113), channel_id=1, source_target_pairs={{0,4},{1,5},{2,6},{3,7},{4,0},{5,1},{6,2},{7,3},{8,12},{9,13},{10,... | collective-permute-start | bytes 786440 | tf_op jit(solution)/shard_map/ppermute | solution.py:400
  191.2 13.0 %collective-permute-start.30 = (bf16[4,128,256]{2,1,0:T(8,128)(2,1)S(1)}, bf16[4,128,256]{2,1,0:T(8,128)(2,1)S(1)}, u32[]{:S(2)}, u32[]{:S(2)}) collective-permute-start(bf16[4,128,256]{2,1,0:T(8,128)(2,1)S(1)} %get-tuple-element.114.refs_3_), channel_id=1, source_target_pairs={{0,6},{1,7},{2,4},{3,5},{4,2},{5,3},{6,0},{7,1},{8,14},{9,15},{10,... | collective-permute-start | bytes 786440 | tf_op jit(solution)/shard_map/ppermute | solution.py:400
  195.5 11.2 %collective-permute-start.25 = (bf16[128,768]{1,0:T(8,128)(2,1)S(1)}, bf16[128,768]{1,0:T(8,128)(2,1)S(1)}, u32[]{:S(2)}, u32[]{:S(2)}) collective-permute-start(bf16[128,768]{1,0:T(8,128)(2,1)S(1)} %get-tuple-element.109), channel_id=1, source_target_pairs={{0,1},{1,0},{2,3},{3,2},{4,5},{5,4},{6,7},{7,6},{8,9},{9,8},{10,11... | collective-permute-start | bytes 589832 | tf_op jit(solution)/shard_map/ppermute | solution.py:400
  195.6 11.3 %collective-permute-start.26 = (bf16[128,768]{1,0:T(8,128)(2,1)S(1)}, bf16[128,768]{1,0:T(8,128)(2,1)S(1)}, u32[]{:S(2)}, u32[]{:S(2)}) collective-permute-start(bf16[128,768]{1,0:T(8,128)(2,1)S(1)} %get-tuple-element.110), channel_id=1, source_target_pairs={{0,8},{1,9},{2,10},{3,11},{4,12},{5,13},{6,14},{7,15},{8,0},{9,1},... | collective-permute-start | bytes 589832 | tf_op jit(solution)/shard_map/ppermute | solution.py:400
  199.4 8.0 %collective-permute-start.27 = (bf16[128,768]{1,0:T(8,128)(2,1)S(1)}, bf16[128,768]{1,0:T(8,128)(2,1)S(1)}, u32[]{:S(2)}, u32[]{:S(2)}) collective-permute-start(bf16[128,768]{1,0:T(8,128)(2,1)S(1)} %get-tuple-element.111), channel_id=1, source_target_pairs={{0,9},{1,8},{2,11},{3,10},{4,13},{5,12},{6,15},{7,14},{8,1},{9,0},... | collective-permute-start | bytes 589832 | tf_op jit(solution)/shard_map/ppermute | solution.py:400
  204.3 3.1 %collective-permute-start.31 = (bf16[128,256]{1,0:T(8,128)(2,1)S(1)}, bf16[128,256]{1,0:T(8,128)(2,1)S(1)}, u32[]{:S(2)}, u32[]{:S(2)}) collective-permute-start(bf16[128,256]{1,0:T(8,128)(2,1)S(1)} %get-tuple-element.116), channel_id=1, source_target_pairs={{0,1},{1,0},{2,3},{3,2},{4,5},{5,4},{6,7},{7,6},{8,9},{9,8},{10,11... | collective-permute-start | bytes 196616 | tf_op jit(solution)/shard_map/ppermute | solution.py:400
  204.4 5.0 %collective-permute-start.32 = (bf16[128,256]{1,0:T(8,128)(2,1)S(1)}, bf16[128,256]{1,0:T(8,128)(2,1)S(1)}, u32[]{:S(2)}, u32[]{:S(2)}) collective-permute-start(bf16[128,256]{1,0:T(8,128)(2,1)S(1)} %get-tuple-element.117), channel_id=1, source_target_pairs={{0,8},{1,9},{2,10},{3,11},{4,12},{5,13},{6,14},{7,15},{8,0},{9,1},... | collective-permute-start | bytes 196616 | tf_op jit(solution)/shard_map/ppermute | solution.py:400
  206.7 4.0 %collective-permute-start.33 = (bf16[128,256]{1,0:T(8,128)(2,1)S(1)}, bf16[128,256]{1,0:T(8,128)(2,1)S(1)}, u32[]{:S(2)}, u32[]{:S(2)}) collective-permute-start(bf16[128,256]{1,0:T(8,128)(2,1)S(1)} %get-tuple-element.118), channel_id=1, source_target_pairs={{0,9},{1,8},{2,11},{3,10},{4,13},{5,12},{6,15},{7,14},{8,1},{9,0},... | collective-permute-start | bytes 196616 | tf_op jit(solution)/shard_map/ppermute | solution.py:400

commit v12 on v11

--- a/solution.py
+++ b/solution.py
@@ -44,7 +44,7 @@
     share = tiles // grid
     apart = int(steps[0] == 0)
     single = pltpu.HBM((tiles, rows, LANES), jnp.bfloat16)
-    double = pltpu.HBM((2, tiles, rows, LANES), jnp.bfloat16)
+    double = jax.ShapeDtypeStruct((2, tiles, rows, LANES), jnp.bfloat16)
     single_spec = pl.BlockSpec((share, rows, LANES), lambda at, plane: (at, 0, 0))
     double_spec = pl.BlockSpec((2, share, rows, LANES), lambda at, plane: (0, at, 0, 0))
     others = len(steps) - apart
@@ -419,8 +419,9 @@
     (packed_3,) = pack(at_plane, (3,), *inputs, after=(pair_0,))
     packed_3, got_1, got_2 = lax.optimization_barrier((packed_3, got_1, got_2))
     got_3 = send(packed_3, flip(n, 3 * PLANE))
-    a_12, w_12 = unpack_pair(got_1, got_2, after=(pair_0, mid_0, next_0))
+    a_12, w_12 = unpack_pair(got_1, got_2, after=(pair_0,))
     pair_12, mid_12 = to_pair(a_12), to_mid(w_12)
+    pair_0, mid_0, next_0 = lax.optimization_barrier((pair_0, mid_0, next_0))
     core_0, core_pair_0 = to_core(a_0), to_core(pair_0)
 
     order = jnp.array([[1, 2, 3], [1, 3, 2], [2, 3, 1], [3, 2, 1]], jnp.int32)[plane]
@@ -470,7 +471,7 @@
 
     rows_stack, *own = stack_product(mid, places, a_blocks, [w_own, w_mid])
     own = totals_of(mid, [w_own, w_mid], ([0],), (own[0],)) + own
-    own[0], got_3 = lax.optimization_barrier((own[0], got_3))
+    own[1], got_3 = lax.optimization_barrier((own[1], got_3))
     (ordered_3,) = reorder(order[2:], got_3, w_12)
     next_3 = to_next(ordered_3)
     own_sums = across_plane(own)

time: 213 us -> 210 us (0.986)
  waiting for transfers between devices: 112 us -> 116 us
  local copies, waits for them, and re-layouts: 4.57 us -> 1.26 us
  starting transfers between devices: 47.2 us -> 44.1 us
    ppermute x34, waiting for transfers between devices: 112 us -> 116 us  [send(): return lax.ppermute(array, 'fsdp', perm=perm)]
    unnamed x10 -> x0, local copies, waits for them, and re-layouts: 3.27 us -> none
    ppermute x34, starting transfers between devices: 47.2 us -> 44.1 us  [send(): return lax.ppermute(array, 'fsdp', perm=perm)]
  transfers between devices with their start and end apart: 34 -> 34, of which waited for: 15 -> 13; matrix products, arithmetic and copies ran while one was open for 1% -> 1% of each run, Pallas kernels for 19% -> 19%
where the time goes in v12:
time: 210 us
  waiting for transfers between devices  116 us (55%)
  Pallas kernels  48 us (23%)
  starting transfers between devices  44.1 us (21%)
    ppermute x34, waiting for transfers between devices, send(): return lax.ppermute(array, 'fsdp', perm=perm)  116 us
    ppermute x34, starting transfers between devices, send(): return lax.ppermute(array, 'fsdp', perm=perm)  44.1 us
    pallas_call x4, Pallas kernels, product(): pl.pallas_call(functools.partial(product_kernel, [places[group] for group...  14.5 us
    pallas_call x1, Pallas kernels, stack_product(): pl.pallas_call(functools.partial(stack_product_kernel, places, a_at, w_at...  11 us
    pallas_call x2, Pallas kernels, pack(): pl.pallas_call(functools.partial(pack_kernel, apart, len(steps)), out_sha...  9.54 us
    pallas_call x2, Pallas kernels, reorder(): pl.pallas_call(functools.partial(reorder_kernel, count), out_shape=[pltpu...  7.97 us
  transfers between devices with their start and end apart: 34, of which 13 were waited for; matrix products, arithmetic and copies ran while one was open for 1% of the time, Pallas kernels for 19%

profile of v12, /device:TPU:0, one launch (start us, length us, event | category | flops | bytes accessed | tf_op | source)
XLA Modules:
  0.0 209.9 jit_solution(5494965570753225492)
XLA Ops:
  0.0 5.4 %pack.2 = (bf16[28,128,128]{2,1,0:T(8,128)(2,1)}, bf16[28,128,128]{2,1,0:T(8,128)(2,1)}, bf16[2,28,128,128]{3,2,1,0:T(8,128)(2,1)S(1)}, bf16[2,28,128,128]{3,2,1,0:T(8,128)(2,1)S(1)}) custom-call(s32[1]{0:T(128)} %bitcast.3.plane_ref.choice_ref, bf16[128,14336]{1,0:T(8,128)(2,1)} %refs_0_.3, bf16[128,14336]{1,0:T(8,128)(2,1)} %refs_1_.3, ...), custom_call_target="tpu_custom_call" | custom-call | bytes 13762560 | tf_op jit(solution)/shard_map/pack/pallas_call | solution.py:63
  5.4 3.0 %collective-permute-start.3 = (bf16[2,28,128,128]{3,2,1,0:T(8,128)(2,1)S(1)}, bf16[2,28,128,128]{3,2,1,0:T(8,128)(2,1)S(1)}, u32[]{:S(2)}, u32[]{:S(2)}) collective-permute-start(bf16[2,28,128,128]{3,2,1,0:T(8,128)(2,1)S(1)} %get-tuple-element.68), channel_id=1, source_target_pairs={{0,2},{1,3},{2,0},{3,1},{4,6},{5,7},{6,4},{7,5},{8,10},{9,11},{10,... | collective-permute-start | bytes 5505032 | tf_op jit(solution)/shard_map/ppermute | solution.py:400
  8.4 1.5 collective-permute-start.4
  9.9 1.6 collective-permute-start
  11.5 2.6 %collective-permute-start.2 = (bf16[28,128,128]{2,1,0:T(8,128)(2,1)}, bf16[28,128,128]{2,1,0:T(8,128)(2,1)S(1)}, u32[]{:S(2)}, u32[]{:S(2)}) collective-permute-start(bf16[28,128,128]{2,1,0:T(8,128)(2,1)} %get-tuple-element.66.refs_12_.refs_0_), channel_id=1, source_target_pairs={{8,0},{9,1},{10,2},{11,3},{12,4},{13,5},{14,6},{15,7},{24,8},{25,9... | collective-permute-start | bytes 2752520 | tf_op jit(solution)/shard_map/ppermute | solution.py:400
  14.1 1.6 collective-permute-start.1
  15.7 17.7 %collective-permute-done.refs_3_.refs_0_.refs_1_ = bf16[28,128,128]{2,1,0:T(8,128)(2,1)S(1)} collective-permute-done((bf16[28,128,128]{2,1,0:T(8,128)(2,1)}, bf16[28,128,128]{2,1,0:T(8,128)(2,1)S(1)}, u32[]{:S(2)}, u32[]{:S(2)}) %collective-permute-start) | collective-permute-done | bytes 917536 | tf_op jit(solution)/shard_map/ppermute | solution.py:400
  33.4 4.1 %pack.3 = bf16[2,28,128,128]{3,2,1,0:T(8,128)(2,1)} custom-call(s32[1]{0:T(128)} %bitcast.3.plane_ref.choice_ref, bf16[128,14336]{1,0:T(8,128)(2,1)} %refs_0_.3, bf16[128,14336]{1,0:T(8,128)(2,1)} %refs_1_.3, bf16[14336,128]{1,0:T(8,128)(2,1)} %refs_2_.3, bf16[28,128,128]{2,1,0:T(8,128)(2,1)S(1)} %collective-permute-done.refs_3_.refs_0_.refs_1_), custom_call_target="tpu_custom_call" | custom-call | bytes 4587520 | tf_op jit(solution)/shard_map/pack/pallas_call | solution.py:63
  37.6 10.9 %collective-permute-done.3.one = bf16[2,28,128,128]{3,2,1,0:T(8,128)(2,1)S(1)} collective-permute-done((bf16[2,28,128,128]{3,2,1,0:T(8,128)(2,1)S(1)}, bf16[2,28,128,128]{3,2,1,0:T(8,128)(2,1)S(1)}, u32[]{:S(2)}, u32[]{:S(2)}) %collective-permute-start.3) | collective-permute-done | bytes 1835040 | tf_op jit(solution)/shard_map/ppermute | solution.py:400
  48.4 1.5 collective-permute-done.4.two
  49.9 1.5 collective-permute-start.5
  51.4 2.8 %unpack_pair.1 = (bf16[2,28,128,128]{3,2,1,0:T(8,128)(2,1)}, bf16[2,28,128,128]{3,2,1,0:T(8,128)(2,1)}) custom-call(bf16[2,28,128,128]{3,2,1,0:T(8,128)(2,1)S(1)} %collective-permute-done.3.one, bf16[2,28,128,128]{3,2,1,0:T(8,128)(2,1)S(1)} %collective-permute-done.4.two, bf16[28,128,128]{2,1,0:T(8,128)(2,1)S(1)} %collective-permute-done.refs_3_.refs_0_.refs_1_), custom_call_target="tpu_custom_call" | custom-call | bytes 7340032 | tf_op jit(solution)/shard_map/unpack_pair/pallas_call | solution.py:106
  54.2 1.6 collective-permute-start.8
  56.3 1.9 collective-permute-start.13
  58.2 0.7 constant_dynamic-slice_fusion
  59.1 0.7 collective-permute-done.7.refs_3_
  59.7 31.9 %collective-permute-done.5.packed = bf16[2,28,128,128]{3,2,1,0:T(8,128)(2,1)} collective-permute-done((bf16[2,28,128,128]{3,2,1,0:T(8,128)(2,1)}, bf16[2,28,128,128]{3,2,1,0:T(8,128)(2,1)}, u32[]{:S(2)}, u32[]{:S(2)}) %collective-permute-start.5) | collective-permute-done | bytes 1835040 | tf_op jit(solution)/shard_map/ppermute | solution.py:400
  91.7 4.4 %reorder.2 = (bf16[28,128,128]{2,1,0:T(8,128)(2,1)}, bf16[28,128,128]{2,1,0:T(8,128)(2,1)}, bf16[28,128,128]{2,1,0:T(8,128)(2,1)}, bf16[28,128,128]{2,1,0:T(8,128)(2,1)}) custom-call(s32[4]{0:T(128)S(1)} %pad_add_fusion.1.order_ref, bf16[2,28,128,128]{3,2,1,0:T(8,128)(2,1)} %collective-permute-done.5.packed, ...), custom_call_target="tpu_custom_call" | custom-call | bytes 7340032 | tf_op jit(solution)/shard_map/reorder/pallas_call | solution.py:144
  96.1 1.7 collective-permute-start.11
  97.9 1.6 collective-permute-start.12
  99.5 0.5 collective-permute-start.10
  100.0 16.5 %collective-permute-done.11.refs_9_ = bf16[28,128,128]{2,1,0:T(8,128)(2,1)} collective-permute-done((bf16[28,128,128]{2,1,0:T(8,128)(2,1)}, bf16[28,128,128]{2,1,0:T(8,128)(2,1)}, u32[]{:S(2)}, u32[]{:S(2)}) %collective-permute-start.11) | collective-permute-done | bytes 917536 | tf_op jit(solution)/shard_map/ppermute | solution.py:400
  116.5 0.6 slice.14
  117.1 6.3 %collective-permute-start.16 = (bf16[28,128,128]{2,1,0:T(8,128)(2,1)}, bf16[28,128,128]{2,1,0:T(8,128)(2,1)}, u32[]{:S(2)}, u32[]{:S(2)}) collective-permute-start(bf16[28,128,128]{2,1,0:T(8,128)(2,1)} %get-tuple-element.92), channel_id=1, source_target_pairs={{8,0},{9,1},{10,2},{11,3},{12,4},{13,5},{14,6},{15,7},{24,8},{25,9... | collective-permute-start | bytes 2752520 | tf_op jit(solution)/shard_map/ppermute | solution.py:400
  123.4 11.0 %stack_product.1 = (bf16[28,2048,128]{2,1,0:T(8,128)(2,1)S(1)}, bf16[4,128,512]{2,1,0:T(8,128)(2,1)S(1)}, bf16[4,128,512]{2,1,0:T(8,128)(2,1)S(1)}, bf16[4,128,512]{2,1,0:T(8,128)(2,1)S(1)}) custom-call(s32[1]{0:T(128)} %bitcast.2.choice_ref, bf16[28,128,128]{2,1,0:T(8,128)(2,1)} %get-tuple-element.65.refs_0_, ...), custom_call_target="tpu_custom_call" | custom-call | flops 5637144576 | bytes 18350080 | tf_op jit(solution)/shard_map/stack_product/pallas_call | solution.py:236
  134.4 3.5 %reorder.3 = bf16[28,128,128]{2,1,0:T(8,128)(2,1)} custom-call(s32[1]{0:T(128)} %bitcast.5.order_ref, bf16[2,28,128,128]{3,2,1,0:T(8,128)(2,1)} %collective-permute-done.5.packed, bf16[2,28,128,128]{3,2,1,0:T(8,128)(2,1)} %get-tuple-element.77.w_12.refs_13_.refs_1_), custom_call_target="tpu_custom_call" | custom-call | bytes 7340032 | tf_op jit(solution)/shard_map/reorder/pallas_call | solution.py:144
  138.0 3.0 %collective-permute-start.21 = (bf16[28,128,128]{2,1,0:T(8,128)(2,1)}, bf16[28,128,128]{2,1,0:T(8,128)(2,1)S(1)}, u32[]{:S(2)}, u32[]{:S(2)}) collective-permute-start(bf16[28,128,128]{2,1,0:T(8,128)(2,1)} %reorder.3), channel_id=1, source_target_pairs={{8,0},{9,1},{10,2},{11,3},{12,4},{13,5},{14,6},{15,7},{24,8},{25,9... | collective-permute-start | bytes 2752520 | tf_op jit(solution)/shard_map/ppermute | solution.py:400
  141.0 1.5 collective-permute-start.18
  142.5 0.5 collective-permute-start.19
  143.0 1.3 collective-permute-done.16.refs_1_
  144.3 1.4 collective-permute-start.20
  145.8 4.1 %product.4.refs_3_.refs_0_ = f32[4,128,512]{2,1,0:T(8,128)S(1)} custom-call(s32[1]{0:T(128)} %bitcast.2.choice_ref, bf16[28,2048,128]{2,1,0:T(8,128)(2,1)S(1)} %get-tuple-element.89.a, bf16[28,128,128]{2,1,0:T(8,128)(2,1)} %get-tuple-element.66.refs_12_.refs_0_, bf16[2,28,128,128]{3,2,1,0:T(8,128)(2,1)} %get-tuple-element.77.w_12.refs_13_.refs_1_, ...), custom_call_target="tpu_custom_call" | custom-call | flops 1879048192 | bytes 7340032 | tf_op jit(solution)/shard_map/product/pallas_call | solution.py:305
  149.9 14.1 %collective-permute-done.17.refs_2_.refs_0_ = bf16[28,128,128]{2,1,0:T(8,128)(2,1)S(1)} collective-permute-done((bf16[28,128,128]{2,1,0:T(8,128)(2,1)}, bf16[28,128,128]{2,1,0:T(8,128)(2,1)S(1)}, u32[]{:S(2)}, u32[]{:S(2)}) %collective-permute-start.17) | collective-permute-done | bytes 917536 | tf_op jit(solution)/shard_map/ppermute | solution.py:400
  164.0 5.3 %product.5 = (bf16[4,128,256]{2,1,0:T(8,128)(2,1)S(1)}, bf16[4,128,256]{2,1,0:T(8,128)(2,1)S(1)}, bf16[4,128,256]{2,1,0:T(8,128)(2,1)S(1)}, f32[4,128,256]{2,1,0:T(8,128)S(1)}) custom-call(s32[1]{0:T(128)} %bitcast.3.plane_ref.choice_ref, bf16[28,2048,128]{2,1,0:T(8,128)(2,1)S(1)} %get-tuple-element.89.a, ...), custom_call_target="tpu_custom_call" | custom-call | flops 3758096384 | bytes 16515072 | tf_op jit(solution)/shard_map/product/pallas_call | solution.py:305
  169.3 1.4 collective-permute-start.22
  171.2 1.6 collective-permute-start.24
  172.9 10.4 %collective-permute-done.21.refs_1_ = bf16[28,128,128]{2,1,0:T(8,128)(2,1)S(1)} collective-permute-done((bf16[28,128,128]{2,1,0:T(8,128)(2,1)}, bf16[28,128,128]{2,1,0:T(8,128)(2,1)S(1)}, u32[]{:S(2)}, u32[]{:S(2)}) %collective-permute-start.21) | collective-permute-done | bytes 917536 | tf_op jit(solution)/shard_map/ppermute | solution.py:400
  183.3 3.6 %product.6 = (bf16[4,128,256]{2,1,0:T(8,128)(2,1)S(1)}, bf16[4,128,256]{2,1,0:T(8,128)(2,1)S(1)}, bf16[4,128,256]{2,1,0:T(8,128)(2,1)S(1)}) custom-call(s32[1]{0:T(128)} %bitcast.3.plane_ref.choice_ref, bf16[28,2048,128]{2,1,0:T(8,128)(2,1)S(1)} %get-tuple-element.89.a, bf16[28,128,128]{2,1,0:T(8,128)(2,1)S(1)} %collective-permute-done.17.refs_2_.refs_0_, ...), custom_call_target="tpu_custom_call" | custom-call | flops 2818572288 | bytes 12845056 | tf_op jit(solution)/shard_map/product/pallas_call | solution.py:305
  186.9 1.5 collective-permute-start.28
  188.7 1.7 collective-permute-start.30
  190.4 1.5 product.7.refs_8_.refs_0_
  192.4 2.2 %collective-permute-start.26 = (bf16[128,768]{1,0:T(8,128)(2,1)S(1)}, bf16[128,768]{1,0:T(8,128)(2,1)S(1)}, u32[]{:S(2)}, u32[]{:S(2)}) collective-permute-start(bf16[128,768]{1,0:T(8,128)(2,1)S(1)} %get-tuple-element.116), channel_id=1, source_target_pairs={{0,8},{1,9},{2,10},{3,11},{4,12},{5,13},{6,14},{7,15},{8,0},{9,1},... | collective-permute-start | bytes 589832 | tf_op jit(solution)/shard_map/ppermute | solution.py:400
  194.6 1.6 collective-permute-done.28.refs_1_
  196.2 5.5 %collective-permute-done.29.refs_2_ = bf16[4,128,256]{2,1,0:T(8,128)(2,1)S(1)} collective-permute-done((bf16[4,128,256]{2,1,0:T(8,128)(2,1)S(1)}, bf16[4,128,256]{2,1,0:T(8,128)(2,1)S(1)}, u32[]{:S(2)}, u32[]{:S(2)}) %collective-permute-start.29) | collective-permute-done | bytes 262176 | tf_op jit(solution)/shard_map/ppermute | solution.py:400
  201.9 2.2 %collective-permute-start.32 = (bf16[128,256]{1,0:T(8,128)(2,1)S(1)}, bf16[128,256]{1,0:T(8,128)(2,1)S(1)}, u32[]{:S(2)}, u32[]{:S(2)}) collective-permute-start(bf16[128,256]{1,0:T(8,128)(2,1)S(1)} %get-tuple-element.123), channel_id=1, source_target_pairs={{0,8},{1,9},{2,10},{3,11},{4,12},{5,13},{6,14},{7,15},{8,0},{9,1},... | collective-permute-start | bytes 196616 | tf_op jit(solution)/shard_map/ppermute | solution.py:400
  204.2 2.5 %collective-permute-done.32.refs_6_ = bf16[128,256]{1,0:T(8,128)(2,1)S(1)} collective-permute-done((bf16[128,256]{1,0:T(8,128)(2,1)S(1)}, bf16[128,256]{1,0:T(8,128)(2,1)S(1)}, u32[]{:S(2)}, u32[]{:S(2)}) %collective-permute-start.32) | collective-permute-done | bytes 65568 | tf_op jit(solution)/shard_map/ppermute | solution.py:400
  206.8 1.4 collective-permute-done.33.refs_7_
  208.1 1.8 assemble.1
  (39 shorter events, 2.3 us)
Async XLA Ops:
  5.4 43.0 %collective-permute-start.3 = (bf16[2,28,128,128]{3,2,1,0:T(8,128)(2,1)S(1)}, bf16[2,28,128,128]{3,2,1,0:T(8,128)(2,1)S(1)}, u32[]{:S(2)}, u32[]{:S(2)}) collective-permute-start(bf16[2,28,128,128]{3,2,1,0:T(8,128)(2,1)S(1)} %get-tuple-element.68), channel_id=1, source_target_pairs={{0,2},{1,3},{2,0},{3,1},{4,6},{5,7},{6,4},{7,5},{8,10},{9,11},{10,... | collective-permute-start | bytes 5505032 | tf_op jit(solution)/shard_map/ppermute | solution.py:400
  8.4 41.5 %collective-permute-start.4 = (bf16[2,28,128,128]{3,2,1,0:T(8,128)(2,1)S(1)}, bf16[2,28,128,128]{3,2,1,0:T(8,128)(2,1)S(1)}, u32[]{:S(2)}, u32[]{:S(2)}) collective-permute-start(bf16[2,28,128,128]{3,2,1,0:T(8,128)(2,1)S(1)} %get-tuple-element.69), channel_id=1, source_target_pairs={{0,4},{1,5},{2,6},{3,7},{4,0},{5,1},{6,2},{7,3},{8,12},{9,13},{10,... | collective-permute-start | bytes 5505032 | tf_op jit(solution)/shard_map/ppermute | solution.py:400
  9.9 23.5 %collective-permute-start = (bf16[28,128,128]{2,1,0:T(8,128)(2,1)}, bf16[28,128,128]{2,1,0:T(8,128)(2,1)S(1)}, u32[]{:S(2)}, u32[]{:S(2)}) collective-permute-start(bf16[28,128,128]{2,1,0:T(8,128)(2,1)} %get-tuple-element.65.refs_0_), channel_id=1, source_target_pairs={{0,8},{1,9},{2,10},{3,11},{4,12},{5,13},{6,14},{7,15},{8,0},{9,1},... | collective-permute-start | bytes 2752520 | tf_op jit(solution)/shard_map/ppermute | solution.py:400
  11.5 44.3 %collective-permute-start.2 = (bf16[28,128,128]{2,1,0:T(8,128)(2,1)}, bf16[28,128,128]{2,1,0:T(8,128)(2,1)S(1)}, u32[]{:S(2)}, u32[]{:S(2)}) collective-permute-start(bf16[28,128,128]{2,1,0:T(8,128)(2,1)} %get-tuple-element.66.refs_12_.refs_0_), channel_id=1, source_target_pairs={{8,0},{9,1},{10,2},{11,3},{12,4},{13,5},{14,6},{15,7},{24,8},{25,9... | collective-permute-start | bytes 2752520 | tf_op jit(solution)/shard_map/ppermute | solution.py:400
  14.1 41.7 %collective-permute-start.1 = (bf16[28,128,128]{2,1,0:T(8,128)(2,1)}, bf16[28,128,128]{2,1,0:T(8,128)(2,1)}, u32[]{:S(2)}, u32[]{:S(2)}) collective-permute-start(bf16[28,128,128]{2,1,0:T(8,128)(2,1)} %get-tuple-element.66.refs_12_.refs_0_), channel_id=1, source_target_pairs={{8,16},{9,17},{10,18},{11,19},{12,20},{13,21},{14,22},{15,23},{16,... | collective-permute-start | bytes 2752520 | tf_op jit(solution)/shard_map/ppermute | solution.py:400
  49.9 41.8 %collective-permute-start.5 = (bf16[2,28,128,128]{3,2,1,0:T(8,128)(2,1)}, bf16[2,28,128,128]{3,2,1,0:T(8,128)(2,1)}, u32[]{:S(2)}, u32[]{:S(2)}) collective-permute-start(bf16[2,28,128,128]{3,2,1,0:T(8,128)(2,1)} %pack.3), channel_id=1, source_target_pairs={{0,6},{1,7},{2,4},{3,5},{4,2},{5,3},{6,0},{7,1},{8,14},{9,15},{10,... | collective-permute-start | bytes 5505032 | tf_op jit(solution)/shard_map/ppermute | solution.py:400
  54.2 45.3 %collective-permute-start.8 = (bf16[2,28,128,128]{3,2,1,0:T(8,128)(2,1)}, bf16[2,28,128,128]{3,2,1,0:T(8,128)(2,1)}, u32[]{:S(2)}, u32[]{:S(2)}) collective-permute-start(bf16[2,28,128,128]{3,2,1,0:T(8,128)(2,1)} %get-tuple-element.79.refs_4_), channel_id=1, source_target_pairs={{0,8},{1,9},{2,10},{3,11},{4,12},{5,13},{6,14},{7,15},{8,0},{9,1},... | collective-permute-start | bytes 5505032 | tf_op jit(solution)/shard_map/ppermute | solution.py:400
  55.8 3.2 %collective-permute-start.6 = (bf16[28,128,128]{2,1,0:T(8,128)(2,1)}, bf16[28,128,128]{2,1,0:T(8,128)(2,1)S(1)}, u32[]{:S(2)}, u32[]{:S(2)}) collective-permute-start(bf16[28,128,128]{2,1,0:T(8,128)(2,1)} %get-tuple-element.65.refs_0_), channel_id=1, source_target_pairs={{0,1},{1,0},{2,3},{3,2},{4,5},{5,4},{6,7},{7,6},{8,9},{9,8},{10,11... | collective-permute-start | bytes 2752520 | tf_op jit(solution)/shard_map/ppermute | solution.py:400
  55.8 3.9 %collective-permute-start.7 = (bf16[28,128,128]{2,1,0:T(8,128)(2,1)S(1)}, bf16[28,128,128]{2,1,0:T(8,128)(2,1)}, u32[]{:S(2)}, u32[]{:S(2)}) collective-permute-start(bf16[28,128,128]{2,1,0:T(8,128)(2,1)S(1)} %collective-permute-done.refs_3_.refs_0_.refs_1_), channel_id=1, source_target_pairs={{0,1},{1,0},{2,3},{3,2},{4,5},{5,4},{6,7},{7,6},{8,9},{9,8},{10,11... | collective-permute-start | bytes 2752520 | tf_op jit(solution)/shard_map/ppermute | solution.py:400
  56.3 43.6 %collective-permute-start.13 = (bf16[2,28,128,128]{3,2,1,0:T(8,128)(2,1)}, bf16[2,28,128,128]{3,2,1,0:T(8,128)(2,1)}, u32[]{:S(2)}, u32[]{:S(2)}) collective-permute-start(bf16[2,28,128,128]{3,2,1,0:T(8,128)(2,1)} %get-tuple-element.77.w_12.refs_13_.refs_1_), channel_id=1, source_target_pairs={{8,16},{9,17},{10,18},{11,19},{12,20},{13,21},{14,22},{15,23},{16,... | collective-permute-start | bytes 5505032 | tf_op jit(solution)/shard_map/ppermute | solution.py:400
  96.1 20.4 %collective-permute-start.11 = (bf16[28,128,128]{2,1,0:T(8,128)(2,1)}, bf16[28,128,128]{2,1,0:T(8,128)(2,1)}, u32[]{:S(2)}, u32[]{:S(2)}) collective-permute-start(bf16[28,128,128]{2,1,0:T(8,128)(2,1)} %get-tuple-element.81.refs_8_), channel_id=1, source_target_pairs={{0,8},{1,9},{2,10},{3,11},{4,12},{5,13},{6,14},{7,15},{8,0},{9,1},... | collective-permute-start | bytes 2752520 | tf_op jit(solution)/shard_map/ppermute | solution.py:400
  97.9 18.7 %collective-permute-start.12 = (bf16[28,128,128]{2,1,0:T(8,128)(2,1)}, bf16[28,128,128]{2,1,0:T(8,128)(2,1)}, u32[]{:S(2)}, u32[]{:S(2)}) collective-permute-start(bf16[28,128,128]{2,1,0:T(8,128)(2,1)} %get-tuple-element.84.refs_14_.refs_2_), channel_id=1, source_target_pairs={{8,16},{9,17},{10,18},{11,19},{12,20},{13,21},{14,22},{15,23},{16,... | collective-permute-start | bytes 2752520 | tf_op jit(solution)/shard_map/ppermute | solution.py:400
  99.5 23.9 %collective-permute-start.9 = (bf16[2,28,128,128]{3,2,1,0:T(8,128)(2,1)}, bf16[2,28,128,128]{3,2,1,0:T(8,128)(2,1)}, u32[]{:S(2)}, u32[]{:S(2)}) collective-permute-start(bf16[2,28,128,128]{3,2,1,0:T(8,128)(2,1)} %get-tuple-element.79.refs_4_), channel_id=1, source_target_pairs={{0,1},{1,0},{2,3},{3,2},{4,5},{5,4},{6,7},{7,6},{8,9},{9,8},{10,11... | collective-permute-start | bytes 5505032 | tf_op jit(solution)/shard_map/ppermute | solution.py:400
  99.5 23.9 %collective-permute-start.10 = (bf16[2,28,128,128]{3,2,1,0:T(8,128)(2,1)}, bf16[2,28,128,128]{3,2,1,0:T(8,128)(2,1)}, u32[]{:S(2)}, u32[]{:S(2)}) collective-permute-start(bf16[2,28,128,128]{3,2,1,0:T(8,128)(2,1)} %collective-permute-done.8.refs_5_), channel_id=1, source_target_pairs={{0,1},{1,0},{2,3},{3,2},{4,5},{5,4},{6,7},{7,6},{8,9},{9,8},{10,11... | collective-permute-start | bytes 5505032 | tf_op jit(solution)/shard_map/ppermute | solution.py:400
  100.0 23.4 %collective-permute-start.14 = (bf16[28,128,128]{2,1,0:T(8,128)(2,1)}, bf16[28,128,128]{2,1,0:T(8,128)(2,1)}, u32[]{:S(2)}, u32[]{:S(2)}) collective-permute-start(bf16[28,128,128]{2,1,0:T(8,128)(2,1)} %get-tuple-element.81.refs_8_), channel_id=1, source_target_pairs={{0,1},{1,0},{2,3},{3,2},{4,5},{5,4},{6,7},{7,6},{8,9},{9,8},{10,11... | collective-permute-start | bytes 2752520 | tf_op jit(solution)/shard_map/ppermute | solution.py:400
  116.5 6.9 %collective-permute-start.15 = (bf16[28,128,128]{2,1,0:T(8,128)(2,1)}, bf16[28,128,128]{2,1,0:T(8,128)(2,1)}, u32[]{:S(2)}, u32[]{:S(2)}) collective-permute-start(bf16[28,128,128]{2,1,0:T(8,128)(2,1)} %collective-permute-done.11.refs_9_), channel_id=1, source_target_pairs={{0,1},{1,0},{2,3},{3,2},{4,5},{5,4},{6,7},{7,6},{8,9},{9,8},{10,11... | collective-permute-start | bytes 2752520 | tf_op jit(solution)/shard_map/ppermute | solution.py:400
  117.1 27.2 %collective-permute-start.16 = (bf16[28,128,128]{2,1,0:T(8,128)(2,1)}, bf16[28,128,128]{2,1,0:T(8,128)(2,1)}, u32[]{:S(2)}, u32[]{:S(2)}) collective-permute-start(bf16[28,128,128]{2,1,0:T(8,128)(2,1)} %get-tuple-element.92), channel_id=1, source_target_pairs={{8,0},{9,1},{10,2},{11,3},{12,4},{13,5},{14,6},{15,7},{24,8},{25,9... | collective-permute-start | bytes 2752520 | tf_op jit(solution)/shard_map/ppermute | solution.py:400
  123.4 40.6 %collective-permute-start.17 = (bf16[28,128,128]{2,1,0:T(8,128)(2,1)}, bf16[28,128,128]{2,1,0:T(8,128)(2,1)S(1)}, u32[]{:S(2)}, u32[]{:S(2)}) collective-permute-start(bf16[28,128,128]{2,1,0:T(8,128)(2,1)} %get-tuple-element.93), channel_id=1, source_target_pairs={{8,0},{9,1},{10,2},{11,3},{12,4},{13,5},{14,6},{15,7},{24,8},{25,9... | collective-permute-start | bytes 2752520 | tf_op jit(solution)/shard_map/ppermute | solution.py:400
  138.0 45.3 %collective-permute-start.21 = (bf16[28,128,128]{2,1,0:T(8,128)(2,1)}, bf16[28,128,128]{2,1,0:T(8,128)(2,1)S(1)}, u32[]{:S(2)}, u32[]{:S(2)}) collective-permute-start(bf16[28,128,128]{2,1,0:T(8,128)(2,1)} %reorder.3), channel_id=1, source_target_pairs={{8,0},{9,1},{10,2},{11,3},{12,4},{13,5},{14,6},{15,7},{24,8},{25,9... | collective-permute-start | bytes 2752520 | tf_op jit(solution)/shard_map/ppermute | solution.py:400
  141.0 28.3 %collective-permute-start.18 = (bf16[4,128,512]{2,1,0:T(8,128)(2,1)S(1)}, bf16[4,128,512]{2,1,0:T(8,128)(2,1)S(1)}, u32[]{:S(2)}, u32[]{:S(2)}) collective-permute-start(bf16[4,128,512]{2,1,0:T(8,128)(2,1)S(1)} %get-tuple-element.97.refs_6_), channel_id=1, source_target_pairs={{0,2},{1,3},{2,0},{3,1},{4,6},{5,7},{6,4},{7,5},{8,10},{9,11},{10,... | collective-permute-start | bytes 1572872 | tf_op jit(solution)/shard_map/ppermute | solution.py:400
  142.5 26.8 %collective-permute-start.19 = (bf16[4,128,512]{2,1,0:T(8,128)(2,1)S(1)}, bf16[4,128,512]{2,1,0:T(8,128)(2,1)S(1)}, u32[]{:S(2)}, u32[]{:S(2)}) collective-permute-start(bf16[4,128,512]{2,1,0:T(8,128)(2,1)S(1)} %get-tuple-element.98), channel_id=1, source_target_pairs={{0,4},{1,5},{2,6},{3,7},{4,0},{5,1},{6,2},{7,3},{8,12},{9,13},{10,... | collective-permute-start | bytes 1572872 | tf_op jit(solution)/shard_map/ppermute | solution.py:400
  144.3 25.0 %collective-permute-start.20 = (bf16[4,128,512]{2,1,0:T(8,128)(2,1)S(1)}, bf16[4,128,512]{2,1,0:T(8,128)(2,1)S(1)}, u32[]{:S(2)}, u32[]{:S(2)}) collective-permute-start(bf16[4,128,512]{2,1,0:T(8,128)(2,1)S(1)} %get-tuple-element.99), channel_id=1, source_target_pairs={{0,6},{1,7},{2,4},{3,5},{4,2},{5,3},{6,0},{7,1},{8,14},{9,15},{10,... | collective-permute-start | bytes 1572872 | tf_op jit(solution)/shard_map/ppermute | solution.py:400
  169.3 17.5 %collective-permute-start.22 = (bf16[4,128,256]{2,1,0:T(8,128)(2,1)S(1)}, bf16[4,128,256]{2,1,0:T(8,128)(2,1)S(1)}, u32[]{:S(2)}, u32[]{:S(2)}) collective-permute-start(bf16[4,128,256]{2,1,0:T(8,128)(2,1)S(1)} %get-tuple-element.108), channel_id=1, source_target_pairs={{0,2},{1,3},{2,0},{3,1},{4,6},{5,7},{6,4},{7,5},{8,10},{9,11},{10,... | collective-permute-start | bytes 786440 | tf_op jit(solution)/shard_map/ppermute | solution.py:400
  170.7 16.1 %collective-permute-start.23 = (bf16[4,128,256]{2,1,0:T(8,128)(2,1)S(1)}, bf16[4,128,256]{2,1,0:T(8,128)(2,1)S(1)}, u32[]{:S(2)}, u32[]{:S(2)}) collective-permute-start(bf16[4,128,256]{2,1,0:T(8,128)(2,1)S(1)} %get-tuple-element.109), channel_id=1, source_target_pairs={{0,4},{1,5},{2,6},{3,7},{4,0},{5,1},{6,2},{7,3},{8,12},{9,13},{10,... | collective-permute-start | bytes 786440 | tf_op jit(solution)/shard_map/ppermute | solution.py:400
  171.2 15.6 %collective-permute-start.24 = (bf16[4,128,256]{2,1,0:T(8,128)(2,1)S(1)}, bf16[4,128,256]{2,1,0:T(8,128)(2,1)S(1)}, u32[]{:S(2)}, u32[]{:S(2)}) collective-permute-start(bf16[4,128,256]{2,1,0:T(8,128)(2,1)S(1)} %get-tuple-element.110), channel_id=1, source_target_pairs={{0,6},{1,7},{2,4},{3,5},{4,2},{5,3},{6,0},{7,1},{8,14},{9,15},{10,... | collective-permute-start | bytes 786440 | tf_op jit(solution)/shard_map/ppermute | solution.py:400
  186.9 9.3 %collective-permute-start.28 = (bf16[4,128,256]{2,1,0:T(8,128)(2,1)S(1)}, bf16[4,128,256]{2,1,0:T(8,128)(2,1)S(1)}, u32[]{:S(2)}, u32[]{:S(2)}) collective-permute-start(bf16[4,128,256]{2,1,0:T(8,128)(2,1)S(1)} %get-tuple-element.118), channel_id=1, source_target_pairs={{0,2},{1,3},{2,0},{3,1},{4,6},{5,7},{6,4},{7,5},{8,10},{9,11},{10,... | collective-permute-start | bytes 786440 | tf_op jit(solution)/shard_map/ppermute | solution.py:400
  188.4 13.3 %collective-permute-start.29 = (bf16[4,128,256]{2,1,0:T(8,128)(2,1)S(1)}, bf16[4,128,256]{2,1,0:T(8,128)(2,1)S(1)}, u32[]{:S(2)}, u32[]{:S(2)}) collective-permute-start(bf16[4,128,256]{2,1,0:T(8,128)(2,1)S(1)} %get-tuple-element.119), channel_id=1, source_target_pairs={{0,4},{1,5},{2,6},{3,7},{4,0},{5,1},{6,2},{7,3},{8,12},{9,13},{10,... | collective-permute-start | bytes 786440 | tf_op jit(solution)/shard_map/ppermute | solution.py:400
  188.7 13.0 %collective-permute-start.30 = (bf16[4,128,256]{2,1,0:T(8,128)(2,1)S(1)}, bf16[4,128,256]{2,1,0:T(8,128)(2,1)S(1)}, u32[]{:S(2)}, u32[]{:S(2)}) collective-permute-start(bf16[4,128,256]{2,1,0:T(8,128)(2,1)S(1)} %get-tuple-element.120.refs_3_), channel_id=1, source_target_pairs={{0,6},{1,7},{2,4},{3,5},{4,2},{5,3},{6,0},{7,1},{8,14},{9,15},{10,... | collective-permute-start | bytes 786440 | tf_op jit(solution)/shard_map/ppermute | solution.py:400
  192.3 11.8 %collective-permute-start.25 = (bf16[128,768]{1,0:T(8,128)(2,1)S(1)}, bf16[128,768]{1,0:T(8,128)(2,1)S(1)}, u32[]{:S(2)}, u32[]{:S(2)}) collective-permute-start(bf16[128,768]{1,0:T(8,128)(2,1)S(1)} %get-tuple-element.115), channel_id=1, source_target_pairs={{0,1},{1,0},{2,3},{3,2},{4,5},{5,4},{6,7},{7,6},{8,9},{9,8},{10,11... | collective-permute-start | bytes 589832 | tf_op jit(solution)/shard_map/ppermute | solution.py:400
  192.4 11.8 %collective-permute-start.26 = (bf16[128,768]{1,0:T(8,128)(2,1)S(1)}, bf16[128,768]{1,0:T(8,128)(2,1)S(1)}, u32[]{:S(2)}, u32[]{:S(2)}) collective-permute-start(bf16[128,768]{1,0:T(8,128)(2,1)S(1)} %get-tuple-element.116), channel_id=1, source_target_pairs={{0,8},{1,9},{2,10},{3,11},{4,12},{5,13},{6,14},{7,15},{8,0},{9,1},... | collective-permute-start | bytes 589832 | tf_op jit(solution)/shard_map/ppermute | solution.py:400
  196.2 8.1 %collective-permute-start.27 = (bf16[128,768]{1,0:T(8,128)(2,1)S(1)}, bf16[128,768]{1,0:T(8,128)(2,1)S(1)}, u32[]{:S(2)}, u32[]{:S(2)}) collective-permute-start(bf16[128,768]{1,0:T(8,128)(2,1)S(1)} %get-tuple-element.117), channel_id=1, source_target_pairs={{0,9},{1,8},{2,11},{3,10},{4,13},{5,12},{6,15},{7,14},{8,1},{9,0},... | collective-permute-start | bytes 589832 | tf_op jit(solution)/shard_map/ppermute | solution.py:400
  201.8 2.4 %collective-permute-start.31 = (bf16[128,256]{1,0:T(8,128)(2,1)S(1)}, bf16[128,256]{1,0:T(8,128)(2,1)S(1)}, u32[]{:S(2)}, u32[]{:S(2)}) collective-permute-start(bf16[128,256]{1,0:T(8,128)(2,1)S(1)} %get-tuple-element.122), channel_id=1, source_target_pairs={{0,1},{1,0},{2,3},{3,2},{4,5},{5,4},{6,7},{7,6},{8,9},{9,8},{10,11... | collective-permute-start | bytes 196616 | tf_op jit(solution)/shard_map/ppermute | solution.py:400
  201.9 4.9 %collective-permute-start.32 = (bf16[128,256]{1,0:T(8,128)(2,1)S(1)}, bf16[128,256]{1,0:T(8,128)(2,1)S(1)}, u32[]{:S(2)}, u32[]{:S(2)}) collective-permute-start(bf16[128,256]{1,0:T(8,128)(2,1)S(1)} %get-tuple-element.123), channel_id=1, source_target_pairs={{0,8},{1,9},{2,10},{3,11},{4,12},{5,13},{6,14},{7,15},{8,0},{9,1},... | collective-permute-start | bytes 196616 | tf_op jit(solution)/shard_map/ppermute | solution.py:400
  204.1 4.0 %collective-permute-start.33 = (bf16[128,256]{1,0:T(8,128)(2,1)S(1)}, bf16[128,256]{1,0:T(8,128)(2,1)S(1)}, u32[]{:S(2)}, u32[]{:S(2)}) collective-permute-start(bf16[128,256]{1,0:T(8,128)(2,1)S(1)} %get-tuple-element.124), channel_id=1, source_target_pairs={{0,9},{1,8},{2,11},{3,10},{4,13},{5,12},{6,15},{7,14},{8,1},{9,0},... | collective-permute-start | bytes 196616 | tf_op jit(solution)/shard_map/ppermute | solution.py:400

commit v13 on v12

--- a/solution.py
+++ b/solution.py
@@ -117,6 +117,37 @@
         cost_estimate=pl.CostEstimate(flops=0, bytes_accessed=8 * one.size, transcendentals=0),
         name="unpack_pair",
     )(one, two, *after)
+
+
+def unpack_kernel(packed, a, w, held, in_sem, out_sem):
+    into = [pltpu.make_async_copy(packed.at[at], held.at[at], in_sem.at[at]) for at in range(2)]
+    out_of = [
+        pltpu.make_async_copy(held.at[at], out, out_sem.at[at]) for at, out in enumerate((a, w))
+    ]
+    for copy in into:
+        copy.start()
+    for copy_in, copy_out in zip(into, out_of):
+        copy_in.wait()
+        copy_out.start()
+    for copy in out_of:
+        copy.wait()
+
+
+def unpack(packed):
+    return pl.pallas_call(
+        unpack_kernel,
+        out_shape=[pltpu.HBM(packed.shape[1:], packed.dtype)] * 2,
+        in_specs=[pl.BlockSpec(memory_space=pl.ANY)],
+        out_specs=[pl.BlockSpec(memory_space=pl.ANY)] * 2,
+        scratch_shapes=[
+            pltpu.VMEM(packed.shape, packed.dtype),
+            pltpu.SemaphoreType.DMA((2,)),
+            pltpu.SemaphoreType.DMA((2,)),
+        ],
+        compiler_params=pltpu.CompilerParams(vmem_limit_bytes=LIMIT),
+        cost_estimate=pl.CostEstimate(flops=0, bytes_accessed=4 * packed.size, transcendentals=0),
+        name="unpack",
+    )(packed)
 
 
 def reorder_kernel(count, order_ref, packed, w_12, *refs):
@@ -426,11 +457,12 @@
 
     order = jnp.array([[1, 2, 3], [1, 3, 2], [2, 3, 1], [3, 2, 1]], jnp.int32)[plane]
     got_3, core_0, core_pair_0 = lax.optimization_barrier((got_3, core_0, core_pair_0))
-    known = jnp.array([0, 3], jnp.int32)
-    a_3, w_3, ordered_1, ordered_2 = reorder(jnp.concatenate([known, order[:2]]), got_3, w_12)
+    a_3, w_3 = unpack(got_3)
     pair_3 = to_pair(a_3)
     a_12, pair_12, a_3 = lax.optimization_barrier((a_12, pair_12, a_3))
+    a_12, pair_12, mid_12, got_3 = lax.optimization_barrier((a_12, pair_12, mid_12, got_3))
     core_12, core_pair_12 = to_core(a_12), to_core(pair_12)
+    ordered_1, ordered_2 = reorder(order[:2], got_3, w_12)
     mid_3 = to_mid(w_3)
     ordered_1, ordered_2, pair_3, mid_3, mid_12 = lax.optimization_barrier(
         (ordered_1, ordered_2, pair_3, mid_3, mid_12)

time: 210 us -> 208 us (level)
  waiting for transfers between devices: 116 us -> 110 us
  local copies, waits for them, and re-layouts: 1.26 us -> 6.54 us
    ppermute x34, waiting for transfers between devices: 116 us -> 110 us  [send(): return lax.ppermute(array, 'fsdp', perm=perm)]
    unnamed x0 -> x16, local copies, waits for them, and re-layouts: none -> 5.2 us
where the time goes in v13:
time: 208 us; the launch traced here: 207 us
  waiting for transfers between devices  110 us (53%)
  Pallas kernels  47.3 us (23%)
  starting transfers between devices  42.7 us (21%)
  local copies, waits for them, and re-layouts  6.54 us (3%)
    ppermute x34, waiting for transfers between devices, send(): return lax.ppermute(array, 'fsdp', perm=perm)  110 us
    ppermute x34, starting transfers between devices, send(): return lax.ppermute(array, 'fsdp', perm=perm)  42.7 us
    pallas_call x4, Pallas kernels, product(): pl.pallas_call(functools.partial(product_kernel, [places[group] for group...  14.5 us
    pallas_call x1, Pallas kernels, stack_product(): pl.pallas_call(functools.partial(stack_product_kernel, places, a_at, w_at...  11 us
    pallas_call x2, Pallas kernels, pack(): pl.pallas_call(functools.partial(pack_kernel, apart, len(steps)), out_sha...  8.3 us
    pallas_call x2, Pallas kernels, reorder(): pl.pallas_call(functools.partial(reorder_kernel, count), out_shape=[pltpu...  6.82 us
    unnamed x16, local copies, waits for them, and re-layouts  5.2 us
  transfers between devices with their start and end apart: 34, of which 13 were waited for; matrix products, arithmetic and copies ran while one was open for 1% of the time, Pallas kernels for 19%

profile of v13, /device:TPU:0, one launch (start us, length us, event | category | flops | bytes accessed | tf_op | source)
XLA Modules:
  0.0 207.2 jit_solution(11033422313780284442)
XLA Ops:
  0.0 5.4 %pack.2 = (bf16[28,128,128]{2,1,0:T(8,128)(2,1)}, bf16[28,128,128]{2,1,0:T(8,128)(2,1)}, bf16[2,28,128,128]{3,2,1,0:T(8,128)(2,1)S(1)}, bf16[2,28,128,128]{3,2,1,0:T(8,128)(2,1)S(1)}) custom-call(s32[1]{0:T(128)} %bitcast.3.plane_ref.choice_ref, bf16[128,14336]{1,0:T(8,128)(2,1)} %refs_0_.3, bf16[128,14336]{1,0:T(8,128)(2,1)} %refs_1_.3, ...), custom_call_target="tpu_custom_call" | custom-call | bytes 13762560 | tf_op jit(solution)/shard_map/pack/pallas_call | solution.py:63
  5.4 3.0 %collective-permute-start.3 = (bf16[2,28,128,128]{3,2,1,0:T(8,128)(2,1)S(1)}, bf16[2,28,128,128]{3,2,1,0:T(8,128)(2,1)S(1)}, u32[]{:S(2)}, u32[]{:S(2)}) collective-permute-start(bf16[2,28,128,128]{3,2,1,0:T(8,128)(2,1)S(1)} %get-tuple-element.72), channel_id=1, source_target_pairs={{0,2},{1,3},{2,0},{3,1},{4,6},{5,7},{6,4},{7,5},{8,10},{9,11},{10,... | collective-permute-start | bytes 5505032 | tf_op jit(solution)/shard_map/ppermute | solution.py:431
  8.4 1.5 collective-permute-start.4
  9.9 1.6 collective-permute-start
  11.5 2.6 %collective-permute-start.2 = (bf16[28,128,128]{2,1,0:T(8,128)(2,1)}, bf16[28,128,128]{2,1,0:T(8,128)(2,1)S(1)}, u32[]{:S(2)}, u32[]{:S(2)}) collective-permute-start(bf16[28,128,128]{2,1,0:T(8,128)(2,1)} %get-tuple-element.70.refs_12_.refs_0_), channel_id=1, source_target_pairs={{8,0},{9,1},{10,2},{11,3},{12,4},{13,5},{14,6},{15,7},{24,8},{25,9... | collective-permute-start | bytes 2752520 | tf_op jit(solution)/shard_map/ppermute | solution.py:431
  14.8 18.6 %collective-permute-done.refs_3_.refs_0_.refs_1_ = bf16[28,128,128]{2,1,0:T(8,128)(2,1)S(1)} collective-permute-done((bf16[28,128,128]{2,1,0:T(8,128)(2,1)}, bf16[28,128,128]{2,1,0:T(8,128)(2,1)S(1)}, u32[]{:S(2)}, u32[]{:S(2)}) %collective-permute-start) | collective-permute-done | bytes 917536 | tf_op jit(solution)/shard_map/ppermute | solution.py:431
  33.4 2.9 %pack.3 = bf16[2,28,128,128]{3,2,1,0:T(8,128)(2,1)S(1)} custom-call(s32[1]{0:T(128)} %bitcast.3.plane_ref.choice_ref, bf16[128,14336]{1,0:T(8,128)(2,1)} %refs_0_.3, bf16[128,14336]{1,0:T(8,128)(2,1)} %refs_1_.3, bf16[14336,128]{1,0:T(8,128)(2,1)} %refs_2_.3, bf16[28,128,128]{2,1,0:T(8,128)(2,1)S(1)} %collective-permute-done.refs_3_.refs_0_.refs_1_), custom_call_target="tpu_custom_call" | custom-call | bytes 4587520 | tf_op jit(solution)/shard_map/pack/pallas_call | solution.py:63
  36.3 12.1 %collective-permute-done.3.one = bf16[2,28,128,128]{3,2,1,0:T(8,128)(2,1)S(1)} collective-permute-done((bf16[2,28,128,128]{3,2,1,0:T(8,128)(2,1)S(1)}, bf16[2,28,128,128]{3,2,1,0:T(8,128)(2,1)S(1)}, u32[]{:S(2)}, u32[]{:S(2)}) %collective-permute-start.3) | collective-permute-done | bytes 1835040 | tf_op jit(solution)/shard_map/ppermute | solution.py:431
  48.4 1.5 collective-permute-done.4.two
  49.9 1.5 collective-permute-start.5
  51.4 2.7 %unpack_pair.1 = (bf16[2,28,128,128]{3,2,1,0:T(8,128)(2,1)}, bf16[2,28,128,128]{3,2,1,0:T(8,128)(2,1)}) custom-call(bf16[2,28,128,128]{3,2,1,0:T(8,128)(2,1)S(1)} %collective-permute-done.3.one, bf16[2,28,128,128]{3,2,1,0:T(8,128)(2,1)S(1)} %collective-permute-done.4.two, bf16[28,128,128]{2,1,0:T(8,128)(2,1)S(1)} %collective-permute-done.refs_3_.refs_0_.refs_1_), custom_call_target="tpu_custom_call" | custom-call | bytes 7340032 | tf_op jit(solution)/shard_map/unpack_pair/pallas_call | solution.py:106
  54.1 1.6 collective-permute-start.8
  55.8 1.9 collective-permute-start.9
  57.7 1.0 copy-done
  59.1 2.0 collective-permute-done.6.refs_2_
  61.1 0.9 copy-done.2
  62.4 0.9 copy-done.4
  63.4 28.0 %collective-permute-done.5.packed = bf16[2,28,128,128]{3,2,1,0:T(8,128)(2,1)S(1)} collective-permute-done((bf16[2,28,128,128]{3,2,1,0:T(8,128)(2,1)S(1)}, bf16[2,28,128,128]{3,2,1,0:T(8,128)(2,1)S(1)}, u32[]{:S(2)}, u32[]{:S(2)}) %collective-permute-start.5) | collective-permute-done | bytes 1835040 | tf_op jit(solution)/shard_map/ppermute | solution.py:431
  91.4 1.7 unpack.1
  93.1 1.6 collective-permute-start.12
  94.7 1.6 collective-permute-start.13
  97.6 3.5 %reorder.2 = (bf16[28,128,128]{2,1,0:T(8,128)(2,1)}, bf16[28,128,128]{2,1,0:T(8,128)(2,1)}) custom-call(s32[2]{0:T(128)S(1)} %slice_bitcast_fusion.order_ref, bf16[2,28,128,128]{3,2,1,0:T(8,128)(2,1)S(1)} %collective-permute-done.5.packed, bf16[2,28,128,128]{3,2,1,0:T(8,128)(2,1)} %get-tuple-element.84.w_12.refs_13_.refs_1_), custom_call_target="tpu_custom_call" | custom-call | bytes 7340032 | tf_op jit(solution)/shard_map/reorder/pallas_call | solution.py:175
  101.1 13.4 %collective-permute-done.12.refs_9_ = bf16[28,128,128]{2,1,0:T(8,128)(2,1)} collective-permute-done((bf16[28,128,128]{2,1,0:T(8,128)(2,1)}, bf16[28,128,128]{2,1,0:T(8,128)(2,1)}, u32[]{:S(2)}, u32[]{:S(2)}) %collective-permute-start.12) | collective-permute-done | bytes 917536 | tf_op jit(solution)/shard_map/ppermute | solution.py:431
  115.2 5.8 %collective-permute-start.16 = (bf16[28,128,128]{2,1,0:T(8,128)(2,1)}, bf16[28,128,128]{2,1,0:T(8,128)(2,1)}, u32[]{:S(2)}, u32[]{:S(2)}) collective-permute-start(bf16[28,128,128]{2,1,0:T(8,128)(2,1)} %get-tuple-element.100), channel_id=1, source_target_pairs={{8,0},{9,1},{10,2},{11,3},{12,4},{13,5},{14,6},{15,7},{24,8},{25,9... | collective-permute-start | bytes 2752520 | tf_op jit(solution)/shard_map/ppermute | solution.py:431
  121.0 1.2 copy-done.3
  122.2 1.2 copy-done.5
  123.3 11.0 %stack_product.1 = (bf16[28,2048,128]{2,1,0:T(8,128)(2,1)S(1)}, bf16[4,128,512]{2,1,0:T(8,128)(2,1)S(1)}, bf16[4,128,512]{2,1,0:T(8,128)(2,1)S(1)}, bf16[4,128,512]{2,1,0:T(8,128)(2,1)S(1)}) custom-call(s32[1]{0:T(128)} %bitcast.2.choice_ref, bf16[28,128,128]{2,1,0:T(8,128)(2,1)} %get-tuple-element.69.refs_0_, ...), custom_call_target="tpu_custom_call" | custom-call | flops 5637144576 | bytes 18350080 | tf_op jit(solution)/shard_map/stack_product/pallas_call | solution.py:267
  134.3 3.3 %reorder.3 = bf16[28,128,128]{2,1,0:T(8,128)(2,1)} custom-call(s32[1]{0:T(128)} %bitcast.5.order_ref, bf16[2,28,128,128]{3,2,1,0:T(8,128)(2,1)S(1)} %collective-permute-done.5.packed, bf16[2,28,128,128]{3,2,1,0:T(8,128)(2,1)} %get-tuple-element.84.w_12.refs_13_.refs_1_), custom_call_target="tpu_custom_call" | custom-call | bytes 7340032 | tf_op jit(solution)/shard_map/reorder/pallas_call | solution.py:175
  137.7 3.0 %collective-permute-start.21 = (bf16[28,128,128]{2,1,0:T(8,128)(2,1)}, bf16[28,128,128]{2,1,0:T(8,128)(2,1)S(1)}, u32[]{:S(2)}, u32[]{:S(2)}) collective-permute-start(bf16[28,128,128]{2,1,0:T(8,128)(2,1)} %reorder.3), channel_id=1, source_target_pairs={{8,0},{9,1},{10,2},{11,3},{12,4},{13,5},{14,6},{15,7},{24,8},{25,9... | collective-permute-start | bytes 2752520 | tf_op jit(solution)/shard_map/ppermute | solution.py:431
  140.7 1.4 collective-permute-start.18
  142.6 1.6 collective-permute-start.20
  144.2 4.2 %product.4.refs_3_.refs_0_ = f32[4,128,512]{2,1,0:T(8,128)S(1)} custom-call(s32[1]{0:T(128)} %bitcast.2.choice_ref, bf16[28,2048,128]{2,1,0:T(8,128)(2,1)S(1)} %get-tuple-element.97.a, bf16[28,128,128]{2,1,0:T(8,128)(2,1)} %get-tuple-element.70.refs_12_.refs_0_, bf16[2,28,128,128]{3,2,1,0:T(8,128)(2,1)} %get-tuple-element.84.w_12.refs_13_.refs_1_, ...), custom_call_target="tpu_custom_call" | custom-call | flops 1879048192 | bytes 7340032 | tf_op jit(solution)/shard_map/product/pallas_call | solution.py:336
  148.4 13.2 %collective-permute-done.17.refs_2_.refs_0_ = bf16[28,128,128]{2,1,0:T(8,128)(2,1)S(1)} collective-permute-done((bf16[28,128,128]{2,1,0:T(8,128)(2,1)}, bf16[28,128,128]{2,1,0:T(8,128)(2,1)S(1)}, u32[]{:S(2)}, u32[]{:S(2)}) %collective-permute-start.17) | collective-permute-done | bytes 917536 | tf_op jit(solution)/shard_map/ppermute | solution.py:431
  161.6 5.3 %product.5 = (bf16[4,128,256]{2,1,0:T(8,128)(2,1)S(1)}, bf16[4,128,256]{2,1,0:T(8,128)(2,1)S(1)}, bf16[4,128,256]{2,1,0:T(8,128)(2,1)S(1)}, f32[4,128,256]{2,1,0:T(8,128)S(1)}) custom-call(s32[1]{0:T(128)} %bitcast.3.plane_ref.choice_ref, bf16[28,2048,128]{2,1,0:T(8,128)(2,1)S(1)} %get-tuple-element.97.a, bf16[28,128,128]{2,1,0:T(8,128)(2,1)S(1)} %copy-done.1, ...), custom_call_target="tpu_custom_call" | custom-call | flops 3758096384 | bytes 16515072 | tf_op jit(solution)/shard_map/product/pallas_call | solution.py:336
  166.9 1.3 collective-permute-start.22
  168.7 1.7 collective-permute-start.24
  170.5 10.4 %collective-permute-done.21.refs_1_ = bf16[28,128,128]{2,1,0:T(8,128)(2,1)S(1)} collective-permute-done((bf16[28,128,128]{2,1,0:T(8,128)(2,1)}, bf16[28,128,128]{2,1,0:T(8,128)(2,1)S(1)}, u32[]{:S(2)}, u32[]{:S(2)}) %collective-permute-start.21) | collective-permute-done | bytes 917536 | tf_op jit(solution)/shard_map/ppermute | solution.py:431
  180.8 3.6 %product.6 = (bf16[4,128,256]{2,1,0:T(8,128)(2,1)S(1)}, bf16[4,128,256]{2,1,0:T(8,128)(2,1)S(1)}, bf16[4,128,256]{2,1,0:T(8,128)(2,1)S(1)}) custom-call(s32[1]{0:T(128)} %bitcast.3.plane_ref.choice_ref, bf16[28,2048,128]{2,1,0:T(8,128)(2,1)S(1)} %get-tuple-element.97.a, bf16[28,128,128]{2,1,0:T(8,128)(2,1)S(1)} %collective-permute-done.17.refs_2_.refs_0_, ...), custom_call_target="tpu_custom_call" | custom-call | flops 2818572288 | bytes 12845056 | tf_op jit(solution)/shard_map/product/pallas_call | solution.py:336
  184.4 1.3 collective-permute-start.28
  186.2 1.8 collective-permute-start.30
  188.0 1.5 product.7.refs_8_.refs_0_
  190.0 2.2 %collective-permute-start.26 = (bf16[128,768]{1,0:T(8,128)(2,1)S(1)}, bf16[128,768]{1,0:T(8,128)(2,1)S(1)}, u32[]{:S(2)}, u32[]{:S(2)}) collective-permute-start(bf16[128,768]{1,0:T(8,128)(2,1)S(1)} %get-tuple-element.124), channel_id=1, source_target_pairs={{0,8},{1,9},{2,10},{3,11},{4,12},{5,13},{6,14},{7,15},{8,0},{9,1},... | collective-permute-start | bytes 589832 | tf_op jit(solution)/shard_map/ppermute | solution.py:431
  192.1 1.6 collective-permute-done.28.refs_1_
  193.7 5.3 %collective-permute-done.29.refs_2_ = bf16[4,128,256]{2,1,0:T(8,128)(2,1)S(1)} collective-permute-done((bf16[4,128,256]{2,1,0:T(8,128)(2,1)S(1)}, bf16[4,128,256]{2,1,0:T(8,128)(2,1)S(1)}, u32[]{:S(2)}, u32[]{:S(2)}) %collective-permute-start.29) | collective-permute-done | bytes 262176 | tf_op jit(solution)/shard_map/ppermute | solution.py:431
  199.2 2.2 %collective-permute-start.32 = (bf16[128,256]{1,0:T(8,128)(2,1)S(1)}, bf16[128,256]{1,0:T(8,128)(2,1)S(1)}, u32[]{:S(2)}, u32[]{:S(2)}) collective-permute-start(bf16[128,256]{1,0:T(8,128)(2,1)S(1)} %get-tuple-element.131), channel_id=1, source_target_pairs={{0,8},{1,9},{2,10},{3,11},{4,12},{5,13},{6,14},{7,15},{8,0},{9,1},... | collective-permute-start | bytes 196616 | tf_op jit(solution)/shard_map/ppermute | solution.py:431
  201.6 2.5 %collective-permute-done.32.refs_6_ = bf16[128,256]{1,0:T(8,128)(2,1)S(1)} collective-permute-done((bf16[128,256]{1,0:T(8,128)(2,1)S(1)}, bf16[128,256]{1,0:T(8,128)(2,1)S(1)}, u32[]{:S(2)}, u32[]{:S(2)}) %collective-permute-start.32) | collective-permute-done | bytes 65568 | tf_op jit(solution)/shard_map/ppermute | solution.py:431
  204.1 1.4 collective-permute-done.33.refs_7_
  205.5 1.8 assemble.1
  (54 shorter events, 5.9 us)
Async XLA Ops:
  5.4 43.0 %collective-permute-start.3 = (bf16[2,28,128,128]{3,2,1,0:T(8,128)(2,1)S(1)}, bf16[2,28,128,128]{3,2,1,0:T(8,128)(2,1)S(1)}, u32[]{:S(2)}, u32[]{:S(2)}) collective-permute-start(bf16[2,28,128,128]{3,2,1,0:T(8,128)(2,1)S(1)} %get-tuple-element.72), channel_id=1, source_target_pairs={{0,2},{1,3},{2,0},{3,1},{4,6},{5,7},{6,4},{7,5},{8,10},{9,11},{10,... | collective-permute-start | bytes 5505032 | tf_op jit(solution)/shard_map/ppermute | solution.py:431
  8.4 41.5 %collective-permute-start.4 = (bf16[2,28,128,128]{3,2,1,0:T(8,128)(2,1)S(1)}, bf16[2,28,128,128]{3,2,1,0:T(8,128)(2,1)S(1)}, u32[]{:S(2)}, u32[]{:S(2)}) collective-permute-start(bf16[2,28,128,128]{3,2,1,0:T(8,128)(2,1)S(1)} %get-tuple-element.73), channel_id=1, source_target_pairs={{0,4},{1,5},{2,6},{3,7},{4,0},{5,1},{6,2},{7,3},{8,12},{9,13},{10,... | collective-permute-start | bytes 5505032 | tf_op jit(solution)/shard_map/ppermute | solution.py:431
  9.9 23.5 %collective-permute-start = (bf16[28,128,128]{2,1,0:T(8,128)(2,1)}, bf16[28,128,128]{2,1,0:T(8,128)(2,1)S(1)}, u32[]{:S(2)}, u32[]{:S(2)}) collective-permute-start(bf16[28,128,128]{2,1,0:T(8,128)(2,1)} %get-tuple-element.69.refs_0_), channel_id=1, source_target_pairs={{0,8},{1,9},{2,10},{3,11},{4,12},{5,13},{6,14},{7,15},{8,0},{9,1},... | collective-permute-start | bytes 2752520 | tf_op jit(solution)/shard_map/ppermute | solution.py:431
  11.5 46.1 %collective-permute-start.2 = (bf16[28,128,128]{2,1,0:T(8,128)(2,1)}, bf16[28,128,128]{2,1,0:T(8,128)(2,1)S(1)}, u32[]{:S(2)}, u32[]{:S(2)}) collective-permute-start(bf16[28,128,128]{2,1,0:T(8,128)(2,1)} %get-tuple-element.70.refs_12_.refs_0_), channel_id=1, source_target_pairs={{8,0},{9,1},{10,2},{11,3},{12,4},{13,5},{14,6},{15,7},{24,8},{25,9... | collective-permute-start | bytes 2752520 | tf_op jit(solution)/shard_map/ppermute | solution.py:431
  14.1 44.5 %collective-permute-start.1 = (bf16[28,128,128]{2,1,0:T(8,128)(2,1)}, bf16[28,128,128]{2,1,0:T(8,128)(2,1)S(1)}, u32[]{:S(2)}, u32[]{:S(2)}) collective-permute-start(bf16[28,128,128]{2,1,0:T(8,128)(2,1)} %get-tuple-element.70.refs_12_.refs_0_), channel_id=1, source_target_pairs={{8,16},{9,17},{10,18},{11,19},{12,20},{13,21},{14,22},{15,23},{16,... | collective-permute-start | bytes 2752520 | tf_op jit(solution)/shard_map/ppermute | solution.py:431
  36.3 22.3 %copy-start.7 = (bf16[28,128,128]{2,1,0:T(8,128)(2,1)S(1)}, bf16[28,128,128]{2,1,0:T(8,128)(2,1)}, u32[]{:S(2)}) copy-start(bf16[28,128,128]{2,1,0:T(8,128)(2,1)} %get-tuple-element.69.refs_0_) | copy-start | bytes 2752516
  49.9 41.5 %collective-permute-start.5 = (bf16[2,28,128,128]{3,2,1,0:T(8,128)(2,1)S(1)}, bf16[2,28,128,128]{3,2,1,0:T(8,128)(2,1)S(1)}, u32[]{:S(2)}, u32[]{:S(2)}) collective-permute-start(bf16[2,28,128,128]{3,2,1,0:T(8,128)(2,1)S(1)} %pack.3), channel_id=1, source_target_pairs={{0,6},{1,7},{2,4},{3,5},{4,2},{5,3},{6,0},{7,1},{8,14},{9,15},{10,... | collective-permute-start | bytes 5505032 | tf_op jit(solution)/shard_map/ppermute | solution.py:431
  54.1 42.2 %collective-permute-start.8 = (bf16[2,28,128,128]{3,2,1,0:T(8,128)(2,1)}, bf16[2,28,128,128]{3,2,1,0:T(8,128)(2,1)}, u32[]{:S(2)}, u32[]{:S(2)}) collective-permute-start(bf16[2,28,128,128]{3,2,1,0:T(8,128)(2,1)} %get-tuple-element.85.refs_4_), channel_id=1, source_target_pairs={{0,8},{1,9},{2,10},{3,11},{4,12},{5,13},{6,14},{7,15},{8,0},{9,1},... | collective-permute-start | bytes 5505032 | tf_op jit(solution)/shard_map/ppermute | solution.py:431
  55.8 40.6 %collective-permute-start.9 = (bf16[2,28,128,128]{3,2,1,0:T(8,128)(2,1)}, bf16[2,28,128,128]{3,2,1,0:T(8,128)(2,1)}, u32[]{:S(2)}, u32[]{:S(2)}) collective-permute-start(bf16[2,28,128,128]{3,2,1,0:T(8,128)(2,1)} %get-tuple-element.84.w_12.refs_13_.refs_1_), channel_id=1, source_target_pairs={{8,16},{9,17},{10,18},{11,19},{12,20},{13,21},{14,22},{15,23},{16,... | collective-permute-start | bytes 5505032 | tf_op jit(solution)/shard_map/ppermute | solution.py:431
  57.7 1.0 copy-start
  58.6 2.5 %collective-permute-start.6 = (bf16[28,128,128]{2,1,0:T(8,128)(2,1)S(1)}, bf16[28,128,128]{2,1,0:T(8,128)(2,1)S(1)}, u32[]{:S(2)}, u32[]{:S(2)}) collective-permute-start(bf16[28,128,128]{2,1,0:T(8,128)(2,1)S(1)} %copy-done.7), channel_id=1, source_target_pairs={{0,1},{1,0},{2,3},{3,2},{4,5},{5,4},{6,7},{7,6},{8,9},{9,8},{10,11... | collective-permute-start | bytes 2752520 | tf_op jit(solution)/shard_map/ppermute | solution.py:431
  58.6 32.7 %copy-start.6 = (bf16[28,128,128]{2,1,0:T(8,128)(2,1)}, bf16[28,128,128]{2,1,0:T(8,128)(2,1)S(1)}, u32[]{:S(2)}) copy-start(bf16[28,128,128]{2,1,0:T(8,128)(2,1)S(1)} %collective-permute-done.1.refs_15_.refs_3_) | copy-start | bytes 2752516
  58.6 3.8 %collective-permute-start.7 = (bf16[28,128,128]{2,1,0:T(8,128)(2,1)S(1)}, bf16[28,128,128]{2,1,0:T(8,128)(2,1)S(1)}, u32[]{:S(2)}, u32[]{:S(2)}) collective-permute-start(bf16[28,128,128]{2,1,0:T(8,128)(2,1)S(1)} %collective-permute-done.refs_3_.refs_0_.refs_1_), channel_id=1, source_target_pairs={{0,1},{1,0},{2,3},{3,2},{4,5},{5,4},{6,7},{7,6},{8,9},{9,8},{10,11... | collective-permute-start | bytes 2752520 | tf_op jit(solution)/shard_map/ppermute | solution.py:431
  61.1 0.9 copy-start.2
  62.4 0.9 copy-start.4
  93.1 21.4 %collective-permute-start.12 = (bf16[28,128,128]{2,1,0:T(8,128)(2,1)}, bf16[28,128,128]{2,1,0:T(8,128)(2,1)}, u32[]{:S(2)}, u32[]{:S(2)}) collective-permute-start(bf16[28,128,128]{2,1,0:T(8,128)(2,1)} %get-tuple-element.87.refs_8_), channel_id=1, source_target_pairs={{0,8},{1,9},{2,10},{3,11},{4,12},{5,13},{6,14},{7,15},{8,0},{9,1},... | collective-permute-start | bytes 2752520 | tf_op jit(solution)/shard_map/ppermute | solution.py:431
  94.7 19.8 %collective-permute-start.13 = (bf16[28,128,128]{2,1,0:T(8,128)(2,1)}, bf16[28,128,128]{2,1,0:T(8,128)(2,1)}, u32[]{:S(2)}, u32[]{:S(2)}) collective-permute-start(bf16[28,128,128]{2,1,0:T(8,128)(2,1)} %get-tuple-element.91.refs_14_.refs_2_), channel_id=1, source_target_pairs={{8,16},{9,17},{10,18},{11,19},{12,20},{13,21},{14,22},{15,23},{16,... | collective-permute-start | bytes 2752520 | tf_op jit(solution)/shard_map/ppermute | solution.py:431
  96.3 24.6 %collective-permute-start.10 = (bf16[2,28,128,128]{3,2,1,0:T(8,128)(2,1)}, bf16[2,28,128,128]{3,2,1,0:T(8,128)(2,1)}, u32[]{:S(2)}, u32[]{:S(2)}) collective-permute-start(bf16[2,28,128,128]{3,2,1,0:T(8,128)(2,1)} %get-tuple-element.85.refs_4_), channel_id=1, source_target_pairs={{0,1},{1,0},{2,3},{3,2},{4,5},{5,4},{6,7},{7,6},{8,9},{9,8},{10,11... | collective-permute-start | bytes 5505032 | tf_op jit(solution)/shard_map/ppermute | solution.py:431
  96.3 24.6 %collective-permute-start.11 = (bf16[2,28,128,128]{3,2,1,0:T(8,128)(2,1)}, bf16[2,28,128,128]{3,2,1,0:T(8,128)(2,1)}, u32[]{:S(2)}, u32[]{:S(2)}) collective-permute-start(bf16[2,28,128,128]{3,2,1,0:T(8,128)(2,1)} %collective-permute-done.8.refs_5_), channel_id=1, source_target_pairs={{0,1},{1,0},{2,3},{3,2},{4,5},{5,4},{6,7},{7,6},{8,9},{9,8},{10,11... | collective-permute-start | bytes 5505032 | tf_op jit(solution)/shard_map/ppermute | solution.py:431
  97.5 23.4 %collective-permute-start.14 = (bf16[28,128,128]{2,1,0:T(8,128)(2,1)}, bf16[28,128,128]{2,1,0:T(8,128)(2,1)}, u32[]{:S(2)}, u32[]{:S(2)}) collective-permute-start(bf16[28,128,128]{2,1,0:T(8,128)(2,1)} %get-tuple-element.87.refs_8_), channel_id=1, source_target_pairs={{0,1},{1,0},{2,3},{3,2},{4,5},{5,4},{6,7},{7,6},{8,9},{9,8},{10,11... | collective-permute-start | bytes 2752520 | tf_op jit(solution)/shard_map/ppermute | solution.py:431
  114.5 6.5 %collective-permute-start.15 = (bf16[28,128,128]{2,1,0:T(8,128)(2,1)}, bf16[28,128,128]{2,1,0:T(8,128)(2,1)}, u32[]{:S(2)}, u32[]{:S(2)}) collective-permute-start(bf16[28,128,128]{2,1,0:T(8,128)(2,1)} %collective-permute-done.12.refs_9_), channel_id=1, source_target_pairs={{0,1},{1,0},{2,3},{3,2},{4,5},{5,4},{6,7},{7,6},{8,9},{9,8},{10,11... | collective-permute-start | bytes 2752520 | tf_op jit(solution)/shard_map/ppermute | solution.py:431
  115.2 27.5 %collective-permute-start.16 = (bf16[28,128,128]{2,1,0:T(8,128)(2,1)}, bf16[28,128,128]{2,1,0:T(8,128)(2,1)}, u32[]{:S(2)}, u32[]{:S(2)}) collective-permute-start(bf16[28,128,128]{2,1,0:T(8,128)(2,1)} %get-tuple-element.100), channel_id=1, source_target_pairs={{8,0},{9,1},{10,2},{11,3},{12,4},{13,5},{14,6},{15,7},{24,8},{25,9... | collective-permute-start | bytes 2752520 | tf_op jit(solution)/shard_map/ppermute | solution.py:431
  120.9 40.6 %collective-permute-start.17 = (bf16[28,128,128]{2,1,0:T(8,128)(2,1)}, bf16[28,128,128]{2,1,0:T(8,128)(2,1)S(1)}, u32[]{:S(2)}, u32[]{:S(2)}) collective-permute-start(bf16[28,128,128]{2,1,0:T(8,128)(2,1)} %get-tuple-element.101), channel_id=1, source_target_pairs={{8,0},{9,1},{10,2},{11,3},{12,4},{13,5},{14,6},{15,7},{24,8},{25,9... | collective-permute-start | bytes 2752520 | tf_op jit(solution)/shard_map/ppermute | solution.py:431
  121.0 1.2 copy-start.3
  122.1 1.2 copy-start.5
  137.7 43.2 %collective-permute-start.21 = (bf16[28,128,128]{2,1,0:T(8,128)(2,1)}, bf16[28,128,128]{2,1,0:T(8,128)(2,1)S(1)}, u32[]{:S(2)}, u32[]{:S(2)}) collective-permute-start(bf16[28,128,128]{2,1,0:T(8,128)(2,1)} %reorder.3), channel_id=1, source_target_pairs={{8,0},{9,1},{10,2},{11,3},{12,4},{13,5},{14,6},{15,7},{24,8},{25,9... | collective-permute-start | bytes 2752520 | tf_op jit(solution)/shard_map/ppermute | solution.py:431
  140.7 26.2 %collective-permute-start.18 = (bf16[4,128,512]{2,1,0:T(8,128)(2,1)S(1)}, bf16[4,128,512]{2,1,0:T(8,128)(2,1)S(1)}, u32[]{:S(2)}, u32[]{:S(2)}) collective-permute-start(bf16[4,128,512]{2,1,0:T(8,128)(2,1)S(1)} %get-tuple-element.105.refs_6_), channel_id=1, source_target_pairs={{0,2},{1,3},{2,0},{3,1},{4,6},{5,7},{6,4},{7,5},{8,10},{9,11},{10,... | collective-permute-start | bytes 1572872 | tf_op jit(solution)/shard_map/ppermute | solution.py:431
  142.1 24.8 %collective-permute-start.19 = (bf16[4,128,512]{2,1,0:T(8,128)(2,1)S(1)}, bf16[4,128,512]{2,1,0:T(8,128)(2,1)S(1)}, u32[]{:S(2)}, u32[]{:S(2)}) collective-permute-start(bf16[4,128,512]{2,1,0:T(8,128)(2,1)S(1)} %get-tuple-element.106), channel_id=1, source_target_pairs={{0,4},{1,5},{2,6},{3,7},{4,0},{5,1},{6,2},{7,3},{8,12},{9,13},{10,... | collective-permute-start | bytes 1572872 | tf_op jit(solution)/shard_map/ppermute | solution.py:431
  142.6 24.3 %collective-permute-start.20 = (bf16[4,128,512]{2,1,0:T(8,128)(2,1)S(1)}, bf16[4,128,512]{2,1,0:T(8,128)(2,1)S(1)}, u32[]{:S(2)}, u32[]{:S(2)}) collective-permute-start(bf16[4,128,512]{2,1,0:T(8,128)(2,1)S(1)} %get-tuple-element.107), channel_id=1, source_target_pairs={{0,6},{1,7},{2,4},{3,5},{4,2},{5,3},{6,0},{7,1},{8,14},{9,15},{10,... | collective-permute-start | bytes 1572872 | tf_op jit(solution)/shard_map/ppermute | solution.py:431
  144.2 17.4 %copy-start.1 = (bf16[28,128,128]{2,1,0:T(8,128)(2,1)S(1)}, bf16[28,128,128]{2,1,0:T(8,128)(2,1)}, u32[]{:S(2)}) copy-start(bf16[28,128,128]{2,1,0:T(8,128)(2,1)} %copy-done) | copy-start | bytes 2752516
  166.9 17.5 %collective-permute-start.22 = (bf16[4,128,256]{2,1,0:T(8,128)(2,1)S(1)}, bf16[4,128,256]{2,1,0:T(8,128)(2,1)S(1)}, u32[]{:S(2)}, u32[]{:S(2)}) collective-permute-start(bf16[4,128,256]{2,1,0:T(8,128)(2,1)S(1)} %get-tuple-element.116), channel_id=1, source_target_pairs={{0,2},{1,3},{2,0},{3,1},{4,6},{5,7},{6,4},{7,5},{8,10},{9,11},{10,... | collective-permute-start | bytes 786440 | tf_op jit(solution)/shard_map/ppermute | solution.py:431
  168.2 16.2 %collective-permute-start.23 = (bf16[4,128,256]{2,1,0:T(8,128)(2,1)S(1)}, bf16[4,128,256]{2,1,0:T(8,128)(2,1)S(1)}, u32[]{:S(2)}, u32[]{:S(2)}) collective-permute-start(bf16[4,128,256]{2,1,0:T(8,128)(2,1)S(1)} %get-tuple-element.117), channel_id=1, source_target_pairs={{0,4},{1,5},{2,6},{3,7},{4,0},{5,1},{6,2},{7,3},{8,12},{9,13},{10,... | collective-permute-start | bytes 786440 | tf_op jit(solution)/shard_map/ppermute | solution.py:431
  168.7 15.7 %collective-permute-start.24 = (bf16[4,128,256]{2,1,0:T(8,128)(2,1)S(1)}, bf16[4,128,256]{2,1,0:T(8,128)(2,1)S(1)}, u32[]{:S(2)}, u32[]{:S(2)}) collective-permute-start(bf16[4,128,256]{2,1,0:T(8,128)(2,1)S(1)} %get-tuple-element.118), channel_id=1, source_target_pairs={{0,6},{1,7},{2,4},{3,5},{4,2},{5,3},{6,0},{7,1},{8,14},{9,15},{10,... | collective-permute-start | bytes 786440 | tf_op jit(solution)/shard_map/ppermute | solution.py:431
  184.4 9.3 %collective-permute-start.28 = (bf16[4,128,256]{2,1,0:T(8,128)(2,1)S(1)}, bf16[4,128,256]{2,1,0:T(8,128)(2,1)S(1)}, u32[]{:S(2)}, u32[]{:S(2)}) collective-permute-start(bf16[4,128,256]{2,1,0:T(8,128)(2,1)S(1)} %get-tuple-element.126), channel_id=1, source_target_pairs={{0,2},{1,3},{2,0},{3,1},{4,6},{5,7},{6,4},{7,5},{8,10},{9,11},{10,... | collective-permute-start | bytes 786440 | tf_op jit(solution)/shard_map/ppermute | solution.py:431
  185.7 13.3 %collective-permute-start.29 = (bf16[4,128,256]{2,1,0:T(8,128)(2,1)S(1)}, bf16[4,128,256]{2,1,0:T(8,128)(2,1)S(1)}, u32[]{:S(2)}, u32[]{:S(2)}) collective-permute-start(bf16[4,128,256]{2,1,0:T(8,128)(2,1)S(1)} %get-tuple-element.127), channel_id=1, source_target_pairs={{0,4},{1,5},{2,6},{3,7},{4,0},{5,1},{6,2},{7,3},{8,12},{9,13},{10,... | collective-permute-start | bytes 786440 | tf_op jit(solution)/shard_map/ppermute | solution.py:431
  186.2 12.8 %collective-permute-start.30 = (bf16[4,128,256]{2,1,0:T(8,128)(2,1)S(1)}, bf16[4,128,256]{2,1,0:T(8,128)(2,1)S(1)}, u32[]{:S(2)}, u32[]{:S(2)}) collective-permute-start(bf16[4,128,256]{2,1,0:T(8,128)(2,1)S(1)} %get-tuple-element.128.refs_3_), channel_id=1, source_target_pairs={{0,6},{1,7},{2,4},{3,5},{4,2},{5,3},{6,0},{7,1},{8,14},{9,15},{10,... | collective-permute-start | bytes 786440 | tf_op jit(solution)/shard_map/ppermute | solution.py:431
  189.9 11.5 %collective-permute-start.25 = (bf16[128,768]{1,0:T(8,128)(2,1)S(1)}, bf16[128,768]{1,0:T(8,128)(2,1)S(1)}, u32[]{:S(2)}, u32[]{:S(2)}) collective-permute-start(bf16[128,768]{1,0:T(8,128)(2,1)S(1)} %get-tuple-element.123), channel_id=1, source_target_pairs={{0,1},{1,0},{2,3},{3,2},{4,5},{5,4},{6,7},{7,6},{8,9},{9,8},{10,11... | collective-permute-start | bytes 589832 | tf_op jit(solution)/shard_map/ppermute | solution.py:431
  190.0 11.6 %collective-permute-start.26 = (bf16[128,768]{1,0:T(8,128)(2,1)S(1)}, bf16[128,768]{1,0:T(8,128)(2,1)S(1)}, u32[]{:S(2)}, u32[]{:S(2)}) collective-permute-start(bf16[128,768]{1,0:T(8,128)(2,1)S(1)} %get-tuple-element.124), channel_id=1, source_target_pairs={{0,8},{1,9},{2,10},{3,11},{4,12},{5,13},{6,14},{7,15},{8,0},{9,1},... | collective-permute-start | bytes 589832 | tf_op jit(solution)/shard_map/ppermute | solution.py:431
  193.7 7.8 %collective-permute-start.27 = (bf16[128,768]{1,0:T(8,128)(2,1)S(1)}, bf16[128,768]{1,0:T(8,128)(2,1)S(1)}, u32[]{:S(2)}, u32[]{:S(2)}) collective-permute-start(bf16[128,768]{1,0:T(8,128)(2,1)S(1)} %get-tuple-element.125), channel_id=1, source_target_pairs={{0,9},{1,8},{2,11},{3,10},{4,13},{5,12},{6,15},{7,14},{8,1},{9,0},... | collective-permute-start | bytes 589832 | tf_op jit(solution)/shard_map/ppermute | solution.py:431
  199.2 2.4 %collective-permute-start.31 = (bf16[128,256]{1,0:T(8,128)(2,1)S(1)}, bf16[128,256]{1,0:T(8,128)(2,1)S(1)}, u32[]{:S(2)}, u32[]{:S(2)}) collective-permute-start(bf16[128,256]{1,0:T(8,128)(2,1)S(1)} %get-tuple-element.130), channel_id=1, source_target_pairs={{0,1},{1,0},{2,3},{3,2},{4,5},{5,4},{6,7},{7,6},{8,9},{9,8},{10,11... | collective-permute-start | bytes 196616 | tf_op jit(solution)/shard_map/ppermute | solution.py:431
  199.2 4.9 %collective-permute-start.32 = (bf16[128,256]{1,0:T(8,128)(2,1)S(1)}, bf16[128,256]{1,0:T(8,128)(2,1)S(1)}, u32[]{:S(2)}, u32[]{:S(2)}) collective-permute-start(bf16[128,256]{1,0:T(8,128)(2,1)S(1)} %get-tuple-element.131), channel_id=1, source_target_pairs={{0,8},{1,9},{2,10},{3,11},{4,12},{5,13},{6,14},{7,15},{8,0},{9,1},... | collective-permute-start | bytes 196616 | tf_op jit(solution)/shard_map/ppermute | solution.py:431
  201.4 4.0 %collective-permute-start.33 = (bf16[128,256]{1,0:T(8,128)(2,1)S(1)}, bf16[128,256]{1,0:T(8,128)(2,1)S(1)}, u32[]{:S(2)}, u32[]{:S(2)}) collective-permute-start(bf16[128,256]{1,0:T(8,128)(2,1)S(1)} %get-tuple-element.132), channel_id=1, source_target_pairs={{0,9},{1,8},{2,11},{3,10},{4,13},{5,12},{6,15},{7,14},{8,1},{9,0},... | collective-permute-start | bytes 196616 | tf_op jit(solution)/shard_map/ppermute | solution.py:431

commit v14 on v13

--- a/solution.py
+++ b/solution.py
@@ -151,14 +151,16 @@
 
 
 def reorder_kernel(count, order_ref, packed, w_12, *refs):
-    outs, (held, in_sem, out_sem) = refs[-3 - count : -3], refs[-3:]
+    out, held, in_sem, out_sem = refs
     into = [
         pltpu.make_async_copy(source, held.at[at], in_sem.at[at])
         for at, source in enumerate((packed.at[0], w_12.at[0], w_12.at[1], packed.at[1]))
     ]
     out_of = [
-        pltpu.make_async_copy(held.at[order_ref[at]], out, out_sem.at[at])
-        for at, out in enumerate(outs)
+        pltpu.make_async_copy(
+            held.at[order_ref[at]], out if count == 1 else out.at[at], out_sem.at[at]
+        )
+        for at in range(count)
     ]
     for copy in into:
         copy.start()
@@ -174,10 +176,10 @@
     shape, count = packed.shape[1:], order.shape[0]
     return pl.pallas_call(
         functools.partial(reorder_kernel, count),
-        out_shape=[pltpu.HBM(shape, packed.dtype)] * count,
+        out_shape=pltpu.HBM(shape if count == 1 else (count,) + shape, packed.dtype),
         in_specs=[pl.BlockSpec(memory_space=pltpu.SMEM)]
         + [pl.BlockSpec(memory_space=pl.ANY)] * 2,
-        out_specs=[pl.BlockSpec(memory_space=pl.ANY)] * count,
+        out_specs=pl.BlockSpec(memory_space=pl.ANY),
         scratch_shapes=[
             pltpu.VMEM((4,) + shape, packed.dtype),
             pltpu.SemaphoreType.DMA((4,)),
@@ -462,12 +464,12 @@
     a_12, pair_12, a_3 = lax.optimization_barrier((a_12, pair_12, a_3))
     a_12, pair_12, mid_12, got_3 = lax.optimization_barrier((a_12, pair_12, mid_12, got_3))
     core_12, core_pair_12 = to_core(a_12), to_core(pair_12)
-    ordered_1, ordered_2 = reorder(order[:2], got_3, w_12)
+    ordered_12 = reorder(order[:2], got_3, w_12)
     mid_3 = to_mid(w_3)
-    ordered_1, ordered_2, pair_3, mid_3, mid_12 = lax.optimization_barrier(
-        (ordered_1, ordered_2, pair_3, mid_3, mid_12)
+    ordered_12, pair_3, mid_3, mid_12 = lax.optimization_barrier(
+        (ordered_12, pair_3, mid_3, mid_12)
     )
-    next_1, next_2 = to_next(ordered_1), to_next(ordered_2)
+    next_12 = to_next(ordered_12)
     core_3, core_pair_3 = to_core(a_3), to_core(pair_3)
 
     a_0, w_0, a_12, w_12, a_3, w_3 = far([a_0, w_0, a_12, w_12, a_3, w_3])
@@ -504,10 +506,10 @@
     rows_stack, *own = stack_product(mid, places, a_blocks, [w_own, w_mid])
     own = totals_of(mid, [w_own, w_mid], ([0],), (own[0],)) + own
     own[1], got_3 = lax.optimization_barrier((own[1], got_3))
-    (ordered_3,) = reorder(order[2:], got_3, w_12)
+    ordered_3 = reorder(order[2:], got_3, w_12)
     next_3 = to_next(ordered_3)
     own_sums = across_plane(own)
-    first, one, two, three = [(block, None) for block in (next_0, next_1, next_2, next_3)]
+    first, one, two, three = (next_0, None), (next_12, 0), (next_12, 1), (next_3, None)
     w_low = [[first, one], [one, first], [one, two], [one, two]]
     w_high = [[two, three], [two, three], [first, three], [three, first]]
     low = totals_of(at_plane, w_low, ([3, 1, 2, 0],), (own[0],))

time: 208 us -> 208 us (level)
    ppermute x34 -> x33, waiting for transfers between devices: 110 us -> 109 us  [send(): return lax.ppermute(array, 'fsdp', perm=perm)]
    ppermute x34 -> x33, starting transfers between devices: 42.7 us -> 42.6 us  [send(): return lax.ppermute(array, 'fsdp', perm=perm)]
  transfers between devices with their start and end apart: 34 -> 33, of which waited for: 13 -> 15; matrix products, arithmetic and copies ran while one was open for 1% -> 1% of each run, Pallas kernels for 19% -> 20%
where the time goes in v14:
time: 208 us
  waiting for transfers between devices  109 us (52%)
  Pallas kernels  48.9 us (24%)
  starting transfers between devices  42.6 us (20%)
  local copies, waits for them, and re-layouts  6.52 us (3%)
    ppermute x33, waiting for transfers between devices, send(): return lax.ppermute(array, 'fsdp', perm=perm)  109 us
    ppermute x33, starting transfers between devices, send(): return lax.ppermute(array, 'fsdp', perm=perm)  42.6 us
    pallas_call x4, Pallas kernels, product(): pl.pallas_call(functools.partial(product_kernel, [places[group] for group...  16 us
    pallas_call x1, Pallas kernels, stack_product(): pl.pallas_call(functools.partial(stack_product_kernel, places, a_at, w_at...  11 us
    pallas_call x2, Pallas kernels, pack(): pl.pallas_call(functools.partial(pack_kernel, apart, len(steps)), out_sha...  8.3 us
    pallas_call x2, Pallas kernels, reorder(): pl.pallas_call(functools.partial(reorder_kernel, count), out_shape=pltpu....  6.79 us
    unnamed x16, local copies, waits for them, and re-layouts  5.18 us
  transfers between devices with their start and end apart: 33, of which 15 were waited for; matrix products, arithmetic and copies ran while one was open for 1% of the time, Pallas kernels for 20%

profile of v14, /device:TPU:0, one launch (start us, length us, event | category | flops | bytes accessed | tf_op | source)
XLA Modules:
  0.0 207.5 jit_solution(4007334668560364332)
XLA Ops:
  0.0 5.4 %pack.2 = (bf16[28,128,128]{2,1,0:T(8,128)(2,1)}, bf16[28,128,128]{2,1,0:T(8,128)(2,1)}, bf16[2,28,128,128]{3,2,1,0:T(8,128)(2,1)S(1)}, bf16[2,28,128,128]{3,2,1,0:T(8,128)(2,1)S(1)}) custom-call(s32[1]{0:T(128)} %bitcast.3.plane_ref.choice_ref, bf16[128,14336]{1,0:T(8,128)(2,1)} %refs_0_.3, bf16[128,14336]{1,0:T(8,128)(2,1)} %refs_1_.3, ...), custom_call_target="tpu_custom_call" | custom-call | bytes 13762560 | tf_op jit(solution)/shard_map/pack/pallas_call | solution.py:63
  5.4 3.0 %collective-permute-start.3 = (bf16[2,28,128,128]{3,2,1,0:T(8,128)(2,1)S(1)}, bf16[2,28,128,128]{3,2,1,0:T(8,128)(2,1)S(1)}, u32[]{:S(2)}, u32[]{:S(2)}) collective-permute-start(bf16[2,28,128,128]{3,2,1,0:T(8,128)(2,1)S(1)} %get-tuple-element.69), channel_id=1, source_target_pairs={{0,2},{1,3},{2,0},{3,1},{4,6},{5,7},{6,4},{7,5},{8,10},{9,11},{10,... | collective-permute-start | bytes 5505032 | tf_op jit(solution)/shard_map/ppermute | solution.py:433
  8.4 1.5 collective-permute-start.4
  9.9 1.6 collective-permute-start
  11.5 2.6 %collective-permute-start.2 = (bf16[28,128,128]{2,1,0:T(8,128)(2,1)}, bf16[28,128,128]{2,1,0:T(8,128)(2,1)S(1)}, u32[]{:S(2)}, u32[]{:S(2)}) collective-permute-start(bf16[28,128,128]{2,1,0:T(8,128)(2,1)} %get-tuple-element.67.refs_12_.refs_0_), channel_id=1, source_target_pairs={{8,0},{9,1},{10,2},{11,3},{12,4},{13,5},{14,6},{15,7},{24,8},{25,9... | collective-permute-start | bytes 2752520 | tf_op jit(solution)/shard_map/ppermute | solution.py:433
  14.8 18.6 %collective-permute-done.refs_3_.refs_0_.refs_1_ = bf16[28,128,128]{2,1,0:T(8,128)(2,1)S(1)} collective-permute-done((bf16[28,128,128]{2,1,0:T(8,128)(2,1)}, bf16[28,128,128]{2,1,0:T(8,128)(2,1)S(1)}, u32[]{:S(2)}, u32[]{:S(2)}) %collective-permute-start) | collective-permute-done | bytes 917536 | tf_op jit(solution)/shard_map/ppermute | solution.py:433
  33.4 2.9 %pack.3 = bf16[2,28,128,128]{3,2,1,0:T(8,128)(2,1)S(1)} custom-call(s32[1]{0:T(128)} %bitcast.3.plane_ref.choice_ref, bf16[128,14336]{1,0:T(8,128)(2,1)} %refs_0_.3, bf16[128,14336]{1,0:T(8,128)(2,1)} %refs_1_.3, bf16[14336,128]{1,0:T(8,128)(2,1)} %refs_2_.3, bf16[28,128,128]{2,1,0:T(8,128)(2,1)S(1)} %collective-permute-done.refs_3_.refs_0_.refs_1_), custom_call_target="tpu_custom_call" | custom-call | bytes 4587520 | tf_op jit(solution)/shard_map/pack/pallas_call | solution.py:63
  36.3 12.1 %collective-permute-done.3.one = bf16[2,28,128,128]{3,2,1,0:T(8,128)(2,1)S(1)} collective-permute-done((bf16[2,28,128,128]{3,2,1,0:T(8,128)(2,1)S(1)}, bf16[2,28,128,128]{3,2,1,0:T(8,128)(2,1)S(1)}, u32[]{:S(2)}, u32[]{:S(2)}) %collective-permute-start.3) | collective-permute-done | bytes 1835040 | tf_op jit(solution)/shard_map/ppermute | solution.py:433
  48.4 1.5 collective-permute-done.4.two
  49.9 1.5 collective-permute-start.5
  51.4 2.8 %unpack_pair.1 = (bf16[2,28,128,128]{3,2,1,0:T(8,128)(2,1)}, bf16[2,28,128,128]{3,2,1,0:T(8,128)(2,1)}) custom-call(bf16[2,28,128,128]{3,2,1,0:T(8,128)(2,1)S(1)} %collective-permute-done.3.one, bf16[2,28,128,128]{3,2,1,0:T(8,128)(2,1)S(1)} %collective-permute-done.4.two, bf16[28,128,128]{2,1,0:T(8,128)(2,1)S(1)} %collective-permute-done.refs_3_.refs_0_.refs_1_), custom_call_target="tpu_custom_call" | custom-call | bytes 7340032 | tf_op jit(solution)/shard_map/unpack_pair/pallas_call | solution.py:106
  54.2 1.6 collective-permute-start.8
  55.8 1.9 collective-permute-start.9
  57.8 0.9 copy-done
  59.2 2.0 collective-permute-done.6.refs_2_
  61.2 0.9 copy-done.2
  62.5 0.9 copy-done.4
  63.4 27.9 %collective-permute-done.5.packed = bf16[2,28,128,128]{3,2,1,0:T(8,128)(2,1)S(1)} collective-permute-done((bf16[2,28,128,128]{3,2,1,0:T(8,128)(2,1)S(1)}, bf16[2,28,128,128]{3,2,1,0:T(8,128)(2,1)S(1)}, u32[]{:S(2)}, u32[]{:S(2)}) %collective-permute-start.5) | collective-permute-done | bytes 1835040 | tf_op jit(solution)/shard_map/ppermute | solution.py:433
  91.4 1.7 unpack.1
  93.1 1.6 collective-permute-start.12
  94.7 1.6 collective-permute-start.13
  97.6 3.5 %reorder.2 = bf16[2,28,128,128]{3,2,1,0:T(8,128)(2,1)} custom-call(s32[2]{0:T(128)S(1)} %slice_bitcast_fusion.order_ref, bf16[2,28,128,128]{3,2,1,0:T(8,128)(2,1)S(1)} %collective-permute-done.5.packed, bf16[2,28,128,128]{3,2,1,0:T(8,128)(2,1)} %get-tuple-element.81.w_12.refs_13_.refs_1_), custom_call_target="tpu_custom_call" | custom-call | bytes 7340032 | tf_op jit(solution)/shard_map/reorder/pallas_call | solution.py:177
  101.1 13.5 %collective-permute-done.12.refs_9_ = bf16[28,128,128]{2,1,0:T(8,128)(2,1)} collective-permute-done((bf16[28,128,128]{2,1,0:T(8,128)(2,1)}, bf16[28,128,128]{2,1,0:T(8,128)(2,1)}, u32[]{:S(2)}, u32[]{:S(2)}) %collective-permute-start.12) | collective-permute-done | bytes 917536 | tf_op jit(solution)/shard_map/ppermute | solution.py:433
  114.6 5.8 %collective-permute-start.16 = (bf16[2,28,128,128]{3,2,1,0:T(8,128)(2,1)}, bf16[2,28,128,128]{3,2,1,0:T(8,128)(2,1)}, u32[]{:S(2)}, u32[]{:S(2)}) collective-permute-start(bf16[2,28,128,128]{3,2,1,0:T(8,128)(2,1)} %reorder.2), channel_id=1, source_target_pairs={{8,0},{9,1},{10,2},{11,3},{12,4},{13,5},{14,6},{15,7},{24,8},{25,9... | collective-permute-start | bytes 5505032 | tf_op jit(solution)/shard_map/ppermute | solution.py:433
  121.0 1.2 copy-done.3
  122.2 1.2 copy-done.5
  123.4 11.0 %stack_product.1 = (bf16[28,2048,128]{2,1,0:T(8,128)(2,1)S(1)}, bf16[4,128,512]{2,1,0:T(8,128)(2,1)S(1)}, bf16[4,128,512]{2,1,0:T(8,128)(2,1)S(1)}, bf16[4,128,512]{2,1,0:T(8,128)(2,1)S(1)}) custom-call(s32[1]{0:T(128)} %bitcast.2.choice_ref, bf16[28,128,128]{2,1,0:T(8,128)(2,1)} %get-tuple-element.66.refs_0_, ...), custom_call_target="tpu_custom_call" | custom-call | flops 5637144576 | bytes 18350080 | tf_op jit(solution)/shard_map/stack_product/pallas_call | solution.py:269
  134.4 3.3 %reorder.3 = bf16[28,128,128]{2,1,0:T(8,128)(2,1)} custom-call(s32[1]{0:T(128)} %bitcast.5.order_ref, bf16[2,28,128,128]{3,2,1,0:T(8,128)(2,1)S(1)} %collective-permute-done.5.packed, bf16[2,28,128,128]{3,2,1,0:T(8,128)(2,1)} %get-tuple-element.81.w_12.refs_13_.refs_1_), custom_call_target="tpu_custom_call" | custom-call | bytes 7340032 | tf_op jit(solution)/shard_map/reorder/pallas_call | solution.py:177
  137.7 3.0 %collective-permute-start.20 = (bf16[28,128,128]{2,1,0:T(8,128)(2,1)}, bf16[28,128,128]{2,1,0:T(8,128)(2,1)S(1)}, u32[]{:S(2)}, u32[]{:S(2)}) collective-permute-start(bf16[28,128,128]{2,1,0:T(8,128)(2,1)} %reorder.3), channel_id=1, source_target_pairs={{8,0},{9,1},{10,2},{11,3},{12,4},{13,5},{14,6},{15,7},{24,8},{25,9... | collective-permute-start | bytes 2752520 | tf_op jit(solution)/shard_map/ppermute | solution.py:433
  140.7 1.4 collective-permute-start.17
  142.6 1.6 collective-permute-start.19
  144.2 4.2 %product.4.refs_2_.refs_0_ = f32[4,128,512]{2,1,0:T(8,128)S(1)} custom-call(s32[1]{0:T(128)} %bitcast.2.choice_ref, bf16[28,2048,128]{2,1,0:T(8,128)(2,1)S(1)} %get-tuple-element.92.a, bf16[28,128,128]{2,1,0:T(8,128)(2,1)} %get-tuple-element.67.refs_12_.refs_0_, bf16[2,28,128,128]{3,2,1,0:T(8,128)(2,1)} %get-tuple-element.81.w_12.refs_13_.refs_1_, ...), custom_call_target="tpu_custom_call" | custom-call | flops 1879048192 | bytes 7340032 | tf_op jit(solution)/shard_map/product/pallas_call | solution.py:338
  148.3 12.7 %collective-permute-done.16.refs_1_.refs_0_ = bf16[2,28,128,128]{3,2,1,0:T(8,128)(2,1)} collective-permute-done((bf16[2,28,128,128]{3,2,1,0:T(8,128)(2,1)}, bf16[2,28,128,128]{3,2,1,0:T(8,128)(2,1)}, u32[]{:S(2)}, u32[]{:S(2)}) %collective-permute-start.16) | collective-permute-done | bytes 1835040 | tf_op jit(solution)/shard_map/ppermute | solution.py:433
  161.0 5.3 %product.5 = (bf16[4,128,256]{2,1,0:T(8,128)(2,1)S(1)}, bf16[4,128,256]{2,1,0:T(8,128)(2,1)S(1)}, bf16[4,128,256]{2,1,0:T(8,128)(2,1)S(1)}, f32[4,128,256]{2,1,0:T(8,128)S(1)}) custom-call(s32[1]{0:T(128)} %bitcast.3.plane_ref.choice_ref, bf16[28,2048,128]{2,1,0:T(8,128)(2,1)S(1)} %get-tuple-element.92.a, bf16[28,128,128]{2,1,0:T(8,128)(2,1)S(1)} %copy-done.1, ...), custom_call_target="tpu_custom_call" | custom-call | flops 3758096384 | bytes 16515072 | tf_op jit(solution)/shard_map/product/pallas_call | solution.py:338
  166.7 0.9 collective-permute-start.21
  167.7 0.8 collective-permute-start.22
  168.5 1.8 collective-permute-start.23
  170.2 10.1 %collective-permute-done.20.refs_1_ = bf16[28,128,128]{2,1,0:T(8,128)(2,1)S(1)} collective-permute-done((bf16[28,128,128]{2,1,0:T(8,128)(2,1)}, bf16[28,128,128]{2,1,0:T(8,128)(2,1)S(1)}, u32[]{:S(2)}, u32[]{:S(2)}) %collective-permute-start.20) | collective-permute-done | bytes 917536 | tf_op jit(solution)/shard_map/ppermute | solution.py:433
  180.3 4.2 %product.6 = (bf16[4,128,256]{2,1,0:T(8,128)(2,1)S(1)}, bf16[4,128,256]{2,1,0:T(8,128)(2,1)S(1)}, bf16[4,128,256]{2,1,0:T(8,128)(2,1)S(1)}) custom-call(s32[1]{0:T(128)} %bitcast.3.plane_ref.choice_ref, bf16[28,2048,128]{2,1,0:T(8,128)(2,1)S(1)} %get-tuple-element.92.a, bf16[2,28,128,128]{3,2,1,0:T(8,128)(2,1)} %collective-permute-done.16.refs_1_.refs_0_, ...), custom_call_target="tpu_custom_call" | custom-call | flops 2818572288 | bytes 12845056 | tf_op jit(solution)/shard_map/product/pallas_call | solution.py:338
  184.5 1.5 collective-permute-start.27
  186.0 2.1 collective-permute-start.29
  188.1 2.3 %product.7.refs_8_.refs_0_ = f32[4,128,256]{2,1,0:T(8,128)S(1)} custom-call(s32[1]{0:T(128)} %bitcast.3.plane_ref.choice_ref, bf16[28,2048,128]{2,1,0:T(8,128)(2,1)S(1)} %get-tuple-element.92.a, bf16[2,28,128,128]{3,2,1,0:T(8,128)(2,1)} %collective-permute-done.16.refs_1_.refs_0_, bf16[28,128,128]{2,1,0:T(8,128)(2,1)S(1)} %collective-permute-done.20.refs_1_, ...), custom_call_target="tpu_custom_call" | custom-call | flops 939524096 | bytes 5505024 | tf_op jit(solution)/shard_map/product/pallas_call | solution.py:338
  190.8 2.2 %collective-permute-start.25 = (bf16[128,768]{1,0:T(8,128)(2,1)S(1)}, bf16[128,768]{1,0:T(8,128)(2,1)S(1)}, u32[]{:S(2)}, u32[]{:S(2)}) collective-permute-start(bf16[128,768]{1,0:T(8,128)(2,1)S(1)} %get-tuple-element.118), channel_id=1, source_target_pairs={{0,8},{1,9},{2,10},{3,11},{4,12},{5,13},{6,14},{7,15},{8,0},{9,1},... | collective-permute-start | bytes 589832 | tf_op jit(solution)/shard_map/ppermute | solution.py:433
  193.8 5.5 %collective-permute-done.28.refs_2_ = bf16[4,128,256]{2,1,0:T(8,128)(2,1)S(1)} collective-permute-done((bf16[4,128,256]{2,1,0:T(8,128)(2,1)S(1)}, bf16[4,128,256]{2,1,0:T(8,128)(2,1)S(1)}, u32[]{:S(2)}, u32[]{:S(2)}) %collective-permute-start.28) | collective-permute-done | bytes 262176 | tf_op jit(solution)/shard_map/ppermute | solution.py:433
  199.5 2.2 %collective-permute-start.31 = (bf16[128,256]{1,0:T(8,128)(2,1)S(1)}, bf16[128,256]{1,0:T(8,128)(2,1)S(1)}, u32[]{:S(2)}, u32[]{:S(2)}) collective-permute-start(bf16[128,256]{1,0:T(8,128)(2,1)S(1)} %get-tuple-element.125), channel_id=1, source_target_pairs={{0,8},{1,9},{2,10},{3,11},{4,12},{5,13},{6,14},{7,15},{8,0},{9,1},... | collective-permute-start | bytes 196616 | tf_op jit(solution)/shard_map/ppermute | solution.py:433
  202.5 1.9 collective-permute-done.31.refs_6_
  204.4 1.4 collective-permute-done.32.refs_7_
  205.7 1.8 assemble.1
  (52 shorter events, 6.7 us)
Async XLA Ops:
  5.4 43.0 %collective-permute-start.3 = (bf16[2,28,128,128]{3,2,1,0:T(8,128)(2,1)S(1)}, bf16[2,28,128,128]{3,2,1,0:T(8,128)(2,1)S(1)}, u32[]{:S(2)}, u32[]{:S(2)}) collective-permute-start(bf16[2,28,128,128]{3,2,1,0:T(8,128)(2,1)S(1)} %get-tuple-element.69), channel_id=1, source_target_pairs={{0,2},{1,3},{2,0},{3,1},{4,6},{5,7},{6,4},{7,5},{8,10},{9,11},{10,... | collective-permute-start | bytes 5505032 | tf_op jit(solution)/shard_map/ppermute | solution.py:433
  8.4 41.5 %collective-permute-start.4 = (bf16[2,28,128,128]{3,2,1,0:T(8,128)(2,1)S(1)}, bf16[2,28,128,128]{3,2,1,0:T(8,128)(2,1)S(1)}, u32[]{:S(2)}, u32[]{:S(2)}) collective-permute-start(bf16[2,28,128,128]{3,2,1,0:T(8,128)(2,1)S(1)} %get-tuple-element.70), channel_id=1, source_target_pairs={{0,4},{1,5},{2,6},{3,7},{4,0},{5,1},{6,2},{7,3},{8,12},{9,13},{10,... | collective-permute-start | bytes 5505032 | tf_op jit(solution)/shard_map/ppermute | solution.py:433
  9.9 23.5 %collective-permute-start = (bf16[28,128,128]{2,1,0:T(8,128)(2,1)}, bf16[28,128,128]{2,1,0:T(8,128)(2,1)S(1)}, u32[]{:S(2)}, u32[]{:S(2)}) collective-permute-start(bf16[28,128,128]{2,1,0:T(8,128)(2,1)} %get-tuple-element.66.refs_0_), channel_id=1, source_target_pairs={{0,8},{1,9},{2,10},{3,11},{4,12},{5,13},{6,14},{7,15},{8,0},{9,1},... | collective-permute-start | bytes 2752520 | tf_op jit(solution)/shard_map/ppermute | solution.py:433
  11.5 46.2 %collective-permute-start.2 = (bf16[28,128,128]{2,1,0:T(8,128)(2,1)}, bf16[28,128,128]{2,1,0:T(8,128)(2,1)S(1)}, u32[]{:S(2)}, u32[]{:S(2)}) collective-permute-start(bf16[28,128,128]{2,1,0:T(8,128)(2,1)} %get-tuple-element.67.refs_12_.refs_0_), channel_id=1, source_target_pairs={{8,0},{9,1},{10,2},{11,3},{12,4},{13,5},{14,6},{15,7},{24,8},{25,9... | collective-permute-start | bytes 2752520 | tf_op jit(solution)/shard_map/ppermute | solution.py:433
  14.1 44.6 %collective-permute-start.1 = (bf16[28,128,128]{2,1,0:T(8,128)(2,1)}, bf16[28,128,128]{2,1,0:T(8,128)(2,1)S(1)}, u32[]{:S(2)}, u32[]{:S(2)}) collective-permute-start(bf16[28,128,128]{2,1,0:T(8,128)(2,1)} %get-tuple-element.67.refs_12_.refs_0_), channel_id=1, source_target_pairs={{8,16},{9,17},{10,18},{11,19},{12,20},{13,21},{14,22},{15,23},{16,... | collective-permute-start | bytes 2752520 | tf_op jit(solution)/shard_map/ppermute | solution.py:433
  36.3 22.4 %copy-start.7 = (bf16[28,128,128]{2,1,0:T(8,128)(2,1)S(1)}, bf16[28,128,128]{2,1,0:T(8,128)(2,1)}, u32[]{:S(2)}) copy-start(bf16[28,128,128]{2,1,0:T(8,128)(2,1)} %get-tuple-element.66.refs_0_) | copy-start | bytes 2752516
  49.9 41.5 %collective-permute-start.5 = (bf16[2,28,128,128]{3,2,1,0:T(8,128)(2,1)S(1)}, bf16[2,28,128,128]{3,2,1,0:T(8,128)(2,1)S(1)}, u32[]{:S(2)}, u32[]{:S(2)}) collective-permute-start(bf16[2,28,128,128]{3,2,1,0:T(8,128)(2,1)S(1)} %pack.3), channel_id=1, source_target_pairs={{0,6},{1,7},{2,4},{3,5},{4,2},{5,3},{6,0},{7,1},{8,14},{9,15},{10,... | collective-permute-start | bytes 5505032 | tf_op jit(solution)/shard_map/ppermute | solution.py:433
  54.2 42.1 %collective-permute-start.8 = (bf16[2,28,128,128]{3,2,1,0:T(8,128)(2,1)}, bf16[2,28,128,128]{3,2,1,0:T(8,128)(2,1)}, u32[]{:S(2)}, u32[]{:S(2)}) collective-permute-start(bf16[2,28,128,128]{3,2,1,0:T(8,128)(2,1)} %get-tuple-element.82.refs_4_), channel_id=1, source_target_pairs={{0,8},{1,9},{2,10},{3,11},{4,12},{5,13},{6,14},{7,15},{8,0},{9,1},... | collective-permute-start | bytes 5505032 | tf_op jit(solution)/shard_map/ppermute | solution.py:433
  55.8 40.5 %collective-permute-start.9 = (bf16[2,28,128,128]{3,2,1,0:T(8,128)(2,1)}, bf16[2,28,128,128]{3,2,1,0:T(8,128)(2,1)}, u32[]{:S(2)}, u32[]{:S(2)}) collective-permute-start(bf16[2,28,128,128]{3,2,1,0:T(8,128)(2,1)} %get-tuple-element.81.w_12.refs_13_.refs_1_), channel_id=1, source_target_pairs={{8,16},{9,17},{10,18},{11,19},{12,20},{13,21},{14,22},{15,23},{16,... | collective-permute-start | bytes 5505032 | tf_op jit(solution)/shard_map/ppermute | solution.py:433
  57.8 0.9 copy-start
  58.7 2.5 %collective-permute-start.6 = (bf16[28,128,128]{2,1,0:T(8,128)(2,1)S(1)}, bf16[28,128,128]{2,1,0:T(8,128)(2,1)S(1)}, u32[]{:S(2)}, u32[]{:S(2)}) collective-permute-start(bf16[28,128,128]{2,1,0:T(8,128)(2,1)S(1)} %copy-done.7), channel_id=1, source_target_pairs={{0,1},{1,0},{2,3},{3,2},{4,5},{5,4},{6,7},{7,6},{8,9},{9,8},{10,11... | collective-permute-start | bytes 2752520 | tf_op jit(solution)/shard_map/ppermute | solution.py:433
  58.7 32.7 %copy-start.6 = (bf16[28,128,128]{2,1,0:T(8,128)(2,1)}, bf16[28,128,128]{2,1,0:T(8,128)(2,1)S(1)}, u32[]{:S(2)}) copy-start(bf16[28,128,128]{2,1,0:T(8,128)(2,1)S(1)} %collective-permute-done.1.refs_15_.refs_3_) | copy-start | bytes 2752516
  58.7 3.8 %collective-permute-start.7 = (bf16[28,128,128]{2,1,0:T(8,128)(2,1)S(1)}, bf16[28,128,128]{2,1,0:T(8,128)(2,1)S(1)}, u32[]{:S(2)}, u32[]{:S(2)}) collective-permute-start(bf16[28,128,128]{2,1,0:T(8,128)(2,1)S(1)} %collective-permute-done.refs_3_.refs_0_.refs_1_), channel_id=1, source_target_pairs={{0,1},{1,0},{2,3},{3,2},{4,5},{5,4},{6,7},{7,6},{8,9},{9,8},{10,11... | collective-permute-start | bytes 2752520 | tf_op jit(solution)/shard_map/ppermute | solution.py:433
  61.2 0.9 copy-start.2
  62.5 0.9 copy-start.4
  93.1 21.5 %collective-permute-start.12 = (bf16[28,128,128]{2,1,0:T(8,128)(2,1)}, bf16[28,128,128]{2,1,0:T(8,128)(2,1)}, u32[]{:S(2)}, u32[]{:S(2)}) collective-permute-start(bf16[28,128,128]{2,1,0:T(8,128)(2,1)} %get-tuple-element.84.refs_8_), channel_id=1, source_target_pairs={{0,8},{1,9},{2,10},{3,11},{4,12},{5,13},{6,14},{7,15},{8,0},{9,1},... | collective-permute-start | bytes 2752520 | tf_op jit(solution)/shard_map/ppermute | solution.py:433
  94.7 19.9 %collective-permute-start.13 = (bf16[28,128,128]{2,1,0:T(8,128)(2,1)}, bf16[28,128,128]{2,1,0:T(8,128)(2,1)}, u32[]{:S(2)}, u32[]{:S(2)}) collective-permute-start(bf16[28,128,128]{2,1,0:T(8,128)(2,1)} %get-tuple-element.86.refs_14_.refs_2_), channel_id=1, source_target_pairs={{8,16},{9,17},{10,18},{11,19},{12,20},{13,21},{14,22},{15,23},{16,... | collective-permute-start | bytes 2752520 | tf_op jit(solution)/shard_map/ppermute | solution.py:433
  96.3 24.7 %collective-permute-start.10 = (bf16[2,28,128,128]{3,2,1,0:T(8,128)(2,1)}, bf16[2,28,128,128]{3,2,1,0:T(8,128)(2,1)}, u32[]{:S(2)}, u32[]{:S(2)}) collective-permute-start(bf16[2,28,128,128]{3,2,1,0:T(8,128)(2,1)} %get-tuple-element.82.refs_4_), channel_id=1, source_target_pairs={{0,1},{1,0},{2,3},{3,2},{4,5},{5,4},{6,7},{7,6},{8,9},{9,8},{10,11... | collective-permute-start | bytes 5505032 | tf_op jit(solution)/shard_map/ppermute | solution.py:433
  96.3 24.7 %collective-permute-start.11 = (bf16[2,28,128,128]{3,2,1,0:T(8,128)(2,1)}, bf16[2,28,128,128]{3,2,1,0:T(8,128)(2,1)}, u32[]{:S(2)}, u32[]{:S(2)}) collective-permute-start(bf16[2,28,128,128]{3,2,1,0:T(8,128)(2,1)} %collective-permute-done.8.refs_5_), channel_id=1, source_target_pairs={{0,1},{1,0},{2,3},{3,2},{4,5},{5,4},{6,7},{7,6},{8,9},{9,8},{10,11... | collective-permute-start | bytes 5505032 | tf_op jit(solution)/shard_map/ppermute | solution.py:433
  97.5 23.5 %collective-permute-start.14 = (bf16[28,128,128]{2,1,0:T(8,128)(2,1)}, bf16[28,128,128]{2,1,0:T(8,128)(2,1)}, u32[]{:S(2)}, u32[]{:S(2)}) collective-permute-start(bf16[28,128,128]{2,1,0:T(8,128)(2,1)} %get-tuple-element.84.refs_8_), channel_id=1, source_target_pairs={{0,1},{1,0},{2,3},{3,2},{4,5},{5,4},{6,7},{7,6},{8,9},{9,8},{10,11... | collective-permute-start | bytes 2752520 | tf_op jit(solution)/shard_map/ppermute | solution.py:433
  114.6 6.4 %collective-permute-start.15 = (bf16[28,128,128]{2,1,0:T(8,128)(2,1)}, bf16[28,128,128]{2,1,0:T(8,128)(2,1)}, u32[]{:S(2)}, u32[]{:S(2)}) collective-permute-start(bf16[28,128,128]{2,1,0:T(8,128)(2,1)} %collective-permute-done.12.refs_9_), channel_id=1, source_target_pairs={{0,1},{1,0},{2,3},{3,2},{4,5},{5,4},{6,7},{7,6},{8,9},{9,8},{10,11... | collective-permute-start | bytes 2752520 | tf_op jit(solution)/shard_map/ppermute | solution.py:433
  114.6 46.4 %collective-permute-start.16 = (bf16[2,28,128,128]{3,2,1,0:T(8,128)(2,1)}, bf16[2,28,128,128]{3,2,1,0:T(8,128)(2,1)}, u32[]{:S(2)}, u32[]{:S(2)}) collective-permute-start(bf16[2,28,128,128]{3,2,1,0:T(8,128)(2,1)} %reorder.2), channel_id=1, source_target_pairs={{8,0},{9,1},{10,2},{11,3},{12,4},{13,5},{14,6},{15,7},{24,8},{25,9... | collective-permute-start | bytes 5505032 | tf_op jit(solution)/shard_map/ppermute | solution.py:433
  121.0 1.2 copy-start.3
  122.2 1.2 copy-start.5
  137.7 42.6 %collective-permute-start.20 = (bf16[28,128,128]{2,1,0:T(8,128)(2,1)}, bf16[28,128,128]{2,1,0:T(8,128)(2,1)S(1)}, u32[]{:S(2)}, u32[]{:S(2)}) collective-permute-start(bf16[28,128,128]{2,1,0:T(8,128)(2,1)} %reorder.3), channel_id=1, source_target_pairs={{8,0},{9,1},{10,2},{11,3},{12,4},{13,5},{14,6},{15,7},{24,8},{25,9... | collective-permute-start | bytes 2752520 | tf_op jit(solution)/shard_map/ppermute | solution.py:433
  140.7 25.6 %collective-permute-start.17 = (bf16[4,128,512]{2,1,0:T(8,128)(2,1)S(1)}, bf16[4,128,512]{2,1,0:T(8,128)(2,1)S(1)}, u32[]{:S(2)}, u32[]{:S(2)}) collective-permute-start(bf16[4,128,512]{2,1,0:T(8,128)(2,1)S(1)} %get-tuple-element.99.refs_6_), channel_id=1, source_target_pairs={{0,2},{1,3},{2,0},{3,1},{4,6},{5,7},{6,4},{7,5},{8,10},{9,11},{10,... | collective-permute-start | bytes 1572872 | tf_op jit(solution)/shard_map/ppermute | solution.py:433
  142.1 24.6 %collective-permute-start.18 = (bf16[4,128,512]{2,1,0:T(8,128)(2,1)S(1)}, bf16[4,128,512]{2,1,0:T(8,128)(2,1)S(1)}, u32[]{:S(2)}, u32[]{:S(2)}) collective-permute-start(bf16[4,128,512]{2,1,0:T(8,128)(2,1)S(1)} %get-tuple-element.100), channel_id=1, source_target_pairs={{0,4},{1,5},{2,6},{3,7},{4,0},{5,1},{6,2},{7,3},{8,12},{9,13},{10,... | collective-permute-start | bytes 1572872 | tf_op jit(solution)/shard_map/ppermute | solution.py:433
  142.6 24.1 %collective-permute-start.19 = (bf16[4,128,512]{2,1,0:T(8,128)(2,1)S(1)}, bf16[4,128,512]{2,1,0:T(8,128)(2,1)S(1)}, u32[]{:S(2)}, u32[]{:S(2)}) collective-permute-start(bf16[4,128,512]{2,1,0:T(8,128)(2,1)S(1)} %get-tuple-element.101), channel_id=1, source_target_pairs={{0,6},{1,7},{2,4},{3,5},{4,2},{5,3},{6,0},{7,1},{8,14},{9,15},{10,... | collective-permute-start | bytes 1572872 | tf_op jit(solution)/shard_map/ppermute | solution.py:433
  144.2 16.8 %copy-start.1 = (bf16[28,128,128]{2,1,0:T(8,128)(2,1)S(1)}, bf16[28,128,128]{2,1,0:T(8,128)(2,1)}, u32[]{:S(2)}) copy-start(bf16[28,128,128]{2,1,0:T(8,128)(2,1)} %copy-done) | copy-start | bytes 2752516
  166.7 17.8 %collective-permute-start.21 = (bf16[4,128,256]{2,1,0:T(8,128)(2,1)S(1)}, bf16[4,128,256]{2,1,0:T(8,128)(2,1)S(1)}, u32[]{:S(2)}, u32[]{:S(2)}) collective-permute-start(bf16[4,128,256]{2,1,0:T(8,128)(2,1)S(1)} %get-tuple-element.110), channel_id=1, source_target_pairs={{0,2},{1,3},{2,0},{3,1},{4,6},{5,7},{6,4},{7,5},{8,10},{9,11},{10,... | collective-permute-start | bytes 786440 | tf_op jit(solution)/shard_map/ppermute | solution.py:433
  167.7 16.8 %collective-permute-start.22 = (bf16[4,128,256]{2,1,0:T(8,128)(2,1)S(1)}, bf16[4,128,256]{2,1,0:T(8,128)(2,1)S(1)}, u32[]{:S(2)}, u32[]{:S(2)}) collective-permute-start(bf16[4,128,256]{2,1,0:T(8,128)(2,1)S(1)} %get-tuple-element.111), channel_id=1, source_target_pairs={{0,4},{1,5},{2,6},{3,7},{4,0},{5,1},{6,2},{7,3},{8,12},{9,13},{10,... | collective-permute-start | bytes 786440 | tf_op jit(solution)/shard_map/ppermute | solution.py:433
  168.5 16.0 %collective-permute-start.23 = (bf16[4,128,256]{2,1,0:T(8,128)(2,1)S(1)}, bf16[4,128,256]{2,1,0:T(8,128)(2,1)S(1)}, u32[]{:S(2)}, u32[]{:S(2)}) collective-permute-start(bf16[4,128,256]{2,1,0:T(8,128)(2,1)S(1)} %get-tuple-element.112), channel_id=1, source_target_pairs={{0,6},{1,7},{2,4},{3,5},{4,2},{5,3},{6,0},{7,1},{8,14},{9,15},{10,... | collective-permute-start | bytes 786440 | tf_op jit(solution)/shard_map/ppermute | solution.py:433
  184.5 9.3 %collective-permute-start.27 = (bf16[4,128,256]{2,1,0:T(8,128)(2,1)S(1)}, bf16[4,128,256]{2,1,0:T(8,128)(2,1)S(1)}, u32[]{:S(2)}, u32[]{:S(2)}) collective-permute-start(bf16[4,128,256]{2,1,0:T(8,128)(2,1)S(1)} %get-tuple-element.120), channel_id=1, source_target_pairs={{0,2},{1,3},{2,0},{3,1},{4,6},{5,7},{6,4},{7,5},{8,10},{9,11},{10,... | collective-permute-start | bytes 786440 | tf_op jit(solution)/shard_map/ppermute | solution.py:433
  186.0 13.3 %collective-permute-start.28 = (bf16[4,128,256]{2,1,0:T(8,128)(2,1)S(1)}, bf16[4,128,256]{2,1,0:T(8,128)(2,1)S(1)}, u32[]{:S(2)}, u32[]{:S(2)}) collective-permute-start(bf16[4,128,256]{2,1,0:T(8,128)(2,1)S(1)} %get-tuple-element.121), channel_id=1, source_target_pairs={{0,4},{1,5},{2,6},{3,7},{4,0},{5,1},{6,2},{7,3},{8,12},{9,13},{10,... | collective-permute-start | bytes 786440 | tf_op jit(solution)/shard_map/ppermute | solution.py:433
  186.0 13.3 %collective-permute-start.29 = (bf16[4,128,256]{2,1,0:T(8,128)(2,1)S(1)}, bf16[4,128,256]{2,1,0:T(8,128)(2,1)S(1)}, u32[]{:S(2)}, u32[]{:S(2)}) collective-permute-start(bf16[4,128,256]{2,1,0:T(8,128)(2,1)S(1)} %get-tuple-element.122.refs_3_), channel_id=1, source_target_pairs={{0,6},{1,7},{2,4},{3,5},{4,2},{5,3},{6,0},{7,1},{8,14},{9,15},{10,... | collective-permute-start | bytes 786440 | tf_op jit(solution)/shard_map/ppermute | solution.py:433
  190.8 10.9 %collective-permute-start.24 = (bf16[128,768]{1,0:T(8,128)(2,1)S(1)}, bf16[128,768]{1,0:T(8,128)(2,1)S(1)}, u32[]{:S(2)}, u32[]{:S(2)}) collective-permute-start(bf16[128,768]{1,0:T(8,128)(2,1)S(1)} %get-tuple-element.117), channel_id=1, source_target_pairs={{0,1},{1,0},{2,3},{3,2},{4,5},{5,4},{6,7},{7,6},{8,9},{9,8},{10,11... | collective-permute-start | bytes 589832 | tf_op jit(solution)/shard_map/ppermute | solution.py:433
  190.8 11.0 %collective-permute-start.25 = (bf16[128,768]{1,0:T(8,128)(2,1)S(1)}, bf16[128,768]{1,0:T(8,128)(2,1)S(1)}, u32[]{:S(2)}, u32[]{:S(2)}) collective-permute-start(bf16[128,768]{1,0:T(8,128)(2,1)S(1)} %get-tuple-element.118), channel_id=1, source_target_pairs={{0,8},{1,9},{2,10},{3,11},{4,12},{5,13},{6,14},{7,15},{8,0},{9,1},... | collective-permute-start | bytes 589832 | tf_op jit(solution)/shard_map/ppermute | solution.py:433
  193.8 8.7 %collective-permute-start.26 = (bf16[128,768]{1,0:T(8,128)(2,1)S(1)}, bf16[128,768]{1,0:T(8,128)(2,1)S(1)}, u32[]{:S(2)}, u32[]{:S(2)}) collective-permute-start(bf16[128,768]{1,0:T(8,128)(2,1)S(1)} %get-tuple-element.119), channel_id=1, source_target_pairs={{0,9},{1,8},{2,11},{3,10},{4,13},{5,12},{6,15},{7,14},{8,1},{9,0},... | collective-permute-start | bytes 589832 | tf_op jit(solution)/shard_map/ppermute | solution.py:433
  199.4 3.0 %collective-permute-start.30 = (bf16[128,256]{1,0:T(8,128)(2,1)S(1)}, bf16[128,256]{1,0:T(8,128)(2,1)S(1)}, u32[]{:S(2)}, u32[]{:S(2)}) collective-permute-start(bf16[128,256]{1,0:T(8,128)(2,1)S(1)} %get-tuple-element.124), channel_id=1, source_target_pairs={{0,1},{1,0},{2,3},{3,2},{4,5},{5,4},{6,7},{7,6},{8,9},{9,8},{10,11... | collective-permute-start | bytes 196616 | tf_op jit(solution)/shard_map/ppermute | solution.py:433
  199.5 4.9 %collective-permute-start.31 = (bf16[128,256]{1,0:T(8,128)(2,1)S(1)}, bf16[128,256]{1,0:T(8,128)(2,1)S(1)}, u32[]{:S(2)}, u32[]{:S(2)}) collective-permute-start(bf16[128,256]{1,0:T(8,128)(2,1)S(1)} %get-tuple-element.125), channel_id=1, source_target_pairs={{0,8},{1,9},{2,10},{3,11},{4,12},{5,13},{6,14},{7,15},{8,0},{9,1},... | collective-permute-start | bytes 196616 | tf_op jit(solution)/shard_map/ppermute | solution.py:433
  201.7 4.0 %collective-permute-start.32 = (bf16[128,256]{1,0:T(8,128)(2,1)S(1)}, bf16[128,256]{1,0:T(8,128)(2,1)S(1)}, u32[]{:S(2)}, u32[]{:S(2)}) collective-permute-start(bf16[128,256]{1,0:T(8,128)(2,1)S(1)} %get-tuple-element.126), channel_id=1, source_target_pairs={{0,9},{1,8},{2,11},{3,10},{4,13},{5,12},{6,15},{7,14},{8,1},{9,0},... | collective-permute-start | bytes 196616 | tf_op jit(solution)/shard_map/ppermute | solution.py:433

commit v15 on v14

--- a/solution.py
+++ b/solution.py
@@ -444,7 +444,8 @@
     def to_pair(array):
         return send(array, flip(n, PAIR))
 
-    a_0, w_0, packed_1, packed_2 = pack(at_plane, (0, 1, 2), *inputs)
+    packed_1, packed_2 = pack(at_plane, (1, 2), *inputs)
+    a_0, w_0 = pack(at_plane, (0,), *inputs, after=(packed_1,))
     pair_0, mid_0, next_0 = to_pair(a_0), to_mid(w_0), to_next(w_0)
     got_1 = send(packed_1, flip(n, PLANE))
     got_2 = send(packed_2, flip(n, 2 * PLANE))

time: 208 us -> 206 us (level)
  waiting for transfers between devices: 109 us -> 105 us
  Pallas kernels: 48.9 us -> 51.2 us
    ppermute x33, waiting for transfers between devices: 109 us -> 105 us  [send(): return lax.ppermute(array, 'fsdp', perm=perm)]
    pallas_call x2 -> x3, Pallas kernels: 8.3 us -> 10.7 us  [pack(): pl.pallas_call(functools.partial(pack_kernel, apart, len(steps)), out_sha...]
  transfers between devices with their start and end apart: 33 -> 33, of which waited for: 15 -> 16; matrix products, arithmetic and copies ran while one was open for 1% -> 1% of each run, Pallas kernels for 20% -> 22%
where the time goes in v15:
time: 206 us
  waiting for transfers between devices  105 us (51%)
  Pallas kernels  51.2 us (25%)
  starting transfers between devices  42.7 us (21%)
  local copies, waits for them, and re-layouts  6.5 us (3%)
    ppermute x33, waiting for transfers between devices, send(): return lax.ppermute(array, 'fsdp', perm=perm)  105 us
    ppermute x33, starting transfers between devices, send(): return lax.ppermute(array, 'fsdp', perm=perm)  42.7 us
    pallas_call x4, Pallas kernels, product(): pl.pallas_call(functools.partial(product_kernel, [places[group] for group...  16 us
    pallas_call x1, Pallas kernels, stack_product(): pl.pallas_call(functools.partial(stack_product_kernel, places, a_at, w_at...  11 us
    pallas_call x3, Pallas kernels, pack(): pl.pallas_call(functools.partial(pack_kernel, apart, len(steps)), out_sha...  10.7 us
    pallas_call x2, Pallas kernels, reorder(): pl.pallas_call(functools.partial(reorder_kernel, count), out_shape=pltpu....  6.79 us
    unnamed x16, local copies, waits for them, and re-layouts  5.2 us
  transfers between devices with their start and end apart: 33, of which 16 were waited for; matrix products, arithmetic and copies ran while one was open for 1% of the time, Pallas kernels for 22%

profile of v15, /device:TPU:0, one launch (start us, length us, event | category | flops | bytes accessed | tf_op | source)
XLA Modules:
  0.0 205.6 jit_solution(14151117159057419144)
XLA Ops:
  0.0 3.9 %pack.3 = (bf16[2,28,128,128]{3,2,1,0:T(8,128)(2,1)S(1)}, bf16[2,28,128,128]{3,2,1,0:T(8,128)(2,1)S(1)}) custom-call(s32[1]{0:T(128)} %bitcast.3.plane_ref.choice_ref, bf16[128,14336]{1,0:T(8,128)(2,1)} %refs_0_.5, bf16[128,14336]{1,0:T(8,128)(2,1)} %refs_1_.5, bf16[14336,128]{1,0:T(8,128)(2,1)} %refs_2_.5, bf16[128,14336]{1,0:T(8,128)(2,1)} %refs_0_.5, ...), custom_call_target="tpu_custom_call" | custom-call | bytes 9175040 | tf_op jit(solution)/shard_map/pack/pallas_call | solution.py:63
  3.9 3.0 %collective-permute-start.4 = (bf16[2,28,128,128]{3,2,1,0:T(8,128)(2,1)S(1)}, bf16[2,28,128,128]{3,2,1,0:T(8,128)(2,1)S(1)}, u32[]{:S(2)}, u32[]{:S(2)}) collective-permute-start(bf16[2,28,128,128]{3,2,1,0:T(8,128)(2,1)S(1)} %get-tuple-element.70), channel_id=1, source_target_pairs={{0,4},{1,5},{2,6},{3,7},{4,0},{5,1},{6,2},{7,3},{8,12},{9,13},{10,... | collective-permute-start | bytes 5505032 | tf_op jit(solution)/shard_map/ppermute | solution.py:433
  6.9 1.5 collective-permute-start.3
  8.4 3.9 %pack.4 = (bf16[28,128,128]{2,1,0:T(8,128)(2,1)}, bf16[28,128,128]{2,1,0:T(8,128)(2,1)}) custom-call(s32[1]{0:T(128)} %bitcast.3.plane_ref.choice_ref, bf16[128,14336]{1,0:T(8,128)(2,1)} %refs_0_.5, bf16[128,14336]{1,0:T(8,128)(2,1)} %refs_1_.5, bf16[14336,128]{1,0:T(8,128)(2,1)} %refs_2_.5, bf16[2,28,128,128]{3,2,1,0:T(8,128)(2,1)S(1)} %get-tuple-element.66.refs_3_), custom_call_target="tpu_custom_call" | custom-call | bytes 4587520 | tf_op jit(solution)/shard_map/pack/pallas_call | solution.py:63
  12.3 1.6 collective-permute-start
  13.9 2.6 %collective-permute-start.2 = (bf16[28,128,128]{2,1,0:T(8,128)(2,1)}, bf16[28,128,128]{2,1,0:T(8,128)(2,1)S(1)}, u32[]{:S(2)}, u32[]{:S(2)}) collective-permute-start(bf16[28,128,128]{2,1,0:T(8,128)(2,1)} %get-tuple-element.68.refs_12_.refs_0_), channel_id=1, source_target_pairs={{8,0},{9,1},{10,2},{11,3},{12,4},{13,5},{14,6},{15,7},{24,8},{25,9... | collective-permute-start | bytes 2752520 | tf_op jit(solution)/shard_map/ppermute | solution.py:433
  17.2 18.6 %collective-permute-done.refs_3_.refs_0_.refs_1_ = bf16[28,128,128]{2,1,0:T(8,128)(2,1)S(1)} collective-permute-done((bf16[28,128,128]{2,1,0:T(8,128)(2,1)}, bf16[28,128,128]{2,1,0:T(8,128)(2,1)S(1)}, u32[]{:S(2)}, u32[]{:S(2)}) %collective-permute-start) | collective-permute-done | bytes 917536 | tf_op jit(solution)/shard_map/ppermute | solution.py:433
  35.8 2.9 %pack.5 = bf16[2,28,128,128]{3,2,1,0:T(8,128)(2,1)S(1)} custom-call(s32[1]{0:T(128)} %bitcast.3.plane_ref.choice_ref, bf16[128,14336]{1,0:T(8,128)(2,1)} %refs_0_.5, bf16[128,14336]{1,0:T(8,128)(2,1)} %refs_1_.5, bf16[14336,128]{1,0:T(8,128)(2,1)} %refs_2_.5, bf16[28,128,128]{2,1,0:T(8,128)(2,1)S(1)} %collective-permute-done.refs_3_.refs_0_.refs_1_), custom_call_target="tpu_custom_call" | custom-call | bytes 4587520 | tf_op jit(solution)/shard_map/pack/pallas_call | solution.py:63
  38.7 8.2 %collective-permute-done.4.two = bf16[2,28,128,128]{3,2,1,0:T(8,128)(2,1)S(1)} collective-permute-done((bf16[2,28,128,128]{3,2,1,0:T(8,128)(2,1)S(1)}, bf16[2,28,128,128]{3,2,1,0:T(8,128)(2,1)S(1)}, u32[]{:S(2)}, u32[]{:S(2)}) %collective-permute-start.4) | collective-permute-done | bytes 1835040 | tf_op jit(solution)/shard_map/ppermute | solution.py:433
  46.9 1.5 collective-permute-done.3.one
  48.4 1.4 collective-permute-start.5
  49.8 2.8 %unpack_pair.1 = (bf16[2,28,128,128]{3,2,1,0:T(8,128)(2,1)}, bf16[2,28,128,128]{3,2,1,0:T(8,128)(2,1)}) custom-call(bf16[2,28,128,128]{3,2,1,0:T(8,128)(2,1)S(1)} %collective-permute-done.3.one, bf16[2,28,128,128]{3,2,1,0:T(8,128)(2,1)S(1)} %collective-permute-done.4.two, bf16[28,128,128]{2,1,0:T(8,128)(2,1)S(1)} %collective-permute-done.refs_3_.refs_0_.refs_1_), custom_call_target="tpu_custom_call" | custom-call | bytes 7340032 | tf_op jit(solution)/shard_map/unpack_pair/pallas_call | solution.py:106
  52.6 1.6 collective-permute-start.8
  54.3 1.9 collective-permute-start.9
  56.2 0.9 copy-done
  57.6 2.0 collective-permute-done.6.refs_2_
  59.6 1.0 copy-done.2
  60.9 0.9 copy-done.4
  61.9 28.0 %collective-permute-done.5.packed = bf16[2,28,128,128]{3,2,1,0:T(8,128)(2,1)S(1)} collective-permute-done((bf16[2,28,128,128]{3,2,1,0:T(8,128)(2,1)S(1)}, bf16[2,28,128,128]{3,2,1,0:T(8,128)(2,1)S(1)}, u32[]{:S(2)}, u32[]{:S(2)}) %collective-permute-start.5) | collective-permute-done | bytes 1835040 | tf_op jit(solution)/shard_map/ppermute | solution.py:433
  89.8 1.7 unpack.1
  91.6 1.6 collective-permute-start.12
  93.2 1.6 collective-permute-start.13
  96.1 3.5 %reorder.2 = bf16[2,28,128,128]{3,2,1,0:T(8,128)(2,1)} custom-call(s32[2]{0:T(128)S(1)} %slice_bitcast_fusion.order_ref, bf16[2,28,128,128]{3,2,1,0:T(8,128)(2,1)S(1)} %collective-permute-done.5.packed, bf16[2,28,128,128]{3,2,1,0:T(8,128)(2,1)} %get-tuple-element.81.w_12.refs_13_.refs_1_), custom_call_target="tpu_custom_call" | custom-call | bytes 7340032 | tf_op jit(solution)/shard_map/reorder/pallas_call | solution.py:177
  99.6 13.4 %collective-permute-done.12.refs_9_ = bf16[28,128,128]{2,1,0:T(8,128)(2,1)} collective-permute-done((bf16[28,128,128]{2,1,0:T(8,128)(2,1)}, bf16[28,128,128]{2,1,0:T(8,128)(2,1)}, u32[]{:S(2)}, u32[]{:S(2)}) %collective-permute-start.12) | collective-permute-done | bytes 917536 | tf_op jit(solution)/shard_map/ppermute | solution.py:433
  113.1 5.8 %collective-permute-start.16 = (bf16[2,28,128,128]{3,2,1,0:T(8,128)(2,1)}, bf16[2,28,128,128]{3,2,1,0:T(8,128)(2,1)}, u32[]{:S(2)}, u32[]{:S(2)}) collective-permute-start(bf16[2,28,128,128]{3,2,1,0:T(8,128)(2,1)} %reorder.2), channel_id=1, source_target_pairs={{8,0},{9,1},{10,2},{11,3},{12,4},{13,5},{14,6},{15,7},{24,8},{25,9... | collective-permute-start | bytes 5505032 | tf_op jit(solution)/shard_map/ppermute | solution.py:433
  119.5 1.2 copy-done.3
  120.6 1.2 copy-done.5
  121.8 11.0 %stack_product.1 = (bf16[28,2048,128]{2,1,0:T(8,128)(2,1)S(1)}, bf16[4,128,512]{2,1,0:T(8,128)(2,1)S(1)}, bf16[4,128,512]{2,1,0:T(8,128)(2,1)S(1)}, bf16[4,128,512]{2,1,0:T(8,128)(2,1)S(1)}) custom-call(s32[1]{0:T(128)} %bitcast.2.choice_ref, bf16[28,128,128]{2,1,0:T(8,128)(2,1)} %get-tuple-element.67.refs_0_, ...), custom_call_target="tpu_custom_call" | custom-call | flops 5637144576 | bytes 18350080 | tf_op jit(solution)/shard_map/stack_product/pallas_call | solution.py:269
  132.8 3.3 %reorder.3 = bf16[28,128,128]{2,1,0:T(8,128)(2,1)} custom-call(s32[1]{0:T(128)} %bitcast.5.order_ref, bf16[2,28,128,128]{3,2,1,0:T(8,128)(2,1)S(1)} %collective-permute-done.5.packed, bf16[2,28,128,128]{3,2,1,0:T(8,128)(2,1)} %get-tuple-element.81.w_12.refs_13_.refs_1_), custom_call_target="tpu_custom_call" | custom-call | bytes 7340032 | tf_op jit(solution)/shard_map/reorder/pallas_call | solution.py:177
  136.1 3.0 %collective-permute-start.20 = (bf16[28,128,128]{2,1,0:T(8,128)(2,1)}, bf16[28,128,128]{2,1,0:T(8,128)(2,1)S(1)}, u32[]{:S(2)}, u32[]{:S(2)}) collective-permute-start(bf16[28,128,128]{2,1,0:T(8,128)(2,1)} %reorder.3), channel_id=1, source_target_pairs={{8,0},{9,1},{10,2},{11,3},{12,4},{13,5},{14,6},{15,7},{24,8},{25,9... | collective-permute-start | bytes 2752520 | tf_op jit(solution)/shard_map/ppermute | solution.py:433
  139.7 1.4 collective-permute-start.18
  141.1 1.5 collective-permute-start.19
  142.6 4.2 %product.4.refs_2_.refs_0_ = f32[4,128,512]{2,1,0:T(8,128)S(1)} custom-call(s32[1]{0:T(128)} %bitcast.2.choice_ref, bf16[28,2048,128]{2,1,0:T(8,128)(2,1)S(1)} %get-tuple-element.92.a, bf16[28,128,128]{2,1,0:T(8,128)(2,1)} %get-tuple-element.68.refs_12_.refs_0_, bf16[2,28,128,128]{3,2,1,0:T(8,128)(2,1)} %get-tuple-element.81.w_12.refs_13_.refs_1_, ...), custom_call_target="tpu_custom_call" | custom-call | flops 1879048192 | bytes 7340032 | tf_op jit(solution)/shard_map/product/pallas_call | solution.py:338
  146.8 12.7 %collective-permute-done.16.refs_1_.refs_0_ = bf16[2,28,128,128]{3,2,1,0:T(8,128)(2,1)} collective-permute-done((bf16[2,28,128,128]{3,2,1,0:T(8,128)(2,1)}, bf16[2,28,128,128]{3,2,1,0:T(8,128)(2,1)}, u32[]{:S(2)}, u32[]{:S(2)}) %collective-permute-start.16) | collective-permute-done | bytes 1835040 | tf_op jit(solution)/shard_map/ppermute | solution.py:433
  159.5 5.3 %product.5 = (bf16[4,128,256]{2,1,0:T(8,128)(2,1)S(1)}, bf16[4,128,256]{2,1,0:T(8,128)(2,1)S(1)}, bf16[4,128,256]{2,1,0:T(8,128)(2,1)S(1)}, f32[4,128,256]{2,1,0:T(8,128)S(1)}) custom-call(s32[1]{0:T(128)} %bitcast.3.plane_ref.choice_ref, bf16[28,2048,128]{2,1,0:T(8,128)(2,1)S(1)} %get-tuple-element.92.a, bf16[28,128,128]{2,1,0:T(8,128)(2,1)S(1)} %copy-done.1, ...), custom_call_target="tpu_custom_call" | custom-call | flops 3758096384 | bytes 16515072 | tf_op jit(solution)/shard_map/product/pallas_call | solution.py:338
  164.9 0.9 collective-permute-start.21
  165.8 1.4 collective-permute-start.22
  167.2 1.2 collective-permute-start.23
  168.4 10.3 %collective-permute-done.20.refs_1_ = bf16[28,128,128]{2,1,0:T(8,128)(2,1)S(1)} collective-permute-done((bf16[28,128,128]{2,1,0:T(8,128)(2,1)}, bf16[28,128,128]{2,1,0:T(8,128)(2,1)S(1)}, u32[]{:S(2)}, u32[]{:S(2)}) %collective-permute-start.20) | collective-permute-done | bytes 917536 | tf_op jit(solution)/shard_map/ppermute | solution.py:433
  178.7 4.2 %product.6 = (bf16[4,128,256]{2,1,0:T(8,128)(2,1)S(1)}, bf16[4,128,256]{2,1,0:T(8,128)(2,1)S(1)}, bf16[4,128,256]{2,1,0:T(8,128)(2,1)S(1)}) custom-call(s32[1]{0:T(128)} %bitcast.3.plane_ref.choice_ref, bf16[28,2048,128]{2,1,0:T(8,128)(2,1)S(1)} %get-tuple-element.92.a, bf16[2,28,128,128]{3,2,1,0:T(8,128)(2,1)} %collective-permute-done.16.refs_1_.refs_0_, ...), custom_call_target="tpu_custom_call" | custom-call | flops 2818572288 | bytes 12845056 | tf_op jit(solution)/shard_map/product/pallas_call | solution.py:338
  184.4 2.2 %collective-permute-start.29 = (bf16[4,128,256]{2,1,0:T(8,128)(2,1)S(1)}, bf16[4,128,256]{2,1,0:T(8,128)(2,1)S(1)}, u32[]{:S(2)}, u32[]{:S(2)}) collective-permute-start(bf16[4,128,256]{2,1,0:T(8,128)(2,1)S(1)} %get-tuple-element.122.refs_3_), channel_id=1, source_target_pairs={{0,6},{1,7},{2,4},{3,5},{4,2},{5,3},{6,0},{7,1},{8,14},{9,15},{10,... | collective-permute-start | bytes 786440 | tf_op jit(solution)/shard_map/ppermute | solution.py:433
  186.5 2.3 %product.7.refs_8_.refs_0_ = f32[4,128,256]{2,1,0:T(8,128)S(1)} custom-call(s32[1]{0:T(128)} %bitcast.3.plane_ref.choice_ref, bf16[28,2048,128]{2,1,0:T(8,128)(2,1)S(1)} %get-tuple-element.92.a, bf16[2,28,128,128]{3,2,1,0:T(8,128)(2,1)} %collective-permute-done.16.refs_1_.refs_0_, bf16[28,128,128]{2,1,0:T(8,128)(2,1)S(1)} %collective-permute-done.20.refs_1_, ...), custom_call_target="tpu_custom_call" | custom-call | flops 939524096 | bytes 5505024 | tf_op jit(solution)/shard_map/product/pallas_call | solution.py:338
  189.3 2.2 %collective-permute-start.25 = (bf16[128,768]{1,0:T(8,128)(2,1)S(1)}, bf16[128,768]{1,0:T(8,128)(2,1)S(1)}, u32[]{:S(2)}, u32[]{:S(2)}) collective-permute-start(bf16[128,768]{1,0:T(8,128)(2,1)S(1)} %get-tuple-element.118), channel_id=1, source_target_pairs={{0,8},{1,9},{2,10},{3,11},{4,12},{5,13},{6,14},{7,15},{8,0},{9,1},... | collective-permute-start | bytes 589832 | tf_op jit(solution)/shard_map/ppermute | solution.py:433
  192.5 4.3 %collective-permute-done.29.refs_3_ = bf16[4,128,256]{2,1,0:T(8,128)(2,1)S(1)} collective-permute-done((bf16[4,128,256]{2,1,0:T(8,128)(2,1)S(1)}, bf16[4,128,256]{2,1,0:T(8,128)(2,1)S(1)}, u32[]{:S(2)}, u32[]{:S(2)}) %collective-permute-start.29) | collective-permute-done | bytes 262176 | tf_op jit(solution)/shard_map/ppermute | solution.py:433
  197.1 2.3 %collective-permute-start.31 = (bf16[128,256]{1,0:T(8,128)(2,1)S(1)}, bf16[128,256]{1,0:T(8,128)(2,1)S(1)}, u32[]{:S(2)}, u32[]{:S(2)}) collective-permute-start(bf16[128,256]{1,0:T(8,128)(2,1)S(1)} %get-tuple-element.125), channel_id=1, source_target_pairs={{0,8},{1,9},{2,10},{3,11},{4,12},{5,13},{6,14},{7,15},{8,0},{9,1},... | collective-permute-start | bytes 196616 | tf_op jit(solution)/shard_map/ppermute | solution.py:433
  199.5 1.5 collective-permute-done.26.refs_3_
  201.0 1.9 collective-permute-done.31.refs_6_
  203.8 1.8 assemble.1
  (53 shorter events, 8.1 us)
Async XLA Ops:
  3.9 43.0 %collective-permute-start.4 = (bf16[2,28,128,128]{3,2,1,0:T(8,128)(2,1)S(1)}, bf16[2,28,128,128]{3,2,1,0:T(8,128)(2,1)S(1)}, u32[]{:S(2)}, u32[]{:S(2)}) collective-permute-start(bf16[2,28,128,128]{3,2,1,0:T(8,128)(2,1)S(1)} %get-tuple-element.70), channel_id=1, source_target_pairs={{0,4},{1,5},{2,6},{3,7},{4,0},{5,1},{6,2},{7,3},{8,12},{9,13},{10,... | collective-permute-start | bytes 5505032 | tf_op jit(solution)/shard_map/ppermute | solution.py:433
  6.9 41.5 %collective-permute-start.3 = (bf16[2,28,128,128]{3,2,1,0:T(8,128)(2,1)S(1)}, bf16[2,28,128,128]{3,2,1,0:T(8,128)(2,1)S(1)}, u32[]{:S(2)}, u32[]{:S(2)}) collective-permute-start(bf16[2,28,128,128]{3,2,1,0:T(8,128)(2,1)S(1)} %get-tuple-element.66.refs_3_), channel_id=1, source_target_pairs={{0,2},{1,3},{2,0},{3,1},{4,6},{5,7},{6,4},{7,5},{8,10},{9,11},{10,... | collective-permute-start | bytes 5505032 | tf_op jit(solution)/shard_map/ppermute | solution.py:433
  12.3 23.5 %collective-permute-start = (bf16[28,128,128]{2,1,0:T(8,128)(2,1)}, bf16[28,128,128]{2,1,0:T(8,128)(2,1)S(1)}, u32[]{:S(2)}, u32[]{:S(2)}) collective-permute-start(bf16[28,128,128]{2,1,0:T(8,128)(2,1)} %get-tuple-element.67.refs_0_), channel_id=1, source_target_pairs={{0,8},{1,9},{2,10},{3,11},{4,12},{5,13},{6,14},{7,15},{8,0},{9,1},... | collective-permute-start | bytes 2752520 | tf_op jit(solution)/shard_map/ppermute | solution.py:433
  13.9 42.3 %collective-permute-start.2 = (bf16[28,128,128]{2,1,0:T(8,128)(2,1)}, bf16[28,128,128]{2,1,0:T(8,128)(2,1)S(1)}, u32[]{:S(2)}, u32[]{:S(2)}) collective-permute-start(bf16[28,128,128]{2,1,0:T(8,128)(2,1)} %get-tuple-element.68.refs_12_.refs_0_), channel_id=1, source_target_pairs={{8,0},{9,1},{10,2},{11,3},{12,4},{13,5},{14,6},{15,7},{24,8},{25,9... | collective-permute-start | bytes 2752520 | tf_op jit(solution)/shard_map/ppermute | solution.py:433
  16.5 40.7 %collective-permute-start.1 = (bf16[28,128,128]{2,1,0:T(8,128)(2,1)}, bf16[28,128,128]{2,1,0:T(8,128)(2,1)S(1)}, u32[]{:S(2)}, u32[]{:S(2)}) collective-permute-start(bf16[28,128,128]{2,1,0:T(8,128)(2,1)} %get-tuple-element.68.refs_12_.refs_0_), channel_id=1, source_target_pairs={{8,16},{9,17},{10,18},{11,19},{12,20},{13,21},{14,22},{15,23},{16,... | collective-permute-start | bytes 2752520 | tf_op jit(solution)/shard_map/ppermute | solution.py:433
  38.7 18.4 %copy-start.7 = (bf16[28,128,128]{2,1,0:T(8,128)(2,1)S(1)}, bf16[28,128,128]{2,1,0:T(8,128)(2,1)}, u32[]{:S(2)}) copy-start(bf16[28,128,128]{2,1,0:T(8,128)(2,1)} %get-tuple-element.67.refs_0_) | copy-start | bytes 2752516
  48.4 41.5 %collective-permute-start.5 = (bf16[2,28,128,128]{3,2,1,0:T(8,128)(2,1)S(1)}, bf16[2,28,128,128]{3,2,1,0:T(8,128)(2,1)S(1)}, u32[]{:S(2)}, u32[]{:S(2)}) collective-permute-start(bf16[2,28,128,128]{3,2,1,0:T(8,128)(2,1)S(1)} %pack.5), channel_id=1, source_target_pairs={{0,6},{1,7},{2,4},{3,5},{4,2},{5,3},{6,0},{7,1},{8,14},{9,15},{10,... | collective-permute-start | bytes 5505032 | tf_op jit(solution)/shard_map/ppermute | solution.py:433
  52.6 42.2 %collective-permute-start.8 = (bf16[2,28,128,128]{3,2,1,0:T(8,128)(2,1)}, bf16[2,28,128,128]{3,2,1,0:T(8,128)(2,1)}, u32[]{:S(2)}, u32[]{:S(2)}) collective-permute-start(bf16[2,28,128,128]{3,2,1,0:T(8,128)(2,1)} %get-tuple-element.82.refs_4_), channel_id=1, source_target_pairs={{0,8},{1,9},{2,10},{3,11},{4,12},{5,13},{6,14},{7,15},{8,0},{9,1},... | collective-permute-start | bytes 5505032 | tf_op jit(solution)/shard_map/ppermute | solution.py:433
  54.3 40.5 %collective-permute-start.9 = (bf16[2,28,128,128]{3,2,1,0:T(8,128)(2,1)}, bf16[2,28,128,128]{3,2,1,0:T(8,128)(2,1)}, u32[]{:S(2)}, u32[]{:S(2)}) collective-permute-start(bf16[2,28,128,128]{3,2,1,0:T(8,128)(2,1)} %get-tuple-element.81.w_12.refs_13_.refs_1_), channel_id=1, source_target_pairs={{8,16},{9,17},{10,18},{11,19},{12,20},{13,21},{14,22},{15,23},{16,... | collective-permute-start | bytes 5505032 | tf_op jit(solution)/shard_map/ppermute | solution.py:433
  56.2 0.9 copy-start
  57.1 2.5 %collective-permute-start.6 = (bf16[28,128,128]{2,1,0:T(8,128)(2,1)S(1)}, bf16[28,128,128]{2,1,0:T(8,128)(2,1)S(1)}, u32[]{:S(2)}, u32[]{:S(2)}) collective-permute-start(bf16[28,128,128]{2,1,0:T(8,128)(2,1)S(1)} %copy-done.7), channel_id=1, source_target_pairs={{0,1},{1,0},{2,3},{3,2},{4,5},{5,4},{6,7},{7,6},{8,9},{9,8},{10,11... | collective-permute-start | bytes 2752520 | tf_op jit(solution)/shard_map/ppermute | solution.py:433
  57.1 32.7 %copy-start.6 = (bf16[28,128,128]{2,1,0:T(8,128)(2,1)}, bf16[28,128,128]{2,1,0:T(8,128)(2,1)S(1)}, u32[]{:S(2)}) copy-start(bf16[28,128,128]{2,1,0:T(8,128)(2,1)S(1)} %collective-permute-done.1.refs_15_.refs_3_) | copy-start | bytes 2752516
  57.1 3.8 %collective-permute-start.7 = (bf16[28,128,128]{2,1,0:T(8,128)(2,1)S(1)}, bf16[28,128,128]{2,1,0:T(8,128)(2,1)S(1)}, u32[]{:S(2)}, u32[]{:S(2)}) collective-permute-start(bf16[28,128,128]{2,1,0:T(8,128)(2,1)S(1)} %collective-permute-done.refs_3_.refs_0_.refs_1_), channel_id=1, source_target_pairs={{0,1},{1,0},{2,3},{3,2},{4,5},{5,4},{6,7},{7,6},{8,9},{9,8},{10,11... | collective-permute-start | bytes 2752520 | tf_op jit(solution)/shard_map/ppermute | solution.py:433
  59.6 1.0 copy-start.2
  60.9 0.9 copy-start.4
  91.6 21.5 %collective-permute-start.12 = (bf16[28,128,128]{2,1,0:T(8,128)(2,1)}, bf16[28,128,128]{2,1,0:T(8,128)(2,1)}, u32[]{:S(2)}, u32[]{:S(2)}) collective-permute-start(bf16[28,128,128]{2,1,0:T(8,128)(2,1)} %get-tuple-element.84.refs_8_), channel_id=1, source_target_pairs={{0,8},{1,9},{2,10},{3,11},{4,12},{5,13},{6,14},{7,15},{8,0},{9,1},... | collective-permute-start | bytes 2752520 | tf_op jit(solution)/shard_map/ppermute | solution.py:433
  93.2 19.8 %collective-permute-start.13 = (bf16[28,128,128]{2,1,0:T(8,128)(2,1)}, bf16[28,128,128]{2,1,0:T(8,128)(2,1)}, u32[]{:S(2)}, u32[]{:S(2)}) collective-permute-start(bf16[28,128,128]{2,1,0:T(8,128)(2,1)} %get-tuple-element.86.refs_14_.refs_2_), channel_id=1, source_target_pairs={{8,16},{9,17},{10,18},{11,19},{12,20},{13,21},{14,22},{15,23},{16,... | collective-permute-start | bytes 2752520 | tf_op jit(solution)/shard_map/ppermute | solution.py:433
  94.8 24.6 %collective-permute-start.10 = (bf16[2,28,128,128]{3,2,1,0:T(8,128)(2,1)}, bf16[2,28,128,128]{3,2,1,0:T(8,128)(2,1)}, u32[]{:S(2)}, u32[]{:S(2)}) collective-permute-start(bf16[2,28,128,128]{3,2,1,0:T(8,128)(2,1)} %get-tuple-element.82.refs_4_), channel_id=1, source_target_pairs={{0,1},{1,0},{2,3},{3,2},{4,5},{5,4},{6,7},{7,6},{8,9},{9,8},{10,11... | collective-permute-start | bytes 5505032 | tf_op jit(solution)/shard_map/ppermute | solution.py:433
  94.8 24.6 %collective-permute-start.11 = (bf16[2,28,128,128]{3,2,1,0:T(8,128)(2,1)}, bf16[2,28,128,128]{3,2,1,0:T(8,128)(2,1)}, u32[]{:S(2)}, u32[]{:S(2)}) collective-permute-start(bf16[2,28,128,128]{3,2,1,0:T(8,128)(2,1)} %collective-permute-done.8.refs_5_), channel_id=1, source_target_pairs={{0,1},{1,0},{2,3},{3,2},{4,5},{5,4},{6,7},{7,6},{8,9},{9,8},{10,11... | collective-permute-start | bytes 5505032 | tf_op jit(solution)/shard_map/ppermute | solution.py:433
  96.0 23.4 %collective-permute-start.14 = (bf16[28,128,128]{2,1,0:T(8,128)(2,1)}, bf16[28,128,128]{2,1,0:T(8,128)(2,1)}, u32[]{:S(2)}, u32[]{:S(2)}) collective-permute-start(bf16[28,128,128]{2,1,0:T(8,128)(2,1)} %get-tuple-element.84.refs_8_), channel_id=1, source_target_pairs={{0,1},{1,0},{2,3},{3,2},{4,5},{5,4},{6,7},{7,6},{8,9},{9,8},{10,11... | collective-permute-start | bytes 2752520 | tf_op jit(solution)/shard_map/ppermute | solution.py:433
  113.1 6.4 %collective-permute-start.15 = (bf16[28,128,128]{2,1,0:T(8,128)(2,1)}, bf16[28,128,128]{2,1,0:T(8,128)(2,1)}, u32[]{:S(2)}, u32[]{:S(2)}) collective-permute-start(bf16[28,128,128]{2,1,0:T(8,128)(2,1)} %collective-permute-done.12.refs_9_), channel_id=1, source_target_pairs={{0,1},{1,0},{2,3},{3,2},{4,5},{5,4},{6,7},{7,6},{8,9},{9,8},{10,11... | collective-permute-start | bytes 2752520 | tf_op jit(solution)/shard_map/ppermute | solution.py:433
  113.1 46.4 %collective-permute-start.16 = (bf16[2,28,128,128]{3,2,1,0:T(8,128)(2,1)}, bf16[2,28,128,128]{3,2,1,0:T(8,128)(2,1)}, u32[]{:S(2)}, u32[]{:S(2)}) collective-permute-start(bf16[2,28,128,128]{3,2,1,0:T(8,128)(2,1)} %reorder.2), channel_id=1, source_target_pairs={{8,0},{9,1},{10,2},{11,3},{12,4},{13,5},{14,6},{15,7},{24,8},{25,9... | collective-permute-start | bytes 5505032 | tf_op jit(solution)/shard_map/ppermute | solution.py:433
  119.5 1.2 copy-start.3
  120.6 1.2 copy-start.5
  136.1 42.6 %collective-permute-start.20 = (bf16[28,128,128]{2,1,0:T(8,128)(2,1)}, bf16[28,128,128]{2,1,0:T(8,128)(2,1)S(1)}, u32[]{:S(2)}, u32[]{:S(2)}) collective-permute-start(bf16[28,128,128]{2,1,0:T(8,128)(2,1)} %reorder.3), channel_id=1, source_target_pairs={{8,0},{9,1},{10,2},{11,3},{12,4},{13,5},{14,6},{15,7},{24,8},{25,9... | collective-permute-start | bytes 2752520 | tf_op jit(solution)/shard_map/ppermute | solution.py:433
  139.1 25.6 %collective-permute-start.17 = (bf16[4,128,512]{2,1,0:T(8,128)(2,1)S(1)}, bf16[4,128,512]{2,1,0:T(8,128)(2,1)S(1)}, u32[]{:S(2)}, u32[]{:S(2)}) collective-permute-start(bf16[4,128,512]{2,1,0:T(8,128)(2,1)S(1)} %get-tuple-element.99.refs_6_), channel_id=1, source_target_pairs={{0,2},{1,3},{2,0},{3,1},{4,6},{5,7},{6,4},{7,5},{8,10},{9,11},{10,... | collective-permute-start | bytes 1572872 | tf_op jit(solution)/shard_map/ppermute | solution.py:433
  139.7 25.1 %collective-permute-start.18 = (bf16[4,128,512]{2,1,0:T(8,128)(2,1)S(1)}, bf16[4,128,512]{2,1,0:T(8,128)(2,1)S(1)}, u32[]{:S(2)}, u32[]{:S(2)}) collective-permute-start(bf16[4,128,512]{2,1,0:T(8,128)(2,1)S(1)} %get-tuple-element.100), channel_id=1, source_target_pairs={{0,4},{1,5},{2,6},{3,7},{4,0},{5,1},{6,2},{7,3},{8,12},{9,13},{10,... | collective-permute-start | bytes 1572872 | tf_op jit(solution)/shard_map/ppermute | solution.py:433
  141.1 23.8 %collective-permute-start.19 = (bf16[4,128,512]{2,1,0:T(8,128)(2,1)S(1)}, bf16[4,128,512]{2,1,0:T(8,128)(2,1)S(1)}, u32[]{:S(2)}, u32[]{:S(2)}) collective-permute-start(bf16[4,128,512]{2,1,0:T(8,128)(2,1)S(1)} %get-tuple-element.101), channel_id=1, source_target_pairs={{0,6},{1,7},{2,4},{3,5},{4,2},{5,3},{6,0},{7,1},{8,14},{9,15},{10,... | collective-permute-start | bytes 1572872 | tf_op jit(solution)/shard_map/ppermute | solution.py:433
  142.6 16.9 %copy-start.1 = (bf16[28,128,128]{2,1,0:T(8,128)(2,1)S(1)}, bf16[28,128,128]{2,1,0:T(8,128)(2,1)}, u32[]{:S(2)}) copy-start(bf16[28,128,128]{2,1,0:T(8,128)(2,1)} %copy-done) | copy-start | bytes 2752516
  164.9 18.0 %collective-permute-start.21 = (bf16[4,128,256]{2,1,0:T(8,128)(2,1)S(1)}, bf16[4,128,256]{2,1,0:T(8,128)(2,1)S(1)}, u32[]{:S(2)}, u32[]{:S(2)}) collective-permute-start(bf16[4,128,256]{2,1,0:T(8,128)(2,1)S(1)} %get-tuple-element.110), channel_id=1, source_target_pairs={{0,2},{1,3},{2,0},{3,1},{4,6},{5,7},{6,4},{7,5},{8,10},{9,11},{10,... | collective-permute-start | bytes 786440 | tf_op jit(solution)/shard_map/ppermute | solution.py:433
  165.8 17.2 %collective-permute-start.22 = (bf16[4,128,256]{2,1,0:T(8,128)(2,1)S(1)}, bf16[4,128,256]{2,1,0:T(8,128)(2,1)S(1)}, u32[]{:S(2)}, u32[]{:S(2)}) collective-permute-start(bf16[4,128,256]{2,1,0:T(8,128)(2,1)S(1)} %get-tuple-element.111), channel_id=1, source_target_pairs={{0,4},{1,5},{2,6},{3,7},{4,0},{5,1},{6,2},{7,3},{8,12},{9,13},{10,... | collective-permute-start | bytes 786440 | tf_op jit(solution)/shard_map/ppermute | solution.py:433
  167.2 15.7 %collective-permute-start.23 = (bf16[4,128,256]{2,1,0:T(8,128)(2,1)S(1)}, bf16[4,128,256]{2,1,0:T(8,128)(2,1)S(1)}, u32[]{:S(2)}, u32[]{:S(2)}) collective-permute-start(bf16[4,128,256]{2,1,0:T(8,128)(2,1)S(1)} %get-tuple-element.112), channel_id=1, source_target_pairs={{0,6},{1,7},{2,4},{3,5},{4,2},{5,3},{6,0},{7,1},{8,14},{9,15},{10,... | collective-permute-start | bytes 786440 | tf_op jit(solution)/shard_map/ppermute | solution.py:433
  183.0 9.3 %collective-permute-start.27 = (bf16[4,128,256]{2,1,0:T(8,128)(2,1)S(1)}, bf16[4,128,256]{2,1,0:T(8,128)(2,1)S(1)}, u32[]{:S(2)}, u32[]{:S(2)}) collective-permute-start(bf16[4,128,256]{2,1,0:T(8,128)(2,1)S(1)} %get-tuple-element.120), channel_id=1, source_target_pairs={{0,2},{1,3},{2,0},{3,1},{4,6},{5,7},{6,4},{7,5},{8,10},{9,11},{10,... | collective-permute-start | bytes 786440 | tf_op jit(solution)/shard_map/ppermute | solution.py:433
  183.6 8.9 %collective-permute-start.28 = (bf16[4,128,256]{2,1,0:T(8,128)(2,1)S(1)}, bf16[4,128,256]{2,1,0:T(8,128)(2,1)S(1)}, u32[]{:S(2)}, u32[]{:S(2)}) collective-permute-start(bf16[4,128,256]{2,1,0:T(8,128)(2,1)S(1)} %get-tuple-element.121), channel_id=1, source_target_pairs={{0,4},{1,5},{2,6},{3,7},{4,0},{5,1},{6,2},{7,3},{8,12},{9,13},{10,... | collective-permute-start | bytes 786440 | tf_op jit(solution)/shard_map/ppermute | solution.py:433
  184.4 12.5 %collective-permute-start.29 = (bf16[4,128,256]{2,1,0:T(8,128)(2,1)S(1)}, bf16[4,128,256]{2,1,0:T(8,128)(2,1)S(1)}, u32[]{:S(2)}, u32[]{:S(2)}) collective-permute-start(bf16[4,128,256]{2,1,0:T(8,128)(2,1)S(1)} %get-tuple-element.122.refs_3_), channel_id=1, source_target_pairs={{0,6},{1,7},{2,4},{3,5},{4,2},{5,3},{6,0},{7,1},{8,14},{9,15},{10,... | collective-permute-start | bytes 786440 | tf_op jit(solution)/shard_map/ppermute | solution.py:433
  189.2 10.1 %collective-permute-start.24 = (bf16[128,768]{1,0:T(8,128)(2,1)S(1)}, bf16[128,768]{1,0:T(8,128)(2,1)S(1)}, u32[]{:S(2)}, u32[]{:S(2)}) collective-permute-start(bf16[128,768]{1,0:T(8,128)(2,1)S(1)} %get-tuple-element.117), channel_id=1, source_target_pairs={{0,1},{1,0},{2,3},{3,2},{4,5},{5,4},{6,7},{7,6},{8,9},{9,8},{10,11... | collective-permute-start | bytes 589832 | tf_op jit(solution)/shard_map/ppermute | solution.py:433
  189.3 10.2 %collective-permute-start.25 = (bf16[128,768]{1,0:T(8,128)(2,1)S(1)}, bf16[128,768]{1,0:T(8,128)(2,1)S(1)}, u32[]{:S(2)}, u32[]{:S(2)}) collective-permute-start(bf16[128,768]{1,0:T(8,128)(2,1)S(1)} %get-tuple-element.118), channel_id=1, source_target_pairs={{0,8},{1,9},{2,10},{3,11},{4,12},{5,13},{6,14},{7,15},{8,0},{9,1},... | collective-permute-start | bytes 589832 | tf_op jit(solution)/shard_map/ppermute | solution.py:433
  192.3 8.7 %collective-permute-start.26 = (bf16[128,768]{1,0:T(8,128)(2,1)S(1)}, bf16[128,768]{1,0:T(8,128)(2,1)S(1)}, u32[]{:S(2)}, u32[]{:S(2)}) collective-permute-start(bf16[128,768]{1,0:T(8,128)(2,1)S(1)} %get-tuple-element.119), channel_id=1, source_target_pairs={{0,9},{1,8},{2,11},{3,10},{4,13},{5,12},{6,15},{7,14},{8,1},{9,0},... | collective-permute-start | bytes 589832 | tf_op jit(solution)/shard_map/ppermute | solution.py:433
  197.0 4.0 %collective-permute-start.30 = (bf16[128,256]{1,0:T(8,128)(2,1)S(1)}, bf16[128,256]{1,0:T(8,128)(2,1)S(1)}, u32[]{:S(2)}, u32[]{:S(2)}) collective-permute-start(bf16[128,256]{1,0:T(8,128)(2,1)S(1)} %get-tuple-element.124), channel_id=1, source_target_pairs={{0,1},{1,0},{2,3},{3,2},{4,5},{5,4},{6,7},{7,6},{8,9},{9,8},{10,11... | collective-permute-start | bytes 196616 | tf_op jit(solution)/shard_map/ppermute | solution.py:433
  197.1 5.9 %collective-permute-start.31 = (bf16[128,256]{1,0:T(8,128)(2,1)S(1)}, bf16[128,256]{1,0:T(8,128)(2,1)S(1)}, u32[]{:S(2)}, u32[]{:S(2)}) collective-permute-start(bf16[128,256]{1,0:T(8,128)(2,1)S(1)} %get-tuple-element.125), channel_id=1, source_target_pairs={{0,8},{1,9},{2,10},{3,11},{4,12},{5,13},{6,14},{7,15},{8,0},{9,1},... | collective-permute-start | bytes 196616 | tf_op jit(solution)/shard_map/ppermute | solution.py:433
  199.3 4.5 %collective-permute-start.32 = (bf16[128,256]{1,0:T(8,128)(2,1)S(1)}, bf16[128,256]{1,0:T(8,128)(2,1)S(1)}, u32[]{:S(2)}, u32[]{:S(2)}) collective-permute-start(bf16[128,256]{1,0:T(8,128)(2,1)S(1)} %get-tuple-element.126), channel_id=1, source_target_pairs={{0,9},{1,8},{2,11},{3,10},{4,13},{5,12},{6,15},{7,14},{8,1},{9,0},... | collective-permute-start | bytes 196616 | tf_op jit(solution)/shard_map/ppermute | solution.py:433

commit v16 on v15

--- a/solution.py
+++ b/solution.py
@@ -369,7 +369,7 @@
         for piece in range(4):
             for at in range(blocks_wide):
                 total = own[piece, :, pl.ds(at * LANES, LANES)]
-                for step, ref in zip((1, 2, 3), others):
+                for step, ref in zip((3, 1, 2), others):
                     source = at ^ step if relative else at
                     total += ref[piece, :, pl.ds(source * LANES, LANES)].astype(jnp.float32)
                 outs[piece][:, pl.ds((first + at) * LANES, LANES)] = total.astype(jnp.bfloat16)
@@ -493,7 +493,7 @@
         return [totals[group] for group in sorted(totals)]
 
     def across_plane(totals):
-        return [send(totals[step], flip(n, step * PLANE)) for step in (1, 2, 3)]
+        return [send(totals[step], flip(n, step * PLANE)) for step in (3, 1, 2)]
 
     pieces = []
 

time: 206 us -> 206 us (level)
  transfers between devices with their start and end apart: 33 -> 33, of which waited for: 16 -> 17; matrix products, arithmetic and copies ran while one was open for 1% -> 1% of each run, Pallas kernels for 22% -> 22%
where the time goes in v16:
time: 206 us
  waiting for transfers between devices  105 us (51%)
  Pallas kernels  51.2 us (25%)
  starting transfers between devices  42.7 us (21%)
  local copies, waits for them, and re-layouts  6.5 us (3%)
    ppermute x33, waiting for transfers between devices, send(): return lax.ppermute(array, 'fsdp', perm=perm)  105 us
    ppermute x33, starting transfers between devices, send(): return lax.ppermute(array, 'fsdp', perm=perm)  42.7 us
    pallas_call x4, Pallas kernels, product(): pl.pallas_call(functools.partial(product_kernel, [places[group] for group...  16 us
    pallas_call x1, Pallas kernels, stack_product(): pl.pallas_call(functools.partial(stack_product_kernel, places, a_at, w_at...  11 us
    pallas_call x3, Pallas kernels, pack(): pl.pallas_call(functools.partial(pack_kernel, apart, len(steps)), out_sha...  10.7 us
    pallas_call x2, Pallas kernels, reorder(): pl.pallas_call(functools.partial(reorder_kernel, count), out_shape=pltpu....  6.79 us
    unnamed x16, local copies, waits for them, and re-layouts  5.2 us
  transfers between devices with their start and end apart: 33, of which 17 were waited for; matrix products, arithmetic and copies ran while one was open for 1% of the time, Pallas kernels for 22%

profile of v16, /device:TPU:0, one launch (start us, length us, event | category | flops | bytes accessed | tf_op | source)
XLA Modules:
  0.0 205.8 jit_solution(15374093158933461883)
XLA Ops:
  0.0 3.9 %pack.3 = (bf16[2,28,128,128]{3,2,1,0:T(8,128)(2,1)S(1)}, bf16[2,28,128,128]{3,2,1,0:T(8,128)(2,1)S(1)}) custom-call(s32[1]{0:T(128)} %bitcast.3.plane_ref.choice_ref, bf16[128,14336]{1,0:T(8,128)(2,1)} %refs_0_.5, bf16[128,14336]{1,0:T(8,128)(2,1)} %refs_1_.5, bf16[14336,128]{1,0:T(8,128)(2,1)} %refs_2_.5, bf16[128,14336]{1,0:T(8,128)(2,1)} %refs_0_.5, ...), custom_call_target="tpu_custom_call" | custom-call | bytes 9175040 | tf_op jit(solution)/shard_map/pack/pallas_call | solution.py:63
  3.9 3.0 %collective-permute-start.4 = (bf16[2,28,128,128]{3,2,1,0:T(8,128)(2,1)S(1)}, bf16[2,28,128,128]{3,2,1,0:T(8,128)(2,1)S(1)}, u32[]{:S(2)}, u32[]{:S(2)}) collective-permute-start(bf16[2,28,128,128]{3,2,1,0:T(8,128)(2,1)S(1)} %get-tuple-element.70), channel_id=1, source_target_pairs={{0,4},{1,5},{2,6},{3,7},{4,0},{5,1},{6,2},{7,3},{8,12},{9,13},{10,... | collective-permute-start | bytes 5505032 | tf_op jit(solution)/shard_map/ppermute | solution.py:433
  6.9 1.5 collective-permute-start.3
  8.4 3.9 %pack.4 = (bf16[28,128,128]{2,1,0:T(8,128)(2,1)}, bf16[28,128,128]{2,1,0:T(8,128)(2,1)}) custom-call(s32[1]{0:T(128)} %bitcast.3.plane_ref.choice_ref, bf16[128,14336]{1,0:T(8,128)(2,1)} %refs_0_.5, bf16[128,14336]{1,0:T(8,128)(2,1)} %refs_1_.5, bf16[14336,128]{1,0:T(8,128)(2,1)} %refs_2_.5, bf16[2,28,128,128]{3,2,1,0:T(8,128)(2,1)S(1)} %get-tuple-element.66.refs_3_), custom_call_target="tpu_custom_call" | custom-call | bytes 4587520 | tf_op jit(solution)/shard_map/pack/pallas_call | solution.py:63
  12.3 1.6 collective-permute-start
  13.9 2.6 %collective-permute-start.2 = (bf16[28,128,128]{2,1,0:T(8,128)(2,1)}, bf16[28,128,128]{2,1,0:T(8,128)(2,1)S(1)}, u32[]{:S(2)}, u32[]{:S(2)}) collective-permute-start(bf16[28,128,128]{2,1,0:T(8,128)(2,1)} %get-tuple-element.68.refs_12_.refs_0_), channel_id=1, source_target_pairs={{8,0},{9,1},{10,2},{11,3},{12,4},{13,5},{14,6},{15,7},{24,8},{25,9... | collective-permute-start | bytes 2752520 | tf_op jit(solution)/shard_map/ppermute | solution.py:433
  17.2 18.6 %collective-permute-done.refs_3_.refs_0_.refs_1_ = bf16[28,128,128]{2,1,0:T(8,128)(2,1)S(1)} collective-permute-done((bf16[28,128,128]{2,1,0:T(8,128)(2,1)}, bf16[28,128,128]{2,1,0:T(8,128)(2,1)S(1)}, u32[]{:S(2)}, u32[]{:S(2)}) %collective-permute-start) | collective-permute-done | bytes 917536 | tf_op jit(solution)/shard_map/ppermute | solution.py:433
  35.8 2.9 %pack.5 = bf16[2,28,128,128]{3,2,1,0:T(8,128)(2,1)S(1)} custom-call(s32[1]{0:T(128)} %bitcast.3.plane_ref.choice_ref, bf16[128,14336]{1,0:T(8,128)(2,1)} %refs_0_.5, bf16[128,14336]{1,0:T(8,128)(2,1)} %refs_1_.5, bf16[14336,128]{1,0:T(8,128)(2,1)} %refs_2_.5, bf16[28,128,128]{2,1,0:T(8,128)(2,1)S(1)} %collective-permute-done.refs_3_.refs_0_.refs_1_), custom_call_target="tpu_custom_call" | custom-call | bytes 4587520 | tf_op jit(solution)/shard_map/pack/pallas_call | solution.py:63
  38.7 8.2 %collective-permute-done.4.two = bf16[2,28,128,128]{3,2,1,0:T(8,128)(2,1)S(1)} collective-permute-done((bf16[2,28,128,128]{3,2,1,0:T(8,128)(2,1)S(1)}, bf16[2,28,128,128]{3,2,1,0:T(8,128)(2,1)S(1)}, u32[]{:S(2)}, u32[]{:S(2)}) %collective-permute-start.4) | collective-permute-done | bytes 1835040 | tf_op jit(solution)/shard_map/ppermute | solution.py:433
  46.9 1.5 collective-permute-done.3.one
  48.4 1.4 collective-permute-start.5
  49.8 2.8 %unpack_pair.1 = (bf16[2,28,128,128]{3,2,1,0:T(8,128)(2,1)}, bf16[2,28,128,128]{3,2,1,0:T(8,128)(2,1)}) custom-call(bf16[2,28,128,128]{3,2,1,0:T(8,128)(2,1)S(1)} %collective-permute-done.3.one, bf16[2,28,128,128]{3,2,1,0:T(8,128)(2,1)S(1)} %collective-permute-done.4.two, bf16[28,128,128]{2,1,0:T(8,128)(2,1)S(1)} %collective-permute-done.refs_3_.refs_0_.refs_1_), custom_call_target="tpu_custom_call" | custom-call | bytes 7340032 | tf_op jit(solution)/shard_map/unpack_pair/pallas_call | solution.py:106
  52.6 1.6 collective-permute-start.8
  54.3 1.9 collective-permute-start.9
  57.6 2.0 collective-permute-done.6.refs_2_
  59.6 1.0 copy-done.2
  60.9 0.9 copy-done.4
  61.9 28.0 %collective-permute-done.5.packed = bf16[2,28,128,128]{3,2,1,0:T(8,128)(2,1)S(1)} collective-permute-done((bf16[2,28,128,128]{3,2,1,0:T(8,128)(2,1)S(1)}, bf16[2,28,128,128]{3,2,1,0:T(8,128)(2,1)S(1)}, u32[]{:S(2)}, u32[]{:S(2)}) %collective-permute-start.5) | collective-permute-done | bytes 1835040 | tf_op jit(solution)/shard_map/ppermute | solution.py:433
  89.8 1.7 unpack.1
  91.6 1.6 collective-permute-start.12
  93.2 1.6 collective-permute-start.13
  96.1 3.5 %reorder.2 = bf16[2,28,128,128]{3,2,1,0:T(8,128)(2,1)} custom-call(s32[2]{0:T(128)S(1)} %slice_bitcast_fusion.order_ref, bf16[2,28,128,128]{3,2,1,0:T(8,128)(2,1)S(1)} %collective-permute-done.5.packed, bf16[2,28,128,128]{3,2,1,0:T(8,128)(2,1)} %get-tuple-element.81.w_12.refs_13_.refs_1_), custom_call_target="tpu_custom_call" | custom-call | bytes 7340032 | tf_op jit(solution)/shard_map/reorder/pallas_call | solution.py:177
  99.6 13.4 %collective-permute-done.12.refs_9_ = bf16[28,128,128]{2,1,0:T(8,128)(2,1)} collective-permute-done((bf16[28,128,128]{2,1,0:T(8,128)(2,1)}, bf16[28,128,128]{2,1,0:T(8,128)(2,1)}, u32[]{:S(2)}, u32[]{:S(2)}) %collective-permute-start.12) | collective-permute-done | bytes 917536 | tf_op jit(solution)/shard_map/ppermute | solution.py:433
  113.1 5.8 %collective-permute-start.16 = (bf16[2,28,128,128]{3,2,1,0:T(8,128)(2,1)}, bf16[2,28,128,128]{3,2,1,0:T(8,128)(2,1)}, u32[]{:S(2)}, u32[]{:S(2)}) collective-permute-start(bf16[2,28,128,128]{3,2,1,0:T(8,128)(2,1)} %reorder.2), channel_id=1, source_target_pairs={{8,0},{9,1},{10,2},{11,3},{12,4},{13,5},{14,6},{15,7},{24,8},{25,9... | collective-permute-start | bytes 5505032 | tf_op jit(solution)/shard_map/ppermute | solution.py:433
  119.5 1.2 copy-done.3
  120.6 1.2 copy-done.5
  121.8 11.0 %stack_product.1 = (bf16[28,2048,128]{2,1,0:T(8,128)(2,1)S(1)}, bf16[4,128,512]{2,1,0:T(8,128)(2,1)S(1)}, bf16[4,128,512]{2,1,0:T(8,128)(2,1)S(1)}, bf16[4,128,512]{2,1,0:T(8,128)(2,1)S(1)}) custom-call(s32[1]{0:T(128)} %bitcast.2.choice_ref, bf16[28,128,128]{2,1,0:T(8,128)(2,1)} %get-tuple-element.67.refs_0_, ...), custom_call_target="tpu_custom_call" | custom-call | flops 5637144576 | bytes 18350080 | tf_op jit(solution)/shard_map/stack_product/pallas_call | solution.py:269
  132.8 3.3 %reorder.3 = bf16[28,128,128]{2,1,0:T(8,128)(2,1)} custom-call(s32[1]{0:T(128)} %bitcast.5.order_ref, bf16[2,28,128,128]{3,2,1,0:T(8,128)(2,1)S(1)} %collective-permute-done.5.packed, bf16[2,28,128,128]{3,2,1,0:T(8,128)(2,1)} %get-tuple-element.81.w_12.refs_13_.refs_1_), custom_call_target="tpu_custom_call" | custom-call | bytes 7340032 | tf_op jit(solution)/shard_map/reorder/pallas_call | solution.py:177
  136.1 3.0 %collective-permute-start.20 = (bf16[28,128,128]{2,1,0:T(8,128)(2,1)}, bf16[28,128,128]{2,1,0:T(8,128)(2,1)S(1)}, u32[]{:S(2)}, u32[]{:S(2)}) collective-permute-start(bf16[28,128,128]{2,1,0:T(8,128)(2,1)} %reorder.3), channel_id=1, source_target_pairs={{8,0},{9,1},{10,2},{11,3},{12,4},{13,5},{14,6},{15,7},{24,8},{25,9... | collective-permute-start | bytes 2752520 | tf_op jit(solution)/shard_map/ppermute | solution.py:433
  139.7 2.4 %collective-permute-start.17 = (bf16[4,128,512]{2,1,0:T(8,128)(2,1)S(1)}, bf16[4,128,512]{2,1,0:T(8,128)(2,1)S(1)}, u32[]{:S(2)}, u32[]{:S(2)}) collective-permute-start(bf16[4,128,512]{2,1,0:T(8,128)(2,1)S(1)} %get-tuple-element.99), channel_id=1, source_target_pairs={{0,6},{1,7},{2,4},{3,5},{4,2},{5,3},{6,0},{7,1},{8,14},{9,15},{10,... | collective-permute-start | bytes 1572872 | tf_op jit(solution)/shard_map/ppermute | solution.py:433
  142.6 4.2 %product.4.refs_2_.refs_0_ = f32[4,128,512]{2,1,0:T(8,128)S(1)} custom-call(s32[1]{0:T(128)} %bitcast.2.choice_ref, bf16[28,2048,128]{2,1,0:T(8,128)(2,1)S(1)} %get-tuple-element.92.a, bf16[28,128,128]{2,1,0:T(8,128)(2,1)} %get-tuple-element.68.refs_12_.refs_0_, bf16[2,28,128,128]{3,2,1,0:T(8,128)(2,1)} %get-tuple-element.81.w_12.refs_13_.refs_1_, ...), custom_call_target="tpu_custom_call" | custom-call | flops 1879048192 | bytes 7340032 | tf_op jit(solution)/shard_map/product/pallas_call | solution.py:338
  146.8 12.7 %collective-permute-done.16.refs_1_.refs_0_ = bf16[2,28,128,128]{3,2,1,0:T(8,128)(2,1)} collective-permute-done((bf16[2,28,128,128]{3,2,1,0:T(8,128)(2,1)}, bf16[2,28,128,128]{3,2,1,0:T(8,128)(2,1)}, u32[]{:S(2)}, u32[]{:S(2)}) %collective-permute-start.16) | collective-permute-done | bytes 1835040 | tf_op jit(solution)/shard_map/ppermute | solution.py:433
  159.5 5.3 %product.5 = (bf16[4,128,256]{2,1,0:T(8,128)(2,1)S(1)}, bf16[4,128,256]{2,1,0:T(8,128)(2,1)S(1)}, bf16[4,128,256]{2,1,0:T(8,128)(2,1)S(1)}, f32[4,128,256]{2,1,0:T(8,128)S(1)}) custom-call(s32[1]{0:T(128)} %bitcast.3.plane_ref.choice_ref, bf16[28,2048,128]{2,1,0:T(8,128)(2,1)S(1)} %get-tuple-element.92.a, bf16[28,128,128]{2,1,0:T(8,128)(2,1)S(1)} %copy-done.1, ...), custom_call_target="tpu_custom_call" | custom-call | flops 3758096384 | bytes 16515072 | tf_op jit(solution)/shard_map/product/pallas_call | solution.py:338
  165.0 1.4 collective-permute-done.19.refs_3_
  167.0 1.5 collective-permute-start.22
  168.4 1.4 collective-permute-start.23
  169.9 8.9 %collective-permute-done.20.refs_1_ = bf16[28,128,128]{2,1,0:T(8,128)(2,1)S(1)} collective-permute-done((bf16[28,128,128]{2,1,0:T(8,128)(2,1)}, bf16[28,128,128]{2,1,0:T(8,128)(2,1)S(1)}, u32[]{:S(2)}, u32[]{:S(2)}) %collective-permute-start.20) | collective-permute-done | bytes 917536 | tf_op jit(solution)/shard_map/ppermute | solution.py:433
  178.7 4.2 %product.6 = (bf16[4,128,256]{2,1,0:T(8,128)(2,1)S(1)}, bf16[4,128,256]{2,1,0:T(8,128)(2,1)S(1)}, bf16[4,128,256]{2,1,0:T(8,128)(2,1)S(1)}) custom-call(s32[1]{0:T(128)} %bitcast.3.plane_ref.choice_ref, bf16[28,2048,128]{2,1,0:T(8,128)(2,1)S(1)} %get-tuple-element.92.a, bf16[2,28,128,128]{3,2,1,0:T(8,128)(2,1)} %collective-permute-done.16.refs_1_.refs_0_, ...), custom_call_target="tpu_custom_call" | custom-call | flops 2818572288 | bytes 12845056 | tf_op jit(solution)/shard_map/product/pallas_call | solution.py:338
  183.8 1.5 collective-permute-start.28
  185.3 1.2 collective-permute-start.29
  186.5 2.3 %product.7.refs_8_.refs_0_ = f32[4,128,256]{2,1,0:T(8,128)S(1)} custom-call(s32[1]{0:T(128)} %bitcast.3.plane_ref.choice_ref, bf16[28,2048,128]{2,1,0:T(8,128)(2,1)S(1)} %get-tuple-element.92.a, bf16[2,28,128,128]{3,2,1,0:T(8,128)(2,1)} %collective-permute-done.16.refs_1_.refs_0_, bf16[28,128,128]{2,1,0:T(8,128)(2,1)S(1)} %collective-permute-done.20.refs_1_, ...), custom_call_target="tpu_custom_call" | custom-call | flops 939524096 | bytes 5505024 | tf_op jit(solution)/shard_map/product/pallas_call | solution.py:338
  189.3 2.2 %collective-permute-start.25 = (bf16[128,768]{1,0:T(8,128)(2,1)S(1)}, bf16[128,768]{1,0:T(8,128)(2,1)S(1)}, u32[]{:S(2)}, u32[]{:S(2)}) collective-permute-start(bf16[128,768]{1,0:T(8,128)(2,1)S(1)} %get-tuple-element.118), channel_id=1, source_target_pairs={{0,8},{1,9},{2,10},{3,11},{4,12},{5,13},{6,14},{7,15},{8,0},{9,1},... | collective-permute-start | bytes 589832 | tf_op jit(solution)/shard_map/ppermute | solution.py:433
  191.5 1.7 collective-permute-done.27.refs_1_
  193.2 3.7 %collective-permute-done.28.refs_2_ = bf16[4,128,256]{2,1,0:T(8,128)(2,1)S(1)} collective-permute-done((bf16[4,128,256]{2,1,0:T(8,128)(2,1)S(1)}, bf16[4,128,256]{2,1,0:T(8,128)(2,1)S(1)}, u32[]{:S(2)}, u32[]{:S(2)}) %collective-permute-start.28) | collective-permute-done | bytes 262176 | tf_op jit(solution)/shard_map/ppermute | solution.py:433
  197.7 2.2 %collective-permute-start.31 = (bf16[128,256]{1,0:T(8,128)(2,1)S(1)}, bf16[128,256]{1,0:T(8,128)(2,1)S(1)}, u32[]{:S(2)}, u32[]{:S(2)}) collective-permute-start(bf16[128,256]{1,0:T(8,128)(2,1)S(1)} %get-tuple-element.125), channel_id=1, source_target_pairs={{0,8},{1,9},{2,10},{3,11},{4,12},{5,13},{6,14},{7,15},{8,0},{9,1},... | collective-permute-start | bytes 196616 | tf_op jit(solution)/shard_map/ppermute | solution.py:433
  201.0 1.7 collective-permute-done.31.refs_6_
  202.7 1.3 collective-permute-done.32.refs_7_
  204.0 1.8 assemble.1
  (53 shorter events, 9.5 us)
Async XLA Ops:
  3.9 43.0 %collective-permute-start.4 = (bf16[2,28,128,128]{3,2,1,0:T(8,128)(2,1)S(1)}, bf16[2,28,128,128]{3,2,1,0:T(8,128)(2,1)S(1)}, u32[]{:S(2)}, u32[]{:S(2)}) collective-permute-start(bf16[2,28,128,128]{3,2,1,0:T(8,128)(2,1)S(1)} %get-tuple-element.70), channel_id=1, source_target_pairs={{0,4},{1,5},{2,6},{3,7},{4,0},{5,1},{6,2},{7,3},{8,12},{9,13},{10,... | collective-permute-start | bytes 5505032 | tf_op jit(solution)/shard_map/ppermute | solution.py:433
  6.9 41.5 %collective-permute-start.3 = (bf16[2,28,128,128]{3,2,1,0:T(8,128)(2,1)S(1)}, bf16[2,28,128,128]{3,2,1,0:T(8,128)(2,1)S(1)}, u32[]{:S(2)}, u32[]{:S(2)}) collective-permute-start(bf16[2,28,128,128]{3,2,1,0:T(8,128)(2,1)S(1)} %get-tuple-element.66.refs_3_), channel_id=1, source_target_pairs={{0,2},{1,3},{2,0},{3,1},{4,6},{5,7},{6,4},{7,5},{8,10},{9,11},{10,... | collective-permute-start | bytes 5505032 | tf_op jit(solution)/shard_map/ppermute | solution.py:433
  12.3 23.5 %collective-permute-start = (bf16[28,128,128]{2,1,0:T(8,128)(2,1)}, bf16[28,128,128]{2,1,0:T(8,128)(2,1)S(1)}, u32[]{:S(2)}, u32[]{:S(2)}) collective-permute-start(bf16[28,128,128]{2,1,0:T(8,128)(2,1)} %get-tuple-element.67.refs_0_), channel_id=1, source_target_pairs={{0,8},{1,9},{2,10},{3,11},{4,12},{5,13},{6,14},{7,15},{8,0},{9,1},... | collective-permute-start | bytes 2752520 | tf_op jit(solution)/shard_map/ppermute | solution.py:433
  13.9 42.3 %collective-permute-start.2 = (bf16[28,128,128]{2,1,0:T(8,128)(2,1)}, bf16[28,128,128]{2,1,0:T(8,128)(2,1)S(1)}, u32[]{:S(2)}, u32[]{:S(2)}) collective-permute-start(bf16[28,128,128]{2,1,0:T(8,128)(2,1)} %get-tuple-element.68.refs_12_.refs_0_), channel_id=1, source_target_pairs={{8,0},{9,1},{10,2},{11,3},{12,4},{13,5},{14,6},{15,7},{24,8},{25,9... | collective-permute-start | bytes 2752520 | tf_op jit(solution)/shard_map/ppermute | solution.py:433
  16.5 40.7 %collective-permute-start.1 = (bf16[28,128,128]{2,1,0:T(8,128)(2,1)}, bf16[28,128,128]{2,1,0:T(8,128)(2,1)S(1)}, u32[]{:S(2)}, u32[]{:S(2)}) collective-permute-start(bf16[28,128,128]{2,1,0:T(8,128)(2,1)} %get-tuple-element.68.refs_12_.refs_0_), channel_id=1, source_target_pairs={{8,16},{9,17},{10,18},{11,19},{12,20},{13,21},{14,22},{15,23},{16,... | collective-permute-start | bytes 2752520 | tf_op jit(solution)/shard_map/ppermute | solution.py:433
  38.7 18.4 %copy-start.7 = (bf16[28,128,128]{2,1,0:T(8,128)(2,1)S(1)}, bf16[28,128,128]{2,1,0:T(8,128)(2,1)}, u32[]{:S(2)}) copy-start(bf16[28,128,128]{2,1,0:T(8,128)(2,1)} %get-tuple-element.67.refs_0_) | copy-start | bytes 2752516
  48.4 41.5 %collective-permute-start.5 = (bf16[2,28,128,128]{3,2,1,0:T(8,128)(2,1)S(1)}, bf16[2,28,128,128]{3,2,1,0:T(8,128)(2,1)S(1)}, u32[]{:S(2)}, u32[]{:S(2)}) collective-permute-start(bf16[2,28,128,128]{3,2,1,0:T(8,128)(2,1)S(1)} %pack.5), channel_id=1, source_target_pairs={{0,6},{1,7},{2,4},{3,5},{4,2},{5,3},{6,0},{7,1},{8,14},{9,15},{10,... | collective-permute-start | bytes 5505032 | tf_op jit(solution)/shard_map/ppermute | solution.py:433
  52.6 42.2 %collective-permute-start.8 = (bf16[2,28,128,128]{3,2,1,0:T(8,128)(2,1)}, bf16[2,28,128,128]{3,2,1,0:T(8,128)(2,1)}, u32[]{:S(2)}, u32[]{:S(2)}) collective-permute-start(bf16[2,28,128,128]{3,2,1,0:T(8,128)(2,1)} %get-tuple-element.82.refs_4_), channel_id=1, source_target_pairs={{0,8},{1,9},{2,10},{3,11},{4,12},{5,13},{6,14},{7,15},{8,0},{9,1},... | collective-permute-start | bytes 5505032 | tf_op jit(solution)/shard_map/ppermute | solution.py:433
  54.3 40.5 %collective-permute-start.9 = (bf16[2,28,128,128]{3,2,1,0:T(8,128)(2,1)}, bf16[2,28,128,128]{3,2,1,0:T(8,128)(2,1)}, u32[]{:S(2)}, u32[]{:S(2)}) collective-permute-start(bf16[2,28,128,128]{3,2,1,0:T(8,128)(2,1)} %get-tuple-element.81.w_12.refs_13_.refs_1_), channel_id=1, source_target_pairs={{8,16},{9,17},{10,18},{11,19},{12,20},{13,21},{14,22},{15,23},{16,... | collective-permute-start | bytes 5505032 | tf_op jit(solution)/shard_map/ppermute | solution.py:433
  56.2 0.9 copy-start
  57.1 2.5 %collective-permute-start.6 = (bf16[28,128,128]{2,1,0:T(8,128)(2,1)S(1)}, bf16[28,128,128]{2,1,0:T(8,128)(2,1)S(1)}, u32[]{:S(2)}, u32[]{:S(2)}) collective-permute-start(bf16[28,128,128]{2,1,0:T(8,128)(2,1)S(1)} %copy-done.7), channel_id=1, source_target_pairs={{0,1},{1,0},{2,3},{3,2},{4,5},{5,4},{6,7},{7,6},{8,9},{9,8},{10,11... | collective-permute-start | bytes 2752520 | tf_op jit(solution)/shard_map/ppermute | solution.py:433
  57.1 32.7 %copy-start.6 = (bf16[28,128,128]{2,1,0:T(8,128)(2,1)}, bf16[28,128,128]{2,1,0:T(8,128)(2,1)S(1)}, u32[]{:S(2)}) copy-start(bf16[28,128,128]{2,1,0:T(8,128)(2,1)S(1)} %collective-permute-done.1.refs_15_.refs_3_) | copy-start | bytes 2752516
  57.1 3.8 %collective-permute-start.7 = (bf16[28,128,128]{2,1,0:T(8,128)(2,1)S(1)}, bf16[28,128,128]{2,1,0:T(8,128)(2,1)S(1)}, u32[]{:S(2)}, u32[]{:S(2)}) collective-permute-start(bf16[28,128,128]{2,1,0:T(8,128)(2,1)S(1)} %collective-permute-done.refs_3_.refs_0_.refs_1_), channel_id=1, source_target_pairs={{0,1},{1,0},{2,3},{3,2},{4,5},{5,4},{6,7},{7,6},{8,9},{9,8},{10,11... | collective-permute-start | bytes 2752520 | tf_op jit(solution)/shard_map/ppermute | solution.py:433
  59.6 1.0 copy-start.2
  60.9 0.9 copy-start.4
  91.6 21.5 %collective-permute-start.12 = (bf16[28,128,128]{2,1,0:T(8,128)(2,1)}, bf16[28,128,128]{2,1,0:T(8,128)(2,1)}, u32[]{:S(2)}, u32[]{:S(2)}) collective-permute-start(bf16[28,128,128]{2,1,0:T(8,128)(2,1)} %get-tuple-element.84.refs_8_), channel_id=1, source_target_pairs={{0,8},{1,9},{2,10},{3,11},{4,12},{5,13},{6,14},{7,15},{8,0},{9,1},... | collective-permute-start | bytes 2752520 | tf_op jit(solution)/shard_map/ppermute | solution.py:433
  93.2 19.8 %collective-permute-start.13 = (bf16[28,128,128]{2,1,0:T(8,128)(2,1)}, bf16[28,128,128]{2,1,0:T(8,128)(2,1)}, u32[]{:S(2)}, u32[]{:S(2)}) collective-permute-start(bf16[28,128,128]{2,1,0:T(8,128)(2,1)} %get-tuple-element.86.refs_14_.refs_2_), channel_id=1, source_target_pairs={{8,16},{9,17},{10,18},{11,19},{12,20},{13,21},{14,22},{15,23},{16,... | collective-permute-start | bytes 2752520 | tf_op jit(solution)/shard_map/ppermute | solution.py:433
  94.8 24.6 %collective-permute-start.10 = (bf16[2,28,128,128]{3,2,1,0:T(8,128)(2,1)}, bf16[2,28,128,128]{3,2,1,0:T(8,128)(2,1)}, u32[]{:S(2)}, u32[]{:S(2)}) collective-permute-start(bf16[2,28,128,128]{3,2,1,0:T(8,128)(2,1)} %get-tuple-element.82.refs_4_), channel_id=1, source_target_pairs={{0,1},{1,0},{2,3},{3,2},{4,5},{5,4},{6,7},{7,6},{8,9},{9,8},{10,11... | collective-permute-start | bytes 5505032 | tf_op jit(solution)/shard_map/ppermute | solution.py:433
  94.8 24.6 %collective-permute-start.11 = (bf16[2,28,128,128]{3,2,1,0:T(8,128)(2,1)}, bf16[2,28,128,128]{3,2,1,0:T(8,128)(2,1)}, u32[]{:S(2)}, u32[]{:S(2)}) collective-permute-start(bf16[2,28,128,128]{3,2,1,0:T(8,128)(2,1)} %collective-permute-done.8.refs_5_), channel_id=1, source_target_pairs={{0,1},{1,0},{2,3},{3,2},{4,5},{5,4},{6,7},{7,6},{8,9},{9,8},{10,11... | collective-permute-start | bytes 5505032 | tf_op jit(solution)/shard_map/ppermute | solution.py:433
  96.0 23.4 %collective-permute-start.14 = (bf16[28,128,128]{2,1,0:T(8,128)(2,1)}, bf16[28,128,128]{2,1,0:T(8,128)(2,1)}, u32[]{:S(2)}, u32[]{:S(2)}) collective-permute-start(bf16[28,128,128]{2,1,0:T(8,128)(2,1)} %get-tuple-element.84.refs_8_), channel_id=1, source_target_pairs={{0,1},{1,0},{2,3},{3,2},{4,5},{5,4},{6,7},{7,6},{8,9},{9,8},{10,11... | collective-permute-start | bytes 2752520 | tf_op jit(solution)/shard_map/ppermute | solution.py:433
  113.1 6.4 %collective-permute-start.15 = (bf16[28,128,128]{2,1,0:T(8,128)(2,1)}, bf16[28,128,128]{2,1,0:T(8,128)(2,1)}, u32[]{:S(2)}, u32[]{:S(2)}) collective-permute-start(bf16[28,128,128]{2,1,0:T(8,128)(2,1)} %collective-permute-done.12.refs_9_), channel_id=1, source_target_pairs={{0,1},{1,0},{2,3},{3,2},{4,5},{5,4},{6,7},{7,6},{8,9},{9,8},{10,11... | collective-permute-start | bytes 2752520 | tf_op jit(solution)/shard_map/ppermute | solution.py:433
  113.1 46.4 %collective-permute-start.16 = (bf16[2,28,128,128]{3,2,1,0:T(8,128)(2,1)}, bf16[2,28,128,128]{3,2,1,0:T(8,128)(2,1)}, u32[]{:S(2)}, u32[]{:S(2)}) collective-permute-start(bf16[2,28,128,128]{3,2,1,0:T(8,128)(2,1)} %reorder.2), channel_id=1, source_target_pairs={{8,0},{9,1},{10,2},{11,3},{12,4},{13,5},{14,6},{15,7},{24,8},{25,9... | collective-permute-start | bytes 5505032 | tf_op jit(solution)/shard_map/ppermute | solution.py:433
  119.5 1.2 copy-start.3
  120.6 1.2 copy-start.5
  136.1 42.6 %collective-permute-start.20 = (bf16[28,128,128]{2,1,0:T(8,128)(2,1)}, bf16[28,128,128]{2,1,0:T(8,128)(2,1)S(1)}, u32[]{:S(2)}, u32[]{:S(2)}) collective-permute-start(bf16[28,128,128]{2,1,0:T(8,128)(2,1)} %reorder.3), channel_id=1, source_target_pairs={{8,0},{9,1},{10,2},{11,3},{12,4},{13,5},{14,6},{15,7},{24,8},{25,9... | collective-permute-start | bytes 2752520 | tf_op jit(solution)/shard_map/ppermute | solution.py:433
  139.1 25.6 %collective-permute-start.18 = (bf16[4,128,512]{2,1,0:T(8,128)(2,1)S(1)}, bf16[4,128,512]{2,1,0:T(8,128)(2,1)S(1)}, u32[]{:S(2)}, u32[]{:S(2)}) collective-permute-start(bf16[4,128,512]{2,1,0:T(8,128)(2,1)S(1)} %get-tuple-element.100.refs_6_), channel_id=1, source_target_pairs={{0,2},{1,3},{2,0},{3,1},{4,6},{5,7},{6,4},{7,5},{8,10},{9,11},{10,... | collective-permute-start | bytes 1572872 | tf_op jit(solution)/shard_map/ppermute | solution.py:433
  139.7 25.4 %collective-permute-start.17 = (bf16[4,128,512]{2,1,0:T(8,128)(2,1)S(1)}, bf16[4,128,512]{2,1,0:T(8,128)(2,1)S(1)}, u32[]{:S(2)}, u32[]{:S(2)}) collective-permute-start(bf16[4,128,512]{2,1,0:T(8,128)(2,1)S(1)} %get-tuple-element.99), channel_id=1, source_target_pairs={{0,6},{1,7},{2,4},{3,5},{4,2},{5,3},{6,0},{7,1},{8,14},{9,15},{10,... | collective-permute-start | bytes 1572872 | tf_op jit(solution)/shard_map/ppermute | solution.py:433
  142.0 24.4 %collective-permute-start.19 = (bf16[4,128,512]{2,1,0:T(8,128)(2,1)S(1)}, bf16[4,128,512]{2,1,0:T(8,128)(2,1)S(1)}, u32[]{:S(2)}, u32[]{:S(2)}) collective-permute-start(bf16[4,128,512]{2,1,0:T(8,128)(2,1)S(1)} %get-tuple-element.101), channel_id=1, source_target_pairs={{0,4},{1,5},{2,6},{3,7},{4,0},{5,1},{6,2},{7,3},{8,12},{9,13},{10,... | collective-permute-start | bytes 1572872 | tf_op jit(solution)/shard_map/ppermute | solution.py:433
  142.6 16.9 %copy-start.1 = (bf16[28,128,128]{2,1,0:T(8,128)(2,1)S(1)}, bf16[28,128,128]{2,1,0:T(8,128)(2,1)}, u32[]{:S(2)}) copy-start(bf16[28,128,128]{2,1,0:T(8,128)(2,1)} %copy-done) | copy-start | bytes 2752516
  166.4 16.6 %collective-permute-start.21 = (bf16[4,128,256]{2,1,0:T(8,128)(2,1)S(1)}, bf16[4,128,256]{2,1,0:T(8,128)(2,1)S(1)}, u32[]{:S(2)}, u32[]{:S(2)}) collective-permute-start(bf16[4,128,256]{2,1,0:T(8,128)(2,1)S(1)} %get-tuple-element.110), channel_id=1, source_target_pairs={{0,6},{1,7},{2,4},{3,5},{4,2},{5,3},{6,0},{7,1},{8,14},{9,15},{10,... | collective-permute-start | bytes 786440 | tf_op jit(solution)/shard_map/ppermute | solution.py:433
  167.0 16.0 %collective-permute-start.22 = (bf16[4,128,256]{2,1,0:T(8,128)(2,1)S(1)}, bf16[4,128,256]{2,1,0:T(8,128)(2,1)S(1)}, u32[]{:S(2)}, u32[]{:S(2)}) collective-permute-start(bf16[4,128,256]{2,1,0:T(8,128)(2,1)S(1)} %get-tuple-element.111), channel_id=1, source_target_pairs={{0,2},{1,3},{2,0},{3,1},{4,6},{5,7},{6,4},{7,5},{8,10},{9,11},{10,... | collective-permute-start | bytes 786440 | tf_op jit(solution)/shard_map/ppermute | solution.py:433
  168.4 14.5 %collective-permute-start.23 = (bf16[4,128,256]{2,1,0:T(8,128)(2,1)S(1)}, bf16[4,128,256]{2,1,0:T(8,128)(2,1)S(1)}, u32[]{:S(2)}, u32[]{:S(2)}) collective-permute-start(bf16[4,128,256]{2,1,0:T(8,128)(2,1)S(1)} %get-tuple-element.112), channel_id=1, source_target_pairs={{0,4},{1,5},{2,6},{3,7},{4,0},{5,1},{6,2},{7,3},{8,12},{9,13},{10,... | collective-permute-start | bytes 786440 | tf_op jit(solution)/shard_map/ppermute | solution.py:433
  183.0 10.2 %collective-permute-start.27 = (bf16[4,128,256]{2,1,0:T(8,128)(2,1)S(1)}, bf16[4,128,256]{2,1,0:T(8,128)(2,1)S(1)}, u32[]{:S(2)}, u32[]{:S(2)}) collective-permute-start(bf16[4,128,256]{2,1,0:T(8,128)(2,1)S(1)} %get-tuple-element.120.refs_3_), channel_id=1, source_target_pairs={{0,6},{1,7},{2,4},{3,5},{4,2},{5,3},{6,0},{7,1},{8,14},{9,15},{10,... | collective-permute-start | bytes 786440 | tf_op jit(solution)/shard_map/ppermute | solution.py:433
  183.8 13.1 %collective-permute-start.28 = (bf16[4,128,256]{2,1,0:T(8,128)(2,1)S(1)}, bf16[4,128,256]{2,1,0:T(8,128)(2,1)S(1)}, u32[]{:S(2)}, u32[]{:S(2)}) collective-permute-start(bf16[4,128,256]{2,1,0:T(8,128)(2,1)S(1)} %get-tuple-element.121), channel_id=1, source_target_pairs={{0,2},{1,3},{2,0},{3,1},{4,6},{5,7},{6,4},{7,5},{8,10},{9,11},{10,... | collective-permute-start | bytes 786440 | tf_op jit(solution)/shard_map/ppermute | solution.py:433
  185.3 12.2 %collective-permute-start.29 = (bf16[4,128,256]{2,1,0:T(8,128)(2,1)S(1)}, bf16[4,128,256]{2,1,0:T(8,128)(2,1)S(1)}, u32[]{:S(2)}, u32[]{:S(2)}) collective-permute-start(bf16[4,128,256]{2,1,0:T(8,128)(2,1)S(1)} %get-tuple-element.122), channel_id=1, source_target_pairs={{0,4},{1,5},{2,6},{3,7},{4,0},{5,1},{6,2},{7,3},{8,12},{9,13},{10,... | collective-permute-start | bytes 786440 | tf_op jit(solution)/shard_map/ppermute | solution.py:433
  189.2 10.7 %collective-permute-start.24 = (bf16[128,768]{1,0:T(8,128)(2,1)S(1)}, bf16[128,768]{1,0:T(8,128)(2,1)S(1)}, u32[]{:S(2)}, u32[]{:S(2)}) collective-permute-start(bf16[128,768]{1,0:T(8,128)(2,1)S(1)} %get-tuple-element.117), channel_id=1, source_target_pairs={{0,1},{1,0},{2,3},{3,2},{4,5},{5,4},{6,7},{7,6},{8,9},{9,8},{10,11... | collective-permute-start | bytes 589832 | tf_op jit(solution)/shard_map/ppermute | solution.py:433
  189.3 10.8 %collective-permute-start.25 = (bf16[128,768]{1,0:T(8,128)(2,1)S(1)}, bf16[128,768]{1,0:T(8,128)(2,1)S(1)}, u32[]{:S(2)}, u32[]{:S(2)}) collective-permute-start(bf16[128,768]{1,0:T(8,128)(2,1)S(1)} %get-tuple-element.118), channel_id=1, source_target_pairs={{0,8},{1,9},{2,10},{3,11},{4,12},{5,13},{6,14},{7,15},{8,0},{9,1},... | collective-permute-start | bytes 589832 | tf_op jit(solution)/shard_map/ppermute | solution.py:433
  193.2 7.8 %collective-permute-start.26 = (bf16[128,768]{1,0:T(8,128)(2,1)S(1)}, bf16[128,768]{1,0:T(8,128)(2,1)S(1)}, u32[]{:S(2)}, u32[]{:S(2)}) collective-permute-start(bf16[128,768]{1,0:T(8,128)(2,1)S(1)} %get-tuple-element.119), channel_id=1, source_target_pairs={{0,9},{1,8},{2,11},{3,10},{4,13},{5,12},{6,15},{7,14},{8,1},{9,0},... | collective-permute-start | bytes 589832 | tf_op jit(solution)/shard_map/ppermute | solution.py:433
  197.6 3.4 %collective-permute-start.30 = (bf16[128,256]{1,0:T(8,128)(2,1)S(1)}, bf16[128,256]{1,0:T(8,128)(2,1)S(1)}, u32[]{:S(2)}, u32[]{:S(2)}) collective-permute-start(bf16[128,256]{1,0:T(8,128)(2,1)S(1)} %get-tuple-element.124), channel_id=1, source_target_pairs={{0,1},{1,0},{2,3},{3,2},{4,5},{5,4},{6,7},{7,6},{8,9},{9,8},{10,11... | collective-permute-start | bytes 196616 | tf_op jit(solution)/shard_map/ppermute | solution.py:433
  197.7 5.0 %collective-permute-start.31 = (bf16[128,256]{1,0:T(8,128)(2,1)S(1)}, bf16[128,256]{1,0:T(8,128)(2,1)S(1)}, u32[]{:S(2)}, u32[]{:S(2)}) collective-permute-start(bf16[128,256]{1,0:T(8,128)(2,1)S(1)} %get-tuple-element.125), channel_id=1, source_target_pairs={{0,8},{1,9},{2,10},{3,11},{4,12},{5,13},{6,14},{7,15},{8,0},{9,1},... | collective-permute-start | bytes 196616 | tf_op jit(solution)/shard_map/ppermute | solution.py:433
  200.0 4.0 %collective-permute-start.32 = (bf16[128,256]{1,0:T(8,128)(2,1)S(1)}, bf16[128,256]{1,0:T(8,128)(2,1)S(1)}, u32[]{:S(2)}, u32[]{:S(2)}) collective-permute-start(bf16[128,256]{1,0:T(8,128)(2,1)S(1)} %get-tuple-element.126), channel_id=1, source_target_pairs={{0,9},{1,8},{2,11},{3,10},{4,13},{5,12},{6,15},{7,14},{8,1},{9,0},... | collective-permute-start | bytes 196616 | tf_op jit(solution)/shard_map/ppermute | solution.py:433
